TPU v7x, 32 devices: a whole 2x2x4 slice. The times are simulated.
32 devices in a mesh: seq: 8 (over z, y), batch: 4 (over x, core).
Axes of the slice: x: 2, y: 2, z: 4, core: 2. Of those that a mesh axis runs over, the one named last changes fastest.
Arguments:
- tokens: bfloat16 [4, 16384, 256], P('batch', 'seq'), may hold values from -6 to 6
- cotangent: bfloat16 [4, 16384, 256], P('batch', 'seq'), may hold values from -3 to 3
- first_factor: bfloat16 [32, 512, 512], P('seq', 'batch'), may hold values from -0.25 to 0.25
- second_factor: bfloat16 [512, 32, 32], P('seq', 'batch'), may hold values from -1 to 1
- gate_source: int32 [256], replicated, may hold values from 0 to 255
- alternate: int32 [512], replicated, may hold values from 0 to 511, each once
Outputs:
- grad_tokens: bfloat16 [4, 16384, 256], P('batch', 'seq')
- grad_first: bfloat16 [32, 512, 512], P('seq', 'batch')
- grad_second: bfloat16 [512, 32, 32], P('seq', 'batch')
Inputs may be any that keep to these rules, and one draw needn't show every extreme that they name: `alternate`: a permutation: each of 0 to 511 once.
All inputs are finite; a program needn't handle non-finite values.
Results may differ from a plain program's by a relative error of at most 0.012.
Values may be sent and summed in bfloat16 or wider, within the bound.
No kernel may reach another device: no remote copies, remote signals or barrier semaphores. Data moves between devices by JAX's collectives and lax.ppermute only.
A program may use at most 64 MiB of HBM per device.

v0:
```python
import jax
import jax.numpy as jnp
from jax import lax
from jax.sharding import PartitionSpec as P


def shards(tokens, cotangent, first_factor, second_factor, gate_source, alternate):
    inputs = tokens[0]
    rows_here = inputs.shape[0]
    width = inputs.shape[1]
    order_len = alternate.shape[0]
    blocks_here = rows_here // order_len
    select = (lax.broadcasted_iota(jnp.int32, (width, width), 0) == gate_source[None, :]).astype(
        jnp.bfloat16
    )
    gate = jax.nn.sigmoid(jnp.dot(inputs, select, preferred_element_type=jnp.float32))
    first_full = lax.all_gather(first_factor, "batch", axis=1, tiled=True)
    second_full = lax.all_gather(second_factor, "batch", axis=1, tiled=True)
    blocked = inputs.reshape(blocks_here, order_len, width)
    mixed = jnp.einsum(
        "ikj,ijc->ikc", first_full, blocked, preferred_element_type=jnp.float32
    ).astype(jnp.bfloat16)
    shuffled = jnp.take(mixed, alternate, axis=1)
    piece = lax.all_to_all(shuffled, "seq", split_axis=1, concat_axis=0, tiled=True)
    z_blocks = jnp.einsum("jmi,ijc->jmc", second_full, piece, preferred_element_type=jnp.float32)
    j_here = z_blocks.shape[0]
    count_second = z_blocks.shape[1]
    z_out = z_blocks.reshape(rows_here, width)
    cot = cotangent[0].astype(jnp.float32)
    dz_out = (cot * gate).astype(jnp.bfloat16)
    dgate = cot * z_out * gate * (1.0 - gate)
    dz_blocks = dz_out.reshape(j_here, count_second, width)
    term_second = jnp.einsum("jmc,ijc->jmi", dz_blocks, piece, preferred_element_type=jnp.float32)
    second_back = lax.all_gather(second_factor, "batch", axis=1, tiled=True)
    first_back = lax.all_gather(first_factor, "batch", axis=1, tiled=True)
    grad_two = lax.psum_scatter(
        term_second.astype(jnp.bfloat16), "batch", scatter_dimension=1, tiled=True
    )
    dregrouped = jnp.einsum(
        "jmi,jmc->ijc", second_back, dz_blocks, preferred_element_type=jnp.float32
    ).astype(jnp.bfloat16)
    positions = lax.iota(jnp.int32, order_len)
    inverse = jnp.zeros((order_len,), jnp.int32).at[alternate].set(positions)
    restored = jnp.take(
        lax.all_to_all(dregrouped, "seq", split_axis=0, concat_axis=1, tiled=True), inverse, axis=1
    )
    dmix_in = jnp.einsum("ikj,ikc->ijc", first_back, restored, preferred_element_type=jnp.float32)
    term_first = jnp.einsum("ikc,ijc->ikj", restored, blocked, preferred_element_type=jnp.float32)
    grad_one = lax.psum_scatter(
        term_first.astype(jnp.bfloat16), "batch", scatter_dimension=1, tiled=True
    )
    spread = jnp.dot(dgate, select.T.astype(jnp.float32), precision=lax.Precision.HIGHEST)
    grad_tokens = (dmix_in.reshape(rows_here, width) + spread).astype(jnp.bfloat16)
    return (grad_tokens[None], grad_one, grad_two)


def solution(mesh):
    in_specs = (
        P("batch", "seq", None),
        P("batch", "seq", None),
        P("seq", "batch", None),
        P("seq", "batch", None),
        P(),
        P(),
    )
    out_specs = (P("batch", "seq", None), P("seq", "batch", None), P("seq", "batch", None))
    return jax.shard_map(shards, mesh=mesh, in_specs=in_specs, out_specs=out_specs, check_vma=False)
```

profile of v0, /device:TPU:0, one launch (start us, length us, event | category | flops | bytes accessed | tf_op | source)
XLA Modules:
  0.0 155.5 jit_solution(1480054415057846499)
XLA Ops:
  7.2 0.0 copy-start
  7.2 0.0 copy-start.7
  7.2 0.0 all-gather.2.cloned.1.call-start
  7.2 0.7 all-gather.2.cloned.1.call-update
  7.9 1.0 copy.43
  8.9 1.5 copy.41
  10.4 0.0 copy-done
  10.4 0.0 copy-done.7
  10.4 0.0 copy-start.5
  10.4 2.2 %fusion.6 = (bf16[2048,256]{0,1:T(8,128)(2,1)S(1)}, f32[2048,256]{0,1:T(8,128)}) fusion(bf16[1,2048,256]{1,2,0:T(8,128)(2,1)S(1)} %copy.41, bf16[1,2048,256]{2,1,0:T(8,128)(2,1)S(1)} %copy-done, s32[256]{0:T(256)S(1)} %copy-done.7), kind=kOutput, calls=%fused_computation.13 | convolution fusion | flops 271712256 | bytes 5243904 | tf_op jit(solution)/shard_map/dot_general | solution.py:16
  12.6 0.0 copy-done.5
  12.6 0.5 copy.42
  13.1 0.0 copy-start.1
  13.1 8.6 %all_gather.8 = bf16[64,32,32]{2,1,0:T(8,128)(2,1)S(1)} all-gather(bf16[64,8,32]{2,1,0:T(8,128)(2,1)S(1)} %copy.43), channel_id=1, replica_groups=mesh['seq'=8,'batch'=4] {'batch'}, dimensions={1}, use_global_device_ids=true | all-gather | bytes 163840 | tf_op jit(solution)/shard_map/all_gather | solution.py:34
  21.7 0.0 copy-start.3
  21.7 0.8 copy-done.3
  22.6 0.5 fusion.11
  23.0 0.0 copy-start.6
  23.1 1.6 %copy.44 = bf16[32,64,256]{2,1,0:T(8,128)(2,1)} copy(bf16[32,64,256]{2,0,1:T(8,128)(2,1)S(1)} %fusion.11) | data formatting | bytes 2097152 | tf_op jit(solution)/shard_map/convert_element_type | solution.py:41
  24.6 0.0 copy-done.1
  24.6 5.9 %all-to-all-start = ((bf16[32,64,256]{2,1,0:T(8,128)(2,1)}), bf16[32,64,256]{2,1,0:T(8,128)(2,1)}, u32[]{:S(2)}, u32[]{:S(2)}) async-start(bf16[32,64,256]{2,1,0:T(8,128)(2,1)} %copy.44), calls=%async_computation | async-start | bytes 2097152 | tf_op jit(solution)/shard_map/all_to_all | solution.py:45
  30.5 0.0 copy-done.6
  30.5 4.4 %all-gather.2.cloned.1.call-done = bf16[4,512,512]{2,1,0:T(8,128)(2,1)} async-done(((bf16[4,128,512]{2,1,0:T(8,128)(2,1)}), bf16[4,512,512]{2,1,0:T(8,128)(2,1)}) %all-gather.2.cloned.1.call-update) | async-done | bytes 2097168 | tf_op jit(solution)/shard_map/all_gather | solution.py:35
  34.9 2.3 %convolution_convert_fusion.1 = bf16[4,512,256]{2,1,0:T(8,128)(2,1)S(1)} fusion(bf16[4,512,512]{2,1,0:T(8,128)(2,1)} %all-gather.2.cloned.1.call-done, bf16[4,512,256]{2,1,0:T(8,128)(2,1)S(1)} %bitcast.51), kind=kOutput, calls=%fused_computation.19 | convolution fusion | flops 537395200 | bytes 4194304 | tf_op jit(solution)/shard_map/ikj,ijc->ikc/dot_general | solution.py:20
  37.2 0.8 copy.49
  38.0 2.4 %gather_fusion.1 = bf16[512,4,256]{2,1,0:T(4,128)(2,1)S(1)} fusion(bf16[4,512,256]{2,0,1:T(4,128)(2,1)S(1)} %copy.49, s32[1024]{0:T(1024)S(1)} %pad_clamp_fusion), kind=kCustom, calls=%fused_computation.1.clone | custom fusion | bytes 2099200 | tf_op jit(solution)/shard_map/jit(_take)/gather | solution.py:23
  40.4 2.7 %select_bitcast_fusion = bf16[4,512,256]{2,0,1:T(4,128)(2,1)} fusion(bf16[512,4,256]{2,1,0:T(4,128)(2,1)S(1)} %gather_fusion.1, pred[512]{0:T(512)(128)(4,1)S(1)} %compare_and_fusion), kind=kLoop, calls=%fused_computation.26 | loop fusion | flops 524288 | bytes 2097664 | tf_op jit(solution)/shard_map/jit(_take)/select_n | solution.py:23
  43.1 13.7 %all-to-all-done = bf16[32,64,256]{2,1,0:T(8,128)(2,1)} async-done(((bf16[32,64,256]{2,1,0:T(8,128)(2,1)}), bf16[32,64,256]{2,1,0:T(8,128)(2,1)}, u32[]{:S(2)}, u32[]{:S(2)}) %all-to-all-start) | async-done | bytes 1048608 | tf_op jit(solution)/shard_map/all_to_all | solution.py:45
  56.9 4.2 %all-to-all-start.1 = ((bf16[4,512,256]{2,0,1:T(4,128)(2,1)}), bf16[4,512,256]{2,0,1:T(4,128)(2,1)}, u32[]{:S(2)}, u32[]{:S(2)}) async-start(bf16[4,512,256]{2,0,1:T(4,128)(2,1)} %select_bitcast_fusion), calls=%async_computation.1 | async-start | bytes 2097152 | tf_op jit(solution)/shard_map/all_to_all | solution.py:24
  61.1 0.0 reduce-scatter.5.cloned.1.call-start
  61.2 2.4 %scatter_custom_fusion = s32[512]{0:T(512)S(1)} fusion(s32[512]{0:T(512)S(1)} %compare_select_fusion.1, s32[512]{0:T(512)S(1)} %iota.9, s32[]{:T(128)} %constant.3.clone.1), kind=kCustom, calls=%fused_computation.41 | custom fusion | bytes 2052 | tf_op jit(solution)/shard_map/scatter | solution.py:43
  63.6 1.3 copy.45
  64.9 0.8 copy.46
  65.8 2.4 %gather_fusion = bf16[512,4,256]{2,1,0:T(4,128)(2,1)S(1)} fusion(bf16[4,512,256]{2,0,1:T(4,128)(2,1)S(1)} %copy.46, s32[1024]{0:T(1024)S(1)} %pad_clamp_fusion.1), kind=kCustom, calls=%fused_computation.clone | custom fusion | bytes 2099200 | tf_op jit(solution)/shard_map/jit(_take)/gather | solution.py:44
  68.2 1.8 %select_bitcast_fusion.1 = bf16[4,512,256]{2,0,1:T(4,128)(2,1)S(1)} fusion(bf16[512,4,256]{2,1,0:T(4,128)(2,1)S(1)} %gather_fusion, pred[512]{0:T(512)(128)(4,1)S(1)} %compare_and_fusion.1), kind=kLoop, calls=%fused_computation.27 | loop fusion | flops 524288 | bytes 2097664 | tf_op jit(solution)/shard_map/jit(_take)/select_n | solution.py:44
  70.0 16.8 %all-to-all-done.1 = bf16[4,512,256]{2,0,1:T(4,128)(2,1)} async-done(((bf16[4,512,256]{2,0,1:T(4,128)(2,1)}), bf16[4,512,256]{2,0,1:T(4,128)(2,1)}, u32[]{:S(2)}, u32[]{:S(2)}) %all-to-all-start.1) | async-done | bytes 1048608 | tf_op jit(solution)/shard_map/all_to_all | solution.py:24
  86.7 2.8 %copy.59 = bf16[4,8,64,256]{3,0,1,2:T(4,128)(2,1)} copy(bf16[4,8,64,256]{3,0,2,1:T(4,128)(2,1)} %bitcast.14) | data formatting | bytes 2097152 | tf_op jit(solution)/shard_map/all_to_all | solution.py:24
  89.5 1.3 all_to_all.33
  90.9 2.4 %convolution_convert_fusion.3 = bf16[64,32,32]{2,1,0:T(8,128)(2,1)} fusion(bf16[64,32,256]{2,1,0:T(8,128)(2,1)} %bitcast.54, bf16[32,64,256]{2,0,1:T(8,128)(2,1)S(1)} %all_to_all.33), kind=kOutput, calls=%fused_computation.22 | convolution fusion | flops 33619968 | bytes 2228224 | tf_op jit(solution)/shard_map/jmc,ijc->jmi/dot_general | solution.py:33
  93.3 2.3 %copy.53 = bf16[64,32,32]{0,2,1:T(8,128)(2,1)} copy(bf16[64,32,32]{2,1,0:T(8,128)(2,1)} %convolution_convert_fusion.3) | data formatting | bytes 262144 | tf_op jit(solution)/shard_map/convert_element_type | solution.py:37
  95.5 0.0 reduce-scatter.5.cloned.1.call-update
  95.6 0.2 reduce-scatter.3.cloned.1.call-start
  95.8 2.1 %convolution_convert_fusion = bf16[4,512,512]{2,1,0:T(8,128)(2,1)} fusion(bf16[4,512,256]{2,1,0:T(8,128)(2,1)S(1)} %bitcast.52, bf16[4,512,256]{2,0,1:T(4,128)(2,1)S(1)} %select_bitcast_fusion.1), kind=kOutput, calls=%fused_computation.17 | convolution fusion | flops 537919488 | bytes 4194304 | tf_op jit(solution)/shard_map/ikc,ijc->ikj/dot_general | solution.py:48
  97.9 0.0 reduce-scatter.3.cloned.1.call-update
  97.9 3.7 %convolution_bitcast_fusion = f32[4,512,256]{1,2,0:T(8,128)} fusion(bf16[4,512,512]{2,1,0:T(8,128)(2,1)} %all-gather.2.cloned.1.call-done, bf16[4,512,256]{2,0,1:T(4,128)(2,1)S(1)} %select_bitcast_fusion.1), kind=kOutput, calls=%fused_computation.18 | convolution fusion | flops 536870912 | bytes 5242880 | tf_op jit(solution)/shard_map/ikj,ikc->ijc/dot_general | solution.py:47
  101.6 0.0 copy-start.4
  101.6 3.0 %copy.48 = f32[4,512,256]{2,1,0:T(8,128)} copy(f32[4,512,256]{1,2,0:T(8,128)} %convolution_bitcast_fusion) | data formatting | bytes 4194304 | tf_op jit(solution)/shard_map/ikj,ikc->ijc/dot_general | solution.py:47
  104.6 0.0 copy-done.4
  104.6 1.8 %fusion.24 = f32[64,256,32]{1,2,0:T(8,128)} fusion(bf16[64,32,32]{2,1,0:T(8,128)(2,1)S(1)} %copy-done.4, bf16[32,64,256]{2,0,1:T(8,128)(2,1)S(1)} %all_to_all.33), kind=kOutput, calls=%fused_computation.44 | convolution fusion | flops 33554432 | bytes 3276800 | tf_op jit(solution)/shard_map/jmi,ijc->jmc/dot_general | solution.py:25
  106.4 0.0 copy-start.2
  106.4 3.1 %copy.51 = f32[2048,256]{0,1:T(8,128)} copy(f32[2048,256]{1,0:T(8,128)} %bitcast.56) | data formatting | bytes 4194304 | tf_op jit(solution)/shard_map/reshape | solution.py:28
  109.4 0.0 copy-done.2
  109.4 5.4 %fusion.5 = bf16[1,2048,256]{2,1,0:T(8,128)(2,1)} fusion(f32[2048,256]{1,0:T(8,128)S(1)} %bitcast.55, f32[2048,256]{0,1:T(8,128)} %get-tuple-element.11, f32[2048,256]{0,1:T(8,128)} %copy.51, bf16[1,2048,256]{1,2,0:T(8,128)(2,1)} %copy-done.5, s32[256]{0:T(256)S(1)} %copy-done.7), kind=kOutput, calls=%fused_computation.12 | convolution fusion | flops 1614348288 | bytes 8389632 | tf_op jit(solution)/shard_map/dot_general | solution.py:52
  114.8 0.0 reduce-scatter.5.cloned.1.call-done
  114.8 34.1 %reduce-scatter.3.cloned.1.call-done = bf16[4,128,512]{2,1,0:T(8,128)(2,1)} async-done(((bf16[4,512,512]{2,1,0:T(8,128)(2,1)}), bf16[4,128,512]{2,1,0:T(8,128)(2,1)}) %reduce-scatter.3.cloned.1.call-update) | async-done | bytes 524304 | tf_op jit(solution)/shard_map/reduce_scatter | solution.py:49
  (7 shorter events, 0.0 us)
Async XLA Ops:
  7.2 3.2 %copy-start = (bf16[1,2048,256]{2,1,0:T(8,128)(2,1)S(1)}, bf16[1,2048,256]{2,1,0:T(8,128)(2,1)}, u32[]{:S(2)}) copy-start(bf16[1,2048,256]{2,1,0:T(8,128)(2,1)} %param.8) | copy-start | bytes 3145732
  7.2 3.2 %copy-start.7 = (s32[256]{0:T(256)S(1)}, s32[256]{0:T(256)}, u32[]{:S(2)}) copy-start(s32[256]{0:T(256)} %param.12) | copy-start | bytes 3076
  7.2 27.7 %all-gather.2.cloned.1.call-start = ((), (), s32[]{:S(2)}) async-start(), calls=%async_computation.4 | async-start | bytes 2621440 | tf_op jit(solution)/shard_map/all_gather | solution.py:35
  10.4 2.2 %copy-start.5 = (bf16[1,2048,256]{1,2,0:T(8,128)(2,1)}, bf16[1,2048,256]{1,2,0:T(8,128)(2,1)S(1)}, u32[]{:S(2)}) copy-start(bf16[1,2048,256]{1,2,0:T(8,128)(2,1)S(1)} %copy.41) | copy-start | bytes 3145732
  13.1 11.5 %copy-start.1 = (bf16[2048,256]{1,0:T(8,128)(2,1)}, bf16[2048,256]{1,0:T(8,128)(2,1)S(1)}, u32[]{:S(2)}) copy-start(bf16[2048,256]{1,0:T(8,128)(2,1)S(1)} %copy.42) | copy-start | bytes 3145732
  21.7 0.8 copy-start.3
  23.0 7.4 %copy-start.6 = (s32[512]{0:T(512)S(1)}, s32[512]{0:T(512)}, u32[]{:S(2)}) copy-start(s32[512]{0:T(512)} %param.13) | copy-start | bytes 6148
  24.6 32.2 %all-to-all-start = ((bf16[32,64,256]{2,1,0:T(8,128)(2,1)}), bf16[32,64,256]{2,1,0:T(8,128)(2,1)}, u32[]{:S(2)}, u32[]{:S(2)}) async-start(bf16[32,64,256]{2,1,0:T(8,128)(2,1)} %copy.44), calls=%async_computation | async-start | bytes 2097152 | tf_op jit(solution)/shard_map/all_to_all | solution.py:45
  56.9 29.9 %all-to-all-start.1 = ((bf16[4,512,256]{2,0,1:T(4,128)(2,1)}), bf16[4,512,256]{2,0,1:T(4,128)(2,1)}, u32[]{:S(2)}, u32[]{:S(2)}) async-start(bf16[4,512,256]{2,0,1:T(4,128)(2,1)} %select_bitcast_fusion), calls=%async_computation.1 | async-start | bytes 2097152 | tf_op jit(solution)/shard_map/all_to_all | solution.py:24
  61.1 53.7 %reduce-scatter.5.cloned.1.call-start = ((), (), s32[]{:S(2)}) async-start(), calls=%async_computation.6 | async-start | bytes 327680 | tf_op jit(solution)/shard_map/reduce_scatter | solution.py:36
  95.6 53.4 %reduce-scatter.3.cloned.1.call-start = ((), (), s32[]{:S(2)}) async-start(), calls=%async_computation.5 | async-start | bytes 2621440 | tf_op jit(solution)/shard_map/reduce_scatter | solution.py:49
  101.6 3.0 %copy-start.4 = (bf16[64,32,32]{2,1,0:T(8,128)(2,1)S(1)}, bf16[64,32,32]{2,1,0:T(8,128)(2,1)}, u32[]{:S(2)}) copy-start(bf16[64,32,32]{2,1,0:T(8,128)(2,1)} %copy-done.3) | copy-start | bytes 393220
  106.4 3.1 %copy-start.2 = (f32[4,512,256]{2,1,0:T(8,128)S(1)}, f32[4,512,256]{2,1,0:T(8,128)}, u32[]{:S(2)}) copy-start(f32[4,512,256]{2,1,0:T(8,128)} %copy.48) | copy-start | bytes 6291460
Sparse Core Ops, SparseCore 0:
  9.6 25.2 all-gather.1
  95.7 18.4 reduce-scatter.4
  117.5 31.3 reduce-scatter.2
where the time goes:
time: 156 us; the launch traced here: 155 us
  waiting for transfers between devices  69.7 us (45%)
  local copies, waits for them, and re-layouts  27.9 us (18%)
  matrix products  20.3 us (13%)
  between operations  14 us (9%)
  starting transfers between devices  10.4 us (7%)
  blocking collectives  8.62 us (6%)
  other arithmetic  4.51 us (3%)
    reduce_scatter x1, waiting for transfers between devices, shards(): lax.psum_scatter(term_first.astype(jnp.bfloat16), 'batch', scatter_dimens...  34.1 us
    all_to_all x1, waiting for transfers between devices, shards(): lax.all_to_all(shuffled, 'seq', split_axis=1, concat_axis=0, tiled=True)  16.8 us
    all_to_all x1, waiting for transfers between devices, shards(): lax.all_to_all(dregrouped, 'seq', split_axis=0, concat_axis=1, tiled=True)  13.7 us
    all_gather x1, blocking collectives, shards(): second_back = lax.all_gather(second_factor, 'batch', axis=1, tiled=True)  8.62 us
    all_to_all x1, starting transfers between devices, shards(): lax.all_to_all(dregrouped, 'seq', split_axis=0, concat_axis=1, tiled=True)  5.86 us
    dot_general x1, matrix products, shards(): jnp.dot(dgate, select.T.astype(jnp.float32), precision=lax.Precision.HIGH...  5.39 us
    all_gather x1, waiting for transfers between devices, shards(): first_back = lax.all_gather(first_factor, 'batch', axis=1, tiled=True)  4.38 us
    all_to_all x1, starting transfers between devices, shards(): lax.all_to_all(shuffled, 'seq', split_axis=1, concat_axis=0, tiled=True)  4.23 us
  transfers between devices with their start and end apart: 5, of which 4 were waited for; matrix products, arithmetic and copies ran while one was open for 28% of the time, Pallas kernels for 0%

commit v1 on v0

v1 whole, which is shorter than its diff:
```python
import functools

import jax
import jax.numpy as jnp
from jax import lax
from jax.experimental import pallas as pl
from jax.experimental.pallas import tpu as pltpu
from jax.sharding import PartitionSpec as P

BF16 = jnp.bfloat16
F32 = jnp.float32
LANE_GROUP = 16


def iota(shape, dim):
    return lax.broadcasted_iota(jnp.int32, shape, dim)


def one_hot(mask):
    return jnp.where(mask, 1.0, 0.0).astype(BF16)


def dot(a, b, da=1, db=0):
    return lax.dot_general(a, b, (((da,), (db,)), ((), ())), preferred_element_type=F32)


def call(body, outs, ins, scratch=(), flops=0, limit=40 << 20):
    size = sum(o.size * o.dtype.itemsize for o in outs) + sum(v.size * v.dtype.itemsize for v in ins)
    return pl.pallas_call(
        body,
        out_shape=outs,
        in_specs=[pl.BlockSpec(memory_space=pltpu.VMEM)] * len(ins),
        out_specs=[pl.BlockSpec(memory_space=pltpu.VMEM)] * len(outs),
        scratch_shapes=list(scratch),
        compiler_params=pltpu.CompilerParams(vmem_limit_bytes=limit),
        cost_estimate=pl.CostEstimate(flops=int(flops), bytes_accessed=int(size), transcendentals=0),
    )(*ins)


def of(shape, dtype=BF16):
    return jax.ShapeDtypeStruct(shape, dtype)


def swap(value, axis, step, size):
    return lax.ppermute(value, axis, [(p, p ^ step) for p in range(size)])


def pack_body(order, s_ref, out_ref):
    rows, j_here = s_ref.shape
    groups = j_here // LANE_GROUP
    lanes = order * LANE_GROUP
    m_here = rows // order
    s = s_ref[...]
    lane = iota((j_here, lanes), 1)
    keep = (iota((rows, lanes), 0) % order) == (iota((rows, lanes), 1) // LANE_GROUP)
    for g in range(groups):
        place = one_hot(iota((j_here, lanes), 0) == g * LANE_GROUP + lane % LANE_GROUP)
        wide = jnp.where(keep, dot(s, place), 0.0)
        packed = jnp.sum(wide.reshape(m_here, order, lanes), axis=1)
        out_ref[g * m_here : (g + 1) * m_here, :] = packed.astype(BF16)


def gate_body(x_ref, cot_ref, src_ref, dz_ref, h_ref):
    width = x_ref.shape[1]
    select = one_hot(iota((width, width), 0) == src_ref[...])
    step = 512

    @pl.loop(0, x_ref.shape[0] // step)
    def _(n):
        rows = pl.ds(pl.multiple_of(n * step, step), step)
        gate = jax.nn.sigmoid(dot(x_ref[rows, :], select))
        part = cot_ref[rows, :].astype(F32) * gate
        dz_ref[rows, :] = part.astype(BF16)
        h_ref[rows, :] = part * (1.0 - gate)


def regroup_back_body(batch, seq, order, *refs):
    pieces, dz_ref = refs[:batch], refs[batch]
    outs, second_ref, d_scr, r_scr = refs[batch + 1 : -3], refs[-3], refs[-2], refs[-1]
    me, here = lax.axis_index("batch"), lax.axis_index("seq")
    groups = second_ref.shape[0]
    lanes = order * LANE_GROUP
    m_here = order // batch
    for d in range(batch):
        piece = pieces[d][...].astype(F32)
        first = pl.multiple_of((me ^ d) * m_here, m_here)
        for g in range(groups):
            d_scr[g, pl.ds(first, m_here), :] = piece[g * m_here : (g + 1) * m_here]
    width = dz_ref.shape[1]

    @pl.loop(0, groups)
    def _(g):
        packed = d_scr[g].astype(BF16)
        second_ref[g] = packed
        tiled = one_hot((iota((order, lanes), 1) % order) == iota((order, lanes), 0))
        keep = (iota((lanes, lanes), 0) % LANE_GROUP) == (iota((lanes, lanes), 1) // order)
        weights = jnp.where(keep, dot(packed, tiled, 0, 0), 0.0).astype(BF16)
        dz = dz_ref[pl.ds(pl.multiple_of(g * lanes, lanes), lanes), :]
        result = dot(weights, dz).astype(BF16).reshape(order, LANE_GROUP, width)
        r_scr[:, pl.ds(pl.multiple_of(g * LANE_GROUP, LANE_GROUP), LANE_GROUP), :] = result

    blocks = order // seq
    for d in range(seq):
        outs[d][...] = r_scr[pl.ds((here ^ d) * blocks, blocks)]


def mix_body(batch, seq, *refs):
    pieces, x_ref, alt_ref = refs[:batch], refs[batch], refs[batch + 1]
    outs, p_scr, mix_scr, reg_scr = refs[batch + 2 : -3], refs[-3], refs[-2], refs[-1]
    me, here = lax.axis_index("batch"), lax.axis_index("seq")
    blocks, rows, order = pieces[0].shape
    j_here = order // seq
    from_rows = jnp.where(iota((order, order), 0) == alt_ref[...], 1.0, 0.0)
    p_scr[...] = from_rows.T.astype(BF16)

    @pl.loop(0, blocks)
    def _(i):
        x = x_ref[pl.ds(pl.multiple_of(i * order, order), order), :]
        for d in range(batch):
            first = pl.multiple_of((me ^ d) * rows, rows)
            mix_scr[pl.ds(first, rows), :] = dot(pieces[d][i], x).astype(BF16)
        reg_scr[...] = dot(p_scr[...], mix_scr[...]).astype(BF16)
        for d in range(seq):
            first = pl.multiple_of((here ^ d) * j_here, j_here)
            outs[d][i] = reg_scr[pl.ds(first, j_here), :]


def first_grad_body(batch, seq, *refs):
    pieces, x_ref, alt_ref = refs[:seq], refs[seq], refs[seq + 1]
    outs, dmixed_ref = refs[seq + 2 : seq + 2 + batch], refs[seq + 2 + batch]
    p_scr, reg_scr, part_scr = refs[-3:]
    me, here = lax.axis_index("batch"), lax.axis_index("seq")
    blocks, j_here, width = pieces[0].shape
    order = j_here * seq
    rows = order // batch
    p_scr[...] = one_hot(iota((order, order), 0) == alt_ref[...])

    @pl.loop(0, blocks)
    def _(i):
        for d in range(seq):
            first = pl.multiple_of((here ^ d) * j_here, j_here)
            reg_scr[pl.ds(first, j_here), :] = pieces[d][i]
        dmixed = dot(p_scr[...], reg_scr[...]).astype(BF16)
        dmixed_ref[i] = dmixed
        x = x_ref[pl.ds(pl.multiple_of(i * order, order), order), :]
        part_scr[...] = dot(dmixed, x, 1, 1).astype(BF16)
        for d in range(batch):
            first = pl.multiple_of((me ^ d) * rows, rows)
            outs[d][i] = part_scr[pl.ds(first, rows), :]


def mix_back_body(batch, *refs):
    pieces, dmixed_ref, out_ref = refs[:batch], refs[batch], refs[batch + 1]
    me = lax.axis_index("batch")
    blocks, rows, order = pieces[0].shape

    @pl.loop(0, blocks)
    def _(i):
        total = None
        for d in range(batch):
            first = pl.multiple_of((me ^ d) * rows, rows)
            term = dot(pieces[d][i], dmixed_ref[i, pl.ds(first, rows), :], 0, 0)
            total = term if total is None else total + term
        out_ref[pl.ds(pl.multiple_of(i * order, order), order), :] = total


def gather_blocks(seq, pieces, scr):
    here = lax.axis_index("seq")
    blocks = pieces[0].shape[0]
    for d in range(seq):
        scr[pl.ds((here ^ d) * blocks, blocks)] = pieces[d][...]


def second_grad_body(batch, seq, *refs):
    pieces, dz_ref = refs[:seq], refs[seq]
    outs, reg_ref, y_scr = refs[seq + 1 : seq + 1 + batch], refs[-2], refs[-1]
    me = lax.axis_index("batch")
    order, j_here, width = reg_ref.shape
    groups, lanes, m_here = j_here // LANE_GROUP, order * LANE_GROUP, order // batch
    gather_blocks(seq, pieces, reg_ref)

    @pl.loop(0, groups)
    def _(g):
        js = pl.ds(pl.multiple_of(g * LANE_GROUP, LANE_GROUP), LANE_GROUP)
        reg = reg_ref[:, js, :].reshape(lanes, width)
        dz = dz_ref[pl.ds(pl.multiple_of(g * lanes, lanes), lanes), :]
        wide = dot(dz, reg, 1, 1)
        col = iota((order, lanes), 1) % LANE_GROUP
        packed = wide[:order]
        for jj in range(1, LANE_GROUP):
            packed = jnp.where(col == jj, wide[jj * order : (jj + 1) * order], packed)
        y_scr[g] = packed

    for d in range(batch):
        first = pl.multiple_of((me ^ d) * m_here, m_here)
        rows = [y_scr[g, pl.ds(first, m_here), :] for g in range(groups)]
        outs[d][...] = jnp.concatenate(rows, axis=0).astype(BF16)


def tokens_body(reg_ref, second_ref, h_ref, src_ref, back_ref, out_ref):
    order, j_here, width = reg_ref.shape
    groups, lanes = j_here // LANE_GROUP, order * LANE_GROUP
    select = one_hot(iota((width, width), 0) == src_ref[...])

    @pl.loop(0, groups)
    def _(g):
        js = pl.ds(pl.multiple_of(g * LANE_GROUP, LANE_GROUP), LANE_GROUP)
        reg = reg_ref[:, js, :].reshape(lanes, width)
        packed = second_ref[g].astype(F32)
        col = iota((order, lanes), 1) % LANE_GROUP
        weights = jnp.concatenate(
            [jnp.where(col == jj, packed, 0.0).astype(BF16) for jj in range(LANE_GROUP)], axis=0
        )
        rows = pl.ds(pl.multiple_of(g * lanes, lanes), lanes)
        dgate = dot(weights, reg) * h_ref[rows, :]
        high = dgate.astype(BF16)
        low = (dgate - high.astype(F32)).astype(BF16)
        spread = dot(high, select, 1, 1) + dot(low, select, 1, 1)
        out_ref[rows, :] = (back_ref[rows, :] + spread).astype(BF16)


def pair_body(own_a, own_b, got_a, got_b, out_a, out_b):
    out_a[...] = own_a[...].astype(F32) + got_a[...].astype(F32)
    out_b[...] = (own_b[...].astype(F32) + got_b[...].astype(F32)).astype(BF16)


def add_body(own, got, out):
    out[...] = (own[...] + got[...].astype(F32)).astype(BF16)


def unpack_body(order, *refs):
    pieces, out_ref = refs[:-1], refs[-1]
    rows, j_here = out_ref.shape
    groups, lanes, m_here = j_here // LANE_GROUP, order * LANE_GROUP, rows // order
    total = pieces[0][...].astype(F32)
    for piece in pieces[1:]:
        total = total + piece[...].astype(F32)
    lane = iota((j_here, lanes), 1)
    keep = (iota((rows, lanes), 0) % order) == (iota((rows, lanes), 1) // LANE_GROUP)
    result = jnp.zeros((rows, j_here), F32)
    for g in range(groups):
        place = one_hot(iota((j_here, lanes), 0) == g * LANE_GROUP + lane % LANE_GROUP)
        packed = total[g * m_here : (g + 1) * m_here]
        wide = jnp.broadcast_to(packed[:, None, :], (m_here, order, lanes)).reshape(rows, lanes)
        result = result + dot(jnp.where(keep, wide, 0.0).astype(BF16), place, 1, 1)
    out_ref[...] = result.astype(BF16)


def packed_shards(tokens, cotangent, first_factor, second_factor, gate_source, alternate, batch, seq):
    x, cot = tokens[0], cotangent[0]
    rows_here, width = x.shape
    blocks, k_here, order = first_factor.shape
    j_here, m_here, count = second_factor.shape
    groups, lanes = j_here // LANE_GROUP, count * LANE_GROUP
    src = gate_source.reshape(1, width)
    alt = alternate.reshape(1, order)
    big = 2 * rows_here * order * width

    flat = jnp.transpose(second_factor, (1, 2, 0)).reshape(m_here * count, j_here)
    (mine,) = call(functools.partial(pack_body, count), [of((groups * m_here, lanes))], [flat])
    packed = [mine] + [swap(mine, "batch", d, batch) for d in range(1, batch)]
    dz, h = call(
        gate_body, [of((rows_here, width)), of((rows_here, width), F32)], [x, cot, src], flops=big // 2
    )
    piece = of((blocks, j_here, width))
    *back, second = call(
        functools.partial(regroup_back_body, batch, seq, count),
        [piece] * seq + [of((groups, count, lanes))],
        [*packed, dz],
        [pltpu.VMEM((groups, count, lanes), F32), pltpu.VMEM((count, j_here, width), BF16)],
        flops=2 * big,
    )
    order_of = sorted(range(1, seq), key=lambda d: -d)
    back_got = {d: swap(back[d], "seq", d, seq) for d in order_of}
    back_got[0] = back[0]

    first_ready, _ = lax.optimization_barrier((first_factor, packed[1:]))
    across = swap(first_ready, "batch", 2, batch)
    first = [first_ready, swap(first_ready, "batch", 1, batch), across, swap(across, "batch", 1, batch)]
    regrouped = call(
        functools.partial(mix_body, batch, seq),
        [piece] * seq,
        [*first, x, alt],
        [pltpu.VMEM((order, order), BF16), pltpu.VMEM((order, width), BF16), pltpu.VMEM((order, width), BF16)],
        flops=2 * big,
    )
    got = {d: swap(regrouped[d], "seq", d, seq) for d in order_of}
    got[0] = regrouped[0]

    *parts, dmixed = call(
        functools.partial(first_grad_body, batch, seq),
        [of((blocks, k_here, order))] * batch + [of((blocks, order, width))],
        [*[back_got[d] for d in range(seq)], x, alt],
        [pltpu.VMEM((order, order), BF16), pltpu.VMEM((order, width), BF16), pltpu.VMEM((order, order), BF16)],
        flops=2 * big,
    )
    near = swap(parts[1], "batch", 1, batch)
    far = swap(parts[3], "batch", 1, batch)
    (dmix_in,) = call(
        functools.partial(mix_back_body, batch), [of((rows_here, width), F32)], [*first, dmixed], flops=big
    )
    kept, sent = call(
        pair_body, [of(parts[0].shape, F32), of(parts[0].shape)], [parts[0], parts[2], near, far]
    )
    (grad_one,) = call(add_body, [of(parts[0].shape)], [kept, swap(sent, "batch", 2, batch)])

    *terms, gathered = call(
        functools.partial(second_grad_body, batch, seq),
        [of((groups * m_here, lanes))] * batch + [of((count, j_here, width))],
        [*[got[d] for d in range(seq)], dz],
        [pltpu.VMEM((groups, count, lanes), F32)],
        flops=2 * big,
    )
    terms_got = [terms[0]] + [swap(terms[d], "batch", d, batch) for d in range(1, batch)]
    (grad_tokens,) = call(
        tokens_body, [of((rows_here, width))], [gathered, second, h, src, dmix_in], flops=2 * big
    )
    (grad_flat,) = call(
        functools.partial(unpack_body, count), [of((m_here * count, j_here))], terms_got
    )
    grad_two = jnp.transpose(grad_flat.reshape(m_here, count, j_here), (2, 0, 1))
    return (grad_tokens[None], grad_one, grad_two)


def wide_shards(tokens, cotangent, first_factor, second_factor, gate_source, alternate):
    inputs = tokens[0]
    rows_here = inputs.shape[0]
    width = inputs.shape[1]
    order_len = alternate.shape[0]
    blocks_here = rows_here // order_len
    select = one_hot(lax.broadcasted_iota(jnp.int32, (width, width), 0) == gate_source[None, :])
    gate = jax.nn.sigmoid(jnp.dot(inputs, select, preferred_element_type=F32))
    first_full = lax.all_gather(first_factor, "batch", axis=1, tiled=True)
    second_full = lax.all_gather(second_factor, "batch", axis=1, tiled=True)
    blocked = inputs.reshape(blocks_here, order_len, width)
    mixed = jnp.einsum("ikj,ijc->ikc", first_full, blocked, preferred_element_type=F32).astype(BF16)
    shuffled = jnp.take(mixed, alternate, axis=1)
    piece = lax.all_to_all(shuffled, "seq", split_axis=1, concat_axis=0, tiled=True)
    z_blocks = jnp.einsum("jmi,ijc->jmc", second_full, piece, preferred_element_type=F32)
    j_here, count_second = z_blocks.shape[:2]
    z_out = z_blocks.reshape(rows_here, width)
    cot = cotangent[0].astype(F32)
    dz_out = (cot * gate).astype(BF16)
    dgate = cot * z_out * gate * (1.0 - gate)
    dz_blocks = dz_out.reshape(j_here, count_second, width)
    term_second = jnp.einsum("jmc,ijc->jmi", dz_blocks, piece, preferred_element_type=F32)
    grad_two = lax.psum_scatter(term_second.astype(BF16), "batch", scatter_dimension=1, tiled=True)
    dregrouped = jnp.einsum("jmi,jmc->ijc", second_full, dz_blocks, preferred_element_type=F32).astype(BF16)
    positions = lax.iota(jnp.int32, order_len)
    inverse = jnp.zeros((order_len,), jnp.int32).at[alternate].set(positions)
    restored = jnp.take(
        lax.all_to_all(dregrouped, "seq", split_axis=0, concat_axis=1, tiled=True), inverse, axis=1
    )
    dmix_in = jnp.einsum("ikj,ikc->ijc", first_full, restored, preferred_element_type=F32)
    term_first = jnp.einsum("ikc,ijc->ikj", restored, blocked, preferred_element_type=F32)
    grad_one = lax.psum_scatter(term_first.astype(BF16), "batch", scatter_dimension=1, tiled=True)
    spread = jnp.dot(dgate, select.T.astype(F32), precision=lax.Precision.HIGHEST)
    grad_tokens = (dmix_in.reshape(rows_here, width) + spread).astype(BF16)
    return (grad_tokens[None], grad_one, grad_two)


def solution(mesh):
    batch, seq = mesh.shape["batch"], mesh.shape["seq"]

    def shards(*args):
        j_here, m_here, count = args[3].shape
        if batch == 4 and seq & (seq - 1) == 0 and j_here % LANE_GROUP == 0 and m_here % 8 == 0 and count <= 32:
            return packed_shards(*args, batch, seq)
        return wide_shards(*args)

    in_specs = (
        P("batch", "seq", None),
        P("batch", "seq", None),
        P("seq", "batch", None),
        P("seq", "batch", None),
        P(),
        P(),
    )
    out_specs = (P("batch", "seq", None), P("seq", "batch", None), P("seq", "batch", None))
    return jax.shard_map(shards, mesh=mesh, in_specs=in_specs, out_specs=out_specs, check_vma=False)
```

time: 156 us -> 92.3 us (0.59)
  waiting for transfers between devices: 69.7 us -> 30.1 us
  starting transfers between devices: 10.4 us -> 38.7 us
  local copies, waits for them, and re-layouts: 27.9 us -> 3.98 us
  matrix products: 20.3 us -> 0 us
  Pallas kernels: 0 us -> 18.5 us
  between operations: 14 us -> 0.8 us
  blocking collectives: 8.62 us -> 0 us
  other arithmetic: 4.51 us -> 0 us
    ppermute x0 -> x26, starting transfers between devices: none -> 38.7 us  [swap(): return lax.ppermute(value, axis, [(p, p ^ step) for p in range(size)])]
    reduce_scatter x2 -> x0, waiting for transfers between devices: 34.1 us -> none  [the longest x1 34.1 us: shards(): lax.psum_scatter(term_first.astype(jnp.bfloat16), 'batch', scatter_dimens...]
    all_to_all x2 -> x0, waiting for transfers between devices: 30.5 us -> none  [the longest x1 16.8 us: shards(): lax.all_to_all(shuffled, 'seq', split_axis=1, concat_axis=0, tiled=True)]
    ppermute x0 -> x26, waiting for transfers between devices: none -> 30.1 us  [swap(): return lax.ppermute(value, axis, [(p, p ^ step) for p in range(size)])]
    dot_general x8 -> x0, matrix products: 20.3 us -> none  [the longest x1 5.39 us: shards(): jnp.dot(dgate, select.T.astype(jnp.float32), precision=lax.Precision.HIGH...]
    pallas_call x0 -> x11, Pallas kernels: none -> 18.5 us  [call(): pl.pallas_call(body, out_shape=outs, in_specs=[pl.BlockSpec(memory_space=...]
    all_to_all x2 -> x0, starting transfers between devices: 10.1 us -> none  [the longest x1 5.86 us: shards(): lax.all_to_all(dregrouped, 'seq', split_axis=0, concat_axis=1, tiled=True)]
    all_gather x1 -> x0, blocking collectives: 8.62 us -> none  [shards(): second_back = lax.all_gather(second_factor, 'batch', axis=1, tiled=True)]
  transfers between devices with their start and end apart: 5 -> 26, of which waited for: 4 -> 10; matrix products, arithmetic and copies ran while one was open for 28% -> 0% of each run, Pallas kernels for 0% -> 18%
where the time goes in v1:
time: 92.3 us; the launch traced here: 92 us
  starting transfers between devices  38.7 us (42%)
  waiting for transfers between devices  30.1 us (33%)
  Pallas kernels  18.5 us (20%)
  local copies, waits for them, and re-layouts  3.98 us (4%)
    ppermute x26, starting transfers between devices, swap(): return lax.ppermute(value, axis, [(p, p ^ step) for p in range(size)])  38.7 us
    ppermute x26, waiting for transfers between devices, swap(): return lax.ppermute(value, axis, [(p, p ^ step) for p in range(size)])  30.1 us
    pallas_call x11, Pallas kernels, call(): pl.pallas_call(body, out_shape=outs, in_specs=[pl.BlockSpec(memory_space=...  18.5 us
    unnamed x16, local copies, waits for them, and re-layouts  3.98 us
  transfers between devices with their start and end apart: 26, of which 10 were waited for; matrix products, arithmetic and copies ran while one was open for 0% of the time, Pallas kernels for 18%

profile of v1, /device:TPU:0, one launch (start us, length us, event | category | flops | bytes accessed | tf_op | source)
XLA Modules:
  0.0 92.0 jit_solution(18087223130995485311)
XLA Ops:
  0.6 0.8 copy-done.4
  1.5 0.4 shard_map.85.refs_0_
  1.9 0.5 collective-permute-start
  2.4 2.6 %collective-permute-start.1 = (bf16[32,512]{1,0:T(8,128)(2,1)S(1)}, bf16[32,512]{1,0:T(8,128)(2,1)S(1)}, u32[]{:S(2)}, u32[]{:S(2)}) collective-permute-start(bf16[32,512]{1,0:T(8,128)(2,1)S(1)} %shard_map.85.refs_0_), channel_id=1, source_target_pairs={{0,2},{1,3},{2,0},{3,1},{4,6},{5,7},{6,4},{7,5},{8,10},{9,11},{10,... | collective-permute-start | bytes 98312 | tf_op jit(solution)/shard_map/ppermute | solution.py:45
  5.0 0.1 collective-permute-start.2
  5.0 0.0 collective-permute-done.refs_1_
  5.0 1.9 %collective-permute-done.1.refs_2_ = bf16[32,512]{1,0:T(8,128)(2,1)S(1)} collective-permute-done((bf16[32,512]{1,0:T(8,128)(2,1)S(1)}, bf16[32,512]{1,0:T(8,128)(2,1)S(1)}, u32[]{:S(2)}, u32[]{:S(2)}) %collective-permute-start.1) | collective-permute-done | bytes 32800 | tf_op jit(solution)/shard_map/ppermute | solution.py:45
  7.0 1.4 %collective-permute-done.2.refs_3_ = bf16[32,512]{1,0:T(8,128)(2,1)S(1)} collective-permute-done((bf16[32,512]{1,0:T(8,128)(2,1)S(1)}, bf16[32,512]{1,0:T(8,128)(2,1)S(1)}, u32[]{:S(2)}, u32[]{:S(2)}) %collective-permute-start.2) | collective-permute-done | bytes 32800 | tf_op jit(solution)/shard_map/ppermute | solution.py:45
  8.3 0.8 collective-permute-start.4
  9.1 1.2 %copy-done = bf16[1,2048,256]{2,1,0:T(8,128)(2,1)S(1)} copy-done((bf16[1,2048,256]{2,1,0:T(8,128)(2,1)S(1)}, bf16[1,2048,256]{2,1,0:T(8,128)(2,1)}, u32[]{:S(2)}) %copy-start) | copy-done | bytes 1048600
  10.3 1.2 %copy-done.1 = bf16[1,2048,256]{2,1,0:T(8,128)(2,1)S(1)} copy-done((bf16[1,2048,256]{2,1,0:T(8,128)(2,1)S(1)}, bf16[1,2048,256]{2,1,0:T(8,128)(2,1)}, u32[]{:S(2)}) %copy-start.1) | copy-done | bytes 1048600
  11.5 0.7 copy-done.5
  12.2 1.2 %shard_map.87 = (bf16[2048,256]{1,0:T(8,128)(2,1)S(1)}, f32[2048,256]{1,0:T(8,128)S(1)}) custom-call(bf16[2048,256]{1,0:T(8,128)(2,1)S(1)} %bitcast.12, bf16[2048,256]{1,0:T(8,128)(2,1)S(1)} %bitcast.11, s32[1,256]{1,0:T(1,128)S(1)} %bitcast.16), custom_call_target="tpu_custom_call" | custom-call | flops 268435456 | bytes 5243904 | tf_op jit(solution)/shard_map/pallas_call | solution.py:29
  13.4 0.0 copy-start.2
  13.4 0.0 copy-start.7
  13.4 2.0 %shard_map.89 = (bf16[4,64,256]{2,1,0:T(8,128)(2,1)S(1)}, bf16[4,64,256]{2,1,0:T(8,128)(2,1)S(1)}, bf16[4,64,256]{2,1,0:T(8,128)(2,1)S(1)}, bf16[4,64,256]{2,1,0...) custom-call(bf16[32,512]{1,0:T(8,128)(2,1)S(1)} %shard_map.85.refs_0, ...), custom_call_target="tpu_custom_call" | custom-call | flops 1073741824 | bytes 2359296 | tf_op jit(solution)/shard_map/pallas_call | solution.py:29
  15.4 0.0 copy-start.3
  15.4 1.8 %collective-permute-start.13 = (bf16[4,64,256]{2,1,0:T(8,128)(2,1)S(1)}, bf16[4,64,256]{2,1,0:T(8,128)(2,1)S(1)}, u32[]{:S(2)}, u32[]{:S(2)}) collective-permute-start(bf16[4,64,256]{2,1,0:T(8,128)(2,1)S(1)} %get-tuple-element.49), channel_id=1, source_target_pairs={{0,4},{4,0},{8,12},{12,8},{16,20},{20,16},{24,28},{28,24},{1,5},{5... | collective-permute-start | bytes 393224 | tf_op jit(solution)/shard_map/ppermute | solution.py:45
  17.1 1.6 %collective-permute-start.14 = (bf16[4,64,256]{2,1,0:T(8,128)(2,1)S(1)}, bf16[4,64,256]{2,1,0:T(8,128)(2,1)S(1)}, u32[]{:S(2)}, u32[]{:S(2)}) collective-permute-start(bf16[4,64,256]{2,1,0:T(8,128)(2,1)S(1)} %get-tuple-element.50), channel_id=1, source_target_pairs={{0,8},{4,12},{8,0},{12,4},{16,24},{20,28},{24,16},{28,20},{1,9},{5... | collective-permute-start | bytes 393224 | tf_op jit(solution)/shard_map/ppermute | solution.py:45
  18.7 0.2 collective-permute-start.15
  18.9 2.8 %collective-permute-start.16 = (bf16[4,64,256]{2,1,0:T(8,128)(2,1)S(1)}, bf16[4,64,256]{2,1,0:T(8,128)(2,1)S(1)}, u32[]{:S(2)}, u32[]{:S(2)}) collective-permute-start(bf16[4,64,256]{2,1,0:T(8,128)(2,1)S(1)} %get-tuple-element.52), channel_id=1, source_target_pairs={{0,16},{4,20},{8,24},{12,28},{16,0},{20,4},{24,8},{28,12},{1,17},{... | collective-permute-start | bytes 393224 | tf_op jit(solution)/shard_map/ppermute | solution.py:45
  21.7 0.0 collective-permute-done.13.refs_1_
  21.7 3.0 %collective-permute-start.17 = (bf16[4,64,256]{2,1,0:T(8,128)(2,1)S(1)}, bf16[4,64,256]{2,1,0:T(8,128)(2,1)S(1)}, u32[]{:S(2)}, u32[]{:S(2)}) collective-permute-start(bf16[4,64,256]{2,1,0:T(8,128)(2,1)S(1)} %get-tuple-element.53), channel_id=1, source_target_pairs={{0,20},{4,16},{8,28},{12,24},{16,4},{20,0},{24,12},{28,8},{1,21},{... | collective-permute-start | bytes 393224 | tf_op jit(solution)/shard_map/ppermute | solution.py:45
  24.7 3.3 %collective-permute-done.14.refs_2_ = bf16[4,64,256]{2,1,0:T(8,128)(2,1)S(1)} collective-permute-done((bf16[4,64,256]{2,1,0:T(8,128)(2,1)S(1)}, bf16[4,64,256]{2,1,0:T(8,128)(2,1)S(1)}, u32[]{:S(2)}, u32[]{:S(2)}) %collective-permute-start.14) | collective-permute-done | bytes 131104 | tf_op jit(solution)/shard_map/ppermute | solution.py:45
  27.9 2.0 %collective-permute-start.18 = (bf16[4,64,256]{2,1,0:T(8,128)(2,1)S(1)}, bf16[4,64,256]{2,1,0:T(8,128)(2,1)S(1)}, u32[]{:S(2)}, u32[]{:S(2)}) collective-permute-start(bf16[4,64,256]{2,1,0:T(8,128)(2,1)S(1)} %get-tuple-element.54), channel_id=1, source_target_pairs={{0,24},{4,28},{8,16},{12,20},{16,8},{20,12},{24,0},{28,4},{1,25},{... | collective-permute-start | bytes 393224 | tf_op jit(solution)/shard_map/ppermute | solution.py:45
  29.9 0.0 collective-permute-done.15.refs_3_
  29.9 2.3 %collective-permute-start.19 = (bf16[4,64,256]{2,1,0:T(8,128)(2,1)S(1)}, bf16[4,64,256]{2,1,0:T(8,128)(2,1)S(1)}, u32[]{:S(2)}, u32[]{:S(2)}) collective-permute-start(bf16[4,64,256]{2,1,0:T(8,128)(2,1)S(1)} %get-tuple-element.55), channel_id=1, source_target_pairs={{0,28},{4,24},{8,20},{12,16},{16,12},{20,8},{24,4},{28,0},{1,29},{... | collective-permute-start | bytes 393224 | tf_op jit(solution)/shard_map/ppermute | solution.py:45
  32.2 8.8 %collective-permute-done.17.refs_5_ = bf16[4,64,256]{2,1,0:T(8,128)(2,1)S(1)} collective-permute-done((bf16[4,64,256]{2,1,0:T(8,128)(2,1)S(1)}, bf16[4,64,256]{2,1,0:T(8,128)(2,1)S(1)}, u32[]{:S(2)}, u32[]{:S(2)}) %collective-permute-start.17) | collective-permute-done | bytes 131104 | tf_op jit(solution)/shard_map/ppermute | solution.py:45
  41.0 0.0 collective-permute-done.18.refs_6_
  41.0 0.0 collective-permute-done.19.refs_7_
  41.1 3.0 %shard_map.90 = (bf16[4,128,512]{2,1,0:T(8,128)(2,1)S(1)}, bf16[4,128,512]{2,1,0:T(8,128)(2,1)S(1)}, bf16[4,128,512]{2,1,0:T(8,128)(2,1)S(1)}, bf16[4,128,512]{2,1,0:T(8,128)(2,1)S(1)}, bf16[4,512,256]{2,1,0:T(8,128)(2,1)S(1)}) custom-call(bf16[4,64,256]{2,1,0:T(8,128)(2,1)S(1)} %get-tuple-element.48.refs_0_, ...), custom_call_target="tpu_custom_call" | custom-call | flops 1073741824 | bytes 5244928 | tf_op jit(solution)/shard_map/pallas_call | solution.py:29
  44.1 0.1 collective-permute-start.20
  44.2 0.5 collective-permute-start.21
  44.7 0.1 collective-permute-start.3
  44.8 0.0 collective-permute-done.4.refs_2_
  44.8 0.4 collective-permute-start.5
  45.2 0.9 collective-permute-done.20.got_a
  46.1 0.7 collective-permute-done.21.got_b
  46.8 0.2 shard_map.93
  47.0 1.2 %collective-permute-start.22 = (bf16[4,128,512]{2,1,0:T(8,128)(2,1)S(1)}, bf16[4,128,512]{2,1,0:T(8,128)(2,1)S(1)}, u32[]{:S(2)}, u32[]{:S(2)}) collective-permute-start(bf16[4,128,512]{2,1,0:T(8,128)(2,1)S(1)} %get-tuple-element.62), channel_id=1, source_target_pairs={{0,2},{1,3},{2,0},{3,1},{4,6},{5,7},{6,4},{7,5},{8,10},{9,11},{10,... | collective-permute-start | bytes 1572872 | tf_op jit(solution)/shard_map/ppermute | solution.py:45
  48.3 0.0 collective-permute-done.3.refs_1_
  48.3 0.0 collective-permute-done.5.refs_3_
  48.3 2.7 %shard_map.86 = (bf16[4,64,256]{2,1,0:T(8,128)(2,1)S(1)}, bf16[4,64,256]{2,1,0:T(8,128)(2,1)S(1)}, bf16[4,64,256]{2,1,0:T(8,128)(2,1)S(1)}, bf16[4,64,256]{2,1,0...) custom-call(bf16[4,128,512]{2,1,0:T(8,128)(2,1)S(1)} %copy-done.3, ...), custom_call_target="tpu_custom_call" | custom-call | flops 1073741824 | bytes 4196352 | tf_op jit(solution)/shard_map/pallas_call | solution.py:29
  51.0 7.2 %collective-permute-start.10 = (bf16[4,64,256]{2,1,0:T(8,128)(2,1)S(1)}, bf16[4,64,256]{2,1,0:T(8,128)(2,1)S(1)}, u32[]{:S(2)}, u32[]{:S(2)}) collective-permute-start(bf16[4,64,256]{2,1,0:T(8,128)(2,1)S(1)} %get-tuple-element.41), channel_id=1, source_target_pairs={{0,20},{4,16},{8,28},{12,24},{16,4},{20,0},{24,12},{28,8},{1,21},{... | collective-permute-start | bytes 393224 | tf_op jit(solution)/shard_map/ppermute | solution.py:45
  58.2 0.3 collective-permute-start.11
  58.4 4.1 %collective-permute-start.12 = (bf16[4,64,256]{2,1,0:T(8,128)(2,1)S(1)}, bf16[4,64,256]{2,1,0:T(8,128)(2,1)S(1)}, u32[]{:S(2)}, u32[]{:S(2)}) collective-permute-start(bf16[4,64,256]{2,1,0:T(8,128)(2,1)S(1)} %get-tuple-element.43), channel_id=1, source_target_pairs={{0,28},{4,24},{8,20},{12,16},{16,12},{20,8},{24,4},{28,0},{1,29},{... | collective-permute-start | bytes 393224 | tf_op jit(solution)/shard_map/ppermute | solution.py:45
  62.6 0.9 collective-permute-start.6
  63.5 7.4 %collective-permute-done.10.refs_5_ = bf16[4,64,256]{2,1,0:T(8,128)(2,1)S(1)} collective-permute-done((bf16[4,64,256]{2,1,0:T(8,128)(2,1)S(1)}, bf16[4,64,256]{2,1,0:T(8,128)(2,1)S(1)}, u32[]{:S(2)}, u32[]{:S(2)}) %collective-permute-start.10) | collective-permute-done | bytes 131104 | tf_op jit(solution)/shard_map/ppermute | solution.py:45
  70.9 3.4 %collective-permute-start.8 = (bf16[4,64,256]{2,1,0:T(8,128)(2,1)S(1)}, bf16[4,64,256]{2,1,0:T(8,128)(2,1)S(1)}, u32[]{:S(2)}, u32[]{:S(2)}) collective-permute-start(bf16[4,64,256]{2,1,0:T(8,128)(2,1)S(1)} %get-tuple-element.39), channel_id=1, source_target_pairs={{0,12},{4,8},{8,4},{12,0},{16,28},{20,24},{24,20},{28,16},{1,13},{... | collective-permute-start | bytes 393224 | tf_op jit(solution)/shard_map/ppermute | solution.py:45
  74.3 1.2 %collective-permute-start.9 = (bf16[4,64,256]{2,1,0:T(8,128)(2,1)S(1)}, bf16[4,64,256]{2,1,0:T(8,128)(2,1)S(1)}, u32[]{:S(2)}, u32[]{:S(2)}) collective-permute-start(bf16[4,64,256]{2,1,0:T(8,128)(2,1)S(1)} %get-tuple-element.40), channel_id=1, source_target_pairs={{0,16},{4,20},{8,24},{12,28},{16,0},{20,4},{24,8},{28,12},{1,17},{... | collective-permute-start | bytes 393224 | tf_op jit(solution)/shard_map/ppermute | solution.py:45
  75.4 1.9 %shard_map.91.back_ref = f32[2048,256]{1,0:T(8,128)S(1)} custom-call(bf16[4,128,512]{2,1,0:T(8,128)(2,1)S(1)} %copy-done.3, bf16[4,128,512]{2,1,0:T(8,128)(2,1)S(1)} %collective-permute-done.3.refs_1_, bf16[4,128,512]{2,1,0:T(8,128)(2,1)S(1)} %collective-permute-done.4.refs_2_, bf16[4,128,512]{2,1,0:T(8,128)(2,1)S(1)} %collective-permute-done.5.refs_3_, ...), custom_call_target="tpu_custom_call" | custom-call | flops 536870912 | bytes 5242880 | tf_op jit(solution)/shard_map/pallas_call | solution.py:29
  77.3 0.0 copy-start.6
  77.3 0.0 collective-permute-done.6.refs_1_
  77.3 0.9 %collective-permute-done.7.refs_2_ = bf16[4,64,256]{2,1,0:T(8,128)(2,1)S(1)} collective-permute-done((bf16[4,64,256]{2,1,0:T(8,128)(2,1)S(1)}, bf16[4,64,256]{2,1,0:T(8,128)(2,1)S(1)}, u32[]{:S(2)}, u32[]{:S(2)}) %collective-permute-start.7) | collective-permute-done | bytes 131104 | tf_op jit(solution)/shard_map/ppermute | solution.py:45
  78.3 2.8 %collective-permute-done.8.refs_3_ = bf16[4,64,256]{2,1,0:T(8,128)(2,1)S(1)} collective-permute-done((bf16[4,64,256]{2,1,0:T(8,128)(2,1)S(1)}, bf16[4,64,256]{2,1,0:T(8,128)(2,1)S(1)}, u32[]{:S(2)}, u32[]{:S(2)}) %collective-permute-start.8) | collective-permute-done | bytes 131104 | tf_op jit(solution)/shard_map/ppermute | solution.py:45
  81.1 1.9 %collective-permute-done.9.refs_4_ = bf16[4,64,256]{2,1,0:T(8,128)(2,1)S(1)} collective-permute-done((bf16[4,64,256]{2,1,0:T(8,128)(2,1)S(1)}, bf16[4,64,256]{2,1,0:T(8,128)(2,1)S(1)}, u32[]{:S(2)}, u32[]{:S(2)}) %collective-permute-start.9) | collective-permute-done | bytes 131104 | tf_op jit(solution)/shard_map/ppermute | solution.py:45
  82.9 1.4 %shard_map.88 = (bf16[32,512]{1,0:T(8,128)(2,1)S(1)}, bf16[32,512]{1,0:T(8,128)(2,1)S(1)}, bf16[32,512]{1,0:T(8,128)(2,1)S(1)}, bf16[32,512]{1,0:T(8,128)(2,1)S(1)}, bf16[32,64,256]{2,1,0:T(8,128)(2,1)S(1)}) custom-call(bf16[4,64,256]{2,1,0:T(8,128)(2,1)S(1)} %get-tuple-element.36.refs_0_, bf16[4,64,256]{2,1,0:T(8,128)(2,1)S(1)} %collective-permute-done.6.refs_1_, ...), custom_call_target="tpu_custom_call" | custom-call | flops 1073741824 | bytes 3276800 | tf_op jit(solution)/shard_map/pallas_call | solution.py:29
  84.4 0.1 collective-permute-start.23
  84.5 1.2 %collective-permute-start.24 = (bf16[32,512]{1,0:T(8,128)(2,1)S(1)}, bf16[32,512]{1,0:T(8,128)(2,1)S(1)}, u32[]{:S(2)}, u32[]{:S(2)}) collective-permute-start(bf16[32,512]{1,0:T(8,128)(2,1)S(1)} %get-tuple-element.65), channel_id=1, source_target_pairs={{0,2},{1,3},{2,0},{3,1},{4,6},{5,7},{6,4},{7,5},{8,10},{9,11},{10,... | collective-permute-start | bytes 98312 | tf_op jit(solution)/shard_map/ppermute | solution.py:45
  85.6 0.7 collective-permute-start.25
  86.3 3.7 %shard_map.92 = bf16[2048,256]{1,0:T(8,128)(2,1)} custom-call(bf16[32,64,256]{2,1,0:T(8,128)(2,1)S(1)} %get-tuple-element.45.reg_ref, bf16[4,32,512]{2,1,0:T(8,128)(2,1)S(1)} %get-tuple-element.46.second_ref, f32[2048,256]{1,0:T(8,128)S(1)} %get-tuple-element.47.h_ref, s32[1,256]{1,0:T(1,128)S(1)} %bitcast.17, f32[2048,256]{1,0:T(8,128)S(1)} %shard_map.91.back_ref), custom_call_target="tpu_custom_call" | custom-call | flops 1073741824 | bytes 6423552 | tf_op jit(solution)/shard_map/pallas_call | solution.py:29
  90.1 0.0 collective-permute-done.22.got
  90.1 0.9 shard_map.94
  91.0 1.1 %shard_map.95 = bf16[256,64]{1,0:T(8,128)(2,1)} custom-call(bf16[32,512]{1,0:T(8,128)(2,1)S(1)} %get-tuple-element.63.refs_0_, bf16[32,512]{1,0:T(8,128)(2,1)S(1)} %collective-permute-done.23.refs_1_, bf16[32,512]{1,0:T(8,128)(2,1)S(1)} %collective-permute-done.24.refs_2_, bf16[32,512]{1,0:T(8,128)(2,1)S(1)} %collective-permute-done.25.refs_3_), custom_call_target="tpu_custom_call" | custom-call | bytes 163840 | tf_op jit(solution)/shard_map/pallas_call | solution.py:29
  (15 shorter events, 0.0 us)
Async XLA Ops:
  0.6 0.8 copy-start.4
  1.9 3.2 %collective-permute-start = (bf16[32,512]{1,0:T(8,128)(2,1)S(1)}, bf16[32,512]{1,0:T(8,128)(2,1)S(1)}, u32[]{:S(2)}, u32[]{:S(2)}) collective-permute-start(bf16[32,512]{1,0:T(8,128)(2,1)S(1)} %shard_map.85.refs_0_), channel_id=1, source_target_pairs={{0,1},{1,0},{2,3},{3,2},{4,5},{5,4},{6,7},{7,6},{8,9},{9,8},{10,11... | collective-permute-start | bytes 98312 | tf_op jit(solution)/shard_map/ppermute | solution.py:45
  2.4 4.5 %collective-permute-start.1 = (bf16[32,512]{1,0:T(8,128)(2,1)S(1)}, bf16[32,512]{1,0:T(8,128)(2,1)S(1)}, u32[]{:S(2)}, u32[]{:S(2)}) collective-permute-start(bf16[32,512]{1,0:T(8,128)(2,1)S(1)} %shard_map.85.refs_0_), channel_id=1, source_target_pairs={{0,2},{1,3},{2,0},{3,1},{4,6},{5,7},{6,4},{7,5},{8,10},{9,11},{10,... | collective-permute-start | bytes 98312 | tf_op jit(solution)/shard_map/ppermute | solution.py:45
  5.0 3.3 %collective-permute-start.2 = (bf16[32,512]{1,0:T(8,128)(2,1)S(1)}, bf16[32,512]{1,0:T(8,128)(2,1)S(1)}, u32[]{:S(2)}, u32[]{:S(2)}) collective-permute-start(bf16[32,512]{1,0:T(8,128)(2,1)S(1)} %shard_map.85.refs_0_), channel_id=1, source_target_pairs={{0,3},{1,2},{2,1},{3,0},{4,7},{5,6},{6,5},{7,4},{8,11},{9,10},{10,... | collective-permute-start | bytes 98312 | tf_op jit(solution)/shard_map/ppermute | solution.py:45
  8.3 36.4 %collective-permute-start.4 = (bf16[4,128,512]{2,1,0:T(8,128)(2,1)}, bf16[4,128,512]{2,1,0:T(8,128)(2,1)S(1)}, u32[]{:S(2)}, u32[]{:S(2)}) collective-permute-start(bf16[4,128,512]{2,1,0:T(8,128)(2,1)} %refs_0_.1), channel_id=1, source_target_pairs={{0,2},{1,3},{2,0},{3,1},{4,6},{5,7},{6,4},{7,5},{8,10},{9,11},{10,... | collective-permute-start | bytes 1572872 | tf_op jit(solution)/shard_map/ppermute | solution.py:45
  9.1 1.2 %copy-start = (bf16[1,2048,256]{2,1,0:T(8,128)(2,1)S(1)}, bf16[1,2048,256]{2,1,0:T(8,128)(2,1)}, u32[]{:S(2)}) copy-start(bf16[1,2048,256]{2,1,0:T(8,128)(2,1)} %param.7) | copy-start | bytes 3145732
  10.3 1.2 %copy-start.1 = (bf16[1,2048,256]{2,1,0:T(8,128)(2,1)S(1)}, bf16[1,2048,256]{2,1,0:T(8,128)(2,1)}, u32[]{:S(2)}) copy-start(bf16[1,2048,256]{2,1,0:T(8,128)(2,1)} %param.6) | copy-start | bytes 3145732
  11.5 0.7 copy-start.5
  13.4 27.7 %copy-start.2 = (bf16[1,2048,256]{2,1,0:T(8,128)(2,1)S(1)}, bf16[1,2048,256]{2,1,0:T(8,128)(2,1)}, u32[]{:S(2)}) copy-start(bf16[1,2048,256]{2,1,0:T(8,128)(2,1)} %param.6) | copy-start | bytes 3145732
  13.4 27.7 %copy-start.7 = (s32[512]{0:T(512)S(1)}, s32[512]{0:T(512)}, u32[]{:S(2)}) copy-start(s32[512]{0:T(512)} %param.11) | copy-start | bytes 6148
  15.4 29.3 %copy-start.3 = (bf16[4,128,512]{2,1,0:T(8,128)(2,1)S(1)}, bf16[4,128,512]{2,1,0:T(8,128)(2,1)}, u32[]{:S(2)}) copy-start(bf16[4,128,512]{2,1,0:T(8,128)(2,1)} %refs_0_.1) | copy-start | bytes 1572868
  15.4 6.3 %collective-permute-start.13 = (bf16[4,64,256]{2,1,0:T(8,128)(2,1)S(1)}, bf16[4,64,256]{2,1,0:T(8,128)(2,1)S(1)}, u32[]{:S(2)}, u32[]{:S(2)}) collective-permute-start(bf16[4,64,256]{2,1,0:T(8,128)(2,1)S(1)} %get-tuple-element.49), channel_id=1, source_target_pairs={{0,4},{4,0},{8,12},{12,8},{16,20},{20,16},{24,28},{28,24},{1,5},{5... | collective-permute-start | bytes 393224 | tf_op jit(solution)/shard_map/ppermute | solution.py:45
  17.1 10.8 %collective-permute-start.14 = (bf16[4,64,256]{2,1,0:T(8,128)(2,1)S(1)}, bf16[4,64,256]{2,1,0:T(8,128)(2,1)S(1)}, u32[]{:S(2)}, u32[]{:S(2)}) collective-permute-start(bf16[4,64,256]{2,1,0:T(8,128)(2,1)S(1)} %get-tuple-element.50), channel_id=1, source_target_pairs={{0,8},{4,12},{8,0},{12,4},{16,24},{20,28},{24,16},{28,20},{1,9},{5... | collective-permute-start | bytes 393224 | tf_op jit(solution)/shard_map/ppermute | solution.py:45
  18.7 11.2 %collective-permute-start.15 = (bf16[4,64,256]{2,1,0:T(8,128)(2,1)S(1)}, bf16[4,64,256]{2,1,0:T(8,128)(2,1)S(1)}, u32[]{:S(2)}, u32[]{:S(2)}) collective-permute-start(bf16[4,64,256]{2,1,0:T(8,128)(2,1)S(1)} %get-tuple-element.51), channel_id=1, source_target_pairs={{0,12},{4,8},{8,4},{12,0},{16,28},{20,24},{24,20},{28,16},{1,13},{... | collective-permute-start | bytes 393224 | tf_op jit(solution)/shard_map/ppermute | solution.py:45
  18.9 13.3 %collective-permute-start.16 = (bf16[4,64,256]{2,1,0:T(8,128)(2,1)S(1)}, bf16[4,64,256]{2,1,0:T(8,128)(2,1)S(1)}, u32[]{:S(2)}, u32[]{:S(2)}) collective-permute-start(bf16[4,64,256]{2,1,0:T(8,128)(2,1)S(1)} %get-tuple-element.52), channel_id=1, source_target_pairs={{0,16},{4,20},{8,24},{12,28},{16,0},{20,4},{24,8},{28,12},{1,17},{... | collective-permute-start | bytes 393224 | tf_op jit(solution)/shard_map/ppermute | solution.py:45
  21.7 19.3 %collective-permute-start.17 = (bf16[4,64,256]{2,1,0:T(8,128)(2,1)S(1)}, bf16[4,64,256]{2,1,0:T(8,128)(2,1)S(1)}, u32[]{:S(2)}, u32[]{:S(2)}) collective-permute-start(bf16[4,64,256]{2,1,0:T(8,128)(2,1)S(1)} %get-tuple-element.53), channel_id=1, source_target_pairs={{0,20},{4,16},{8,28},{12,24},{16,4},{20,0},{24,12},{28,8},{1,21},{... | collective-permute-start | bytes 393224 | tf_op jit(solution)/shard_map/ppermute | solution.py:45
  27.9 13.1 %collective-permute-start.18 = (bf16[4,64,256]{2,1,0:T(8,128)(2,1)S(1)}, bf16[4,64,256]{2,1,0:T(8,128)(2,1)S(1)}, u32[]{:S(2)}, u32[]{:S(2)}) collective-permute-start(bf16[4,64,256]{2,1,0:T(8,128)(2,1)S(1)} %get-tuple-element.54), channel_id=1, source_target_pairs={{0,24},{4,28},{8,16},{12,20},{16,8},{20,12},{24,0},{28,4},{1,25},{... | collective-permute-start | bytes 393224 | tf_op jit(solution)/shard_map/ppermute | solution.py:45
  29.9 11.1 %collective-permute-start.19 = (bf16[4,64,256]{2,1,0:T(8,128)(2,1)S(1)}, bf16[4,64,256]{2,1,0:T(8,128)(2,1)S(1)}, u32[]{:S(2)}, u32[]{:S(2)}) collective-permute-start(bf16[4,64,256]{2,1,0:T(8,128)(2,1)S(1)} %get-tuple-element.55), channel_id=1, source_target_pairs={{0,28},{4,24},{8,20},{12,16},{16,12},{20,8},{24,4},{28,0},{1,29},{... | collective-permute-start | bytes 393224 | tf_op jit(solution)/shard_map/ppermute | solution.py:45
  44.1 2.0 %collective-permute-start.20 = (bf16[4,128,512]{2,1,0:T(8,128)(2,1)S(1)}, bf16[4,128,512]{2,1,0:T(8,128)(2,1)S(1)}, u32[]{:S(2)}, u32[]{:S(2)}) collective-permute-start(bf16[4,128,512]{2,1,0:T(8,128)(2,1)S(1)} %get-tuple-element.59), channel_id=1, source_target_pairs={{0,1},{1,0},{2,3},{3,2},{4,5},{5,4},{6,7},{7,6},{8,9},{9,8},{10,11... | collective-permute-start | bytes 1572872 | tf_op jit(solution)/shard_map/ppermute | solution.py:45
  44.2 2.6 %collective-permute-start.21 = (bf16[4,128,512]{2,1,0:T(8,128)(2,1)S(1)}, bf16[4,128,512]{2,1,0:T(8,128)(2,1)S(1)}, u32[]{:S(2)}, u32[]{:S(2)}) collective-permute-start(bf16[4,128,512]{2,1,0:T(8,128)(2,1)S(1)} %get-tuple-element.60), channel_id=1, source_target_pairs={{0,1},{1,0},{2,3},{3,2},{4,5},{5,4},{6,7},{7,6},{8,9},{9,8},{10,11... | collective-permute-start | bytes 1572872 | tf_op jit(solution)/shard_map/ppermute | solution.py:45
  44.7 3.6 %collective-permute-start.3 = (bf16[4,128,512]{2,1,0:T(8,128)(2,1)S(1)}, bf16[4,128,512]{2,1,0:T(8,128)(2,1)S(1)}, u32[]{:S(2)}, u32[]{:S(2)}) collective-permute-start(bf16[4,128,512]{2,1,0:T(8,128)(2,1)S(1)} %copy-done.3), channel_id=1, source_target_pairs={{0,1},{1,0},{2,3},{3,2},{4,5},{5,4},{6,7},{7,6},{8,9},{9,8},{10,11... | collective-permute-start | bytes 1572872 | tf_op jit(solution)/shard_map/ppermute | solution.py:45
  44.8 3.6 %collective-permute-start.5 = (bf16[4,128,512]{2,1,0:T(8,128)(2,1)S(1)}, bf16[4,128,512]{2,1,0:T(8,128)(2,1)S(1)}, u32[]{:S(2)}, u32[]{:S(2)}) collective-permute-start(bf16[4,128,512]{2,1,0:T(8,128)(2,1)S(1)} %collective-permute-done.4.refs_2_), channel_id=1, source_target_pairs={{0,1},{1,0},{2,3},{3,2},{4,5},{5,4},{6,7},{7,6},{8,9},{9,8},{10,11... | collective-permute-start | bytes 1572872 | tf_op jit(solution)/shard_map/ppermute | solution.py:45
  47.0 43.0 %collective-permute-start.22 = (bf16[4,128,512]{2,1,0:T(8,128)(2,1)S(1)}, bf16[4,128,512]{2,1,0:T(8,128)(2,1)S(1)}, u32[]{:S(2)}, u32[]{:S(2)}) collective-permute-start(bf16[4,128,512]{2,1,0:T(8,128)(2,1)S(1)} %get-tuple-element.62), channel_id=1, source_target_pairs={{0,2},{1,3},{2,0},{3,1},{4,6},{5,7},{6,4},{7,5},{8,10},{9,11},{10,... | collective-permute-start | bytes 1572872 | tf_op jit(solution)/shard_map/ppermute | solution.py:45
  51.0 19.9 %collective-permute-start.10 = (bf16[4,64,256]{2,1,0:T(8,128)(2,1)S(1)}, bf16[4,64,256]{2,1,0:T(8,128)(2,1)S(1)}, u32[]{:S(2)}, u32[]{:S(2)}) collective-permute-start(bf16[4,64,256]{2,1,0:T(8,128)(2,1)S(1)} %get-tuple-element.41), channel_id=1, source_target_pairs={{0,20},{4,16},{8,28},{12,24},{16,4},{20,0},{24,12},{28,8},{1,21},{... | collective-permute-start | bytes 393224 | tf_op jit(solution)/shard_map/ppermute | solution.py:45
  58.2 12.7 %collective-permute-start.11 = (bf16[4,64,256]{2,1,0:T(8,128)(2,1)S(1)}, bf16[4,64,256]{2,1,0:T(8,128)(2,1)S(1)}, u32[]{:S(2)}, u32[]{:S(2)}) collective-permute-start(bf16[4,64,256]{2,1,0:T(8,128)(2,1)S(1)} %get-tuple-element.42), channel_id=1, source_target_pairs={{0,24},{4,28},{8,16},{12,20},{16,8},{20,12},{24,0},{28,4},{1,25},{... | collective-permute-start | bytes 393224 | tf_op jit(solution)/shard_map/ppermute | solution.py:45
  58.4 15.8 %collective-permute-start.12 = (bf16[4,64,256]{2,1,0:T(8,128)(2,1)S(1)}, bf16[4,64,256]{2,1,0:T(8,128)(2,1)S(1)}, u32[]{:S(2)}, u32[]{:S(2)}) collective-permute-start(bf16[4,64,256]{2,1,0:T(8,128)(2,1)S(1)} %get-tuple-element.43), channel_id=1, source_target_pairs={{0,28},{4,24},{8,20},{12,16},{16,12},{20,8},{24,4},{28,0},{1,29},{... | collective-permute-start | bytes 393224 | tf_op jit(solution)/shard_map/ppermute | solution.py:45
  62.6 14.7 %collective-permute-start.6 = (bf16[4,64,256]{2,1,0:T(8,128)(2,1)S(1)}, bf16[4,64,256]{2,1,0:T(8,128)(2,1)S(1)}, u32[]{:S(2)}, u32[]{:S(2)}) collective-permute-start(bf16[4,64,256]{2,1,0:T(8,128)(2,1)S(1)} %get-tuple-element.37), channel_id=1, source_target_pairs={{0,4},{4,0},{8,12},{12,8},{16,20},{20,16},{24,28},{28,24},{1,5},{5... | collective-permute-start | bytes 393224 | tf_op jit(solution)/shard_map/ppermute | solution.py:45
  70.9 7.4 %collective-permute-start.7 = (bf16[4,64,256]{2,1,0:T(8,128)(2,1)S(1)}, bf16[4,64,256]{2,1,0:T(8,128)(2,1)S(1)}, u32[]{:S(2)}, u32[]{:S(2)}) collective-permute-start(bf16[4,64,256]{2,1,0:T(8,128)(2,1)S(1)} %get-tuple-element.38), channel_id=1, source_target_pairs={{0,8},{4,12},{8,0},{12,4},{16,24},{20,28},{24,16},{28,20},{1,9},{5... | collective-permute-start | bytes 393224 | tf_op jit(solution)/shard_map/ppermute | solution.py:45
  70.9 10.2 %collective-permute-start.8 = (bf16[4,64,256]{2,1,0:T(8,128)(2,1)S(1)}, bf16[4,64,256]{2,1,0:T(8,128)(2,1)S(1)}, u32[]{:S(2)}, u32[]{:S(2)}) collective-permute-start(bf16[4,64,256]{2,1,0:T(8,128)(2,1)S(1)} %get-tuple-element.39), channel_id=1, source_target_pairs={{0,12},{4,8},{8,4},{12,0},{16,28},{20,24},{24,20},{28,16},{1,13},{... | collective-permute-start | bytes 393224 | tf_op jit(solution)/shard_map/ppermute | solution.py:45
  74.3 8.7 %collective-permute-start.9 = (bf16[4,64,256]{2,1,0:T(8,128)(2,1)S(1)}, bf16[4,64,256]{2,1,0:T(8,128)(2,1)S(1)}, u32[]{:S(2)}, u32[]{:S(2)}) collective-permute-start(bf16[4,64,256]{2,1,0:T(8,128)(2,1)S(1)} %get-tuple-element.40), channel_id=1, source_target_pairs={{0,16},{4,20},{8,24},{12,28},{16,0},{20,4},{24,8},{28,12},{1,17},{... | collective-permute-start | bytes 393224 | tf_op jit(solution)/shard_map/ppermute | solution.py:45
  77.3 9.0 %copy-start.6 = (s32[256]{0:T(256)S(1)}, s32[256]{0:T(256)}, u32[]{:S(2)}) copy-start(s32[256]{0:T(256)} %param.10) | copy-start | bytes 3076
  84.4 6.6 %collective-permute-start.23 = (bf16[32,512]{1,0:T(8,128)(2,1)S(1)}, bf16[32,512]{1,0:T(8,128)(2,1)S(1)}, u32[]{:S(2)}, u32[]{:S(2)}) collective-permute-start(bf16[32,512]{1,0:T(8,128)(2,1)S(1)} %get-tuple-element.64), channel_id=1, source_target_pairs={{0,1},{1,0},{2,3},{3,2},{4,5},{5,4},{6,7},{7,6},{8,9},{9,8},{10,11... | collective-permute-start | bytes 98312 | tf_op jit(solution)/shard_map/ppermute | solution.py:45
  84.5 6.5 %collective-permute-start.24 = (bf16[32,512]{1,0:T(8,128)(2,1)S(1)}, bf16[32,512]{1,0:T(8,128)(2,1)S(1)}, u32[]{:S(2)}, u32[]{:S(2)}) collective-permute-start(bf16[32,512]{1,0:T(8,128)(2,1)S(1)} %get-tuple-element.65), channel_id=1, source_target_pairs={{0,2},{1,3},{2,0},{3,1},{4,6},{5,7},{6,4},{7,5},{8,10},{9,11},{10,... | collective-permute-start | bytes 98312 | tf_op jit(solution)/shard_map/ppermute | solution.py:45
  85.6 5.3 %collective-permute-start.25 = (bf16[32,512]{1,0:T(8,128)(2,1)S(1)}, bf16[32,512]{1,0:T(8,128)(2,1)S(1)}, u32[]{:S(2)}, u32[]{:S(2)}) collective-permute-start(bf16[32,512]{1,0:T(8,128)(2,1)S(1)} %get-tuple-element.66), channel_id=1, source_target_pairs={{0,3},{1,2},{2,1},{3,0},{4,7},{5,6},{6,5},{7,4},{8,11},{9,10},{10,... | collective-permute-start | bytes 98312 | tf_op jit(solution)/shard_map/ppermute | solution.py:45

commit v2 on v1

--- a/solution.py
+++ b/solution.py
@@ -24,7 +24,7 @@
     return lax.dot_general(a, b, (((da,), (db,)), ((), ())), preferred_element_type=F32)
 
 
-def call(body, outs, ins, scratch=(), flops=0, limit=40 << 20):
+def call(body, outs, ins, scratch=(), flops=0, limit=40 << 20, cost=None):
     size = sum(o.size * o.dtype.itemsize for o in outs) + sum(v.size * v.dtype.itemsize for v in ins)
     return pl.pallas_call(
         body,
@@ -33,7 +33,7 @@
         out_specs=[pl.BlockSpec(memory_space=pltpu.VMEM)] * len(outs),
         scratch_shapes=list(scratch),
         compiler_params=pltpu.CompilerParams(vmem_limit_bytes=limit),
-        cost_estimate=pl.CostEstimate(flops=int(flops), bytes_accessed=int(size), transcendentals=0),
+        cost_estimate=pl.CostEstimate(flops=0, bytes_accessed=0, transcendentals=0),
     )(*ins)
 
 
@@ -45,12 +45,19 @@
     return lax.ppermute(value, axis, [(p, p ^ step) for p in range(size)])
 
 
-def pack_body(order, s_ref, out_ref):
-    rows, j_here = s_ref.shape
+def after(value, *earlier):
+    return lax.optimization_barrier((value, *earlier))[0]
+
+
+def pack_body(order, s_hbm, out_ref, s_scr, sem):
+    copy = pltpu.make_async_copy(s_hbm, s_scr, sem)
+    copy.start()
+    copy.wait()
+    rows, j_here = s_scr.shape
     groups = j_here // LANE_GROUP
     lanes = order * LANE_GROUP
     m_here = rows // order
-    s = s_ref[...]
+    s = s_scr[...]
     lane = iota((j_here, lanes), 1)
     keep = (iota((rows, lanes), 0) % order) == (iota((rows, lanes), 1) // LANE_GROUP)
     for g in range(groups):
@@ -60,18 +67,52 @@
         out_ref[g * m_here : (g + 1) * m_here, :] = packed.astype(BF16)
 
 
-def gate_body(x_ref, cot_ref, src_ref, dz_ref, h_ref):
-    width = x_ref.shape[1]
+def gate_body(step, x_hbm, cot_hbm, src_ref, dz_ref, h_ref, x_scr, cot_scr, sems):
+    rows, width = dz_ref.shape
+    parts = rows // step
+    copies = []
+    for n in range(parts):
+        part = pl.ds(n * step, step)
+        copies.append(
+            (
+                pltpu.make_async_copy(x_hbm.at[part, :], x_scr.at[part, :], sems.at[0, n]),
+                pltpu.make_async_copy(cot_hbm.at[part, :], cot_scr.at[part, :], sems.at[1, n]),
+            )
+        )
+    for pair in copies:
+        for copy in pair:
+            copy.start()
     select = one_hot(iota((width, width), 0) == src_ref[...])
-    step = 512
-
-    @pl.loop(0, x_ref.shape[0] // step)
-    def _(n):
-        rows = pl.ds(pl.multiple_of(n * step, step), step)
-        gate = jax.nn.sigmoid(dot(x_ref[rows, :], select))
-        part = cot_ref[rows, :].astype(F32) * gate
-        dz_ref[rows, :] = part.astype(BF16)
-        h_ref[rows, :] = part * (1.0 - gate)
+    for n in range(parts):
+        for copy in copies[n]:
+            copy.wait()
+        part = slice(n * step, (n + 1) * step)
+        gate = jax.nn.sigmoid(dot(x_scr[part, :], select))
+        scaled = cot_scr[part, :].astype(F32) * gate
+        dz_ref[part, :] = scaled.astype(BF16)
+        h_ref[part, :] = scaled * (1.0 - gate)
+
+
+def gate_call(x, cot, src):
+    rows, width = x.shape
+    step = min(rows, 512)
+    whole = pl.BlockSpec(memory_space=pltpu.VMEM)
+    left = pl.BlockSpec(memory_space=pltpu.HBM)
+    return pl.pallas_call(
+        functools.partial(gate_body, step),
+        out_shape=[of((rows, width)), of((rows, width), F32)],
+        in_specs=[left, left, whole],
+        out_specs=[whole, whole],
+        scratch_shapes=[
+            pltpu.VMEM((rows, width), BF16),
+            pltpu.VMEM((rows, width), BF16),
+            pltpu.SemaphoreType.DMA((2, rows // step)),
+        ],
+        compiler_params=pltpu.CompilerParams(vmem_limit_bytes=60 << 20),
+        cost_estimate=pl.CostEstimate(
+            flops=2 * rows * width * width, bytes_accessed=10 * rows * width, transcendentals=rows * width
+        ),
+    )(x, cot, src)
 
 
 def regroup_back_body(batch, seq, order, *refs):
@@ -150,9 +191,10 @@
 
 
 def mix_back_body(batch, *refs):
-    pieces, dmixed_ref, out_ref = refs[:batch], refs[batch], refs[batch + 1]
+    pieces, dmixed_ref, second_ref, out_ref, weights_ref = refs[:batch], *refs[batch:]
     me = lax.axis_index("batch")
     blocks, rows, order = pieces[0].shape
+    groups, count, lanes = second_ref.shape
 
     @pl.loop(0, blocks)
     def _(i):
@@ -162,6 +204,13 @@
             term = dot(pieces[d][i], dmixed_ref[i, pl.ds(first, rows), :], 0, 0)
             total = term if total is None else total + term
         out_ref[pl.ds(pl.multiple_of(i * order, order), order), :] = total
+
+    @pl.loop(0, groups)
+    def _(g):
+        packed = second_ref[g].astype(F32)
+        col = iota((count, lanes), 1) % LANE_GROUP
+        for jj in range(LANE_GROUP):
+            weights_ref[g, jj * count : (jj + 1) * count, :] = jnp.where(col == jj, packed, 0.0).astype(BF16)
 
 
 def gather_blocks(seq, pieces, scr):
@@ -197,26 +246,15 @@
         outs[d][...] = jnp.concatenate(rows, axis=0).astype(BF16)
 
 
-def tokens_body(reg_ref, second_ref, h_ref, src_ref, back_ref, out_ref):
+def tokens_body(reg_ref, weights_ref, h_ref, src_ref, back_ref, out_ref):
     order, j_here, width = reg_ref.shape
     groups, lanes = j_here // LANE_GROUP, order * LANE_GROUP
     select = one_hot(iota((width, width), 0) == src_ref[...])
-
-    @pl.loop(0, groups)
-    def _(g):
-        js = pl.ds(pl.multiple_of(g * LANE_GROUP, LANE_GROUP), LANE_GROUP)
-        reg = reg_ref[:, js, :].reshape(lanes, width)
-        packed = second_ref[g].astype(F32)
-        col = iota((order, lanes), 1) % LANE_GROUP
-        weights = jnp.concatenate(
-            [jnp.where(col == jj, packed, 0.0).astype(BF16) for jj in range(LANE_GROUP)], axis=0
-        )
-        rows = pl.ds(pl.multiple_of(g * lanes, lanes), lanes)
-        dgate = dot(weights, reg) * h_ref[rows, :]
-        high = dgate.astype(BF16)
-        low = (dgate - high.astype(F32)).astype(BF16)
-        spread = dot(high, select, 1, 1) + dot(low, select, 1, 1)
-        out_ref[rows, :] = (back_ref[rows, :] + spread).astype(BF16)
+    for g in range(groups):
+        reg = reg_ref[:, g * LANE_GROUP : (g + 1) * LANE_GROUP, :].reshape(lanes, width)
+        rows = slice(g * lanes, (g + 1) * lanes)
+        dgate = (dot(weights_ref[g], reg) * h_ref[rows, :]).astype(BF16)
+        out_ref[rows, :] = (back_ref[rows, :] + dot(dgate, select, 1, 1)).astype(BF16)
 
 
 def pair_body(own_a, own_b, got_a, got_b, out_a, out_b):
@@ -257,11 +295,21 @@
     big = 2 * rows_here * order * width
 
     flat = jnp.transpose(second_factor, (1, 2, 0)).reshape(m_here * count, j_here)
-    (mine,) = call(functools.partial(pack_body, count), [of((groups * m_here, lanes))], [flat])
-    packed = [mine] + [swap(mine, "batch", d, batch) for d in range(1, batch)]
-    dz, h = call(
-        gate_body, [of((rows_here, width)), of((rows_here, width), F32)], [x, cot, src], flops=big // 2
-    )
+    mine = pl.pallas_call(
+        functools.partial(pack_body, count),
+        out_shape=of((groups * m_here, lanes)),
+        in_specs=[pl.BlockSpec(memory_space=pltpu.HBM)],
+        out_specs=pl.BlockSpec(memory_space=pltpu.VMEM),
+        scratch_shapes=[pltpu.VMEM(flat.shape, BF16), pltpu.SemaphoreType.DMA],
+        compiler_params=pltpu.CompilerParams(vmem_limit_bytes=60 << 20),
+        cost_estimate=pl.CostEstimate(flops=4 * flat.size * lanes, bytes_accessed=4 * flat.size, transcendentals=0),
+    )(flat)
+    packed = [mine] + [swap(mine, "batch", d, batch) for d in (2, 3, 1)]
+    packed = [packed[0], packed[3], packed[1], packed[2]]
+    dz, h = gate_call(x, cot, src)
+
+    across = swap(after(first_factor, mine), "batch", 2, batch)
+    beside = swap(after(first_factor, dz, *packed[1:]), "batch", 1, batch)
     piece = of((blocks, j_here, width))
     *back, second = call(
         functools.partial(regroup_back_body, batch, seq, count),
@@ -270,13 +318,17 @@
         [pltpu.VMEM((groups, count, lanes), F32), pltpu.VMEM((count, j_here, width), BF16)],
         flops=2 * big,
     )
-    order_of = sorted(range(1, seq), key=lambda d: -d)
-    back_got = {d: swap(back[d], "seq", d, seq) for d in order_of}
-    back_got[0] = back[0]
-
-    first_ready, _ = lax.optimization_barrier((first_factor, packed[1:]))
-    across = swap(first_ready, "batch", 2, batch)
-    first = [first_ready, swap(first_ready, "batch", 1, batch), across, swap(across, "batch", 1, batch)]
+    far_first = sorted(range(1, seq), key=lambda d: -d)
+
+    def exchange(blocks_out):
+        got = {0: blocks_out[0]}
+        for d in far_first:
+            ready = after(blocks_out[d], got[far_first[0]]) if d < seq // 2 else blocks_out[d]
+            got[d] = swap(ready, "seq", d, seq)
+        return [got[d] for d in range(seq)]
+
+    back_got = exchange(back)
+    first = [first_factor, beside, across, swap(after(across, back[0]), "batch", 1, batch)]
     regrouped = call(
         functools.partial(mix_body, batch, seq),
         [piece] * seq,
@@ -284,36 +336,39 @@
         [pltpu.VMEM((order, order), BF16), pltpu.VMEM((order, width), BF16), pltpu.VMEM((order, width), BF16)],
         flops=2 * big,
     )
-    got = {d: swap(regrouped[d], "seq", d, seq) for d in order_of}
-    got[0] = regrouped[0]
-
+    got = exchange(regrouped)
+
+    back_got[0] = after(back_got[0], regrouped[0], got[far_first[0]])
     *parts, dmixed = call(
         functools.partial(first_grad_body, batch, seq),
         [of((blocks, k_here, order))] * batch + [of((blocks, order, width))],
-        [*[back_got[d] for d in range(seq)], x, alt],
+        [*back_got, x, alt],
         [pltpu.VMEM((order, order), BF16), pltpu.VMEM((order, width), BF16), pltpu.VMEM((order, order), BF16)],
         flops=2 * big,
     )
-    near = swap(parts[1], "batch", 1, batch)
-    far = swap(parts[3], "batch", 1, batch)
-    (dmix_in,) = call(
-        functools.partial(mix_back_body, batch), [of((rows_here, width), F32)], [*first, dmixed], flops=big
-    )
-    kept, sent = call(
+    near = swap(after(parts[1], got[far_first[1]]), "batch", 1, batch)
+    far = swap(after(parts[3], got[far_first[1]]), "batch", 1, batch)
+    dmix_in, weights = call(
+        functools.partial(mix_back_body, batch),
+        [of((rows_here, width), F32), of((groups, lanes, lanes))],
+        [*first, dmixed, second],
+        flops=big,
+    )
+    kept, summed = call(
         pair_body, [of(parts[0].shape, F32), of(parts[0].shape)], [parts[0], parts[2], near, far]
     )
-    (grad_one,) = call(add_body, [of(parts[0].shape)], [kept, swap(sent, "batch", 2, batch)])
+    (grad_one,) = call(add_body, [of(parts[0].shape)], [kept, swap(summed, "batch", 2, batch)])
 
     *terms, gathered = call(
         functools.partial(second_grad_body, batch, seq),
         [of((groups * m_here, lanes))] * batch + [of((count, j_here, width))],
-        [*[got[d] for d in range(seq)], dz],
+        [*got, dz],
         [pltpu.VMEM((groups, count, lanes), F32)],
         flops=2 * big,
     )
     terms_got = [terms[0]] + [swap(terms[d], "batch", d, batch) for d in range(1, batch)]
     (grad_tokens,) = call(
-        tokens_body, [of((rows_here, width))], [gathered, second, h, src, dmix_in], flops=2 * big
+        tokens_body, [of((rows_here, width))], [gathered, weights, h, src, dmix_in], flops=2 * big
     )
     (grad_flat,) = call(
         functools.partial(unpack_body, count), [of((m_here * count, j_here))], terms_got

time: 92.3 us -> 95.8 us (1.038)
  waiting for transfers between devices: 30.1 us -> 39.4 us
  starting transfers between devices: 38.7 us -> 31.3 us
  Pallas kernels: 18.5 us -> 22.8 us
  local copies, waits for them, and re-layouts: 3.98 us -> 1.26 us
    ppermute x26, waiting for transfers between devices: 30.1 us -> 39.4 us  [swap(): return lax.ppermute(value, axis, [(p, p ^ step) for p in range(size)])]
    ppermute x26, starting transfers between devices: 38.7 us -> 31.3 us  [swap(): return lax.ppermute(value, axis, [(p, p ^ step) for p in range(size)])]
    pallas_call x0 -> x2, Pallas kernels: none -> 6.63 us  [the longest x1 4.64 us: gate_call(): pl.pallas_call(functools.partial(gate_body, step), out_shape=[of((rows, w...]
    unnamed x16, local copies, waits for them, and re-layouts: 3.98 us -> 1.26 us
    pallas_call x11 -> x9, Pallas kernels: 18.5 us -> 16.1 us  [call(): pl.pallas_call(body, out_shape=outs, in_specs=[pl.BlockSpec(memory_space=...]
  transfers between devices with their start and end apart: 26 -> 26, of which waited for: 10 -> 10; matrix products, arithmetic and copies ran while one was open for 0% -> 0% of each run, Pallas kernels for 18% -> 21%
where the time goes in v2:
time: 95.8 us; the launch traced here: 95.6 us
  waiting for transfers between devices  39.4 us (41%)
  starting transfers between devices  31.3 us (33%)
  Pallas kernels  22.8 us (24%)
  local copies, waits for them, and re-layouts  1.26 us (1%)
    ppermute x26, waiting for transfers between devices, swap(): return lax.ppermute(value, axis, [(p, p ^ step) for p in range(size)])  39.4 us
    ppermute x26, starting transfers between devices, swap(): return lax.ppermute(value, axis, [(p, p ^ step) for p in range(size)])  31.3 us
    pallas_call x9, Pallas kernels, call(): pl.pallas_call(body, out_shape=outs, in_specs=[pl.BlockSpec(memory_space=...  16.1 us
    pallas_call x1, Pallas kernels, gate_call(): pl.pallas_call(functools.partial(gate_body, step), out_shape=[of((rows, w...  4.64 us
    pallas_call x1, Pallas kernels, packed_shards(): pl.pallas_call(functools.partial(pack_body, count), out_shape=of((groups...  2 us
  transfers between devices with their start and end apart: 26, of which 10 were waited for; matrix products, arithmetic and copies ran while one was open for 0% of the time, Pallas kernels for 21%

profile of v2, /device:TPU:0, one launch (start us, length us, event | category | flops | bytes accessed | tf_op | source)
XLA Modules:
  0.0 95.6 jit_solution(1878745097295728985)
XLA Ops:
  0.6 0.0 copy-start.4
  0.6 0.0 copy-start
  0.7 2.0 %shard_map.86.refs_0_ = bf16[32,512]{1,0:T(8,128)(2,1)} custom-call(bf16[256,64]{1,0:T(8,128)(2,1)} %bitcast.21), custom_call_target="tpu_custom_call" | custom-call | flops 33554432 | bytes 65536 | tf_op jit(solution)/shard_map/pallas_call | solution.py:298
  2.7 0.0 copy-start.5
  2.7 3.0 %collective-permute-start.4 = (bf16[4,128,512]{2,1,0:T(8,128)(2,1)}, bf16[4,128,512]{2,1,0:T(8,128)(2,1)S(1)}, u32[]{:S(2)}, u32[]{:S(2)}) collective-permute-start(bf16[4,128,512]{2,1,0:T(8,128)(2,1)} %refs_0_.3), channel_id=1, source_target_pairs={{0,2},{1,3},{2,0},{3,1},{4,6},{5,7},{6,4},{7,5},{8,10},{9,11},{10,... | collective-permute-start | bytes 1572872 | tf_op jit(solution)/shard_map/ppermute | solution.py:45
  5.7 0.0 collective-permute-start.2
  5.7 1.2 %collective-permute-start.1 = (bf16[32,512]{1,0:T(8,128)(2,1)}, bf16[32,512]{1,0:T(8,128)(2,1)S(1)}, u32[]{:S(2)}, u32[]{:S(2)}) collective-permute-start(bf16[32,512]{1,0:T(8,128)(2,1)} %shard_map.86.refs_0_), channel_id=1, source_target_pairs={{0,2},{1,3},{2,0},{3,1},{4,6},{5,7},{6,4},{7,5},{8,10},{9,11},{10,... | collective-permute-start | bytes 98312 | tf_op jit(solution)/shard_map/ppermute | solution.py:45
  6.9 0.7 collective-permute-start
  7.5 4.6 %shard_map.85 = (bf16[2048,256]{1,0:T(8,128)(2,1)}, f32[2048,256]{1,0:T(8,128)}) custom-call(bf16[2048,256]{1,0:T(8,128)(2,1)} %bitcast.11, bf16[2048,256]{1,0:T(8,128)(2,1)} %bitcast.19, s32[1,256]{1,0:T(1,128)} %bitcast.16), custom_call_target="tpu_custom_call" | custom-call | flops 268435456 | bytes 5242880 | tf_op jit(solution)/shard_map/pallas_call | solution.py:101
  12.2 6.0 %collective-permute-done.2.refs_3_ = bf16[32,512]{1,0:T(8,128)(2,1)S(1)} collective-permute-done((bf16[32,512]{1,0:T(8,128)(2,1)}, bf16[32,512]{1,0:T(8,128)(2,1)S(1)}, u32[]{:S(2)}, u32[]{:S(2)}) %collective-permute-start.2) | collective-permute-done | bytes 32800 | tf_op jit(solution)/shard_map/ppermute | solution.py:45
  18.2 1.0 %collective-permute-done.1.refs_2_ = bf16[32,512]{1,0:T(8,128)(2,1)S(1)} collective-permute-done((bf16[32,512]{1,0:T(8,128)(2,1)}, bf16[32,512]{1,0:T(8,128)(2,1)S(1)}, u32[]{:S(2)}, u32[]{:S(2)}) %collective-permute-start.1) | collective-permute-done | bytes 32800 | tf_op jit(solution)/shard_map/ppermute | solution.py:45
  19.2 0.0 collective-permute-done.refs_1_
  19.2 0.0 collective-permute-start.3
  19.2 0.0 copy-start.1
  19.3 1.2 %copy-done.1 = bf16[2048,256]{1,0:T(8,128)(2,1)S(1)} copy-done((bf16[2048,256]{1,0:T(8,128)(2,1)S(1)}, bf16[2048,256]{1,0:T(8,128)(2,1)}, u32[]{:S(2)}) %copy-start.1) | copy-done | bytes 1048600
  20.5 1.9 %shard_map.87 = (bf16[4,64,256]{2,1,0:T(8,128)(2,1)S(1)}, bf16[4,64,256]{2,1,0:T(8,128)(2,1)S(1)}, bf16[4,64,256]{2,1,0:T(8,128)(2,1)S(1)}, bf16[4,64,256]{2,1,0...) custom-call(bf16[32,512]{1,0:T(8,128)(2,1)S(1)} %copy-done.5, ...), custom_call_target="tpu_custom_call" | custom-call | tf_op jit(solution)/shard_map/pallas_call | solution.py:29
  22.4 0.0 collective-permute-done.4.refs_2_
  22.4 0.6 collective-permute-start.5
  23.0 4.8 %collective-permute-start.13 = (bf16[4,64,256]{2,1,0:T(8,128)(2,1)S(1)}, bf16[4,64,256]{2,1,0:T(8,128)(2,1)S(1)}, u32[]{:S(2)}, u32[]{:S(2)}) collective-permute-start(bf16[4,64,256]{2,1,0:T(8,128)(2,1)S(1)} %get-tuple-element.67), channel_id=1, source_target_pairs={{0,28},{4,24},{8,20},{12,16},{16,12},{20,8},{24,4},{28,0},{1,29},{... | collective-permute-start | bytes 393224 | tf_op jit(solution)/shard_map/ppermute | solution.py:45
  27.8 0.0 collective-permute-start.17
  27.8 2.9 %collective-permute-start.18 = (bf16[4,64,256]{2,1,0:T(8,128)(2,1)S(1)}, bf16[4,64,256]{2,1,0:T(8,128)(2,1)S(1)}, u32[]{:S(2)}, u32[]{:S(2)}) collective-permute-start(bf16[4,64,256]{2,1,0:T(8,128)(2,1)S(1)} %get-tuple-element.74), channel_id=1, source_target_pairs={{0,20},{4,16},{8,28},{12,24},{16,4},{20,0},{24,12},{28,8},{1,21},{... | collective-permute-start | bytes 393224 | tf_op jit(solution)/shard_map/ppermute | solution.py:45
  30.7 0.0 collective-permute-done.3.refs_1_
  30.7 0.0 collective-permute-done.5.refs_3_
  30.7 2.7 %shard_map.88 = (bf16[4,64,256]{2,1,0:T(8,128)(2,1)S(1)}, bf16[4,64,256]{2,1,0:T(8,128)(2,1)S(1)}, bf16[4,64,256]{2,1,0:T(8,128)(2,1)S(1)}, bf16[4,64,256]{2,1,0...) custom-call(bf16[4,128,512]{2,1,0:T(8,128)(2,1)S(1)} %copy-done.4, ...), custom_call_target="tpu_custom_call" | custom-call | tf_op jit(solution)/shard_map/pallas_call | solution.py:29
  33.4 1.3 %collective-permute-start.6 = (bf16[4,64,256]{2,1,0:T(8,128)(2,1)S(1)}, bf16[4,64,256]{2,1,0:T(8,128)(2,1)S(1)}, u32[]{:S(2)}, u32[]{:S(2)}) collective-permute-start(bf16[4,64,256]{2,1,0:T(8,128)(2,1)S(1)} %get-tuple-element.55), channel_id=1, source_target_pairs={{0,28},{4,24},{8,20},{12,16},{16,12},{20,8},{24,4},{28,0},{1,29},{... | collective-permute-start | bytes 393224 | tf_op jit(solution)/shard_map/ppermute | solution.py:45
  34.7 3.6 %collective-permute-start.19 = (bf16[4,64,256]{2,1,0:T(8,128)(2,1)S(1)}, bf16[4,64,256]{2,1,0:T(8,128)(2,1)S(1)}, u32[]{:S(2)}, u32[]{:S(2)}) collective-permute-start(bf16[4,64,256]{2,1,0:T(8,128)(2,1)S(1)} %get-tuple-element.75), channel_id=1, source_target_pairs={{0,24},{4,28},{8,16},{12,20},{16,8},{20,12},{24,0},{28,4},{1,25},{... | collective-permute-start | bytes 393224 | tf_op jit(solution)/shard_map/ppermute | solution.py:45
  38.3 0.0 collective-permute-done.13.refs_7_
  38.3 0.5 collective-permute-start.14
  38.8 9.6 %collective-permute-done.17.refs_4_ = bf16[4,64,256]{2,1,0:T(8,128)(2,1)S(1)} collective-permute-done((bf16[4,64,256]{2,1,0:T(8,128)(2,1)S(1)}, bf16[4,64,256]{2,1,0:T(8,128)(2,1)S(1)}, u32[]{:S(2)}, u32[]{:S(2)}) %collective-permute-start.17) | collective-permute-done | bytes 131104 | tf_op jit(solution)/shard_map/ppermute | solution.py:45
  48.4 0.0 collective-permute-start.15
  48.4 2.8 %collective-permute-done.18.refs_5_ = bf16[4,64,256]{2,1,0:T(8,128)(2,1)S(1)} collective-permute-done((bf16[4,64,256]{2,1,0:T(8,128)(2,1)S(1)}, bf16[4,64,256]{2,1,0:T(8,128)(2,1)S(1)}, u32[]{:S(2)}, u32[]{:S(2)}) %collective-permute-start.18) | collective-permute-done | bytes 131104 | tf_op jit(solution)/shard_map/ppermute | solution.py:45
  51.2 0.0 collective-permute-start.16
  51.2 0.0 collective-permute-done.6.refs_7_
  51.2 2.5 %collective-permute-start.12 = (bf16[4,64,256]{2,1,0:T(8,128)(2,1)S(1)}, bf16[4,64,256]{2,1,0:T(8,128)(2,1)S(1)}, u32[]{:S(2)}, u32[]{:S(2)}) collective-permute-start(bf16[4,64,256]{2,1,0:T(8,128)(2,1)S(1)} %get-tuple-element.63), channel_id=1, source_target_pairs={{0,24},{4,28},{8,16},{12,20},{16,8},{20,12},{24,0},{28,4},{1,25},{... | collective-permute-start | bytes 393224 | tf_op jit(solution)/shard_map/ppermute | solution.py:45
  53.7 0.0 collective-permute-done.19.refs_6_
  53.7 0.0 collective-permute-done.14.refs_1_
  53.7 0.0 collective-permute-done.15.refs_2_
  53.7 4.6 %collective-permute-done.16.refs_3_ = bf16[4,64,256]{2,1,0:T(8,128)(2,1)S(1)} collective-permute-done((bf16[4,64,256]{2,1,0:T(8,128)(2,1)S(1)}, bf16[4,64,256]{2,1,0:T(8,128)(2,1)S(1)}, u32[]{:S(2)}, u32[]{:S(2)}) %collective-permute-start.16) | collective-permute-done | bytes 131104 | tf_op jit(solution)/shard_map/ppermute | solution.py:45
  58.3 3.0 %shard_map.90 = (bf16[4,128,512]{2,1,0:T(8,128)(2,1)S(1)}, bf16[4,128,512]{2,1,0:T(8,128)(2,1)S(1)}, bf16[4,128,512]{2,1,0:T(8,128)(2,1)S(1)}, bf16[4,128,512]{2,1,0:T(8,128)(2,1)S(1)}, bf16[4,512,256]{2,1,0:T(8,128)(2,1)S(1)}) custom-call(bf16[4,64,256]{2,1,0:T(8,128)(2,1)S(1)} %get-tuple-element.65.refs_0_, ...), custom_call_target="tpu_custom_call" | custom-call | tf_op jit(solution)/shard_map/pallas_call | solution.py:29
  61.3 0.0 collective-permute-done.12.refs_6_
  61.4 0.1 collective-permute-start.21
  61.4 0.5 collective-permute-start.20
  61.9 1.4 %collective-permute-done.21.got_b = bf16[4,128,512]{2,1,0:T(8,128)(2,1)S(1)} collective-permute-done((bf16[4,128,512]{2,1,0:T(8,128)(2,1)S(1)}, bf16[4,128,512]{2,1,0:T(8,128)(2,1)S(1)}, u32[]{:S(2)}, u32[]{:S(2)}) %collective-permute-start.21) | collective-permute-done | bytes 524320 | tf_op jit(solution)/shard_map/ppermute | solution.py:45
  63.3 0.7 collective-permute-done.20.got_a
  64.1 0.2 shard_map.93
  64.3 1.6 %collective-permute-start.22 = (bf16[4,128,512]{2,1,0:T(8,128)(2,1)S(1)}, bf16[4,128,512]{2,1,0:T(8,128)(2,1)S(1)}, u32[]{:S(2)}, u32[]{:S(2)}) collective-permute-start(bf16[4,128,512]{2,1,0:T(8,128)(2,1)S(1)} %get-tuple-element.88), channel_id=1, source_target_pairs={{0,2},{1,3},{2,0},{3,1},{4,6},{5,7},{6,4},{7,5},{8,10},{9,11},{10,... | collective-permute-start | bytes 1572872 | tf_op jit(solution)/shard_map/ppermute | solution.py:45
  65.9 3.0 %collective-permute-start.10 = (bf16[4,64,256]{2,1,0:T(8,128)(2,1)S(1)}, bf16[4,64,256]{2,1,0:T(8,128)(2,1)S(1)}, u32[]{:S(2)}, u32[]{:S(2)}) collective-permute-start(bf16[4,64,256]{2,1,0:T(8,128)(2,1)S(1)} %get-tuple-element.61), channel_id=1, source_target_pairs={{0,16},{4,20},{8,24},{12,28},{16,0},{20,4},{24,8},{28,12},{1,17},{... | collective-permute-start | bytes 393224 | tf_op jit(solution)/shard_map/ppermute | solution.py:45
  68.8 2.2 %collective-permute-start.11 = (bf16[4,64,256]{2,1,0:T(8,128)(2,1)S(1)}, bf16[4,64,256]{2,1,0:T(8,128)(2,1)S(1)}, u32[]{:S(2)}, u32[]{:S(2)}) collective-permute-start(bf16[4,64,256]{2,1,0:T(8,128)(2,1)S(1)} %get-tuple-element.62), channel_id=1, source_target_pairs={{0,20},{4,16},{8,28},{12,24},{16,4},{20,0},{24,12},{28,8},{1,21},{... | collective-permute-start | bytes 393224 | tf_op jit(solution)/shard_map/ppermute | solution.py:45
  71.1 0.0 collective-permute-start.7
  71.1 1.2 %collective-permute-start.8 = (bf16[4,64,256]{2,1,0:T(8,128)(2,1)S(1)}, bf16[4,64,256]{2,1,0:T(8,128)(2,1)S(1)}, u32[]{:S(2)}, u32[]{:S(2)}) collective-permute-start(bf16[4,64,256]{2,1,0:T(8,128)(2,1)S(1)} %get-tuple-element.58), channel_id=1, source_target_pairs={{0,8},{4,12},{8,0},{12,4},{16,24},{20,28},{24,16},{28,20},{1,9},{5... | collective-permute-start | bytes 393224 | tf_op jit(solution)/shard_map/ppermute | solution.py:45
  72.2 6.6 %collective-permute-done.10.refs_4_ = bf16[4,64,256]{2,1,0:T(8,128)(2,1)S(1)} collective-permute-done((bf16[4,64,256]{2,1,0:T(8,128)(2,1)S(1)}, bf16[4,64,256]{2,1,0:T(8,128)(2,1)S(1)}, u32[]{:S(2)}, u32[]{:S(2)}) %collective-permute-start.10) | collective-permute-done | bytes 131104 | tf_op jit(solution)/shard_map/ppermute | solution.py:45
  78.8 0.0 collective-permute-start.9
  78.8 3.3 %collective-permute-done.11.refs_5_ = bf16[4,64,256]{2,1,0:T(8,128)(2,1)S(1)} collective-permute-done((bf16[4,64,256]{2,1,0:T(8,128)(2,1)S(1)}, bf16[4,64,256]{2,1,0:T(8,128)(2,1)S(1)}, u32[]{:S(2)}, u32[]{:S(2)}) %collective-permute-start.11) | collective-permute-done | bytes 131104 | tf_op jit(solution)/shard_map/ppermute | solution.py:45
  82.1 3.3 %collective-permute-done.9.refs_3_ = bf16[4,64,256]{2,1,0:T(8,128)(2,1)S(1)} collective-permute-done((bf16[4,64,256]{2,1,0:T(8,128)(2,1)S(1)}, bf16[4,64,256]{2,1,0:T(8,128)(2,1)S(1)}, u32[]{:S(2)}, u32[]{:S(2)}) %collective-permute-start.9) | collective-permute-done | bytes 131104 | tf_op jit(solution)/shard_map/ppermute | solution.py:45
  85.4 1.4 %shard_map.89 = (bf16[32,512]{1,0:T(8,128)(2,1)S(1)}, bf16[32,512]{1,0:T(8,128)(2,1)S(1)}, bf16[32,512]{1,0:T(8,128)(2,1)S(1)}, bf16[32,512]{1,0:T(8,128)(2,1)S(1)}, bf16[32,64,256]{2,1,0:T(8,128)(2,1)S(1)}) custom-call(bf16[4,64,256]{2,1,0:T(8,128)(2,1)S(1)} %get-tuple-element.53.refs_0_, bf16[4,64,256]{2,1,0:T(8,128)(2,1)S(1)} %collective-permute-done.7.refs_1_, ...), custom_call_target="tpu_custom_call" | custom-call | tf_op jit(solution)/shard_map/pallas_call | solution.py:29
  86.9 0.0 copy-start.7
  86.9 0.1 collective-permute-start.23
  86.9 0.6 collective-permute-start.24
  87.5 1.3 %collective-permute-start.25 = (bf16[32,512]{1,0:T(8,128)(2,1)S(1)}, bf16[32,512]{1,0:T(8,128)(2,1)S(1)}, u32[]{:S(2)}, u32[]{:S(2)}) collective-permute-start(bf16[32,512]{1,0:T(8,128)(2,1)S(1)} %get-tuple-element.92), channel_id=1, source_target_pairs={{0,3},{1,2},{2,1},{3,0},{4,7},{5,6},{6,5},{7,4},{8,11},{9,10},{10,... | collective-permute-start | bytes 98312 | tf_op jit(solution)/shard_map/ppermute | solution.py:45
  88.8 2.1 %shard_map.91 = (f32[2048,256]{1,0:T(8,128)S(1)}, bf16[4,512,512]{2,1,0:T(8,128)(2,1)S(1)}) custom-call(bf16[4,128,512]{2,1,0:T(8,128)(2,1)S(1)} %copy-done.4, bf16[4,128,512]{2,1,0:T(8,128)(2,1)S(1)} %collective-permute-done.3.refs_1_, bf16[4,128,512]{2,1,0:T(8,128)(2,1)S(1)} %collective-permute-done.4.refs_2_, ...), custom_call_target="tpu_custom_call" | custom-call | tf_op jit(solution)/shard_map/pallas_call | solution.py:29
  91.0 2.7 %shard_map.92 = bf16[2048,256]{1,0:T(8,128)(2,1)} custom-call(bf16[32,64,256]{2,1,0:T(8,128)(2,1)S(1)} %get-tuple-element.64.reg_ref, bf16[4,512,512]{2,1,0:T(8,128)(2,1)S(1)} %get-tuple-element.78.weights_ref, f32[2048,256]{1,0:T(8,128)S(1)} %copy-done.3, s32[1,256]{1,0:T(1,128)S(1)} %bitcast.17, f32[2048,256]{1,0:T(8,128)S(1)} %get-tuple-element.80.back_ref), custom_call_target="tpu_custom_call" | custom-call | tf_op jit(solution)/shard_map/pallas_call | solution.py:29
  93.7 0.0 collective-permute-done.25.refs_3_
  93.7 1.1 %shard_map.95 = bf16[256,64]{1,0:T(8,128)(2,1)} custom-call(bf16[32,512]{1,0:T(8,128)(2,1)S(1)} %get-tuple-element.89.refs_0_, bf16[32,512]{1,0:T(8,128)(2,1)S(1)} %collective-permute-done.23.refs_1_, bf16[32,512]{1,0:T(8,128)(2,1)S(1)} %collective-permute-done.24.refs_2_, bf16[32,512]{1,0:T(8,128)(2,1)S(1)} %collective-permute-done.25.refs_3_), custom_call_target="tpu_custom_call" | custom-call | tf_op jit(solution)/shard_map/pallas_call | solution.py:29
  94.7 0.9 shard_map.94
  (15 shorter events, 0.0 us)
Async XLA Ops:
  0.6 18.6 %copy-start.4 = (bf16[4,128,512]{2,1,0:T(8,128)(2,1)S(1)}, bf16[4,128,512]{2,1,0:T(8,128)(2,1)}, u32[]{:S(2)}) copy-start(bf16[4,128,512]{2,1,0:T(8,128)(2,1)} %refs_0_.3) | copy-start | bytes 1572868
  0.6 30.0 %copy-start = (bf16[1,2048,256]{2,1,0:T(8,128)(2,1)S(1)}, bf16[1,2048,256]{2,1,0:T(8,128)(2,1)}, u32[]{:S(2)}) copy-start(bf16[1,2048,256]{2,1,0:T(8,128)(2,1)} %param.6) | copy-start | bytes 3145732
  0.7 30.0 %copy-start.6 = (s32[512]{0:T(512)S(1)}, s32[512]{0:T(512)}, u32[]{:S(2)}) copy-start(s32[512]{0:T(512)} %param.11) | copy-start | bytes 6148
  2.7 16.6 %copy-start.5 = (bf16[32,512]{1,0:T(8,128)(2,1)S(1)}, bf16[32,512]{1,0:T(8,128)(2,1)}, u32[]{:S(2)}) copy-start(bf16[32,512]{1,0:T(8,128)(2,1)} %shard_map.86.refs_0_) | copy-start | bytes 98308
  2.7 19.8 %collective-permute-start.4 = (bf16[4,128,512]{2,1,0:T(8,128)(2,1)}, bf16[4,128,512]{2,1,0:T(8,128)(2,1)S(1)}, u32[]{:S(2)}, u32[]{:S(2)}) collective-permute-start(bf16[4,128,512]{2,1,0:T(8,128)(2,1)} %refs_0_.3), channel_id=1, source_target_pairs={{0,2},{1,3},{2,0},{3,1},{4,6},{5,7},{6,4},{7,5},{8,10},{9,11},{10,... | collective-permute-start | bytes 1572872 | tf_op jit(solution)/shard_map/ppermute | solution.py:45
  5.7 12.6 %collective-permute-start.2 = (bf16[32,512]{1,0:T(8,128)(2,1)}, bf16[32,512]{1,0:T(8,128)(2,1)S(1)}, u32[]{:S(2)}, u32[]{:S(2)}) collective-permute-start(bf16[32,512]{1,0:T(8,128)(2,1)} %shard_map.86.refs_0_), channel_id=1, source_target_pairs={{0,3},{1,2},{2,1},{3,0},{4,7},{5,6},{6,5},{7,4},{8,11},{9,10},{10,... | collective-permute-start | bytes 98312 | tf_op jit(solution)/shard_map/ppermute | solution.py:45
  5.7 13.5 %collective-permute-start.1 = (bf16[32,512]{1,0:T(8,128)(2,1)}, bf16[32,512]{1,0:T(8,128)(2,1)S(1)}, u32[]{:S(2)}, u32[]{:S(2)}) collective-permute-start(bf16[32,512]{1,0:T(8,128)(2,1)} %shard_map.86.refs_0_), channel_id=1, source_target_pairs={{0,2},{1,3},{2,0},{3,1},{4,6},{5,7},{6,4},{7,5},{8,10},{9,11},{10,... | collective-permute-start | bytes 98312 | tf_op jit(solution)/shard_map/ppermute | solution.py:45
  6.9 12.4 %collective-permute-start = (bf16[32,512]{1,0:T(8,128)(2,1)}, bf16[32,512]{1,0:T(8,128)(2,1)S(1)}, u32[]{:S(2)}, u32[]{:S(2)}) collective-permute-start(bf16[32,512]{1,0:T(8,128)(2,1)} %shard_map.86.refs_0_), channel_id=1, source_target_pairs={{0,1},{1,0},{2,3},{3,2},{4,5},{5,4},{6,7},{7,6},{8,9},{9,8},{10,11... | collective-permute-start | bytes 98312 | tf_op jit(solution)/shard_map/ppermute | solution.py:45
  19.2 11.4 %collective-permute-start.3 = (bf16[4,128,512]{2,1,0:T(8,128)(2,1)S(1)}, bf16[4,128,512]{2,1,0:T(8,128)(2,1)S(1)}, u32[]{:S(2)}, u32[]{:S(2)}) collective-permute-start(bf16[4,128,512]{2,1,0:T(8,128)(2,1)S(1)} %copy-done.4), channel_id=1, source_target_pairs={{0,1},{1,0},{2,3},{3,2},{4,5},{5,4},{6,7},{7,6},{8,9},{9,8},{10,11... | collective-permute-start | bytes 1572872 | tf_op jit(solution)/shard_map/ppermute | solution.py:45
  19.2 1.2 %copy-start.1 = (bf16[2048,256]{1,0:T(8,128)(2,1)S(1)}, bf16[2048,256]{1,0:T(8,128)(2,1)}, u32[]{:S(2)}) copy-start(bf16[2048,256]{1,0:T(8,128)(2,1)} %get-tuple-element.48.refs_4_.refs_8_) | copy-start | bytes 3145732
  22.4 8.2 %collective-permute-start.5 = (bf16[4,128,512]{2,1,0:T(8,128)(2,1)S(1)}, bf16[4,128,512]{2,1,0:T(8,128)(2,1)S(1)}, u32[]{:S(2)}, u32[]{:S(2)}) collective-permute-start(bf16[4,128,512]{2,1,0:T(8,128)(2,1)S(1)} %collective-permute-done.4.refs_2_), channel_id=1, source_target_pairs={{0,1},{1,0},{2,3},{3,2},{4,5},{5,4},{6,7},{7,6},{8,9},{9,8},{10,11... | collective-permute-start | bytes 1572872 | tf_op jit(solution)/shard_map/ppermute | solution.py:45
  23.0 15.3 %collective-permute-start.13 = (bf16[4,64,256]{2,1,0:T(8,128)(2,1)S(1)}, bf16[4,64,256]{2,1,0:T(8,128)(2,1)S(1)}, u32[]{:S(2)}, u32[]{:S(2)}) collective-permute-start(bf16[4,64,256]{2,1,0:T(8,128)(2,1)S(1)} %get-tuple-element.67), channel_id=1, source_target_pairs={{0,28},{4,24},{8,20},{12,16},{16,12},{20,8},{24,4},{28,0},{1,29},{... | collective-permute-start | bytes 393224 | tf_op jit(solution)/shard_map/ppermute | solution.py:45
  27.8 20.6 %collective-permute-start.17 = (bf16[4,64,256]{2,1,0:T(8,128)(2,1)S(1)}, bf16[4,64,256]{2,1,0:T(8,128)(2,1)S(1)}, u32[]{:S(2)}, u32[]{:S(2)}) collective-permute-start(bf16[4,64,256]{2,1,0:T(8,128)(2,1)S(1)} %get-tuple-element.73), channel_id=1, source_target_pairs={{0,16},{4,20},{8,24},{12,28},{16,0},{20,4},{24,8},{28,12},{1,17},{... | collective-permute-start | bytes 393224 | tf_op jit(solution)/shard_map/ppermute | solution.py:45
  27.8 23.4 %collective-permute-start.18 = (bf16[4,64,256]{2,1,0:T(8,128)(2,1)S(1)}, bf16[4,64,256]{2,1,0:T(8,128)(2,1)S(1)}, u32[]{:S(2)}, u32[]{:S(2)}) collective-permute-start(bf16[4,64,256]{2,1,0:T(8,128)(2,1)S(1)} %get-tuple-element.74), channel_id=1, source_target_pairs={{0,20},{4,16},{8,28},{12,24},{16,4},{20,0},{24,12},{28,8},{1,21},{... | collective-permute-start | bytes 393224 | tf_op jit(solution)/shard_map/ppermute | solution.py:45
  33.4 17.7 %collective-permute-start.6 = (bf16[4,64,256]{2,1,0:T(8,128)(2,1)S(1)}, bf16[4,64,256]{2,1,0:T(8,128)(2,1)S(1)}, u32[]{:S(2)}, u32[]{:S(2)}) collective-permute-start(bf16[4,64,256]{2,1,0:T(8,128)(2,1)S(1)} %get-tuple-element.55), channel_id=1, source_target_pairs={{0,28},{4,24},{8,20},{12,16},{16,12},{20,8},{24,4},{28,0},{1,29},{... | collective-permute-start | bytes 393224 | tf_op jit(solution)/shard_map/ppermute | solution.py:45
  34.7 19.0 %collective-permute-start.19 = (bf16[4,64,256]{2,1,0:T(8,128)(2,1)S(1)}, bf16[4,64,256]{2,1,0:T(8,128)(2,1)S(1)}, u32[]{:S(2)}, u32[]{:S(2)}) collective-permute-start(bf16[4,64,256]{2,1,0:T(8,128)(2,1)S(1)} %get-tuple-element.75), channel_id=1, source_target_pairs={{0,24},{4,28},{8,16},{12,20},{16,8},{20,12},{24,0},{28,4},{1,25},{... | collective-permute-start | bytes 393224 | tf_op jit(solution)/shard_map/ppermute | solution.py:45
  38.3 15.4 %collective-permute-start.14 = (bf16[4,64,256]{2,1,0:T(8,128)(2,1)S(1)}, bf16[4,64,256]{2,1,0:T(8,128)(2,1)S(1)}, u32[]{:S(2)}, u32[]{:S(2)}) collective-permute-start(bf16[4,64,256]{2,1,0:T(8,128)(2,1)S(1)} %get-tuple-element.68), channel_id=1, source_target_pairs={{0,4},{4,0},{8,12},{12,8},{16,20},{20,16},{24,28},{28,24},{1,5},{5... | collective-permute-start | bytes 393224 | tf_op jit(solution)/shard_map/ppermute | solution.py:45
  48.4 5.3 %collective-permute-start.15 = (bf16[4,64,256]{2,1,0:T(8,128)(2,1)S(1)}, bf16[4,64,256]{2,1,0:T(8,128)(2,1)S(1)}, u32[]{:S(2)}, u32[]{:S(2)}) collective-permute-start(bf16[4,64,256]{2,1,0:T(8,128)(2,1)S(1)} %get-tuple-element.70), channel_id=1, source_target_pairs={{0,8},{4,12},{8,0},{12,4},{16,24},{20,28},{24,16},{28,20},{1,9},{5... | collective-permute-start | bytes 393224 | tf_op jit(solution)/shard_map/ppermute | solution.py:45
  51.2 7.1 %collective-permute-start.16 = (bf16[4,64,256]{2,1,0:T(8,128)(2,1)S(1)}, bf16[4,64,256]{2,1,0:T(8,128)(2,1)S(1)}, u32[]{:S(2)}, u32[]{:S(2)}) collective-permute-start(bf16[4,64,256]{2,1,0:T(8,128)(2,1)S(1)} %get-tuple-element.72), channel_id=1, source_target_pairs={{0,12},{4,8},{8,4},{12,0},{16,28},{20,24},{24,20},{28,16},{1,13},{... | collective-permute-start | bytes 393224 | tf_op jit(solution)/shard_map/ppermute | solution.py:45
  51.2 10.2 %collective-permute-start.12 = (bf16[4,64,256]{2,1,0:T(8,128)(2,1)S(1)}, bf16[4,64,256]{2,1,0:T(8,128)(2,1)S(1)}, u32[]{:S(2)}, u32[]{:S(2)}) collective-permute-start(bf16[4,64,256]{2,1,0:T(8,128)(2,1)S(1)} %get-tuple-element.63), channel_id=1, source_target_pairs={{0,24},{4,28},{8,16},{12,20},{16,8},{20,12},{24,0},{28,4},{1,25},{... | collective-permute-start | bytes 393224 | tf_op jit(solution)/shard_map/ppermute | solution.py:45
  53.7 31.7 %copy-start.2 = (bf16[2048,256]{1,0:T(8,128)(2,1)S(1)}, bf16[2048,256]{1,0:T(8,128)(2,1)}, u32[]{:S(2)}) copy-start(bf16[2048,256]{1,0:T(8,128)(2,1)} %get-tuple-element.48.refs_4_.refs_8_) | copy-start | bytes 3145732
  61.4 2.0 %collective-permute-start.21 = (bf16[4,128,512]{2,1,0:T(8,128)(2,1)S(1)}, bf16[4,128,512]{2,1,0:T(8,128)(2,1)S(1)}, u32[]{:S(2)}, u32[]{:S(2)}) collective-permute-start(bf16[4,128,512]{2,1,0:T(8,128)(2,1)S(1)} %get-tuple-element.86), channel_id=1, source_target_pairs={{0,1},{1,0},{2,3},{3,2},{4,5},{5,4},{6,7},{7,6},{8,9},{9,8},{10,11... | collective-permute-start | bytes 1572872 | tf_op jit(solution)/shard_map/ppermute | solution.py:45
  61.4 2.6 %collective-permute-start.20 = (bf16[4,128,512]{2,1,0:T(8,128)(2,1)S(1)}, bf16[4,128,512]{2,1,0:T(8,128)(2,1)S(1)}, u32[]{:S(2)}, u32[]{:S(2)}) collective-permute-start(bf16[4,128,512]{2,1,0:T(8,128)(2,1)S(1)} %get-tuple-element.84), channel_id=1, source_target_pairs={{0,1},{1,0},{2,3},{3,2},{4,5},{5,4},{6,7},{7,6},{8,9},{9,8},{10,11... | collective-permute-start | bytes 1572872 | tf_op jit(solution)/shard_map/ppermute | solution.py:45
  64.3 30.4 %collective-permute-start.22 = (bf16[4,128,512]{2,1,0:T(8,128)(2,1)S(1)}, bf16[4,128,512]{2,1,0:T(8,128)(2,1)S(1)}, u32[]{:S(2)}, u32[]{:S(2)}) collective-permute-start(bf16[4,128,512]{2,1,0:T(8,128)(2,1)S(1)} %get-tuple-element.88), channel_id=1, source_target_pairs={{0,2},{1,3},{2,0},{3,1},{4,6},{5,7},{6,4},{7,5},{8,10},{9,11},{10,... | collective-permute-start | bytes 1572872 | tf_op jit(solution)/shard_map/ppermute | solution.py:45
  65.9 12.9 %collective-permute-start.10 = (bf16[4,64,256]{2,1,0:T(8,128)(2,1)S(1)}, bf16[4,64,256]{2,1,0:T(8,128)(2,1)S(1)}, u32[]{:S(2)}, u32[]{:S(2)}) collective-permute-start(bf16[4,64,256]{2,1,0:T(8,128)(2,1)S(1)} %get-tuple-element.61), channel_id=1, source_target_pairs={{0,16},{4,20},{8,24},{12,28},{16,0},{20,4},{24,8},{28,12},{1,17},{... | collective-permute-start | bytes 393224 | tf_op jit(solution)/shard_map/ppermute | solution.py:45
  68.8 13.2 %collective-permute-start.11 = (bf16[4,64,256]{2,1,0:T(8,128)(2,1)S(1)}, bf16[4,64,256]{2,1,0:T(8,128)(2,1)S(1)}, u32[]{:S(2)}, u32[]{:S(2)}) collective-permute-start(bf16[4,64,256]{2,1,0:T(8,128)(2,1)S(1)} %get-tuple-element.62), channel_id=1, source_target_pairs={{0,20},{4,16},{8,28},{12,24},{16,4},{20,0},{24,12},{28,8},{1,21},{... | collective-permute-start | bytes 393224 | tf_op jit(solution)/shard_map/ppermute | solution.py:45
  71.1 11.0 %collective-permute-start.7 = (bf16[4,64,256]{2,1,0:T(8,128)(2,1)S(1)}, bf16[4,64,256]{2,1,0:T(8,128)(2,1)S(1)}, u32[]{:S(2)}, u32[]{:S(2)}) collective-permute-start(bf16[4,64,256]{2,1,0:T(8,128)(2,1)S(1)} %get-tuple-element.56), channel_id=1, source_target_pairs={{0,4},{4,0},{8,12},{12,8},{16,20},{20,16},{24,28},{28,24},{1,5},{5... | collective-permute-start | bytes 393224 | tf_op jit(solution)/shard_map/ppermute | solution.py:45
  71.1 11.0 %collective-permute-start.8 = (bf16[4,64,256]{2,1,0:T(8,128)(2,1)S(1)}, bf16[4,64,256]{2,1,0:T(8,128)(2,1)S(1)}, u32[]{:S(2)}, u32[]{:S(2)}) collective-permute-start(bf16[4,64,256]{2,1,0:T(8,128)(2,1)S(1)} %get-tuple-element.58), channel_id=1, source_target_pairs={{0,8},{4,12},{8,0},{12,4},{16,24},{20,28},{24,16},{28,20},{1,9},{5... | collective-permute-start | bytes 393224 | tf_op jit(solution)/shard_map/ppermute | solution.py:45
  78.8 6.6 %collective-permute-start.9 = (bf16[4,64,256]{2,1,0:T(8,128)(2,1)S(1)}, bf16[4,64,256]{2,1,0:T(8,128)(2,1)S(1)}, u32[]{:S(2)}, u32[]{:S(2)}) collective-permute-start(bf16[4,64,256]{2,1,0:T(8,128)(2,1)S(1)} %get-tuple-element.60), channel_id=1, source_target_pairs={{0,12},{4,8},{8,4},{12,0},{16,28},{20,24},{24,20},{28,16},{1,13},{... | collective-permute-start | bytes 393224 | tf_op jit(solution)/shard_map/ppermute | solution.py:45
  86.8 4.1 %copy-start.3 = (f32[2048,256]{1,0:T(8,128)S(1)}, f32[2048,256]{1,0:T(8,128)}, u32[]{:S(2)}) copy-start(f32[2048,256]{1,0:T(8,128)} %get-tuple-element.79.h_ref) | copy-start | bytes 6291460
  86.9 4.1 %copy-start.7 = (s32[256]{0:T(256)S(1)}, s32[256]{0:T(256)}, u32[]{:S(2)}) copy-start(s32[256]{0:T(256)} %param.10) | copy-start | bytes 3076
  86.9 6.8 %collective-permute-start.23 = (bf16[32,512]{1,0:T(8,128)(2,1)S(1)}, bf16[32,512]{1,0:T(8,128)(2,1)S(1)}, u32[]{:S(2)}, u32[]{:S(2)}) collective-permute-start(bf16[32,512]{1,0:T(8,128)(2,1)S(1)} %get-tuple-element.90), channel_id=1, source_target_pairs={{0,1},{1,0},{2,3},{3,2},{4,5},{5,4},{6,7},{7,6},{8,9},{9,8},{10,11... | collective-permute-start | bytes 98312 | tf_op jit(solution)/shard_map/ppermute | solution.py:45
  86.9 6.7 %collective-permute-start.24 = (bf16[32,512]{1,0:T(8,128)(2,1)S(1)}, bf16[32,512]{1,0:T(8,128)(2,1)S(1)}, u32[]{:S(2)}, u32[]{:S(2)}) collective-permute-start(bf16[32,512]{1,0:T(8,128)(2,1)S(1)} %get-tuple-element.91), channel_id=1, source_target_pairs={{0,2},{1,3},{2,0},{3,1},{4,6},{5,7},{6,4},{7,5},{8,10},{9,11},{10,... | collective-permute-start | bytes 98312 | tf_op jit(solution)/shard_map/ppermute | solution.py:45
  87.5 6.1 %collective-permute-start.25 = (bf16[32,512]{1,0:T(8,128)(2,1)S(1)}, bf16[32,512]{1,0:T(8,128)(2,1)S(1)}, u32[]{:S(2)}, u32[]{:S(2)}) collective-permute-start(bf16[32,512]{1,0:T(8,128)(2,1)S(1)} %get-tuple-element.92), channel_id=1, source_target_pairs={{0,3},{1,2},{2,1},{3,0},{4,7},{5,6},{6,5},{7,4},{8,11},{9,10},{10,... | collective-permute-start | bytes 98312 | tf_op jit(solution)/shard_map/ppermute | solution.py:45

commit v3 on v2

--- a/solution.py
+++ b/solution.py
@@ -10,6 +10,7 @@
 BF16 = jnp.bfloat16
 F32 = jnp.float32
 LANE_GROUP = 16
+CFG = {'cost': {}, 'direct': False, 'rsdirect': False, 'f2early': False, 'order': [[7, 6, 5, 4, 3, 2, 1], [7, 6, 5, 4, 3, 2, 1]], 'deps': {'h3': ['h7'], 'h2': ['h7'], 'h1': ['h7'], 'fx': ['h7', 'h4'], 'F1': ['M', 'H1', 'H2', 'H3', 'fx'], 'near': ['H7', 'H6'], 'far': ['H7', 'H6'], 'pair': ['F2'], 'unpack': ['add'], 'H1': ['h3'], 'H2': ['M']}}
 
 
 def iota(shape, dim):
@@ -24,16 +25,18 @@
     return lax.dot_general(a, b, (((da,), (db,)), ((), ())), preferred_element_type=F32)
 
 
-def call(body, outs, ins, scratch=(), flops=0, limit=40 << 20, cost=None):
-    size = sum(o.size * o.dtype.itemsize for o in outs) + sum(v.size * v.dtype.itemsize for v in ins)
+def call(body, outs, ins, scratch=(), spaces={}, limit=40 << 20, weight=0):
+    name = getattr(body, "func", body).__name__
+    weight = CFG['cost'].get(name, 0)
     return pl.pallas_call(
         body,
+        name=name,
         out_shape=outs,
-        in_specs=[pl.BlockSpec(memory_space=pltpu.VMEM)] * len(ins),
+        in_specs=[pl.BlockSpec(memory_space=spaces.get(n, pltpu.VMEM)) for n in range(len(ins))],
         out_specs=[pl.BlockSpec(memory_space=pltpu.VMEM)] * len(outs),
         scratch_shapes=list(scratch),
         compiler_params=pltpu.CompilerParams(vmem_limit_bytes=limit),
-        cost_estimate=pl.CostEstimate(flops=0, bytes_accessed=0, transcendentals=0),
+        cost_estimate=pl.CostEstimate(flops=0, bytes_accessed=weight, transcendentals=0),
     )(*ins)
 
 
@@ -49,15 +52,12 @@
     return lax.optimization_barrier((value, *earlier))[0]
 
 
-def pack_body(order, s_hbm, out_ref, s_scr, sem):
-    copy = pltpu.make_async_copy(s_hbm, s_scr, sem)
-    copy.start()
-    copy.wait()
-    rows, j_here = s_scr.shape
+def pack_body(order, s_ref, out_ref):
+    rows, j_here = s_ref.shape
     groups = j_here // LANE_GROUP
     lanes = order * LANE_GROUP
     m_here = rows // order
-    s = s_scr[...]
+    s = s_ref[...]
     lane = iota((j_here, lanes), 1)
     keep = (iota((rows, lanes), 0) % order) == (iota((rows, lanes), 1) // LANE_GROUP)
     for g in range(groups):
@@ -67,78 +67,72 @@
         out_ref[g * m_here : (g + 1) * m_here, :] = packed.astype(BF16)
 
 
-def gate_body(step, x_hbm, cot_hbm, src_ref, dz_ref, h_ref, x_scr, cot_scr, sems):
-    rows, width = dz_ref.shape
+def gate_body(step, x_hbm, cot_hbm, src_ref, dz_hbm, x_scr, cot_scr, dz_scr, sems):
+    rows, width = x_scr.shape
     parts = rows // step
-    copies = []
+    reads, writes = [], []
     for n in range(parts):
         part = pl.ds(n * step, step)
-        copies.append(
-            (
-                pltpu.make_async_copy(x_hbm.at[part, :], x_scr.at[part, :], sems.at[0, n]),
-                pltpu.make_async_copy(cot_hbm.at[part, :], cot_scr.at[part, :], sems.at[1, n]),
-            )
-        )
-    for pair in copies:
-        for copy in pair:
-            copy.start()
+        reads.append(pltpu.make_async_copy(x_hbm.at[part, :], x_scr.at[part, :], sems.at[0, n]))
+        reads.append(pltpu.make_async_copy(cot_hbm.at[part, :], cot_scr.at[part, :], sems.at[1, n]))
+        writes.append(pltpu.make_async_copy(dz_scr.at[part, :], dz_hbm.at[part, :], sems.at[2, n]))
+    for copy in reads:
+        copy.start()
     select = one_hot(iota((width, width), 0) == src_ref[...])
     for n in range(parts):
-        for copy in copies[n]:
-            copy.wait()
+        reads[2 * n].wait()
+        reads[2 * n + 1].wait()
         part = slice(n * step, (n + 1) * step)
         gate = jax.nn.sigmoid(dot(x_scr[part, :], select))
-        scaled = cot_scr[part, :].astype(F32) * gate
-        dz_ref[part, :] = scaled.astype(BF16)
-        h_ref[part, :] = scaled * (1.0 - gate)
+        dz_scr[part, :] = (cot_scr[part, :].astype(F32) * gate).astype(BF16)
+        writes[n].start()
+    for copy in writes:
+        copy.wait()
 
 
 def gate_call(x, cot, src):
     rows, width = x.shape
-    step = min(rows, 512)
-    whole = pl.BlockSpec(memory_space=pltpu.VMEM)
+    step = min(rows, 256)
     left = pl.BlockSpec(memory_space=pltpu.HBM)
     return pl.pallas_call(
         functools.partial(gate_body, step),
-        out_shape=[of((rows, width)), of((rows, width), F32)],
-        in_specs=[left, left, whole],
-        out_specs=[whole, whole],
-        scratch_shapes=[
-            pltpu.VMEM((rows, width), BF16),
-            pltpu.VMEM((rows, width), BF16),
-            pltpu.SemaphoreType.DMA((2, rows // step)),
-        ],
+        name="gate_body",
+        out_shape=of((rows, width)),
+        in_specs=[left, left, pl.BlockSpec(memory_space=pltpu.VMEM)],
+        out_specs=left,
+        scratch_shapes=[pltpu.VMEM((rows, width), BF16)] * 3 + [pltpu.SemaphoreType.DMA((3, rows // step))],
         compiler_params=pltpu.CompilerParams(vmem_limit_bytes=60 << 20),
-        cost_estimate=pl.CostEstimate(
-            flops=2 * rows * width * width, bytes_accessed=10 * rows * width, transcendentals=rows * width
-        ),
+        cost_estimate=pl.CostEstimate(flops=0, bytes_accessed=0, transcendentals=0),
     )(x, cot, src)
 
 
 def regroup_back_body(batch, seq, order, *refs):
-    pieces, dz_ref = refs[:batch], refs[batch]
-    outs, second_ref, d_scr, r_scr = refs[batch + 1 : -3], refs[-3], refs[-2], refs[-1]
+    pieces, dz_hbm = refs[:batch], refs[batch]
+    outs, second_ref, d_scr, r_scr, dz_ref, sems = refs[batch + 1 : -5], *refs[-5:]
     me, here = lax.axis_index("batch"), lax.axis_index("seq")
     groups = second_ref.shape[0]
     lanes = order * LANE_GROUP
     m_here = order // batch
+    reads = []
+    for g in range(groups):
+        part = pl.ds(g * lanes, lanes)
+        reads.append(pltpu.make_async_copy(dz_hbm.at[part, :], dz_ref.at[part, :], sems.at[g]))
+        reads[g].start()
     for d in range(batch):
         piece = pieces[d][...].astype(F32)
         first = pl.multiple_of((me ^ d) * m_here, m_here)
         for g in range(groups):
             d_scr[g, pl.ds(first, m_here), :] = piece[g * m_here : (g + 1) * m_here]
     width = dz_ref.shape[1]
-
-    @pl.loop(0, groups)
-    def _(g):
+    tiled = one_hot((iota((order, lanes), 1) % order) == iota((order, lanes), 0))
+    keep = (iota((lanes, lanes), 0) % LANE_GROUP) == (iota((lanes, lanes), 1) // order)
+    for g in range(groups):
         packed = d_scr[g].astype(BF16)
         second_ref[g] = packed
-        tiled = one_hot((iota((order, lanes), 1) % order) == iota((order, lanes), 0))
-        keep = (iota((lanes, lanes), 0) % LANE_GROUP) == (iota((lanes, lanes), 1) // order)
         weights = jnp.where(keep, dot(packed, tiled, 0, 0), 0.0).astype(BF16)
-        dz = dz_ref[pl.ds(pl.multiple_of(g * lanes, lanes), lanes), :]
-        result = dot(weights, dz).astype(BF16).reshape(order, LANE_GROUP, width)
-        r_scr[:, pl.ds(pl.multiple_of(g * LANE_GROUP, LANE_GROUP), LANE_GROUP), :] = result
+        reads[g].wait()
+        result = dot(weights, dz_ref[g * lanes : (g + 1) * lanes, :]).astype(BF16)
+        r_scr[:, g * LANE_GROUP : (g + 1) * LANE_GROUP, :] = result.reshape(order, LANE_GROUP, width)
 
     blocks = order // seq
     for d in range(seq):
@@ -191,7 +185,8 @@
 
 
 def mix_back_body(batch, *refs):
-    pieces, dmixed_ref, second_ref, out_ref, weights_ref = refs[:batch], *refs[batch:]
+    pieces, dmixed_ref, second_ref, x_ref, cot_ref, src_ref = refs[:batch], *refs[batch:-3]
+    out_ref, weights_ref, h_ref = refs[-3:]
     me = lax.axis_index("batch")
     blocks, rows, order = pieces[0].shape
     groups, count, lanes = second_ref.shape
@@ -204,6 +199,15 @@
             term = dot(pieces[d][i], dmixed_ref[i, pl.ds(first, rows), :], 0, 0)
             total = term if total is None else total + term
         out_ref[pl.ds(pl.multiple_of(i * order, order), order), :] = total
+
+    width = x_ref.shape[1]
+    select = one_hot(iota((width, width), 0) == src_ref[...])
+
+    @pl.loop(0, blocks)
+    def _(i):
+        part = pl.ds(pl.multiple_of(i * order, order), order)
+        gate = jax.nn.sigmoid(dot(x_ref[part, :], select))
+        h_ref[part, :] = cot_ref[part, :].astype(F32) * gate * (1.0 - gate)
 
     @pl.loop(0, groups)
     def _(g):
@@ -260,6 +264,13 @@
 def pair_body(own_a, own_b, got_a, got_b, out_a, out_b):
     out_a[...] = own_a[...].astype(F32) + got_a[...].astype(F32)
     out_b[...] = (own_b[...].astype(F32) + got_b[...].astype(F32)).astype(BF16)
+
+
+def sum_body(own, *refs):
+    total = own[...].astype(F32)
+    for got in refs[:-1]:
+        total = total + got[...].astype(F32)
+    refs[-1][...] = total.astype(BF16)
 
 
 def add_body(own, got, out):
@@ -292,83 +303,98 @@
     groups, lanes = j_here // LANE_GROUP, count * LANE_GROUP
     src = gate_source.reshape(1, width)
     alt = alternate.reshape(1, order)
-    big = 2 * rows_here * order * width
 
     flat = jnp.transpose(second_factor, (1, 2, 0)).reshape(m_here * count, j_here)
-    mine = pl.pallas_call(
-        functools.partial(pack_body, count),
-        out_shape=of((groups * m_here, lanes)),
-        in_specs=[pl.BlockSpec(memory_space=pltpu.HBM)],
-        out_specs=pl.BlockSpec(memory_space=pltpu.VMEM),
-        scratch_shapes=[pltpu.VMEM(flat.shape, BF16), pltpu.SemaphoreType.DMA],
-        compiler_params=pltpu.CompilerParams(vmem_limit_bytes=60 << 20),
-        cost_estimate=pl.CostEstimate(flops=4 * flat.size * lanes, bytes_accessed=4 * flat.size, transcendentals=0),
-    )(flat)
-    packed = [mine] + [swap(mine, "batch", d, batch) for d in (2, 3, 1)]
-    packed = [packed[0], packed[3], packed[1], packed[2]]
-    dz, h = gate_call(x, cot, src)
-
-    across = swap(after(first_factor, mine), "batch", 2, batch)
-    beside = swap(after(first_factor, dz, *packed[1:]), "batch", 1, batch)
+    vals = {}
+
+    def dep(name, value):
+        earlier = [vals[n] for n in CFG['deps'].get(name, ()) if n in vals]
+        return after(value, *earlier) if earlier else value
+
+    def keep(name, value):
+        vals[name] = value
+        return value
+
+    def move(name, value, axis, step, size):
+        return keep(name, swap(dep(name, value), axis, step, size))
+
+    (mine,) = call(functools.partial(pack_body, count), [of((groups * m_here, lanes))], [flat])
+    packed = {0: mine}
+    for d in (3, 2, 1):
+        packed[d] = move(f"D{d}", mine, "batch", d, batch)
+    dz = keep("gate", gate_call(x, cot, src))
+    first_ready = after(first_factor, dz) if CFG['f2early'] else after(first_factor, dz, *[packed[d] for d in (1, 2, 3)])
+    across = move("f2", first_ready, "batch", 2, batch)
+    beside = move("f1", first_ready, "batch", 1, batch)
+    direct = move("f3", first_ready, "batch", 3, batch) if CFG['direct'] else None
     piece = of((blocks, j_here, width))
     *back, second = call(
         functools.partial(regroup_back_body, batch, seq, count),
         [piece] * seq + [of((groups, count, lanes))],
-        [*packed, dz],
-        [pltpu.VMEM((groups, count, lanes), F32), pltpu.VMEM((count, j_here, width), BF16)],
-        flops=2 * big,
-    )
-    far_first = sorted(range(1, seq), key=lambda d: -d)
-
-    def exchange(blocks_out):
-        got = {0: blocks_out[0]}
-        for d in far_first:
-            ready = after(blocks_out[d], got[far_first[0]]) if d < seq // 2 else blocks_out[d]
-            got[d] = swap(ready, "seq", d, seq)
-        return [got[d] for d in range(seq)]
-
-    back_got = exchange(back)
-    first = [first_factor, beside, across, swap(after(across, back[0]), "batch", 1, batch)]
+        [*[packed[d] for d in range(batch)], dz],
+        [
+            pltpu.VMEM((groups, count, lanes), F32),
+            pltpu.VMEM((count, j_here, width), BF16),
+            pltpu.VMEM((rows_here, width), BF16),
+            pltpu.SemaphoreType.DMA((groups,)),
+        ],
+        spaces={batch: pltpu.HBM},
+        limit=56 << 20,
+    )
+    keep("A2", back[0])
+    back_got = {0: back[0]}
+    for d in CFG['order'][0]:
+        back_got[d] = move(f"h{d}", back[d], "seq", d, seq)
+    if direct is None:
+        direct = move("fx", across, "batch", 1, batch)
+    first = [first_factor, beside, across, direct]
     regrouped = call(
         functools.partial(mix_body, batch, seq),
         [piece] * seq,
-        [*first, x, alt],
+        [dep("M", first_factor), *first[1:], x, alt],
         [pltpu.VMEM((order, order), BF16), pltpu.VMEM((order, width), BF16), pltpu.VMEM((order, width), BF16)],
-        flops=2 * big,
-    )
-    got = exchange(regrouped)
-
-    back_got[0] = after(back_got[0], regrouped[0], got[far_first[0]])
+    )
+    keep("M", regrouped[0])
+    got = {0: regrouped[0]}
+    for d in CFG['order'][1]:
+        got[d] = move(f"H{d}", regrouped[d], "seq", d, seq)
     *parts, dmixed = call(
         functools.partial(first_grad_body, batch, seq),
         [of((blocks, k_here, order))] * batch + [of((blocks, order, width))],
-        [*back_got, x, alt],
+        [dep("F1", back_got[0]), *[back_got[d] for d in range(1, seq)], x, alt],
         [pltpu.VMEM((order, order), BF16), pltpu.VMEM((order, width), BF16), pltpu.VMEM((order, order), BF16)],
-        flops=2 * big,
-    )
-    near = swap(after(parts[1], got[far_first[1]]), "batch", 1, batch)
-    far = swap(after(parts[3], got[far_first[1]]), "batch", 1, batch)
-    dmix_in, weights = call(
+    )
+    keep("F1", dmixed)
+    if CFG['rsdirect']:
+        others = [move(f"rs{d}", parts[d], "batch", d, batch) for d in (3, 2, 1)]
+    else:
+        near = move("near", parts[1], "batch", 1, batch)
+        far = move("far", parts[3], "batch", 1, batch)
+    dmix_in, weights, h = call(
         functools.partial(mix_back_body, batch),
-        [of((rows_here, width), F32), of((groups, lanes, lanes))],
-        [*first, dmixed, second],
-        flops=big,
-    )
-    kept, summed = call(
-        pair_body, [of(parts[0].shape, F32), of(parts[0].shape)], [parts[0], parts[2], near, far]
-    )
-    (grad_one,) = call(add_body, [of(parts[0].shape)], [kept, swap(summed, "batch", 2, batch)])
-
+        [of((rows_here, width), F32), of((groups, lanes, lanes)), of((rows_here, width), F32)],
+        [dep("F2", first_factor), *first[1:], dmixed, second, x, cot, src],
+    )
+    keep("F2", dmix_in)
+    if CFG['rsdirect']:
+        (grad_one,) = call(sum_body, [of(parts[0].shape)], [dep("sum", parts[0]), *others])
+    else:
+        kept, summed = call(
+            pair_body, [of(parts[0].shape, F32), of(parts[0].shape)], [dep("pair", parts[0]), parts[2], near, far]
+        )
+        keep("pair", summed)
+        rx = move("rx", summed, "batch", 2, batch)
+        (grad_one,) = call(add_body, [of(parts[0].shape)], [kept, rx])
+    keep("add", grad_one)
     *terms, gathered = call(
         functools.partial(second_grad_body, batch, seq),
         [of((groups * m_here, lanes))] * batch + [of((count, j_here, width))],
-        [*got, dz],
+        [after(got[0], dmix_in), *[got[d] for d in range(1, seq)], dz],
         [pltpu.VMEM((groups, count, lanes), F32)],
-        flops=2 * big,
-    )
-    terms_got = [terms[0]] + [swap(terms[d], "batch", d, batch) for d in range(1, batch)]
+    )
+    terms_got = [dep("unpack", terms[0])] + [move(f"R{d}", terms[d], "batch", d, batch) for d in (1, 2, 3)]
     (grad_tokens,) = call(
-        tokens_body, [of((rows_here, width))], [gathered, weights, h, src, dmix_in], flops=2 * big
+        tokens_body, [of((rows_here, width))], [gathered, weights, h, src, dmix_in]
     )
     (grad_flat,) = call(
         functools.partial(unpack_body, count), [of((m_here * count, j_here))], terms_got

time: 95.8 us -> 89.4 us (0.933)
  waiting for transfers between devices: 39.4 us -> 31.2 us
  Pallas kernels: 22.8 us -> 24.9 us
    ppermute x26, waiting for transfers between devices: 39.4 us -> 31.2 us  [swap(): return lax.ppermute(value, axis, [(p, p ^ step) for p in range(size)])]
    pallas_call x11, Pallas kernels: 22.8 us -> 24.9 us  [the longest x10 20.5 us: call(): pl.pallas_call(body, name=name, out_shape=outs, in_specs=[pl.BlockSpec(me...]
  transfers between devices with their start and end apart: 26 -> 26, of which waited for: 10 -> 9; matrix products, arithmetic and copies ran while one was open for 0% -> 0% of each run, Pallas kernels for 21% -> 26%
where the time goes in v3:
time: 89.4 us; the launch traced here: 89.1 us
  waiting for transfers between devices  31.2 us (35%)
  starting transfers between devices  31.1 us (35%)
  Pallas kernels  24.9 us (28%)
  local copies, waits for them, and re-layouts  0.96 us (1%)
  between operations  0.94 us (1%)
    ppermute x26, waiting for transfers between devices, swap(): return lax.ppermute(value, axis, [(p, p ^ step) for p in range(size)])  31.2 us
    ppermute x26, starting transfers between devices, swap(): return lax.ppermute(value, axis, [(p, p ^ step) for p in range(size)])  31.1 us
    pallas_call x10, Pallas kernels, call(): pl.pallas_call(body, name=name, out_shape=outs, in_specs=[pl.BlockSpec(me...  20.5 us
    pallas_call x1, Pallas kernels, gate_call(): pl.pallas_call(functools.partial(gate_body, step), name='gate_body', out_...  4.4 us
  transfers between devices with their start and end apart: 26, of which 9 were waited for; matrix products, arithmetic and copies ran while one was open for 0% of the time, Pallas kernels for 26%

profile of v3, /device:TPU:0, one launch (start us, length us, event | category | flops | bytes accessed | tf_op | source)
XLA Modules:
  0.0 89.1 jit_solution(19911075811823538)
XLA Ops:
  0.7 0.9 copy-done.7
  1.5 0.4 pack_body.1.refs_0_
  2.0 0.0 copy-start.6
  2.0 2.4 %collective-permute-start.2 = (bf16[32,512]{1,0:T(8,128)(2,1)S(1)}, bf16[32,512]{1,0:T(8,128)(2,1)S(1)}, u32[]{:S(2)}, u32[]{:S(2)}) collective-permute-start(bf16[32,512]{1,0:T(8,128)(2,1)S(1)} %pack_body.1.refs_0_), channel_id=1, source_target_pairs={{0,3},{1,2},{2,1},{3,0},{4,7},{5,6},{6,5},{7,4},{8,11},{9,10},{10,... | collective-permute-start | bytes 98312 | tf_op jit(solution)/shard_map/ppermute | solution.py:48
  4.4 0.6 collective-permute-start.1
  5.0 0.0 collective-permute-start
  5.1 4.4 %gate_body.1.refs_4_.refs_8_ = bf16[2048,256]{1,0:T(8,128)(2,1)} custom-call(bf16[2048,256]{1,0:T(8,128)(2,1)} %bitcast.11, bf16[2048,256]{1,0:T(8,128)(2,1)} %bitcast.15, s32[1,256]{1,0:T(1,128)} %bitcast.18), custom_call_target="tpu_custom_call" | custom-call | tf_op jit(solution)/shard_map/gate_body/pallas_call | solution.py:97
  9.5 0.0 collective-permute-done.2.refs_3_
  9.5 0.0 collective-permute-done.1.refs_2_
  9.5 0.0 collective-permute-done.refs_1_
  9.6 1.8 %collective-permute-start.4 = (bf16[4,128,512]{2,1,0:T(8,128)(2,1)S(1)}, bf16[4,128,512]{2,1,0:T(8,128)(2,1)S(1)}, u32[]{:S(2)}, u32[]{:S(2)}) collective-permute-start(bf16[4,128,512]{2,1,0:T(8,128)(2,1)S(1)} %copy-done.3), channel_id=1, source_target_pairs={{0,2},{1,3},{2,0},{3,1},{4,6},{5,7},{6,4},{7,5},{8,10},{9,11},{10,... | collective-permute-start | bytes 1572872 | tf_op jit(solution)/shard_map/ppermute | solution.py:48
  11.4 4.7 %regroup_back_body.1 = (bf16[4,64,256]{2,1,0:T(8,128)(2,1)}, bf16[4,64,256]{2,1,0:T(8,128)(2,1)}, bf16[4,64,256]{2,1,0:T(8,128)(2,1)}, bf16[4,64,256]{2,1,0:T(8,...) custom-call(bf16[32,512]{1,0:T(8,128)(2,1)} %copy-done.6, ...), custom_call_target="tpu_custom_call" | custom-call | tf_op jit(solution)/shard_map/regroup_back_body/pallas_call | solution.py:31
  16.1 0.0 copy-start.5
  16.1 4.6 %collective-permute-start.5 = (bf16[4,64,256]{2,1,0:T(8,128)(2,1)}, bf16[4,64,256]{2,1,0:T(8,128)(2,1)S(1)}, u32[]{:S(2)}, u32[]{:S(2)}) collective-permute-start(bf16[4,64,256]{2,1,0:T(8,128)(2,1)} %get-tuple-element.49), channel_id=1, source_target_pairs={{0,28},{4,24},{8,20},{12,16},{16,12},{20,8},{24,4},{28,0},{1,29},{... | collective-permute-start | bytes 393224 | tf_op jit(solution)/shard_map/ppermute | solution.py:48
  20.8 0.0 collective-permute-start.6
  20.8 0.0 collective-permute-start.3
  20.8 4.8 %collective-permute-done.5.refs_7_ = bf16[4,64,256]{2,1,0:T(8,128)(2,1)S(1)} collective-permute-done((bf16[4,64,256]{2,1,0:T(8,128)(2,1)}, bf16[4,64,256]{2,1,0:T(8,128)(2,1)S(1)}, u32[]{:S(2)}, u32[]{:S(2)}) %collective-permute-start.5) | collective-permute-done | bytes 131104 | tf_op jit(solution)/shard_map/ppermute | solution.py:48
  25.6 6.5 %collective-permute-done.6.refs_4_ = bf16[4,64,256]{2,1,0:T(8,128)(2,1)S(1)} collective-permute-done((bf16[4,64,256]{2,1,0:T(8,128)(2,1)}, bf16[4,64,256]{2,1,0:T(8,128)(2,1)S(1)}, u32[]{:S(2)}, u32[]{:S(2)}) %collective-permute-start.6) | collective-permute-done | bytes 131104 | tf_op jit(solution)/shard_map/ppermute | solution.py:48
  32.1 0.0 collective-permute-done.4.refs_2_
  32.1 3.9 %collective-permute-start.14 = (bf16[4,64,256]{2,1,0:T(8,128)(2,1)}, bf16[4,64,256]{2,1,0:T(8,128)(2,1)S(1)}, u32[]{:S(2)}, u32[]{:S(2)}) collective-permute-start(bf16[4,64,256]{2,1,0:T(8,128)(2,1)} %get-tuple-element.66), channel_id=1, source_target_pairs={{0,20},{4,16},{8,28},{12,24},{16,4},{20,0},{24,12},{28,8},{1,21},{... | collective-permute-start | bytes 393224 | tf_op jit(solution)/shard_map/ppermute | solution.py:48
  36.0 0.0 copy-start.2
  36.1 0.0 copy-start.8
  36.1 2.7 %mix_body.1 = (bf16[4,64,256]{2,1,0:T(8,128)(2,1)S(1)}, bf16[4,64,256]{2,1,0:T(8,128)(2,1)S(1)}, bf16[4,64,256]{2,1,0:T(8,128)(2,1)S(1)}, bf16[4,64,256]{2,1,0:T...) custom-call(bf16[4,128,512]{2,1,0:T(8,128)(2,1)S(1)} %copy-done.3, ...), custom_call_target="tpu_custom_call" | custom-call | tf_op jit(solution)/shard_map/mix_body/pallas_call | solution.py:31
  38.8 0.1 collective-permute-start.10
  38.9 1.8 %collective-permute-done.8.refs_3_ = bf16[4,64,256]{2,1,0:T(8,128)(2,1)S(1)} collective-permute-done((bf16[4,64,256]{2,1,0:T(8,128)(2,1)}, bf16[4,64,256]{2,1,0:T(8,128)(2,1)S(1)}, u32[]{:S(2)}, u32[]{:S(2)}) %collective-permute-start.8) | collective-permute-done | bytes 131104 | tf_op jit(solution)/shard_map/ppermute | solution.py:48
  40.7 1.2 %collective-permute-start.9 = (bf16[4,64,256]{2,1,0:T(8,128)(2,1)S(1)}, bf16[4,64,256]{2,1,0:T(8,128)(2,1)S(1)}, u32[]{:S(2)}, u32[]{:S(2)}) collective-permute-start(bf16[4,64,256]{2,1,0:T(8,128)(2,1)S(1)} %get-tuple-element.57), channel_id=1, source_target_pairs={{0,4},{4,0},{8,12},{12,8},{16,20},{20,16},{24,28},{28,24},{1,5},{5... | collective-permute-start | bytes 393224 | tf_op jit(solution)/shard_map/ppermute | solution.py:48
  41.9 0.4 collective-permute-start.11
  42.4 1.9 %collective-permute-start.15 = (bf16[4,64,256]{2,1,0:T(8,128)(2,1)S(1)}, bf16[4,64,256]{2,1,0:T(8,128)(2,1)S(1)}, u32[]{:S(2)}, u32[]{:S(2)}) collective-permute-start(bf16[4,64,256]{2,1,0:T(8,128)(2,1)S(1)} %copy-done.15), channel_id=1, source_target_pairs={{0,24},{4,28},{8,16},{12,20},{16,8},{20,12},{24,0},{28,4},{1,25},{... | collective-permute-start | bytes 393224 | tf_op jit(solution)/shard_map/ppermute | solution.py:48
  44.3 0.0 collective-permute-done.14.refs_5_
  44.3 0.5 collective-permute-start.12
  44.8 0.4 collective-permute-done.10.refs_2_
  45.2 1.7 %collective-permute-start.13 = (bf16[4,64,256]{2,1,0:T(8,128)(2,1)S(1)}, bf16[4,64,256]{2,1,0:T(8,128)(2,1)S(1)}, u32[]{:S(2)}, u32[]{:S(2)}) collective-permute-start(bf16[4,64,256]{2,1,0:T(8,128)(2,1)S(1)} %copy-done.13), channel_id=1, source_target_pairs={{0,8},{4,12},{8,0},{12,4},{16,24},{20,28},{24,16},{28,20},{1,9},{5... | collective-permute-start | bytes 393224 | tf_op jit(solution)/shard_map/ppermute | solution.py:48
  46.9 1.0 %collective-permute-done.9.refs_1_ = bf16[4,64,256]{2,1,0:T(8,128)(2,1)S(1)} collective-permute-done((bf16[4,64,256]{2,1,0:T(8,128)(2,1)S(1)}, bf16[4,64,256]{2,1,0:T(8,128)(2,1)S(1)}, u32[]{:S(2)}, u32[]{:S(2)}) %collective-permute-start.9) | collective-permute-done | bytes 131104 | tf_op jit(solution)/shard_map/ppermute | solution.py:48
  47.9 3.1 %collective-permute-start.18 = (bf16[4,64,256]{2,1,0:T(8,128)(2,1)S(1)}, bf16[4,64,256]{2,1,0:T(8,128)(2,1)S(1)}, u32[]{:S(2)}, u32[]{:S(2)}) collective-permute-start(bf16[4,64,256]{2,1,0:T(8,128)(2,1)S(1)} %get-tuple-element.74), channel_id=1, source_target_pairs={{0,24},{4,28},{8,16},{12,20},{16,8},{20,12},{24,0},{28,4},{1,25},{... | collective-permute-start | bytes 393224 | tf_op jit(solution)/shard_map/ppermute | solution.py:48
  51.0 1.1 %collective-permute-done.11.refs_3_ = bf16[4,64,256]{2,1,0:T(8,128)(2,1)S(1)} collective-permute-done((bf16[4,64,256]{2,1,0:T(8,128)(2,1)S(1)}, bf16[4,64,256]{2,1,0:T(8,128)(2,1)S(1)}, u32[]{:S(2)}, u32[]{:S(2)}) %collective-permute-start.11) | collective-permute-done | bytes 131104 | tf_op jit(solution)/shard_map/ppermute | solution.py:48
  52.1 1.6 %collective-permute-start.19 = (bf16[4,64,256]{2,1,0:T(8,128)(2,1)S(1)}, bf16[4,64,256]{2,1,0:T(8,128)(2,1)S(1)}, u32[]{:S(2)}, u32[]{:S(2)}) collective-permute-start(bf16[4,64,256]{2,1,0:T(8,128)(2,1)S(1)} %get-tuple-element.75), channel_id=1, source_target_pairs={{0,28},{4,24},{8,20},{12,16},{16,12},{20,8},{24,4},{28,0},{1,29},{... | collective-permute-start | bytes 393224 | tf_op jit(solution)/shard_map/ppermute | solution.py:48
  53.7 0.0 collective-permute-done.15.refs_6_
  53.7 0.0 collective-permute-done.12.refs_1_
  53.7 3.7 %collective-permute-done.13.refs_2_ = bf16[4,64,256]{2,1,0:T(8,128)(2,1)S(1)} collective-permute-done((bf16[4,64,256]{2,1,0:T(8,128)(2,1)S(1)}, bf16[4,64,256]{2,1,0:T(8,128)(2,1)S(1)}, u32[]{:S(2)}, u32[]{:S(2)}) %collective-permute-start.13) | collective-permute-done | bytes 131104 | tf_op jit(solution)/shard_map/ppermute | solution.py:48
  57.4 3.0 %first_grad_body.1 = (bf16[4,128,512]{2,1,0:T(8,128)(2,1)S(1)}, bf16[4,128,512]{2,1,0:T(8,128)(2,1)S(1)}, bf16[4,128,512]{2,1,0:T(8,128)(2,1)S(1)}, bf16[4,128,5...) custom-call(bf16[4,64,256]{2,1,0:T(8,128)(2,1)S(1)} %copy-done.5, bf16[4,64,256]{2,1,0:T(8,128)(2,1)S(1)} %collective-permute-done.12.refs_1_, ...), custom_call_target="tpu_custom_call" | custom-call | tf_op jit(solution)/shard_map/first_grad_body/pallas_call | solution.py:31
  60.5 0.0 collective-permute-done.18.refs_6_
  60.5 0.0 collective-permute-done.19.refs_7_
  60.5 0.1 collective-permute-start.21
  60.6 0.5 collective-permute-start.20
  61.1 3.3 %mix_back_body.1 = (f32[2048,256]{1,0:T(8,128)S(1)}, bf16[4,512,512]{2,1,0:T(8,128)(2,1)S(1)}, f32[2048,256]{1,0:T(8,128)S(1)}) custom-call(bf16[4,128,512]{2,1,0:T(8,128)(2,1)S(1)} %copy-done.3, bf16[4,128,512]{2,1,0:T(8,128)(2,1)S(1)} %collective-permute-done.3.refs_1_, bf16[4,128,512]{2,1,0:T(8,128)(2,1)S(1)} %collective-permute-done.4.refs_2_, ...), custom_call_target="tpu_custom_call" | custom-call | tf_op jit(solution)/shard_map/mix_back_body/pallas_call | solution.py:31
  64.4 0.0 copy-start.1
  64.4 0.0 collective-permute-done.21.got_b
  64.4 0.2 pair_body.1
  64.6 0.8 collective-permute-start.22
  65.5 3.7 %collective-permute-start.16 = (bf16[4,64,256]{2,1,0:T(8,128)(2,1)S(1)}, bf16[4,64,256]{2,1,0:T(8,128)(2,1)S(1)}, u32[]{:S(2)}, u32[]{:S(2)}) collective-permute-start(bf16[4,64,256]{2,1,0:T(8,128)(2,1)S(1)} %get-tuple-element.72), channel_id=1, source_target_pairs={{0,16},{4,20},{8,24},{12,28},{16,0},{20,4},{24,8},{28,12},{1,17},{... | collective-permute-start | bytes 393224 | tf_op jit(solution)/shard_map/ppermute | solution.py:48
  69.1 0.1 collective-permute-start.17
  69.2 9.9 %collective-permute-done.16.refs_4_ = bf16[4,64,256]{2,1,0:T(8,128)(2,1)S(1)} collective-permute-done((bf16[4,64,256]{2,1,0:T(8,128)(2,1)S(1)}, bf16[4,64,256]{2,1,0:T(8,128)(2,1)S(1)}, u32[]{:S(2)}, u32[]{:S(2)}) %collective-permute-start.16) | collective-permute-done | bytes 131104 | tf_op jit(solution)/shard_map/ppermute | solution.py:48
  79.1 2.0 %collective-permute-done.17.refs_5_ = bf16[4,64,256]{2,1,0:T(8,128)(2,1)S(1)} collective-permute-done((bf16[4,64,256]{2,1,0:T(8,128)(2,1)S(1)}, bf16[4,64,256]{2,1,0:T(8,128)(2,1)S(1)}, u32[]{:S(2)}, u32[]{:S(2)}) %collective-permute-start.17) | collective-permute-done | bytes 131104 | tf_op jit(solution)/shard_map/ppermute | solution.py:48
  81.1 1.4 %second_grad_body.1 = (bf16[32,512]{1,0:T(8,128)(2,1)S(1)}, bf16[32,512]{1,0:T(8,128)(2,1)S(1)}, bf16[32,512]{1,0:T(8,128)(2,1)S(1)}, bf16[32,512]{1,0:T(8,128)(2,1)S(1)}, bf16[32,64,256]{2,1,0:T(8,128)(2,1)S(1)}) custom-call(bf16[4,64,256]{2,1,0:T(8,128)(2,1)S(1)} %get-tuple-element.71.refs_0_, bf16[4,64,256]{2,1,0:T(8,128)(2,1)S(1)} %collective-permute-done.9.refs_1_, ...), custom_call_target="tpu_custom_call" | custom-call | tf_op jit(solution)/shard_map/second_grad_body/pallas_call | solution.py:31
  82.5 0.1 collective-permute-start.23
  82.6 1.3 %collective-permute-start.24 = (bf16[32,512]{1,0:T(8,128)(2,1)S(1)}, bf16[32,512]{1,0:T(8,128)(2,1)S(1)}, u32[]{:S(2)}, u32[]{:S(2)}) collective-permute-start(bf16[32,512]{1,0:T(8,128)(2,1)S(1)} %get-tuple-element.91), channel_id=1, source_target_pairs={{0,2},{1,3},{2,0},{3,1},{4,6},{5,7},{6,4},{7,5},{8,10},{9,11},{10,... | collective-permute-start | bytes 98312 | tf_op jit(solution)/shard_map/ppermute | solution.py:48
  83.9 0.6 collective-permute-start.25
  84.4 2.7 %tokens_body.1 = bf16[2048,256]{1,0:T(8,128)(2,1)} custom-call(bf16[32,64,256]{2,1,0:T(8,128)(2,1)S(1)} %get-tuple-element.76.reg_ref, bf16[4,512,512]{2,1,0:T(8,128)(2,1)S(1)} %get-tuple-element.77.weights_ref, f32[2048,256]{1,0:T(8,128)S(1)} %get-tuple-element.78.h_ref, s32[1,256]{1,0:T(1,128)S(1)} %bitcast.20, f32[2048,256]{1,0:T(8,128)S(1)} %get-tuple-element.70.back_ref), custom_call_target="tpu_custom_call" | custom-call | tf_op jit(solution)/shard_map/tokens_body/pallas_call | solution.py:31
  87.1 0.0 collective-permute-done.22.got
  87.1 0.9 %add_body.1 = bf16[4,128,512]{2,1,0:T(8,128)(2,1)} custom-call(f32[4,128,512]{2,1,0:T(8,128)S(1)} %get-tuple-element.86.own, bf16[4,128,512]{2,1,0:T(8,128)(2,1)S(1)} %collective-permute-done.22.got), custom_call_target="tpu_custom_call" | custom-call | tf_op jit(solution)/shard_map/add_body/pallas_call | solution.py:31
  88.0 0.0 collective-permute-done.23.refs_1_
  88.0 0.0 collective-permute-done.24.refs_2_
  88.0 0.0 collective-permute-done.25.refs_3_
  88.1 1.1 %unpack_body.1 = bf16[256,64]{1,0:T(8,128)(2,1)} custom-call(bf16[32,512]{1,0:T(8,128)(2,1)S(1)} %get-tuple-element.89.refs_0_, bf16[32,512]{1,0:T(8,128)(2,1)S(1)} %collective-permute-done.23.refs_1_, bf16[32,512]{1,0:T(8,128)(2,1)S(1)} %collective-permute-done.24.refs_2_, bf16[32,512]{1,0:T(8,128)(2,1)S(1)} %collective-permute-done.25.refs_3_), custom_call_target="tpu_custom_call" | custom-call | tf_op jit(solution)/shard_map/unpack_body/pallas_call | solution.py:31
  (31 shorter events, 0.1 us)
Async XLA Ops:
  0.6 8.9 %copy-start.3 = (bf16[4,128,512]{2,1,0:T(8,128)(2,1)S(1)}, bf16[4,128,512]{2,1,0:T(8,128)(2,1)}, u32[]{:S(2)}) copy-start(bf16[4,128,512]{2,1,0:T(8,128)(2,1)} %refs_0_.3) | copy-start | bytes 1572868
  0.6 0.9 %copy-start.7 = (bf16[64,8,32]{0,2,1:T(8,128)(2,1)S(1)}, bf16[64,8,32]{0,2,1:T(8,128)(2,1)}, u32[]{:S(2)}) copy-start(bf16[64,8,32]{0,2,1:T(8,128)(2,1)} %param.9) | copy-start | bytes 98308
  2.0 9.4 %copy-start.6 = (bf16[32,512]{1,0:T(8,128)(2,1)}, bf16[32,512]{1,0:T(8,128)(2,1)S(1)}, u32[]{:S(2)}) copy-start(bf16[32,512]{1,0:T(8,128)(2,1)S(1)} %pack_body.1.refs_0_) | copy-start | bytes 98308
  2.0 7.5 %collective-permute-start.2 = (bf16[32,512]{1,0:T(8,128)(2,1)S(1)}, bf16[32,512]{1,0:T(8,128)(2,1)S(1)}, u32[]{:S(2)}, u32[]{:S(2)}) collective-permute-start(bf16[32,512]{1,0:T(8,128)(2,1)S(1)} %pack_body.1.refs_0_), channel_id=1, source_target_pairs={{0,3},{1,2},{2,1},{3,0},{4,7},{5,6},{6,5},{7,4},{8,11},{9,10},{10,... | collective-permute-start | bytes 98312 | tf_op jit(solution)/shard_map/ppermute | solution.py:48
  4.4 5.1 %collective-permute-start.1 = (bf16[32,512]{1,0:T(8,128)(2,1)S(1)}, bf16[32,512]{1,0:T(8,128)(2,1)S(1)}, u32[]{:S(2)}, u32[]{:S(2)}) collective-permute-start(bf16[32,512]{1,0:T(8,128)(2,1)S(1)} %pack_body.1.refs_0_), channel_id=1, source_target_pairs={{0,2},{1,3},{2,0},{3,1},{4,6},{5,7},{6,4},{7,5},{8,10},{9,11},{10,... | collective-permute-start | bytes 98312 | tf_op jit(solution)/shard_map/ppermute | solution.py:48
  5.0 4.5 %collective-permute-start = (bf16[32,512]{1,0:T(8,128)(2,1)S(1)}, bf16[32,512]{1,0:T(8,128)(2,1)S(1)}, u32[]{:S(2)}, u32[]{:S(2)}) collective-permute-start(bf16[32,512]{1,0:T(8,128)(2,1)S(1)} %pack_body.1.refs_0_), channel_id=1, source_target_pairs={{0,1},{1,0},{2,3},{3,2},{4,5},{5,4},{6,7},{7,6},{8,9},{9,8},{10,11... | collective-permute-start | bytes 98312 | tf_op jit(solution)/shard_map/ppermute | solution.py:48
  5.1 30.9 %copy-start = (bf16[1,2048,256]{2,1,0:T(8,128)(2,1)S(1)}, bf16[1,2048,256]{2,1,0:T(8,128)(2,1)}, u32[]{:S(2)}) copy-start(bf16[1,2048,256]{2,1,0:T(8,128)(2,1)} %param.6) | copy-start | bytes 3145732
  5.1 30.9 %copy-start.9 = (s32[512]{0:T(512)S(1)}, s32[512]{0:T(512)}, u32[]{:S(2)}) copy-start(s32[512]{0:T(512)} %param.11) | copy-start | bytes 6148
  9.5 1.9 %copy-start.10 = (bf16[32,512]{1,0:T(8,128)(2,1)}, bf16[32,512]{1,0:T(8,128)(2,1)S(1)}, u32[]{:S(2)}) copy-start(bf16[32,512]{1,0:T(8,128)(2,1)S(1)} %collective-permute-done.2.refs_3_) | copy-start | bytes 98308
  9.5 1.9 %copy-start.11 = (bf16[32,512]{1,0:T(8,128)(2,1)}, bf16[32,512]{1,0:T(8,128)(2,1)S(1)}, u32[]{:S(2)}) copy-start(bf16[32,512]{1,0:T(8,128)(2,1)S(1)} %collective-permute-done.1.refs_2_) | copy-start | bytes 98308
  9.6 1.8 %copy-start.12 = (bf16[32,512]{1,0:T(8,128)(2,1)}, bf16[32,512]{1,0:T(8,128)(2,1)S(1)}, u32[]{:S(2)}) copy-start(bf16[32,512]{1,0:T(8,128)(2,1)S(1)} %collective-permute-done.refs_1_) | copy-start | bytes 98308
  9.6 22.5 %collective-permute-start.4 = (bf16[4,128,512]{2,1,0:T(8,128)(2,1)S(1)}, bf16[4,128,512]{2,1,0:T(8,128)(2,1)S(1)}, u32[]{:S(2)}, u32[]{:S(2)}) collective-permute-start(bf16[4,128,512]{2,1,0:T(8,128)(2,1)S(1)} %copy-done.3), channel_id=1, source_target_pairs={{0,2},{1,3},{2,0},{3,1},{4,6},{5,7},{6,4},{7,5},{8,10},{9,11},{10,... | collective-permute-start | bytes 1572872 | tf_op jit(solution)/shard_map/ppermute | solution.py:48
  16.1 26.3 %copy-start.15 = (bf16[4,64,256]{2,1,0:T(8,128)(2,1)S(1)}, bf16[4,64,256]{2,1,0:T(8,128)(2,1)}, u32[]{:S(2)}) copy-start(bf16[4,64,256]{2,1,0:T(8,128)(2,1)} %get-tuple-element.67) | copy-start | bytes 393220
  16.1 28.2 %copy-start.14 = (bf16[4,64,256]{2,1,0:T(8,128)(2,1)S(1)}, bf16[4,64,256]{2,1,0:T(8,128)(2,1)}, u32[]{:S(2)}) copy-start(bf16[4,64,256]{2,1,0:T(8,128)(2,1)} %get-tuple-element.63) | copy-start | bytes 393220
  16.1 29.1 %copy-start.13 = (bf16[4,64,256]{2,1,0:T(8,128)(2,1)S(1)}, bf16[4,64,256]{2,1,0:T(8,128)(2,1)}, u32[]{:S(2)}) copy-start(bf16[4,64,256]{2,1,0:T(8,128)(2,1)} %get-tuple-element.65) | copy-start | bytes 393220
  16.1 41.3 %copy-start.5 = (bf16[4,64,256]{2,1,0:T(8,128)(2,1)S(1)}, bf16[4,64,256]{2,1,0:T(8,128)(2,1)}, u32[]{:S(2)}) copy-start(bf16[4,64,256]{2,1,0:T(8,128)(2,1)} %get-tuple-element.61.refs_0_) | copy-start | bytes 393220
  16.1 9.4 %collective-permute-start.5 = (bf16[4,64,256]{2,1,0:T(8,128)(2,1)}, bf16[4,64,256]{2,1,0:T(8,128)(2,1)S(1)}, u32[]{:S(2)}, u32[]{:S(2)}) collective-permute-start(bf16[4,64,256]{2,1,0:T(8,128)(2,1)} %get-tuple-element.49), channel_id=1, source_target_pairs={{0,28},{4,24},{8,20},{12,16},{16,12},{20,8},{24,4},{28,0},{1,29},{... | collective-permute-start | bytes 393224 | tf_op jit(solution)/shard_map/ppermute | solution.py:48
  20.8 11.3 %collective-permute-start.6 = (bf16[4,64,256]{2,1,0:T(8,128)(2,1)}, bf16[4,64,256]{2,1,0:T(8,128)(2,1)S(1)}, u32[]{:S(2)}, u32[]{:S(2)}) collective-permute-start(bf16[4,64,256]{2,1,0:T(8,128)(2,1)} %get-tuple-element.50), channel_id=1, source_target_pairs={{0,16},{4,20},{8,24},{12,28},{16,0},{20,4},{24,8},{28,12},{1,17},{... | collective-permute-start | bytes 393224 | tf_op jit(solution)/shard_map/ppermute | solution.py:48
  20.8 15.2 %collective-permute-start.3 = (bf16[4,128,512]{2,1,0:T(8,128)(2,1)S(1)}, bf16[4,128,512]{2,1,0:T(8,128)(2,1)S(1)}, u32[]{:S(2)}, u32[]{:S(2)}) collective-permute-start(bf16[4,128,512]{2,1,0:T(8,128)(2,1)S(1)} %copy-done.3), channel_id=1, source_target_pairs={{0,1},{1,0},{2,3},{3,2},{4,5},{5,4},{6,7},{7,6},{8,9},{9,8},{10,11... | collective-permute-start | bytes 1572872 | tf_op jit(solution)/shard_map/ppermute | solution.py:48
  32.1 4.0 %collective-permute-start.7 = (bf16[4,128,512]{2,1,0:T(8,128)(2,1)S(1)}, bf16[4,128,512]{2,1,0:T(8,128)(2,1)S(1)}, u32[]{:S(2)}, u32[]{:S(2)}) collective-permute-start(bf16[4,128,512]{2,1,0:T(8,128)(2,1)S(1)} %collective-permute-done.4.refs_2_), channel_id=1, source_target_pairs={{0,1},{1,0},{2,3},{3,2},{4,5},{5,4},{6,7},{7,6},{8,9},{9,8},{10,11... | collective-permute-start | bytes 1572872 | tf_op jit(solution)/shard_map/ppermute | solution.py:48
  32.1 8.6 %collective-permute-start.8 = (bf16[4,64,256]{2,1,0:T(8,128)(2,1)}, bf16[4,64,256]{2,1,0:T(8,128)(2,1)S(1)}, u32[]{:S(2)}, u32[]{:S(2)}) collective-permute-start(bf16[4,64,256]{2,1,0:T(8,128)(2,1)} %get-tuple-element.56), channel_id=1, source_target_pairs={{0,12},{4,8},{8,4},{12,0},{16,28},{20,24},{24,20},{28,16},{1,13},{... | collective-permute-start | bytes 393224 | tf_op jit(solution)/shard_map/ppermute | solution.py:48
  32.1 12.2 %collective-permute-start.14 = (bf16[4,64,256]{2,1,0:T(8,128)(2,1)}, bf16[4,64,256]{2,1,0:T(8,128)(2,1)S(1)}, u32[]{:S(2)}, u32[]{:S(2)}) collective-permute-start(bf16[4,64,256]{2,1,0:T(8,128)(2,1)} %get-tuple-element.66), channel_id=1, source_target_pairs={{0,20},{4,16},{8,28},{12,24},{16,4},{20,0},{24,12},{28,8},{1,21},{... | collective-permute-start | bytes 393224 | tf_op jit(solution)/shard_map/ppermute | solution.py:48
  36.0 25.0 %copy-start.2 = (bf16[1,2048,256]{2,1,0:T(8,128)(2,1)S(1)}, bf16[1,2048,256]{2,1,0:T(8,128)(2,1)}, u32[]{:S(2)}) copy-start(bf16[1,2048,256]{2,1,0:T(8,128)(2,1)} %param.7) | copy-start | bytes 3145732
  36.1 25.0 %copy-start.4 = (bf16[4,32,512]{2,1,0:T(8,128)(2,1)S(1)}, bf16[4,32,512]{2,1,0:T(8,128)(2,1)}, u32[]{:S(2)}) copy-start(bf16[4,32,512]{2,1,0:T(8,128)(2,1)} %get-tuple-element.69.refs_5_) | copy-start | bytes 393220
  36.1 25.0 %copy-start.8 = (s32[256]{0:T(256)S(1)}, s32[256]{0:T(256)}, u32[]{:S(2)}) copy-start(s32[256]{0:T(256)} %param.10) | copy-start | bytes 3076
  38.8 6.4 %collective-permute-start.10 = (bf16[4,64,256]{2,1,0:T(8,128)(2,1)S(1)}, bf16[4,64,256]{2,1,0:T(8,128)(2,1)S(1)}, u32[]{:S(2)}, u32[]{:S(2)}) collective-permute-start(bf16[4,64,256]{2,1,0:T(8,128)(2,1)S(1)} %get-tuple-element.59), channel_id=1, source_target_pairs={{0,8},{4,12},{8,0},{12,4},{16,24},{20,28},{24,16},{28,20},{1,9},{5... | collective-permute-start | bytes 393224 | tf_op jit(solution)/shard_map/ppermute | solution.py:48
  40.7 7.2 %collective-permute-start.9 = (bf16[4,64,256]{2,1,0:T(8,128)(2,1)S(1)}, bf16[4,64,256]{2,1,0:T(8,128)(2,1)S(1)}, u32[]{:S(2)}, u32[]{:S(2)}) collective-permute-start(bf16[4,64,256]{2,1,0:T(8,128)(2,1)S(1)} %get-tuple-element.57), channel_id=1, source_target_pairs={{0,4},{4,0},{8,12},{12,8},{16,20},{20,16},{24,28},{28,24},{1,5},{5... | collective-permute-start | bytes 393224 | tf_op jit(solution)/shard_map/ppermute | solution.py:48
  41.9 10.2 %collective-permute-start.11 = (bf16[4,64,256]{2,1,0:T(8,128)(2,1)S(1)}, bf16[4,64,256]{2,1,0:T(8,128)(2,1)S(1)}, u32[]{:S(2)}, u32[]{:S(2)}) collective-permute-start(bf16[4,64,256]{2,1,0:T(8,128)(2,1)S(1)} %get-tuple-element.60), channel_id=1, source_target_pairs={{0,12},{4,8},{8,4},{12,0},{16,28},{20,24},{24,20},{28,16},{1,13},{... | collective-permute-start | bytes 393224 | tf_op jit(solution)/shard_map/ppermute | solution.py:48
  42.4 11.3 %collective-permute-start.15 = (bf16[4,64,256]{2,1,0:T(8,128)(2,1)S(1)}, bf16[4,64,256]{2,1,0:T(8,128)(2,1)S(1)}, u32[]{:S(2)}, u32[]{:S(2)}) collective-permute-start(bf16[4,64,256]{2,1,0:T(8,128)(2,1)S(1)} %copy-done.15), channel_id=1, source_target_pairs={{0,24},{4,28},{8,16},{12,20},{16,8},{20,12},{24,0},{28,4},{1,25},{... | collective-permute-start | bytes 393224 | tf_op jit(solution)/shard_map/ppermute | solution.py:48
  44.3 9.4 %collective-permute-start.12 = (bf16[4,64,256]{2,1,0:T(8,128)(2,1)S(1)}, bf16[4,64,256]{2,1,0:T(8,128)(2,1)S(1)}, u32[]{:S(2)}, u32[]{:S(2)}) collective-permute-start(bf16[4,64,256]{2,1,0:T(8,128)(2,1)S(1)} %copy-done.14), channel_id=1, source_target_pairs={{0,4},{4,0},{8,12},{12,8},{16,20},{20,16},{24,28},{28,24},{1,5},{5... | collective-permute-start | bytes 393224 | tf_op jit(solution)/shard_map/ppermute | solution.py:48
  45.2 12.2 %collective-permute-start.13 = (bf16[4,64,256]{2,1,0:T(8,128)(2,1)S(1)}, bf16[4,64,256]{2,1,0:T(8,128)(2,1)S(1)}, u32[]{:S(2)}, u32[]{:S(2)}) collective-permute-start(bf16[4,64,256]{2,1,0:T(8,128)(2,1)S(1)} %copy-done.13), channel_id=1, source_target_pairs={{0,8},{4,12},{8,0},{12,4},{16,24},{20,28},{24,16},{28,20},{1,9},{5... | collective-permute-start | bytes 393224 | tf_op jit(solution)/shard_map/ppermute | solution.py:48
  47.9 12.5 %collective-permute-start.18 = (bf16[4,64,256]{2,1,0:T(8,128)(2,1)S(1)}, bf16[4,64,256]{2,1,0:T(8,128)(2,1)S(1)}, u32[]{:S(2)}, u32[]{:S(2)}) collective-permute-start(bf16[4,64,256]{2,1,0:T(8,128)(2,1)S(1)} %get-tuple-element.74), channel_id=1, source_target_pairs={{0,24},{4,28},{8,16},{12,20},{16,8},{20,12},{24,0},{28,4},{1,25},{... | collective-permute-start | bytes 393224 | tf_op jit(solution)/shard_map/ppermute | solution.py:48
  52.1 8.4 %collective-permute-start.19 = (bf16[4,64,256]{2,1,0:T(8,128)(2,1)S(1)}, bf16[4,64,256]{2,1,0:T(8,128)(2,1)S(1)}, u32[]{:S(2)}, u32[]{:S(2)}) collective-permute-start(bf16[4,64,256]{2,1,0:T(8,128)(2,1)S(1)} %get-tuple-element.75), channel_id=1, source_target_pairs={{0,28},{4,24},{8,20},{12,16},{16,12},{20,8},{24,4},{28,0},{1,29},{... | collective-permute-start | bytes 393224 | tf_op jit(solution)/shard_map/ppermute | solution.py:48
  60.5 3.9 %collective-permute-start.21 = (bf16[4,128,512]{2,1,0:T(8,128)(2,1)S(1)}, bf16[4,128,512]{2,1,0:T(8,128)(2,1)S(1)}, u32[]{:S(2)}, u32[]{:S(2)}) collective-permute-start(bf16[4,128,512]{2,1,0:T(8,128)(2,1)S(1)} %get-tuple-element.85), channel_id=1, source_target_pairs={{0,1},{1,0},{2,3},{3,2},{4,5},{5,4},{6,7},{7,6},{8,9},{9,8},{10,11... | collective-permute-start | bytes 1572872 | tf_op jit(solution)/shard_map/ppermute | solution.py:48
  60.6 3.8 %collective-permute-start.20 = (bf16[4,128,512]{2,1,0:T(8,128)(2,1)S(1)}, bf16[4,128,512]{2,1,0:T(8,128)(2,1)S(1)}, u32[]{:S(2)}, u32[]{:S(2)}) collective-permute-start(bf16[4,128,512]{2,1,0:T(8,128)(2,1)S(1)} %get-tuple-element.83), channel_id=1, source_target_pairs={{0,1},{1,0},{2,3},{3,2},{4,5},{5,4},{6,7},{7,6},{8,9},{9,8},{10,11... | collective-permute-start | bytes 1572872 | tf_op jit(solution)/shard_map/ppermute | solution.py:48
  64.4 16.7 %copy-start.1 = (bf16[2048,256]{1,0:T(8,128)(2,1)S(1)}, bf16[2048,256]{1,0:T(8,128)(2,1)}, u32[]{:S(2)}) copy-start(bf16[2048,256]{1,0:T(8,128)(2,1)} %gate_body.1.refs_4_.refs_8_) | copy-start | bytes 3145732
  64.6 22.5 %collective-permute-start.22 = (bf16[4,128,512]{2,1,0:T(8,128)(2,1)S(1)}, bf16[4,128,512]{2,1,0:T(8,128)(2,1)S(1)}, u32[]{:S(2)}, u32[]{:S(2)}) collective-permute-start(bf16[4,128,512]{2,1,0:T(8,128)(2,1)S(1)} %get-tuple-element.87), channel_id=1, source_target_pairs={{0,2},{1,3},{2,0},{3,1},{4,6},{5,7},{6,4},{7,5},{8,10},{9,11},{10,... | collective-permute-start | bytes 1572872 | tf_op jit(solution)/shard_map/ppermute | solution.py:48
  65.5 13.6 %collective-permute-start.16 = (bf16[4,64,256]{2,1,0:T(8,128)(2,1)S(1)}, bf16[4,64,256]{2,1,0:T(8,128)(2,1)S(1)}, u32[]{:S(2)}, u32[]{:S(2)}) collective-permute-start(bf16[4,64,256]{2,1,0:T(8,128)(2,1)S(1)} %get-tuple-element.72), channel_id=1, source_target_pairs={{0,16},{4,20},{8,24},{12,28},{16,0},{20,4},{24,8},{28,12},{1,17},{... | collective-permute-start | bytes 393224 | tf_op jit(solution)/shard_map/ppermute | solution.py:48
  69.1 11.9 %collective-permute-start.17 = (bf16[4,64,256]{2,1,0:T(8,128)(2,1)S(1)}, bf16[4,64,256]{2,1,0:T(8,128)(2,1)S(1)}, u32[]{:S(2)}, u32[]{:S(2)}) collective-permute-start(bf16[4,64,256]{2,1,0:T(8,128)(2,1)S(1)} %get-tuple-element.73), channel_id=1, source_target_pairs={{0,20},{4,16},{8,28},{12,24},{16,4},{20,0},{24,12},{28,8},{1,21},{... | collective-permute-start | bytes 393224 | tf_op jit(solution)/shard_map/ppermute | solution.py:48
  82.5 5.6 %collective-permute-start.23 = (bf16[32,512]{1,0:T(8,128)(2,1)S(1)}, bf16[32,512]{1,0:T(8,128)(2,1)S(1)}, u32[]{:S(2)}, u32[]{:S(2)}) collective-permute-start(bf16[32,512]{1,0:T(8,128)(2,1)S(1)} %get-tuple-element.90), channel_id=1, source_target_pairs={{0,1},{1,0},{2,3},{3,2},{4,5},{5,4},{6,7},{7,6},{8,9},{9,8},{10,11... | collective-permute-start | bytes 98312 | tf_op jit(solution)/shard_map/ppermute | solution.py:48
  82.6 5.5 %collective-permute-start.24 = (bf16[32,512]{1,0:T(8,128)(2,1)S(1)}, bf16[32,512]{1,0:T(8,128)(2,1)S(1)}, u32[]{:S(2)}, u32[]{:S(2)}) collective-permute-start(bf16[32,512]{1,0:T(8,128)(2,1)S(1)} %get-tuple-element.91), channel_id=1, source_target_pairs={{0,2},{1,3},{2,0},{3,1},{4,6},{5,7},{6,4},{7,5},{8,10},{9,11},{10,... | collective-permute-start | bytes 98312 | tf_op jit(solution)/shard_map/ppermute | solution.py:48
  83.9 4.2 %collective-permute-start.25 = (bf16[32,512]{1,0:T(8,128)(2,1)S(1)}, bf16[32,512]{1,0:T(8,128)(2,1)S(1)}, u32[]{:S(2)}, u32[]{:S(2)}) collective-permute-start(bf16[32,512]{1,0:T(8,128)(2,1)S(1)} %get-tuple-element.92), channel_id=1, source_target_pairs={{0,3},{1,2},{2,1},{3,0},{4,7},{5,6},{6,5},{7,4},{8,11},{9,10},{10,... | collective-permute-start | bytes 98312 | tf_op jit(solution)/shard_map/ppermute | solution.py:48

commit v4 on v3

--- a/solution.py
+++ b/solution.py
@@ -10,7 +10,7 @@
 BF16 = jnp.bfloat16
 F32 = jnp.float32
 LANE_GROUP = 16
-CFG = {'cost': {}, 'direct': False, 'rsdirect': False, 'f2early': False, 'order': [[7, 6, 5, 4, 3, 2, 1], [7, 6, 5, 4, 3, 2, 1]], 'deps': {'h3': ['h7'], 'h2': ['h7'], 'h1': ['h7'], 'fx': ['h7', 'h4'], 'F1': ['M', 'H1', 'H2', 'H3', 'fx'], 'near': ['H7', 'H6'], 'far': ['H7', 'H6'], 'pair': ['F2'], 'unpack': ['add'], 'H1': ['h3'], 'H2': ['M']}}
+CFG = {'cost': {}, 'direct': False, 'rsdirect': False, 'f2early': False, 'order': [[7, 6, 5, 4, 3, 2, 1], [7, 6, 5, 4, 3, 2, 1]], 'deps': {'h3': ['h7'], 'h2': ['h7'], 'h1': ['h7'], 'fx': ['A2'], 'F1': ['M'], 'pair': ['F2'], 'unpack': ['add']}, 'a2a': [True, True]}
 
 
 def iota(shape, dim):
@@ -67,57 +67,23 @@
         out_ref[g * m_here : (g + 1) * m_here, :] = packed.astype(BF16)
 
 
-def gate_body(step, x_hbm, cot_hbm, src_ref, dz_hbm, x_scr, cot_scr, dz_scr, sems):
-    rows, width = x_scr.shape
-    parts = rows // step
-    reads, writes = [], []
-    for n in range(parts):
-        part = pl.ds(n * step, step)
-        reads.append(pltpu.make_async_copy(x_hbm.at[part, :], x_scr.at[part, :], sems.at[0, n]))
-        reads.append(pltpu.make_async_copy(cot_hbm.at[part, :], cot_scr.at[part, :], sems.at[1, n]))
-        writes.append(pltpu.make_async_copy(dz_scr.at[part, :], dz_hbm.at[part, :], sems.at[2, n]))
-    for copy in reads:
-        copy.start()
+def gate_body(x_ref, cot_ref, src_ref, dz_ref):
+    rows, width = x_ref.shape
+    step = min(rows, 512)
     select = one_hot(iota((width, width), 0) == src_ref[...])
-    for n in range(parts):
-        reads[2 * n].wait()
-        reads[2 * n + 1].wait()
+    for n in range(rows // step):
         part = slice(n * step, (n + 1) * step)
-        gate = jax.nn.sigmoid(dot(x_scr[part, :], select))
-        dz_scr[part, :] = (cot_scr[part, :].astype(F32) * gate).astype(BF16)
-        writes[n].start()
-    for copy in writes:
-        copy.wait()
-
-
-def gate_call(x, cot, src):
-    rows, width = x.shape
-    step = min(rows, 256)
-    left = pl.BlockSpec(memory_space=pltpu.HBM)
-    return pl.pallas_call(
-        functools.partial(gate_body, step),
-        name="gate_body",
-        out_shape=of((rows, width)),
-        in_specs=[left, left, pl.BlockSpec(memory_space=pltpu.VMEM)],
-        out_specs=left,
-        scratch_shapes=[pltpu.VMEM((rows, width), BF16)] * 3 + [pltpu.SemaphoreType.DMA((3, rows // step))],
-        compiler_params=pltpu.CompilerParams(vmem_limit_bytes=60 << 20),
-        cost_estimate=pl.CostEstimate(flops=0, bytes_accessed=0, transcendentals=0),
-    )(x, cot, src)
+        gate = jax.nn.sigmoid(dot(x_ref[part, :], select))
+        dz_ref[part, :] = (cot_ref[part, :].astype(F32) * gate).astype(BF16)
 
 
 def regroup_back_body(batch, seq, order, *refs):
-    pieces, dz_hbm = refs[:batch], refs[batch]
-    outs, second_ref, d_scr, r_scr, dz_ref, sems = refs[batch + 1 : -5], *refs[-5:]
+    pieces, dz_ref = refs[:batch], refs[batch]
+    outs, second_ref, d_scr, r_scr = refs[batch + 1 : -3], *refs[-3:]
     me, here = lax.axis_index("batch"), lax.axis_index("seq")
     groups = second_ref.shape[0]
     lanes = order * LANE_GROUP
     m_here = order // batch
-    reads = []
-    for g in range(groups):
-        part = pl.ds(g * lanes, lanes)
-        reads.append(pltpu.make_async_copy(dz_hbm.at[part, :], dz_ref.at[part, :], sems.at[g]))
-        reads[g].start()
     for d in range(batch):
         piece = pieces[d][...].astype(F32)
         first = pl.multiple_of((me ^ d) * m_here, m_here)
@@ -130,13 +96,15 @@
         packed = d_scr[g].astype(BF16)
         second_ref[g] = packed
         weights = jnp.where(keep, dot(packed, tiled, 0, 0), 0.0).astype(BF16)
-        reads[g].wait()
         result = dot(weights, dz_ref[g * lanes : (g + 1) * lanes, :]).astype(BF16)
         r_scr[:, g * LANE_GROUP : (g + 1) * LANE_GROUP, :] = result.reshape(order, LANE_GROUP, width)
 
     blocks = order // seq
-    for d in range(seq):
-        outs[d][...] = r_scr[pl.ds((here ^ d) * blocks, blocks)]
+    if len(outs) == 1:
+        outs[0][...] = r_scr[...].reshape(outs[0].shape)
+    else:
+        for d in range(seq):
+            outs[d][...] = r_scr[pl.ds((here ^ d) * blocks, blocks)]
 
 
 def mix_body(batch, seq, *refs):
@@ -155,26 +123,33 @@
             first = pl.multiple_of((me ^ d) * rows, rows)
             mix_scr[pl.ds(first, rows), :] = dot(pieces[d][i], x).astype(BF16)
         reg_scr[...] = dot(p_scr[...], mix_scr[...]).astype(BF16)
-        for d in range(seq):
-            first = pl.multiple_of((here ^ d) * j_here, j_here)
-            outs[d][i] = reg_scr[pl.ds(first, j_here), :]
+        if len(outs) == 1:
+            outs[0][:, i] = reg_scr[...].reshape(seq, j_here, x.shape[1])
+        else:
+            for d in range(seq):
+                first = pl.multiple_of((here ^ d) * j_here, j_here)
+                outs[d][i] = reg_scr[pl.ds(first, j_here), :]
 
 
 def first_grad_body(batch, seq, *refs):
-    pieces, x_ref, alt_ref = refs[:seq], refs[seq], refs[seq + 1]
-    outs, dmixed_ref = refs[seq + 2 : seq + 2 + batch], refs[seq + 2 + batch]
+    count = len(refs) - batch - 6
+    pieces, x_ref, alt_ref = refs[:count], refs[count], refs[count + 1]
+    outs, dmixed_ref = refs[count + 2 : count + 2 + batch], refs[count + 2 + batch]
     p_scr, reg_scr, part_scr = refs[-3:]
     me, here = lax.axis_index("batch"), lax.axis_index("seq")
-    blocks, j_here, width = pieces[0].shape
+    blocks, j_here, width = pieces[0].shape[-3:]
     order = j_here * seq
     rows = order // batch
     p_scr[...] = one_hot(iota((order, order), 0) == alt_ref[...])
 
     @pl.loop(0, blocks)
     def _(i):
-        for d in range(seq):
-            first = pl.multiple_of((here ^ d) * j_here, j_here)
-            reg_scr[pl.ds(first, j_here), :] = pieces[d][i]
+        if count == 1:
+            reg_scr[...] = pieces[0][:, i].reshape(order, width)
+        else:
+            for d in range(seq):
+                first = pl.multiple_of((here ^ d) * j_here, j_here)
+                reg_scr[pl.ds(first, j_here), :] = pieces[d][i]
         dmixed = dot(p_scr[...], reg_scr[...]).astype(BF16)
         dmixed_ref[i] = dmixed
         x = x_ref[pl.ds(pl.multiple_of(i * order, order), order), :]
@@ -225,12 +200,18 @@
 
 
 def second_grad_body(batch, seq, *refs):
-    pieces, dz_ref = refs[:seq], refs[seq]
-    outs, reg_ref, y_scr = refs[seq + 1 : seq + 1 + batch], refs[-2], refs[-1]
+    count = len(refs) - batch - 3 if len(refs) > batch + 4 else 1
+    if count == 1:
+        pieces, dz_ref = refs[:1], refs[1]
+        outs, reg_ref, y_scr = refs[2 : 2 + batch], refs[0], refs[-1]
+    else:
+        pieces, dz_ref = refs[:seq], refs[seq]
+        outs, reg_ref, y_scr = refs[seq + 1 : seq + 1 + batch], refs[-2], refs[-1]
     me = lax.axis_index("batch")
     order, j_here, width = reg_ref.shape
     groups, lanes, m_here = j_here // LANE_GROUP, order * LANE_GROUP, order // batch
-    gather_blocks(seq, pieces, reg_ref)
+    if count > 1:
+        gather_blocks(seq, pieces, reg_ref)
 
     @pl.loop(0, groups)
     def _(g):
@@ -322,7 +303,8 @@
     packed = {0: mine}
     for d in (3, 2, 1):
         packed[d] = move(f"D{d}", mine, "batch", d, batch)
-    dz = keep("gate", gate_call(x, cot, src))
+    (dz,) = call(gate_body, [of((rows_here, width))], [x, cot, src], limit=16 << 20)
+    keep("gate", dz)
     first_ready = after(first_factor, dz) if CFG['f2early'] else after(first_factor, dz, *[packed[d] for d in (1, 2, 3)])
     across = move("f2", first_ready, "batch", 2, batch)
     beside = move("f1", first_ready, "batch", 1, batch)
@@ -330,38 +312,40 @@
     piece = of((blocks, j_here, width))
     *back, second = call(
         functools.partial(regroup_back_body, batch, seq, count),
-        [piece] * seq + [of((groups, count, lanes))],
+        ([of((seq, blocks, j_here, width))] if CFG['a2a'][0] else [piece] * seq) + [of((groups, count, lanes))],
         [*[packed[d] for d in range(batch)], dz],
         [
             pltpu.VMEM((groups, count, lanes), F32),
             pltpu.VMEM((count, j_here, width), BF16),
-            pltpu.VMEM((rows_here, width), BF16),
-            pltpu.SemaphoreType.DMA((groups,)),
         ],
-        spaces={batch: pltpu.HBM},
-        limit=56 << 20,
     )
     keep("A2", back[0])
     back_got = {0: back[0]}
-    for d in CFG['order'][0]:
-        back_got[d] = move(f"h{d}", back[d], "seq", d, seq)
+    if CFG['a2a'][0]:
+        back_got[0] = keep("h0", lax.all_to_all(dep("h0", back[0]), "seq", 0, 0, tiled=True))
+    else:
+        for d in CFG['order'][0]:
+            back_got[d] = move(f"h{d}", back[d], "seq", d, seq)
     if direct is None:
         direct = move("fx", across, "batch", 1, batch)
     first = [first_factor, beside, across, direct]
     regrouped = call(
         functools.partial(mix_body, batch, seq),
-        [piece] * seq,
+        [of((seq, blocks, j_here, width))] if CFG['a2a'][1] else [piece] * seq,
         [dep("M", first_factor), *first[1:], x, alt],
         [pltpu.VMEM((order, order), BF16), pltpu.VMEM((order, width), BF16), pltpu.VMEM((order, width), BF16)],
     )
     keep("M", regrouped[0])
     got = {0: regrouped[0]}
-    for d in CFG['order'][1]:
-        got[d] = move(f"H{d}", regrouped[d], "seq", d, seq)
+    if CFG['a2a'][1]:
+        got[0] = keep("H0", lax.all_to_all(dep("H0", regrouped[0]), "seq", 0, 0, tiled=True))
+    else:
+        for d in CFG['order'][1]:
+            got[d] = move(f"H{d}", regrouped[d], "seq", d, seq)
     *parts, dmixed = call(
         functools.partial(first_grad_body, batch, seq),
         [of((blocks, k_here, order))] * batch + [of((blocks, order, width))],
-        [dep("F1", back_got[0]), *[back_got[d] for d in range(1, seq)], x, alt],
+        [dep("F1", back_got[0]), *[back_got[d] for d in range(1, seq) if d in back_got], x, alt],
         [pltpu.VMEM((order, order), BF16), pltpu.VMEM((order, width), BF16), pltpu.VMEM((order, order), BF16)],
     )
     keep("F1", dmixed)
@@ -386,12 +370,17 @@
         rx = move("rx", summed, "batch", 2, batch)
         (grad_one,) = call(add_body, [of(parts[0].shape)], [kept, rx])
     keep("add", grad_one)
+    received = [after(got[0], dmix_in), *[got[d] for d in range(1, seq) if d in got]]
+    if len(received) == 1:
+        received = [received[0].reshape(count, j_here, width)]
     *terms, gathered = call(
         functools.partial(second_grad_body, batch, seq),
-        [of((groups * m_here, lanes))] * batch + [of((count, j_here, width))],
-        [after(got[0], dmix_in), *[got[d] for d in range(1, seq)], dz],
+        [of((groups * m_here, lanes))] * batch + ([of((count, j_here, width))] if len(received) > 1 else []),
+        [*received, dz],
         [pltpu.VMEM((groups, count, lanes), F32)],
     )
+    if len(received) == 1:
+        terms, gathered = [*terms, gathered], received[0]
     terms_got = [dep("unpack", terms[0])] + [move(f"R{d}", terms[d], "batch", d, batch) for d in (1, 2, 3)]
     (grad_tokens,) = call(
         tokens_body, [of((rows_here, width))], [gathered, weights, h, src, dmix_in]

time: 89.4 us -> 85.2 us (0.953)
  local copies, waits for them, and re-layouts: 0.96 us -> 18.4 us
  starting transfers between devices: 31.1 us -> 18.2 us
  Pallas kernels: 24.9 us -> 19.3 us
  waiting for transfers between devices: 31.2 us -> 27.8 us
    ppermute x26 -> x12, starting transfers between devices: 31.1 us -> 8.5 us  [swap(): return lax.ppermute(value, axis, [(p, p ^ step) for p in range(size)])]
    unnamed x32 -> x52, local copies, waits for them, and re-layouts: 0.96 us -> 18.4 us
    ppermute x26 -> x12, waiting for transfers between devices: 31.2 us -> 14.4 us  [swap(): return lax.ppermute(value, axis, [(p, p ^ step) for p in range(size)])]
    all_to_all x0 -> x2, waiting for transfers between devices: none -> 13.4 us  [the longest x1 10.2 us: packed_shards(): lax.all_to_all(dep('H0', regrouped[0]), 'seq', 0, 0, tiled=True)]
    all_to_all x0 -> x2, starting transfers between devices: none -> 9.73 us  [the longest x1 6.09 us: packed_shards(): lax.all_to_all(dep('h0', back[0]), 'seq', 0, 0, tiled=True)]
    pallas_call x1 -> x0, Pallas kernels: 4.4 us -> none  [gate_call(): pl.pallas_call(functools.partial(gate_body, step), name='gate_body', out_...]
    pallas_call x10 -> x11, Pallas kernels: 20.5 us -> 19.3 us  [call(): pl.pallas_call(body, name=name, out_shape=outs, in_specs=[pl.BlockSpec(me...]
  transfers between devices with their start and end apart: 26 -> 14, of which waited for: 9 -> 4; matrix products, arithmetic and copies ran while one was open for 0% -> 0% of each run, Pallas kernels for 26% -> 19%
where the time goes in v4:
time: 85.2 us; the launch traced here: 84.5 us
  waiting for transfers between devices  27.8 us (33%)
  Pallas kernels  19.3 us (23%)
  local copies, waits for them, and re-layouts  18.4 us (22%)
  starting transfers between devices  18.2 us (21%)
    pallas_call x11, Pallas kernels, call(): pl.pallas_call(body, name=name, out_shape=outs, in_specs=[pl.BlockSpec(me...  19.3 us
    unnamed x52, local copies, waits for them, and re-layouts  18.4 us
    ppermute x12, waiting for transfers between devices, swap(): return lax.ppermute(value, axis, [(p, p ^ step) for p in range(size)])  14.4 us
    all_to_all x1, waiting for transfers between devices, packed_shards(): lax.all_to_all(dep('H0', regrouped[0]), 'seq', 0, 0, tiled=True)  10.2 us
    ppermute x12, starting transfers between devices, swap(): return lax.ppermute(value, axis, [(p, p ^ step) for p in range(size)])  8.5 us
    all_to_all x1, starting transfers between devices, packed_shards(): lax.all_to_all(dep('h0', back[0]), 'seq', 0, 0, tiled=True)  6.09 us
    all_to_all x1, starting transfers between devices, packed_shards(): lax.all_to_all(dep('H0', regrouped[0]), 'seq', 0, 0, tiled=True)  3.64 us
    all_to_all x1, waiting for transfers between devices, packed_shards(): lax.all_to_all(dep('h0', back[0]), 'seq', 0, 0, tiled=True)  3.19 us
  transfers between devices with their start and end apart: 14, of which 4 were waited for; matrix products, arithmetic and copies ran while one was open for 0% of the time, Pallas kernels for 19%

profile of v4, /device:TPU:0, one launch (start us, length us, event | category | flops | bytes accessed | tf_op | source)
XLA Modules:
  0.0 84.5 jit_solution(8319532050428046198)
XLA Ops:
  0.6 0.0 copy-start.22
  0.6 0.8 copy-done.22
  1.5 0.4 pack_body.1.refs_0_
  1.9 2.4 %collective-permute-start.2 = (bf16[32,512]{1,0:T(8,128)(2,1)S(1)}, bf16[32,512]{1,0:T(8,128)(2,1)S(1)}, u32[]{:S(2)}, u32[]{:S(2)}) collective-permute-start(bf16[32,512]{1,0:T(8,128)(2,1)S(1)} %pack_body.1.refs_0_), channel_id=1, source_target_pairs={{0,3},{1,2},{2,1},{3,0},{4,7},{5,6},{6,5},{7,4},{8,11},{9,10},{10,... | collective-permute-start | bytes 98312 | tf_op jit(solution)/shard_map/ppermute | solution.py:48
  4.3 0.6 collective-permute-start.1
  5.0 0.0 collective-permute-start
  5.0 1.2 %copy-done = bf16[1,2048,256]{2,1,0:T(8,128)(2,1)S(1)} copy-done((bf16[1,2048,256]{2,1,0:T(8,128)(2,1)S(1)}, bf16[1,2048,256]{2,1,0:T(8,128)(2,1)}, u32[]{:S(2)}) %copy-start) | copy-done | bytes 1048600
  6.2 1.2 %copy-done.4 = bf16[1,2048,256]{2,1,0:T(8,128)(2,1)S(1)} copy-done((bf16[1,2048,256]{2,1,0:T(8,128)(2,1)S(1)}, bf16[1,2048,256]{2,1,0:T(8,128)(2,1)}, u32[]{:S(2)}) %copy-start.4) | copy-done | bytes 1048600
  7.5 0.7 copy-done.23
  8.1 0.5 gate_body.1.refs_4_.refs_1_
  8.6 0.0 copy-start.1
  8.6 0.0 copy-start.25
  8.7 0.0 collective-permute-done.2.refs_3_
  8.7 0.0 collective-permute-done.1.refs_2_
  8.7 0.0 collective-permute-done.refs_1_
  8.7 1.4 %regroup_back_body.1 = (bf16[8,4,64,256]{3,2,1,0:T(8,128)(2,1)S(1)}, bf16[4,32,512]{2,1,0:T(8,128)(2,1)S(1)}) custom-call(bf16[32,512]{1,0:T(8,128)(2,1)S(1)} %pack_body.1.refs_0_, bf16[32,512]{1,0:T(8,128)(2,1)S(1)} %collective-permute-done.refs_1_, bf16[32,512]{1,0:T(8,128)(2,1)S(1)} %collective-permute-done.1.refs_2_, ...), custom_call_target="tpu_custom_call" | custom-call | tf_op jit(solution)/shard_map/regroup_back_body/pallas_call | solution.py:31
  10.1 0.0 copy-start.21
  10.1 1.0 %copy-done.21 = bf16[8,4,64,256]{3,2,1,0:T(8,128)(2,1)} copy-done((bf16[8,4,64,256]{3,2,1,0:T(8,128)(2,1)}, bf16[8,4,64,256]{3,2,1,0:T(8,128)(2,1)S(1)}, u32[]{:S(2)}) %copy-start.21) | copy-done | bytes 1048600
  11.1 6.1 %all-to-all-start.1 = ((bf16[8,4,64,256]{3,2,1,0:T(8,128)(2,1)}), bf16[8,4,64,256]{3,2,1,0:T(8,128)(2,1)S(1)}, u32[]{:S(2)}, u32[]{:S(2)}) async-start(bf16[8,4,64,256]{3,2,1,0:T(8,128)(2,1)} %copy-done.21), calls=%async_computation.1 | async-start | bytes 2097152 | tf_op jit(solution)/shard_map/all_to_all | solution.py:325
  17.2 1.5 %collective-permute-start.4 = (bf16[4,128,512]{2,1,0:T(8,128)(2,1)}, bf16[4,128,512]{2,1,0:T(8,128)(2,1)S(1)}, u32[]{:S(2)}, u32[]{:S(2)}) collective-permute-start(bf16[4,128,512]{2,1,0:T(8,128)(2,1)} %refs_0_.3), channel_id=1, source_target_pairs={{0,2},{1,3},{2,0},{3,1},{4,6},{5,7},{6,4},{7,5},{8,10},{9,11},{10,... | collective-permute-start | bytes 1572872 | tf_op jit(solution)/shard_map/ppermute | solution.py:48
  18.7 0.0 collective-permute-start.3
  18.7 12.5 %collective-permute-done.4.refs_2_ = bf16[4,128,512]{2,1,0:T(8,128)(2,1)S(1)} collective-permute-done((bf16[4,128,512]{2,1,0:T(8,128)(2,1)}, bf16[4,128,512]{2,1,0:T(8,128)(2,1)S(1)}, u32[]{:S(2)}, u32[]{:S(2)}) %collective-permute-start.4) | collective-permute-done | bytes 524320 | tf_op jit(solution)/shard_map/ppermute | solution.py:48
  31.2 0.0 collective-permute-start.5
  31.2 0.0 collective-permute-done.3.refs_1_
  31.2 1.9 %collective-permute-done.5.refs_3_ = bf16[4,128,512]{2,1,0:T(8,128)(2,1)S(1)} collective-permute-done((bf16[4,128,512]{2,1,0:T(8,128)(2,1)S(1)}, bf16[4,128,512]{2,1,0:T(8,128)(2,1)S(1)}, u32[]{:S(2)}, u32[]{:S(2)}) %collective-permute-start.5) | collective-permute-done | bytes 524320 | tf_op jit(solution)/shard_map/ppermute | solution.py:48
  33.1 1.0 %copy-done.13 = bf16[4,128,512]{2,1,0:T(8,128)(2,1)S(1)} copy-done((bf16[4,128,512]{2,1,0:T(8,128)(2,1)S(1)}, bf16[4,128,512]{2,1,0:T(8,128)(2,1)}, u32[]{:S(2)}) %copy-start.13) | copy-done | bytes 524312
  34.2 2.6 %mix_body.1 = bf16[8,4,64,256]{3,2,1,0:T(8,128)(2,1)S(1)} custom-call(bf16[4,128,512]{2,1,0:T(8,128)(2,1)S(1)} %copy-done.13, bf16[4,128,512]{2,1,0:T(8,128)(2,1)S(1)} %collective-permute-done.3.refs_1_, bf16[4,128,512]{2,1,0:T(8,128)(2,1)S(1)} %collective-permute-done.4.refs_2_, bf16[4,128,512]{2,1,0:T(8,128)(2,1)S(1)} %collective-permute-done.5.refs_3_, ...), custom_call_target="tpu_custom_call" | custom-call | tf_op jit(solution)/shard_map/mix_body/pallas_call | solution.py:31
  36.8 0.0 copy-start.6
  36.8 1.0 %copy-done.6 = bf16[8,4,64,256]{3,2,1,0:T(8,128)(2,1)} copy-done((bf16[8,4,64,256]{3,2,1,0:T(8,128)(2,1)}, bf16[8,4,64,256]{3,2,1,0:T(8,128)(2,1)S(1)}, u32[]{:S(2)}) %copy-start.6) | copy-done | bytes 1048600
  37.8 0.8 copy-done.15
  38.6 0.8 copy-done.17
  39.4 0.8 copy-done.19
  40.2 3.2 %all-to-all-done.1.refs_0_ = bf16[8,4,64,256]{3,2,1,0:T(8,128)(2,1)S(1)} async-done(((bf16[8,4,64,256]{3,2,1,0:T(8,128)(2,1)}), bf16[8,4,64,256]{3,2,1,0:T(8,128)(2,1)S(1)}, u32[]{:S(2)}, u32[]{:S(2)}) %all-to-all-start.1) | async-done | bytes 1048608 | tf_op jit(solution)/shard_map/all_to_all | solution.py:325
  43.4 1.0 %copy-done.2 = bf16[8,4,64,256]{3,2,1,0:T(8,128)(2,1)} copy-done((bf16[8,4,64,256]{3,2,1,0:T(8,128)(2,1)}, bf16[8,4,64,256]{3,2,1,0:T(8,128)(2,1)S(1)}, u32[]{:S(2)}) %copy-start.2) | copy-done | bytes 1048600
  44.4 3.6 %all-to-all-start = ((bf16[8,4,64,256]{3,2,1,0:T(8,128)(2,1)}), bf16[8,4,64,256]{3,2,1,0:T(8,128)(2,1)S(1)}, u32[]{:S(2)}, u32[]{:S(2)}) async-start(bf16[8,4,64,256]{3,2,1,0:T(8,128)(2,1)} %copy-done.6), calls=%async_computation | async-start | bytes 2097152 | tf_op jit(solution)/shard_map/all_to_all | solution.py:341
  48.0 1.2 %copy-done.3 = bf16[8,4,64,256]{3,2,1,0:T(8,128)(2,1)S(1)} copy-done((bf16[8,4,64,256]{3,2,1,0:T(8,128)(2,1)S(1)}, bf16[8,4,64,256]{3,2,1,0:T(8,128)(2,1)}, u32[]{:S(2)}) %copy-start.3) | copy-done | bytes 1048600
  49.3 2.9 %first_grad_body.1 = (bf16[4,128,512]{2,1,0:T(8,128)(2,1)S(1)}, bf16[4,128,512]{2,1,0:T(8,128)(2,1)S(1)}, bf16[4,128,512]{2,1,0:T(8,128)(2,1)S(1)}, bf16[4,128,5...) custom-call(bf16[8,4,64,256]{3,2,1,0:T(8,128)(2,1)S(1)} %copy-done.3, bf16[2048,256]{1,0:T(8,128)(2,1)S(1)} %bitcast.14, ...), custom_call_target="tpu_custom_call" | custom-call | tf_op jit(solution)/shard_map/first_grad_body/pallas_call | solution.py:31
  52.2 0.1 collective-permute-start.6
  52.3 0.5 collective-permute-start.7
  52.8 0.0 copy-done.24
  52.8 0.0 copy-start.18
  52.8 1.0 %copy-done.18 = bf16[4,128,512]{2,1,0:T(8,128)(2,1)S(1)} copy-done((bf16[4,128,512]{2,1,0:T(8,128)(2,1)S(1)}, bf16[4,128,512]{2,1,0:T(8,128)(2,1)}, u32[]{:S(2)}) %copy-start.18) | copy-done | bytes 524312
  53.8 1.0 %copy-done.20 = bf16[4,128,512]{2,1,0:T(8,128)(2,1)S(1)} copy-done((bf16[4,128,512]{2,1,0:T(8,128)(2,1)S(1)}, bf16[4,128,512]{2,1,0:T(8,128)(2,1)}, u32[]{:S(2)}) %copy-start.20) | copy-done | bytes 524312
  54.9 3.3 %mix_back_body.1 = (f32[2048,256]{1,0:T(8,128)S(1)}, bf16[4,512,512]{2,1,0:T(8,128)(2,1)S(1)}, f32[2048,256]{1,0:T(8,128)S(1)}) custom-call(bf16[4,128,512]{2,1,0:T(8,128)(2,1)S(1)} %copy-done.14, bf16[4,128,512]{2,1,0:T(8,128)(2,1)S(1)} %copy-done.18, bf16[4,128,512]{2,1,0:T(8,128)(2,1)S(1)} %copy-done.16, bf16[4,128,512]{2,1,0:T(8,128)(2,1)S(1)} %copy-done.20, ...), custom_call_target="tpu_custom_call" | custom-call | tf_op jit(solution)/shard_map/mix_back_body/pallas_call | solution.py:31
  58.2 1.4 %copy-done.7 = f32[2048,256]{1,0:T(8,128)} copy-done((f32[2048,256]{1,0:T(8,128)}, f32[2048,256]{1,0:T(8,128)S(1)}, u32[]{:S(2)}) %copy-start.7) | copy-done | bytes 2097176
  59.6 1.3 %copy-done.9 = bf16[4,512,512]{2,1,0:T(8,128)(2,1)} copy-done((bf16[4,512,512]{2,1,0:T(8,128)(2,1)}, bf16[4,512,512]{2,1,0:T(8,128)(2,1)S(1)}, u32[]{:S(2)}) %copy-start.9) | copy-done | bytes 2097176
  60.9 0.0 collective-permute-done.6.got_a
  60.9 0.0 collective-permute-done.7.got_b
  60.9 1.1 %pair_body.1 = (f32[4,128,512]{2,1,0:T(8,128)S(1)}, bf16[4,128,512]{2,1,0:T(8,128)(2,1)}) custom-call(bf16[4,128,512]{2,1,0:T(8,128)(2,1)S(1)} %get-tuple-element.36.own_a, bf16[4,128,512]{2,1,0:T(8,128)(2,1)S(1)} %get-tuple-element.37.own_b, bf16[4,128,512]{2,1,0:T(8,128)(2,1)S(1)} %collective-permute-done.6.got_a, ...), custom_call_target="tpu_custom_call" | custom-call | tf_op jit(solution)/shard_map/pair_body/pallas_call | solution.py:31
  62.0 0.4 copy-done.11
  62.4 1.4 %collective-permute-start.8 = (bf16[4,128,512]{2,1,0:T(8,128)(2,1)}, bf16[4,128,512]{2,1,0:T(8,128)(2,1)}, u32[]{:S(2)}, u32[]{:S(2)}) collective-permute-start(bf16[4,128,512]{2,1,0:T(8,128)(2,1)} %get-tuple-element.41), channel_id=1, source_target_pairs={{0,2},{1,3},{2,0},{3,1},{4,6},{5,7},{6,4},{7,5},{8,10},{9,11},{10,... | collective-permute-start | bytes 1572872 | tf_op jit(solution)/shard_map/ppermute | solution.py:48
  63.8 10.2 %all-to-all-done = bf16[8,4,64,256]{3,2,1,0:T(8,128)(2,1)S(1)} async-done(((bf16[8,4,64,256]{3,2,1,0:T(8,128)(2,1)}), bf16[8,4,64,256]{3,2,1,0:T(8,128)(2,1)S(1)}, u32[]{:S(2)}, u32[]{:S(2)}) %all-to-all-start) | async-done | bytes 1048608 | tf_op jit(solution)/shard_map/all_to_all | solution.py:341
  74.0 1.3 %second_grad_body.1 = (bf16[32,512]{1,0:T(8,128)(2,1)S(1)}, bf16[32,512]{1,0:T(8,128)(2,1)S(1)}, bf16[32,512]{1,0:T(8,128)(2,1)S(1)}, bf16[32,512]{1,0:T(8,128)(2,1)S(1)}) custom-call(bf16[32,64,256]{2,1,0:T(8,128)(2,1)S(1)} %bitcast.16, bf16[2048,256]{1,0:T(8,128)(2,1)S(1)} %gate_body.1.refs_4_.refs_1_), custom_call_target="tpu_custom_call" | custom-call | tf_op jit(solution)/shard_map/second_grad_body/pallas_call | solution.py:31
  75.3 0.1 collective-permute-start.9
  75.4 1.5 %collective-permute-start.10 = (bf16[32,512]{1,0:T(8,128)(2,1)S(1)}, bf16[32,512]{1,0:T(8,128)(2,1)S(1)}, u32[]{:S(2)}, u32[]{:S(2)}) collective-permute-start(bf16[32,512]{1,0:T(8,128)(2,1)S(1)} %get-tuple-element.45), channel_id=1, source_target_pairs={{0,2},{1,3},{2,0},{3,1},{4,6},{5,7},{6,4},{7,5},{8,10},{9,11},{10,... | collective-permute-start | bytes 98312 | tf_op jit(solution)/shard_map/ppermute | solution.py:48
  76.9 0.4 collective-permute-start.11
  77.3 0.0 collective-permute-done.8.got
  77.3 1.9 %add_body.1 = bf16[4,128,512]{2,1,0:T(8,128)(2,1)} custom-call(f32[4,128,512]{2,1,0:T(8,128)S(1)} %get-tuple-element.40.own, bf16[4,128,512]{2,1,0:T(8,128)(2,1)} %collective-permute-done.8.got), custom_call_target="tpu_custom_call" | custom-call | tf_op jit(solution)/shard_map/add_body/pallas_call | solution.py:31
  79.2 1.6 %copy-done.12 = f32[2048,256]{1,0:T(8,128)S(1)} copy-done((f32[2048,256]{1,0:T(8,128)S(1)}, f32[2048,256]{1,0:T(8,128)}, u32[]{:S(2)}) %copy-start.12) | copy-done | bytes 2097176
  80.8 2.7 %tokens_body.1 = bf16[2048,256]{1,0:T(8,128)(2,1)} custom-call(bf16[32,64,256]{2,1,0:T(8,128)(2,1)S(1)} %bitcast.17, bf16[4,512,512]{2,1,0:T(8,128)(2,1)S(1)} %copy-done.10, f32[2048,256]{1,0:T(8,128)S(1)} %copy-done.12, s32[1,256]{1,0:T(1,128)S(1)} %bitcast.23, f32[2048,256]{1,0:T(8,128)S(1)} %copy-done.8), custom_call_target="tpu_custom_call" | custom-call | tf_op jit(solution)/shard_map/tokens_body/pallas_call | solution.py:31
  83.5 0.0 collective-permute-done.9.refs_1_
  83.5 0.0 collective-permute-done.10.refs_2_
  83.5 0.0 collective-permute-done.11.refs_3_
  83.5 1.1 %unpack_body.1 = bf16[256,64]{1,0:T(8,128)(2,1)} custom-call(bf16[32,512]{1,0:T(8,128)(2,1)S(1)} %get-tuple-element.43.refs_0_, bf16[32,512]{1,0:T(8,128)(2,1)S(1)} %collective-permute-done.9.refs_1_, bf16[32,512]{1,0:T(8,128)(2,1)S(1)} %collective-permute-done.10.refs_2_, bf16[32,512]{1,0:T(8,128)(2,1)S(1)} %collective-permute-done.11.refs_3_), custom_call_target="tpu_custom_call" | custom-call | tf_op jit(solution)/shard_map/unpack_body/pallas_call | solution.py:31
  (27 shorter events, 0.0 us)
Async XLA Ops:
  0.6 0.8 copy-start.22
  1.9 6.8 %collective-permute-start.2 = (bf16[32,512]{1,0:T(8,128)(2,1)S(1)}, bf16[32,512]{1,0:T(8,128)(2,1)S(1)}, u32[]{:S(2)}, u32[]{:S(2)}) collective-permute-start(bf16[32,512]{1,0:T(8,128)(2,1)S(1)} %pack_body.1.refs_0_), channel_id=1, source_target_pairs={{0,3},{1,2},{2,1},{3,0},{4,7},{5,6},{6,5},{7,4},{8,11},{9,10},{10,... | collective-permute-start | bytes 98312 | tf_op jit(solution)/shard_map/ppermute | solution.py:48
  4.3 4.3 %collective-permute-start.1 = (bf16[32,512]{1,0:T(8,128)(2,1)S(1)}, bf16[32,512]{1,0:T(8,128)(2,1)S(1)}, u32[]{:S(2)}, u32[]{:S(2)}) collective-permute-start(bf16[32,512]{1,0:T(8,128)(2,1)S(1)} %pack_body.1.refs_0_), channel_id=1, source_target_pairs={{0,2},{1,3},{2,0},{3,1},{4,6},{5,7},{6,4},{7,5},{8,10},{9,11},{10,... | collective-permute-start | bytes 98312 | tf_op jit(solution)/shard_map/ppermute | solution.py:48
  5.0 3.7 %collective-permute-start = (bf16[32,512]{1,0:T(8,128)(2,1)S(1)}, bf16[32,512]{1,0:T(8,128)(2,1)S(1)}, u32[]{:S(2)}, u32[]{:S(2)}) collective-permute-start(bf16[32,512]{1,0:T(8,128)(2,1)S(1)} %pack_body.1.refs_0_), channel_id=1, source_target_pairs={{0,1},{1,0},{2,3},{3,2},{4,5},{5,4},{6,7},{7,6},{8,9},{9,8},{10,11... | collective-permute-start | bytes 98312 | tf_op jit(solution)/shard_map/ppermute | solution.py:48
  5.0 1.2 %copy-start = (bf16[1,2048,256]{2,1,0:T(8,128)(2,1)S(1)}, bf16[1,2048,256]{2,1,0:T(8,128)(2,1)}, u32[]{:S(2)}) copy-start(bf16[1,2048,256]{2,1,0:T(8,128)(2,1)} %param.6) | copy-start | bytes 3145732
  6.2 1.2 %copy-start.4 = (bf16[1,2048,256]{2,1,0:T(8,128)(2,1)S(1)}, bf16[1,2048,256]{2,1,0:T(8,128)(2,1)}, u32[]{:S(2)}) copy-start(bf16[1,2048,256]{2,1,0:T(8,128)(2,1)} %param.7) | copy-start | bytes 3145732
  7.5 0.7 copy-start.23
  8.6 24.5 %copy-start.1 = (bf16[1,2048,256]{2,1,0:T(8,128)(2,1)S(1)}, bf16[1,2048,256]{2,1,0:T(8,128)(2,1)}, u32[]{:S(2)}) copy-start(bf16[1,2048,256]{2,1,0:T(8,128)(2,1)} %param.6) | copy-start | bytes 3145732
  8.6 24.5 %copy-start.25 = (s32[512]{0:T(512)S(1)}, s32[512]{0:T(512)}, u32[]{:S(2)}) copy-start(s32[512]{0:T(512)} %param.11) | copy-start | bytes 6148
  10.1 1.0 %copy-start.21 = (bf16[8,4,64,256]{3,2,1,0:T(8,128)(2,1)}, bf16[8,4,64,256]{3,2,1,0:T(8,128)(2,1)S(1)}, u32[]{:S(2)}) copy-start(bf16[8,4,64,256]{3,2,1,0:T(8,128)(2,1)S(1)} %get-tuple-element.26) | copy-start | bytes 3145732
  11.1 32.2 %all-to-all-start.1 = ((bf16[8,4,64,256]{3,2,1,0:T(8,128)(2,1)}), bf16[8,4,64,256]{3,2,1,0:T(8,128)(2,1)S(1)}, u32[]{:S(2)}, u32[]{:S(2)}) async-start(bf16[8,4,64,256]{3,2,1,0:T(8,128)(2,1)} %copy-done.21), calls=%async_computation.1 | async-start | bytes 2097152 | tf_op jit(solution)/shard_map/all_to_all | solution.py:325
  17.2 14.0 %collective-permute-start.4 = (bf16[4,128,512]{2,1,0:T(8,128)(2,1)}, bf16[4,128,512]{2,1,0:T(8,128)(2,1)S(1)}, u32[]{:S(2)}, u32[]{:S(2)}) collective-permute-start(bf16[4,128,512]{2,1,0:T(8,128)(2,1)} %refs_0_.3), channel_id=1, source_target_pairs={{0,2},{1,3},{2,0},{3,1},{4,6},{5,7},{6,4},{7,5},{8,10},{9,11},{10,... | collective-permute-start | bytes 1572872 | tf_op jit(solution)/shard_map/ppermute | solution.py:48
  18.7 12.5 %collective-permute-start.3 = (bf16[4,128,512]{2,1,0:T(8,128)(2,1)}, bf16[4,128,512]{2,1,0:T(8,128)(2,1)S(1)}, u32[]{:S(2)}, u32[]{:S(2)}) collective-permute-start(bf16[4,128,512]{2,1,0:T(8,128)(2,1)} %refs_0_.3), channel_id=1, source_target_pairs={{0,1},{1,0},{2,3},{3,2},{4,5},{5,4},{6,7},{7,6},{8,9},{9,8},{10,11... | collective-permute-start | bytes 1572872 | tf_op jit(solution)/shard_map/ppermute | solution.py:48
  31.2 1.9 %collective-permute-start.5 = (bf16[4,128,512]{2,1,0:T(8,128)(2,1)S(1)}, bf16[4,128,512]{2,1,0:T(8,128)(2,1)S(1)}, u32[]{:S(2)}, u32[]{:S(2)}) collective-permute-start(bf16[4,128,512]{2,1,0:T(8,128)(2,1)S(1)} %collective-permute-done.4.refs_2_), channel_id=1, source_target_pairs={{0,1},{1,0},{2,3},{3,2},{4,5},{5,4},{6,7},{7,6},{8,9},{9,8},{10,11... | collective-permute-start | bytes 1572872 | tf_op jit(solution)/shard_map/ppermute | solution.py:48
  33.1 1.0 %copy-start.13 = (bf16[4,128,512]{2,1,0:T(8,128)(2,1)S(1)}, bf16[4,128,512]{2,1,0:T(8,128)(2,1)}, u32[]{:S(2)}) copy-start(bf16[4,128,512]{2,1,0:T(8,128)(2,1)} %refs_0_.3) | copy-start | bytes 1572868
  36.8 1.0 %copy-start.6 = (bf16[8,4,64,256]{3,2,1,0:T(8,128)(2,1)}, bf16[8,4,64,256]{3,2,1,0:T(8,128)(2,1)S(1)}, u32[]{:S(2)}) copy-start(bf16[8,4,64,256]{3,2,1,0:T(8,128)(2,1)S(1)} %mix_body.1) | copy-start | bytes 3145732
  37.8 0.8 copy-start.15
  38.6 0.8 copy-start.17
  39.4 0.8 copy-start.19
  40.2 12.6 %copy-start.24 = (s32[256]{0:T(256)S(1)}, s32[256]{0:T(256)}, u32[]{:S(2)}) copy-start(s32[256]{0:T(256)} %param.10) | copy-start | bytes 3076
  43.4 1.0 %copy-start.2 = (bf16[8,4,64,256]{3,2,1,0:T(8,128)(2,1)}, bf16[8,4,64,256]{3,2,1,0:T(8,128)(2,1)S(1)}, u32[]{:S(2)}) copy-start(bf16[8,4,64,256]{3,2,1,0:T(8,128)(2,1)S(1)} %all-to-all-done.1.refs_0_) | copy-start | bytes 3145732
  44.4 29.6 %all-to-all-start = ((bf16[8,4,64,256]{3,2,1,0:T(8,128)(2,1)}), bf16[8,4,64,256]{3,2,1,0:T(8,128)(2,1)S(1)}, u32[]{:S(2)}, u32[]{:S(2)}) async-start(bf16[8,4,64,256]{3,2,1,0:T(8,128)(2,1)} %copy-done.6), calls=%async_computation | async-start | bytes 2097152 | tf_op jit(solution)/shard_map/all_to_all | solution.py:341
  48.0 1.2 %copy-start.3 = (bf16[8,4,64,256]{3,2,1,0:T(8,128)(2,1)S(1)}, bf16[8,4,64,256]{3,2,1,0:T(8,128)(2,1)}, u32[]{:S(2)}) copy-start(bf16[8,4,64,256]{3,2,1,0:T(8,128)(2,1)} %copy-done.2) | copy-start | bytes 3145732
  49.2 3.5 %copy-start.5 = (bf16[1,2048,256]{2,1,0:T(8,128)(2,1)S(1)}, bf16[1,2048,256]{2,1,0:T(8,128)(2,1)}, u32[]{:S(2)}) copy-start(bf16[1,2048,256]{2,1,0:T(8,128)(2,1)} %param.7) | copy-start | bytes 3145732
  49.3 3.5 %copy-start.14 = (bf16[4,128,512]{2,1,0:T(8,128)(2,1)S(1)}, bf16[4,128,512]{2,1,0:T(8,128)(2,1)}, u32[]{:S(2)}) copy-start(bf16[4,128,512]{2,1,0:T(8,128)(2,1)} %refs_0_.3) | copy-start | bytes 1572868
  49.3 3.5 %copy-start.16 = (bf16[4,128,512]{2,1,0:T(8,128)(2,1)S(1)}, bf16[4,128,512]{2,1,0:T(8,128)(2,1)}, u32[]{:S(2)}) copy-start(bf16[4,128,512]{2,1,0:T(8,128)(2,1)} %copy-done.15) | copy-start | bytes 1572868
  52.2 8.7 %collective-permute-start.6 = (bf16[4,128,512]{2,1,0:T(8,128)(2,1)S(1)}, bf16[4,128,512]{2,1,0:T(8,128)(2,1)S(1)}, u32[]{:S(2)}, u32[]{:S(2)}) collective-permute-start(bf16[4,128,512]{2,1,0:T(8,128)(2,1)S(1)} %get-tuple-element.38), channel_id=1, source_target_pairs={{0,1},{1,0},{2,3},{3,2},{4,5},{5,4},{6,7},{7,6},{8,9},{9,8},{10,11... | collective-permute-start | bytes 1572872 | tf_op jit(solution)/shard_map/ppermute | solution.py:48
  52.3 8.6 %collective-permute-start.7 = (bf16[4,128,512]{2,1,0:T(8,128)(2,1)S(1)}, bf16[4,128,512]{2,1,0:T(8,128)(2,1)S(1)}, u32[]{:S(2)}, u32[]{:S(2)}) collective-permute-start(bf16[4,128,512]{2,1,0:T(8,128)(2,1)S(1)} %get-tuple-element.39), channel_id=1, source_target_pairs={{0,1},{1,0},{2,3},{3,2},{4,5},{5,4},{6,7},{7,6},{8,9},{9,8},{10,11... | collective-permute-start | bytes 1572872 | tf_op jit(solution)/shard_map/ppermute | solution.py:48
  52.8 1.0 %copy-start.18 = (bf16[4,128,512]{2,1,0:T(8,128)(2,1)S(1)}, bf16[4,128,512]{2,1,0:T(8,128)(2,1)}, u32[]{:S(2)}) copy-start(bf16[4,128,512]{2,1,0:T(8,128)(2,1)} %copy-done.17) | copy-start | bytes 1572868
  53.8 1.0 %copy-start.20 = (bf16[4,128,512]{2,1,0:T(8,128)(2,1)S(1)}, bf16[4,128,512]{2,1,0:T(8,128)(2,1)}, u32[]{:S(2)}) copy-start(bf16[4,128,512]{2,1,0:T(8,128)(2,1)} %copy-done.19) | copy-start | bytes 1572868
  58.2 1.4 %copy-start.7 = (f32[2048,256]{1,0:T(8,128)}, f32[2048,256]{1,0:T(8,128)S(1)}, u32[]{:S(2)}) copy-start(f32[2048,256]{1,0:T(8,128)S(1)} %get-tuple-element.31.back_ref) | copy-start | bytes 6291460
  59.6 1.3 %copy-start.9 = (bf16[4,512,512]{2,1,0:T(8,128)(2,1)}, bf16[4,512,512]{2,1,0:T(8,128)(2,1)S(1)}, u32[]{:S(2)}) copy-start(bf16[4,512,512]{2,1,0:T(8,128)(2,1)S(1)} %get-tuple-element.33.weights_ref) | copy-start | bytes 6291460
  60.9 1.5 %copy-start.11 = (f32[2048,256]{1,0:T(8,128)}, f32[2048,256]{1,0:T(8,128)S(1)}, u32[]{:S(2)}) copy-start(f32[2048,256]{1,0:T(8,128)S(1)} %get-tuple-element.34.h_ref) | copy-start | bytes 6291460
  62.4 14.9 %collective-permute-start.8 = (bf16[4,128,512]{2,1,0:T(8,128)(2,1)}, bf16[4,128,512]{2,1,0:T(8,128)(2,1)}, u32[]{:S(2)}, u32[]{:S(2)}) collective-permute-start(bf16[4,128,512]{2,1,0:T(8,128)(2,1)} %get-tuple-element.41), channel_id=1, source_target_pairs={{0,2},{1,3},{2,0},{3,1},{4,6},{5,7},{6,4},{7,5},{8,10},{9,11},{10,... | collective-permute-start | bytes 1572872 | tf_op jit(solution)/shard_map/ppermute | solution.py:48
  74.0 5.2 %copy-start.8 = (f32[2048,256]{1,0:T(8,128)S(1)}, f32[2048,256]{1,0:T(8,128)}, u32[]{:S(2)}) copy-start(f32[2048,256]{1,0:T(8,128)} %copy-done.7) | copy-start | bytes 6291460
  74.0 5.2 %copy-start.10 = (bf16[4,512,512]{2,1,0:T(8,128)(2,1)S(1)}, bf16[4,512,512]{2,1,0:T(8,128)(2,1)}, u32[]{:S(2)}) copy-start(bf16[4,512,512]{2,1,0:T(8,128)(2,1)} %copy-done.9) | copy-start | bytes 6291460
  75.3 8.2 %collective-permute-start.9 = (bf16[32,512]{1,0:T(8,128)(2,1)S(1)}, bf16[32,512]{1,0:T(8,128)(2,1)S(1)}, u32[]{:S(2)}, u32[]{:S(2)}) collective-permute-start(bf16[32,512]{1,0:T(8,128)(2,1)S(1)} %get-tuple-element.44), channel_id=1, source_target_pairs={{0,1},{1,0},{2,3},{3,2},{4,5},{5,4},{6,7},{7,6},{8,9},{9,8},{10,11... | collective-permute-start | bytes 98312 | tf_op jit(solution)/shard_map/ppermute | solution.py:48
  75.4 8.1 %collective-permute-start.10 = (bf16[32,512]{1,0:T(8,128)(2,1)S(1)}, bf16[32,512]{1,0:T(8,128)(2,1)S(1)}, u32[]{:S(2)}, u32[]{:S(2)}) collective-permute-start(bf16[32,512]{1,0:T(8,128)(2,1)S(1)} %get-tuple-element.45), channel_id=1, source_target_pairs={{0,2},{1,3},{2,0},{3,1},{4,6},{5,7},{6,4},{7,5},{8,10},{9,11},{10,... | collective-permute-start | bytes 98312 | tf_op jit(solution)/shard_map/ppermute | solution.py:48
  76.9 6.6 %collective-permute-start.11 = (bf16[32,512]{1,0:T(8,128)(2,1)S(1)}, bf16[32,512]{1,0:T(8,128)(2,1)S(1)}, u32[]{:S(2)}, u32[]{:S(2)}) collective-permute-start(bf16[32,512]{1,0:T(8,128)(2,1)S(1)} %get-tuple-element.46), channel_id=1, source_target_pairs={{0,3},{1,2},{2,1},{3,0},{4,7},{5,6},{6,5},{7,4},{8,11},{9,10},{10,... | collective-permute-start | bytes 98312 | tf_op jit(solution)/shard_map/ppermute | solution.py:48
  79.2 1.6 %copy-start.12 = (f32[2048,256]{1,0:T(8,128)S(1)}, f32[2048,256]{1,0:T(8,128)}, u32[]{:S(2)}) copy-start(f32[2048,256]{1,0:T(8,128)} %copy-done.11) | copy-start | bytes 6291460

commit v5 on v4

--- a/solution.py
+++ b/solution.py
@@ -10,7 +10,7 @@
 BF16 = jnp.bfloat16
 F32 = jnp.float32
 LANE_GROUP = 16
-CFG = {'cost': {}, 'direct': False, 'rsdirect': False, 'f2early': False, 'order': [[7, 6, 5, 4, 3, 2, 1], [7, 6, 5, 4, 3, 2, 1]], 'deps': {'h3': ['h7'], 'h2': ['h7'], 'h1': ['h7'], 'fx': ['A2'], 'F1': ['M'], 'pair': ['F2'], 'unpack': ['add']}, 'a2a': [True, True]}
+CFG = {'cost': {}, 'direct': False, 'rsdirect': False, 'f2early': False, 'order': [[7, 4, 6, 5, 3, 2, 1], [7, 6, 5, 4, 3, 2, 1]], 'deps': {'h3': ['h7'], 'h2': ['h7'], 'h1': ['h7'], 'fx': ['h7', 'h4'], 'F1': ['M'], 'pair': ['F2'], 'unpack': ['add']}, 'a2a': [False, True]}
 
 
 def iota(shape, dim):

time: 85.2 us -> 118 us (1.38)
  waiting for transfers between devices: 27.8 us -> 51.4 us
  starting transfers between devices: 18.2 us -> 25.3 us
  local copies, waits for them, and re-layouts: 18.4 us -> 21.2 us
    ppermute x12 -> x19, waiting for transfers between devices: 14.4 us -> 51.4 us  [swap(): return lax.ppermute(value, axis, [(p, p ^ step) for p in range(size)])]
    ppermute x12 -> x19, starting transfers between devices: 8.5 us -> 21.4 us  [swap(): return lax.ppermute(value, axis, [(p, p ^ step) for p in range(size)])]
    all_to_all x1, waiting for transfers between devices: 10.2 us -> 0.01 us  [packed_shards(): lax.all_to_all(dep('H0', regrouped[0]), 'seq', 0, 0, tiled=True)]
    all_to_all x1 -> x0, starting transfers between devices: 6.09 us -> none  [packed_shards(): lax.all_to_all(dep('h0', back[0]), 'seq', 0, 0, tiled=True)]
    all_to_all x1 -> x0, waiting for transfers between devices: 3.19 us -> none  [packed_shards(): lax.all_to_all(dep('h0', back[0]), 'seq', 0, 0, tiled=True)]
    unnamed x52 -> x64, local copies, waits for them, and re-layouts: 18.4 us -> 21.2 us
  transfers between devices with their start and end apart: 14 -> 20, of which waited for: 4 -> 5; matrix products, arithmetic and copies ran while one was open for 0% -> 0% of each run, Pallas kernels for 19% -> 12%
where the time goes in v5:
time: 118 us; the launch traced here: 117 us
  waiting for transfers between devices  51.4 us (44%)
  starting transfers between devices  25.3 us (21%)
  local copies, waits for them, and re-layouts  21.2 us (18%)
  Pallas kernels  18.5 us (16%)
    ppermute x19, waiting for transfers between devices, swap(): return lax.ppermute(value, axis, [(p, p ^ step) for p in range(size)])  51.4 us
    ppermute x19, starting transfers between devices, swap(): return lax.ppermute(value, axis, [(p, p ^ step) for p in range(size)])  21.4 us
    unnamed x64, local copies, waits for them, and re-layouts  21.2 us
    pallas_call x11, Pallas kernels, call(): pl.pallas_call(body, name=name, out_shape=outs, in_specs=[pl.BlockSpec(me...  18.5 us
    all_to_all x1, starting transfers between devices, packed_shards(): lax.all_to_all(dep('H0', regrouped[0]), 'seq', 0, 0, tiled=True)  3.89 us
  transfers between devices with their start and end apart: 20, of which 5 were waited for; matrix products, arithmetic and copies ran while one was open for 0% of the time, Pallas kernels for 12%

profile of v5, /device:TPU:0, one launch (start us, length us, event | category | flops | bytes accessed | tf_op | source)
XLA Modules:
  0.0 117.3 jit_solution(10436807281798792748)
XLA Ops:
  0.6 0.8 copy-done.23
  1.5 0.4 pack_body.1.refs_0_
  1.9 2.4 %collective-permute-start.2 = (bf16[32,512]{1,0:T(8,128)(2,1)S(1)}, bf16[32,512]{1,0:T(8,128)(2,1)S(1)}, u32[]{:S(2)}, u32[]{:S(2)}) collective-permute-start(bf16[32,512]{1,0:T(8,128)(2,1)S(1)} %pack_body.1.refs_0_), channel_id=1, source_target_pairs={{0,3},{1,2},{2,1},{3,0},{4,7},{5,6},{6,5},{7,4},{8,11},{9,10},{10,... | collective-permute-start | bytes 98312 | tf_op jit(solution)/shard_map/ppermute | solution.py:48
  4.3 0.6 collective-permute-start.1
  5.0 0.0 collective-permute-start
  5.0 1.2 %copy-done = bf16[1,2048,256]{2,1,0:T(8,128)(2,1)S(1)} copy-done((bf16[1,2048,256]{2,1,0:T(8,128)(2,1)S(1)}, bf16[1,2048,256]{2,1,0:T(8,128)(2,1)}, u32[]{:S(2)}) %copy-start) | copy-done | bytes 1048600
  6.2 1.2 %copy-done.2 = bf16[1,2048,256]{2,1,0:T(8,128)(2,1)S(1)} copy-done((bf16[1,2048,256]{2,1,0:T(8,128)(2,1)S(1)}, bf16[1,2048,256]{2,1,0:T(8,128)(2,1)}, u32[]{:S(2)}) %copy-start.2) | copy-done | bytes 1048600
  7.5 0.7 copy-done.24
  8.1 0.5 gate_body.1.refs_4_.refs_1_
  8.6 0.0 collective-permute-done.2.refs_3_
  8.7 0.0 collective-permute-done.refs_1_
  8.7 0.5 copy-done.11
  9.2 1.7 %collective-permute-start.4 = (bf16[4,128,512]{2,1,0:T(8,128)(2,1)S(1)}, bf16[4,128,512]{2,1,0:T(8,128)(2,1)S(1)}, u32[]{:S(2)}, u32[]{:S(2)}) collective-permute-start(bf16[4,128,512]{2,1,0:T(8,128)(2,1)S(1)} %copy-done.11), channel_id=1, source_target_pairs={{0,2},{1,3},{2,0},{3,1},{4,6},{5,7},{6,4},{7,5},{8,10},{9,11},{10,... | collective-permute-start | bytes 1572872 | tf_op jit(solution)/shard_map/ppermute | solution.py:48
  10.9 1.5 %regroup_back_body.1 = (bf16[4,64,256]{2,1,0:T(8,128)(2,1)S(1)}, bf16[4,64,256]{2,1,0:T(8,128)(2,1)S(1)}, bf16[4,64,256]{2,1,0:T(8,128)(2,1)S(1)}, bf16[4,64,256...) custom-call(bf16[32,512]{1,0:T(8,128)(2,1)S(1)} %pack_body.1.refs_0_, ...), custom_call_target="tpu_custom_call" | custom-call | tf_op jit(solution)/shard_map/regroup_back_body/pallas_call | solution.py:31
  12.4 0.6 copy-done.27
  13.1 0.7 copy-done.28
  13.7 0.7 copy-done.29
  14.4 0.7 copy-done.30
  15.0 0.6 copy-done.31
  15.7 4.6 %collective-permute-start.5 = (bf16[4,64,256]{2,1,0:T(8,128)(2,1)S(1)}, bf16[4,64,256]{2,1,0:T(8,128)(2,1)S(1)}, u32[]{:S(2)}, u32[]{:S(2)}) collective-permute-start(bf16[4,64,256]{2,1,0:T(8,128)(2,1)S(1)} %get-tuple-element.36), channel_id=1, source_target_pairs={{0,28},{4,24},{8,20},{12,16},{16,12},{20,8},{24,4},{28,0},{1,29},{... | collective-permute-start | bytes 393224 | tf_op jit(solution)/shard_map/ppermute | solution.py:48
  20.2 0.0 collective-permute-start.6
  20.3 0.0 collective-permute-start.3
  20.3 4.6 %collective-permute-done.5.refs_7_ = bf16[4,64,256]{2,1,0:T(8,128)(2,1)S(1)} collective-permute-done((bf16[4,64,256]{2,1,0:T(8,128)(2,1)S(1)}, bf16[4,64,256]{2,1,0:T(8,128)(2,1)S(1)}, u32[]{:S(2)}, u32[]{:S(2)}) %collective-permute-start.5) | collective-permute-done | bytes 131104 | tf_op jit(solution)/shard_map/ppermute | solution.py:48
  24.8 6.5 %collective-permute-done.6.refs_4_ = bf16[4,64,256]{2,1,0:T(8,128)(2,1)S(1)} collective-permute-done((bf16[4,64,256]{2,1,0:T(8,128)(2,1)S(1)}, bf16[4,64,256]{2,1,0:T(8,128)(2,1)S(1)}, u32[]{:S(2)}, u32[]{:S(2)}) %collective-permute-start.6) | collective-permute-done | bytes 131104 | tf_op jit(solution)/shard_map/ppermute | solution.py:48
  31.3 0.6 copy-done.21
  32.0 0.0 collective-permute-done.4.refs_2_
  32.0 1.9 %collective-permute-done.7.refs_3_ = bf16[4,128,512]{2,1,0:T(8,128)(2,1)S(1)} collective-permute-done((bf16[4,128,512]{2,1,0:T(8,128)(2,1)S(1)}, bf16[4,128,512]{2,1,0:T(8,128)(2,1)S(1)}, u32[]{:S(2)}, u32[]{:S(2)}) %collective-permute-start.7) | collective-permute-done | bytes 524320 | tf_op jit(solution)/shard_map/ppermute | solution.py:48
  33.9 2.6 %mix_body.1 = bf16[8,4,64,256]{3,2,1,0:T(8,128)(2,1)S(1)} custom-call(bf16[4,128,512]{2,1,0:T(8,128)(2,1)S(1)} %copy-done.11, bf16[4,128,512]{2,1,0:T(8,128)(2,1)S(1)} %collective-permute-done.3.refs_1_, bf16[4,128,512]{2,1,0:T(8,128)(2,1)S(1)} %collective-permute-done.4.refs_2_, bf16[4,128,512]{2,1,0:T(8,128)(2,1)S(1)} %collective-permute-done.7.refs_3_, ...), custom_call_target="tpu_custom_call" | custom-call | tf_op jit(solution)/shard_map/mix_body/pallas_call | solution.py:31
  36.5 0.0 copy-start.4
  36.6 1.0 copy-done.4
  37.5 0.8 copy-done.13
  38.3 0.8 copy-done.15
  39.1 0.8 copy-done.17
  39.9 3.9 %all-to-all-start = ((bf16[8,4,64,256]{3,2,1,0:T(8,128)(2,1)}), bf16[8,4,64,256]{3,2,1,0:T(8,128)(2,1)S(1)}, u32[]{:S(2)}, u32[]{:S(2)}) async-start(bf16[8,4,64,256]{3,2,1,0:T(8,128)(2,1)} %copy-done.4), calls=%async_computation | async-start | bytes 2097152 | tf_op jit(solution)/shard_map/all_to_all | solution.py:341
  43.8 0.0 copy-start.12
  43.8 3.9 %collective-permute-start.11 = (bf16[4,64,256]{2,1,0:T(8,128)(2,1)}, bf16[4,64,256]{2,1,0:T(8,128)(2,1)S(1)}, u32[]{:S(2)}, u32[]{:S(2)}) collective-permute-start(bf16[4,64,256]{2,1,0:T(8,128)(2,1)} %copy-done.31), channel_id=1, source_target_pairs={{0,20},{4,16},{8,28},{12,24},{16,4},{20,0},{24,12},{28,8},{1,21},{... | collective-permute-start | bytes 393224 | tf_op jit(solution)/shard_map/ppermute | solution.py:48
  47.7 1.5 %collective-permute-start.12 = (bf16[4,64,256]{2,1,0:T(8,128)(2,1)}, bf16[4,64,256]{2,1,0:T(8,128)(2,1)S(1)}, u32[]{:S(2)}, u32[]{:S(2)}) collective-permute-start(bf16[4,64,256]{2,1,0:T(8,128)(2,1)} %copy-done.30), channel_id=1, source_target_pairs={{0,24},{4,28},{8,16},{12,20},{16,8},{20,12},{24,0},{28,4},{1,25},{... | collective-permute-start | bytes 393224 | tf_op jit(solution)/shard_map/ppermute | solution.py:48
  49.2 0.6 collective-permute-start.8
  49.7 0.0 collective-permute-start.9
  49.7 2.9 %collective-permute-start.10 = (bf16[4,64,256]{2,1,0:T(8,128)(2,1)}, bf16[4,64,256]{2,1,0:T(8,128)(2,1)S(1)}, u32[]{:S(2)}, u32[]{:S(2)}) collective-permute-start(bf16[4,64,256]{2,1,0:T(8,128)(2,1)} %copy-done.27), channel_id=1, source_target_pairs={{0,12},{4,8},{8,4},{12,0},{16,28},{20,24},{24,20},{28,16},{1,13},{... | collective-permute-start | bytes 393224 | tf_op jit(solution)/shard_map/ppermute | solution.py:48
  52.7 27.5 %collective-permute-done.11.refs_5_ = bf16[4,64,256]{2,1,0:T(8,128)(2,1)S(1)} collective-permute-done((bf16[4,64,256]{2,1,0:T(8,128)(2,1)}, bf16[4,64,256]{2,1,0:T(8,128)(2,1)S(1)}, u32[]{:S(2)}, u32[]{:S(2)}) %collective-permute-start.11) | collective-permute-done | bytes 131104 | tf_op jit(solution)/shard_map/ppermute | solution.py:48
  80.2 0.9 copy-done.22
  81.1 3.0 %first_grad_body.1 = (bf16[4,128,512]{2,1,0:T(8,128)(2,1)S(1)}, bf16[4,128,512]{2,1,0:T(8,128)(2,1)S(1)}, bf16[4,128,512]{2,1,0:T(8,128)(2,1)S(1)}, bf16[4,128,5...) custom-call(bf16[4,64,256]{2,1,0:T(8,128)(2,1)S(1)} %get-tuple-element.40.refs_0_, ...), custom_call_target="tpu_custom_call" | custom-call | tf_op jit(solution)/shard_map/first_grad_body/pallas_call | solution.py:31
  84.2 0.1 collective-permute-start.13
  84.2 0.5 collective-permute-start.14
  84.7 0.0 copy-start.16
  84.8 1.0 copy-done.16
  85.8 1.0 copy-done.18
  86.8 3.3 %mix_back_body.1 = (f32[2048,256]{1,0:T(8,128)S(1)}, bf16[4,512,512]{2,1,0:T(8,128)(2,1)S(1)}, f32[2048,256]{1,0:T(8,128)S(1)}) custom-call(bf16[4,128,512]{2,1,0:T(8,128)(2,1)S(1)} %copy-done.12, bf16[4,128,512]{2,1,0:T(8,128)(2,1)S(1)} %copy-done.16, bf16[4,128,512]{2,1,0:T(8,128)(2,1)S(1)} %copy-done.14, bf16[4,128,512]{2,1,0:T(8,128)(2,1)S(1)} %copy-done.18, ...), custom_call_target="tpu_custom_call" | custom-call | tf_op jit(solution)/shard_map/mix_back_body/pallas_call | solution.py:31
  90.1 1.4 %copy-done.5 = f32[2048,256]{1,0:T(8,128)} copy-done((f32[2048,256]{1,0:T(8,128)}, f32[2048,256]{1,0:T(8,128)S(1)}, u32[]{:S(2)}) %copy-start.5) | copy-done | bytes 2097176
  91.5 1.3 %copy-done.9 = f32[2048,256]{1,0:T(8,128)} copy-done((f32[2048,256]{1,0:T(8,128)}, f32[2048,256]{1,0:T(8,128)S(1)}, u32[]{:S(2)}) %copy-start.9) | copy-done | bytes 2097176
  92.9 1.1 pair_body.1
  94.0 1.0 copy-done.19
  95.0 0.6 collective-permute-start.15
  95.6 1.3 %second_grad_body.1 = (bf16[32,512]{1,0:T(8,128)(2,1)S(1)}, bf16[32,512]{1,0:T(8,128)(2,1)S(1)}, bf16[32,512]{1,0:T(8,128)(2,1)S(1)}, bf16[32,512]{1,0:T(8,128)(2,1)S(1)}) custom-call(bf16[32,64,256]{2,1,0:T(8,128)(2,1)S(1)} %bitcast.16, bf16[2048,256]{1,0:T(8,128)(2,1)S(1)} %gate_body.1.refs_4_.refs_1_), custom_call_target="tpu_custom_call" | custom-call | tf_op jit(solution)/shard_map/second_grad_body/pallas_call | solution.py:31
  97.0 0.1 collective-permute-start.16
  97.1 1.5 %collective-permute-start.17 = (bf16[32,512]{1,0:T(8,128)(2,1)S(1)}, bf16[32,512]{1,0:T(8,128)(2,1)S(1)}, u32[]{:S(2)}, u32[]{:S(2)}) collective-permute-start(bf16[32,512]{1,0:T(8,128)(2,1)S(1)} %get-tuple-element.65), channel_id=1, source_target_pairs={{0,2},{1,3},{2,0},{3,1},{4,6},{5,7},{6,4},{7,5},{8,10},{9,11},{10,... | collective-permute-start | bytes 98312 | tf_op jit(solution)/shard_map/ppermute | solution.py:48
  98.5 0.4 collective-permute-start.18
  98.9 10.9 %collective-permute-done.15.got = bf16[4,128,512]{2,1,0:T(8,128)(2,1)S(1)} collective-permute-done((bf16[4,128,512]{2,1,0:T(8,128)(2,1)}, bf16[4,128,512]{2,1,0:T(8,128)(2,1)S(1)}, u32[]{:S(2)}, u32[]{:S(2)}) %collective-permute-start.15) | collective-permute-done | bytes 524320 | tf_op jit(solution)/shard_map/ppermute | solution.py:48
  109.8 1.2 %copy-done.20 = f32[4,128,512]{2,1,0:T(8,128)S(1)} copy-done((f32[4,128,512]{2,1,0:T(8,128)S(1)}, f32[4,128,512]{2,1,0:T(8,128)}, u32[]{:S(2)}) %copy-start.20) | copy-done | bytes 1048600
  111.0 0.9 add_body.1
  112.0 1.6 %copy-done.10 = f32[2048,256]{1,0:T(8,128)S(1)} copy-done((f32[2048,256]{1,0:T(8,128)S(1)}, f32[2048,256]{1,0:T(8,128)}, u32[]{:S(2)}) %copy-start.10) | copy-done | bytes 2097176
  113.6 2.7 %tokens_body.1 = bf16[2048,256]{1,0:T(8,128)(2,1)} custom-call(bf16[32,64,256]{2,1,0:T(8,128)(2,1)S(1)} %bitcast.17, bf16[4,512,512]{2,1,0:T(8,128)(2,1)S(1)} %copy-done.8, f32[2048,256]{1,0:T(8,128)S(1)} %copy-done.10, s32[1,256]{1,0:T(1,128)S(1)} %bitcast.23, f32[2048,256]{1,0:T(8,128)S(1)} %copy-done.6), custom_call_target="tpu_custom_call" | custom-call | tf_op jit(solution)/shard_map/tokens_body/pallas_call | solution.py:31
  116.3 1.1 unpack_body.1
  (51 shorter events, 0.1 us)
Async XLA Ops:
  0.6 0.8 copy-start.23
  1.9 6.7 %collective-permute-start.2 = (bf16[32,512]{1,0:T(8,128)(2,1)S(1)}, bf16[32,512]{1,0:T(8,128)(2,1)S(1)}, u32[]{:S(2)}, u32[]{:S(2)}) collective-permute-start(bf16[32,512]{1,0:T(8,128)(2,1)S(1)} %pack_body.1.refs_0_), channel_id=1, source_target_pairs={{0,3},{1,2},{2,1},{3,0},{4,7},{5,6},{6,5},{7,4},{8,11},{9,10},{10,... | collective-permute-start | bytes 98312 | tf_op jit(solution)/shard_map/ppermute | solution.py:48
  4.3 4.3 %collective-permute-start.1 = (bf16[32,512]{1,0:T(8,128)(2,1)S(1)}, bf16[32,512]{1,0:T(8,128)(2,1)S(1)}, u32[]{:S(2)}, u32[]{:S(2)}) collective-permute-start(bf16[32,512]{1,0:T(8,128)(2,1)S(1)} %pack_body.1.refs_0_), channel_id=1, source_target_pairs={{0,2},{1,3},{2,0},{3,1},{4,6},{5,7},{6,4},{7,5},{8,10},{9,11},{10,... | collective-permute-start | bytes 98312 | tf_op jit(solution)/shard_map/ppermute | solution.py:48
  5.0 3.7 %collective-permute-start = (bf16[32,512]{1,0:T(8,128)(2,1)S(1)}, bf16[32,512]{1,0:T(8,128)(2,1)S(1)}, u32[]{:S(2)}, u32[]{:S(2)}) collective-permute-start(bf16[32,512]{1,0:T(8,128)(2,1)S(1)} %pack_body.1.refs_0_), channel_id=1, source_target_pairs={{0,1},{1,0},{2,3},{3,2},{4,5},{5,4},{6,7},{7,6},{8,9},{9,8},{10,11... | collective-permute-start | bytes 98312 | tf_op jit(solution)/shard_map/ppermute | solution.py:48
  5.0 1.2 %copy-start = (bf16[1,2048,256]{2,1,0:T(8,128)(2,1)S(1)}, bf16[1,2048,256]{2,1,0:T(8,128)(2,1)}, u32[]{:S(2)}) copy-start(bf16[1,2048,256]{2,1,0:T(8,128)(2,1)} %param.6) | copy-start | bytes 3145732
  6.2 1.2 %copy-start.2 = (bf16[1,2048,256]{2,1,0:T(8,128)(2,1)S(1)}, bf16[1,2048,256]{2,1,0:T(8,128)(2,1)}, u32[]{:S(2)}) copy-start(bf16[1,2048,256]{2,1,0:T(8,128)(2,1)} %param.7) | copy-start | bytes 3145732
  7.5 0.7 copy-start.24
  8.1 1.0 copy-start.11
  8.1 25.7 %copy-start.1 = (bf16[1,2048,256]{2,1,0:T(8,128)(2,1)S(1)}, bf16[1,2048,256]{2,1,0:T(8,128)(2,1)}, u32[]{:S(2)}) copy-start(bf16[1,2048,256]{2,1,0:T(8,128)(2,1)} %param.6) | copy-start | bytes 3145732
  8.1 25.7 %copy-start.26 = (s32[512]{0:T(512)S(1)}, s32[512]{0:T(512)}, u32[]{:S(2)}) copy-start(s32[512]{0:T(512)} %param.11) | copy-start | bytes 6148
  9.2 22.8 %collective-permute-start.4 = (bf16[4,128,512]{2,1,0:T(8,128)(2,1)S(1)}, bf16[4,128,512]{2,1,0:T(8,128)(2,1)S(1)}, u32[]{:S(2)}, u32[]{:S(2)}) collective-permute-start(bf16[4,128,512]{2,1,0:T(8,128)(2,1)S(1)} %copy-done.11), channel_id=1, source_target_pairs={{0,2},{1,3},{2,0},{3,1},{4,6},{5,7},{6,4},{7,5},{8,10},{9,11},{10,... | collective-permute-start | bytes 1572872 | tf_op jit(solution)/shard_map/ppermute | solution.py:48
  12.4 0.6 copy-start.27
  13.1 0.7 copy-start.28
  13.7 0.7 copy-start.29
  14.4 0.7 copy-start.30
  15.0 0.6 copy-start.31
  15.7 9.1 %collective-permute-start.5 = (bf16[4,64,256]{2,1,0:T(8,128)(2,1)S(1)}, bf16[4,64,256]{2,1,0:T(8,128)(2,1)S(1)}, u32[]{:S(2)}, u32[]{:S(2)}) collective-permute-start(bf16[4,64,256]{2,1,0:T(8,128)(2,1)S(1)} %get-tuple-element.36), channel_id=1, source_target_pairs={{0,28},{4,24},{8,20},{12,16},{16,12},{20,8},{24,4},{28,0},{1,29},{... | collective-permute-start | bytes 393224 | tf_op jit(solution)/shard_map/ppermute | solution.py:48
  20.2 11.1 %collective-permute-start.6 = (bf16[4,64,256]{2,1,0:T(8,128)(2,1)S(1)}, bf16[4,64,256]{2,1,0:T(8,128)(2,1)S(1)}, u32[]{:S(2)}, u32[]{:S(2)}) collective-permute-start(bf16[4,64,256]{2,1,0:T(8,128)(2,1)S(1)} %get-tuple-element.37), channel_id=1, source_target_pairs={{0,16},{4,20},{8,24},{12,28},{16,0},{20,4},{24,8},{28,12},{1,17},{... | collective-permute-start | bytes 393224 | tf_op jit(solution)/shard_map/ppermute | solution.py:48
  20.3 11.7 %collective-permute-start.3 = (bf16[4,128,512]{2,1,0:T(8,128)(2,1)S(1)}, bf16[4,128,512]{2,1,0:T(8,128)(2,1)S(1)}, u32[]{:S(2)}, u32[]{:S(2)}) collective-permute-start(bf16[4,128,512]{2,1,0:T(8,128)(2,1)S(1)} %copy-done.11), channel_id=1, source_target_pairs={{0,1},{1,0},{2,3},{3,2},{4,5},{5,4},{6,7},{7,6},{8,9},{9,8},{10,11... | collective-permute-start | bytes 1572872 | tf_op jit(solution)/shard_map/ppermute | solution.py:48
  31.3 0.6 copy-start.21
  32.0 1.9 %collective-permute-start.7 = (bf16[4,128,512]{2,1,0:T(8,128)(2,1)S(1)}, bf16[4,128,512]{2,1,0:T(8,128)(2,1)S(1)}, u32[]{:S(2)}, u32[]{:S(2)}) collective-permute-start(bf16[4,128,512]{2,1,0:T(8,128)(2,1)S(1)} %collective-permute-done.4.refs_2_), channel_id=1, source_target_pairs={{0,1},{1,0},{2,3},{3,2},{4,5},{5,4},{6,7},{7,6},{8,9},{9,8},{10,11... | collective-permute-start | bytes 1572872 | tf_op jit(solution)/shard_map/ppermute | solution.py:48
  36.5 1.0 copy-start.4
  37.5 0.8 copy-start.13
  38.3 0.8 copy-start.15
  39.1 0.8 copy-start.17
  39.9 44.8 %copy-start.25 = (s32[256]{0:T(256)S(1)}, s32[256]{0:T(256)}, u32[]{:S(2)}) copy-start(s32[256]{0:T(256)} %param.10) | copy-start | bytes 3076
  39.9 55.7 %all-to-all-start = ((bf16[8,4,64,256]{3,2,1,0:T(8,128)(2,1)}), bf16[8,4,64,256]{3,2,1,0:T(8,128)(2,1)S(1)}, u32[]{:S(2)}, u32[]{:S(2)}) async-start(bf16[8,4,64,256]{3,2,1,0:T(8,128)(2,1)} %copy-done.4), calls=%async_computation | async-start | bytes 2097152 | tf_op jit(solution)/shard_map/all_to_all | solution.py:341
  43.8 40.9 %copy-start.3 = (bf16[1,2048,256]{2,1,0:T(8,128)(2,1)S(1)}, bf16[1,2048,256]{2,1,0:T(8,128)(2,1)}, u32[]{:S(2)}) copy-start(bf16[1,2048,256]{2,1,0:T(8,128)(2,1)} %param.7) | copy-start | bytes 3145732
  43.8 40.9 %copy-start.12 = (bf16[4,128,512]{2,1,0:T(8,128)(2,1)S(1)}, bf16[4,128,512]{2,1,0:T(8,128)(2,1)}, u32[]{:S(2)}) copy-start(bf16[4,128,512]{2,1,0:T(8,128)(2,1)} %refs_0_.3) | copy-start | bytes 1572868
  43.8 40.9 %copy-start.14 = (bf16[4,128,512]{2,1,0:T(8,128)(2,1)S(1)}, bf16[4,128,512]{2,1,0:T(8,128)(2,1)}, u32[]{:S(2)}) copy-start(bf16[4,128,512]{2,1,0:T(8,128)(2,1)} %copy-done.13) | copy-start | bytes 1572868
  43.8 36.4 %collective-permute-start.11 = (bf16[4,64,256]{2,1,0:T(8,128)(2,1)}, bf16[4,64,256]{2,1,0:T(8,128)(2,1)S(1)}, u32[]{:S(2)}, u32[]{:S(2)}) collective-permute-start(bf16[4,64,256]{2,1,0:T(8,128)(2,1)} %copy-done.31), channel_id=1, source_target_pairs={{0,20},{4,16},{8,28},{12,24},{16,4},{20,0},{24,12},{28,8},{1,21},{... | collective-permute-start | bytes 393224 | tf_op jit(solution)/shard_map/ppermute | solution.py:48
  47.7 32.5 %collective-permute-start.12 = (bf16[4,64,256]{2,1,0:T(8,128)(2,1)}, bf16[4,64,256]{2,1,0:T(8,128)(2,1)S(1)}, u32[]{:S(2)}, u32[]{:S(2)}) collective-permute-start(bf16[4,64,256]{2,1,0:T(8,128)(2,1)} %copy-done.30), channel_id=1, source_target_pairs={{0,24},{4,28},{8,16},{12,20},{16,8},{20,12},{24,0},{28,4},{1,25},{... | collective-permute-start | bytes 393224 | tf_op jit(solution)/shard_map/ppermute | solution.py:48
  49.2 31.0 %collective-permute-start.8 = (bf16[4,64,256]{2,1,0:T(8,128)(2,1)}, bf16[4,64,256]{2,1,0:T(8,128)(2,1)S(1)}, u32[]{:S(2)}, u32[]{:S(2)}) collective-permute-start(bf16[4,64,256]{2,1,0:T(8,128)(2,1)} %copy-done.29), channel_id=1, source_target_pairs={{0,4},{4,0},{8,12},{12,8},{16,20},{20,16},{24,28},{28,24},{1,5},{5... | collective-permute-start | bytes 393224 | tf_op jit(solution)/shard_map/ppermute | solution.py:48
  49.7 30.5 %collective-permute-start.9 = (bf16[4,64,256]{2,1,0:T(8,128)(2,1)}, bf16[4,64,256]{2,1,0:T(8,128)(2,1)S(1)}, u32[]{:S(2)}, u32[]{:S(2)}) collective-permute-start(bf16[4,64,256]{2,1,0:T(8,128)(2,1)} %copy-done.28), channel_id=1, source_target_pairs={{0,8},{4,12},{8,0},{12,4},{16,24},{20,28},{24,16},{28,20},{1,9},{5... | collective-permute-start | bytes 393224 | tf_op jit(solution)/shard_map/ppermute | solution.py:48
  49.7 30.5 %collective-permute-start.10 = (bf16[4,64,256]{2,1,0:T(8,128)(2,1)}, bf16[4,64,256]{2,1,0:T(8,128)(2,1)S(1)}, u32[]{:S(2)}, u32[]{:S(2)}) collective-permute-start(bf16[4,64,256]{2,1,0:T(8,128)(2,1)} %copy-done.27), channel_id=1, source_target_pairs={{0,12},{4,8},{8,4},{12,0},{16,28},{20,24},{24,20},{28,16},{1,13},{... | collective-permute-start | bytes 393224 | tf_op jit(solution)/shard_map/ppermute | solution.py:48
  80.2 0.9 copy-start.22
  84.2 8.7 %collective-permute-start.13 = (bf16[4,128,512]{2,1,0:T(8,128)(2,1)S(1)}, bf16[4,128,512]{2,1,0:T(8,128)(2,1)S(1)}, u32[]{:S(2)}, u32[]{:S(2)}) collective-permute-start(bf16[4,128,512]{2,1,0:T(8,128)(2,1)S(1)} %get-tuple-element.58), channel_id=1, source_target_pairs={{0,1},{1,0},{2,3},{3,2},{4,5},{5,4},{6,7},{7,6},{8,9},{9,8},{10,11... | collective-permute-start | bytes 1572872 | tf_op jit(solution)/shard_map/ppermute | solution.py:48
  84.2 8.6 %collective-permute-start.14 = (bf16[4,128,512]{2,1,0:T(8,128)(2,1)S(1)}, bf16[4,128,512]{2,1,0:T(8,128)(2,1)S(1)}, u32[]{:S(2)}, u32[]{:S(2)}) collective-permute-start(bf16[4,128,512]{2,1,0:T(8,128)(2,1)S(1)} %get-tuple-element.59), channel_id=1, source_target_pairs={{0,1},{1,0},{2,3},{3,2},{4,5},{5,4},{6,7},{7,6},{8,9},{9,8},{10,11... | collective-permute-start | bytes 1572872 | tf_op jit(solution)/shard_map/ppermute | solution.py:48
  84.7 1.0 copy-start.16
  85.8 1.0 copy-start.18
  90.1 1.4 %copy-start.5 = (f32[2048,256]{1,0:T(8,128)}, f32[2048,256]{1,0:T(8,128)S(1)}, u32[]{:S(2)}) copy-start(f32[2048,256]{1,0:T(8,128)S(1)} %get-tuple-element.51.back_ref) | copy-start | bytes 6291460
  91.5 1.3 %copy-start.9 = (f32[2048,256]{1,0:T(8,128)}, f32[2048,256]{1,0:T(8,128)S(1)}, u32[]{:S(2)}) copy-start(f32[2048,256]{1,0:T(8,128)S(1)} %get-tuple-element.54.h_ref) | copy-start | bytes 6291460
  92.8 2.1 %copy-start.7 = (bf16[4,512,512]{2,1,0:T(8,128)(2,1)}, bf16[4,512,512]{2,1,0:T(8,128)(2,1)S(1)}, u32[]{:S(2)}) copy-start(bf16[4,512,512]{2,1,0:T(8,128)(2,1)S(1)} %get-tuple-element.53.weights_ref) | copy-start | bytes 6291460
  94.0 1.0 copy-start.19
  95.0 14.8 %collective-permute-start.15 = (bf16[4,128,512]{2,1,0:T(8,128)(2,1)}, bf16[4,128,512]{2,1,0:T(8,128)(2,1)S(1)}, u32[]{:S(2)}, u32[]{:S(2)}) collective-permute-start(bf16[4,128,512]{2,1,0:T(8,128)(2,1)} %get-tuple-element.61), channel_id=1, source_target_pairs={{0,2},{1,3},{2,0},{3,1},{4,6},{5,7},{6,4},{7,5},{8,10},{9,11},{10,... | collective-permute-start | bytes 1572872 | tf_op jit(solution)/shard_map/ppermute | solution.py:48
  95.6 16.3 %copy-start.6 = (f32[2048,256]{1,0:T(8,128)S(1)}, f32[2048,256]{1,0:T(8,128)}, u32[]{:S(2)}) copy-start(f32[2048,256]{1,0:T(8,128)} %copy-done.5) | copy-start | bytes 6291460
  95.6 16.3 %copy-start.8 = (bf16[4,512,512]{2,1,0:T(8,128)(2,1)S(1)}, bf16[4,512,512]{2,1,0:T(8,128)(2,1)}, u32[]{:S(2)}) copy-start(bf16[4,512,512]{2,1,0:T(8,128)(2,1)} %copy-done.7) | copy-start | bytes 6291460
  97.0 19.3 %collective-permute-start.16 = (bf16[32,512]{1,0:T(8,128)(2,1)S(1)}, bf16[32,512]{1,0:T(8,128)(2,1)S(1)}, u32[]{:S(2)}, u32[]{:S(2)}) collective-permute-start(bf16[32,512]{1,0:T(8,128)(2,1)S(1)} %get-tuple-element.64), channel_id=1, source_target_pairs={{0,1},{1,0},{2,3},{3,2},{4,5},{5,4},{6,7},{7,6},{8,9},{9,8},{10,11... | collective-permute-start | bytes 98312 | tf_op jit(solution)/shard_map/ppermute | solution.py:48
  97.1 19.2 %collective-permute-start.17 = (bf16[32,512]{1,0:T(8,128)(2,1)S(1)}, bf16[32,512]{1,0:T(8,128)(2,1)S(1)}, u32[]{:S(2)}, u32[]{:S(2)}) collective-permute-start(bf16[32,512]{1,0:T(8,128)(2,1)S(1)} %get-tuple-element.65), channel_id=1, source_target_pairs={{0,2},{1,3},{2,0},{3,1},{4,6},{5,7},{6,4},{7,5},{8,10},{9,11},{10,... | collective-permute-start | bytes 98312 | tf_op jit(solution)/shard_map/ppermute | solution.py:48
  98.5 17.7 %collective-permute-start.18 = (bf16[32,512]{1,0:T(8,128)(2,1)S(1)}, bf16[32,512]{1,0:T(8,128)(2,1)S(1)}, u32[]{:S(2)}, u32[]{:S(2)}) collective-permute-start(bf16[32,512]{1,0:T(8,128)(2,1)S(1)} %get-tuple-element.66), channel_id=1, source_target_pairs={{0,3},{1,2},{2,1},{3,0},{4,7},{5,6},{6,5},{7,4},{8,11},{9,10},{10,... | collective-permute-start | bytes 98312 | tf_op jit(solution)/shard_map/ppermute | solution.py:48
  109.8 1.2 %copy-start.20 = (f32[4,128,512]{2,1,0:T(8,128)S(1)}, f32[4,128,512]{2,1,0:T(8,128)}, u32[]{:S(2)}) copy-start(f32[4,128,512]{2,1,0:T(8,128)} %copy-done.19) | copy-start | bytes 3145732
  112.0 1.6 %copy-start.10 = (f32[2048,256]{1,0:T(8,128)S(1)}, f32[2048,256]{1,0:T(8,128)}, u32[]{:S(2)}) copy-start(f32[2048,256]{1,0:T(8,128)} %copy-done.9) | copy-start | bytes 6291460

commit v6 on v5

--- a/solution.py
+++ b/solution.py
@@ -10,7 +10,7 @@
 BF16 = jnp.bfloat16
 F32 = jnp.float32
 LANE_GROUP = 16
-CFG = {'cost': {}, 'direct': False, 'rsdirect': False, 'f2early': False, 'order': [[7, 4, 6, 5, 3, 2, 1], [7, 6, 5, 4, 3, 2, 1]], 'deps': {'h3': ['h7'], 'h2': ['h7'], 'h1': ['h7'], 'fx': ['h7', 'h4'], 'F1': ['M'], 'pair': ['F2'], 'unpack': ['add']}, 'a2a': [False, True]}
+CFG = {'cost': {}, 'direct': False, 'rsdirect': False, 'f2early': False, 'order': [[7, 4, 6, 5, 3, 2, 1], [7, 6, 5, 4, 3, 2, 1]], 'deps': {'F1': ['M'], 'pair': ['F2'], 'H0': ['h1', 'h2', 'h3', 'h4', 'h5', 'h6', 'h7'], 'Z1': ['add'], 'h3': ['h7'], 'h2': ['h7'], 'h1': ['h7'], 'fx': ['h7', 'h4']}, 'a2a': [False, True]}
 
 
 def iota(shape, dim):
@@ -25,7 +25,7 @@
     return lax.dot_general(a, b, (((da,), (db,)), ((), ())), preferred_element_type=F32)
 
 
-def call(body, outs, ins, scratch=(), spaces={}, limit=40 << 20, weight=0):
+def call(body, outs, ins, scratch=(), spaces={}, limit=40 << 20, weight=0, out_space=pltpu.VMEM):
     name = getattr(body, "func", body).__name__
     weight = CFG['cost'].get(name, 0)
     return pl.pallas_call(
@@ -33,7 +33,7 @@
         name=name,
         out_shape=outs,
         in_specs=[pl.BlockSpec(memory_space=spaces.get(n, pltpu.VMEM)) for n in range(len(ins))],
-        out_specs=[pl.BlockSpec(memory_space=pltpu.VMEM)] * len(outs),
+        out_specs=[pl.BlockSpec(memory_space=out_space)] * len(outs),
         scratch_shapes=list(scratch),
         compiler_params=pltpu.CompilerParams(vmem_limit_bytes=limit),
         cost_estimate=pl.CostEstimate(flops=0, bytes_accessed=weight, transcendentals=0),
@@ -109,26 +109,31 @@
 
 def mix_body(batch, seq, *refs):
     pieces, x_ref, alt_ref = refs[:batch], refs[batch], refs[batch + 1]
-    outs, p_scr, mix_scr, reg_scr = refs[batch + 2 : -3], refs[-3], refs[-2], refs[-1]
+    outs, p_scr, mix_scr, reg_scr, sems = refs[batch + 2 : -4], *refs[-4:]
     me, here = lax.axis_index("batch"), lax.axis_index("seq")
     blocks, rows, order = pieces[0].shape
     j_here = order // seq
+    width = x_ref.shape[1]
     from_rows = jnp.where(iota((order, order), 0) == alt_ref[...], 1.0, 0.0)
     p_scr[...] = from_rows.T.astype(BF16)
 
-    @pl.loop(0, blocks)
-    def _(i):
-        x = x_ref[pl.ds(pl.multiple_of(i * order, order), order), :]
+    writes = []
+    for i in range(blocks):
+        x = x_ref[i * order : (i + 1) * order, :]
         for d in range(batch):
             first = pl.multiple_of((me ^ d) * rows, rows)
             mix_scr[pl.ds(first, rows), :] = dot(pieces[d][i], x).astype(BF16)
-        reg_scr[...] = dot(p_scr[...], mix_scr[...]).astype(BF16)
+        result = dot(p_scr[...], mix_scr[...]).astype(BF16)
         if len(outs) == 1:
-            outs[0][:, i] = reg_scr[...].reshape(seq, j_here, x.shape[1])
+            reg_scr[i] = result.reshape(seq, j_here, width)
+            writes.append(pltpu.make_async_copy(reg_scr.at[i], outs[0].at[:, i], sems.at[i]))
+            writes[i].start()
         else:
+            reg_scr[i] = result.reshape(seq, j_here, width)
             for d in range(seq):
-                first = pl.multiple_of((here ^ d) * j_here, j_here)
-                outs[d][i] = reg_scr[pl.ds(first, j_here), :]
+                outs[d][i] = reg_scr[i, here ^ d]
+    for write in writes:
+        write.wait()
 
 
 def first_grad_body(batch, seq, *refs):
@@ -160,11 +165,10 @@
 
 
 def mix_back_body(batch, *refs):
-    pieces, dmixed_ref, second_ref, x_ref, cot_ref, src_ref = refs[:batch], *refs[batch:-3]
-    out_ref, weights_ref, h_ref = refs[-3:]
+    pieces, dmixed_ref, x_ref, cot_ref, src_ref = refs[:batch], *refs[batch:-2]
+    out_ref, h_ref = refs[-2:]
     me = lax.axis_index("batch")
     blocks, rows, order = pieces[0].shape
-    groups, count, lanes = second_ref.shape
 
     @pl.loop(0, blocks)
     def _(i):
@@ -173,7 +177,7 @@
             first = pl.multiple_of((me ^ d) * rows, rows)
             term = dot(pieces[d][i], dmixed_ref[i, pl.ds(first, rows), :], 0, 0)
             total = term if total is None else total + term
-        out_ref[pl.ds(pl.multiple_of(i * order, order), order), :] = total
+        out_ref[pl.ds(pl.multiple_of(i * order, order), order), :] = total.astype(BF16)
 
     width = x_ref.shape[1]
     select = one_hot(iota((width, width), 0) == src_ref[...])
@@ -182,14 +186,7 @@
     def _(i):
         part = pl.ds(pl.multiple_of(i * order, order), order)
         gate = jax.nn.sigmoid(dot(x_ref[part, :], select))
-        h_ref[part, :] = cot_ref[part, :].astype(F32) * gate * (1.0 - gate)
-
-    @pl.loop(0, groups)
-    def _(g):
-        packed = second_ref[g].astype(F32)
-        col = iota((count, lanes), 1) % LANE_GROUP
-        for jj in range(LANE_GROUP):
-            weights_ref[g, jj * count : (jj + 1) * count, :] = jnp.where(col == jj, packed, 0.0).astype(BF16)
+        h_ref[part, :] = (cot_ref[part, :].astype(F32) * gate * (1.0 - gate)).astype(BF16)
 
 
 def gather_blocks(seq, pieces, scr):
@@ -231,15 +228,20 @@
         outs[d][...] = jnp.concatenate(rows, axis=0).astype(BF16)
 
 
-def tokens_body(reg_ref, weights_ref, h_ref, src_ref, back_ref, out_ref):
+def tokens_body(reg_ref, second_ref, h_ref, src_ref, back_ref, out_ref):
     order, j_here, width = reg_ref.shape
     groups, lanes = j_here // LANE_GROUP, order * LANE_GROUP
     select = one_hot(iota((width, width), 0) == src_ref[...])
+    col = iota((order, lanes), 1) % LANE_GROUP
     for g in range(groups):
         reg = reg_ref[:, g * LANE_GROUP : (g + 1) * LANE_GROUP, :].reshape(lanes, width)
+        packed = second_ref[g].astype(F32)
+        weights = jnp.concatenate(
+            [jnp.where(col == jj, packed, 0.0).astype(BF16) for jj in range(LANE_GROUP)], axis=0
+        )
         rows = slice(g * lanes, (g + 1) * lanes)
-        dgate = (dot(weights_ref[g], reg) * h_ref[rows, :]).astype(BF16)
-        out_ref[rows, :] = (back_ref[rows, :] + dot(dgate, select, 1, 1)).astype(BF16)
+        dgate = (dot(weights, reg) * h_ref[rows, :].astype(F32)).astype(BF16)
+        out_ref[rows, :] = (back_ref[rows, :].astype(F32) + dot(dgate, select, 1, 1)).astype(BF16)
 
 
 def pair_body(own_a, own_b, got_a, got_b, out_a, out_b):
@@ -333,7 +335,13 @@
         functools.partial(mix_body, batch, seq),
         [of((seq, blocks, j_here, width))] if CFG['a2a'][1] else [piece] * seq,
         [dep("M", first_factor), *first[1:], x, alt],
-        [pltpu.VMEM((order, order), BF16), pltpu.VMEM((order, width), BF16), pltpu.VMEM((order, width), BF16)],
+        [
+            pltpu.VMEM((order, order), BF16),
+            pltpu.VMEM((order, width), BF16),
+            pltpu.VMEM((blocks, seq, j_here, width), BF16),
+            pltpu.SemaphoreType.DMA((blocks,)),
+        ],
+        out_space=pltpu.HBM if CFG['a2a'][1] else pltpu.VMEM,
     )
     keep("M", regrouped[0])
     got = {0: regrouped[0]}
@@ -354,10 +362,10 @@
     else:
         near = move("near", parts[1], "batch", 1, batch)
         far = move("far", parts[3], "batch", 1, batch)
-    dmix_in, weights, h = call(
+    dmix_in, h = call(
         functools.partial(mix_back_body, batch),
-        [of((rows_here, width), F32), of((groups, lanes, lanes)), of((rows_here, width), F32)],
-        [dep("F2", first_factor), *first[1:], dmixed, second, x, cot, src],
+        [of((rows_here, width))] * 2,
+        [dep("F2", first_factor), *first[1:], dmixed, x, cot, src],
     )
     keep("F2", dmix_in)
     if CFG['rsdirect']:
@@ -370,7 +378,7 @@
         rx = move("rx", summed, "batch", 2, batch)
         (grad_one,) = call(add_body, [of(parts[0].shape)], [kept, rx])
     keep("add", grad_one)
-    received = [after(got[0], dmix_in), *[got[d] for d in range(1, seq) if d in got]]
+    received = [dep("Z1", after(got[0], dmix_in)), *[got[d] for d in range(1, seq) if d in got]]
     if len(received) == 1:
         received = [received[0].reshape(count, j_here, width)]
     *terms, gathered = call(
@@ -383,7 +391,7 @@
         terms, gathered = [*terms, gathered], received[0]
     terms_got = [dep("unpack", terms[0])] + [move(f"R{d}", terms[d], "batch", d, batch) for d in (1, 2, 3)]
     (grad_tokens,) = call(
-        tokens_body, [of((rows_here, width))], [gathered, weights, h, src, dmix_in]
+        tokens_body, [of((rows_here, width))], [gathered, second, h, src, dmix_in]
     )
     (grad_flat,) = call(
         functools.partial(unpack_body, count), [of((m_here * count, j_here))], terms_got

time: 118 us -> 89.3 us (0.76)
  waiting for transfers between devices: 51.4 us -> 28.9 us
  starting transfers between devices: 25.3 us -> 22.4 us
  local copies, waits for them, and re-layouts: 21.2 us -> 18.6 us
    ppermute x19, waiting for transfers between devices: 51.4 us -> 28.9 us  [swap(): return lax.ppermute(value, axis, [(p, p ^ step) for p in range(size)])]
    ppermute x19, starting transfers between devices: 21.4 us -> 18.8 us  [swap(): return lax.ppermute(value, axis, [(p, p ^ step) for p in range(size)])]
    unnamed x64, local copies, waits for them, and re-layouts: 21.2 us -> 18.6 us
  transfers between devices with their start and end apart: 20 -> 20, of which waited for: 5 -> 6; matrix products, arithmetic and copies ran while one was open for 0% -> 0% of each run, Pallas kernels for 12% -> 17%
where the time goes in v6:
time: 89.3 us; the launch traced here: 88.7 us
  waiting for transfers between devices  28.9 us (32%)
  starting transfers between devices  22.4 us (25%)
  local copies, waits for them, and re-layouts  18.6 us (21%)
  Pallas kernels  18 us (20%)
    ppermute x19, waiting for transfers between devices, swap(): return lax.ppermute(value, axis, [(p, p ^ step) for p in range(size)])  28.9 us
    ppermute x19, starting transfers between devices, swap(): return lax.ppermute(value, axis, [(p, p ^ step) for p in range(size)])  18.8 us
    unnamed x64, local copies, waits for them, and re-layouts  18.6 us
    pallas_call x11, Pallas kernels, call(): pl.pallas_call(body, name=name, out_shape=outs, in_specs=[pl.BlockSpec(me...  18 us
    all_to_all x1, starting transfers between devices, packed_shards(): lax.all_to_all(dep('H0', regrouped[0]), 'seq', 0, 0, tiled=True)  3.67 us
  transfers between devices with their start and end apart: 20, of which 6 were waited for; matrix products, arithmetic and copies ran while one was open for 0% of the time, Pallas kernels for 17%

profile of v6, /device:TPU:0, one launch (start us, length us, event | category | flops | bytes accessed | tf_op | source)
XLA Modules:
  0.0 88.7 jit_solution(628469298793190377)
XLA Ops:
  0.6 0.8 copy-done.29
  1.5 0.4 pack_body.1.refs_0_
  1.9 2.4 %collective-permute-start.2 = (bf16[32,512]{1,0:T(8,128)(2,1)S(1)}, bf16[32,512]{1,0:T(8,128)(2,1)S(1)}, u32[]{:S(2)}, u32[]{:S(2)}) collective-permute-start(bf16[32,512]{1,0:T(8,128)(2,1)S(1)} %pack_body.1.refs_0_), channel_id=1, source_target_pairs={{0,3},{1,2},{2,1},{3,0},{4,7},{5,6},{6,5},{7,4},{8,11},{9,10},{10,... | collective-permute-start | bytes 98312 | tf_op jit(solution)/shard_map/ppermute | solution.py:48
  4.3 0.6 collective-permute-start.1
  5.0 0.0 collective-permute-start
  5.0 0.7 copy-done.30
  5.7 1.2 %copy-done = bf16[1,2048,256]{2,1,0:T(8,128)(2,1)S(1)} copy-done((bf16[1,2048,256]{2,1,0:T(8,128)(2,1)S(1)}, bf16[1,2048,256]{2,1,0:T(8,128)(2,1)}, u32[]{:S(2)}) %copy-start) | copy-done | bytes 1048600
  6.9 1.2 %copy-done.2 = bf16[1,2048,256]{2,1,0:T(8,128)(2,1)S(1)} copy-done((bf16[1,2048,256]{2,1,0:T(8,128)(2,1)S(1)}, bf16[1,2048,256]{2,1,0:T(8,128)(2,1)}, u32[]{:S(2)}) %copy-start.2) | copy-done | bytes 1048600
  8.1 0.5 gate_body.1.refs_4_.refs_1_
  8.6 0.0 copy-start.1
  8.7 0.0 collective-permute-done.1.refs_2_
  8.7 0.5 copy-done.5
  9.2 1.7 %collective-permute-start.4 = (bf16[4,128,512]{2,1,0:T(8,128)(2,1)S(1)}, bf16[4,128,512]{2,1,0:T(8,128)(2,1)S(1)}, u32[]{:S(2)}, u32[]{:S(2)}) collective-permute-start(bf16[4,128,512]{2,1,0:T(8,128)(2,1)S(1)} %copy-done.5), channel_id=1, source_target_pairs={{0,2},{1,3},{2,0},{3,1},{4,6},{5,7},{6,4},{7,5},{8,10},{9,11},{10,... | collective-permute-start | bytes 1572872 | tf_op jit(solution)/shard_map/ppermute | solution.py:48
  10.9 1.5 %regroup_back_body.1 = (bf16[4,64,256]{2,1,0:T(8,128)(2,1)S(1)}, bf16[4,64,256]{2,1,0:T(8,128)(2,1)S(1)}, bf16[4,64,256]{2,1,0:T(8,128)(2,1)S(1)}, bf16[4,64,256...) custom-call(bf16[32,512]{1,0:T(8,128)(2,1)S(1)} %pack_body.1.refs_0_, ...), custom_call_target="tpu_custom_call" | custom-call | tf_op jit(solution)/shard_map/regroup_back_body/pallas_call | solution.py:31
  12.4 4.6 %collective-permute-start.5 = (bf16[4,64,256]{2,1,0:T(8,128)(2,1)S(1)}, bf16[4,64,256]{2,1,0:T(8,128)(2,1)S(1)}, u32[]{:S(2)}, u32[]{:S(2)}) collective-permute-start(bf16[4,64,256]{2,1,0:T(8,128)(2,1)S(1)} %get-tuple-element.36), channel_id=1, source_target_pairs={{0,28},{4,24},{8,20},{12,16},{16,12},{20,8},{24,4},{28,0},{1,29},{... | collective-permute-start | bytes 393224 | tf_op jit(solution)/shard_map/ppermute | solution.py:48
  17.1 0.0 collective-permute-start.3
  17.1 4.6 %collective-permute-done.5.refs_7_ = bf16[4,64,256]{2,1,0:T(8,128)(2,1)S(1)} collective-permute-done((bf16[4,64,256]{2,1,0:T(8,128)(2,1)S(1)}, bf16[4,64,256]{2,1,0:T(8,128)(2,1)S(1)}, u32[]{:S(2)}, u32[]{:S(2)}) %collective-permute-start.5) | collective-permute-done | bytes 131104 | tf_op jit(solution)/shard_map/ppermute | solution.py:48
  21.6 6.5 %collective-permute-done.6.refs_4_ = bf16[4,64,256]{2,1,0:T(8,128)(2,1)S(1)} collective-permute-done((bf16[4,64,256]{2,1,0:T(8,128)(2,1)S(1)}, bf16[4,64,256]{2,1,0:T(8,128)(2,1)S(1)}, u32[]{:S(2)}, u32[]{:S(2)}) %collective-permute-start.6) | collective-permute-done | bytes 131104 | tf_op jit(solution)/shard_map/ppermute | solution.py:48
  28.1 0.6 copy-done.17
  28.8 0.0 collective-permute-done.4.refs_2_
  28.8 0.9 collective-permute-start.11
  29.7 1.8 %collective-permute-start.12 = (bf16[4,64,256]{2,1,0:T(8,128)(2,1)S(1)}, bf16[4,64,256]{2,1,0:T(8,128)(2,1)S(1)}, u32[]{:S(2)}, u32[]{:S(2)}) collective-permute-start(bf16[4,64,256]{2,1,0:T(8,128)(2,1)S(1)} %get-tuple-element.46), channel_id=1, source_target_pairs={{0,24},{4,28},{8,16},{12,20},{16,8},{20,12},{24,0},{28,4},{1,25},{... | collective-permute-start | bytes 393224 | tf_op jit(solution)/shard_map/ppermute | solution.py:48
  31.4 0.9 %collective-permute-start.8 = (bf16[4,64,256]{2,1,0:T(8,128)(2,1)S(1)}, bf16[4,64,256]{2,1,0:T(8,128)(2,1)S(1)}, u32[]{:S(2)}, u32[]{:S(2)}) collective-permute-start(bf16[4,64,256]{2,1,0:T(8,128)(2,1)S(1)} %get-tuple-element.40), channel_id=1, source_target_pairs={{0,4},{4,0},{8,12},{12,8},{16,20},{20,16},{24,28},{28,24},{1,5},{5... | collective-permute-start | bytes 393224 | tf_op jit(solution)/shard_map/ppermute | solution.py:48
  32.3 1.5 %collective-permute-start.9 = (bf16[4,64,256]{2,1,0:T(8,128)(2,1)S(1)}, bf16[4,64,256]{2,1,0:T(8,128)(2,1)S(1)}, u32[]{:S(2)}, u32[]{:S(2)}) collective-permute-start(bf16[4,64,256]{2,1,0:T(8,128)(2,1)S(1)} %get-tuple-element.42), channel_id=1, source_target_pairs={{0,8},{4,12},{8,0},{12,4},{16,24},{20,28},{24,16},{28,20},{1,9},{5... | collective-permute-start | bytes 393224 | tf_op jit(solution)/shard_map/ppermute | solution.py:48
  33.8 1.1 %collective-permute-start.10 = (bf16[4,64,256]{2,1,0:T(8,128)(2,1)S(1)}, bf16[4,64,256]{2,1,0:T(8,128)(2,1)S(1)}, u32[]{:S(2)}, u32[]{:S(2)}) collective-permute-start(bf16[4,64,256]{2,1,0:T(8,128)(2,1)S(1)} %get-tuple-element.44), channel_id=1, source_target_pairs={{0,12},{4,8},{8,4},{12,0},{16,28},{20,24},{24,20},{28,16},{1,13},{... | collective-permute-start | bytes 393224 | tf_op jit(solution)/shard_map/ppermute | solution.py:48
  34.9 3.3 %mix_body.1 = bf16[8,4,64,256]{3,2,1,0:T(8,128)(2,1)S(1)} custom-call(bf16[4,128,512]{2,1,0:T(8,128)(2,1)S(1)} %copy-done.5, bf16[4,128,512]{2,1,0:T(8,128)(2,1)S(1)} %collective-permute-done.3.refs_1_, bf16[4,128,512]{2,1,0:T(8,128)(2,1)S(1)} %collective-permute-done.4.refs_2_, bf16[4,128,512]{2,1,0:T(8,128)(2,1)S(1)} %collective-permute-done.7.refs_3_, ...), custom_call_target="tpu_custom_call" | custom-call | tf_op jit(solution)/shard_map/mix_body/pallas_call | solution.py:31
  38.2 0.0 copy-start.4
  38.2 1.0 %copy-done.4 = bf16[8,4,64,256]{3,2,1,0:T(8,128)(2,1)} copy-done((bf16[8,4,64,256]{3,2,1,0:T(8,128)(2,1)}, bf16[8,4,64,256]{3,2,1,0:T(8,128)(2,1)S(1)}, u32[]{:S(2)}) %copy-start.4) | copy-done | bytes 1048600
  39.2 2.1 %collective-permute-done.11.refs_5_ = bf16[4,64,256]{2,1,0:T(8,128)(2,1)S(1)} collective-permute-done((bf16[4,64,256]{2,1,0:T(8,128)(2,1)S(1)}, bf16[4,64,256]{2,1,0:T(8,128)(2,1)S(1)}, u32[]{:S(2)}, u32[]{:S(2)}) %collective-permute-start.11) | collective-permute-done | bytes 131104 | tf_op jit(solution)/shard_map/ppermute | solution.py:48
  41.3 0.7 copy-done.19
  42.0 0.0 collective-permute-done.12.refs_6_
  42.0 0.6 copy-done.21
  42.6 0.7 copy-done.23
  43.3 0.7 collective-permute-done.9.refs_2_
  44.0 0.7 copy-done.25
  44.6 1.7 %collective-permute-done.10.refs_3_ = bf16[4,64,256]{2,1,0:T(8,128)(2,1)S(1)} collective-permute-done((bf16[4,64,256]{2,1,0:T(8,128)(2,1)S(1)}, bf16[4,64,256]{2,1,0:T(8,128)(2,1)S(1)}, u32[]{:S(2)}, u32[]{:S(2)}) %collective-permute-start.10) | collective-permute-done | bytes 131104 | tf_op jit(solution)/shard_map/ppermute | solution.py:48
  46.4 0.6 copy-done.27
  47.0 3.7 %all-to-all-start = ((bf16[8,4,64,256]{3,2,1,0:T(8,128)(2,1)}), bf16[8,4,64,256]{3,2,1,0:T(8,128)(2,1)S(1)}, u32[]{:S(2)}, u32[]{:S(2)}) async-start(bf16[8,4,64,256]{3,2,1,0:T(8,128)(2,1)} %copy-done.4), calls=%async_computation | async-start | bytes 2097152 | tf_op jit(solution)/shard_map/all_to_all | solution.py:349
  50.7 0.9 %copy-done.18 = bf16[4,64,256]{2,1,0:T(8,128)(2,1)S(1)} copy-done((bf16[4,64,256]{2,1,0:T(8,128)(2,1)S(1)}, bf16[4,64,256]{2,1,0:T(8,128)(2,1)}, u32[]{:S(2)}) %copy-start.18) | copy-done | bytes 131096
  51.6 0.9 %copy-done.20 = bf16[4,64,256]{2,1,0:T(8,128)(2,1)S(1)} copy-done((bf16[4,64,256]{2,1,0:T(8,128)(2,1)S(1)}, bf16[4,64,256]{2,1,0:T(8,128)(2,1)}, u32[]{:S(2)}) %copy-start.20) | copy-done | bytes 131096
  52.5 0.9 %copy-done.22 = bf16[4,64,256]{2,1,0:T(8,128)(2,1)S(1)} copy-done((bf16[4,64,256]{2,1,0:T(8,128)(2,1)S(1)}, bf16[4,64,256]{2,1,0:T(8,128)(2,1)}, u32[]{:S(2)}) %copy-start.22) | copy-done | bytes 131096
  53.4 0.9 %copy-done.24 = bf16[4,64,256]{2,1,0:T(8,128)(2,1)S(1)} copy-done((bf16[4,64,256]{2,1,0:T(8,128)(2,1)S(1)}, bf16[4,64,256]{2,1,0:T(8,128)(2,1)}, u32[]{:S(2)}) %copy-start.24) | copy-done | bytes 131096
  54.3 0.9 %copy-done.26 = bf16[4,64,256]{2,1,0:T(8,128)(2,1)S(1)} copy-done((bf16[4,64,256]{2,1,0:T(8,128)(2,1)S(1)}, bf16[4,64,256]{2,1,0:T(8,128)(2,1)}, u32[]{:S(2)}) %copy-start.26) | copy-done | bytes 131096
  55.2 0.9 %copy-done.28 = bf16[4,64,256]{2,1,0:T(8,128)(2,1)S(1)} copy-done((bf16[4,64,256]{2,1,0:T(8,128)(2,1)S(1)}, bf16[4,64,256]{2,1,0:T(8,128)(2,1)}, u32[]{:S(2)}) %copy-start.28) | copy-done | bytes 131096
  56.1 3.0 %first_grad_body.1 = (bf16[4,128,512]{2,1,0:T(8,128)(2,1)S(1)}, bf16[4,128,512]{2,1,0:T(8,128)(2,1)S(1)}, bf16[4,128,512]{2,1,0:T(8,128)(2,1)S(1)}, bf16[4,128,5...) custom-call(bf16[4,64,256]{2,1,0:T(8,128)(2,1)S(1)} %get-tuple-element.49.refs_0_, bf16[4,64,256]{2,1,0:T(8,128)(2,1)S(1)} %copy-done.24, ...), custom_call_target="tpu_custom_call" | custom-call | tf_op jit(solution)/shard_map/first_grad_body/pallas_call | solution.py:31
  59.2 0.1 collective-permute-start.13
  59.2 0.5 collective-permute-start.14
  59.8 1.0 %copy-done.10 = bf16[4,128,512]{2,1,0:T(8,128)(2,1)S(1)} copy-done((bf16[4,128,512]{2,1,0:T(8,128)(2,1)S(1)}, bf16[4,128,512]{2,1,0:T(8,128)(2,1)}, u32[]{:S(2)}) %copy-start.10) | copy-done | bytes 524312
  60.8 1.0 %copy-done.12 = bf16[4,128,512]{2,1,0:T(8,128)(2,1)S(1)} copy-done((bf16[4,128,512]{2,1,0:T(8,128)(2,1)S(1)}, bf16[4,128,512]{2,1,0:T(8,128)(2,1)}, u32[]{:S(2)}) %copy-start.12) | copy-done | bytes 524312
  61.8 3.1 %mix_back_body.1 = (bf16[2048,256]{1,0:T(8,128)(2,1)S(1)}, bf16[2048,256]{1,0:T(8,128)(2,1)S(1)}) custom-call(bf16[4,128,512]{2,1,0:T(8,128)(2,1)S(1)} %copy-done.6, bf16[4,128,512]{2,1,0:T(8,128)(2,1)S(1)} %copy-done.10, bf16[4,128,512]{2,1,0:T(8,128)(2,1)S(1)} %copy-done.8, bf16[4,128,512]{2,1,0:T(8,128)(2,1)S(1)} %copy-done.12, ...), custom_call_target="tpu_custom_call" | custom-call | tf_op jit(solution)/shard_map/mix_back_body/pallas_call | solution.py:31
  64.9 1.0 %copy-done.13 = bf16[2048,256]{1,0:T(8,128)(2,1)} copy-done((bf16[2048,256]{1,0:T(8,128)(2,1)}, bf16[2048,256]{1,0:T(8,128)(2,1)S(1)}, u32[]{:S(2)}) %copy-start.13) | copy-done | bytes 1048600
  65.9 0.0 collective-permute-done.13.got_a
  65.9 0.0 collective-permute-done.14.got_b
  65.9 0.2 pair_body.1
  66.1 0.8 copy-done.15
  66.9 0.6 collective-permute-start.15
  67.5 13.3 %collective-permute-done.15.got = bf16[4,128,512]{2,1,0:T(8,128)(2,1)S(1)} collective-permute-done((bf16[4,128,512]{2,1,0:T(8,128)(2,1)S(1)}, bf16[4,128,512]{2,1,0:T(8,128)(2,1)S(1)}, u32[]{:S(2)}, u32[]{:S(2)}) %collective-permute-start.15) | collective-permute-done | bytes 524320 | tf_op jit(solution)/shard_map/ppermute | solution.py:48
  80.8 0.9 add_body.1
  81.7 1.3 %second_grad_body.1 = (bf16[32,512]{1,0:T(8,128)(2,1)S(1)}, bf16[32,512]{1,0:T(8,128)(2,1)S(1)}, bf16[32,512]{1,0:T(8,128)(2,1)S(1)}, bf16[32,512]{1,0:T(8,128)(2,1)S(1)}) custom-call(bf16[32,64,256]{2,1,0:T(8,128)(2,1)S(1)} %bitcast.16, bf16[2048,256]{1,0:T(8,128)(2,1)S(1)} %gate_body.1.refs_4_.refs_1_), custom_call_target="tpu_custom_call" | custom-call | tf_op jit(solution)/shard_map/second_grad_body/pallas_call | solution.py:31
  83.0 0.1 collective-permute-start.16
  83.1 0.7 collective-permute-start.17
  83.8 1.2 %collective-permute-start.18 = (bf16[32,512]{1,0:T(8,128)(2,1)S(1)}, bf16[32,512]{1,0:T(8,128)(2,1)S(1)}, u32[]{:S(2)}, u32[]{:S(2)}) collective-permute-start(bf16[32,512]{1,0:T(8,128)(2,1)S(1)} %get-tuple-element.66), channel_id=1, source_target_pairs={{0,3},{1,2},{2,1},{3,0},{4,7},{5,6},{6,5},{7,4},{8,11},{9,10},{10,... | collective-permute-start | bytes 98312 | tf_op jit(solution)/shard_map/ppermute | solution.py:48
  85.0 2.7 %tokens_body.1 = bf16[2048,256]{1,0:T(8,128)(2,1)} custom-call(bf16[32,64,256]{2,1,0:T(8,128)(2,1)S(1)} %bitcast.17, bf16[4,32,512]{2,1,0:T(8,128)(2,1)S(1)} %get-tuple-element.61.second_ref, bf16[2048,256]{1,0:T(8,128)(2,1)S(1)} %copy-done.16, s32[1,256]{1,0:T(1,128)S(1)} %bitcast.23, bf16[2048,256]{1,0:T(8,128)(2,1)S(1)} %copy-done.14), custom_call_target="tpu_custom_call" | custom-call | tf_op jit(solution)/shard_map/tokens_body/pallas_call | solution.py:31
  87.7 1.1 %unpack_body.1 = bf16[256,64]{1,0:T(8,128)(2,1)} custom-call(bf16[32,512]{1,0:T(8,128)(2,1)S(1)} %get-tuple-element.63.refs_0_, bf16[32,512]{1,0:T(8,128)(2,1)S(1)} %collective-permute-done.16.refs_1_, bf16[32,512]{1,0:T(8,128)(2,1)S(1)} %collective-permute-done.17.refs_2_, bf16[32,512]{1,0:T(8,128)(2,1)S(1)} %collective-permute-done.18.refs_3_), custom_call_target="tpu_custom_call" | custom-call | tf_op jit(solution)/shard_map/unpack_body/pallas_call | solution.py:31
  (51 shorter events, 0.1 us)
Async XLA Ops:
  0.6 0.8 copy-start.29
  1.9 6.8 %collective-permute-start.2 = (bf16[32,512]{1,0:T(8,128)(2,1)S(1)}, bf16[32,512]{1,0:T(8,128)(2,1)S(1)}, u32[]{:S(2)}, u32[]{:S(2)}) collective-permute-start(bf16[32,512]{1,0:T(8,128)(2,1)S(1)} %pack_body.1.refs_0_), channel_id=1, source_target_pairs={{0,3},{1,2},{2,1},{3,0},{4,7},{5,6},{6,5},{7,4},{8,11},{9,10},{10,... | collective-permute-start | bytes 98312 | tf_op jit(solution)/shard_map/ppermute | solution.py:48
  4.3 4.3 %collective-permute-start.1 = (bf16[32,512]{1,0:T(8,128)(2,1)S(1)}, bf16[32,512]{1,0:T(8,128)(2,1)S(1)}, u32[]{:S(2)}, u32[]{:S(2)}) collective-permute-start(bf16[32,512]{1,0:T(8,128)(2,1)S(1)} %pack_body.1.refs_0_), channel_id=1, source_target_pairs={{0,2},{1,3},{2,0},{3,1},{4,6},{5,7},{6,4},{7,5},{8,10},{9,11},{10,... | collective-permute-start | bytes 98312 | tf_op jit(solution)/shard_map/ppermute | solution.py:48
  5.0 3.7 %collective-permute-start = (bf16[32,512]{1,0:T(8,128)(2,1)S(1)}, bf16[32,512]{1,0:T(8,128)(2,1)S(1)}, u32[]{:S(2)}, u32[]{:S(2)}) collective-permute-start(bf16[32,512]{1,0:T(8,128)(2,1)S(1)} %pack_body.1.refs_0_), channel_id=1, source_target_pairs={{0,1},{1,0},{2,3},{3,2},{4,5},{5,4},{6,7},{7,6},{8,9},{9,8},{10,11... | collective-permute-start | bytes 98312 | tf_op jit(solution)/shard_map/ppermute | solution.py:48
  5.0 0.7 copy-start.30
  5.7 1.2 %copy-start = (bf16[1,2048,256]{2,1,0:T(8,128)(2,1)S(1)}, bf16[1,2048,256]{2,1,0:T(8,128)(2,1)}, u32[]{:S(2)}) copy-start(bf16[1,2048,256]{2,1,0:T(8,128)(2,1)} %param.6) | copy-start | bytes 3145732
  6.9 1.2 %copy-start.2 = (bf16[1,2048,256]{2,1,0:T(8,128)(2,1)S(1)}, bf16[1,2048,256]{2,1,0:T(8,128)(2,1)}, u32[]{:S(2)}) copy-start(bf16[1,2048,256]{2,1,0:T(8,128)(2,1)} %param.7) | copy-start | bytes 3145732
  8.1 1.0 %copy-start.5 = (bf16[4,128,512]{2,1,0:T(8,128)(2,1)S(1)}, bf16[4,128,512]{2,1,0:T(8,128)(2,1)}, u32[]{:S(2)}) copy-start(bf16[4,128,512]{2,1,0:T(8,128)(2,1)} %refs_0_.3) | copy-start | bytes 1572868
  8.6 26.3 %copy-start.1 = (bf16[1,2048,256]{2,1,0:T(8,128)(2,1)S(1)}, bf16[1,2048,256]{2,1,0:T(8,128)(2,1)}, u32[]{:S(2)}) copy-start(bf16[1,2048,256]{2,1,0:T(8,128)(2,1)} %param.6) | copy-start | bytes 3145732
  9.2 19.6 %collective-permute-start.4 = (bf16[4,128,512]{2,1,0:T(8,128)(2,1)S(1)}, bf16[4,128,512]{2,1,0:T(8,128)(2,1)S(1)}, u32[]{:S(2)}, u32[]{:S(2)}) collective-permute-start(bf16[4,128,512]{2,1,0:T(8,128)(2,1)S(1)} %copy-done.5), channel_id=1, source_target_pairs={{0,2},{1,3},{2,0},{3,1},{4,6},{5,7},{6,4},{7,5},{8,10},{9,11},{10,... | collective-permute-start | bytes 1572872 | tf_op jit(solution)/shard_map/ppermute | solution.py:48
  12.4 9.2 %collective-permute-start.5 = (bf16[4,64,256]{2,1,0:T(8,128)(2,1)S(1)}, bf16[4,64,256]{2,1,0:T(8,128)(2,1)S(1)}, u32[]{:S(2)}, u32[]{:S(2)}) collective-permute-start(bf16[4,64,256]{2,1,0:T(8,128)(2,1)S(1)} %get-tuple-element.36), channel_id=1, source_target_pairs={{0,28},{4,24},{8,20},{12,16},{16,12},{20,8},{24,4},{28,0},{1,29},{... | collective-permute-start | bytes 393224 | tf_op jit(solution)/shard_map/ppermute | solution.py:48
  17.1 11.1 %collective-permute-start.6 = (bf16[4,64,256]{2,1,0:T(8,128)(2,1)S(1)}, bf16[4,64,256]{2,1,0:T(8,128)(2,1)S(1)}, u32[]{:S(2)}, u32[]{:S(2)}) collective-permute-start(bf16[4,64,256]{2,1,0:T(8,128)(2,1)S(1)} %get-tuple-element.37), channel_id=1, source_target_pairs={{0,16},{4,20},{8,24},{12,28},{16,0},{20,4},{24,8},{28,12},{1,17},{... | collective-permute-start | bytes 393224 | tf_op jit(solution)/shard_map/ppermute | solution.py:48
  17.1 15.3 %collective-permute-start.3 = (bf16[4,128,512]{2,1,0:T(8,128)(2,1)S(1)}, bf16[4,128,512]{2,1,0:T(8,128)(2,1)S(1)}, u32[]{:S(2)}, u32[]{:S(2)}) collective-permute-start(bf16[4,128,512]{2,1,0:T(8,128)(2,1)S(1)} %copy-done.5), channel_id=1, source_target_pairs={{0,1},{1,0},{2,3},{3,2},{4,5},{5,4},{6,7},{7,6},{8,9},{9,8},{10,11... | collective-permute-start | bytes 1572872 | tf_op jit(solution)/shard_map/ppermute | solution.py:48
  28.1 0.6 copy-start.17
  28.8 9.4 %copy-start.7 = (bf16[4,128,512]{2,1,0:T(8,128)(2,1)}, bf16[4,128,512]{2,1,0:T(8,128)(2,1)S(1)}, u32[]{:S(2)}) copy-start(bf16[4,128,512]{2,1,0:T(8,128)(2,1)S(1)} %collective-permute-done.4.refs_2_) | copy-start | bytes 1572868
  28.8 5.0 %collective-permute-start.7 = (bf16[4,128,512]{2,1,0:T(8,128)(2,1)S(1)}, bf16[4,128,512]{2,1,0:T(8,128)(2,1)S(1)}, u32[]{:S(2)}, u32[]{:S(2)}) collective-permute-start(bf16[4,128,512]{2,1,0:T(8,128)(2,1)S(1)} %collective-permute-done.4.refs_2_), channel_id=1, source_target_pairs={{0,1},{1,0},{2,3},{3,2},{4,5},{5,4},{6,7},{7,6},{8,9},{9,8},{10,11... | collective-permute-start | bytes 1572872 | tf_op jit(solution)/shard_map/ppermute | solution.py:48
  28.8 12.5 %collective-permute-start.11 = (bf16[4,64,256]{2,1,0:T(8,128)(2,1)S(1)}, bf16[4,64,256]{2,1,0:T(8,128)(2,1)S(1)}, u32[]{:S(2)}, u32[]{:S(2)}) collective-permute-start(bf16[4,64,256]{2,1,0:T(8,128)(2,1)S(1)} %get-tuple-element.45), channel_id=1, source_target_pairs={{0,20},{4,16},{8,28},{12,24},{16,4},{20,0},{24,12},{28,8},{1,21},{... | collective-permute-start | bytes 393224 | tf_op jit(solution)/shard_map/ppermute | solution.py:48
  29.7 12.3 %collective-permute-start.12 = (bf16[4,64,256]{2,1,0:T(8,128)(2,1)S(1)}, bf16[4,64,256]{2,1,0:T(8,128)(2,1)S(1)}, u32[]{:S(2)}, u32[]{:S(2)}) collective-permute-start(bf16[4,64,256]{2,1,0:T(8,128)(2,1)S(1)} %get-tuple-element.46), channel_id=1, source_target_pairs={{0,24},{4,28},{8,16},{12,20},{16,8},{20,12},{24,0},{28,4},{1,25},{... | collective-permute-start | bytes 393224 | tf_op jit(solution)/shard_map/ppermute | solution.py:48
  31.4 3.5 %copy-start.31 = (s32[512]{0:T(512)S(1)}, s32[512]{0:T(512)}, u32[]{:S(2)}) copy-start(s32[512]{0:T(512)} %param.11) | copy-start | bytes 6148
  31.4 11.2 %collective-permute-start.8 = (bf16[4,64,256]{2,1,0:T(8,128)(2,1)S(1)}, bf16[4,64,256]{2,1,0:T(8,128)(2,1)S(1)}, u32[]{:S(2)}, u32[]{:S(2)}) collective-permute-start(bf16[4,64,256]{2,1,0:T(8,128)(2,1)S(1)} %get-tuple-element.40), channel_id=1, source_target_pairs={{0,4},{4,0},{8,12},{12,8},{16,20},{20,16},{24,28},{28,24},{1,5},{5... | collective-permute-start | bytes 393224 | tf_op jit(solution)/shard_map/ppermute | solution.py:48
  32.3 5.9 %copy-start.9 = (bf16[4,128,512]{2,1,0:T(8,128)(2,1)}, bf16[4,128,512]{2,1,0:T(8,128)(2,1)S(1)}, u32[]{:S(2)}) copy-start(bf16[4,128,512]{2,1,0:T(8,128)(2,1)S(1)} %collective-permute-done.3.refs_1_) | copy-start | bytes 1572868
  32.3 11.7 %collective-permute-start.9 = (bf16[4,64,256]{2,1,0:T(8,128)(2,1)S(1)}, bf16[4,64,256]{2,1,0:T(8,128)(2,1)S(1)}, u32[]{:S(2)}, u32[]{:S(2)}) collective-permute-start(bf16[4,64,256]{2,1,0:T(8,128)(2,1)S(1)} %get-tuple-element.42), channel_id=1, source_target_pairs={{0,8},{4,12},{8,0},{12,4},{16,24},{20,28},{24,16},{28,20},{1,9},{5... | collective-permute-start | bytes 393224 | tf_op jit(solution)/shard_map/ppermute | solution.py:48
  33.8 4.4 %copy-start.11 = (bf16[4,128,512]{2,1,0:T(8,128)(2,1)}, bf16[4,128,512]{2,1,0:T(8,128)(2,1)S(1)}, u32[]{:S(2)}) copy-start(bf16[4,128,512]{2,1,0:T(8,128)(2,1)S(1)} %collective-permute-done.7.refs_3_) | copy-start | bytes 1572868
  33.8 12.6 %collective-permute-start.10 = (bf16[4,64,256]{2,1,0:T(8,128)(2,1)S(1)}, bf16[4,64,256]{2,1,0:T(8,128)(2,1)S(1)}, u32[]{:S(2)}, u32[]{:S(2)}) collective-permute-start(bf16[4,64,256]{2,1,0:T(8,128)(2,1)S(1)} %get-tuple-element.44), channel_id=1, source_target_pairs={{0,12},{4,8},{8,4},{12,0},{16,28},{20,24},{24,20},{28,16},{1,13},{... | collective-permute-start | bytes 393224 | tf_op jit(solution)/shard_map/ppermute | solution.py:48
  38.2 1.0 %copy-start.4 = (bf16[8,4,64,256]{3,2,1,0:T(8,128)(2,1)}, bf16[8,4,64,256]{3,2,1,0:T(8,128)(2,1)S(1)}, u32[]{:S(2)}) copy-start(bf16[8,4,64,256]{3,2,1,0:T(8,128)(2,1)S(1)} %mix_body.1) | copy-start | bytes 3145732
  41.3 0.7 copy-start.19
  42.0 0.6 copy-start.21
  42.6 0.7 copy-start.23
  44.0 0.7 copy-start.25
  46.4 0.6 copy-start.27
  47.0 34.6 %all-to-all-start = ((bf16[8,4,64,256]{3,2,1,0:T(8,128)(2,1)}), bf16[8,4,64,256]{3,2,1,0:T(8,128)(2,1)S(1)}, u32[]{:S(2)}, u32[]{:S(2)}) async-start(bf16[8,4,64,256]{3,2,1,0:T(8,128)(2,1)} %copy-done.4), calls=%async_computation | async-start | bytes 2097152 | tf_op jit(solution)/shard_map/all_to_all | solution.py:349
  50.7 0.9 %copy-start.18 = (bf16[4,64,256]{2,1,0:T(8,128)(2,1)S(1)}, bf16[4,64,256]{2,1,0:T(8,128)(2,1)}, u32[]{:S(2)}) copy-start(bf16[4,64,256]{2,1,0:T(8,128)(2,1)} %copy-done.17) | copy-start | bytes 393220
  51.6 0.9 %copy-start.20 = (bf16[4,64,256]{2,1,0:T(8,128)(2,1)S(1)}, bf16[4,64,256]{2,1,0:T(8,128)(2,1)}, u32[]{:S(2)}) copy-start(bf16[4,64,256]{2,1,0:T(8,128)(2,1)} %copy-done.19) | copy-start | bytes 393220
  52.5 0.9 %copy-start.22 = (bf16[4,64,256]{2,1,0:T(8,128)(2,1)S(1)}, bf16[4,64,256]{2,1,0:T(8,128)(2,1)}, u32[]{:S(2)}) copy-start(bf16[4,64,256]{2,1,0:T(8,128)(2,1)} %copy-done.21) | copy-start | bytes 393220
  53.4 0.9 %copy-start.24 = (bf16[4,64,256]{2,1,0:T(8,128)(2,1)S(1)}, bf16[4,64,256]{2,1,0:T(8,128)(2,1)}, u32[]{:S(2)}) copy-start(bf16[4,64,256]{2,1,0:T(8,128)(2,1)} %copy-done.23) | copy-start | bytes 393220
  54.3 0.9 %copy-start.26 = (bf16[4,64,256]{2,1,0:T(8,128)(2,1)S(1)}, bf16[4,64,256]{2,1,0:T(8,128)(2,1)}, u32[]{:S(2)}) copy-start(bf16[4,64,256]{2,1,0:T(8,128)(2,1)} %copy-done.25) | copy-start | bytes 393220
  55.2 0.9 %copy-start.28 = (bf16[4,64,256]{2,1,0:T(8,128)(2,1)S(1)}, bf16[4,64,256]{2,1,0:T(8,128)(2,1)}, u32[]{:S(2)}) copy-start(bf16[4,64,256]{2,1,0:T(8,128)(2,1)} %copy-done.27) | copy-start | bytes 393220
  56.1 3.6 %copy-start.3 = (bf16[1,2048,256]{2,1,0:T(8,128)(2,1)S(1)}, bf16[1,2048,256]{2,1,0:T(8,128)(2,1)}, u32[]{:S(2)}) copy-start(bf16[1,2048,256]{2,1,0:T(8,128)(2,1)} %param.7) | copy-start | bytes 3145732
  56.1 3.6 %copy-start.6 = (bf16[4,128,512]{2,1,0:T(8,128)(2,1)S(1)}, bf16[4,128,512]{2,1,0:T(8,128)(2,1)}, u32[]{:S(2)}) copy-start(bf16[4,128,512]{2,1,0:T(8,128)(2,1)} %refs_0_.3) | copy-start | bytes 1572868
  56.1 3.6 %copy-start.8 = (bf16[4,128,512]{2,1,0:T(8,128)(2,1)S(1)}, bf16[4,128,512]{2,1,0:T(8,128)(2,1)}, u32[]{:S(2)}) copy-start(bf16[4,128,512]{2,1,0:T(8,128)(2,1)} %copy-done.7) | copy-start | bytes 1572868
  59.2 6.7 %collective-permute-start.13 = (bf16[4,128,512]{2,1,0:T(8,128)(2,1)S(1)}, bf16[4,128,512]{2,1,0:T(8,128)(2,1)S(1)}, u32[]{:S(2)}, u32[]{:S(2)}) collective-permute-start(bf16[4,128,512]{2,1,0:T(8,128)(2,1)S(1)} %get-tuple-element.56), channel_id=1, source_target_pairs={{0,1},{1,0},{2,3},{3,2},{4,5},{5,4},{6,7},{7,6},{8,9},{9,8},{10,11... | collective-permute-start | bytes 1572872 | tf_op jit(solution)/shard_map/ppermute | solution.py:48
  59.2 6.7 %collective-permute-start.14 = (bf16[4,128,512]{2,1,0:T(8,128)(2,1)S(1)}, bf16[4,128,512]{2,1,0:T(8,128)(2,1)S(1)}, u32[]{:S(2)}, u32[]{:S(2)}) collective-permute-start(bf16[4,128,512]{2,1,0:T(8,128)(2,1)S(1)} %get-tuple-element.57), channel_id=1, source_target_pairs={{0,1},{1,0},{2,3},{3,2},{4,5},{5,4},{6,7},{7,6},{8,9},{9,8},{10,11... | collective-permute-start | bytes 1572872 | tf_op jit(solution)/shard_map/ppermute | solution.py:48
  59.7 1.0 %copy-start.10 = (bf16[4,128,512]{2,1,0:T(8,128)(2,1)S(1)}, bf16[4,128,512]{2,1,0:T(8,128)(2,1)}, u32[]{:S(2)}) copy-start(bf16[4,128,512]{2,1,0:T(8,128)(2,1)} %copy-done.9) | copy-start | bytes 1572868
  60.8 1.0 %copy-start.12 = (bf16[4,128,512]{2,1,0:T(8,128)(2,1)S(1)}, bf16[4,128,512]{2,1,0:T(8,128)(2,1)}, u32[]{:S(2)}) copy-start(bf16[4,128,512]{2,1,0:T(8,128)(2,1)} %copy-done.11) | copy-start | bytes 1572868
  64.9 1.0 %copy-start.13 = (bf16[2048,256]{1,0:T(8,128)(2,1)}, bf16[2048,256]{1,0:T(8,128)(2,1)S(1)}, u32[]{:S(2)}) copy-start(bf16[2048,256]{1,0:T(8,128)(2,1)S(1)} %get-tuple-element.51.back_ref) | copy-start | bytes 3145732
  65.9 1.0 %copy-start.15 = (bf16[2048,256]{1,0:T(8,128)(2,1)}, bf16[2048,256]{1,0:T(8,128)(2,1)S(1)}, u32[]{:S(2)}) copy-start(bf16[2048,256]{1,0:T(8,128)(2,1)S(1)} %get-tuple-element.62.h_ref) | copy-start | bytes 3145732
  66.9 13.9 %collective-permute-start.15 = (bf16[4,128,512]{2,1,0:T(8,128)(2,1)S(1)}, bf16[4,128,512]{2,1,0:T(8,128)(2,1)S(1)}, u32[]{:S(2)}, u32[]{:S(2)}) collective-permute-start(bf16[4,128,512]{2,1,0:T(8,128)(2,1)S(1)} %get-tuple-element.59), channel_id=1, source_target_pairs={{0,2},{1,3},{2,0},{3,1},{4,6},{5,7},{6,4},{7,5},{8,10},{9,11},{10,... | collective-permute-start | bytes 1572872 | tf_op jit(solution)/shard_map/ppermute | solution.py:48
  81.7 3.3 %copy-start.14 = (bf16[2048,256]{1,0:T(8,128)(2,1)S(1)}, bf16[2048,256]{1,0:T(8,128)(2,1)}, u32[]{:S(2)}) copy-start(bf16[2048,256]{1,0:T(8,128)(2,1)} %copy-done.13) | copy-start | bytes 3145732
  81.7 3.3 %copy-start.16 = (bf16[2048,256]{1,0:T(8,128)(2,1)S(1)}, bf16[2048,256]{1,0:T(8,128)(2,1)}, u32[]{:S(2)}) copy-start(bf16[2048,256]{1,0:T(8,128)(2,1)} %copy-done.15) | copy-start | bytes 3145732
  83.0 4.7 %collective-permute-start.16 = (bf16[32,512]{1,0:T(8,128)(2,1)S(1)}, bf16[32,512]{1,0:T(8,128)(2,1)S(1)}, u32[]{:S(2)}, u32[]{:S(2)}) collective-permute-start(bf16[32,512]{1,0:T(8,128)(2,1)S(1)} %get-tuple-element.64), channel_id=1, source_target_pairs={{0,1},{1,0},{2,3},{3,2},{4,5},{5,4},{6,7},{7,6},{8,9},{9,8},{10,11... | collective-permute-start | bytes 98312 | tf_op jit(solution)/shard_map/ppermute | solution.py:48
  83.1 4.6 %collective-permute-start.17 = (bf16[32,512]{1,0:T(8,128)(2,1)S(1)}, bf16[32,512]{1,0:T(8,128)(2,1)S(1)}, u32[]{:S(2)}, u32[]{:S(2)}) collective-permute-start(bf16[32,512]{1,0:T(8,128)(2,1)S(1)} %get-tuple-element.65), channel_id=1, source_target_pairs={{0,2},{1,3},{2,0},{3,1},{4,6},{5,7},{6,4},{7,5},{8,10},{9,11},{10,... | collective-permute-start | bytes 98312 | tf_op jit(solution)/shard_map/ppermute | solution.py:48
  83.8 3.9 %collective-permute-start.18 = (bf16[32,512]{1,0:T(8,128)(2,1)S(1)}, bf16[32,512]{1,0:T(8,128)(2,1)S(1)}, u32[]{:S(2)}, u32[]{:S(2)}) collective-permute-start(bf16[32,512]{1,0:T(8,128)(2,1)S(1)} %get-tuple-element.66), channel_id=1, source_target_pairs={{0,3},{1,2},{2,1},{3,0},{4,7},{5,6},{6,5},{7,4},{8,11},{9,10},{10,... | collective-permute-start | bytes 98312 | tf_op jit(solution)/shard_map/ppermute | solution.py:48

commit v7 on v6

--- a/solution.py
+++ b/solution.py
@@ -10,7 +10,7 @@
 BF16 = jnp.bfloat16
 F32 = jnp.float32
 LANE_GROUP = 16
-CFG = {'cost': {}, 'direct': False, 'rsdirect': False, 'f2early': False, 'order': [[7, 4, 6, 5, 3, 2, 1], [7, 6, 5, 4, 3, 2, 1]], 'deps': {'F1': ['M'], 'pair': ['F2'], 'H0': ['h1', 'h2', 'h3', 'h4', 'h5', 'h6', 'h7'], 'Z1': ['add'], 'h3': ['h7'], 'h2': ['h7'], 'h1': ['h7'], 'fx': ['h7', 'h4']}, 'a2a': [False, True]}
+CFG = {'a2a': [False, False], 'cost': {}, 'direct': False, 'rsdirect': False, 'f2early': False, 'order': [[7, 6, 5, 4, 3, 2, 1], [7, 6, 5, 4, 3, 2, 1]], 'deps': {'h3': ['h7'], 'h2': ['h7'], 'h1': ['h7'], 'fx': ['h7', 'h4'], 'F1': ['M', 'H1', 'H2', 'H3', 'fx'], 'near': ['H7', 'H6'], 'far': ['H7', 'H6'], 'pair': ['F2'], 'Z1': ['add'], 'H1': ['h3'], 'H2': ['M']}}
 
 
 def iota(shape, dim):
@@ -108,14 +108,15 @@
 
 
 def mix_body(batch, seq, *refs):
-    pieces, x_ref, alt_ref = refs[:batch], refs[batch], refs[batch + 1]
-    outs, p_scr, mix_scr, reg_scr, sems = refs[batch + 2 : -4], *refs[-4:]
+    pieces, x_ref, alt_ref, cot_ref, src_ref = refs[:batch], *refs[batch : batch + 4]
+    outs, h_ref, p_scr, mix_scr, reg_scr, sems = refs[batch + 4 : -5], *refs[-5:]
     me, here = lax.axis_index("batch"), lax.axis_index("seq")
     blocks, rows, order = pieces[0].shape
     j_here = order // seq
     width = x_ref.shape[1]
     from_rows = jnp.where(iota((order, order), 0) == alt_ref[...], 1.0, 0.0)
     p_scr[...] = from_rows.T.astype(BF16)
+    select = one_hot(iota((width, width), 0) == src_ref[...])
 
     writes = []
     for i in range(blocks):
@@ -132,6 +133,9 @@
             reg_scr[i] = result.reshape(seq, j_here, width)
             for d in range(seq):
                 outs[d][i] = reg_scr[i, here ^ d]
+        gate = jax.nn.sigmoid(dot(x, select))
+        cot = cot_ref[i * order : (i + 1) * order, :].astype(F32)
+        h_ref[i * order : (i + 1) * order, :] = (cot * gate * (1.0 - gate)).astype(BF16)
     for write in writes:
         write.wait()
 
@@ -165,8 +169,7 @@
 
 
 def mix_back_body(batch, *refs):
-    pieces, dmixed_ref, x_ref, cot_ref, src_ref = refs[:batch], *refs[batch:-2]
-    out_ref, h_ref = refs[-2:]
+    pieces, dmixed_ref, out_ref = refs[:batch], *refs[batch:]
     me = lax.axis_index("batch")
     blocks, rows, order = pieces[0].shape
 
@@ -178,15 +181,6 @@
             term = dot(pieces[d][i], dmixed_ref[i, pl.ds(first, rows), :], 0, 0)
             total = term if total is None else total + term
         out_ref[pl.ds(pl.multiple_of(i * order, order), order), :] = total.astype(BF16)
-
-    width = x_ref.shape[1]
-    select = one_hot(iota((width, width), 0) == src_ref[...])
-
-    @pl.loop(0, blocks)
-    def _(i):
-        part = pl.ds(pl.multiple_of(i * order, order), order)
-        gate = jax.nn.sigmoid(dot(x_ref[part, :], select))
-        h_ref[part, :] = (cot_ref[part, :].astype(F32) * gate * (1.0 - gate)).astype(BF16)
 
 
 def gather_blocks(seq, pieces, scr):
@@ -331,17 +325,16 @@
     if direct is None:
         direct = move("fx", across, "batch", 1, batch)
     first = [first_factor, beside, across, direct]
-    regrouped = call(
+    *regrouped, h = call(
         functools.partial(mix_body, batch, seq),
-        [of((seq, blocks, j_here, width))] if CFG['a2a'][1] else [piece] * seq,
-        [dep("M", first_factor), *first[1:], x, alt],
+        [piece] * seq + [of((rows_here, width))],
+        [dep("M", first_factor), *first[1:], x, alt, cot, src],
         [
             pltpu.VMEM((order, order), BF16),
             pltpu.VMEM((order, width), BF16),
             pltpu.VMEM((blocks, seq, j_here, width), BF16),
             pltpu.SemaphoreType.DMA((blocks,)),
         ],
-        out_space=pltpu.HBM if CFG['a2a'][1] else pltpu.VMEM,
     )
     keep("M", regrouped[0])
     got = {0: regrouped[0]}
@@ -362,10 +355,10 @@
     else:
         near = move("near", parts[1], "batch", 1, batch)
         far = move("far", parts[3], "batch", 1, batch)
-    dmix_in, h = call(
+    (dmix_in,) = call(
         functools.partial(mix_back_body, batch),
-        [of((rows_here, width))] * 2,
-        [dep("F2", first_factor), *first[1:], dmixed, x, cot, src],
+        [of((rows_here, width))],
+        [dep("F2", first_factor), *first[1:], dmixed],
     )
     keep("F2", dmix_in)
     if CFG['rsdirect']:

time: 89.3 us -> 84.1 us (0.942)
  local copies, waits for them, and re-layouts: 18.6 us -> 4.48 us
  starting transfers between devices: 22.4 us -> 35.2 us
  Pallas kernels: 18 us -> 16 us
  waiting for transfers between devices: 28.9 us -> 27.3 us
    ppermute x19 -> x26, starting transfers between devices: 18.8 us -> 35.2 us  [swap(): return lax.ppermute(value, axis, [(p, p ^ step) for p in range(size)])]
    unnamed x64 -> x16, local copies, waits for them, and re-layouts: 18.6 us -> 4.48 us
    all_to_all x1 -> x0, starting transfers between devices: 3.67 us -> none  [packed_shards(): lax.all_to_all(dep('H0', regrouped[0]), 'seq', 0, 0, tiled=True)]
    pallas_call x11, Pallas kernels: 18 us -> 16 us  [call(): pl.pallas_call(body, name=name, out_shape=outs, in_specs=[pl.BlockSpec(me...]
    ppermute x19 -> x26, waiting for transfers between devices: 28.9 us -> 27.3 us  [swap(): return lax.ppermute(value, axis, [(p, p ^ step) for p in range(size)])]
  transfers between devices with their start and end apart: 20 -> 26, of which waited for: 6 -> 9; matrix products, arithmetic and copies ran while one was open for 0% -> 0% of each run, Pallas kernels for 17% -> 15%
where the time goes in v7:
time: 84.1 us; the launch traced here: 83.8 us
  starting transfers between devices  35.2 us (42%)
  waiting for transfers between devices  27.3 us (32%)
  Pallas kernels  16 us (19%)
  local copies, waits for them, and re-layouts  4.48 us (5%)
    ppermute x26, starting transfers between devices, swap(): return lax.ppermute(value, axis, [(p, p ^ step) for p in range(size)])  35.2 us
    ppermute x26, waiting for transfers between devices, swap(): return lax.ppermute(value, axis, [(p, p ^ step) for p in range(size)])  27.3 us
    pallas_call x11, Pallas kernels, call(): pl.pallas_call(body, name=name, out_shape=outs, in_specs=[pl.BlockSpec(me...  16 us
    unnamed x16, local copies, waits for them, and re-layouts  4.48 us
  transfers between devices with their start and end apart: 26, of which 9 were waited for; matrix products, arithmetic and copies ran while one was open for 0% of the time, Pallas kernels for 15%

profile of v7, /device:TPU:0, one launch (start us, length us, event | category | flops | bytes accessed | tf_op | source)
XLA Modules:
  0.0 83.8 jit_solution(4057295927402600854)
XLA Ops:
  0.6 0.8 copy-done.5
  1.5 0.4 pack_body.1.refs_0_
  1.9 2.4 %collective-permute-start.2 = (bf16[32,512]{1,0:T(8,128)(2,1)S(1)}, bf16[32,512]{1,0:T(8,128)(2,1)S(1)}, u32[]{:S(2)}, u32[]{:S(2)}) collective-permute-start(bf16[32,512]{1,0:T(8,128)(2,1)S(1)} %pack_body.1.refs_0_), channel_id=1, source_target_pairs={{0,3},{1,2},{2,1},{3,0},{4,7},{5,6},{6,5},{7,4},{8,11},{9,10},{10,... | collective-permute-start | bytes 98312 | tf_op jit(solution)/shard_map/ppermute | solution.py:48
  4.3 0.6 collective-permute-start.1
  5.0 0.0 collective-permute-start
  5.0 0.7 copy-done.6
  5.7 1.2 %copy-done = bf16[1,2048,256]{2,1,0:T(8,128)(2,1)S(1)} copy-done((bf16[1,2048,256]{2,1,0:T(8,128)(2,1)S(1)}, bf16[1,2048,256]{2,1,0:T(8,128)(2,1)}, u32[]{:S(2)}) %copy-start) | copy-done | bytes 1048600
  6.9 1.2 %copy-done.2 = bf16[1,2048,256]{2,1,0:T(8,128)(2,1)S(1)} copy-done((bf16[1,2048,256]{2,1,0:T(8,128)(2,1)S(1)}, bf16[1,2048,256]{2,1,0:T(8,128)(2,1)}, u32[]{:S(2)}) %copy-start.2) | copy-done | bytes 1048600
  8.1 0.5 gate_body.1.refs_4_.refs_8_
  8.6 0.0 copy-start.1
  8.6 0.0 collective-permute-done.2.refs_3_
  8.7 0.0 collective-permute-done.1.refs_2_
  8.7 0.0 collective-permute-done.refs_1_
  8.7 0.5 copy-done.4
  9.2 1.7 %collective-permute-start.4 = (bf16[4,128,512]{2,1,0:T(8,128)(2,1)S(1)}, bf16[4,128,512]{2,1,0:T(8,128)(2,1)S(1)}, u32[]{:S(2)}, u32[]{:S(2)}) collective-permute-start(bf16[4,128,512]{2,1,0:T(8,128)(2,1)S(1)} %copy-done.4), channel_id=1, source_target_pairs={{0,2},{1,3},{2,0},{3,1},{4,6},{5,7},{6,4},{7,5},{8,10},{9,11},{10,... | collective-permute-start | bytes 1572872 | tf_op jit(solution)/shard_map/ppermute | solution.py:48
  10.9 1.5 %regroup_back_body.1 = (bf16[4,64,256]{2,1,0:T(8,128)(2,1)S(1)}, bf16[4,64,256]{2,1,0:T(8,128)(2,1)S(1)}, bf16[4,64,256]{2,1,0:T(8,128)(2,1)S(1)}, bf16[4,64,256...) custom-call(bf16[32,512]{1,0:T(8,128)(2,1)S(1)} %pack_body.1.refs_0_, ...), custom_call_target="tpu_custom_call" | custom-call | tf_op jit(solution)/shard_map/regroup_back_body/pallas_call | solution.py:31
  12.4 4.6 %collective-permute-start.5 = (bf16[4,64,256]{2,1,0:T(8,128)(2,1)S(1)}, bf16[4,64,256]{2,1,0:T(8,128)(2,1)S(1)}, u32[]{:S(2)}, u32[]{:S(2)}) collective-permute-start(bf16[4,64,256]{2,1,0:T(8,128)(2,1)S(1)} %get-tuple-element.47), channel_id=1, source_target_pairs={{0,28},{4,24},{8,20},{12,16},{16,12},{20,8},{24,4},{28,0},{1,29},{... | collective-permute-start | bytes 393224 | tf_op jit(solution)/shard_map/ppermute | solution.py:48
  17.1 4.6 %collective-permute-done.5.refs_7_ = bf16[4,64,256]{2,1,0:T(8,128)(2,1)S(1)} collective-permute-done((bf16[4,64,256]{2,1,0:T(8,128)(2,1)S(1)}, bf16[4,64,256]{2,1,0:T(8,128)(2,1)S(1)}, u32[]{:S(2)}, u32[]{:S(2)}) %collective-permute-start.5) | collective-permute-done | bytes 131104 | tf_op jit(solution)/shard_map/ppermute | solution.py:48
  21.6 6.5 %collective-permute-done.6.refs_4_ = bf16[4,64,256]{2,1,0:T(8,128)(2,1)S(1)} collective-permute-done((bf16[4,64,256]{2,1,0:T(8,128)(2,1)S(1)}, bf16[4,64,256]{2,1,0:T(8,128)(2,1)S(1)}, u32[]{:S(2)}, u32[]{:S(2)}) %collective-permute-start.6) | collective-permute-done | bytes 131104 | tf_op jit(solution)/shard_map/ppermute | solution.py:48
  28.1 0.0 collective-permute-start.7
  28.1 0.1 collective-permute-start.8
  28.2 3.9 %collective-permute-start.14 = (bf16[4,64,256]{2,1,0:T(8,128)(2,1)S(1)}, bf16[4,64,256]{2,1,0:T(8,128)(2,1)S(1)}, u32[]{:S(2)}, u32[]{:S(2)}) collective-permute-start(bf16[4,64,256]{2,1,0:T(8,128)(2,1)S(1)} %get-tuple-element.64), channel_id=1, source_target_pairs={{0,20},{4,16},{8,28},{12,24},{16,4},{20,0},{24,12},{28,8},{1,21},{... | collective-permute-start | bytes 393224 | tf_op jit(solution)/shard_map/ppermute | solution.py:48
  32.2 2.5 %mix_body.1 = (bf16[4,64,256]{2,1,0:T(8,128)(2,1)S(1)}, bf16[4,64,256]{2,1,0:T(8,128)(2,1)S(1)}, bf16[4,64,256]{2,1,0:T(8,128)(2,1)S(1)}, bf16[4,64,256]{2,1,0:T...) custom-call(bf16[4,128,512]{2,1,0:T(8,128)(2,1)S(1)} %copy-done.4, ...), custom_call_target="tpu_custom_call" | custom-call | tf_op jit(solution)/shard_map/mix_body/pallas_call | solution.py:31
  34.7 0.1 collective-permute-start.10
  34.7 1.8 %collective-permute-done.8.refs_3_ = bf16[4,64,256]{2,1,0:T(8,128)(2,1)S(1)} collective-permute-done((bf16[4,64,256]{2,1,0:T(8,128)(2,1)S(1)}, bf16[4,64,256]{2,1,0:T(8,128)(2,1)S(1)}, u32[]{:S(2)}, u32[]{:S(2)}) %collective-permute-start.8) | collective-permute-done | bytes 131104 | tf_op jit(solution)/shard_map/ppermute | solution.py:48
  36.6 1.3 %collective-permute-start.9 = (bf16[4,64,256]{2,1,0:T(8,128)(2,1)S(1)}, bf16[4,64,256]{2,1,0:T(8,128)(2,1)S(1)}, u32[]{:S(2)}, u32[]{:S(2)}) collective-permute-start(bf16[4,64,256]{2,1,0:T(8,128)(2,1)S(1)} %get-tuple-element.55), channel_id=1, source_target_pairs={{0,4},{4,0},{8,12},{12,8},{16,20},{20,16},{24,28},{28,24},{1,5},{5... | collective-permute-start | bytes 393224 | tf_op jit(solution)/shard_map/ppermute | solution.py:48
  37.9 0.3 collective-permute-start.11
  38.2 2.0 %collective-permute-start.15 = (bf16[4,64,256]{2,1,0:T(8,128)(2,1)S(1)}, bf16[4,64,256]{2,1,0:T(8,128)(2,1)S(1)}, u32[]{:S(2)}, u32[]{:S(2)}) collective-permute-start(bf16[4,64,256]{2,1,0:T(8,128)(2,1)S(1)} %get-tuple-element.65), channel_id=1, source_target_pairs={{0,24},{4,28},{8,16},{12,20},{16,8},{20,12},{24,0},{28,4},{1,25},{... | collective-permute-start | bytes 393224 | tf_op jit(solution)/shard_map/ppermute | solution.py:48
  40.2 0.0 collective-permute-done.14.refs_5_
  40.2 0.5 collective-permute-start.12
  40.7 0.0 collective-permute-done.10.refs_2_
  40.7 2.1 %collective-permute-start.13 = (bf16[4,64,256]{2,1,0:T(8,128)(2,1)S(1)}, bf16[4,64,256]{2,1,0:T(8,128)(2,1)S(1)}, u32[]{:S(2)}, u32[]{:S(2)}) collective-permute-start(bf16[4,64,256]{2,1,0:T(8,128)(2,1)S(1)} %get-tuple-element.63), channel_id=1, source_target_pairs={{0,8},{4,12},{8,0},{12,4},{16,24},{20,28},{24,16},{28,20},{1,9},{5... | collective-permute-start | bytes 393224 | tf_op jit(solution)/shard_map/ppermute | solution.py:48
  42.8 1.2 %collective-permute-done.9.refs_1_ = bf16[4,64,256]{2,1,0:T(8,128)(2,1)S(1)} collective-permute-done((bf16[4,64,256]{2,1,0:T(8,128)(2,1)S(1)}, bf16[4,64,256]{2,1,0:T(8,128)(2,1)S(1)}, u32[]{:S(2)}, u32[]{:S(2)}) %collective-permute-start.9) | collective-permute-done | bytes 131104 | tf_op jit(solution)/shard_map/ppermute | solution.py:48
  43.9 4.5 %collective-permute-start.16 = (bf16[4,64,256]{2,1,0:T(8,128)(2,1)S(1)}, bf16[4,64,256]{2,1,0:T(8,128)(2,1)S(1)}, u32[]{:S(2)}, u32[]{:S(2)}) collective-permute-start(bf16[4,64,256]{2,1,0:T(8,128)(2,1)S(1)} %get-tuple-element.72), channel_id=1, source_target_pairs={{0,28},{4,24},{8,20},{12,16},{16,12},{20,8},{24,4},{28,0},{1,29},{... | collective-permute-start | bytes 393224 | tf_op jit(solution)/shard_map/ppermute | solution.py:48
  48.4 0.0 collective-permute-done.11.refs_3_
  48.4 2.0 %collective-permute-start.17 = (bf16[4,64,256]{2,1,0:T(8,128)(2,1)S(1)}, bf16[4,64,256]{2,1,0:T(8,128)(2,1)S(1)}, u32[]{:S(2)}, u32[]{:S(2)}) collective-permute-start(bf16[4,64,256]{2,1,0:T(8,128)(2,1)S(1)} %get-tuple-element.73), channel_id=1, source_target_pairs={{0,24},{4,28},{8,16},{12,20},{16,8},{20,12},{24,0},{28,4},{1,25},{... | collective-permute-start | bytes 393224 | tf_op jit(solution)/shard_map/ppermute | solution.py:48
  50.4 0.0 collective-permute-done.15.refs_6_
  50.4 0.0 collective-permute-done.12.refs_1_
  50.4 0.0 collective-permute-done.13.refs_2_
  50.4 3.0 %first_grad_body.1 = (bf16[4,128,512]{2,1,0:T(8,128)(2,1)S(1)}, bf16[4,128,512]{2,1,0:T(8,128)(2,1)S(1)}, bf16[4,128,512]{2,1,0:T(8,128)(2,1)S(1)}, bf16[4,128,5...) custom-call(bf16[4,64,256]{2,1,0:T(8,128)(2,1)S(1)} %get-tuple-element.59.refs_0_, ...), custom_call_target="tpu_custom_call" | custom-call | tf_op jit(solution)/shard_map/first_grad_body/pallas_call | solution.py:31
  53.4 0.0 collective-permute-done.16.refs_7_
  53.4 1.9 %collective-permute-done.17.refs_6_ = bf16[4,64,256]{2,1,0:T(8,128)(2,1)S(1)} collective-permute-done((bf16[4,64,256]{2,1,0:T(8,128)(2,1)S(1)}, bf16[4,64,256]{2,1,0:T(8,128)(2,1)S(1)}, u32[]{:S(2)}, u32[]{:S(2)}) %collective-permute-start.17) | collective-permute-done | bytes 131104 | tf_op jit(solution)/shard_map/ppermute | solution.py:48
  55.3 0.0 collective-permute-start.19
  55.3 0.5 collective-permute-start.18
  55.8 1.9 %mix_back_body.1.back_ref = bf16[2048,256]{1,0:T(8,128)(2,1)S(1)} custom-call(bf16[4,128,512]{2,1,0:T(8,128)(2,1)S(1)} %copy-done.4, bf16[4,128,512]{2,1,0:T(8,128)(2,1)S(1)} %collective-permute-done.3.refs_1_, bf16[4,128,512]{2,1,0:T(8,128)(2,1)S(1)} %collective-permute-done.4.refs_2_, bf16[4,128,512]{2,1,0:T(8,128)(2,1)S(1)} %collective-permute-done.7.refs_3_, ...), custom_call_target="tpu_custom_call" | custom-call | tf_op jit(solution)/shard_map/mix_back_body/pallas_call | solution.py:31
  57.7 0.0 collective-permute-done.19.got_b
  57.7 0.3 collective-permute-done.18.got_a
  58.0 0.2 pair_body.1
  58.2 0.7 collective-permute-start.20
  58.9 3.9 %collective-permute-start.21 = (bf16[4,64,256]{2,1,0:T(8,128)(2,1)S(1)}, bf16[4,64,256]{2,1,0:T(8,128)(2,1)S(1)}, u32[]{:S(2)}, u32[]{:S(2)}) collective-permute-start(bf16[4,64,256]{2,1,0:T(8,128)(2,1)S(1)} %get-tuple-element.80), channel_id=1, source_target_pairs={{0,16},{4,20},{8,24},{12,28},{16,0},{20,4},{24,8},{28,12},{1,17},{... | collective-permute-start | bytes 393224 | tf_op jit(solution)/shard_map/ppermute | solution.py:48
  62.8 2.1 %collective-permute-start.22 = (bf16[4,64,256]{2,1,0:T(8,128)(2,1)S(1)}, bf16[4,64,256]{2,1,0:T(8,128)(2,1)S(1)}, u32[]{:S(2)}, u32[]{:S(2)}) collective-permute-start(bf16[4,64,256]{2,1,0:T(8,128)(2,1)S(1)} %get-tuple-element.81), channel_id=1, source_target_pairs={{0,20},{4,16},{8,28},{12,24},{16,4},{20,0},{24,12},{28,8},{1,21},{... | collective-permute-start | bytes 393224 | tf_op jit(solution)/shard_map/ppermute | solution.py:48
  64.8 7.4 %collective-permute-done.20.got = bf16[4,128,512]{2,1,0:T(8,128)(2,1)S(1)} collective-permute-done((bf16[4,128,512]{2,1,0:T(8,128)(2,1)S(1)}, bf16[4,128,512]{2,1,0:T(8,128)(2,1)S(1)}, u32[]{:S(2)}, u32[]{:S(2)}) %collective-permute-start.20) | collective-permute-done | bytes 524320 | tf_op jit(solution)/shard_map/ppermute | solution.py:48
  72.2 0.9 %add_body.1 = bf16[4,128,512]{2,1,0:T(8,128)(2,1)} custom-call(f32[4,128,512]{2,1,0:T(8,128)S(1)} %get-tuple-element.77.own, bf16[4,128,512]{2,1,0:T(8,128)(2,1)S(1)} %collective-permute-done.20.got), custom_call_target="tpu_custom_call" | custom-call | tf_op jit(solution)/shard_map/add_body/pallas_call | solution.py:31
  73.1 0.0 collective-permute-done.21.refs_4_
  73.1 3.4 %collective-permute-done.22.refs_5_ = bf16[4,64,256]{2,1,0:T(8,128)(2,1)S(1)} collective-permute-done((bf16[4,64,256]{2,1,0:T(8,128)(2,1)S(1)}, bf16[4,64,256]{2,1,0:T(8,128)(2,1)S(1)}, u32[]{:S(2)}, u32[]{:S(2)}) %collective-permute-start.22) | collective-permute-done | bytes 131104 | tf_op jit(solution)/shard_map/ppermute | solution.py:48
  76.5 1.4 %second_grad_body.1 = (bf16[32,512]{1,0:T(8,128)(2,1)S(1)}, bf16[32,512]{1,0:T(8,128)(2,1)S(1)}, bf16[32,512]{1,0:T(8,128)(2,1)S(1)}, bf16[32,512]{1,0:T(8,128)(2,1)S(1)}, bf16[32,64,256]{2,1,0:T(8,128)(2,1)S(1)}) custom-call(bf16[4,64,256]{2,1,0:T(8,128)(2,1)S(1)} %get-tuple-element.79.refs_0_, bf16[4,64,256]{2,1,0:T(8,128)(2,1)S(1)} %collective-permute-done.9.refs_1_, ...), custom_call_target="tpu_custom_call" | custom-call | tf_op jit(solution)/shard_map/second_grad_body/pallas_call | solution.py:31
  77.9 0.1 collective-permute-start.23
  78.0 1.4 %collective-permute-start.24 = (bf16[32,512]{1,0:T(8,128)(2,1)S(1)}, bf16[32,512]{1,0:T(8,128)(2,1)S(1)}, u32[]{:S(2)}, u32[]{:S(2)}) collective-permute-start(bf16[32,512]{1,0:T(8,128)(2,1)S(1)} %get-tuple-element.87), channel_id=1, source_target_pairs={{0,2},{1,3},{2,0},{3,1},{4,6},{5,7},{6,4},{7,5},{8,10},{9,11},{10,... | collective-permute-start | bytes 98312 | tf_op jit(solution)/shard_map/ppermute | solution.py:48
  79.4 0.4 collective-permute-start.25
  79.8 2.7 %tokens_body.1 = bf16[2048,256]{1,0:T(8,128)(2,1)} custom-call(bf16[32,64,256]{2,1,0:T(8,128)(2,1)S(1)} %get-tuple-element.82.reg_ref, bf16[4,32,512]{2,1,0:T(8,128)(2,1)S(1)} %get-tuple-element.83.second_ref, bf16[2048,256]{1,0:T(8,128)(2,1)S(1)} %get-tuple-element.84.h_ref, s32[1,256]{1,0:T(1,128)S(1)} %bitcast.19, bf16[2048,256]{1,0:T(8,128)(2,1)S(1)} %mix_back_body.1.back_ref), custom_call_target="tpu_custom_call" | custom-call | tf_op jit(solution)/shard_map/tokens_body/pallas_call | solution.py:31
  82.5 0.0 collective-permute-done.23.refs_1_
  82.5 0.0 collective-permute-done.24.refs_2_
  82.6 0.2 collective-permute-done.25.refs_3_
  82.8 1.1 %unpack_body.1 = bf16[256,64]{1,0:T(8,128)(2,1)} custom-call(bf16[32,512]{1,0:T(8,128)(2,1)S(1)} %get-tuple-element.85.refs_0_, bf16[32,512]{1,0:T(8,128)(2,1)S(1)} %collective-permute-done.23.refs_1_, bf16[32,512]{1,0:T(8,128)(2,1)S(1)} %collective-permute-done.24.refs_2_, bf16[32,512]{1,0:T(8,128)(2,1)S(1)} %collective-permute-done.25.refs_3_), custom_call_target="tpu_custom_call" | custom-call | tf_op jit(solution)/shard_map/unpack_body/pallas_call | solution.py:31
  (15 shorter events, 0.0 us)
Async XLA Ops:
  0.6 0.8 %copy-start.5 = (bf16[64,8,32]{0,2,1:T(8,128)(2,1)S(1)}, bf16[64,8,32]{0,2,1:T(8,128)(2,1)}, u32[]{:S(2)}) copy-start(bf16[64,8,32]{0,2,1:T(8,128)(2,1)} %param.9) | copy-start | bytes 98308
  1.9 6.8 %collective-permute-start.2 = (bf16[32,512]{1,0:T(8,128)(2,1)S(1)}, bf16[32,512]{1,0:T(8,128)(2,1)S(1)}, u32[]{:S(2)}, u32[]{:S(2)}) collective-permute-start(bf16[32,512]{1,0:T(8,128)(2,1)S(1)} %pack_body.1.refs_0_), channel_id=1, source_target_pairs={{0,3},{1,2},{2,1},{3,0},{4,7},{5,6},{6,5},{7,4},{8,11},{9,10},{10,... | collective-permute-start | bytes 98312 | tf_op jit(solution)/shard_map/ppermute | solution.py:48
  4.3 4.3 %collective-permute-start.1 = (bf16[32,512]{1,0:T(8,128)(2,1)S(1)}, bf16[32,512]{1,0:T(8,128)(2,1)S(1)}, u32[]{:S(2)}, u32[]{:S(2)}) collective-permute-start(bf16[32,512]{1,0:T(8,128)(2,1)S(1)} %pack_body.1.refs_0_), channel_id=1, source_target_pairs={{0,2},{1,3},{2,0},{3,1},{4,6},{5,7},{6,4},{7,5},{8,10},{9,11},{10,... | collective-permute-start | bytes 98312 | tf_op jit(solution)/shard_map/ppermute | solution.py:48
  5.0 3.7 %collective-permute-start = (bf16[32,512]{1,0:T(8,128)(2,1)S(1)}, bf16[32,512]{1,0:T(8,128)(2,1)S(1)}, u32[]{:S(2)}, u32[]{:S(2)}) collective-permute-start(bf16[32,512]{1,0:T(8,128)(2,1)S(1)} %pack_body.1.refs_0_), channel_id=1, source_target_pairs={{0,1},{1,0},{2,3},{3,2},{4,5},{5,4},{6,7},{7,6},{8,9},{9,8},{10,11... | collective-permute-start | bytes 98312 | tf_op jit(solution)/shard_map/ppermute | solution.py:48
  5.0 0.7 copy-start.6
  5.7 1.2 %copy-start = (bf16[1,2048,256]{2,1,0:T(8,128)(2,1)S(1)}, bf16[1,2048,256]{2,1,0:T(8,128)(2,1)}, u32[]{:S(2)}) copy-start(bf16[1,2048,256]{2,1,0:T(8,128)(2,1)} %param.6) | copy-start | bytes 3145732
  6.9 1.2 %copy-start.2 = (bf16[1,2048,256]{2,1,0:T(8,128)(2,1)S(1)}, bf16[1,2048,256]{2,1,0:T(8,128)(2,1)}, u32[]{:S(2)}) copy-start(bf16[1,2048,256]{2,1,0:T(8,128)(2,1)} %param.7) | copy-start | bytes 3145732
  8.1 1.0 %copy-start.4 = (bf16[4,128,512]{2,1,0:T(8,128)(2,1)S(1)}, bf16[4,128,512]{2,1,0:T(8,128)(2,1)}, u32[]{:S(2)}) copy-start(bf16[4,128,512]{2,1,0:T(8,128)(2,1)} %refs_0_.3) | copy-start | bytes 1572868
  8.1 24.0 %copy-start.3 = (bf16[1,2048,256]{2,1,0:T(8,128)(2,1)S(1)}, bf16[1,2048,256]{2,1,0:T(8,128)(2,1)}, u32[]{:S(2)}) copy-start(bf16[1,2048,256]{2,1,0:T(8,128)(2,1)} %param.7) | copy-start | bytes 3145732
  8.6 23.5 %copy-start.1 = (bf16[1,2048,256]{2,1,0:T(8,128)(2,1)S(1)}, bf16[1,2048,256]{2,1,0:T(8,128)(2,1)}, u32[]{:S(2)}) copy-start(bf16[1,2048,256]{2,1,0:T(8,128)(2,1)} %param.6) | copy-start | bytes 3145732
  9.2 19.0 %collective-permute-start.4 = (bf16[4,128,512]{2,1,0:T(8,128)(2,1)S(1)}, bf16[4,128,512]{2,1,0:T(8,128)(2,1)S(1)}, u32[]{:S(2)}, u32[]{:S(2)}) collective-permute-start(bf16[4,128,512]{2,1,0:T(8,128)(2,1)S(1)} %copy-done.4), channel_id=1, source_target_pairs={{0,2},{1,3},{2,0},{3,1},{4,6},{5,7},{6,4},{7,5},{8,10},{9,11},{10,... | collective-permute-start | bytes 1572872 | tf_op jit(solution)/shard_map/ppermute | solution.py:48
  12.4 9.2 %collective-permute-start.5 = (bf16[4,64,256]{2,1,0:T(8,128)(2,1)S(1)}, bf16[4,64,256]{2,1,0:T(8,128)(2,1)S(1)}, u32[]{:S(2)}, u32[]{:S(2)}) collective-permute-start(bf16[4,64,256]{2,1,0:T(8,128)(2,1)S(1)} %get-tuple-element.47), channel_id=1, source_target_pairs={{0,28},{4,24},{8,20},{12,16},{16,12},{20,8},{24,4},{28,0},{1,29},{... | collective-permute-start | bytes 393224 | tf_op jit(solution)/shard_map/ppermute | solution.py:48
  17.1 11.1 %collective-permute-start.6 = (bf16[4,64,256]{2,1,0:T(8,128)(2,1)S(1)}, bf16[4,64,256]{2,1,0:T(8,128)(2,1)S(1)}, u32[]{:S(2)}, u32[]{:S(2)}) collective-permute-start(bf16[4,64,256]{2,1,0:T(8,128)(2,1)S(1)} %get-tuple-element.48), channel_id=1, source_target_pairs={{0,16},{4,20},{8,24},{12,28},{16,0},{20,4},{24,8},{28,12},{1,17},{... | collective-permute-start | bytes 393224 | tf_op jit(solution)/shard_map/ppermute | solution.py:48
  17.1 15.1 %collective-permute-start.3 = (bf16[4,128,512]{2,1,0:T(8,128)(2,1)S(1)}, bf16[4,128,512]{2,1,0:T(8,128)(2,1)S(1)}, u32[]{:S(2)}, u32[]{:S(2)}) collective-permute-start(bf16[4,128,512]{2,1,0:T(8,128)(2,1)S(1)} %copy-done.4), channel_id=1, source_target_pairs={{0,1},{1,0},{2,3},{3,2},{4,5},{5,4},{6,7},{7,6},{8,9},{9,8},{10,11... | collective-permute-start | bytes 1572872 | tf_op jit(solution)/shard_map/ppermute | solution.py:48
  28.1 4.0 %collective-permute-start.7 = (bf16[4,128,512]{2,1,0:T(8,128)(2,1)S(1)}, bf16[4,128,512]{2,1,0:T(8,128)(2,1)S(1)}, u32[]{:S(2)}, u32[]{:S(2)}) collective-permute-start(bf16[4,128,512]{2,1,0:T(8,128)(2,1)S(1)} %collective-permute-done.4.refs_2_), channel_id=1, source_target_pairs={{0,1},{1,0},{2,3},{3,2},{4,5},{5,4},{6,7},{7,6},{8,9},{9,8},{10,11... | collective-permute-start | bytes 1572872 | tf_op jit(solution)/shard_map/ppermute | solution.py:48
  28.1 4.0 %copy-start.7 = (s32[512]{0:T(512)S(1)}, s32[512]{0:T(512)}, u32[]{:S(2)}) copy-start(s32[512]{0:T(512)} %param.11) | copy-start | bytes 6148
  28.1 8.4 %collective-permute-start.8 = (bf16[4,64,256]{2,1,0:T(8,128)(2,1)S(1)}, bf16[4,64,256]{2,1,0:T(8,128)(2,1)S(1)}, u32[]{:S(2)}, u32[]{:S(2)}) collective-permute-start(bf16[4,64,256]{2,1,0:T(8,128)(2,1)S(1)} %get-tuple-element.54), channel_id=1, source_target_pairs={{0,12},{4,8},{8,4},{12,0},{16,28},{20,24},{24,20},{28,16},{1,13},{... | collective-permute-start | bytes 393224 | tf_op jit(solution)/shard_map/ppermute | solution.py:48
  28.2 12.0 %collective-permute-start.14 = (bf16[4,64,256]{2,1,0:T(8,128)(2,1)S(1)}, bf16[4,64,256]{2,1,0:T(8,128)(2,1)S(1)}, u32[]{:S(2)}, u32[]{:S(2)}) collective-permute-start(bf16[4,64,256]{2,1,0:T(8,128)(2,1)S(1)} %get-tuple-element.64), channel_id=1, source_target_pairs={{0,20},{4,16},{8,28},{12,24},{16,4},{20,0},{24,12},{28,8},{1,21},{... | collective-permute-start | bytes 393224 | tf_op jit(solution)/shard_map/ppermute | solution.py:48
  34.7 6.1 %collective-permute-start.10 = (bf16[4,64,256]{2,1,0:T(8,128)(2,1)S(1)}, bf16[4,64,256]{2,1,0:T(8,128)(2,1)S(1)}, u32[]{:S(2)}, u32[]{:S(2)}) collective-permute-start(bf16[4,64,256]{2,1,0:T(8,128)(2,1)S(1)} %get-tuple-element.57), channel_id=1, source_target_pairs={{0,8},{4,12},{8,0},{12,4},{16,24},{20,28},{24,16},{28,20},{1,9},{5... | collective-permute-start | bytes 393224 | tf_op jit(solution)/shard_map/ppermute | solution.py:48
  36.6 7.4 %collective-permute-start.9 = (bf16[4,64,256]{2,1,0:T(8,128)(2,1)S(1)}, bf16[4,64,256]{2,1,0:T(8,128)(2,1)S(1)}, u32[]{:S(2)}, u32[]{:S(2)}) collective-permute-start(bf16[4,64,256]{2,1,0:T(8,128)(2,1)S(1)} %get-tuple-element.55), channel_id=1, source_target_pairs={{0,4},{4,0},{8,12},{12,8},{16,20},{20,16},{24,28},{28,24},{1,5},{5... | collective-permute-start | bytes 393224 | tf_op jit(solution)/shard_map/ppermute | solution.py:48
  37.9 10.5 %collective-permute-start.11 = (bf16[4,64,256]{2,1,0:T(8,128)(2,1)S(1)}, bf16[4,64,256]{2,1,0:T(8,128)(2,1)S(1)}, u32[]{:S(2)}, u32[]{:S(2)}) collective-permute-start(bf16[4,64,256]{2,1,0:T(8,128)(2,1)S(1)} %get-tuple-element.58), channel_id=1, source_target_pairs={{0,12},{4,8},{8,4},{12,0},{16,28},{20,24},{24,20},{28,16},{1,13},{... | collective-permute-start | bytes 393224 | tf_op jit(solution)/shard_map/ppermute | solution.py:48
  38.2 12.2 %collective-permute-start.15 = (bf16[4,64,256]{2,1,0:T(8,128)(2,1)S(1)}, bf16[4,64,256]{2,1,0:T(8,128)(2,1)S(1)}, u32[]{:S(2)}, u32[]{:S(2)}) collective-permute-start(bf16[4,64,256]{2,1,0:T(8,128)(2,1)S(1)} %get-tuple-element.65), channel_id=1, source_target_pairs={{0,24},{4,28},{8,16},{12,20},{16,8},{20,12},{24,0},{28,4},{1,25},{... | collective-permute-start | bytes 393224 | tf_op jit(solution)/shard_map/ppermute | solution.py:48
  40.2 10.2 %collective-permute-start.12 = (bf16[4,64,256]{2,1,0:T(8,128)(2,1)S(1)}, bf16[4,64,256]{2,1,0:T(8,128)(2,1)S(1)}, u32[]{:S(2)}, u32[]{:S(2)}) collective-permute-start(bf16[4,64,256]{2,1,0:T(8,128)(2,1)S(1)} %get-tuple-element.61), channel_id=1, source_target_pairs={{0,4},{4,0},{8,12},{12,8},{16,20},{20,16},{24,28},{28,24},{1,5},{5... | collective-permute-start | bytes 393224 | tf_op jit(solution)/shard_map/ppermute | solution.py:48
  40.7 9.7 %collective-permute-start.13 = (bf16[4,64,256]{2,1,0:T(8,128)(2,1)S(1)}, bf16[4,64,256]{2,1,0:T(8,128)(2,1)S(1)}, u32[]{:S(2)}, u32[]{:S(2)}) collective-permute-start(bf16[4,64,256]{2,1,0:T(8,128)(2,1)S(1)} %get-tuple-element.63), channel_id=1, source_target_pairs={{0,8},{4,12},{8,0},{12,4},{16,24},{20,28},{24,16},{28,20},{1,9},{5... | collective-permute-start | bytes 393224 | tf_op jit(solution)/shard_map/ppermute | solution.py:48
  43.9 9.5 %collective-permute-start.16 = (bf16[4,64,256]{2,1,0:T(8,128)(2,1)S(1)}, bf16[4,64,256]{2,1,0:T(8,128)(2,1)S(1)}, u32[]{:S(2)}, u32[]{:S(2)}) collective-permute-start(bf16[4,64,256]{2,1,0:T(8,128)(2,1)S(1)} %get-tuple-element.72), channel_id=1, source_target_pairs={{0,28},{4,24},{8,20},{12,16},{16,12},{20,8},{24,4},{28,0},{1,29},{... | collective-permute-start | bytes 393224 | tf_op jit(solution)/shard_map/ppermute | solution.py:48
  48.4 6.9 %collective-permute-start.17 = (bf16[4,64,256]{2,1,0:T(8,128)(2,1)S(1)}, bf16[4,64,256]{2,1,0:T(8,128)(2,1)S(1)}, u32[]{:S(2)}, u32[]{:S(2)}) collective-permute-start(bf16[4,64,256]{2,1,0:T(8,128)(2,1)S(1)} %get-tuple-element.73), channel_id=1, source_target_pairs={{0,24},{4,28},{8,16},{12,20},{16,8},{20,12},{24,0},{28,4},{1,25},{... | collective-permute-start | bytes 393224 | tf_op jit(solution)/shard_map/ppermute | solution.py:48
  55.3 2.4 %collective-permute-start.19 = (bf16[4,128,512]{2,1,0:T(8,128)(2,1)S(1)}, bf16[4,128,512]{2,1,0:T(8,128)(2,1)S(1)}, u32[]{:S(2)}, u32[]{:S(2)}) collective-permute-start(bf16[4,128,512]{2,1,0:T(8,128)(2,1)S(1)} %get-tuple-element.76), channel_id=1, source_target_pairs={{0,1},{1,0},{2,3},{3,2},{4,5},{5,4},{6,7},{7,6},{8,9},{9,8},{10,11... | collective-permute-start | bytes 1572872 | tf_op jit(solution)/shard_map/ppermute | solution.py:48
  55.3 2.7 %collective-permute-start.18 = (bf16[4,128,512]{2,1,0:T(8,128)(2,1)S(1)}, bf16[4,128,512]{2,1,0:T(8,128)(2,1)S(1)}, u32[]{:S(2)}, u32[]{:S(2)}) collective-permute-start(bf16[4,128,512]{2,1,0:T(8,128)(2,1)S(1)} %get-tuple-element.74), channel_id=1, source_target_pairs={{0,1},{1,0},{2,3},{3,2},{4,5},{5,4},{6,7},{7,6},{8,9},{9,8},{10,11... | collective-permute-start | bytes 1572872 | tf_op jit(solution)/shard_map/ppermute | solution.py:48
  58.2 14.0 %collective-permute-start.20 = (bf16[4,128,512]{2,1,0:T(8,128)(2,1)S(1)}, bf16[4,128,512]{2,1,0:T(8,128)(2,1)S(1)}, u32[]{:S(2)}, u32[]{:S(2)}) collective-permute-start(bf16[4,128,512]{2,1,0:T(8,128)(2,1)S(1)} %get-tuple-element.78), channel_id=1, source_target_pairs={{0,2},{1,3},{2,0},{3,1},{4,6},{5,7},{6,4},{7,5},{8,10},{9,11},{10,... | collective-permute-start | bytes 1572872 | tf_op jit(solution)/shard_map/ppermute | solution.py:48
  58.9 14.2 %collective-permute-start.21 = (bf16[4,64,256]{2,1,0:T(8,128)(2,1)S(1)}, bf16[4,64,256]{2,1,0:T(8,128)(2,1)S(1)}, u32[]{:S(2)}, u32[]{:S(2)}) collective-permute-start(bf16[4,64,256]{2,1,0:T(8,128)(2,1)S(1)} %get-tuple-element.80), channel_id=1, source_target_pairs={{0,16},{4,20},{8,24},{12,28},{16,0},{20,4},{24,8},{28,12},{1,17},{... | collective-permute-start | bytes 393224 | tf_op jit(solution)/shard_map/ppermute | solution.py:48
  62.8 13.7 %collective-permute-start.22 = (bf16[4,64,256]{2,1,0:T(8,128)(2,1)S(1)}, bf16[4,64,256]{2,1,0:T(8,128)(2,1)S(1)}, u32[]{:S(2)}, u32[]{:S(2)}) collective-permute-start(bf16[4,64,256]{2,1,0:T(8,128)(2,1)S(1)} %get-tuple-element.81), channel_id=1, source_target_pairs={{0,20},{4,16},{8,28},{12,24},{16,4},{20,0},{24,12},{28,8},{1,21},{... | collective-permute-start | bytes 393224 | tf_op jit(solution)/shard_map/ppermute | solution.py:48
  77.9 4.6 %collective-permute-start.23 = (bf16[32,512]{1,0:T(8,128)(2,1)S(1)}, bf16[32,512]{1,0:T(8,128)(2,1)S(1)}, u32[]{:S(2)}, u32[]{:S(2)}) collective-permute-start(bf16[32,512]{1,0:T(8,128)(2,1)S(1)} %get-tuple-element.86), channel_id=1, source_target_pairs={{0,1},{1,0},{2,3},{3,2},{4,5},{5,4},{6,7},{7,6},{8,9},{9,8},{10,11... | collective-permute-start | bytes 98312 | tf_op jit(solution)/shard_map/ppermute | solution.py:48
  78.0 4.6 %collective-permute-start.24 = (bf16[32,512]{1,0:T(8,128)(2,1)S(1)}, bf16[32,512]{1,0:T(8,128)(2,1)S(1)}, u32[]{:S(2)}, u32[]{:S(2)}) collective-permute-start(bf16[32,512]{1,0:T(8,128)(2,1)S(1)} %get-tuple-element.87), channel_id=1, source_target_pairs={{0,2},{1,3},{2,0},{3,1},{4,6},{5,7},{6,4},{7,5},{8,10},{9,11},{10,... | collective-permute-start | bytes 98312 | tf_op jit(solution)/shard_map/ppermute | solution.py:48
  79.4 3.3 %collective-permute-start.25 = (bf16[32,512]{1,0:T(8,128)(2,1)S(1)}, bf16[32,512]{1,0:T(8,128)(2,1)S(1)}, u32[]{:S(2)}, u32[]{:S(2)}) collective-permute-start(bf16[32,512]{1,0:T(8,128)(2,1)S(1)} %get-tuple-element.88), channel_id=1, source_target_pairs={{0,3},{1,2},{2,1},{3,0},{4,7},{5,6},{6,5},{7,4},{8,11},{9,10},{10,... | collective-permute-start | bytes 98312 | tf_op jit(solution)/shard_map/ppermute | solution.py:48

commit v8 on v7

--- a/solution.py
+++ b/solution.py
@@ -10,7 +10,7 @@
 BF16 = jnp.bfloat16
 F32 = jnp.float32
 LANE_GROUP = 16
-CFG = {'a2a': [False, False], 'cost': {}, 'direct': False, 'rsdirect': False, 'f2early': False, 'order': [[7, 6, 5, 4, 3, 2, 1], [7, 6, 5, 4, 3, 2, 1]], 'deps': {'h3': ['h7'], 'h2': ['h7'], 'h1': ['h7'], 'fx': ['h7', 'h4'], 'F1': ['M', 'H1', 'H2', 'H3', 'fx'], 'near': ['H7', 'H6'], 'far': ['H7', 'H6'], 'pair': ['F2'], 'Z1': ['add'], 'H1': ['h3'], 'H2': ['M']}}
+CFG = {'a2a': [False, False], 'cost': {}, 'direct': False, 'rsdirect': True, 'f2early': False, 'order': [[7, 6, 5, 4, 3, 2, 1], [7, 6, 5, 4, 3, 2, 1]], 'deps': {'h3': ['h7'], 'h2': ['h7'], 'h1': ['h7'], 'fx': ['h7', 'h4'], 'F1': ['M', 'H1', 'H2', 'H3', 'fx'], 'pair': ['F2'], 'H1': ['h3'], 'H2': ['M'], 'f2': ['A2'], 'rs1': ['H7', 'H6'], 'rs2': ['H7', 'H6'], 'rs3': ['H7', 'H6'], 'F2': ['rs1']}}
 
 
 def iota(shape, dim):
@@ -301,10 +301,6 @@
         packed[d] = move(f"D{d}", mine, "batch", d, batch)
     (dz,) = call(gate_body, [of((rows_here, width))], [x, cot, src], limit=16 << 20)
     keep("gate", dz)
-    first_ready = after(first_factor, dz) if CFG['f2early'] else after(first_factor, dz, *[packed[d] for d in (1, 2, 3)])
-    across = move("f2", first_ready, "batch", 2, batch)
-    beside = move("f1", first_ready, "batch", 1, batch)
-    direct = move("f3", first_ready, "batch", 3, batch) if CFG['direct'] else None
     piece = of((blocks, j_here, width))
     *back, second = call(
         functools.partial(regroup_back_body, batch, seq, count),
@@ -316,6 +312,10 @@
         ],
     )
     keep("A2", back[0])
+    first_ready = after(first_factor, dz) if CFG['f2early'] else after(first_factor, dz, *[packed[d] for d in (1, 2, 3)])
+    across = move("f2", first_ready, "batch", 2, batch)
+    beside = move("f1", first_ready, "batch", 1, batch)
+    direct = move("f3", first_ready, "batch", 3, batch) if CFG['direct'] else None
     back_got = {0: back[0]}
     if CFG['a2a'][0]:
         back_got[0] = keep("h0", lax.all_to_all(dep("h0", back[0]), "seq", 0, 0, tiled=True))

time: 84.1 us -> 84.1 us (level); the launches traced: 83.8 us -> 83 us
  waiting for transfers between devices: 27.3 us -> 26.2 us
    ppermute x26, waiting for transfers between devices: 27.3 us -> 26.2 us  [swap(): return lax.ppermute(value, axis, [(p, p ^ step) for p in range(size)])]
    pallas_call x11 -> x10, Pallas kernels: 16 us -> 16 us  [call(): pl.pallas_call(body, name=name, out_shape=outs, in_specs=[pl.BlockSpec(me...]
  transfers between devices with their start and end apart: 26 -> 26, of which waited for: 9 -> 7; matrix products, arithmetic and copies ran while one was open for 0% -> 0% of each run, Pallas kernels for 15% -> 16%
where the time goes in v8:
time: 84.1 us; the launch traced here: 83 us
  starting transfers between devices  35.9 us (43%)
  waiting for transfers between devices  26.2 us (31%)
  Pallas kernels  16 us (19%)
  local copies, waits for them, and re-layouts  3.98 us (5%)
    ppermute x26, starting transfers between devices, swap(): return lax.ppermute(value, axis, [(p, p ^ step) for p in range(size)])  35.9 us
    ppermute x26, waiting for transfers between devices, swap(): return lax.ppermute(value, axis, [(p, p ^ step) for p in range(size)])  26.2 us
    pallas_call x10, Pallas kernels, call(): pl.pallas_call(body, name=name, out_shape=outs, in_specs=[pl.BlockSpec(me...  16 us
    unnamed x16, local copies, waits for them, and re-layouts  3.98 us
  transfers between devices with their start and end apart: 26, of which 7 were waited for; matrix products, arithmetic and copies ran while one was open for 0% of the time, Pallas kernels for 16%

profile of v8, /device:TPU:0, one launch (start us, length us, event | category | flops | bytes accessed | tf_op | source)
XLA Modules:
  0.0 83.0 jit_solution(18223491655940543474)
XLA Ops:
  0.6 0.8 %copy-done.5 = bf16[64,8,32]{0,2,1:T(8,128)(2,1)S(1)} copy-done((bf16[64,8,32]{0,2,1:T(8,128)(2,1)S(1)}, bf16[64,8,32]{0,2,1:T(8,128)(2,1)}, u32[]{:S(2)}) %copy-start.5) | copy-done | bytes 32792
  1.5 0.4 pack_body.1.refs_0_
  1.9 2.4 %collective-permute-start.2 = (bf16[32,512]{1,0:T(8,128)(2,1)S(1)}, bf16[32,512]{1,0:T(8,128)(2,1)S(1)}, u32[]{:S(2)}, u32[]{:S(2)}) collective-permute-start(bf16[32,512]{1,0:T(8,128)(2,1)S(1)} %pack_body.1.refs_0_), channel_id=1, source_target_pairs={{0,3},{1,2},{2,1},{3,0},{4,7},{5,6},{6,5},{7,4},{8,11},{9,10},{10,... | collective-permute-start | bytes 98312 | tf_op jit(solution)/shard_map/ppermute | solution.py:48
  4.3 0.6 collective-permute-start.1
  5.0 0.0 collective-permute-start
  5.0 0.7 copy-done.6
  5.7 1.2 %copy-done = bf16[1,2048,256]{2,1,0:T(8,128)(2,1)S(1)} copy-done((bf16[1,2048,256]{2,1,0:T(8,128)(2,1)S(1)}, bf16[1,2048,256]{2,1,0:T(8,128)(2,1)}, u32[]{:S(2)}) %copy-start) | copy-done | bytes 1048600
  6.9 1.2 %copy-done.2 = bf16[1,2048,256]{2,1,0:T(8,128)(2,1)S(1)} copy-done((bf16[1,2048,256]{2,1,0:T(8,128)(2,1)S(1)}, bf16[1,2048,256]{2,1,0:T(8,128)(2,1)}, u32[]{:S(2)}) %copy-start.2) | copy-done | bytes 1048600
  8.1 0.5 gate_body.1.refs_4_.refs_8_
  8.6 0.0 copy-start.1
  8.6 0.0 collective-permute-done.2.refs_3_
  8.7 0.0 collective-permute-done.1.refs_2_
  8.7 0.0 collective-permute-done.refs_1_
  8.7 1.5 %regroup_back_body.1 = (bf16[4,64,256]{2,1,0:T(8,128)(2,1)S(1)}, bf16[4,64,256]{2,1,0:T(8,128)(2,1)S(1)}, bf16[4,64,256]{2,1,0:T(8,128)(2,1)S(1)}, bf16[4,64,256...) custom-call(bf16[32,512]{1,0:T(8,128)(2,1)S(1)} %pack_body.1.refs_0_, ...), custom_call_target="tpu_custom_call" | custom-call | tf_op jit(solution)/shard_map/regroup_back_body/pallas_call | solution.py:31
  10.2 1.8 %collective-permute-start.4 = (bf16[4,128,512]{2,1,0:T(8,128)(2,1)S(1)}, bf16[4,128,512]{2,1,0:T(8,128)(2,1)S(1)}, u32[]{:S(2)}, u32[]{:S(2)}) collective-permute-start(bf16[4,128,512]{2,1,0:T(8,128)(2,1)S(1)} %copy-done.4), channel_id=1, source_target_pairs={{0,2},{1,3},{2,0},{3,1},{4,6},{5,7},{6,4},{7,5},{8,10},{9,11},{10,... | collective-permute-start | bytes 1572872 | tf_op jit(solution)/shard_map/ppermute | solution.py:48
  12.0 4.6 %collective-permute-start.5 = (bf16[4,64,256]{2,1,0:T(8,128)(2,1)S(1)}, bf16[4,64,256]{2,1,0:T(8,128)(2,1)S(1)}, u32[]{:S(2)}, u32[]{:S(2)}) collective-permute-start(bf16[4,64,256]{2,1,0:T(8,128)(2,1)S(1)} %get-tuple-element.48), channel_id=1, source_target_pairs={{0,28},{4,24},{8,20},{12,16},{16,12},{20,8},{24,4},{28,0},{1,29},{... | collective-permute-start | bytes 393224 | tf_op jit(solution)/shard_map/ppermute | solution.py:48
  16.6 0.0 collective-permute-start.6
  16.6 0.0 collective-permute-start.3
  16.6 4.6 %collective-permute-done.5.refs_7_ = bf16[4,64,256]{2,1,0:T(8,128)(2,1)S(1)} collective-permute-done((bf16[4,64,256]{2,1,0:T(8,128)(2,1)S(1)}, bf16[4,64,256]{2,1,0:T(8,128)(2,1)S(1)}, u32[]{:S(2)}, u32[]{:S(2)}) %collective-permute-start.5) | collective-permute-done | bytes 131104 | tf_op jit(solution)/shard_map/ppermute | solution.py:48
  21.1 6.5 %collective-permute-done.6.refs_4_ = bf16[4,64,256]{2,1,0:T(8,128)(2,1)S(1)} collective-permute-done((bf16[4,64,256]{2,1,0:T(8,128)(2,1)S(1)}, bf16[4,64,256]{2,1,0:T(8,128)(2,1)S(1)}, u32[]{:S(2)}, u32[]{:S(2)}) %collective-permute-start.6) | collective-permute-done | bytes 131104 | tf_op jit(solution)/shard_map/ppermute | solution.py:48
  27.6 0.0 collective-permute-done.4.refs_2_
  27.6 0.0 collective-permute-start.7
  27.7 0.1 collective-permute-start.8
  27.7 3.9 %collective-permute-start.14 = (bf16[4,64,256]{2,1,0:T(8,128)(2,1)S(1)}, bf16[4,64,256]{2,1,0:T(8,128)(2,1)S(1)}, u32[]{:S(2)}, u32[]{:S(2)}) collective-permute-start(bf16[4,64,256]{2,1,0:T(8,128)(2,1)S(1)} %get-tuple-element.64), channel_id=1, source_target_pairs={{0,20},{4,16},{8,28},{12,24},{16,4},{20,0},{24,12},{28,8},{1,21},{... | collective-permute-start | bytes 393224 | tf_op jit(solution)/shard_map/ppermute | solution.py:48
  31.7 0.0 collective-permute-done.3.refs_1_
  31.7 0.0 collective-permute-done.7.refs_3_
  31.7 2.5 %mix_body.1 = (bf16[4,64,256]{2,1,0:T(8,128)(2,1)S(1)}, bf16[4,64,256]{2,1,0:T(8,128)(2,1)S(1)}, bf16[4,64,256]{2,1,0:T(8,128)(2,1)S(1)}, bf16[4,64,256]{2,1,0:T...) custom-call(bf16[4,128,512]{2,1,0:T(8,128)(2,1)S(1)} %copy-done.4, ...), custom_call_target="tpu_custom_call" | custom-call | tf_op jit(solution)/shard_map/mix_body/pallas_call | solution.py:31
  34.2 0.1 collective-permute-start.10
  34.2 1.8 %collective-permute-done.8.refs_3_ = bf16[4,64,256]{2,1,0:T(8,128)(2,1)S(1)} collective-permute-done((bf16[4,64,256]{2,1,0:T(8,128)(2,1)S(1)}, bf16[4,64,256]{2,1,0:T(8,128)(2,1)S(1)}, u32[]{:S(2)}, u32[]{:S(2)}) %collective-permute-start.8) | collective-permute-done | bytes 131104 | tf_op jit(solution)/shard_map/ppermute | solution.py:48
  36.1 1.3 %collective-permute-start.9 = (bf16[4,64,256]{2,1,0:T(8,128)(2,1)S(1)}, bf16[4,64,256]{2,1,0:T(8,128)(2,1)S(1)}, u32[]{:S(2)}, u32[]{:S(2)}) collective-permute-start(bf16[4,64,256]{2,1,0:T(8,128)(2,1)S(1)} %get-tuple-element.55), channel_id=1, source_target_pairs={{0,4},{4,0},{8,12},{12,8},{16,20},{20,16},{24,28},{28,24},{1,5},{5... | collective-permute-start | bytes 393224 | tf_op jit(solution)/shard_map/ppermute | solution.py:48
  37.4 0.3 collective-permute-start.11
  37.7 2.0 %collective-permute-start.15 = (bf16[4,64,256]{2,1,0:T(8,128)(2,1)S(1)}, bf16[4,64,256]{2,1,0:T(8,128)(2,1)S(1)}, u32[]{:S(2)}, u32[]{:S(2)}) collective-permute-start(bf16[4,64,256]{2,1,0:T(8,128)(2,1)S(1)} %get-tuple-element.65), channel_id=1, source_target_pairs={{0,24},{4,28},{8,16},{12,20},{16,8},{20,12},{24,0},{28,4},{1,25},{... | collective-permute-start | bytes 393224 | tf_op jit(solution)/shard_map/ppermute | solution.py:48
  39.7 0.0 collective-permute-done.14.refs_5_
  39.7 0.5 collective-permute-start.12
  40.2 0.0 collective-permute-done.10.refs_2_
  40.2 2.1 %collective-permute-start.13 = (bf16[4,64,256]{2,1,0:T(8,128)(2,1)S(1)}, bf16[4,64,256]{2,1,0:T(8,128)(2,1)S(1)}, u32[]{:S(2)}, u32[]{:S(2)}) collective-permute-start(bf16[4,64,256]{2,1,0:T(8,128)(2,1)S(1)} %get-tuple-element.63), channel_id=1, source_target_pairs={{0,8},{4,12},{8,0},{12,4},{16,24},{20,28},{24,16},{28,20},{1,9},{5... | collective-permute-start | bytes 393224 | tf_op jit(solution)/shard_map/ppermute | solution.py:48
  42.3 1.2 %collective-permute-done.9.refs_1_ = bf16[4,64,256]{2,1,0:T(8,128)(2,1)S(1)} collective-permute-done((bf16[4,64,256]{2,1,0:T(8,128)(2,1)S(1)}, bf16[4,64,256]{2,1,0:T(8,128)(2,1)S(1)}, u32[]{:S(2)}, u32[]{:S(2)}) %collective-permute-start.9) | collective-permute-done | bytes 131104 | tf_op jit(solution)/shard_map/ppermute | solution.py:48
  43.5 4.5 %collective-permute-start.16 = (bf16[4,64,256]{2,1,0:T(8,128)(2,1)S(1)}, bf16[4,64,256]{2,1,0:T(8,128)(2,1)S(1)}, u32[]{:S(2)}, u32[]{:S(2)}) collective-permute-start(bf16[4,64,256]{2,1,0:T(8,128)(2,1)S(1)} %get-tuple-element.67), channel_id=1, source_target_pairs={{0,28},{4,24},{8,20},{12,16},{16,12},{20,8},{24,4},{28,0},{1,29},{... | collective-permute-start | bytes 393224 | tf_op jit(solution)/shard_map/ppermute | solution.py:48
  47.9 0.0 collective-permute-done.11.refs_3_
  47.9 2.0 %collective-permute-start.17 = (bf16[4,64,256]{2,1,0:T(8,128)(2,1)S(1)}, bf16[4,64,256]{2,1,0:T(8,128)(2,1)S(1)}, u32[]{:S(2)}, u32[]{:S(2)}) collective-permute-start(bf16[4,64,256]{2,1,0:T(8,128)(2,1)S(1)} %get-tuple-element.68), channel_id=1, source_target_pairs={{0,24},{4,28},{8,16},{12,20},{16,8},{20,12},{24,0},{28,4},{1,25},{... | collective-permute-start | bytes 393224 | tf_op jit(solution)/shard_map/ppermute | solution.py:48
  49.9 0.0 collective-permute-done.15.refs_6_
  49.9 0.0 collective-permute-done.12.refs_1_
  49.9 3.0 %first_grad_body.1 = (bf16[4,128,512]{2,1,0:T(8,128)(2,1)S(1)}, bf16[4,128,512]{2,1,0:T(8,128)(2,1)S(1)}, bf16[4,128,512]{2,1,0:T(8,128)(2,1)S(1)}, bf16[4,128,5...) custom-call(bf16[4,64,256]{2,1,0:T(8,128)(2,1)S(1)} %get-tuple-element.59.refs_0_, ...), custom_call_target="tpu_custom_call" | custom-call | tf_op jit(solution)/shard_map/first_grad_body/pallas_call | solution.py:31
  53.0 1.8 %collective-permute-done.17.refs_6_ = bf16[4,64,256]{2,1,0:T(8,128)(2,1)S(1)} collective-permute-done((bf16[4,64,256]{2,1,0:T(8,128)(2,1)S(1)}, bf16[4,64,256]{2,1,0:T(8,128)(2,1)S(1)}, u32[]{:S(2)}, u32[]{:S(2)}) %collective-permute-start.17) | collective-permute-done | bytes 131104 | tf_op jit(solution)/shard_map/ppermute | solution.py:48
  54.8 0.6 collective-permute-start.22
  55.4 1.2 %collective-permute-start.21 = (bf16[4,128,512]{2,1,0:T(8,128)(2,1)S(1)}, bf16[4,128,512]{2,1,0:T(8,128)(2,1)S(1)}, u32[]{:S(2)}, u32[]{:S(2)}) collective-permute-start(bf16[4,128,512]{2,1,0:T(8,128)(2,1)S(1)} %get-tuple-element.80), channel_id=1, source_target_pairs={{0,3},{1,2},{2,1},{3,0},{4,7},{5,6},{6,5},{7,4},{8,11},{9,10},{10,... | collective-permute-start | bytes 1572872 | tf_op jit(solution)/shard_map/ppermute | solution.py:48
  56.7 3.9 %collective-permute-start.19 = (bf16[4,64,256]{2,1,0:T(8,128)(2,1)S(1)}, bf16[4,64,256]{2,1,0:T(8,128)(2,1)S(1)}, u32[]{:S(2)}, u32[]{:S(2)}) collective-permute-start(bf16[4,64,256]{2,1,0:T(8,128)(2,1)S(1)} %get-tuple-element.73), channel_id=1, source_target_pairs={{0,16},{4,20},{8,24},{12,28},{16,0},{20,4},{24,8},{28,12},{1,17},{... | collective-permute-start | bytes 393224 | tf_op jit(solution)/shard_map/ppermute | solution.py:48
  60.5 2.1 %collective-permute-start.20 = (bf16[4,64,256]{2,1,0:T(8,128)(2,1)S(1)}, bf16[4,64,256]{2,1,0:T(8,128)(2,1)S(1)}, u32[]{:S(2)}, u32[]{:S(2)}) collective-permute-start(bf16[4,64,256]{2,1,0:T(8,128)(2,1)S(1)} %get-tuple-element.74), channel_id=1, source_target_pairs={{0,20},{4,16},{8,28},{12,24},{16,4},{20,0},{24,12},{28,8},{1,21},{... | collective-permute-start | bytes 393224 | tf_op jit(solution)/shard_map/ppermute | solution.py:48
  62.6 0.0 collective-permute-done.18.refs_2_
  62.6 1.9 %mix_back_body.1.back_ref = bf16[2048,256]{1,0:T(8,128)(2,1)S(1)} custom-call(bf16[4,128,512]{2,1,0:T(8,128)(2,1)S(1)} %copy-done.4, bf16[4,128,512]{2,1,0:T(8,128)(2,1)S(1)} %collective-permute-done.3.refs_1_, bf16[4,128,512]{2,1,0:T(8,128)(2,1)S(1)} %collective-permute-done.4.refs_2_, bf16[4,128,512]{2,1,0:T(8,128)(2,1)S(1)} %collective-permute-done.7.refs_3_, ...), custom_call_target="tpu_custom_call" | custom-call | tf_op jit(solution)/shard_map/mix_back_body/pallas_call | solution.py:31
  64.5 5.9 %collective-permute-done.19.refs_4_ = bf16[4,64,256]{2,1,0:T(8,128)(2,1)S(1)} collective-permute-done((bf16[4,64,256]{2,1,0:T(8,128)(2,1)S(1)}, bf16[4,64,256]{2,1,0:T(8,128)(2,1)S(1)}, u32[]{:S(2)}, u32[]{:S(2)}) %collective-permute-start.19) | collective-permute-done | bytes 131104 | tf_op jit(solution)/shard_map/ppermute | solution.py:48
  70.4 4.3 %collective-permute-done.20.refs_5_ = bf16[4,64,256]{2,1,0:T(8,128)(2,1)S(1)} collective-permute-done((bf16[4,64,256]{2,1,0:T(8,128)(2,1)S(1)}, bf16[4,64,256]{2,1,0:T(8,128)(2,1)S(1)}, u32[]{:S(2)}, u32[]{:S(2)}) %collective-permute-start.20) | collective-permute-done | bytes 131104 | tf_op jit(solution)/shard_map/ppermute | solution.py:48
  74.8 1.4 %second_grad_body.1 = (bf16[32,512]{1,0:T(8,128)(2,1)S(1)}, bf16[32,512]{1,0:T(8,128)(2,1)S(1)}, bf16[32,512]{1,0:T(8,128)(2,1)S(1)}, bf16[32,512]{1,0:T(8,128)(2,1)S(1)}, bf16[32,64,256]{2,1,0:T(8,128)(2,1)S(1)}) custom-call(bf16[4,64,256]{2,1,0:T(8,128)(2,1)S(1)} %get-tuple-element.72.refs_0_, bf16[4,64,256]{2,1,0:T(8,128)(2,1)S(1)} %collective-permute-done.9.refs_1_, ...), custom_call_target="tpu_custom_call" | custom-call | tf_op jit(solution)/shard_map/second_grad_body/pallas_call | solution.py:31
  76.2 0.1 collective-permute-start.23
  76.3 0.7 collective-permute-start.24
  77.0 1.1 %collective-permute-start.25 = (bf16[32,512]{1,0:T(8,128)(2,1)S(1)}, bf16[32,512]{1,0:T(8,128)(2,1)S(1)}, u32[]{:S(2)}, u32[]{:S(2)}) collective-permute-start(bf16[32,512]{1,0:T(8,128)(2,1)S(1)} %get-tuple-element.86), channel_id=1, source_target_pairs={{0,3},{1,2},{2,1},{3,0},{4,7},{5,6},{6,5},{7,4},{8,11},{9,10},{10,... | collective-permute-start | bytes 98312 | tf_op jit(solution)/shard_map/ppermute | solution.py:48
  78.1 2.7 %tokens_body.1 = bf16[2048,256]{1,0:T(8,128)(2,1)} custom-call(bf16[32,64,256]{2,1,0:T(8,128)(2,1)S(1)} %get-tuple-element.75.reg_ref, bf16[4,32,512]{2,1,0:T(8,128)(2,1)S(1)} %get-tuple-element.76.second_ref, bf16[2048,256]{1,0:T(8,128)(2,1)S(1)} %get-tuple-element.77.h_ref, s32[1,256]{1,0:T(1,128)S(1)} %bitcast.19, bf16[2048,256]{1,0:T(8,128)(2,1)S(1)} %mix_back_body.1.back_ref), custom_call_target="tpu_custom_call" | custom-call | tf_op jit(solution)/shard_map/tokens_body/pallas_call | solution.py:31
  80.8 0.0 collective-permute-done.22.refs_1_
  80.8 0.0 collective-permute-done.21.refs_0_
  80.8 1.1 %sum_body.1 = bf16[4,128,512]{2,1,0:T(8,128)(2,1)} custom-call(bf16[4,128,512]{2,1,0:T(8,128)(2,1)S(1)} %get-tuple-element.78.own, bf16[4,128,512]{2,1,0:T(8,128)(2,1)S(1)} %collective-permute-done.21.refs_0_, bf16[4,128,512]{2,1,0:T(8,128)(2,1)S(1)} %collective-permute-done.22.refs_1_, bf16[4,128,512]{2,1,0:T(8,128)(2,1)S(1)} %collective-permute-done.18.refs_2_), custom_call_target="tpu_custom_call" | custom-call | tf_op jit(solution)/shard_map/sum_body/pallas_call | solution.py:31
  81.9 0.0 collective-permute-done.23.refs_1_
  81.9 0.0 collective-permute-done.24.refs_2_
  81.9 0.0 collective-permute-done.25.refs_3_
  81.9 1.1 %unpack_body.1 = bf16[256,64]{1,0:T(8,128)(2,1)} custom-call(bf16[32,512]{1,0:T(8,128)(2,1)S(1)} %get-tuple-element.83.refs_0_, bf16[32,512]{1,0:T(8,128)(2,1)S(1)} %collective-permute-done.23.refs_1_, bf16[32,512]{1,0:T(8,128)(2,1)S(1)} %collective-permute-done.24.refs_2_, bf16[32,512]{1,0:T(8,128)(2,1)S(1)} %collective-permute-done.25.refs_3_), custom_call_target="tpu_custom_call" | custom-call | tf_op jit(solution)/shard_map/unpack_body/pallas_call | solution.py:31
  (14 shorter events, 0.0 us)
Async XLA Ops:
  0.6 0.8 %copy-start.5 = (bf16[64,8,32]{0,2,1:T(8,128)(2,1)S(1)}, bf16[64,8,32]{0,2,1:T(8,128)(2,1)}, u32[]{:S(2)}) copy-start(bf16[64,8,32]{0,2,1:T(8,128)(2,1)} %param.9) | copy-start | bytes 98308
  1.9 6.8 %collective-permute-start.2 = (bf16[32,512]{1,0:T(8,128)(2,1)S(1)}, bf16[32,512]{1,0:T(8,128)(2,1)S(1)}, u32[]{:S(2)}, u32[]{:S(2)}) collective-permute-start(bf16[32,512]{1,0:T(8,128)(2,1)S(1)} %pack_body.1.refs_0_), channel_id=1, source_target_pairs={{0,3},{1,2},{2,1},{3,0},{4,7},{5,6},{6,5},{7,4},{8,11},{9,10},{10,... | collective-permute-start | bytes 98312 | tf_op jit(solution)/shard_map/ppermute | solution.py:48
  4.3 4.3 %collective-permute-start.1 = (bf16[32,512]{1,0:T(8,128)(2,1)S(1)}, bf16[32,512]{1,0:T(8,128)(2,1)S(1)}, u32[]{:S(2)}, u32[]{:S(2)}) collective-permute-start(bf16[32,512]{1,0:T(8,128)(2,1)S(1)} %pack_body.1.refs_0_), channel_id=1, source_target_pairs={{0,2},{1,3},{2,0},{3,1},{4,6},{5,7},{6,4},{7,5},{8,10},{9,11},{10,... | collective-permute-start | bytes 98312 | tf_op jit(solution)/shard_map/ppermute | solution.py:48
  5.0 3.7 %collective-permute-start = (bf16[32,512]{1,0:T(8,128)(2,1)S(1)}, bf16[32,512]{1,0:T(8,128)(2,1)S(1)}, u32[]{:S(2)}, u32[]{:S(2)}) collective-permute-start(bf16[32,512]{1,0:T(8,128)(2,1)S(1)} %pack_body.1.refs_0_), channel_id=1, source_target_pairs={{0,1},{1,0},{2,3},{3,2},{4,5},{5,4},{6,7},{7,6},{8,9},{9,8},{10,11... | collective-permute-start | bytes 98312 | tf_op jit(solution)/shard_map/ppermute | solution.py:48
  5.0 0.7 copy-start.6
  5.7 1.2 %copy-start = (bf16[1,2048,256]{2,1,0:T(8,128)(2,1)S(1)}, bf16[1,2048,256]{2,1,0:T(8,128)(2,1)}, u32[]{:S(2)}) copy-start(bf16[1,2048,256]{2,1,0:T(8,128)(2,1)} %param.6) | copy-start | bytes 3145732
  6.9 1.2 %copy-start.2 = (bf16[1,2048,256]{2,1,0:T(8,128)(2,1)S(1)}, bf16[1,2048,256]{2,1,0:T(8,128)(2,1)}, u32[]{:S(2)}) copy-start(bf16[1,2048,256]{2,1,0:T(8,128)(2,1)} %param.7) | copy-start | bytes 3145732
  8.1 2.1 %copy-start.4 = (bf16[4,128,512]{2,1,0:T(8,128)(2,1)S(1)}, bf16[4,128,512]{2,1,0:T(8,128)(2,1)}, u32[]{:S(2)}) copy-start(bf16[4,128,512]{2,1,0:T(8,128)(2,1)} %refs_0_.2) | copy-start | bytes 1572868
  8.1 23.5 %copy-start.3 = (bf16[1,2048,256]{2,1,0:T(8,128)(2,1)S(1)}, bf16[1,2048,256]{2,1,0:T(8,128)(2,1)}, u32[]{:S(2)}) copy-start(bf16[1,2048,256]{2,1,0:T(8,128)(2,1)} %param.7) | copy-start | bytes 3145732
  8.6 23.0 %copy-start.1 = (bf16[1,2048,256]{2,1,0:T(8,128)(2,1)S(1)}, bf16[1,2048,256]{2,1,0:T(8,128)(2,1)}, u32[]{:S(2)}) copy-start(bf16[1,2048,256]{2,1,0:T(8,128)(2,1)} %param.6) | copy-start | bytes 3145732
  10.2 17.4 %collective-permute-start.4 = (bf16[4,128,512]{2,1,0:T(8,128)(2,1)S(1)}, bf16[4,128,512]{2,1,0:T(8,128)(2,1)S(1)}, u32[]{:S(2)}, u32[]{:S(2)}) collective-permute-start(bf16[4,128,512]{2,1,0:T(8,128)(2,1)S(1)} %copy-done.4), channel_id=1, source_target_pairs={{0,2},{1,3},{2,0},{3,1},{4,6},{5,7},{6,4},{7,5},{8,10},{9,11},{10,... | collective-permute-start | bytes 1572872 | tf_op jit(solution)/shard_map/ppermute | solution.py:48
  12.0 9.1 %collective-permute-start.5 = (bf16[4,64,256]{2,1,0:T(8,128)(2,1)S(1)}, bf16[4,64,256]{2,1,0:T(8,128)(2,1)S(1)}, u32[]{:S(2)}, u32[]{:S(2)}) collective-permute-start(bf16[4,64,256]{2,1,0:T(8,128)(2,1)S(1)} %get-tuple-element.48), channel_id=1, source_target_pairs={{0,28},{4,24},{8,20},{12,16},{16,12},{20,8},{24,4},{28,0},{1,29},{... | collective-permute-start | bytes 393224 | tf_op jit(solution)/shard_map/ppermute | solution.py:48
  16.6 11.1 %collective-permute-start.6 = (bf16[4,64,256]{2,1,0:T(8,128)(2,1)S(1)}, bf16[4,64,256]{2,1,0:T(8,128)(2,1)S(1)}, u32[]{:S(2)}, u32[]{:S(2)}) collective-permute-start(bf16[4,64,256]{2,1,0:T(8,128)(2,1)S(1)} %get-tuple-element.49), channel_id=1, source_target_pairs={{0,16},{4,20},{8,24},{12,28},{16,0},{20,4},{24,8},{28,12},{1,17},{... | collective-permute-start | bytes 393224 | tf_op jit(solution)/shard_map/ppermute | solution.py:48
  16.6 15.1 %collective-permute-start.3 = (bf16[4,128,512]{2,1,0:T(8,128)(2,1)S(1)}, bf16[4,128,512]{2,1,0:T(8,128)(2,1)S(1)}, u32[]{:S(2)}, u32[]{:S(2)}) collective-permute-start(bf16[4,128,512]{2,1,0:T(8,128)(2,1)S(1)} %copy-done.4), channel_id=1, source_target_pairs={{0,1},{1,0},{2,3},{3,2},{4,5},{5,4},{6,7},{7,6},{8,9},{9,8},{10,11... | collective-permute-start | bytes 1572872 | tf_op jit(solution)/shard_map/ppermute | solution.py:48
  27.6 4.0 %collective-permute-start.7 = (bf16[4,128,512]{2,1,0:T(8,128)(2,1)S(1)}, bf16[4,128,512]{2,1,0:T(8,128)(2,1)S(1)}, u32[]{:S(2)}, u32[]{:S(2)}) collective-permute-start(bf16[4,128,512]{2,1,0:T(8,128)(2,1)S(1)} %collective-permute-done.4.refs_2_), channel_id=1, source_target_pairs={{0,1},{1,0},{2,3},{3,2},{4,5},{5,4},{6,7},{7,6},{8,9},{9,8},{10,11... | collective-permute-start | bytes 1572872 | tf_op jit(solution)/shard_map/ppermute | solution.py:48
  27.6 4.0 %copy-start.7 = (s32[512]{0:T(512)S(1)}, s32[512]{0:T(512)}, u32[]{:S(2)}) copy-start(s32[512]{0:T(512)} %param.11) | copy-start | bytes 6148
  27.7 8.4 %collective-permute-start.8 = (bf16[4,64,256]{2,1,0:T(8,128)(2,1)S(1)}, bf16[4,64,256]{2,1,0:T(8,128)(2,1)S(1)}, u32[]{:S(2)}, u32[]{:S(2)}) collective-permute-start(bf16[4,64,256]{2,1,0:T(8,128)(2,1)S(1)} %get-tuple-element.54), channel_id=1, source_target_pairs={{0,12},{4,8},{8,4},{12,0},{16,28},{20,24},{24,20},{28,16},{1,13},{... | collective-permute-start | bytes 393224 | tf_op jit(solution)/shard_map/ppermute | solution.py:48
  27.7 12.0 %collective-permute-start.14 = (bf16[4,64,256]{2,1,0:T(8,128)(2,1)S(1)}, bf16[4,64,256]{2,1,0:T(8,128)(2,1)S(1)}, u32[]{:S(2)}, u32[]{:S(2)}) collective-permute-start(bf16[4,64,256]{2,1,0:T(8,128)(2,1)S(1)} %get-tuple-element.64), channel_id=1, source_target_pairs={{0,20},{4,16},{8,28},{12,24},{16,4},{20,0},{24,12},{28,8},{1,21},{... | collective-permute-start | bytes 393224 | tf_op jit(solution)/shard_map/ppermute | solution.py:48
  34.2 6.0 %collective-permute-start.10 = (bf16[4,64,256]{2,1,0:T(8,128)(2,1)S(1)}, bf16[4,64,256]{2,1,0:T(8,128)(2,1)S(1)}, u32[]{:S(2)}, u32[]{:S(2)}) collective-permute-start(bf16[4,64,256]{2,1,0:T(8,128)(2,1)S(1)} %get-tuple-element.57), channel_id=1, source_target_pairs={{0,8},{4,12},{8,0},{12,4},{16,24},{20,28},{24,16},{28,20},{1,9},{5... | collective-permute-start | bytes 393224 | tf_op jit(solution)/shard_map/ppermute | solution.py:48
  36.1 7.4 %collective-permute-start.9 = (bf16[4,64,256]{2,1,0:T(8,128)(2,1)S(1)}, bf16[4,64,256]{2,1,0:T(8,128)(2,1)S(1)}, u32[]{:S(2)}, u32[]{:S(2)}) collective-permute-start(bf16[4,64,256]{2,1,0:T(8,128)(2,1)S(1)} %get-tuple-element.55), channel_id=1, source_target_pairs={{0,4},{4,0},{8,12},{12,8},{16,20},{20,16},{24,28},{28,24},{1,5},{5... | collective-permute-start | bytes 393224 | tf_op jit(solution)/shard_map/ppermute | solution.py:48
  37.4 10.5 %collective-permute-start.11 = (bf16[4,64,256]{2,1,0:T(8,128)(2,1)S(1)}, bf16[4,64,256]{2,1,0:T(8,128)(2,1)S(1)}, u32[]{:S(2)}, u32[]{:S(2)}) collective-permute-start(bf16[4,64,256]{2,1,0:T(8,128)(2,1)S(1)} %get-tuple-element.58), channel_id=1, source_target_pairs={{0,12},{4,8},{8,4},{12,0},{16,28},{20,24},{24,20},{28,16},{1,13},{... | collective-permute-start | bytes 393224 | tf_op jit(solution)/shard_map/ppermute | solution.py:48
  37.7 12.2 %collective-permute-start.15 = (bf16[4,64,256]{2,1,0:T(8,128)(2,1)S(1)}, bf16[4,64,256]{2,1,0:T(8,128)(2,1)S(1)}, u32[]{:S(2)}, u32[]{:S(2)}) collective-permute-start(bf16[4,64,256]{2,1,0:T(8,128)(2,1)S(1)} %get-tuple-element.65), channel_id=1, source_target_pairs={{0,24},{4,28},{8,16},{12,20},{16,8},{20,12},{24,0},{28,4},{1,25},{... | collective-permute-start | bytes 393224 | tf_op jit(solution)/shard_map/ppermute | solution.py:48
  39.7 10.2 %collective-permute-start.12 = (bf16[4,64,256]{2,1,0:T(8,128)(2,1)S(1)}, bf16[4,64,256]{2,1,0:T(8,128)(2,1)S(1)}, u32[]{:S(2)}, u32[]{:S(2)}) collective-permute-start(bf16[4,64,256]{2,1,0:T(8,128)(2,1)S(1)} %get-tuple-element.61), channel_id=1, source_target_pairs={{0,4},{4,0},{8,12},{12,8},{16,20},{20,16},{24,28},{28,24},{1,5},{5... | collective-permute-start | bytes 393224 | tf_op jit(solution)/shard_map/ppermute | solution.py:48
  40.2 9.7 %collective-permute-start.13 = (bf16[4,64,256]{2,1,0:T(8,128)(2,1)S(1)}, bf16[4,64,256]{2,1,0:T(8,128)(2,1)S(1)}, u32[]{:S(2)}, u32[]{:S(2)}) collective-permute-start(bf16[4,64,256]{2,1,0:T(8,128)(2,1)S(1)} %get-tuple-element.63), channel_id=1, source_target_pairs={{0,8},{4,12},{8,0},{12,4},{16,24},{20,28},{24,16},{28,20},{1,9},{5... | collective-permute-start | bytes 393224 | tf_op jit(solution)/shard_map/ppermute | solution.py:48
  43.5 9.5 %collective-permute-start.16 = (bf16[4,64,256]{2,1,0:T(8,128)(2,1)S(1)}, bf16[4,64,256]{2,1,0:T(8,128)(2,1)S(1)}, u32[]{:S(2)}, u32[]{:S(2)}) collective-permute-start(bf16[4,64,256]{2,1,0:T(8,128)(2,1)S(1)} %get-tuple-element.67), channel_id=1, source_target_pairs={{0,28},{4,24},{8,20},{12,16},{16,12},{20,8},{24,4},{28,0},{1,29},{... | collective-permute-start | bytes 393224 | tf_op jit(solution)/shard_map/ppermute | solution.py:48
  47.9 6.9 %collective-permute-start.17 = (bf16[4,64,256]{2,1,0:T(8,128)(2,1)S(1)}, bf16[4,64,256]{2,1,0:T(8,128)(2,1)S(1)}, u32[]{:S(2)}, u32[]{:S(2)}) collective-permute-start(bf16[4,64,256]{2,1,0:T(8,128)(2,1)S(1)} %get-tuple-element.68), channel_id=1, source_target_pairs={{0,24},{4,28},{8,16},{12,20},{16,8},{20,12},{24,0},{28,4},{1,25},{... | collective-permute-start | bytes 393224 | tf_op jit(solution)/shard_map/ppermute | solution.py:48
  54.8 7.8 %collective-permute-start.18 = (bf16[4,128,512]{2,1,0:T(8,128)(2,1)S(1)}, bf16[4,128,512]{2,1,0:T(8,128)(2,1)S(1)}, u32[]{:S(2)}, u32[]{:S(2)}) collective-permute-start(bf16[4,128,512]{2,1,0:T(8,128)(2,1)S(1)} %get-tuple-element.69), channel_id=1, source_target_pairs={{0,1},{1,0},{2,3},{3,2},{4,5},{5,4},{6,7},{7,6},{8,9},{9,8},{10,11... | collective-permute-start | bytes 1572872 | tf_op jit(solution)/shard_map/ppermute | solution.py:48
  54.8 26.0 %collective-permute-start.22 = (bf16[4,128,512]{2,1,0:T(8,128)(2,1)S(1)}, bf16[4,128,512]{2,1,0:T(8,128)(2,1)S(1)}, u32[]{:S(2)}, u32[]{:S(2)}) collective-permute-start(bf16[4,128,512]{2,1,0:T(8,128)(2,1)S(1)} %get-tuple-element.82), channel_id=1, source_target_pairs={{0,2},{1,3},{2,0},{3,1},{4,6},{5,7},{6,4},{7,5},{8,10},{9,11},{10,... | collective-permute-start | bytes 1572872 | tf_op jit(solution)/shard_map/ppermute | solution.py:48
  55.4 25.4 %collective-permute-start.21 = (bf16[4,128,512]{2,1,0:T(8,128)(2,1)S(1)}, bf16[4,128,512]{2,1,0:T(8,128)(2,1)S(1)}, u32[]{:S(2)}, u32[]{:S(2)}) collective-permute-start(bf16[4,128,512]{2,1,0:T(8,128)(2,1)S(1)} %get-tuple-element.80), channel_id=1, source_target_pairs={{0,3},{1,2},{2,1},{3,0},{4,7},{5,6},{6,5},{7,4},{8,11},{9,10},{10,... | collective-permute-start | bytes 1572872 | tf_op jit(solution)/shard_map/ppermute | solution.py:48
  56.7 13.8 %collective-permute-start.19 = (bf16[4,64,256]{2,1,0:T(8,128)(2,1)S(1)}, bf16[4,64,256]{2,1,0:T(8,128)(2,1)S(1)}, u32[]{:S(2)}, u32[]{:S(2)}) collective-permute-start(bf16[4,64,256]{2,1,0:T(8,128)(2,1)S(1)} %get-tuple-element.73), channel_id=1, source_target_pairs={{0,16},{4,20},{8,24},{12,28},{16,0},{20,4},{24,8},{28,12},{1,17},{... | collective-permute-start | bytes 393224 | tf_op jit(solution)/shard_map/ppermute | solution.py:48
  60.5 14.2 %collective-permute-start.20 = (bf16[4,64,256]{2,1,0:T(8,128)(2,1)S(1)}, bf16[4,64,256]{2,1,0:T(8,128)(2,1)S(1)}, u32[]{:S(2)}, u32[]{:S(2)}) collective-permute-start(bf16[4,64,256]{2,1,0:T(8,128)(2,1)S(1)} %get-tuple-element.74), channel_id=1, source_target_pairs={{0,20},{4,16},{8,28},{12,24},{16,4},{20,0},{24,12},{28,8},{1,21},{... | collective-permute-start | bytes 393224 | tf_op jit(solution)/shard_map/ppermute | solution.py:48
  76.2 5.7 %collective-permute-start.23 = (bf16[32,512]{1,0:T(8,128)(2,1)S(1)}, bf16[32,512]{1,0:T(8,128)(2,1)S(1)}, u32[]{:S(2)}, u32[]{:S(2)}) collective-permute-start(bf16[32,512]{1,0:T(8,128)(2,1)S(1)} %get-tuple-element.84), channel_id=1, source_target_pairs={{0,1},{1,0},{2,3},{3,2},{4,5},{5,4},{6,7},{7,6},{8,9},{9,8},{10,11... | collective-permute-start | bytes 98312 | tf_op jit(solution)/shard_map/ppermute | solution.py:48
  76.3 5.6 %collective-permute-start.24 = (bf16[32,512]{1,0:T(8,128)(2,1)S(1)}, bf16[32,512]{1,0:T(8,128)(2,1)S(1)}, u32[]{:S(2)}, u32[]{:S(2)}) collective-permute-start(bf16[32,512]{1,0:T(8,128)(2,1)S(1)} %get-tuple-element.85), channel_id=1, source_target_pairs={{0,2},{1,3},{2,0},{3,1},{4,6},{5,7},{6,4},{7,5},{8,10},{9,11},{10,... | collective-permute-start | bytes 98312 | tf_op jit(solution)/shard_map/ppermute | solution.py:48
  77.0 4.9 %collective-permute-start.25 = (bf16[32,512]{1,0:T(8,128)(2,1)S(1)}, bf16[32,512]{1,0:T(8,128)(2,1)S(1)}, u32[]{:S(2)}, u32[]{:S(2)}) collective-permute-start(bf16[32,512]{1,0:T(8,128)(2,1)S(1)} %get-tuple-element.86), channel_id=1, source_target_pairs={{0,3},{1,2},{2,1},{3,0},{4,7},{5,6},{6,5},{7,4},{8,11},{9,10},{10,... | collective-permute-start | bytes 98312 | tf_op jit(solution)/shard_map/ppermute | solution.py:48

commit v9 on v8

--- a/solution.py
+++ b/solution.py
@@ -10,7 +10,7 @@
 BF16 = jnp.bfloat16
 F32 = jnp.float32
 LANE_GROUP = 16
-CFG = {'a2a': [False, False], 'cost': {}, 'direct': False, 'rsdirect': True, 'f2early': False, 'order': [[7, 6, 5, 4, 3, 2, 1], [7, 6, 5, 4, 3, 2, 1]], 'deps': {'h3': ['h7'], 'h2': ['h7'], 'h1': ['h7'], 'fx': ['h7', 'h4'], 'F1': ['M', 'H1', 'H2', 'H3', 'fx'], 'pair': ['F2'], 'H1': ['h3'], 'H2': ['M'], 'f2': ['A2'], 'rs1': ['H7', 'H6'], 'rs2': ['H7', 'H6'], 'rs3': ['H7', 'H6'], 'F2': ['rs1']}}
+CFG = {'a2a': [True, True], 'limit': 62914560, 'cost': {}, 'direct': False, 'rsdirect': False, 'f2early': False, 'order': [[7, 6, 5, 4, 3, 2, 1], [7, 6, 5, 4, 3, 2, 1]], 'deps': {'fx': ['A2'], 'F1': ['M'], 'pair': ['F2'], 'Z1': ['add']}}
 
 
 def iota(shape, dim):
@@ -25,7 +25,7 @@
     return lax.dot_general(a, b, (((da,), (db,)), ((), ())), preferred_element_type=F32)
 
 
-def call(body, outs, ins, scratch=(), spaces={}, limit=40 << 20, weight=0, out_space=pltpu.VMEM):
+def call(body, outs, ins, scratch=(), spaces={}, limit=40 << 20, weight=0, far_outs=()):
     name = getattr(body, "func", body).__name__
     weight = CFG['cost'].get(name, 0)
     return pl.pallas_call(
@@ -33,7 +33,9 @@
         name=name,
         out_shape=outs,
         in_specs=[pl.BlockSpec(memory_space=spaces.get(n, pltpu.VMEM)) for n in range(len(ins))],
-        out_specs=[pl.BlockSpec(memory_space=out_space)] * len(outs),
+        out_specs=[
+            pl.BlockSpec(memory_space=pltpu.HBM if n in far_outs else pltpu.VMEM) for n in range(len(outs))
+        ],
         scratch_shapes=list(scratch),
         compiler_params=pltpu.CompilerParams(vmem_limit_bytes=limit),
         cost_estimate=pl.CostEstimate(flops=0, bytes_accessed=weight, transcendentals=0),
@@ -79,7 +81,7 @@
 
 def regroup_back_body(batch, seq, order, *refs):
     pieces, dz_ref = refs[:batch], refs[batch]
-    outs, second_ref, d_scr, r_scr = refs[batch + 1 : -3], *refs[-3:]
+    outs, second_ref, d_scr, r_scr, sems = refs[batch + 1 : -4], *refs[-4:]
     me, here = lax.axis_index("batch"), lax.axis_index("seq")
     groups = second_ref.shape[0]
     lanes = order * LANE_GROUP
@@ -92,16 +94,22 @@
     width = dz_ref.shape[1]
     tiled = one_hot((iota((order, lanes), 1) % order) == iota((order, lanes), 0))
     keep = (iota((lanes, lanes), 0) % LANE_GROUP) == (iota((lanes, lanes), 1) // order)
+    writes = []
     for g in range(groups):
         packed = d_scr[g].astype(BF16)
         second_ref[g] = packed
         weights = jnp.where(keep, dot(packed, tiled, 0, 0), 0.0).astype(BF16)
         result = dot(weights, dz_ref[g * lanes : (g + 1) * lanes, :]).astype(BF16)
-        r_scr[:, g * LANE_GROUP : (g + 1) * LANE_GROUP, :] = result.reshape(order, LANE_GROUP, width)
+        js = slice(g * LANE_GROUP, (g + 1) * LANE_GROUP)
+        r_scr[:, js, :] = result.reshape(order, LANE_GROUP, width)
+        if len(outs) == 1:
+            writes.append(pltpu.make_async_copy(r_scr.at[:, js, :], outs[0].at[:, js, :], sems.at[g]))
+            writes[g].start()
 
     blocks = order // seq
     if len(outs) == 1:
-        outs[0][...] = r_scr[...].reshape(outs[0].shape)
+        for write in writes:
+            write.wait()
     else:
         for d in range(seq):
             outs[d][...] = r_scr[pl.ds((here ^ d) * blocks, blocks)]
@@ -304,12 +312,15 @@
     piece = of((blocks, j_here, width))
     *back, second = call(
         functools.partial(regroup_back_body, batch, seq, count),
-        ([of((seq, blocks, j_here, width))] if CFG['a2a'][0] else [piece] * seq) + [of((groups, count, lanes))],
+        ([of((count, j_here, width))] if CFG['a2a'][0] else [piece] * seq) + [of((groups, count, lanes))],
         [*[packed[d] for d in range(batch)], dz],
         [
             pltpu.VMEM((groups, count, lanes), F32),
             pltpu.VMEM((count, j_here, width), BF16),
+            pltpu.SemaphoreType.DMA((groups,)),
         ],
+        far_outs=(0,) if CFG['a2a'][0] else (),
+        limit=24 << 20,
     )
     keep("A2", back[0])
     first_ready = after(first_factor, dz) if CFG['f2early'] else after(first_factor, dz, *[packed[d] for d in (1, 2, 3)])
@@ -318,7 +329,9 @@
     direct = move("f3", first_ready, "batch", 3, batch) if CFG['direct'] else None
     back_got = {0: back[0]}
     if CFG['a2a'][0]:
-        back_got[0] = keep("h0", lax.all_to_all(dep("h0", back[0]), "seq", 0, 0, tiled=True))
+        back_got[0] = keep("h0", lax.all_to_all(
+            dep("h0", back[0]).reshape(seq, blocks, j_here, width), "seq", 0, 0, tiled=True
+        ))
     else:
         for d in CFG['order'][0]:
             back_got[d] = move(f"h{d}", back[d], "seq", d, seq)
@@ -327,7 +340,7 @@
     first = [first_factor, beside, across, direct]
     *regrouped, h = call(
         functools.partial(mix_body, batch, seq),
-        [piece] * seq + [of((rows_here, width))],
+        ([of((seq, blocks, j_here, width))] if CFG['a2a'][1] else [piece] * seq) + [of((rows_here, width))],
         [dep("M", first_factor), *first[1:], x, alt, cot, src],
         [
             pltpu.VMEM((order, order), BF16),
@@ -335,6 +348,8 @@
             pltpu.VMEM((blocks, seq, j_here, width), BF16),
             pltpu.SemaphoreType.DMA((blocks,)),
         ],
+        far_outs=(0,) if CFG['a2a'][1] else (),
+        limit=CFG['limit'],
     )
     keep("M", regrouped[0])
     got = {0: regrouped[0]}
@@ -348,6 +363,7 @@
         [of((blocks, k_here, order))] * batch + [of((blocks, order, width))],
         [dep("F1", back_got[0]), *[back_got[d] for d in range(1, seq) if d in back_got], x, alt],
         [pltpu.VMEM((order, order), BF16), pltpu.VMEM((order, width), BF16), pltpu.VMEM((order, order), BF16)],
+        limit=CFG['limit'],
     )
     keep("F1", dmixed)
     if CFG['rsdirect']:
@@ -359,13 +375,14 @@
         functools.partial(mix_back_body, batch),
         [of((rows_here, width))],
         [dep("F2", first_factor), *first[1:], dmixed],
+        limit=CFG['limit'],
     )
     keep("F2", dmix_in)
     if CFG['rsdirect']:
         (grad_one,) = call(sum_body, [of(parts[0].shape)], [dep("sum", parts[0]), *others])
     else:
         kept, summed = call(
-            pair_body, [of(parts[0].shape, F32), of(parts[0].shape)], [dep("pair", parts[0]), parts[2], near, far]
+            pair_body, [of(parts[0].shape, F32), of(parts[0].shape)], [dep("pair", parts[0]), parts[2], near, far], limit=CFG['limit']
         )
         keep("pair", summed)
         rx = move("rx", summed, "batch", 2, batch)

time: 84.1 us -> 87.4 us (1.039)
  starting transfers between devices: 35.9 us -> 18.4 us
  Pallas kernels: 16 us -> 29 us
  local copies, waits for them, and re-layouts: 3.98 us -> 8.59 us
  waiting for transfers between devices: 26.2 us -> 30.2 us
    ppermute x26 -> x12, starting transfers between devices: 35.9 us -> 8.51 us  [swap(): return lax.ppermute(value, axis, [(p, p ^ step) for p in range(size)])]
    pallas_call x10 -> x11, Pallas kernels: 16 us -> 29 us  [call(): pl.pallas_call(body, name=name, out_shape=outs, in_specs=[pl.BlockSpec(me...]
    all_to_all x0 -> x2, waiting for transfers between devices: none -> 12.7 us  [the longest x1 9.41 us: packed_shards(): lax.all_to_all(dep('H0', regrouped[0]), 'seq', 0, 0, tiled=True)]
    all_to_all x0 -> x2, starting transfers between devices: none -> 9.88 us  [the longest x1 6.24 us: packed_shards(): lax.all_to_all(dep('h0', back[0]).reshape(seq, blocks, j_here, width), 's...]
    ppermute x26 -> x12, waiting for transfers between devices: 26.2 us -> 17.4 us  [swap(): return lax.ppermute(value, axis, [(p, p ^ step) for p in range(size)])]
    unnamed x16 -> x30, local copies, waits for them, and re-layouts: 3.98 us -> 8.59 us
  transfers between devices with their start and end apart: 26 -> 14, of which waited for: 7 -> 5; matrix products, arithmetic and copies ran while one was open for 0% -> 0% of each run, Pallas kernels for 16% -> 27%
where the time goes in v9:
time: 87.4 us; the launch traced here: 86.9 us
  waiting for transfers between devices  30.2 us (35%)
  Pallas kernels  29 us (33%)
  starting transfers between devices  18.4 us (21%)
  local copies, waits for them, and re-layouts  8.59 us (10%)
    pallas_call x11, Pallas kernels, call(): pl.pallas_call(body, name=name, out_shape=outs, in_specs=[pl.BlockSpec(me...  29 us
    ppermute x12, waiting for transfers between devices, swap(): return lax.ppermute(value, axis, [(p, p ^ step) for p in range(size)])  17.4 us
    all_to_all x1, waiting for transfers between devices, packed_shards(): lax.all_to_all(dep('H0', regrouped[0]), 'seq', 0, 0, tiled=True)  9.41 us
    unnamed x30, local copies, waits for them, and re-layouts  8.59 us
    ppermute x12, starting transfers between devices, swap(): return lax.ppermute(value, axis, [(p, p ^ step) for p in range(size)])  8.51 us
    all_to_all x1, starting transfers between devices, packed_shards(): lax.all_to_all(dep('h0', back[0]).reshape(seq, blocks, j_here, width), 's...  6.24 us
    all_to_all x1, starting transfers between devices, packed_shards(): lax.all_to_all(dep('H0', regrouped[0]), 'seq', 0, 0, tiled=True)  3.64 us
    all_to_all x1, waiting for transfers between devices, packed_shards(): lax.all_to_all(dep('h0', back[0]).reshape(seq, blocks, j_here, width), 's...  3.32 us
  transfers between devices with their start and end apart: 14, of which 5 were waited for; matrix products, arithmetic and copies ran while one was open for 0% of the time, Pallas kernels for 27%

profile of v9, /device:TPU:0, one launch (start us, length us, event | category | flops | bytes accessed | tf_op | source)
XLA Modules:
  0.0 86.9 jit_solution(11985121537580983970)
XLA Ops:
  0.6 0.0 copy-start.5
  0.6 0.8 copy-done.5
  1.5 0.4 pack_body.1.refs_0_
  1.9 2.4 %collective-permute-start.2 = (bf16[32,512]{1,0:T(8,128)(2,1)S(1)}, bf16[32,512]{1,0:T(8,128)(2,1)S(1)}, u32[]{:S(2)}, u32[]{:S(2)}) collective-permute-start(bf16[32,512]{1,0:T(8,128)(2,1)S(1)} %pack_body.1.refs_0_), channel_id=1, source_target_pairs={{0,3},{1,2},{2,1},{3,0},{4,7},{5,6},{6,5},{7,4},{8,11},{9,10},{10,... | collective-permute-start | bytes 98312 | tf_op jit(solution)/shard_map/ppermute | solution.py:50
  4.3 0.6 collective-permute-start.1
  5.0 0.0 collective-permute-start
  5.0 0.0 copy-start.6
  5.0 0.7 copy-done.6
  5.7 0.0 copy-start
  5.7 1.2 %copy-done = bf16[1,2048,256]{2,1,0:T(8,128)(2,1)S(1)} copy-done((bf16[1,2048,256]{2,1,0:T(8,128)(2,1)S(1)}, bf16[1,2048,256]{2,1,0:T(8,128)(2,1)}, u32[]{:S(2)}) %copy-start) | copy-done | bytes 1048600
  6.9 0.0 copy-start.2
  6.9 1.2 %copy-done.2 = bf16[1,2048,256]{2,1,0:T(8,128)(2,1)S(1)} copy-done((bf16[1,2048,256]{2,1,0:T(8,128)(2,1)S(1)}, bf16[1,2048,256]{2,1,0:T(8,128)(2,1)}, u32[]{:S(2)}) %copy-start.2) | copy-done | bytes 1048600
  8.1 0.5 gate_body.1.refs_4_.refs_1_
  8.6 0.0 collective-permute-done.2.refs_3_
  8.6 0.0 collective-permute-done.1.refs_2_
  8.7 0.0 collective-permute-done.refs_1_
  8.7 2.2 %regroup_back_body.1 = (bf16[32,64,256]{2,1,0:T(8,128)(2,1)}, bf16[4,32,512]{2,1,0:T(8,128)(2,1)S(1)}) custom-call(bf16[32,512]{1,0:T(8,128)(2,1)S(1)} %pack_body.1.refs_0_, bf16[32,512]{1,0:T(8,128)(2,1)S(1)} %collective-permute-done.refs_1_, bf16[32,512]{1,0:T(8,128)(2,1)S(1)} %collective-permute-done.1.refs_2_, ...), custom_call_target="tpu_custom_call" | custom-call | tf_op jit(solution)/shard_map/regroup_back_body/pallas_call | solution.py:31
  10.9 0.0 copy-start.9
  10.9 6.2 %all-to-all-start.1 = ((bf16[8,4,64,256]{3,2,1,0:T(8,128)(2,1)}), bf16[8,4,64,256]{3,2,1,0:T(8,128)(2,1)S(1)}, u32[]{:S(2)}, u32[]{:S(2)}) async-start(bf16[8,4,64,256]{3,2,1,0:T(8,128)(2,1)} %bitcast.6), calls=%async_computation.1 | async-start | bytes 2097152 | tf_op jit(solution)/shard_map/all_to_all | solution.py:332
  17.1 0.0 copy-done.9
  17.1 1.6 %collective-permute-start.4 = (bf16[4,128,512]{2,1,0:T(8,128)(2,1)S(1)}, bf16[4,128,512]{2,1,0:T(8,128)(2,1)S(1)}, u32[]{:S(2)}, u32[]{:S(2)}) collective-permute-start(bf16[4,128,512]{2,1,0:T(8,128)(2,1)S(1)} %copy-done.9), channel_id=1, source_target_pairs={{0,2},{1,3},{2,0},{3,1},{4,6},{5,7},{6,4},{7,5},{8,10},{9,11},{10,... | collective-permute-start | bytes 1572872 | tf_op jit(solution)/shard_map/ppermute | solution.py:50
  18.7 0.0 collective-permute-start.3
  18.7 12.3 %collective-permute-done.4.refs_2_ = bf16[4,128,512]{2,1,0:T(8,128)(2,1)S(1)} collective-permute-done((bf16[4,128,512]{2,1,0:T(8,128)(2,1)S(1)}, bf16[4,128,512]{2,1,0:T(8,128)(2,1)S(1)}, u32[]{:S(2)}, u32[]{:S(2)}) %collective-permute-start.4) | collective-permute-done | bytes 524320 | tf_op jit(solution)/shard_map/ppermute | solution.py:50
  30.9 0.0 copy-start.10
  30.9 0.0 collective-permute-start.5
  30.9 0.0 collective-permute-done.3.refs_1_
  31.0 0.0 copy-start.11
  31.0 1.9 %collective-permute-done.5.refs_3_ = bf16[4,128,512]{2,1,0:T(8,128)(2,1)S(1)} collective-permute-done((bf16[4,128,512]{2,1,0:T(8,128)(2,1)S(1)}, bf16[4,128,512]{2,1,0:T(8,128)(2,1)S(1)}, u32[]{:S(2)}, u32[]{:S(2)}) %collective-permute-start.5) | collective-permute-done | bytes 524320 | tf_op jit(solution)/shard_map/ppermute | solution.py:50
  32.9 0.8 copy-done.12
  33.7 0.0 copy-done.10
  33.7 0.0 copy-done.11
  33.7 6.3 %mix_body.1 = (bf16[8,4,64,256]{3,2,1,0:T(8,128)(2,1)}, bf16[2048,256]{1,0:T(8,128)(2,1)}) custom-call(bf16[4,128,512]{2,1,0:T(8,128)(2,1)} %refs_0_.3, bf16[4,128,512]{2,1,0:T(8,128)(2,1)} %copy-done.11, bf16[4,128,512]{2,1,0:T(8,128)(2,1)} %copy-done.10, bf16[4,128,512]{2,1,0:T(8,128)(2,1)} %copy-done.12, bf16[2048,256]{1,0:T(8,128)(2,1)} %bitcast.15, ...), custom_call_target="tpu_custom_call" | custom-call | tf_op jit(solution)/shard_map/mix_body/pallas_call | solution.py:31
  39.9 3.3 %all-to-all-done.1.refs_0_ = bf16[8,4,64,256]{3,2,1,0:T(8,128)(2,1)S(1)} async-done(((bf16[8,4,64,256]{3,2,1,0:T(8,128)(2,1)}), bf16[8,4,64,256]{3,2,1,0:T(8,128)(2,1)S(1)}, u32[]{:S(2)}, u32[]{:S(2)}) %all-to-all-start.1) | async-done | bytes 1048608 | tf_op jit(solution)/shard_map/all_to_all | solution.py:332
  43.3 0.0 copy-start.8
  43.3 1.0 %copy-done.8 = bf16[8,4,64,256]{3,2,1,0:T(8,128)(2,1)} copy-done((bf16[8,4,64,256]{3,2,1,0:T(8,128)(2,1)}, bf16[8,4,64,256]{3,2,1,0:T(8,128)(2,1)S(1)}, u32[]{:S(2)}) %copy-start.8) | copy-done | bytes 1048600
  44.2 3.6 %all-to-all-start = ((bf16[8,4,64,256]{3,2,1,0:T(8,128)(2,1)}), bf16[8,4,64,256]{3,2,1,0:T(8,128)(2,1)S(1)}, u32[]{:S(2)}, u32[]{:S(2)}) async-start(bf16[8,4,64,256]{3,2,1,0:T(8,128)(2,1)} %get-tuple-element.27), calls=%async_computation | async-start | bytes 2097152 | tf_op jit(solution)/shard_map/all_to_all | solution.py:357
  47.9 6.2 %first_grad_body.1 = (bf16[4,128,512]{2,1,0:T(8,128)(2,1)}, bf16[4,128,512]{2,1,0:T(8,128)(2,1)}, bf16[4,128,512]{2,1,0:T(8,128)(2,1)}, bf16[4,128,512]{2,1,0:T(8,128)(2,1)}, bf16[4,512,256]{2,1,0:T(8,128)(2,1)}) custom-call(bf16[8,4,64,256]{3,2,1,0:T(8,128)(2,1)} %copy-done.8, bf16[2048,256]{1,0:T(8,128)(2,1)} %bitcast.16, s32[1,512]{1,0:T(1,128)} %bitcast.27), custom_call_target="tpu_custom_call" | custom-call | tf_op jit(solution)/shard_map/first_grad_body/pallas_call | solution.py:31
  54.1 0.0 collective-permute-start.6
  54.1 0.5 collective-permute-start.7
  54.6 4.7 %mix_back_body.1.back_ref = bf16[2048,256]{1,0:T(8,128)(2,1)} custom-call(bf16[4,128,512]{2,1,0:T(8,128)(2,1)} %refs_0_.3, bf16[4,128,512]{2,1,0:T(8,128)(2,1)} %copy-done.11, bf16[4,128,512]{2,1,0:T(8,128)(2,1)} %copy-done.10, bf16[4,128,512]{2,1,0:T(8,128)(2,1)} %copy-done.12, bf16[4,512,256]{2,1,0:T(8,128)(2,1)} %get-tuple-element.29.refs_4_), custom_call_target="tpu_custom_call" | custom-call | tf_op jit(solution)/shard_map/mix_back_body/pallas_call | solution.py:31
  59.3 0.0 collective-permute-done.6.got_a
  59.3 0.0 copy-start.13
  59.3 0.0 collective-permute-done.7.got_b
  59.3 0.0 copy-start.14
  59.3 0.8 copy-done.13
  60.1 0.2 copy-done.14
  60.2 2.8 %pair_body.1 = (f32[4,128,512]{2,1,0:T(8,128)}, bf16[4,128,512]{2,1,0:T(8,128)(2,1)}) custom-call(bf16[4,128,512]{2,1,0:T(8,128)(2,1)} %get-tuple-element.32.own_a, bf16[4,128,512]{2,1,0:T(8,128)(2,1)} %get-tuple-element.33.own_b, bf16[4,128,512]{2,1,0:T(8,128)(2,1)} %copy-done.13, bf16[4,128,512]{2,1,0:T(8,128)(2,1)} %copy-done.14), custom_call_target="tpu_custom_call" | custom-call | tf_op jit(solution)/shard_map/pair_body/pallas_call | solution.py:31
  63.0 1.4 %collective-permute-start.8 = (bf16[4,128,512]{2,1,0:T(8,128)(2,1)}, bf16[4,128,512]{2,1,0:T(8,128)(2,1)S(1)}, u32[]{:S(2)}, u32[]{:S(2)}) collective-permute-start(bf16[4,128,512]{2,1,0:T(8,128)(2,1)} %get-tuple-element.37), channel_id=1, source_target_pairs={{0,2},{1,3},{2,0},{3,1},{4,6},{5,7},{6,4},{7,5},{8,10},{9,11},{10,... | collective-permute-start | bytes 1572872 | tf_op jit(solution)/shard_map/ppermute | solution.py:50
  64.4 9.4 %all-to-all-done = bf16[8,4,64,256]{3,2,1,0:T(8,128)(2,1)S(1)} async-done(((bf16[8,4,64,256]{3,2,1,0:T(8,128)(2,1)}), bf16[8,4,64,256]{3,2,1,0:T(8,128)(2,1)S(1)}, u32[]{:S(2)}, u32[]{:S(2)}) %all-to-all-start) | async-done | bytes 1048608 | tf_op jit(solution)/shard_map/all_to_all | solution.py:357
  73.8 3.2 %collective-permute-done.8.got = bf16[4,128,512]{2,1,0:T(8,128)(2,1)S(1)} collective-permute-done((bf16[4,128,512]{2,1,0:T(8,128)(2,1)}, bf16[4,128,512]{2,1,0:T(8,128)(2,1)S(1)}, u32[]{:S(2)}, u32[]{:S(2)}) %collective-permute-start.8) | collective-permute-done | bytes 524320 | tf_op jit(solution)/shard_map/ppermute | solution.py:50
  77.1 1.2 %copy-done.4 = f32[4,128,512]{2,1,0:T(8,128)S(1)} copy-done((f32[4,128,512]{2,1,0:T(8,128)S(1)}, f32[4,128,512]{2,1,0:T(8,128)}, u32[]{:S(2)}) %copy-start.4) | copy-done | bytes 1048600
  78.3 0.9 %add_body.1 = bf16[4,128,512]{2,1,0:T(8,128)(2,1)} custom-call(f32[4,128,512]{2,1,0:T(8,128)S(1)} %copy-done.4, bf16[4,128,512]{2,1,0:T(8,128)(2,1)S(1)} %collective-permute-done.8.got), custom_call_target="tpu_custom_call" | custom-call | tf_op jit(solution)/shard_map/add_body/pallas_call | solution.py:31
  79.2 1.3 %second_grad_body.1 = (bf16[32,512]{1,0:T(8,128)(2,1)S(1)}, bf16[32,512]{1,0:T(8,128)(2,1)S(1)}, bf16[32,512]{1,0:T(8,128)(2,1)S(1)}, bf16[32,512]{1,0:T(8,128)(2,1)S(1)}) custom-call(bf16[32,64,256]{2,1,0:T(8,128)(2,1)S(1)} %bitcast.13, bf16[2048,256]{1,0:T(8,128)(2,1)S(1)} %gate_body.1.refs_4_.refs_1_), custom_call_target="tpu_custom_call" | custom-call | tf_op jit(solution)/shard_map/second_grad_body/pallas_call | solution.py:31
  80.5 0.1 collective-permute-start.9
  80.6 1.5 %collective-permute-start.10 = (bf16[32,512]{1,0:T(8,128)(2,1)S(1)}, bf16[32,512]{1,0:T(8,128)(2,1)S(1)}, u32[]{:S(2)}, u32[]{:S(2)}) collective-permute-start(bf16[32,512]{1,0:T(8,128)(2,1)S(1)} %get-tuple-element.43), channel_id=1, source_target_pairs={{0,2},{1,3},{2,0},{3,1},{4,6},{5,7},{6,4},{7,5},{8,10},{9,11},{10,... | collective-permute-start | bytes 98312 | tf_op jit(solution)/shard_map/ppermute | solution.py:50
  82.0 0.4 collective-permute-start.11
  82.5 0.0 copy-done.1
  82.5 0.0 copy-done.3
  82.5 0.7 copy-done.7
  83.1 2.7 %tokens_body.1 = bf16[2048,256]{1,0:T(8,128)(2,1)} custom-call(bf16[32,64,256]{2,1,0:T(8,128)(2,1)S(1)} %bitcast.14, bf16[4,32,512]{2,1,0:T(8,128)(2,1)S(1)} %get-tuple-element.39.second_ref, bf16[2048,256]{1,0:T(8,128)(2,1)S(1)} %copy-done.3, s32[1,256]{1,0:T(1,128)S(1)} %bitcast.23, bf16[2048,256]{1,0:T(8,128)(2,1)S(1)} %copy-done.1), custom_call_target="tpu_custom_call" | custom-call | tf_op jit(solution)/shard_map/tokens_body/pallas_call | solution.py:31
  85.8 0.0 collective-permute-done.9.refs_1_
  85.8 0.0 collective-permute-done.10.refs_2_
  85.8 0.0 collective-permute-done.11.refs_3_
  85.8 1.1 %unpack_body.1 = bf16[256,64]{1,0:T(8,128)(2,1)} custom-call(bf16[32,512]{1,0:T(8,128)(2,1)S(1)} %get-tuple-element.41.refs_0_, bf16[32,512]{1,0:T(8,128)(2,1)S(1)} %collective-permute-done.9.refs_1_, bf16[32,512]{1,0:T(8,128)(2,1)S(1)} %collective-permute-done.10.refs_2_, bf16[32,512]{1,0:T(8,128)(2,1)S(1)} %collective-permute-done.11.refs_3_), custom_call_target="tpu_custom_call" | custom-call | tf_op jit(solution)/shard_map/unpack_body/pallas_call | solution.py:31
  (5 shorter events, 0.0 us)
Async XLA Ops:
  0.6 0.8 copy-start.5
  1.9 6.7 %collective-permute-start.2 = (bf16[32,512]{1,0:T(8,128)(2,1)S(1)}, bf16[32,512]{1,0:T(8,128)(2,1)S(1)}, u32[]{:S(2)}, u32[]{:S(2)}) collective-permute-start(bf16[32,512]{1,0:T(8,128)(2,1)S(1)} %pack_body.1.refs_0_), channel_id=1, source_target_pairs={{0,3},{1,2},{2,1},{3,0},{4,7},{5,6},{6,5},{7,4},{8,11},{9,10},{10,... | collective-permute-start | bytes 98312 | tf_op jit(solution)/shard_map/ppermute | solution.py:50
  4.3 4.3 %collective-permute-start.1 = (bf16[32,512]{1,0:T(8,128)(2,1)S(1)}, bf16[32,512]{1,0:T(8,128)(2,1)S(1)}, u32[]{:S(2)}, u32[]{:S(2)}) collective-permute-start(bf16[32,512]{1,0:T(8,128)(2,1)S(1)} %pack_body.1.refs_0_), channel_id=1, source_target_pairs={{0,2},{1,3},{2,0},{3,1},{4,6},{5,7},{6,4},{7,5},{8,10},{9,11},{10,... | collective-permute-start | bytes 98312 | tf_op jit(solution)/shard_map/ppermute | solution.py:50
  5.0 3.7 %collective-permute-start = (bf16[32,512]{1,0:T(8,128)(2,1)S(1)}, bf16[32,512]{1,0:T(8,128)(2,1)S(1)}, u32[]{:S(2)}, u32[]{:S(2)}) collective-permute-start(bf16[32,512]{1,0:T(8,128)(2,1)S(1)} %pack_body.1.refs_0_), channel_id=1, source_target_pairs={{0,1},{1,0},{2,3},{3,2},{4,5},{5,4},{6,7},{7,6},{8,9},{9,8},{10,11... | collective-permute-start | bytes 98312 | tf_op jit(solution)/shard_map/ppermute | solution.py:50
  5.0 0.7 copy-start.6
  5.7 1.2 %copy-start = (bf16[1,2048,256]{2,1,0:T(8,128)(2,1)S(1)}, bf16[1,2048,256]{2,1,0:T(8,128)(2,1)}, u32[]{:S(2)}) copy-start(bf16[1,2048,256]{2,1,0:T(8,128)(2,1)} %param.6) | copy-start | bytes 3145732
  6.9 1.2 %copy-start.2 = (bf16[1,2048,256]{2,1,0:T(8,128)(2,1)S(1)}, bf16[1,2048,256]{2,1,0:T(8,128)(2,1)}, u32[]{:S(2)}) copy-start(bf16[1,2048,256]{2,1,0:T(8,128)(2,1)} %param.7) | copy-start | bytes 3145732
  10.9 6.3 %copy-start.9 = (bf16[4,128,512]{2,1,0:T(8,128)(2,1)S(1)}, bf16[4,128,512]{2,1,0:T(8,128)(2,1)}, u32[]{:S(2)}) copy-start(bf16[4,128,512]{2,1,0:T(8,128)(2,1)} %refs_0_.3) | copy-start | bytes 1572868
  10.9 32.4 %all-to-all-start.1 = ((bf16[8,4,64,256]{3,2,1,0:T(8,128)(2,1)}), bf16[8,4,64,256]{3,2,1,0:T(8,128)(2,1)S(1)}, u32[]{:S(2)}, u32[]{:S(2)}) async-start(bf16[8,4,64,256]{3,2,1,0:T(8,128)(2,1)} %bitcast.6), calls=%async_computation.1 | async-start | bytes 2097152 | tf_op jit(solution)/shard_map/all_to_all | solution.py:332
  17.1 13.8 %collective-permute-start.4 = (bf16[4,128,512]{2,1,0:T(8,128)(2,1)S(1)}, bf16[4,128,512]{2,1,0:T(8,128)(2,1)S(1)}, u32[]{:S(2)}, u32[]{:S(2)}) collective-permute-start(bf16[4,128,512]{2,1,0:T(8,128)(2,1)S(1)} %copy-done.9), channel_id=1, source_target_pairs={{0,2},{1,3},{2,0},{3,1},{4,6},{5,7},{6,4},{7,5},{8,10},{9,11},{10,... | collective-permute-start | bytes 1572872 | tf_op jit(solution)/shard_map/ppermute | solution.py:50
  18.7 12.3 %collective-permute-start.3 = (bf16[4,128,512]{2,1,0:T(8,128)(2,1)S(1)}, bf16[4,128,512]{2,1,0:T(8,128)(2,1)S(1)}, u32[]{:S(2)}, u32[]{:S(2)}) collective-permute-start(bf16[4,128,512]{2,1,0:T(8,128)(2,1)S(1)} %copy-done.9), channel_id=1, source_target_pairs={{0,1},{1,0},{2,3},{3,2},{4,5},{5,4},{6,7},{7,6},{8,9},{9,8},{10,11... | collective-permute-start | bytes 1572872 | tf_op jit(solution)/shard_map/ppermute | solution.py:50
  30.9 2.7 %copy-start.10 = (bf16[4,128,512]{2,1,0:T(8,128)(2,1)}, bf16[4,128,512]{2,1,0:T(8,128)(2,1)S(1)}, u32[]{:S(2)}) copy-start(bf16[4,128,512]{2,1,0:T(8,128)(2,1)S(1)} %collective-permute-done.4.refs_2_) | copy-start | bytes 1572868
  30.9 1.9 %collective-permute-start.5 = (bf16[4,128,512]{2,1,0:T(8,128)(2,1)S(1)}, bf16[4,128,512]{2,1,0:T(8,128)(2,1)S(1)}, u32[]{:S(2)}, u32[]{:S(2)}) collective-permute-start(bf16[4,128,512]{2,1,0:T(8,128)(2,1)S(1)} %collective-permute-done.4.refs_2_), channel_id=1, source_target_pairs={{0,1},{1,0},{2,3},{3,2},{4,5},{5,4},{6,7},{7,6},{8,9},{9,8},{10,11... | collective-permute-start | bytes 1572872 | tf_op jit(solution)/shard_map/ppermute | solution.py:50
  31.0 2.7 %copy-start.11 = (bf16[4,128,512]{2,1,0:T(8,128)(2,1)}, bf16[4,128,512]{2,1,0:T(8,128)(2,1)S(1)}, u32[]{:S(2)}) copy-start(bf16[4,128,512]{2,1,0:T(8,128)(2,1)S(1)} %collective-permute-done.3.refs_1_) | copy-start | bytes 1572868
  32.9 0.8 copy-start.12
  43.3 1.0 %copy-start.8 = (bf16[8,4,64,256]{3,2,1,0:T(8,128)(2,1)}, bf16[8,4,64,256]{3,2,1,0:T(8,128)(2,1)S(1)}, u32[]{:S(2)}) copy-start(bf16[8,4,64,256]{3,2,1,0:T(8,128)(2,1)S(1)} %all-to-all-done.1.refs_0_) | copy-start | bytes 3145732
  44.2 29.6 %all-to-all-start = ((bf16[8,4,64,256]{3,2,1,0:T(8,128)(2,1)}), bf16[8,4,64,256]{3,2,1,0:T(8,128)(2,1)S(1)}, u32[]{:S(2)}, u32[]{:S(2)}) async-start(bf16[8,4,64,256]{3,2,1,0:T(8,128)(2,1)} %get-tuple-element.27), calls=%async_computation | async-start | bytes 2097152 | tf_op jit(solution)/shard_map/all_to_all | solution.py:357
  54.1 5.2 %collective-permute-start.6 = (bf16[4,128,512]{2,1,0:T(8,128)(2,1)}, bf16[4,128,512]{2,1,0:T(8,128)(2,1)S(1)}, u32[]{:S(2)}, u32[]{:S(2)}) collective-permute-start(bf16[4,128,512]{2,1,0:T(8,128)(2,1)} %get-tuple-element.34), channel_id=1, source_target_pairs={{0,1},{1,0},{2,3},{3,2},{4,5},{5,4},{6,7},{7,6},{8,9},{9,8},{10,11... | collective-permute-start | bytes 1572872 | tf_op jit(solution)/shard_map/ppermute | solution.py:50
  54.1 5.2 %collective-permute-start.7 = (bf16[4,128,512]{2,1,0:T(8,128)(2,1)}, bf16[4,128,512]{2,1,0:T(8,128)(2,1)S(1)}, u32[]{:S(2)}, u32[]{:S(2)}) collective-permute-start(bf16[4,128,512]{2,1,0:T(8,128)(2,1)} %get-tuple-element.35), channel_id=1, source_target_pairs={{0,1},{1,0},{2,3},{3,2},{4,5},{5,4},{6,7},{7,6},{8,9},{9,8},{10,11... | collective-permute-start | bytes 1572872 | tf_op jit(solution)/shard_map/ppermute | solution.py:50
  59.3 0.8 copy-start.13
  59.3 1.0 %copy-start.14 = (bf16[4,128,512]{2,1,0:T(8,128)(2,1)}, bf16[4,128,512]{2,1,0:T(8,128)(2,1)S(1)}, u32[]{:S(2)}) copy-start(bf16[4,128,512]{2,1,0:T(8,128)(2,1)S(1)} %collective-permute-done.7.got_b) | copy-start | bytes 1572868
  63.0 14.0 %collective-permute-start.8 = (bf16[4,128,512]{2,1,0:T(8,128)(2,1)}, bf16[4,128,512]{2,1,0:T(8,128)(2,1)S(1)}, u32[]{:S(2)}, u32[]{:S(2)}) collective-permute-start(bf16[4,128,512]{2,1,0:T(8,128)(2,1)} %get-tuple-element.37), channel_id=1, source_target_pairs={{0,2},{1,3},{2,0},{3,1},{4,6},{5,7},{6,4},{7,5},{8,10},{9,11},{10,... | collective-permute-start | bytes 1572872 | tf_op jit(solution)/shard_map/ppermute | solution.py:50
  77.0 1.2 %copy-start.4 = (f32[4,128,512]{2,1,0:T(8,128)S(1)}, f32[4,128,512]{2,1,0:T(8,128)}, u32[]{:S(2)}) copy-start(f32[4,128,512]{2,1,0:T(8,128)} %get-tuple-element.36.own) | copy-start | bytes 3145732
  79.2 3.3 %copy-start.1 = (bf16[2048,256]{1,0:T(8,128)(2,1)S(1)}, bf16[2048,256]{1,0:T(8,128)(2,1)}, u32[]{:S(2)}) copy-start(bf16[2048,256]{1,0:T(8,128)(2,1)} %mix_back_body.1.back_ref) | copy-start | bytes 3145732
  79.2 3.3 %copy-start.3 = (bf16[2048,256]{1,0:T(8,128)(2,1)S(1)}, bf16[2048,256]{1,0:T(8,128)(2,1)}, u32[]{:S(2)}) copy-start(bf16[2048,256]{1,0:T(8,128)(2,1)} %get-tuple-element.40.h_ref) | copy-start | bytes 3145732
  80.5 5.3 %collective-permute-start.9 = (bf16[32,512]{1,0:T(8,128)(2,1)S(1)}, bf16[32,512]{1,0:T(8,128)(2,1)S(1)}, u32[]{:S(2)}, u32[]{:S(2)}) collective-permute-start(bf16[32,512]{1,0:T(8,128)(2,1)S(1)} %get-tuple-element.42), channel_id=1, source_target_pairs={{0,1},{1,0},{2,3},{3,2},{4,5},{5,4},{6,7},{7,6},{8,9},{9,8},{10,11... | collective-permute-start | bytes 98312 | tf_op jit(solution)/shard_map/ppermute | solution.py:50
  80.6 5.2 %collective-permute-start.10 = (bf16[32,512]{1,0:T(8,128)(2,1)S(1)}, bf16[32,512]{1,0:T(8,128)(2,1)S(1)}, u32[]{:S(2)}, u32[]{:S(2)}) collective-permute-start(bf16[32,512]{1,0:T(8,128)(2,1)S(1)} %get-tuple-element.43), channel_id=1, source_target_pairs={{0,2},{1,3},{2,0},{3,1},{4,6},{5,7},{6,4},{7,5},{8,10},{9,11},{10,... | collective-permute-start | bytes 98312 | tf_op jit(solution)/shard_map/ppermute | solution.py:50
  82.0 3.8 %collective-permute-start.11 = (bf16[32,512]{1,0:T(8,128)(2,1)S(1)}, bf16[32,512]{1,0:T(8,128)(2,1)S(1)}, u32[]{:S(2)}, u32[]{:S(2)}) collective-permute-start(bf16[32,512]{1,0:T(8,128)(2,1)S(1)} %get-tuple-element.44), channel_id=1, source_target_pairs={{0,3},{1,2},{2,1},{3,0},{4,7},{5,6},{6,5},{7,4},{8,11},{9,10},{10,... | collective-permute-start | bytes 98312 | tf_op jit(solution)/shard_map/ppermute | solution.py:50
  82.5 0.7 copy-start.7

commit v10 on v9

--- a/solution.py
+++ b/solution.py
@@ -10,7 +10,7 @@
 BF16 = jnp.bfloat16
 F32 = jnp.float32
 LANE_GROUP = 16
-CFG = {'a2a': [True, True], 'limit': 62914560, 'cost': {}, 'direct': False, 'rsdirect': False, 'f2early': False, 'order': [[7, 6, 5, 4, 3, 2, 1], [7, 6, 5, 4, 3, 2, 1]], 'deps': {'fx': ['A2'], 'F1': ['M'], 'pair': ['F2'], 'Z1': ['add']}}
+CFG = {'a2a': [True, True], 'limit': 62914560, 'cost': {}, 'direct': False, 'rsdirect': False, 'f2early': False, 'order': [[7, 6, 5, 4, 3, 2, 1], [7, 6, 5, 4, 3, 2, 1]], 'deps': {'fx': ['A2'], 'F1': ['M'], 'F2': ['pair']}}
 
 
 def iota(shape, dim):
@@ -230,11 +230,12 @@
         outs[d][...] = jnp.concatenate(rows, axis=0).astype(BF16)
 
 
-def tokens_body(reg_ref, second_ref, h_ref, src_ref, back_ref, out_ref):
+def tokens_body(reg_ref, second_ref, h_ref, src_ref, back_ref, out_hbm, out_ref, sems):
     order, j_here, width = reg_ref.shape
     groups, lanes = j_here // LANE_GROUP, order * LANE_GROUP
     select = one_hot(iota((width, width), 0) == src_ref[...])
     col = iota((order, lanes), 1) % LANE_GROUP
+    writes = []
     for g in range(groups):
         reg = reg_ref[:, g * LANE_GROUP : (g + 1) * LANE_GROUP, :].reshape(lanes, width)
         packed = second_ref[g].astype(F32)
@@ -244,6 +245,10 @@
         rows = slice(g * lanes, (g + 1) * lanes)
         dgate = (dot(weights, reg) * h_ref[rows, :].astype(F32)).astype(BF16)
         out_ref[rows, :] = (back_ref[rows, :].astype(F32) + dot(dgate, select, 1, 1)).astype(BF16)
+        writes.append(pltpu.make_async_copy(out_ref.at[rows, :], out_hbm.at[rows, :], sems.at[g]))
+        writes[g].start()
+    for write in writes:
+        write.wait()
 
 
 def pair_body(own_a, own_b, got_a, got_b, out_a, out_b):
@@ -363,7 +368,7 @@
         [of((blocks, k_here, order))] * batch + [of((blocks, order, width))],
         [dep("F1", back_got[0]), *[back_got[d] for d in range(1, seq) if d in back_got], x, alt],
         [pltpu.VMEM((order, order), BF16), pltpu.VMEM((order, width), BF16), pltpu.VMEM((order, order), BF16)],
-        limit=CFG['limit'],
+        limit=40 << 20,
     )
     keep("F1", dmixed)
     if CFG['rsdirect']:
@@ -371,22 +376,22 @@
     else:
         near = move("near", parts[1], "batch", 1, batch)
         far = move("far", parts[3], "batch", 1, batch)
-    (dmix_in,) = call(
-        functools.partial(mix_back_body, batch),
-        [of((rows_here, width))],
-        [dep("F2", first_factor), *first[1:], dmixed],
-        limit=CFG['limit'],
-    )
-    keep("F2", dmix_in)
     if CFG['rsdirect']:
         (grad_one,) = call(sum_body, [of(parts[0].shape)], [dep("sum", parts[0]), *others])
     else:
         kept, summed = call(
-            pair_body, [of(parts[0].shape, F32), of(parts[0].shape)], [dep("pair", parts[0]), parts[2], near, far], limit=CFG['limit']
+            pair_body, [of(parts[0].shape, F32), of(parts[0].shape)], [dep("pair", parts[0]), parts[2], near, far], limit=40 << 20
         )
         keep("pair", summed)
         rx = move("rx", summed, "batch", 2, batch)
         (grad_one,) = call(add_body, [of(parts[0].shape)], [kept, rx])
+    (dmix_in,) = call(
+        functools.partial(mix_back_body, batch),
+        [of((rows_here, width))],
+        [*first, dep("F2", dmixed)],
+        limit=CFG['limit'],
+    )
+    keep("F2", dmix_in)
     keep("add", grad_one)
     received = [dep("Z1", after(got[0], dmix_in)), *[got[d] for d in range(1, seq) if d in got]]
     if len(received) == 1:
@@ -401,7 +406,11 @@
         terms, gathered = [*terms, gathered], received[0]
     terms_got = [dep("unpack", terms[0])] + [move(f"R{d}", terms[d], "batch", d, batch) for d in (1, 2, 3)]
     (grad_tokens,) = call(
-        tokens_body, [of((rows_here, width))], [gathered, second, h, src, dmix_in]
+        tokens_body,
+        [of((rows_here, width))],
+        [gathered, second, h, src, dmix_in],
+        [pltpu.VMEM((rows_here, width), BF16), pltpu.SemaphoreType.DMA((groups,))],
+        far_outs=(0,),
     )
     (grad_flat,) = call(
         functools.partial(unpack_body, count), [of((m_here * count, j_here))], terms_got

time: 87.4 us -> 83.9 us (0.960)
  Pallas kernels: 29 us -> 24.8 us
    pallas_call x11, Pallas kernels: 29 us -> 24.8 us  [call(): pl.pallas_call(body, name=name, out_shape=outs, in_specs=[pl.BlockSpec(me...]
    all_to_all x1, waiting for transfers between devices: 9.41 us -> 11.1 us  [packed_shards(): lax.all_to_all(dep('H0', regrouped[0]), 'seq', 0, 0, tiled=True)]
    ppermute x12, waiting for transfers between devices: 17.4 us -> 16.3 us  [swap(): return lax.ppermute(value, axis, [(p, p ^ step) for p in range(size)])]
    unnamed x30 -> x32, local copies, waits for them, and re-layouts: 8.59 us -> 8.6 us
  transfers between devices with their start and end apart: 14 -> 14, of which waited for: 5 -> 6; matrix products, arithmetic and copies ran while one was open for 0% -> 0% of each run, Pallas kernels for 27% -> 25%
where the time goes in v10:
time: 83.9 us; the launch traced here: 83.4 us
  waiting for transfers between devices  30.7 us (37%)
  Pallas kernels  24.8 us (30%)
  starting transfers between devices  18.5 us (22%)
  local copies, waits for them, and re-layouts  8.6 us (10%)
    pallas_call x11, Pallas kernels, call(): pl.pallas_call(body, name=name, out_shape=outs, in_specs=[pl.BlockSpec(me...  24.8 us
    ppermute x12, waiting for transfers between devices, swap(): return lax.ppermute(value, axis, [(p, p ^ step) for p in range(size)])  16.3 us
    all_to_all x1, waiting for transfers between devices, packed_shards(): lax.all_to_all(dep('H0', regrouped[0]), 'seq', 0, 0, tiled=True)  11.1 us
    unnamed x32, local copies, waits for them, and re-layouts  8.6 us
    ppermute x12, starting transfers between devices, swap(): return lax.ppermute(value, axis, [(p, p ^ step) for p in range(size)])  8.51 us
    all_to_all x1, starting transfers between devices, packed_shards(): lax.all_to_all(dep('h0', back[0]).reshape(seq, blocks, j_here, width), 's...  6.24 us
    all_to_all x1, starting transfers between devices, packed_shards(): lax.all_to_all(dep('H0', regrouped[0]), 'seq', 0, 0, tiled=True)  3.77 us
    all_to_all x1, waiting for transfers between devices, packed_shards(): lax.all_to_all(dep('h0', back[0]).reshape(seq, blocks, j_here, width), 's...  3.32 us
  transfers between devices with their start and end apart: 14, of which 6 were waited for; matrix products, arithmetic and copies ran while one was open for 0% of the time, Pallas kernels for 25%

profile of v10, /device:TPU:0, one launch (start us, length us, event | category | flops | bytes accessed | tf_op | source)
XLA Modules:
  0.0 83.4 jit_solution(15762389642903183020)
XLA Ops:
  0.6 0.0 copy-start.8
  0.6 0.8 copy-done.8
  1.5 0.4 pack_body.1.refs_0_
  1.9 2.4 %collective-permute-start.2 = (bf16[32,512]{1,0:T(8,128)(2,1)S(1)}, bf16[32,512]{1,0:T(8,128)(2,1)S(1)}, u32[]{:S(2)}, u32[]{:S(2)}) collective-permute-start(bf16[32,512]{1,0:T(8,128)(2,1)S(1)} %pack_body.1.refs_0_), channel_id=1, source_target_pairs={{0,3},{1,2},{2,1},{3,0},{4,7},{5,6},{6,5},{7,4},{8,11},{9,10},{10,... | collective-permute-start | bytes 98312 | tf_op jit(solution)/shard_map/ppermute | solution.py:50
  4.3 0.6 collective-permute-start.1
  5.0 0.0 collective-permute-start
  5.0 0.0 copy-start.9
  5.0 0.7 copy-done.9
  5.7 0.0 copy-start
  5.7 1.2 %copy-done = bf16[1,2048,256]{2,1,0:T(8,128)(2,1)S(1)} copy-done((bf16[1,2048,256]{2,1,0:T(8,128)(2,1)S(1)}, bf16[1,2048,256]{2,1,0:T(8,128)(2,1)}, u32[]{:S(2)}) %copy-start) | copy-done | bytes 1048600
  6.9 0.0 copy-start.5
  6.9 1.2 %copy-done.5 = bf16[1,2048,256]{2,1,0:T(8,128)(2,1)S(1)} copy-done((bf16[1,2048,256]{2,1,0:T(8,128)(2,1)S(1)}, bf16[1,2048,256]{2,1,0:T(8,128)(2,1)}, u32[]{:S(2)}) %copy-start.5) | copy-done | bytes 1048600
  8.1 0.5 gate_body.1.refs_4_.refs_1_
  8.6 0.0 collective-permute-done.2.refs_3_
  8.6 0.0 collective-permute-done.1.refs_2_
  8.7 0.0 collective-permute-done.refs_1_
  8.7 2.2 %regroup_back_body.1 = (bf16[32,64,256]{2,1,0:T(8,128)(2,1)}, bf16[4,32,512]{2,1,0:T(8,128)(2,1)S(1)}) custom-call(bf16[32,512]{1,0:T(8,128)(2,1)S(1)} %pack_body.1.refs_0_, bf16[32,512]{1,0:T(8,128)(2,1)S(1)} %collective-permute-done.refs_1_, bf16[32,512]{1,0:T(8,128)(2,1)S(1)} %collective-permute-done.1.refs_2_, ...), custom_call_target="tpu_custom_call" | custom-call | tf_op jit(solution)/shard_map/regroup_back_body/pallas_call | solution.py:31
  10.9 0.0 copy-start.12
  10.9 6.2 %all-to-all-start.1 = ((bf16[8,4,64,256]{3,2,1,0:T(8,128)(2,1)}), bf16[8,4,64,256]{3,2,1,0:T(8,128)(2,1)S(1)}, u32[]{:S(2)}, u32[]{:S(2)}) async-start(bf16[8,4,64,256]{3,2,1,0:T(8,128)(2,1)} %bitcast.6), calls=%async_computation.1 | async-start | bytes 2097152 | tf_op jit(solution)/shard_map/all_to_all | solution.py:337
  17.1 0.0 copy-done.12
  17.1 1.6 %collective-permute-start.4 = (bf16[4,128,512]{2,1,0:T(8,128)(2,1)S(1)}, bf16[4,128,512]{2,1,0:T(8,128)(2,1)S(1)}, u32[]{:S(2)}, u32[]{:S(2)}) collective-permute-start(bf16[4,128,512]{2,1,0:T(8,128)(2,1)S(1)} %copy-done.12), channel_id=1, source_target_pairs={{0,2},{1,3},{2,0},{3,1},{4,6},{5,7},{6,4},{7,5},{8,10},{9,11},{10,... | collective-permute-start | bytes 1572872 | tf_op jit(solution)/shard_map/ppermute | solution.py:50
  18.7 0.0 collective-permute-start.3
  18.7 12.3 %collective-permute-done.4.refs_2_ = bf16[4,128,512]{2,1,0:T(8,128)(2,1)S(1)} collective-permute-done((bf16[4,128,512]{2,1,0:T(8,128)(2,1)S(1)}, bf16[4,128,512]{2,1,0:T(8,128)(2,1)S(1)}, u32[]{:S(2)}, u32[]{:S(2)}) %collective-permute-start.4) | collective-permute-done | bytes 524320 | tf_op jit(solution)/shard_map/ppermute | solution.py:50
  31.0 0.0 copy-start.13
  31.0 0.0 collective-permute-start.5
  31.0 0.0 collective-permute-done.3.refs_1_
  31.0 0.0 copy-start.14
  31.0 1.9 %collective-permute-done.5.refs_3_ = bf16[4,128,512]{2,1,0:T(8,128)(2,1)S(1)} collective-permute-done((bf16[4,128,512]{2,1,0:T(8,128)(2,1)S(1)}, bf16[4,128,512]{2,1,0:T(8,128)(2,1)S(1)}, u32[]{:S(2)}, u32[]{:S(2)}) %collective-permute-start.5) | collective-permute-done | bytes 524320 | tf_op jit(solution)/shard_map/ppermute | solution.py:50
  32.9 0.8 copy-done.15
  33.7 0.0 copy-done.13
  33.7 0.0 copy-done.14
  33.7 6.2 %mix_body.1 = (bf16[8,4,64,256]{3,2,1,0:T(8,128)(2,1)}, bf16[2048,256]{1,0:T(8,128)(2,1)}) custom-call(bf16[4,128,512]{2,1,0:T(8,128)(2,1)} %refs_0_.3, bf16[4,128,512]{2,1,0:T(8,128)(2,1)} %copy-done.14, bf16[4,128,512]{2,1,0:T(8,128)(2,1)} %copy-done.13, bf16[4,128,512]{2,1,0:T(8,128)(2,1)} %copy-done.15, bf16[2048,256]{1,0:T(8,128)(2,1)} %bitcast.15, ...), custom_call_target="tpu_custom_call" | custom-call | tf_op jit(solution)/shard_map/mix_body/pallas_call | solution.py:31
  40.0 3.3 %all-to-all-done.1.refs_0_ = bf16[8,4,64,256]{3,2,1,0:T(8,128)(2,1)S(1)} async-done(((bf16[8,4,64,256]{3,2,1,0:T(8,128)(2,1)}), bf16[8,4,64,256]{3,2,1,0:T(8,128)(2,1)S(1)}, u32[]{:S(2)}, u32[]{:S(2)}) %all-to-all-start.1) | async-done | bytes 1048608 | tf_op jit(solution)/shard_map/all_to_all | solution.py:337
  43.3 1.0 %copy-done.2 = bf16[8,4,64,256]{3,2,1,0:T(8,128)(2,1)} copy-done((bf16[8,4,64,256]{3,2,1,0:T(8,128)(2,1)}, bf16[8,4,64,256]{3,2,1,0:T(8,128)(2,1)S(1)}, u32[]{:S(2)}) %copy-start.2) | copy-done | bytes 1048600
  44.2 3.8 %all-to-all-start = ((bf16[8,4,64,256]{3,2,1,0:T(8,128)(2,1)}), bf16[8,4,64,256]{3,2,1,0:T(8,128)(2,1)S(1)}, u32[]{:S(2)}, u32[]{:S(2)}) async-start(bf16[8,4,64,256]{3,2,1,0:T(8,128)(2,1)} %get-tuple-element.26), calls=%async_computation | async-start | bytes 2097152 | tf_op jit(solution)/shard_map/all_to_all | solution.py:362
  48.0 0.0 copy-done.1
  48.0 0.0 copy-done.11
  48.0 0.0 copy-start.3
  48.0 1.2 %copy-done.3 = bf16[8,4,64,256]{3,2,1,0:T(8,128)(2,1)S(1)} copy-done((bf16[8,4,64,256]{3,2,1,0:T(8,128)(2,1)S(1)}, bf16[8,4,64,256]{3,2,1,0:T(8,128)(2,1)}, u32[]{:S(2)}) %copy-start.3) | copy-done | bytes 1048600
  49.2 2.9 %first_grad_body.1 = (bf16[4,128,512]{2,1,0:T(8,128)(2,1)S(1)}, bf16[4,128,512]{2,1,0:T(8,128)(2,1)S(1)}, bf16[4,128,512]{2,1,0:T(8,128)(2,1)S(1)}, bf16[4,128,5...) custom-call(bf16[8,4,64,256]{3,2,1,0:T(8,128)(2,1)S(1)} %copy-done.3, bf16[2048,256]{1,0:T(8,128)(2,1)S(1)} %bitcast.17, ...), custom_call_target="tpu_custom_call" | custom-call | tf_op jit(solution)/shard_map/first_grad_body/pallas_call | solution.py:31
  52.2 0.0 copy-start.7
  52.2 0.9 %copy-done.7 = bf16[4,512,256]{2,1,0:T(8,128)(2,1)} copy-done((bf16[4,512,256]{2,1,0:T(8,128)(2,1)}, bf16[4,512,256]{2,1,0:T(8,128)(2,1)S(1)}, u32[]{:S(2)}) %copy-start.7) | copy-done | bytes 1048600
  53.2 0.0 collective-permute-start.6
  53.2 0.5 collective-permute-start.7
  53.7 1.4 %collective-permute-done.6.got_a = bf16[4,128,512]{2,1,0:T(8,128)(2,1)S(1)} collective-permute-done((bf16[4,128,512]{2,1,0:T(8,128)(2,1)S(1)}, bf16[4,128,512]{2,1,0:T(8,128)(2,1)S(1)}, u32[]{:S(2)}, u32[]{:S(2)}) %collective-permute-start.6) | collective-permute-done | bytes 524320 | tf_op jit(solution)/shard_map/ppermute | solution.py:50
  55.1 0.7 collective-permute-done.7.got_b
  55.8 1.0 %pair_body.1 = (f32[4,128,512]{2,1,0:T(8,128)S(1)}, bf16[4,128,512]{2,1,0:T(8,128)(2,1)}) custom-call(bf16[4,128,512]{2,1,0:T(8,128)(2,1)S(1)} %get-tuple-element.29.own_a, bf16[4,128,512]{2,1,0:T(8,128)(2,1)S(1)} %get-tuple-element.30.own_b, bf16[4,128,512]{2,1,0:T(8,128)(2,1)S(1)} %collective-permute-done.6.got_a, ...), custom_call_target="tpu_custom_call" | custom-call | tf_op jit(solution)/shard_map/pair_body/pallas_call | solution.py:31
  56.8 1.4 %collective-permute-start.8 = (bf16[4,128,512]{2,1,0:T(8,128)(2,1)}, bf16[4,128,512]{2,1,0:T(8,128)(2,1)}, u32[]{:S(2)}, u32[]{:S(2)}) collective-permute-start(bf16[4,128,512]{2,1,0:T(8,128)(2,1)} %get-tuple-element.33), channel_id=1, source_target_pairs={{0,2},{1,3},{2,0},{3,1},{4,6},{5,7},{6,4},{7,5},{8,10},{9,11},{10,... | collective-permute-start | bytes 1572872 | tf_op jit(solution)/shard_map/ppermute | solution.py:50
  58.2 4.7 %mix_back_body.1.back_ref = bf16[2048,256]{1,0:T(8,128)(2,1)} custom-call(bf16[4,128,512]{2,1,0:T(8,128)(2,1)} %refs_0_.3, bf16[4,128,512]{2,1,0:T(8,128)(2,1)} %copy-done.14, bf16[4,128,512]{2,1,0:T(8,128)(2,1)} %copy-done.13, bf16[4,128,512]{2,1,0:T(8,128)(2,1)} %copy-done.15, bf16[4,512,256]{2,1,0:T(8,128)(2,1)} %copy-done.7), custom_call_target="tpu_custom_call" | custom-call | tf_op jit(solution)/shard_map/mix_back_body/pallas_call | solution.py:31
  62.9 11.1 %all-to-all-done = bf16[8,4,64,256]{3,2,1,0:T(8,128)(2,1)S(1)} async-done(((bf16[8,4,64,256]{3,2,1,0:T(8,128)(2,1)}), bf16[8,4,64,256]{3,2,1,0:T(8,128)(2,1)S(1)}, u32[]{:S(2)}, u32[]{:S(2)}) %all-to-all-start) | async-done | bytes 1048608 | tf_op jit(solution)/shard_map/all_to_all | solution.py:362
  74.0 1.3 %second_grad_body.1 = (bf16[32,512]{1,0:T(8,128)(2,1)S(1)}, bf16[32,512]{1,0:T(8,128)(2,1)S(1)}, bf16[32,512]{1,0:T(8,128)(2,1)S(1)}, bf16[32,512]{1,0:T(8,128)(2,1)S(1)}) custom-call(bf16[32,64,256]{2,1,0:T(8,128)(2,1)S(1)} %bitcast.13, bf16[2048,256]{1,0:T(8,128)(2,1)S(1)} %gate_body.1.refs_4_.refs_1_), custom_call_target="tpu_custom_call" | custom-call | tf_op jit(solution)/shard_map/second_grad_body/pallas_call | solution.py:31
  75.3 0.1 collective-permute-start.9
  75.4 1.5 %collective-permute-start.10 = (bf16[32,512]{1,0:T(8,128)(2,1)S(1)}, bf16[32,512]{1,0:T(8,128)(2,1)S(1)}, u32[]{:S(2)}, u32[]{:S(2)}) collective-permute-start(bf16[32,512]{1,0:T(8,128)(2,1)S(1)} %get-tuple-element.41), channel_id=1, source_target_pairs={{0,2},{1,3},{2,0},{3,1},{4,6},{5,7},{6,4},{7,5},{8,10},{9,11},{10,... | collective-permute-start | bytes 98312 | tf_op jit(solution)/shard_map/ppermute | solution.py:50
  76.8 0.4 collective-permute-start.11
  77.2 0.0 copy-done.4
  77.3 0.0 copy-done.6
  77.3 0.7 copy-done.10
  77.9 2.5 %tokens_body.1 = bf16[2048,256]{1,0:T(8,128)(2,1)} custom-call(bf16[32,64,256]{2,1,0:T(8,128)(2,1)S(1)} %bitcast.14, bf16[4,32,512]{2,1,0:T(8,128)(2,1)S(1)} %get-tuple-element.36.second_ref, bf16[2048,256]{1,0:T(8,128)(2,1)S(1)} %copy-done.6, s32[1,256]{1,0:T(1,128)S(1)} %bitcast.23, bf16[2048,256]{1,0:T(8,128)(2,1)S(1)} %copy-done.4), custom_call_target="tpu_custom_call" | custom-call | tf_op jit(solution)/shard_map/tokens_body/pallas_call | solution.py:31
  80.4 0.0 collective-permute-done.8.got
  80.4 1.9 %add_body.1 = bf16[4,128,512]{2,1,0:T(8,128)(2,1)} custom-call(f32[4,128,512]{2,1,0:T(8,128)S(1)} %get-tuple-element.38.own, bf16[4,128,512]{2,1,0:T(8,128)(2,1)} %collective-permute-done.8.got), custom_call_target="tpu_custom_call" | custom-call | tf_op jit(solution)/shard_map/add_body/pallas_call | solution.py:31
  82.3 0.0 collective-permute-done.9.refs_1_
  82.3 0.0 collective-permute-done.10.refs_2_
  82.3 0.0 collective-permute-done.11.refs_3_
  82.3 1.1 %unpack_body.1 = bf16[256,64]{1,0:T(8,128)(2,1)} custom-call(bf16[32,512]{1,0:T(8,128)(2,1)S(1)} %get-tuple-element.39.refs_0_, bf16[32,512]{1,0:T(8,128)(2,1)S(1)} %collective-permute-done.9.refs_1_, bf16[32,512]{1,0:T(8,128)(2,1)S(1)} %collective-permute-done.10.refs_2_, bf16[32,512]{1,0:T(8,128)(2,1)S(1)} %collective-permute-done.11.refs_3_), custom_call_target="tpu_custom_call" | custom-call | tf_op jit(solution)/shard_map/unpack_body/pallas_call | solution.py:31
  (7 shorter events, 0.0 us)
Async XLA Ops:
  0.6 0.8 %copy-start.8 = (bf16[64,8,32]{0,2,1:T(8,128)(2,1)S(1)}, bf16[64,8,32]{0,2,1:T(8,128)(2,1)}, u32[]{:S(2)}) copy-start(bf16[64,8,32]{0,2,1:T(8,128)(2,1)} %param.9) | copy-start | bytes 98308
  1.9 6.7 %collective-permute-start.2 = (bf16[32,512]{1,0:T(8,128)(2,1)S(1)}, bf16[32,512]{1,0:T(8,128)(2,1)S(1)}, u32[]{:S(2)}, u32[]{:S(2)}) collective-permute-start(bf16[32,512]{1,0:T(8,128)(2,1)S(1)} %pack_body.1.refs_0_), channel_id=1, source_target_pairs={{0,3},{1,2},{2,1},{3,0},{4,7},{5,6},{6,5},{7,4},{8,11},{9,10},{10,... | collective-permute-start | bytes 98312 | tf_op jit(solution)/shard_map/ppermute | solution.py:50
  4.3 4.3 %collective-permute-start.1 = (bf16[32,512]{1,0:T(8,128)(2,1)S(1)}, bf16[32,512]{1,0:T(8,128)(2,1)S(1)}, u32[]{:S(2)}, u32[]{:S(2)}) collective-permute-start(bf16[32,512]{1,0:T(8,128)(2,1)S(1)} %pack_body.1.refs_0_), channel_id=1, source_target_pairs={{0,2},{1,3},{2,0},{3,1},{4,6},{5,7},{6,4},{7,5},{8,10},{9,11},{10,... | collective-permute-start | bytes 98312 | tf_op jit(solution)/shard_map/ppermute | solution.py:50
  5.0 3.7 %collective-permute-start = (bf16[32,512]{1,0:T(8,128)(2,1)S(1)}, bf16[32,512]{1,0:T(8,128)(2,1)S(1)}, u32[]{:S(2)}, u32[]{:S(2)}) collective-permute-start(bf16[32,512]{1,0:T(8,128)(2,1)S(1)} %pack_body.1.refs_0_), channel_id=1, source_target_pairs={{0,1},{1,0},{2,3},{3,2},{4,5},{5,4},{6,7},{7,6},{8,9},{9,8},{10,11... | collective-permute-start | bytes 98312 | tf_op jit(solution)/shard_map/ppermute | solution.py:50
  5.0 0.7 copy-start.9
  5.7 1.2 %copy-start = (bf16[1,2048,256]{2,1,0:T(8,128)(2,1)S(1)}, bf16[1,2048,256]{2,1,0:T(8,128)(2,1)}, u32[]{:S(2)}) copy-start(bf16[1,2048,256]{2,1,0:T(8,128)(2,1)} %param.6) | copy-start | bytes 3145732
  6.9 1.2 %copy-start.5 = (bf16[1,2048,256]{2,1,0:T(8,128)(2,1)S(1)}, bf16[1,2048,256]{2,1,0:T(8,128)(2,1)}, u32[]{:S(2)}) copy-start(bf16[1,2048,256]{2,1,0:T(8,128)(2,1)} %param.7) | copy-start | bytes 3145732
  10.9 6.3 %copy-start.12 = (bf16[4,128,512]{2,1,0:T(8,128)(2,1)S(1)}, bf16[4,128,512]{2,1,0:T(8,128)(2,1)}, u32[]{:S(2)}) copy-start(bf16[4,128,512]{2,1,0:T(8,128)(2,1)} %refs_0_.3) | copy-start | bytes 1572868
  10.9 32.4 %all-to-all-start.1 = ((bf16[8,4,64,256]{3,2,1,0:T(8,128)(2,1)}), bf16[8,4,64,256]{3,2,1,0:T(8,128)(2,1)S(1)}, u32[]{:S(2)}, u32[]{:S(2)}) async-start(bf16[8,4,64,256]{3,2,1,0:T(8,128)(2,1)} %bitcast.6), calls=%async_computation.1 | async-start | bytes 2097152 | tf_op jit(solution)/shard_map/all_to_all | solution.py:337
  17.1 13.8 %collective-permute-start.4 = (bf16[4,128,512]{2,1,0:T(8,128)(2,1)S(1)}, bf16[4,128,512]{2,1,0:T(8,128)(2,1)S(1)}, u32[]{:S(2)}, u32[]{:S(2)}) collective-permute-start(bf16[4,128,512]{2,1,0:T(8,128)(2,1)S(1)} %copy-done.12), channel_id=1, source_target_pairs={{0,2},{1,3},{2,0},{3,1},{4,6},{5,7},{6,4},{7,5},{8,10},{9,11},{10,... | collective-permute-start | bytes 1572872 | tf_op jit(solution)/shard_map/ppermute | solution.py:50
  18.7 12.3 %collective-permute-start.3 = (bf16[4,128,512]{2,1,0:T(8,128)(2,1)S(1)}, bf16[4,128,512]{2,1,0:T(8,128)(2,1)S(1)}, u32[]{:S(2)}, u32[]{:S(2)}) collective-permute-start(bf16[4,128,512]{2,1,0:T(8,128)(2,1)S(1)} %copy-done.12), channel_id=1, source_target_pairs={{0,1},{1,0},{2,3},{3,2},{4,5},{5,4},{6,7},{7,6},{8,9},{9,8},{10,11... | collective-permute-start | bytes 1572872 | tf_op jit(solution)/shard_map/ppermute | solution.py:50
  31.0 2.7 %copy-start.13 = (bf16[4,128,512]{2,1,0:T(8,128)(2,1)}, bf16[4,128,512]{2,1,0:T(8,128)(2,1)S(1)}, u32[]{:S(2)}) copy-start(bf16[4,128,512]{2,1,0:T(8,128)(2,1)S(1)} %collective-permute-done.4.refs_2_) | copy-start | bytes 1572868
  31.0 1.9 %collective-permute-start.5 = (bf16[4,128,512]{2,1,0:T(8,128)(2,1)S(1)}, bf16[4,128,512]{2,1,0:T(8,128)(2,1)S(1)}, u32[]{:S(2)}, u32[]{:S(2)}) collective-permute-start(bf16[4,128,512]{2,1,0:T(8,128)(2,1)S(1)} %collective-permute-done.4.refs_2_), channel_id=1, source_target_pairs={{0,1},{1,0},{2,3},{3,2},{4,5},{5,4},{6,7},{7,6},{8,9},{9,8},{10,11... | collective-permute-start | bytes 1572872 | tf_op jit(solution)/shard_map/ppermute | solution.py:50
  31.0 2.7 %copy-start.14 = (bf16[4,128,512]{2,1,0:T(8,128)(2,1)}, bf16[4,128,512]{2,1,0:T(8,128)(2,1)S(1)}, u32[]{:S(2)}) copy-start(bf16[4,128,512]{2,1,0:T(8,128)(2,1)S(1)} %collective-permute-done.3.refs_1_) | copy-start | bytes 1572868
  32.9 0.8 copy-start.15
  43.3 1.0 %copy-start.2 = (bf16[8,4,64,256]{3,2,1,0:T(8,128)(2,1)}, bf16[8,4,64,256]{3,2,1,0:T(8,128)(2,1)S(1)}, u32[]{:S(2)}) copy-start(bf16[8,4,64,256]{3,2,1,0:T(8,128)(2,1)S(1)} %all-to-all-done.1.refs_0_) | copy-start | bytes 3145732
  44.2 3.8 %copy-start.1 = (bf16[1,2048,256]{2,1,0:T(8,128)(2,1)S(1)}, bf16[1,2048,256]{2,1,0:T(8,128)(2,1)}, u32[]{:S(2)}) copy-start(bf16[1,2048,256]{2,1,0:T(8,128)(2,1)} %param.6) | copy-start | bytes 3145732
  44.2 3.8 %copy-start.11 = (s32[512]{0:T(512)S(1)}, s32[512]{0:T(512)}, u32[]{:S(2)}) copy-start(s32[512]{0:T(512)} %param.11) | copy-start | bytes 6148
  44.2 29.7 %all-to-all-start = ((bf16[8,4,64,256]{3,2,1,0:T(8,128)(2,1)}), bf16[8,4,64,256]{3,2,1,0:T(8,128)(2,1)S(1)}, u32[]{:S(2)}, u32[]{:S(2)}) async-start(bf16[8,4,64,256]{3,2,1,0:T(8,128)(2,1)} %get-tuple-element.26), calls=%async_computation | async-start | bytes 2097152 | tf_op jit(solution)/shard_map/all_to_all | solution.py:362
  48.0 1.2 %copy-start.3 = (bf16[8,4,64,256]{3,2,1,0:T(8,128)(2,1)S(1)}, bf16[8,4,64,256]{3,2,1,0:T(8,128)(2,1)}, u32[]{:S(2)}) copy-start(bf16[8,4,64,256]{3,2,1,0:T(8,128)(2,1)} %copy-done.2) | copy-start | bytes 3145732
  52.2 1.0 %copy-start.7 = (bf16[4,512,256]{2,1,0:T(8,128)(2,1)}, bf16[4,512,256]{2,1,0:T(8,128)(2,1)S(1)}, u32[]{:S(2)}) copy-start(bf16[4,512,256]{2,1,0:T(8,128)(2,1)S(1)} %get-tuple-element.34.refs_4_) | copy-start | bytes 3145732
  53.2 1.9 %collective-permute-start.6 = (bf16[4,128,512]{2,1,0:T(8,128)(2,1)S(1)}, bf16[4,128,512]{2,1,0:T(8,128)(2,1)S(1)}, u32[]{:S(2)}, u32[]{:S(2)}) collective-permute-start(bf16[4,128,512]{2,1,0:T(8,128)(2,1)S(1)} %get-tuple-element.31), channel_id=1, source_target_pairs={{0,1},{1,0},{2,3},{3,2},{4,5},{5,4},{6,7},{7,6},{8,9},{9,8},{10,11... | collective-permute-start | bytes 1572872 | tf_op jit(solution)/shard_map/ppermute | solution.py:50
  53.2 2.7 %collective-permute-start.7 = (bf16[4,128,512]{2,1,0:T(8,128)(2,1)S(1)}, bf16[4,128,512]{2,1,0:T(8,128)(2,1)S(1)}, u32[]{:S(2)}, u32[]{:S(2)}) collective-permute-start(bf16[4,128,512]{2,1,0:T(8,128)(2,1)S(1)} %get-tuple-element.32), channel_id=1, source_target_pairs={{0,1},{1,0},{2,3},{3,2},{4,5},{5,4},{6,7},{7,6},{8,9},{9,8},{10,11... | collective-permute-start | bytes 1572872 | tf_op jit(solution)/shard_map/ppermute | solution.py:50
  56.8 23.6 %collective-permute-start.8 = (bf16[4,128,512]{2,1,0:T(8,128)(2,1)}, bf16[4,128,512]{2,1,0:T(8,128)(2,1)}, u32[]{:S(2)}, u32[]{:S(2)}) collective-permute-start(bf16[4,128,512]{2,1,0:T(8,128)(2,1)} %get-tuple-element.33), channel_id=1, source_target_pairs={{0,2},{1,3},{2,0},{3,1},{4,6},{5,7},{6,4},{7,5},{8,10},{9,11},{10,... | collective-permute-start | bytes 1572872 | tf_op jit(solution)/shard_map/ppermute | solution.py:50
  74.0 3.3 %copy-start.4 = (bf16[2048,256]{1,0:T(8,128)(2,1)S(1)}, bf16[2048,256]{1,0:T(8,128)(2,1)}, u32[]{:S(2)}) copy-start(bf16[2048,256]{1,0:T(8,128)(2,1)} %mix_back_body.1.back_ref) | copy-start | bytes 3145732
  74.0 3.3 %copy-start.6 = (bf16[2048,256]{1,0:T(8,128)(2,1)S(1)}, bf16[2048,256]{1,0:T(8,128)(2,1)}, u32[]{:S(2)}) copy-start(bf16[2048,256]{1,0:T(8,128)(2,1)} %get-tuple-element.37.h_ref) | copy-start | bytes 3145732
  75.3 7.0 %collective-permute-start.9 = (bf16[32,512]{1,0:T(8,128)(2,1)S(1)}, bf16[32,512]{1,0:T(8,128)(2,1)S(1)}, u32[]{:S(2)}, u32[]{:S(2)}) collective-permute-start(bf16[32,512]{1,0:T(8,128)(2,1)S(1)} %get-tuple-element.40), channel_id=1, source_target_pairs={{0,1},{1,0},{2,3},{3,2},{4,5},{5,4},{6,7},{7,6},{8,9},{9,8},{10,11... | collective-permute-start | bytes 98312 | tf_op jit(solution)/shard_map/ppermute | solution.py:50
  75.4 7.0 %collective-permute-start.10 = (bf16[32,512]{1,0:T(8,128)(2,1)S(1)}, bf16[32,512]{1,0:T(8,128)(2,1)S(1)}, u32[]{:S(2)}, u32[]{:S(2)}) collective-permute-start(bf16[32,512]{1,0:T(8,128)(2,1)S(1)} %get-tuple-element.41), channel_id=1, source_target_pairs={{0,2},{1,3},{2,0},{3,1},{4,6},{5,7},{6,4},{7,5},{8,10},{9,11},{10,... | collective-permute-start | bytes 98312 | tf_op jit(solution)/shard_map/ppermute | solution.py:50
  76.8 5.5 %collective-permute-start.11 = (bf16[32,512]{1,0:T(8,128)(2,1)S(1)}, bf16[32,512]{1,0:T(8,128)(2,1)S(1)}, u32[]{:S(2)}, u32[]{:S(2)}) collective-permute-start(bf16[32,512]{1,0:T(8,128)(2,1)S(1)} %get-tuple-element.42), channel_id=1, source_target_pairs={{0,3},{1,2},{2,1},{3,0},{4,7},{5,6},{6,5},{7,4},{8,11},{9,10},{10,... | collective-permute-start | bytes 98312 | tf_op jit(solution)/shard_map/ppermute | solution.py:50
  77.2 0.7 copy-start.10

commit v11 on v10

--- a/solution.py
+++ b/solution.py
@@ -10,7 +10,7 @@
 BF16 = jnp.bfloat16
 F32 = jnp.float32
 LANE_GROUP = 16
-CFG = {'a2a': [True, True], 'limit': 62914560, 'cost': {}, 'direct': False, 'rsdirect': False, 'f2early': False, 'order': [[7, 6, 5, 4, 3, 2, 1], [7, 6, 5, 4, 3, 2, 1]], 'deps': {'fx': ['A2'], 'F1': ['M'], 'F2': ['pair']}}
+CFG = {'a2a': [True, True], 'limit': 62914560, 'cost': {}, 'direct': False, 'rsdirect': False, 'f2early': False, 'order': [[7, 6, 5, 4, 3, 2, 1], [7, 6, 5, 4, 3, 2, 1]], 'deps': {'fx': ['A2'], 'F1': ['M'], 'F2': ['pair'], 'Z1': ['add']}}
 
 
 def iota(shape, dim):

time: 83.9 us -> 83.9 us (level)
  transfers between devices with their start and end apart: 14 -> 14, of which waited for: 6 -> 6; matrix products, arithmetic and copies ran while one was open for 0% -> 0% of each run, Pallas kernels for 25% -> 21%
where the time goes in v11:
time: 83.9 us; the launch traced here: 83.4 us
  waiting for transfers between devices  30.7 us (37%)
  Pallas kernels  24.8 us (30%)
  starting transfers between devices  18.5 us (22%)
  local copies, waits for them, and re-layouts  8.6 us (10%)
    pallas_call x11, Pallas kernels, call(): pl.pallas_call(body, name=name, out_shape=outs, in_specs=[pl.BlockSpec(me...  24.8 us
    ppermute x12, waiting for transfers between devices, swap(): return lax.ppermute(value, axis, [(p, p ^ step) for p in range(size)])  16.3 us
    all_to_all x1, waiting for transfers between devices, packed_shards(): lax.all_to_all(dep('H0', regrouped[0]), 'seq', 0, 0, tiled=True)  11.1 us
    unnamed x32, local copies, waits for them, and re-layouts  8.6 us
    ppermute x12, starting transfers between devices, swap(): return lax.ppermute(value, axis, [(p, p ^ step) for p in range(size)])  8.51 us
    all_to_all x1, starting transfers between devices, packed_shards(): lax.all_to_all(dep('h0', back[0]).reshape(seq, blocks, j_here, width), 's...  6.24 us
    all_to_all x1, starting transfers between devices, packed_shards(): lax.all_to_all(dep('H0', regrouped[0]), 'seq', 0, 0, tiled=True)  3.77 us
    all_to_all x1, waiting for transfers between devices, packed_shards(): lax.all_to_all(dep('h0', back[0]).reshape(seq, blocks, j_here, width), 's...  3.32 us
  transfers between devices with their start and end apart: 14, of which 6 were waited for; matrix products, arithmetic and copies ran while one was open for 0% of the time, Pallas kernels for 21%

profile of v11, /device:TPU:0, one launch (start us, length us, event | category | flops | bytes accessed | tf_op | source)
XLA Modules:
  0.0 83.4 jit_solution(1897280090185047897)
XLA Ops:
  0.6 0.0 copy-start.8
  0.6 0.8 copy-done.8
  1.5 0.4 pack_body.1.refs_0_
  1.9 2.4 %collective-permute-start.2 = (bf16[32,512]{1,0:T(8,128)(2,1)S(1)}, bf16[32,512]{1,0:T(8,128)(2,1)S(1)}, u32[]{:S(2)}, u32[]{:S(2)}) collective-permute-start(bf16[32,512]{1,0:T(8,128)(2,1)S(1)} %pack_body.1.refs_0_), channel_id=1, source_target_pairs={{0,3},{1,2},{2,1},{3,0},{4,7},{5,6},{6,5},{7,4},{8,11},{9,10},{10,... | collective-permute-start | bytes 98312 | tf_op jit(solution)/shard_map/ppermute | solution.py:50
  4.3 0.6 collective-permute-start.1
  5.0 0.0 collective-permute-start
  5.0 0.0 copy-start.9
  5.0 0.7 copy-done.9
  5.7 0.0 copy-start
  5.7 1.2 %copy-done = bf16[1,2048,256]{2,1,0:T(8,128)(2,1)S(1)} copy-done((bf16[1,2048,256]{2,1,0:T(8,128)(2,1)S(1)}, bf16[1,2048,256]{2,1,0:T(8,128)(2,1)}, u32[]{:S(2)}) %copy-start) | copy-done | bytes 1048600
  6.9 1.2 %copy-done.5 = bf16[1,2048,256]{2,1,0:T(8,128)(2,1)S(1)} copy-done((bf16[1,2048,256]{2,1,0:T(8,128)(2,1)S(1)}, bf16[1,2048,256]{2,1,0:T(8,128)(2,1)}, u32[]{:S(2)}) %copy-start.5) | copy-done | bytes 1048600
  8.1 0.5 gate_body.1.refs_4_.refs_1_
  8.6 0.0 collective-permute-done.2.refs_3_
  8.6 0.0 collective-permute-done.1.refs_2_
  8.7 0.0 collective-permute-done.refs_1_
  8.7 2.2 %regroup_back_body.1 = (bf16[32,64,256]{2,1,0:T(8,128)(2,1)}, bf16[4,32,512]{2,1,0:T(8,128)(2,1)S(1)}) custom-call(bf16[32,512]{1,0:T(8,128)(2,1)S(1)} %pack_body.1.refs_0_, bf16[32,512]{1,0:T(8,128)(2,1)S(1)} %collective-permute-done.refs_1_, bf16[32,512]{1,0:T(8,128)(2,1)S(1)} %collective-permute-done.1.refs_2_, ...), custom_call_target="tpu_custom_call" | custom-call | tf_op jit(solution)/shard_map/regroup_back_body/pallas_call | solution.py:31
  10.9 0.0 copy-start.12
  10.9 6.2 %all-to-all-start.1 = ((bf16[8,4,64,256]{3,2,1,0:T(8,128)(2,1)}), bf16[8,4,64,256]{3,2,1,0:T(8,128)(2,1)S(1)}, u32[]{:S(2)}, u32[]{:S(2)}) async-start(bf16[8,4,64,256]{3,2,1,0:T(8,128)(2,1)} %bitcast.6), calls=%async_computation.1 | async-start | bytes 2097152 | tf_op jit(solution)/shard_map/all_to_all | solution.py:337
  17.1 0.0 copy-done.12
  17.1 1.6 %collective-permute-start.4 = (bf16[4,128,512]{2,1,0:T(8,128)(2,1)S(1)}, bf16[4,128,512]{2,1,0:T(8,128)(2,1)S(1)}, u32[]{:S(2)}, u32[]{:S(2)}) collective-permute-start(bf16[4,128,512]{2,1,0:T(8,128)(2,1)S(1)} %copy-done.12), channel_id=1, source_target_pairs={{0,2},{1,3},{2,0},{3,1},{4,6},{5,7},{6,4},{7,5},{8,10},{9,11},{10,... | collective-permute-start | bytes 1572872 | tf_op jit(solution)/shard_map/ppermute | solution.py:50
  18.7 0.0 collective-permute-start.3
  18.7 12.3 %collective-permute-done.4.refs_2_ = bf16[4,128,512]{2,1,0:T(8,128)(2,1)S(1)} collective-permute-done((bf16[4,128,512]{2,1,0:T(8,128)(2,1)S(1)}, bf16[4,128,512]{2,1,0:T(8,128)(2,1)S(1)}, u32[]{:S(2)}, u32[]{:S(2)}) %collective-permute-start.4) | collective-permute-done | bytes 524320 | tf_op jit(solution)/shard_map/ppermute | solution.py:50
  31.0 0.0 collective-permute-start.5
  31.0 0.0 collective-permute-done.3.refs_1_
  31.0 0.0 copy-start.14
  31.0 1.9 %collective-permute-done.5.refs_3_ = bf16[4,128,512]{2,1,0:T(8,128)(2,1)S(1)} collective-permute-done((bf16[4,128,512]{2,1,0:T(8,128)(2,1)S(1)}, bf16[4,128,512]{2,1,0:T(8,128)(2,1)S(1)}, u32[]{:S(2)}, u32[]{:S(2)}) %collective-permute-start.5) | collective-permute-done | bytes 524320 | tf_op jit(solution)/shard_map/ppermute | solution.py:50
  32.9 0.0 copy-start.15
  32.9 0.8 copy-done.15
  33.7 0.0 copy-done.13
  33.7 0.0 copy-done.14
  33.7 6.2 %mix_body.1 = (bf16[8,4,64,256]{3,2,1,0:T(8,128)(2,1)}, bf16[2048,256]{1,0:T(8,128)(2,1)}) custom-call(bf16[4,128,512]{2,1,0:T(8,128)(2,1)} %refs_0_.3, bf16[4,128,512]{2,1,0:T(8,128)(2,1)} %copy-done.14, bf16[4,128,512]{2,1,0:T(8,128)(2,1)} %copy-done.13, bf16[4,128,512]{2,1,0:T(8,128)(2,1)} %copy-done.15, bf16[2048,256]{1,0:T(8,128)(2,1)} %bitcast.15, ...), custom_call_target="tpu_custom_call" | custom-call | tf_op jit(solution)/shard_map/mix_body/pallas_call | solution.py:31
  40.0 3.3 %all-to-all-done.1.refs_0_ = bf16[8,4,64,256]{3,2,1,0:T(8,128)(2,1)S(1)} async-done(((bf16[8,4,64,256]{3,2,1,0:T(8,128)(2,1)}), bf16[8,4,64,256]{3,2,1,0:T(8,128)(2,1)S(1)}, u32[]{:S(2)}, u32[]{:S(2)}) %all-to-all-start.1) | async-done | bytes 1048608 | tf_op jit(solution)/shard_map/all_to_all | solution.py:337
  43.3 0.0 copy-start.2
  43.3 1.0 %copy-done.2 = bf16[8,4,64,256]{3,2,1,0:T(8,128)(2,1)} copy-done((bf16[8,4,64,256]{3,2,1,0:T(8,128)(2,1)}, bf16[8,4,64,256]{3,2,1,0:T(8,128)(2,1)S(1)}, u32[]{:S(2)}) %copy-start.2) | copy-done | bytes 1048600
  44.2 3.8 %all-to-all-start = ((bf16[8,4,64,256]{3,2,1,0:T(8,128)(2,1)}), bf16[8,4,64,256]{3,2,1,0:T(8,128)(2,1)S(1)}, u32[]{:S(2)}, u32[]{:S(2)}) async-start(bf16[8,4,64,256]{3,2,1,0:T(8,128)(2,1)} %get-tuple-element.27), calls=%async_computation | async-start | bytes 2097152 | tf_op jit(solution)/shard_map/all_to_all | solution.py:362
  48.0 0.0 copy-done.1
  48.0 0.0 copy-done.11
  48.0 0.0 copy-start.3
  48.0 1.2 %copy-done.3 = bf16[8,4,64,256]{3,2,1,0:T(8,128)(2,1)S(1)} copy-done((bf16[8,4,64,256]{3,2,1,0:T(8,128)(2,1)S(1)}, bf16[8,4,64,256]{3,2,1,0:T(8,128)(2,1)}, u32[]{:S(2)}) %copy-start.3) | copy-done | bytes 1048600
  49.2 2.9 %first_grad_body.1 = (bf16[4,128,512]{2,1,0:T(8,128)(2,1)S(1)}, bf16[4,128,512]{2,1,0:T(8,128)(2,1)S(1)}, bf16[4,128,512]{2,1,0:T(8,128)(2,1)S(1)}, bf16[4,128,5...) custom-call(bf16[8,4,64,256]{3,2,1,0:T(8,128)(2,1)S(1)} %copy-done.3, bf16[2048,256]{1,0:T(8,128)(2,1)S(1)} %bitcast.17, ...), custom_call_target="tpu_custom_call" | custom-call | tf_op jit(solution)/shard_map/first_grad_body/pallas_call | solution.py:31
  52.2 0.0 copy-start.7
  52.2 0.9 %copy-done.7 = bf16[4,512,256]{2,1,0:T(8,128)(2,1)} copy-done((bf16[4,512,256]{2,1,0:T(8,128)(2,1)}, bf16[4,512,256]{2,1,0:T(8,128)(2,1)S(1)}, u32[]{:S(2)}) %copy-start.7) | copy-done | bytes 1048600
  53.2 0.0 collective-permute-start.6
  53.2 0.5 collective-permute-start.7
  53.7 1.4 %collective-permute-done.6.got_a = bf16[4,128,512]{2,1,0:T(8,128)(2,1)S(1)} collective-permute-done((bf16[4,128,512]{2,1,0:T(8,128)(2,1)S(1)}, bf16[4,128,512]{2,1,0:T(8,128)(2,1)S(1)}, u32[]{:S(2)}, u32[]{:S(2)}) %collective-permute-start.6) | collective-permute-done | bytes 524320 | tf_op jit(solution)/shard_map/ppermute | solution.py:50
  55.1 0.7 collective-permute-done.7.got_b
  55.8 1.0 %pair_body.1 = (f32[4,128,512]{2,1,0:T(8,128)S(1)}, bf16[4,128,512]{2,1,0:T(8,128)(2,1)}) custom-call(bf16[4,128,512]{2,1,0:T(8,128)(2,1)S(1)} %get-tuple-element.30.own_a, bf16[4,128,512]{2,1,0:T(8,128)(2,1)S(1)} %get-tuple-element.31.own_b, bf16[4,128,512]{2,1,0:T(8,128)(2,1)S(1)} %collective-permute-done.6.got_a, ...), custom_call_target="tpu_custom_call" | custom-call | tf_op jit(solution)/shard_map/pair_body/pallas_call | solution.py:31
  56.8 1.4 %collective-permute-start.8 = (bf16[4,128,512]{2,1,0:T(8,128)(2,1)}, bf16[4,128,512]{2,1,0:T(8,128)(2,1)}, u32[]{:S(2)}, u32[]{:S(2)}) collective-permute-start(bf16[4,128,512]{2,1,0:T(8,128)(2,1)} %get-tuple-element.34), channel_id=1, source_target_pairs={{0,2},{1,3},{2,0},{3,1},{4,6},{5,7},{6,4},{7,5},{8,10},{9,11},{10,... | collective-permute-start | bytes 1572872 | tf_op jit(solution)/shard_map/ppermute | solution.py:50
  58.2 4.7 %mix_back_body.1.back_ref = bf16[2048,256]{1,0:T(8,128)(2,1)} custom-call(bf16[4,128,512]{2,1,0:T(8,128)(2,1)} %refs_0_.3, bf16[4,128,512]{2,1,0:T(8,128)(2,1)} %copy-done.14, bf16[4,128,512]{2,1,0:T(8,128)(2,1)} %copy-done.13, bf16[4,128,512]{2,1,0:T(8,128)(2,1)} %copy-done.15, bf16[4,512,256]{2,1,0:T(8,128)(2,1)} %copy-done.7), custom_call_target="tpu_custom_call" | custom-call | tf_op jit(solution)/shard_map/mix_back_body/pallas_call | solution.py:31
  62.9 11.1 %all-to-all-done = bf16[8,4,64,256]{3,2,1,0:T(8,128)(2,1)S(1)} async-done(((bf16[8,4,64,256]{3,2,1,0:T(8,128)(2,1)}), bf16[8,4,64,256]{3,2,1,0:T(8,128)(2,1)S(1)}, u32[]{:S(2)}, u32[]{:S(2)}) %all-to-all-start) | async-done | bytes 1048608 | tf_op jit(solution)/shard_map/all_to_all | solution.py:362
  74.0 0.0 collective-permute-done.8.got
  74.0 1.9 %add_body.1 = bf16[4,128,512]{2,1,0:T(8,128)(2,1)} custom-call(f32[4,128,512]{2,1,0:T(8,128)S(1)} %get-tuple-element.37.own, bf16[4,128,512]{2,1,0:T(8,128)(2,1)} %collective-permute-done.8.got), custom_call_target="tpu_custom_call" | custom-call | tf_op jit(solution)/shard_map/add_body/pallas_call | solution.py:31
  75.9 1.3 %second_grad_body.1 = (bf16[32,512]{1,0:T(8,128)(2,1)S(1)}, bf16[32,512]{1,0:T(8,128)(2,1)S(1)}, bf16[32,512]{1,0:T(8,128)(2,1)S(1)}, bf16[32,512]{1,0:T(8,128)(2,1)S(1)}) custom-call(bf16[32,64,256]{2,1,0:T(8,128)(2,1)S(1)} %bitcast.13, bf16[2048,256]{1,0:T(8,128)(2,1)S(1)} %gate_body.1.refs_4_.refs_1_), custom_call_target="tpu_custom_call" | custom-call | tf_op jit(solution)/shard_map/second_grad_body/pallas_call | solution.py:31
  77.2 0.1 collective-permute-start.9
  77.3 1.5 %collective-permute-start.10 = (bf16[32,512]{1,0:T(8,128)(2,1)S(1)}, bf16[32,512]{1,0:T(8,128)(2,1)S(1)}, u32[]{:S(2)}, u32[]{:S(2)}) collective-permute-start(bf16[32,512]{1,0:T(8,128)(2,1)S(1)} %get-tuple-element.43), channel_id=1, source_target_pairs={{0,2},{1,3},{2,0},{3,1},{4,6},{5,7},{6,4},{7,5},{8,10},{9,11},{10,... | collective-permute-start | bytes 98312 | tf_op jit(solution)/shard_map/ppermute | solution.py:50
  78.8 0.4 collective-permute-start.11
  79.2 0.0 copy-done.4
  79.2 0.0 copy-done.6
  79.2 0.7 copy-done.10
  79.9 2.5 %tokens_body.1 = bf16[2048,256]{1,0:T(8,128)(2,1)} custom-call(bf16[32,64,256]{2,1,0:T(8,128)(2,1)S(1)} %bitcast.14, bf16[4,32,512]{2,1,0:T(8,128)(2,1)S(1)} %get-tuple-element.39.second_ref, bf16[2048,256]{1,0:T(8,128)(2,1)S(1)} %copy-done.6, s32[1,256]{1,0:T(1,128)S(1)} %bitcast.23, bf16[2048,256]{1,0:T(8,128)(2,1)S(1)} %copy-done.4), custom_call_target="tpu_custom_call" | custom-call | tf_op jit(solution)/shard_map/tokens_body/pallas_call | solution.py:31
  82.3 0.0 collective-permute-done.9.refs_1_
  82.3 0.0 collective-permute-done.10.refs_2_
  82.3 0.0 collective-permute-done.11.refs_3_
  82.4 1.1 %unpack_body.1 = bf16[256,64]{1,0:T(8,128)(2,1)} custom-call(bf16[32,512]{1,0:T(8,128)(2,1)S(1)} %get-tuple-element.41.refs_0_, bf16[32,512]{1,0:T(8,128)(2,1)S(1)} %collective-permute-done.9.refs_1_, bf16[32,512]{1,0:T(8,128)(2,1)S(1)} %collective-permute-done.10.refs_2_, bf16[32,512]{1,0:T(8,128)(2,1)S(1)} %collective-permute-done.11.refs_3_), custom_call_target="tpu_custom_call" | custom-call | tf_op jit(solution)/shard_map/unpack_body/pallas_call | solution.py:31
  (7 shorter events, 0.0 us)
Async XLA Ops:
  0.6 0.8 %copy-start.8 = (bf16[64,8,32]{0,2,1:T(8,128)(2,1)S(1)}, bf16[64,8,32]{0,2,1:T(8,128)(2,1)}, u32[]{:S(2)}) copy-start(bf16[64,8,32]{0,2,1:T(8,128)(2,1)} %param.9) | copy-start | bytes 98308
  1.9 6.7 %collective-permute-start.2 = (bf16[32,512]{1,0:T(8,128)(2,1)S(1)}, bf16[32,512]{1,0:T(8,128)(2,1)S(1)}, u32[]{:S(2)}, u32[]{:S(2)}) collective-permute-start(bf16[32,512]{1,0:T(8,128)(2,1)S(1)} %pack_body.1.refs_0_), channel_id=1, source_target_pairs={{0,3},{1,2},{2,1},{3,0},{4,7},{5,6},{6,5},{7,4},{8,11},{9,10},{10,... | collective-permute-start | bytes 98312 | tf_op jit(solution)/shard_map/ppermute | solution.py:50
  4.3 4.3 %collective-permute-start.1 = (bf16[32,512]{1,0:T(8,128)(2,1)S(1)}, bf16[32,512]{1,0:T(8,128)(2,1)S(1)}, u32[]{:S(2)}, u32[]{:S(2)}) collective-permute-start(bf16[32,512]{1,0:T(8,128)(2,1)S(1)} %pack_body.1.refs_0_), channel_id=1, source_target_pairs={{0,2},{1,3},{2,0},{3,1},{4,6},{5,7},{6,4},{7,5},{8,10},{9,11},{10,... | collective-permute-start | bytes 98312 | tf_op jit(solution)/shard_map/ppermute | solution.py:50
  5.0 3.7 %collective-permute-start = (bf16[32,512]{1,0:T(8,128)(2,1)S(1)}, bf16[32,512]{1,0:T(8,128)(2,1)S(1)}, u32[]{:S(2)}, u32[]{:S(2)}) collective-permute-start(bf16[32,512]{1,0:T(8,128)(2,1)S(1)} %pack_body.1.refs_0_), channel_id=1, source_target_pairs={{0,1},{1,0},{2,3},{3,2},{4,5},{5,4},{6,7},{7,6},{8,9},{9,8},{10,11... | collective-permute-start | bytes 98312 | tf_op jit(solution)/shard_map/ppermute | solution.py:50
  5.0 0.7 copy-start.9
  5.7 1.2 %copy-start = (bf16[1,2048,256]{2,1,0:T(8,128)(2,1)S(1)}, bf16[1,2048,256]{2,1,0:T(8,128)(2,1)}, u32[]{:S(2)}) copy-start(bf16[1,2048,256]{2,1,0:T(8,128)(2,1)} %param.6) | copy-start | bytes 3145732
  6.9 1.2 %copy-start.5 = (bf16[1,2048,256]{2,1,0:T(8,128)(2,1)S(1)}, bf16[1,2048,256]{2,1,0:T(8,128)(2,1)}, u32[]{:S(2)}) copy-start(bf16[1,2048,256]{2,1,0:T(8,128)(2,1)} %param.7) | copy-start | bytes 3145732
  10.9 6.3 %copy-start.12 = (bf16[4,128,512]{2,1,0:T(8,128)(2,1)S(1)}, bf16[4,128,512]{2,1,0:T(8,128)(2,1)}, u32[]{:S(2)}) copy-start(bf16[4,128,512]{2,1,0:T(8,128)(2,1)} %refs_0_.3) | copy-start | bytes 1572868
  10.9 32.4 %all-to-all-start.1 = ((bf16[8,4,64,256]{3,2,1,0:T(8,128)(2,1)}), bf16[8,4,64,256]{3,2,1,0:T(8,128)(2,1)S(1)}, u32[]{:S(2)}, u32[]{:S(2)}) async-start(bf16[8,4,64,256]{3,2,1,0:T(8,128)(2,1)} %bitcast.6), calls=%async_computation.1 | async-start | bytes 2097152 | tf_op jit(solution)/shard_map/all_to_all | solution.py:337
  17.1 13.8 %collective-permute-start.4 = (bf16[4,128,512]{2,1,0:T(8,128)(2,1)S(1)}, bf16[4,128,512]{2,1,0:T(8,128)(2,1)S(1)}, u32[]{:S(2)}, u32[]{:S(2)}) collective-permute-start(bf16[4,128,512]{2,1,0:T(8,128)(2,1)S(1)} %copy-done.12), channel_id=1, source_target_pairs={{0,2},{1,3},{2,0},{3,1},{4,6},{5,7},{6,4},{7,5},{8,10},{9,11},{10,... | collective-permute-start | bytes 1572872 | tf_op jit(solution)/shard_map/ppermute | solution.py:50
  18.7 12.3 %collective-permute-start.3 = (bf16[4,128,512]{2,1,0:T(8,128)(2,1)S(1)}, bf16[4,128,512]{2,1,0:T(8,128)(2,1)S(1)}, u32[]{:S(2)}, u32[]{:S(2)}) collective-permute-start(bf16[4,128,512]{2,1,0:T(8,128)(2,1)S(1)} %copy-done.12), channel_id=1, source_target_pairs={{0,1},{1,0},{2,3},{3,2},{4,5},{5,4},{6,7},{7,6},{8,9},{9,8},{10,11... | collective-permute-start | bytes 1572872 | tf_op jit(solution)/shard_map/ppermute | solution.py:50
  31.0 2.7 %copy-start.13 = (bf16[4,128,512]{2,1,0:T(8,128)(2,1)}, bf16[4,128,512]{2,1,0:T(8,128)(2,1)S(1)}, u32[]{:S(2)}) copy-start(bf16[4,128,512]{2,1,0:T(8,128)(2,1)S(1)} %collective-permute-done.4.refs_2_) | copy-start | bytes 1572868
  31.0 1.9 %collective-permute-start.5 = (bf16[4,128,512]{2,1,0:T(8,128)(2,1)S(1)}, bf16[4,128,512]{2,1,0:T(8,128)(2,1)S(1)}, u32[]{:S(2)}, u32[]{:S(2)}) collective-permute-start(bf16[4,128,512]{2,1,0:T(8,128)(2,1)S(1)} %collective-permute-done.4.refs_2_), channel_id=1, source_target_pairs={{0,1},{1,0},{2,3},{3,2},{4,5},{5,4},{6,7},{7,6},{8,9},{9,8},{10,11... | collective-permute-start | bytes 1572872 | tf_op jit(solution)/shard_map/ppermute | solution.py:50
  31.0 2.7 %copy-start.14 = (bf16[4,128,512]{2,1,0:T(8,128)(2,1)}, bf16[4,128,512]{2,1,0:T(8,128)(2,1)S(1)}, u32[]{:S(2)}) copy-start(bf16[4,128,512]{2,1,0:T(8,128)(2,1)S(1)} %collective-permute-done.3.refs_1_) | copy-start | bytes 1572868
  32.9 0.8 copy-start.15
  43.3 1.0 %copy-start.2 = (bf16[8,4,64,256]{3,2,1,0:T(8,128)(2,1)}, bf16[8,4,64,256]{3,2,1,0:T(8,128)(2,1)S(1)}, u32[]{:S(2)}) copy-start(bf16[8,4,64,256]{3,2,1,0:T(8,128)(2,1)S(1)} %all-to-all-done.1.refs_0_) | copy-start | bytes 3145732
  44.2 3.8 %copy-start.1 = (bf16[1,2048,256]{2,1,0:T(8,128)(2,1)S(1)}, bf16[1,2048,256]{2,1,0:T(8,128)(2,1)}, u32[]{:S(2)}) copy-start(bf16[1,2048,256]{2,1,0:T(8,128)(2,1)} %param.6) | copy-start | bytes 3145732
  44.2 3.8 %copy-start.11 = (s32[512]{0:T(512)S(1)}, s32[512]{0:T(512)}, u32[]{:S(2)}) copy-start(s32[512]{0:T(512)} %param.11) | copy-start | bytes 6148
  44.2 29.7 %all-to-all-start = ((bf16[8,4,64,256]{3,2,1,0:T(8,128)(2,1)}), bf16[8,4,64,256]{3,2,1,0:T(8,128)(2,1)S(1)}, u32[]{:S(2)}, u32[]{:S(2)}) async-start(bf16[8,4,64,256]{3,2,1,0:T(8,128)(2,1)} %get-tuple-element.27), calls=%async_computation | async-start | bytes 2097152 | tf_op jit(solution)/shard_map/all_to_all | solution.py:362
  48.0 1.2 %copy-start.3 = (bf16[8,4,64,256]{3,2,1,0:T(8,128)(2,1)S(1)}, bf16[8,4,64,256]{3,2,1,0:T(8,128)(2,1)}, u32[]{:S(2)}) copy-start(bf16[8,4,64,256]{3,2,1,0:T(8,128)(2,1)} %copy-done.2) | copy-start | bytes 3145732
  52.2 1.0 %copy-start.7 = (bf16[4,512,256]{2,1,0:T(8,128)(2,1)}, bf16[4,512,256]{2,1,0:T(8,128)(2,1)S(1)}, u32[]{:S(2)}) copy-start(bf16[4,512,256]{2,1,0:T(8,128)(2,1)S(1)} %get-tuple-element.35.refs_4_) | copy-start | bytes 3145732
  53.2 1.9 %collective-permute-start.6 = (bf16[4,128,512]{2,1,0:T(8,128)(2,1)S(1)}, bf16[4,128,512]{2,1,0:T(8,128)(2,1)S(1)}, u32[]{:S(2)}, u32[]{:S(2)}) collective-permute-start(bf16[4,128,512]{2,1,0:T(8,128)(2,1)S(1)} %get-tuple-element.32), channel_id=1, source_target_pairs={{0,1},{1,0},{2,3},{3,2},{4,5},{5,4},{6,7},{7,6},{8,9},{9,8},{10,11... | collective-permute-start | bytes 1572872 | tf_op jit(solution)/shard_map/ppermute | solution.py:50
  53.2 2.7 %collective-permute-start.7 = (bf16[4,128,512]{2,1,0:T(8,128)(2,1)S(1)}, bf16[4,128,512]{2,1,0:T(8,128)(2,1)S(1)}, u32[]{:S(2)}, u32[]{:S(2)}) collective-permute-start(bf16[4,128,512]{2,1,0:T(8,128)(2,1)S(1)} %get-tuple-element.33), channel_id=1, source_target_pairs={{0,1},{1,0},{2,3},{3,2},{4,5},{5,4},{6,7},{7,6},{8,9},{9,8},{10,11... | collective-permute-start | bytes 1572872 | tf_op jit(solution)/shard_map/ppermute | solution.py:50
  56.8 17.2 %collective-permute-start.8 = (bf16[4,128,512]{2,1,0:T(8,128)(2,1)}, bf16[4,128,512]{2,1,0:T(8,128)(2,1)}, u32[]{:S(2)}, u32[]{:S(2)}) collective-permute-start(bf16[4,128,512]{2,1,0:T(8,128)(2,1)} %get-tuple-element.34), channel_id=1, source_target_pairs={{0,2},{1,3},{2,0},{3,1},{4,6},{5,7},{6,4},{7,5},{8,10},{9,11},{10,... | collective-permute-start | bytes 1572872 | tf_op jit(solution)/shard_map/ppermute | solution.py:50
  75.9 3.3 %copy-start.4 = (bf16[2048,256]{1,0:T(8,128)(2,1)S(1)}, bf16[2048,256]{1,0:T(8,128)(2,1)}, u32[]{:S(2)}) copy-start(bf16[2048,256]{1,0:T(8,128)(2,1)} %mix_back_body.1.back_ref) | copy-start | bytes 3145732
  75.9 3.3 %copy-start.6 = (bf16[2048,256]{1,0:T(8,128)(2,1)S(1)}, bf16[2048,256]{1,0:T(8,128)(2,1)}, u32[]{:S(2)}) copy-start(bf16[2048,256]{1,0:T(8,128)(2,1)} %get-tuple-element.40.h_ref) | copy-start | bytes 3145732
  77.2 5.1 %collective-permute-start.9 = (bf16[32,512]{1,0:T(8,128)(2,1)S(1)}, bf16[32,512]{1,0:T(8,128)(2,1)S(1)}, u32[]{:S(2)}, u32[]{:S(2)}) collective-permute-start(bf16[32,512]{1,0:T(8,128)(2,1)S(1)} %get-tuple-element.42), channel_id=1, source_target_pairs={{0,1},{1,0},{2,3},{3,2},{4,5},{5,4},{6,7},{7,6},{8,9},{9,8},{10,11... | collective-permute-start | bytes 98312 | tf_op jit(solution)/shard_map/ppermute | solution.py:50
  77.3 5.0 %collective-permute-start.10 = (bf16[32,512]{1,0:T(8,128)(2,1)S(1)}, bf16[32,512]{1,0:T(8,128)(2,1)S(1)}, u32[]{:S(2)}, u32[]{:S(2)}) collective-permute-start(bf16[32,512]{1,0:T(8,128)(2,1)S(1)} %get-tuple-element.43), channel_id=1, source_target_pairs={{0,2},{1,3},{2,0},{3,1},{4,6},{5,7},{6,4},{7,5},{8,10},{9,11},{10,... | collective-permute-start | bytes 98312 | tf_op jit(solution)/shard_map/ppermute | solution.py:50
  78.8 3.6 %collective-permute-start.11 = (bf16[32,512]{1,0:T(8,128)(2,1)S(1)}, bf16[32,512]{1,0:T(8,128)(2,1)S(1)}, u32[]{:S(2)}, u32[]{:S(2)}) collective-permute-start(bf16[32,512]{1,0:T(8,128)(2,1)S(1)} %get-tuple-element.44), channel_id=1, source_target_pairs={{0,3},{1,2},{2,1},{3,0},{4,7},{5,6},{6,5},{7,4},{8,11},{9,10},{10,... | collective-permute-start | bytes 98312 | tf_op jit(solution)/shard_map/ppermute | solution.py:50
  79.2 0.7 copy-start.10

commit v12 on v8

--- a/solution.py
+++ b/solution.py
@@ -10,7 +10,7 @@
 BF16 = jnp.bfloat16
 F32 = jnp.float32
 LANE_GROUP = 16
-CFG = {'a2a': [False, False], 'cost': {}, 'direct': False, 'rsdirect': True, 'f2early': False, 'order': [[7, 6, 5, 4, 3, 2, 1], [7, 6, 5, 4, 3, 2, 1]], 'deps': {'h3': ['h7'], 'h2': ['h7'], 'h1': ['h7'], 'fx': ['h7', 'h4'], 'F1': ['M', 'H1', 'H2', 'H3', 'fx'], 'pair': ['F2'], 'H1': ['h3'], 'H2': ['M'], 'f2': ['A2'], 'rs1': ['H7', 'H6'], 'rs2': ['H7', 'H6'], 'rs3': ['H7', 'H6'], 'F2': ['rs1']}}
+CFG = {'cost': {}, 'direct': False, 'rsdirect': False, 'f2early': False, 'order': [[7, 6, 5, 4, 3, 2, 1], [3, 6, 7, 5, 4, 2, 1]], 'deps': {'h3': ['h7', 'D2'], 'h2': ['h7'], 'h1': ['h7'], 'fx': ['h7', 'h4'], 'F1': ['M', 'H1', 'H2', 'H3', 'fx', 'H6'], 'near': ['H7', 'H6'], 'far': ['h3', 'H3'], 'pair': ['F2'], 'H1': [], 'H2': ['M'], 'Z1': ['add'], 'H6': ['M']}, 'a2a': [False, False]}
 
 
 def iota(shape, dim):
@@ -25,7 +25,7 @@
     return lax.dot_general(a, b, (((da,), (db,)), ((), ())), preferred_element_type=F32)
 
 
-def call(body, outs, ins, scratch=(), spaces={}, limit=40 << 20, weight=0, out_space=pltpu.VMEM):
+def call(body, outs, ins, scratch=(), spaces={}, limit=40 << 20, weight=0, far_outs=()):
     name = getattr(body, "func", body).__name__
     weight = CFG['cost'].get(name, 0)
     return pl.pallas_call(
@@ -33,7 +33,9 @@
         name=name,
         out_shape=outs,
         in_specs=[pl.BlockSpec(memory_space=spaces.get(n, pltpu.VMEM)) for n in range(len(ins))],
-        out_specs=[pl.BlockSpec(memory_space=out_space)] * len(outs),
+        out_specs=[
+            pl.BlockSpec(memory_space=pltpu.HBM if n in far_outs else pltpu.VMEM) for n in range(len(outs))
+        ],
         scratch_shapes=list(scratch),
         compiler_params=pltpu.CompilerParams(vmem_limit_bytes=limit),
         cost_estimate=pl.CostEstimate(flops=0, bytes_accessed=weight, transcendentals=0),
@@ -222,11 +224,12 @@
         outs[d][...] = jnp.concatenate(rows, axis=0).astype(BF16)
 
 
-def tokens_body(reg_ref, second_ref, h_ref, src_ref, back_ref, out_ref):
+def tokens_body(reg_ref, second_ref, h_ref, src_ref, back_ref, out_hbm, out_ref, sems):
     order, j_here, width = reg_ref.shape
     groups, lanes = j_here // LANE_GROUP, order * LANE_GROUP
     select = one_hot(iota((width, width), 0) == src_ref[...])
     col = iota((order, lanes), 1) % LANE_GROUP
+    writes = []
     for g in range(groups):
         reg = reg_ref[:, g * LANE_GROUP : (g + 1) * LANE_GROUP, :].reshape(lanes, width)
         packed = second_ref[g].astype(F32)
@@ -236,6 +239,10 @@
         rows = slice(g * lanes, (g + 1) * lanes)
         dgate = (dot(weights, reg) * h_ref[rows, :].astype(F32)).astype(BF16)
         out_ref[rows, :] = (back_ref[rows, :].astype(F32) + dot(dgate, select, 1, 1)).astype(BF16)
+        writes.append(pltpu.make_async_copy(out_ref.at[rows, :], out_hbm.at[rows, :], sems.at[g]))
+        writes[g].start()
+    for write in writes:
+        write.wait()
 
 
 def pair_body(own_a, own_b, got_a, got_b, out_a, out_b):
@@ -384,7 +391,11 @@
         terms, gathered = [*terms, gathered], received[0]
     terms_got = [dep("unpack", terms[0])] + [move(f"R{d}", terms[d], "batch", d, batch) for d in (1, 2, 3)]
     (grad_tokens,) = call(
-        tokens_body, [of((rows_here, width))], [gathered, second, h, src, dmix_in]
+        tokens_body,
+        [of((rows_here, width))],
+        [gathered, second, h, src, dmix_in],
+        [pltpu.VMEM((rows_here, width), BF16), pltpu.SemaphoreType.DMA((groups,))],
+        far_outs=(0,),
     )
     (grad_flat,) = call(
         functools.partial(unpack_body, count), [of((m_here * count, j_here))], terms_got

time: 84.1 us -> 85.7 us (1.019); the launches traced: 83 us -> 85.4 us
  waiting for transfers between devices: 26.2 us -> 35.5 us
  starting transfers between devices: 35.9 us -> 28.8 us
    ppermute x26, waiting for transfers between devices: 26.2 us -> 35.5 us  [swap(): return lax.ppermute(value, axis, [(p, p ^ step) for p in range(size)])]
    ppermute x26, starting transfers between devices: 35.9 us -> 28.8 us  [swap(): return lax.ppermute(value, axis, [(p, p ^ step) for p in range(size)])]
    pallas_call x10 -> x11, Pallas kernels: 16 us -> 15.8 us  [call(): pl.pallas_call(body, name=name, out_shape=outs, in_specs=[pl.BlockSpec(me...]
  transfers between devices with their start and end apart: 26 -> 26, of which waited for: 7 -> 12; matrix products, arithmetic and copies ran while one was open for 0% -> 0% of each run, Pallas kernels for 16% -> 15%
where the time goes in v12:
time: 85.7 us; the launch traced here: 85.4 us
  waiting for transfers between devices  35.5 us (41%)
  starting transfers between devices  28.8 us (34%)
  Pallas kernels  15.8 us (18%)
  local copies, waits for them, and re-layouts  4.48 us (5%)
    ppermute x26, waiting for transfers between devices, swap(): return lax.ppermute(value, axis, [(p, p ^ step) for p in range(size)])  35.5 us
    ppermute x26, starting transfers between devices, swap(): return lax.ppermute(value, axis, [(p, p ^ step) for p in range(size)])  28.8 us
    pallas_call x11, Pallas kernels, call(): pl.pallas_call(body, name=name, out_shape=outs, in_specs=[pl.BlockSpec(me...  15.8 us
    unnamed x16, local copies, waits for them, and re-layouts  4.48 us
  transfers between devices with their start and end apart: 26, of which 12 were waited for; matrix products, arithmetic and copies ran while one was open for 0% of the time, Pallas kernels for 15%

profile of v12, /device:TPU:0, one launch (start us, length us, event | category | flops | bytes accessed | tf_op | source)
XLA Modules:
  0.0 85.4 jit_solution(15729540072224970782)
XLA Ops:
  0.6 0.8 copy-done.5
  1.5 0.4 pack_body.1.refs_0_
  1.9 3.0 %collective-permute-start.1 = (bf16[32,512]{1,0:T(8,128)(2,1)S(1)}, bf16[32,512]{1,0:T(8,128)(2,1)S(1)}, u32[]{:S(2)}, u32[]{:S(2)}) collective-permute-start(bf16[32,512]{1,0:T(8,128)(2,1)S(1)} %pack_body.1.refs_0_), channel_id=1, source_target_pairs={{0,2},{1,3},{2,0},{3,1},{4,6},{5,7},{6,4},{7,5},{8,10},{9,11},{10,... | collective-permute-start | bytes 98312 | tf_op jit(solution)/shard_map/ppermute | solution.py:50
  4.9 0.0 collective-permute-start
  4.9 0.2 collective-permute-start.2
  5.1 0.7 copy-done.6
  5.8 1.2 %copy-done = bf16[1,2048,256]{2,1,0:T(8,128)(2,1)S(1)} copy-done((bf16[1,2048,256]{2,1,0:T(8,128)(2,1)S(1)}, bf16[1,2048,256]{2,1,0:T(8,128)(2,1)}, u32[]{:S(2)}) %copy-start) | copy-done | bytes 1048600
  7.0 1.2 %copy-done.2 = bf16[1,2048,256]{2,1,0:T(8,128)(2,1)S(1)} copy-done((bf16[1,2048,256]{2,1,0:T(8,128)(2,1)S(1)}, bf16[1,2048,256]{2,1,0:T(8,128)(2,1)}, u32[]{:S(2)}) %copy-start.2) | copy-done | bytes 1048600
  8.2 0.5 gate_body.1.refs_4_.refs_8_
  8.7 0.0 copy-start.1
  8.7 0.0 collective-permute-done.1.refs_2_
  8.7 0.0 collective-permute-done.refs_1_
  8.8 0.0 collective-permute-done.2.refs_3_
  8.8 0.5 copy-done.4
  9.3 1.9 %collective-permute-start.4 = (bf16[4,128,512]{2,1,0:T(8,128)(2,1)S(1)}, bf16[4,128,512]{2,1,0:T(8,128)(2,1)S(1)}, u32[]{:S(2)}, u32[]{:S(2)}) collective-permute-start(bf16[4,128,512]{2,1,0:T(8,128)(2,1)S(1)} %copy-done.4), channel_id=1, source_target_pairs={{0,2},{1,3},{2,0},{3,1},{4,6},{5,7},{6,4},{7,5},{8,10},{9,11},{10,... | collective-permute-start | bytes 1572872 | tf_op jit(solution)/shard_map/ppermute | solution.py:50
  11.2 1.5 %regroup_back_body.1 = (bf16[4,64,256]{2,1,0:T(8,128)(2,1)S(1)}, bf16[4,64,256]{2,1,0:T(8,128)(2,1)S(1)}, bf16[4,64,256]{2,1,0:T(8,128)(2,1)S(1)}, bf16[4,64,256...) custom-call(bf16[32,512]{1,0:T(8,128)(2,1)S(1)} %pack_body.1.refs_0_, ...), custom_call_target="tpu_custom_call" | custom-call | tf_op jit(solution)/shard_map/regroup_back_body/pallas_call | solution.py:31
  12.7 4.6 %collective-permute-start.5 = (bf16[4,64,256]{2,1,0:T(8,128)(2,1)S(1)}, bf16[4,64,256]{2,1,0:T(8,128)(2,1)S(1)}, u32[]{:S(2)}, u32[]{:S(2)}) collective-permute-start(bf16[4,64,256]{2,1,0:T(8,128)(2,1)S(1)} %get-tuple-element.47), channel_id=1, source_target_pairs={{0,28},{4,24},{8,20},{12,16},{16,12},{20,8},{24,4},{28,0},{1,29},{... | collective-permute-start | bytes 393224 | tf_op jit(solution)/shard_map/ppermute | solution.py:50
  17.3 0.0 collective-permute-start.6
  17.3 0.0 collective-permute-start.3
  17.3 4.6 %collective-permute-done.5.refs_7_ = bf16[4,64,256]{2,1,0:T(8,128)(2,1)S(1)} collective-permute-done((bf16[4,64,256]{2,1,0:T(8,128)(2,1)S(1)}, bf16[4,64,256]{2,1,0:T(8,128)(2,1)S(1)}, u32[]{:S(2)}, u32[]{:S(2)}) %collective-permute-start.5) | collective-permute-done | bytes 131104 | tf_op jit(solution)/shard_map/ppermute | solution.py:50
  21.9 6.4 %collective-permute-done.6.refs_4_ = bf16[4,64,256]{2,1,0:T(8,128)(2,1)S(1)} collective-permute-done((bf16[4,64,256]{2,1,0:T(8,128)(2,1)S(1)}, bf16[4,64,256]{2,1,0:T(8,128)(2,1)S(1)}, u32[]{:S(2)}, u32[]{:S(2)}) %collective-permute-start.6) | collective-permute-done | bytes 131104 | tf_op jit(solution)/shard_map/ppermute | solution.py:50
  28.3 0.0 collective-permute-done.4.refs_2_
  28.3 0.0 collective-permute-start.7
  28.3 1.0 %collective-permute-start.15 = (bf16[4,64,256]{2,1,0:T(8,128)(2,1)S(1)}, bf16[4,64,256]{2,1,0:T(8,128)(2,1)S(1)}, u32[]{:S(2)}, u32[]{:S(2)}) collective-permute-start(bf16[4,64,256]{2,1,0:T(8,128)(2,1)S(1)} %get-tuple-element.65), channel_id=1, source_target_pairs={{0,20},{4,16},{8,28},{12,24},{16,4},{20,0},{24,12},{28,8},{1,21},{... | collective-permute-start | bytes 393224 | tf_op jit(solution)/shard_map/ppermute | solution.py:50
  29.3 0.0 collective-permute-done.3.refs_1_
  29.3 0.9 %collective-permute-done.7.refs_3_ = bf16[4,128,512]{2,1,0:T(8,128)(2,1)S(1)} collective-permute-done((bf16[4,128,512]{2,1,0:T(8,128)(2,1)S(1)}, bf16[4,128,512]{2,1,0:T(8,128)(2,1)S(1)}, u32[]{:S(2)}, u32[]{:S(2)}) %collective-permute-start.7) | collective-permute-done | bytes 524320 | tf_op jit(solution)/shard_map/ppermute | solution.py:50
  30.2 2.5 %mix_body.1 = (bf16[4,64,256]{2,1,0:T(8,128)(2,1)S(1)}, bf16[4,64,256]{2,1,0:T(8,128)(2,1)S(1)}, bf16[4,64,256]{2,1,0:T(8,128)(2,1)S(1)}, bf16[4,64,256]{2,1,0:T...) custom-call(bf16[4,128,512]{2,1,0:T(8,128)(2,1)S(1)} %copy-done.4, ...), custom_call_target="tpu_custom_call" | custom-call | tf_op jit(solution)/shard_map/mix_body/pallas_call | solution.py:31
  32.7 2.5 %collective-permute-start.11 = (bf16[4,64,256]{2,1,0:T(8,128)(2,1)S(1)}, bf16[4,64,256]{2,1,0:T(8,128)(2,1)S(1)}, u32[]{:S(2)}, u32[]{:S(2)}) collective-permute-start(bf16[4,64,256]{2,1,0:T(8,128)(2,1)S(1)} %get-tuple-element.57), channel_id=1, source_target_pairs={{0,24},{4,28},{8,16},{12,20},{16,8},{20,12},{24,0},{28,4},{1,25},{... | collective-permute-start | bytes 393224 | tf_op jit(solution)/shard_map/ppermute | solution.py:50
  35.2 0.0 collective-permute-start.9
  35.2 2.0 %collective-permute-start.10 = (bf16[4,64,256]{2,1,0:T(8,128)(2,1)S(1)}, bf16[4,64,256]{2,1,0:T(8,128)(2,1)S(1)}, u32[]{:S(2)}, u32[]{:S(2)}) collective-permute-start(bf16[4,64,256]{2,1,0:T(8,128)(2,1)S(1)} %get-tuple-element.55), channel_id=1, source_target_pairs={{0,12},{4,8},{8,4},{12,0},{16,28},{20,24},{24,20},{28,16},{1,13},{... | collective-permute-start | bytes 393224 | tf_op jit(solution)/shard_map/ppermute | solution.py:50
  37.2 1.5 %collective-permute-start.8 = (bf16[4,64,256]{2,1,0:T(8,128)(2,1)S(1)}, bf16[4,64,256]{2,1,0:T(8,128)(2,1)S(1)}, u32[]{:S(2)}, u32[]{:S(2)}) collective-permute-start(bf16[4,64,256]{2,1,0:T(8,128)(2,1)S(1)} %get-tuple-element.52), channel_id=1, source_target_pairs={{0,4},{4,0},{8,12},{12,8},{16,20},{20,16},{24,28},{28,24},{1,5},{5... | collective-permute-start | bytes 393224 | tf_op jit(solution)/shard_map/ppermute | solution.py:50
  38.7 2.0 %collective-permute-done.15.refs_5_ = bf16[4,64,256]{2,1,0:T(8,128)(2,1)S(1)} collective-permute-done((bf16[4,64,256]{2,1,0:T(8,128)(2,1)S(1)}, bf16[4,64,256]{2,1,0:T(8,128)(2,1)S(1)}, u32[]{:S(2)}, u32[]{:S(2)}) %collective-permute-start.15) | collective-permute-done | bytes 131104 | tf_op jit(solution)/shard_map/ppermute | solution.py:50
  40.7 0.0 collective-permute-start.16
  40.7 0.2 collective-permute-done.11.refs_6_
  41.0 3.2 %collective-permute-start.14 = (bf16[4,64,256]{2,1,0:T(8,128)(2,1)S(1)}, bf16[4,64,256]{2,1,0:T(8,128)(2,1)S(1)}, u32[]{:S(2)}, u32[]{:S(2)}) collective-permute-start(bf16[4,64,256]{2,1,0:T(8,128)(2,1)S(1)} %get-tuple-element.64), channel_id=1, source_target_pairs={{0,12},{4,8},{8,4},{12,0},{16,28},{20,24},{24,20},{28,16},{1,13},{... | collective-permute-start | bytes 393224 | tf_op jit(solution)/shard_map/ppermute | solution.py:50
  44.2 0.0 collective-permute-done.9.refs_2_
  44.2 1.3 %collective-permute-start.12 = (bf16[4,64,256]{2,1,0:T(8,128)(2,1)S(1)}, bf16[4,64,256]{2,1,0:T(8,128)(2,1)S(1)}, u32[]{:S(2)}, u32[]{:S(2)}) collective-permute-start(bf16[4,64,256]{2,1,0:T(8,128)(2,1)S(1)} %get-tuple-element.60), channel_id=1, source_target_pairs={{0,4},{4,0},{8,12},{12,8},{16,20},{20,16},{24,28},{28,24},{1,5},{5... | collective-permute-start | bytes 393224 | tf_op jit(solution)/shard_map/ppermute | solution.py:50
  45.5 3.5 %collective-permute-done.10.refs_3_ = bf16[4,64,256]{2,1,0:T(8,128)(2,1)S(1)} collective-permute-done((bf16[4,64,256]{2,1,0:T(8,128)(2,1)S(1)}, bf16[4,64,256]{2,1,0:T(8,128)(2,1)S(1)}, u32[]{:S(2)}, u32[]{:S(2)}) %collective-permute-start.10) | collective-permute-done | bytes 131104 | tf_op jit(solution)/shard_map/ppermute | solution.py:50
  49.0 0.0 collective-permute-start.13
  49.0 0.0 collective-permute-done.8.refs_1_
  49.0 1.1 %collective-permute-start.17 = (bf16[4,64,256]{2,1,0:T(8,128)(2,1)S(1)}, bf16[4,64,256]{2,1,0:T(8,128)(2,1)S(1)}, u32[]{:S(2)}, u32[]{:S(2)}) collective-permute-start(bf16[4,64,256]{2,1,0:T(8,128)(2,1)S(1)} %get-tuple-element.73), channel_id=1, source_target_pairs={{0,28},{4,24},{8,20},{12,16},{16,12},{20,8},{24,4},{28,0},{1,29},{... | collective-permute-start | bytes 393224 | tf_op jit(solution)/shard_map/ppermute | solution.py:50
  50.2 1.9 %collective-permute-done.14.refs_3_ = bf16[4,64,256]{2,1,0:T(8,128)(2,1)S(1)} collective-permute-done((bf16[4,64,256]{2,1,0:T(8,128)(2,1)S(1)}, bf16[4,64,256]{2,1,0:T(8,128)(2,1)S(1)}, u32[]{:S(2)}, u32[]{:S(2)}) %collective-permute-start.14) | collective-permute-done | bytes 131104 | tf_op jit(solution)/shard_map/ppermute | solution.py:50
  52.1 0.6 collective-permute-done.12.refs_1_
  52.7 4.8 %collective-permute-done.13.refs_2_ = bf16[4,64,256]{2,1,0:T(8,128)(2,1)S(1)} collective-permute-done((bf16[4,64,256]{2,1,0:T(8,128)(2,1)S(1)}, bf16[4,64,256]{2,1,0:T(8,128)(2,1)S(1)}, u32[]{:S(2)}, u32[]{:S(2)}) %collective-permute-start.13) | collective-permute-done | bytes 131104 | tf_op jit(solution)/shard_map/ppermute | solution.py:50
  57.5 3.0 %first_grad_body.1 = (bf16[4,128,512]{2,1,0:T(8,128)(2,1)S(1)}, bf16[4,128,512]{2,1,0:T(8,128)(2,1)S(1)}, bf16[4,128,512]{2,1,0:T(8,128)(2,1)S(1)}, bf16[4,128,5...) custom-call(bf16[4,64,256]{2,1,0:T(8,128)(2,1)S(1)} %get-tuple-element.58.refs_0_, ...), custom_call_target="tpu_custom_call" | custom-call | tf_op jit(solution)/shard_map/first_grad_body/pallas_call | solution.py:31
  60.5 0.1 collective-permute-start.19
  60.6 0.0 collective-permute-done.17.refs_7_
  60.6 0.5 collective-permute-start.18
  61.1 1.9 %mix_back_body.1.back_ref = bf16[2048,256]{1,0:T(8,128)(2,1)S(1)} custom-call(bf16[4,128,512]{2,1,0:T(8,128)(2,1)S(1)} %copy-done.4, bf16[4,128,512]{2,1,0:T(8,128)(2,1)S(1)} %collective-permute-done.3.refs_1_, bf16[4,128,512]{2,1,0:T(8,128)(2,1)S(1)} %collective-permute-done.4.refs_2_, bf16[4,128,512]{2,1,0:T(8,128)(2,1)S(1)} %collective-permute-done.7.refs_3_, ...), custom_call_target="tpu_custom_call" | custom-call | tf_op jit(solution)/shard_map/mix_back_body/pallas_call | solution.py:31
  62.9 0.0 collective-permute-done.19.got_b
  63.0 0.3 collective-permute-done.18.got_a
  63.2 0.2 pair_body.1
  63.5 0.6 collective-permute-start.20
  64.1 3.2 %collective-permute-start.22 = (bf16[4,64,256]{2,1,0:T(8,128)(2,1)S(1)}, bf16[4,64,256]{2,1,0:T(8,128)(2,1)S(1)}, u32[]{:S(2)}, u32[]{:S(2)}) collective-permute-start(bf16[4,64,256]{2,1,0:T(8,128)(2,1)S(1)} %get-tuple-element.81), channel_id=1, source_target_pairs={{0,20},{4,16},{8,28},{12,24},{16,4},{20,0},{24,12},{28,8},{1,21},{... | collective-permute-start | bytes 393224 | tf_op jit(solution)/shard_map/ppermute | solution.py:50
  67.3 10.2 %collective-permute-done.20.got = bf16[4,128,512]{2,1,0:T(8,128)(2,1)S(1)} collective-permute-done((bf16[4,128,512]{2,1,0:T(8,128)(2,1)S(1)}, bf16[4,128,512]{2,1,0:T(8,128)(2,1)S(1)}, u32[]{:S(2)}, u32[]{:S(2)}) %collective-permute-start.20) | collective-permute-done | bytes 524320 | tf_op jit(solution)/shard_map/ppermute | solution.py:50
  77.5 0.9 %add_body.1 = bf16[4,128,512]{2,1,0:T(8,128)(2,1)} custom-call(f32[4,128,512]{2,1,0:T(8,128)S(1)} %get-tuple-element.77.own, bf16[4,128,512]{2,1,0:T(8,128)(2,1)S(1)} %collective-permute-done.20.got), custom_call_target="tpu_custom_call" | custom-call | tf_op jit(solution)/shard_map/add_body/pallas_call | solution.py:31
  78.4 1.4 %second_grad_body.1 = (bf16[32,512]{1,0:T(8,128)(2,1)S(1)}, bf16[32,512]{1,0:T(8,128)(2,1)S(1)}, bf16[32,512]{1,0:T(8,128)(2,1)S(1)}, bf16[32,512]{1,0:T(8,128)(2,1)S(1)}, bf16[32,64,256]{2,1,0:T(8,128)(2,1)S(1)}) custom-call(bf16[4,64,256]{2,1,0:T(8,128)(2,1)S(1)} %get-tuple-element.79.refs_0_, bf16[4,64,256]{2,1,0:T(8,128)(2,1)S(1)} %collective-permute-done.8.refs_1_, ...), custom_call_target="tpu_custom_call" | custom-call | tf_op jit(solution)/shard_map/second_grad_body/pallas_call | solution.py:31
  79.8 0.1 collective-permute-start.23
  79.9 1.1 %collective-permute-start.24 = (bf16[32,512]{1,0:T(8,128)(2,1)S(1)}, bf16[32,512]{1,0:T(8,128)(2,1)S(1)}, u32[]{:S(2)}, u32[]{:S(2)}) collective-permute-start(bf16[32,512]{1,0:T(8,128)(2,1)S(1)} %get-tuple-element.87), channel_id=1, source_target_pairs={{0,2},{1,3},{2,0},{3,1},{4,6},{5,7},{6,4},{7,5},{8,10},{9,11},{10,... | collective-permute-start | bytes 98312 | tf_op jit(solution)/shard_map/ppermute | solution.py:50
  81.0 0.7 collective-permute-start.25
  81.7 2.5 %tokens_body.1 = bf16[2048,256]{1,0:T(8,128)(2,1)} custom-call(bf16[32,64,256]{2,1,0:T(8,128)(2,1)S(1)} %get-tuple-element.82.reg_ref, bf16[4,32,512]{2,1,0:T(8,128)(2,1)S(1)} %get-tuple-element.83.second_ref, bf16[2048,256]{1,0:T(8,128)(2,1)S(1)} %get-tuple-element.84.h_ref, s32[1,256]{1,0:T(1,128)S(1)} %bitcast.19, bf16[2048,256]{1,0:T(8,128)(2,1)S(1)} %mix_back_body.1.back_ref), custom_call_target="tpu_custom_call" | custom-call | tf_op jit(solution)/shard_map/tokens_body/pallas_call | solution.py:31
  84.2 0.0 collective-permute-done.23.refs_1_
  84.2 0.1 collective-permute-done.25.refs_3_
  84.4 1.1 %unpack_body.1 = bf16[256,64]{1,0:T(8,128)(2,1)} custom-call(bf16[32,512]{1,0:T(8,128)(2,1)S(1)} %get-tuple-element.85.refs_0_, bf16[32,512]{1,0:T(8,128)(2,1)S(1)} %collective-permute-done.23.refs_1_, bf16[32,512]{1,0:T(8,128)(2,1)S(1)} %collective-permute-done.24.refs_2_, bf16[32,512]{1,0:T(8,128)(2,1)S(1)} %collective-permute-done.25.refs_3_), custom_call_target="tpu_custom_call" | custom-call | tf_op jit(solution)/shard_map/unpack_body/pallas_call | solution.py:31
  (15 shorter events, 0.0 us)
Async XLA Ops:
  0.6 0.8 copy-start.5
  1.9 6.8 %collective-permute-start.1 = (bf16[32,512]{1,0:T(8,128)(2,1)S(1)}, bf16[32,512]{1,0:T(8,128)(2,1)S(1)}, u32[]{:S(2)}, u32[]{:S(2)}) collective-permute-start(bf16[32,512]{1,0:T(8,128)(2,1)S(1)} %pack_body.1.refs_0_), channel_id=1, source_target_pairs={{0,2},{1,3},{2,0},{3,1},{4,6},{5,7},{6,4},{7,5},{8,10},{9,11},{10,... | collective-permute-start | bytes 98312 | tf_op jit(solution)/shard_map/ppermute | solution.py:50
  4.9 3.9 %collective-permute-start = (bf16[32,512]{1,0:T(8,128)(2,1)S(1)}, bf16[32,512]{1,0:T(8,128)(2,1)S(1)}, u32[]{:S(2)}, u32[]{:S(2)}) collective-permute-start(bf16[32,512]{1,0:T(8,128)(2,1)S(1)} %pack_body.1.refs_0_), channel_id=1, source_target_pairs={{0,1},{1,0},{2,3},{3,2},{4,5},{5,4},{6,7},{7,6},{8,9},{9,8},{10,11... | collective-permute-start | bytes 98312 | tf_op jit(solution)/shard_map/ppermute | solution.py:50
  4.9 3.9 %collective-permute-start.2 = (bf16[32,512]{1,0:T(8,128)(2,1)S(1)}, bf16[32,512]{1,0:T(8,128)(2,1)S(1)}, u32[]{:S(2)}, u32[]{:S(2)}) collective-permute-start(bf16[32,512]{1,0:T(8,128)(2,1)S(1)} %pack_body.1.refs_0_), channel_id=1, source_target_pairs={{0,3},{1,2},{2,1},{3,0},{4,7},{5,6},{6,5},{7,4},{8,11},{9,10},{10,... | collective-permute-start | bytes 98312 | tf_op jit(solution)/shard_map/ppermute | solution.py:50
  5.1 0.7 copy-start.6
  5.8 1.2 %copy-start = (bf16[1,2048,256]{2,1,0:T(8,128)(2,1)S(1)}, bf16[1,2048,256]{2,1,0:T(8,128)(2,1)}, u32[]{:S(2)}) copy-start(bf16[1,2048,256]{2,1,0:T(8,128)(2,1)} %param.6) | copy-start | bytes 3145732
  7.0 1.2 %copy-start.2 = (bf16[1,2048,256]{2,1,0:T(8,128)(2,1)S(1)}, bf16[1,2048,256]{2,1,0:T(8,128)(2,1)}, u32[]{:S(2)}) copy-start(bf16[1,2048,256]{2,1,0:T(8,128)(2,1)} %param.7) | copy-start | bytes 3145732
  8.2 1.0 %copy-start.4 = (bf16[4,128,512]{2,1,0:T(8,128)(2,1)S(1)}, bf16[4,128,512]{2,1,0:T(8,128)(2,1)}, u32[]{:S(2)}) copy-start(bf16[4,128,512]{2,1,0:T(8,128)(2,1)} %refs_0_.3) | copy-start | bytes 1572868
  8.2 22.0 %copy-start.3 = (bf16[1,2048,256]{2,1,0:T(8,128)(2,1)S(1)}, bf16[1,2048,256]{2,1,0:T(8,128)(2,1)}, u32[]{:S(2)}) copy-start(bf16[1,2048,256]{2,1,0:T(8,128)(2,1)} %param.7) | copy-start | bytes 3145732
  8.7 21.5 %copy-start.1 = (bf16[1,2048,256]{2,1,0:T(8,128)(2,1)S(1)}, bf16[1,2048,256]{2,1,0:T(8,128)(2,1)}, u32[]{:S(2)}) copy-start(bf16[1,2048,256]{2,1,0:T(8,128)(2,1)} %param.6) | copy-start | bytes 3145732
  9.3 19.0 %collective-permute-start.4 = (bf16[4,128,512]{2,1,0:T(8,128)(2,1)S(1)}, bf16[4,128,512]{2,1,0:T(8,128)(2,1)S(1)}, u32[]{:S(2)}, u32[]{:S(2)}) collective-permute-start(bf16[4,128,512]{2,1,0:T(8,128)(2,1)S(1)} %copy-done.4), channel_id=1, source_target_pairs={{0,2},{1,3},{2,0},{3,1},{4,6},{5,7},{6,4},{7,5},{8,10},{9,11},{10,... | collective-permute-start | bytes 1572872 | tf_op jit(solution)/shard_map/ppermute | solution.py:50
  12.7 9.2 %collective-permute-start.5 = (bf16[4,64,256]{2,1,0:T(8,128)(2,1)S(1)}, bf16[4,64,256]{2,1,0:T(8,128)(2,1)S(1)}, u32[]{:S(2)}, u32[]{:S(2)}) collective-permute-start(bf16[4,64,256]{2,1,0:T(8,128)(2,1)S(1)} %get-tuple-element.47), channel_id=1, source_target_pairs={{0,28},{4,24},{8,20},{12,16},{16,12},{20,8},{24,4},{28,0},{1,29},{... | collective-permute-start | bytes 393224 | tf_op jit(solution)/shard_map/ppermute | solution.py:50
  17.3 12.9 %copy-start.7 = (s32[512]{0:T(512)S(1)}, s32[512]{0:T(512)}, u32[]{:S(2)}) copy-start(s32[512]{0:T(512)} %param.11) | copy-start | bytes 6148
  17.3 11.0 %collective-permute-start.6 = (bf16[4,64,256]{2,1,0:T(8,128)(2,1)S(1)}, bf16[4,64,256]{2,1,0:T(8,128)(2,1)S(1)}, u32[]{:S(2)}, u32[]{:S(2)}) collective-permute-start(bf16[4,64,256]{2,1,0:T(8,128)(2,1)S(1)} %get-tuple-element.48), channel_id=1, source_target_pairs={{0,16},{4,20},{8,24},{12,28},{16,0},{20,4},{24,8},{28,12},{1,17},{... | collective-permute-start | bytes 393224 | tf_op jit(solution)/shard_map/ppermute | solution.py:50
  17.3 12.0 %collective-permute-start.3 = (bf16[4,128,512]{2,1,0:T(8,128)(2,1)S(1)}, bf16[4,128,512]{2,1,0:T(8,128)(2,1)S(1)}, u32[]{:S(2)}, u32[]{:S(2)}) collective-permute-start(bf16[4,128,512]{2,1,0:T(8,128)(2,1)S(1)} %copy-done.4), channel_id=1, source_target_pairs={{0,1},{1,0},{2,3},{3,2},{4,5},{5,4},{6,7},{7,6},{8,9},{9,8},{10,11... | collective-permute-start | bytes 1572872 | tf_op jit(solution)/shard_map/ppermute | solution.py:50
  28.3 1.9 %collective-permute-start.7 = (bf16[4,128,512]{2,1,0:T(8,128)(2,1)S(1)}, bf16[4,128,512]{2,1,0:T(8,128)(2,1)S(1)}, u32[]{:S(2)}, u32[]{:S(2)}) collective-permute-start(bf16[4,128,512]{2,1,0:T(8,128)(2,1)S(1)} %collective-permute-done.4.refs_2_), channel_id=1, source_target_pairs={{0,1},{1,0},{2,3},{3,2},{4,5},{5,4},{6,7},{7,6},{8,9},{9,8},{10,11... | collective-permute-start | bytes 1572872 | tf_op jit(solution)/shard_map/ppermute | solution.py:50
  28.3 12.4 %collective-permute-start.15 = (bf16[4,64,256]{2,1,0:T(8,128)(2,1)S(1)}, bf16[4,64,256]{2,1,0:T(8,128)(2,1)S(1)}, u32[]{:S(2)}, u32[]{:S(2)}) collective-permute-start(bf16[4,64,256]{2,1,0:T(8,128)(2,1)S(1)} %get-tuple-element.65), channel_id=1, source_target_pairs={{0,20},{4,16},{8,28},{12,24},{16,4},{20,0},{24,12},{28,8},{1,21},{... | collective-permute-start | bytes 393224 | tf_op jit(solution)/shard_map/ppermute | solution.py:50
  32.7 8.3 %collective-permute-start.11 = (bf16[4,64,256]{2,1,0:T(8,128)(2,1)S(1)}, bf16[4,64,256]{2,1,0:T(8,128)(2,1)S(1)}, u32[]{:S(2)}, u32[]{:S(2)}) collective-permute-start(bf16[4,64,256]{2,1,0:T(8,128)(2,1)S(1)} %get-tuple-element.57), channel_id=1, source_target_pairs={{0,24},{4,28},{8,16},{12,20},{16,8},{20,12},{24,0},{28,4},{1,25},{... | collective-permute-start | bytes 393224 | tf_op jit(solution)/shard_map/ppermute | solution.py:50
  35.2 8.9 %collective-permute-start.9 = (bf16[4,64,256]{2,1,0:T(8,128)(2,1)S(1)}, bf16[4,64,256]{2,1,0:T(8,128)(2,1)S(1)}, u32[]{:S(2)}, u32[]{:S(2)}) collective-permute-start(bf16[4,64,256]{2,1,0:T(8,128)(2,1)S(1)} %get-tuple-element.54), channel_id=1, source_target_pairs={{0,8},{4,12},{8,0},{12,4},{16,24},{20,28},{24,16},{28,20},{1,9},{5... | collective-permute-start | bytes 393224 | tf_op jit(solution)/shard_map/ppermute | solution.py:50
  35.2 13.8 %collective-permute-start.10 = (bf16[4,64,256]{2,1,0:T(8,128)(2,1)S(1)}, bf16[4,64,256]{2,1,0:T(8,128)(2,1)S(1)}, u32[]{:S(2)}, u32[]{:S(2)}) collective-permute-start(bf16[4,64,256]{2,1,0:T(8,128)(2,1)S(1)} %get-tuple-element.55), channel_id=1, source_target_pairs={{0,12},{4,8},{8,4},{12,0},{16,28},{20,24},{24,20},{28,16},{1,13},{... | collective-permute-start | bytes 393224 | tf_op jit(solution)/shard_map/ppermute | solution.py:50
  37.2 11.8 %collective-permute-start.8 = (bf16[4,64,256]{2,1,0:T(8,128)(2,1)S(1)}, bf16[4,64,256]{2,1,0:T(8,128)(2,1)S(1)}, u32[]{:S(2)}, u32[]{:S(2)}) collective-permute-start(bf16[4,64,256]{2,1,0:T(8,128)(2,1)S(1)} %get-tuple-element.52), channel_id=1, source_target_pairs={{0,4},{4,0},{8,12},{12,8},{16,20},{20,16},{24,28},{28,24},{1,5},{5... | collective-permute-start | bytes 393224 | tf_op jit(solution)/shard_map/ppermute | solution.py:50
  40.7 9.4 %collective-permute-start.16 = (bf16[4,64,256]{2,1,0:T(8,128)(2,1)S(1)}, bf16[4,64,256]{2,1,0:T(8,128)(2,1)S(1)}, u32[]{:S(2)}, u32[]{:S(2)}) collective-permute-start(bf16[4,64,256]{2,1,0:T(8,128)(2,1)S(1)} %get-tuple-element.66), channel_id=1, source_target_pairs={{0,24},{4,28},{8,16},{12,20},{16,8},{20,12},{24,0},{28,4},{1,25},{... | collective-permute-start | bytes 393224 | tf_op jit(solution)/shard_map/ppermute | solution.py:50
  41.0 11.1 %collective-permute-start.14 = (bf16[4,64,256]{2,1,0:T(8,128)(2,1)S(1)}, bf16[4,64,256]{2,1,0:T(8,128)(2,1)S(1)}, u32[]{:S(2)}, u32[]{:S(2)}) collective-permute-start(bf16[4,64,256]{2,1,0:T(8,128)(2,1)S(1)} %get-tuple-element.64), channel_id=1, source_target_pairs={{0,12},{4,8},{8,4},{12,0},{16,28},{20,24},{24,20},{28,16},{1,13},{... | collective-permute-start | bytes 393224 | tf_op jit(solution)/shard_map/ppermute | solution.py:50
  44.2 8.5 %collective-permute-start.12 = (bf16[4,64,256]{2,1,0:T(8,128)(2,1)S(1)}, bf16[4,64,256]{2,1,0:T(8,128)(2,1)S(1)}, u32[]{:S(2)}, u32[]{:S(2)}) collective-permute-start(bf16[4,64,256]{2,1,0:T(8,128)(2,1)S(1)} %get-tuple-element.60), channel_id=1, source_target_pairs={{0,4},{4,0},{8,12},{12,8},{16,20},{20,16},{24,28},{28,24},{1,5},{5... | collective-permute-start | bytes 393224 | tf_op jit(solution)/shard_map/ppermute | solution.py:50
  49.0 8.5 %collective-permute-start.13 = (bf16[4,64,256]{2,1,0:T(8,128)(2,1)S(1)}, bf16[4,64,256]{2,1,0:T(8,128)(2,1)S(1)}, u32[]{:S(2)}, u32[]{:S(2)}) collective-permute-start(bf16[4,64,256]{2,1,0:T(8,128)(2,1)S(1)} %get-tuple-element.62), channel_id=1, source_target_pairs={{0,8},{4,12},{8,0},{12,4},{16,24},{20,28},{24,16},{28,20},{1,9},{5... | collective-permute-start | bytes 393224 | tf_op jit(solution)/shard_map/ppermute | solution.py:50
  49.0 11.6 %collective-permute-start.17 = (bf16[4,64,256]{2,1,0:T(8,128)(2,1)S(1)}, bf16[4,64,256]{2,1,0:T(8,128)(2,1)S(1)}, u32[]{:S(2)}, u32[]{:S(2)}) collective-permute-start(bf16[4,64,256]{2,1,0:T(8,128)(2,1)S(1)} %get-tuple-element.73), channel_id=1, source_target_pairs={{0,28},{4,24},{8,20},{12,16},{16,12},{20,8},{24,4},{28,0},{1,29},{... | collective-permute-start | bytes 393224 | tf_op jit(solution)/shard_map/ppermute | solution.py:50
  60.5 2.5 %collective-permute-start.19 = (bf16[4,128,512]{2,1,0:T(8,128)(2,1)S(1)}, bf16[4,128,512]{2,1,0:T(8,128)(2,1)S(1)}, u32[]{:S(2)}, u32[]{:S(2)}) collective-permute-start(bf16[4,128,512]{2,1,0:T(8,128)(2,1)S(1)} %get-tuple-element.76), channel_id=1, source_target_pairs={{0,1},{1,0},{2,3},{3,2},{4,5},{5,4},{6,7},{7,6},{8,9},{9,8},{10,11... | collective-permute-start | bytes 1572872 | tf_op jit(solution)/shard_map/ppermute | solution.py:50
  60.6 2.6 %collective-permute-start.18 = (bf16[4,128,512]{2,1,0:T(8,128)(2,1)S(1)}, bf16[4,128,512]{2,1,0:T(8,128)(2,1)S(1)}, u32[]{:S(2)}, u32[]{:S(2)}) collective-permute-start(bf16[4,128,512]{2,1,0:T(8,128)(2,1)S(1)} %get-tuple-element.74), channel_id=1, source_target_pairs={{0,1},{1,0},{2,3},{3,2},{4,5},{5,4},{6,7},{7,6},{8,9},{9,8},{10,11... | collective-permute-start | bytes 1572872 | tf_op jit(solution)/shard_map/ppermute | solution.py:50
  63.5 14.0 %collective-permute-start.20 = (bf16[4,128,512]{2,1,0:T(8,128)(2,1)S(1)}, bf16[4,128,512]{2,1,0:T(8,128)(2,1)S(1)}, u32[]{:S(2)}, u32[]{:S(2)}) collective-permute-start(bf16[4,128,512]{2,1,0:T(8,128)(2,1)S(1)} %get-tuple-element.78), channel_id=1, source_target_pairs={{0,2},{1,3},{2,0},{3,1},{4,6},{5,7},{6,4},{7,5},{8,10},{9,11},{10,... | collective-permute-start | bytes 1572872 | tf_op jit(solution)/shard_map/ppermute | solution.py:50
  64.1 14.3 %collective-permute-start.21 = (bf16[4,64,256]{2,1,0:T(8,128)(2,1)S(1)}, bf16[4,64,256]{2,1,0:T(8,128)(2,1)S(1)}, u32[]{:S(2)}, u32[]{:S(2)}) collective-permute-start(bf16[4,64,256]{2,1,0:T(8,128)(2,1)S(1)} %get-tuple-element.80), channel_id=1, source_target_pairs={{0,16},{4,20},{8,24},{12,28},{16,0},{20,4},{24,8},{28,12},{1,17},{... | collective-permute-start | bytes 393224 | tf_op jit(solution)/shard_map/ppermute | solution.py:50
  64.1 14.3 %collective-permute-start.22 = (bf16[4,64,256]{2,1,0:T(8,128)(2,1)S(1)}, bf16[4,64,256]{2,1,0:T(8,128)(2,1)S(1)}, u32[]{:S(2)}, u32[]{:S(2)}) collective-permute-start(bf16[4,64,256]{2,1,0:T(8,128)(2,1)S(1)} %get-tuple-element.81), channel_id=1, source_target_pairs={{0,20},{4,16},{8,28},{12,24},{16,4},{20,0},{24,12},{28,8},{1,21},{... | collective-permute-start | bytes 393224 | tf_op jit(solution)/shard_map/ppermute | solution.py:50
  79.8 4.4 %collective-permute-start.23 = (bf16[32,512]{1,0:T(8,128)(2,1)S(1)}, bf16[32,512]{1,0:T(8,128)(2,1)S(1)}, u32[]{:S(2)}, u32[]{:S(2)}) collective-permute-start(bf16[32,512]{1,0:T(8,128)(2,1)S(1)} %get-tuple-element.86), channel_id=1, source_target_pairs={{0,1},{1,0},{2,3},{3,2},{4,5},{5,4},{6,7},{7,6},{8,9},{9,8},{10,11... | collective-permute-start | bytes 98312 | tf_op jit(solution)/shard_map/ppermute | solution.py:50
  79.9 4.3 %collective-permute-start.24 = (bf16[32,512]{1,0:T(8,128)(2,1)S(1)}, bf16[32,512]{1,0:T(8,128)(2,1)S(1)}, u32[]{:S(2)}, u32[]{:S(2)}) collective-permute-start(bf16[32,512]{1,0:T(8,128)(2,1)S(1)} %get-tuple-element.87), channel_id=1, source_target_pairs={{0,2},{1,3},{2,0},{3,1},{4,6},{5,7},{6,4},{7,5},{8,10},{9,11},{10,... | collective-permute-start | bytes 98312 | tf_op jit(solution)/shard_map/ppermute | solution.py:50
  81.0 3.3 %collective-permute-start.25 = (bf16[32,512]{1,0:T(8,128)(2,1)S(1)}, bf16[32,512]{1,0:T(8,128)(2,1)S(1)}, u32[]{:S(2)}, u32[]{:S(2)}) collective-permute-start(bf16[32,512]{1,0:T(8,128)(2,1)S(1)} %get-tuple-element.88), channel_id=1, source_target_pairs={{0,3},{1,2},{2,1},{3,0},{4,7},{5,6},{6,5},{7,4},{8,11},{9,10},{10,... | collective-permute-start | bytes 98312 | tf_op jit(solution)/shard_map/ppermute | solution.py:50

commit v13 on v11

--- a/solution.py
+++ b/solution.py
@@ -10,7 +10,7 @@
 BF16 = jnp.bfloat16
 F32 = jnp.float32
 LANE_GROUP = 16
-CFG = {'a2a': [True, True], 'limit': 62914560, 'cost': {}, 'direct': False, 'rsdirect': False, 'f2early': False, 'order': [[7, 6, 5, 4, 3, 2, 1], [7, 6, 5, 4, 3, 2, 1]], 'deps': {'fx': ['A2'], 'F1': ['M'], 'F2': ['pair'], 'Z1': ['add']}}
+CFG = {'a2a': [True, True], 'limit': 62914560, 'cost': {'add_body': 18000000, 'mix_back_body': 18000000}, 'direct': False, 'rsdirect': False, 'f2early': False, 'order': [[7, 6, 5, 4, 3, 2, 1], [7, 6, 5, 4, 3, 2, 1]], 'deps': {'fx': ['A2'], 'F1': ['M'], 'F2': ['pair'], 'Z1': ['add']}}
 
 
 def iota(shape, dim):

time: 83.9 us -> 83.9 us (level)
  no operation moved by 1% of the time
where the time goes in v13:
time: 83.9 us; the launch traced here: 83.4 us
  waiting for transfers between devices  30.7 us (37%)
  Pallas kernels  24.8 us (30%)
  starting transfers between devices  18.5 us (22%)
  local copies, waits for them, and re-layouts  8.6 us (10%)
    pallas_call x11, Pallas kernels, call(): pl.pallas_call(body, name=name, out_shape=outs, in_specs=[pl.BlockSpec(me...  24.8 us
    ppermute x12, waiting for transfers between devices, swap(): return lax.ppermute(value, axis, [(p, p ^ step) for p in range(size)])  16.3 us
    all_to_all x1, waiting for transfers between devices, packed_shards(): lax.all_to_all(dep('H0', regrouped[0]), 'seq', 0, 0, tiled=True)  11.1 us
    unnamed x32, local copies, waits for them, and re-layouts  8.6 us
    ppermute x12, starting transfers between devices, swap(): return lax.ppermute(value, axis, [(p, p ^ step) for p in range(size)])  8.51 us
    all_to_all x1, starting transfers between devices, packed_shards(): lax.all_to_all(dep('h0', back[0]).reshape(seq, blocks, j_here, width), 's...  6.24 us
    all_to_all x1, starting transfers between devices, packed_shards(): lax.all_to_all(dep('H0', regrouped[0]), 'seq', 0, 0, tiled=True)  3.77 us
    all_to_all x1, waiting for transfers between devices, packed_shards(): lax.all_to_all(dep('h0', back[0]).reshape(seq, blocks, j_here, width), 's...  3.32 us
  transfers between devices with their start and end apart: 14, of which 6 were waited for; matrix products, arithmetic and copies ran while one was open for 0% of the time, Pallas kernels for 21%

profile of v13, /device:TPU:0, one launch (start us, length us, event | category | flops | bytes accessed | tf_op | source)
XLA Modules:
  0.0 83.4 jit_solution(1897280090185047897)
XLA Ops:
  0.6 0.0 copy-start.8
  0.6 0.8 copy-done.8
  1.5 0.4 pack_body.1.refs_0_
  1.9 2.4 %collective-permute-start.2 = (bf16[32,512]{1,0:T(8,128)(2,1)S(1)}, bf16[32,512]{1,0:T(8,128)(2,1)S(1)}, u32[]{:S(2)}, u32[]{:S(2)}) collective-permute-start(bf16[32,512]{1,0:T(8,128)(2,1)S(1)} %pack_body.1.refs_0_), channel_id=1, source_target_pairs={{0,3},{1,2},{2,1},{3,0},{4,7},{5,6},{6,5},{7,4},{8,11},{9,10},{10,... | collective-permute-start | bytes 98312 | tf_op jit(solution)/shard_map/ppermute | solution.py:50
  4.3 0.6 collective-permute-start.1
  5.0 0.0 collective-permute-start
  5.0 0.0 copy-start.9
  5.0 0.7 copy-done.9
  5.7 0.0 copy-start
  5.7 1.2 %copy-done = bf16[1,2048,256]{2,1,0:T(8,128)(2,1)S(1)} copy-done((bf16[1,2048,256]{2,1,0:T(8,128)(2,1)S(1)}, bf16[1,2048,256]{2,1,0:T(8,128)(2,1)}, u32[]{:S(2)}) %copy-start) | copy-done | bytes 1048600
  6.9 1.2 %copy-done.5 = bf16[1,2048,256]{2,1,0:T(8,128)(2,1)S(1)} copy-done((bf16[1,2048,256]{2,1,0:T(8,128)(2,1)S(1)}, bf16[1,2048,256]{2,1,0:T(8,128)(2,1)}, u32[]{:S(2)}) %copy-start.5) | copy-done | bytes 1048600
  8.1 0.5 gate_body.1.refs_4_.refs_1_
  8.6 0.0 collective-permute-done.2.refs_3_
  8.6 0.0 collective-permute-done.1.refs_2_
  8.7 0.0 collective-permute-done.refs_1_
  8.7 2.2 %regroup_back_body.1 = (bf16[32,64,256]{2,1,0:T(8,128)(2,1)}, bf16[4,32,512]{2,1,0:T(8,128)(2,1)S(1)}) custom-call(bf16[32,512]{1,0:T(8,128)(2,1)S(1)} %pack_body.1.refs_0_, bf16[32,512]{1,0:T(8,128)(2,1)S(1)} %collective-permute-done.refs_1_, bf16[32,512]{1,0:T(8,128)(2,1)S(1)} %collective-permute-done.1.refs_2_, ...), custom_call_target="tpu_custom_call" | custom-call | tf_op jit(solution)/shard_map/regroup_back_body/pallas_call | solution.py:31
  10.9 0.0 copy-start.12
  10.9 6.2 %all-to-all-start.1 = ((bf16[8,4,64,256]{3,2,1,0:T(8,128)(2,1)}), bf16[8,4,64,256]{3,2,1,0:T(8,128)(2,1)S(1)}, u32[]{:S(2)}, u32[]{:S(2)}) async-start(bf16[8,4,64,256]{3,2,1,0:T(8,128)(2,1)} %bitcast.6), calls=%async_computation.1 | async-start | bytes 2097152 | tf_op jit(solution)/shard_map/all_to_all | solution.py:337
  17.1 0.0 copy-done.12
  17.1 1.6 %collective-permute-start.4 = (bf16[4,128,512]{2,1,0:T(8,128)(2,1)S(1)}, bf16[4,128,512]{2,1,0:T(8,128)(2,1)S(1)}, u32[]{:S(2)}, u32[]{:S(2)}) collective-permute-start(bf16[4,128,512]{2,1,0:T(8,128)(2,1)S(1)} %copy-done.12), channel_id=1, source_target_pairs={{0,2},{1,3},{2,0},{3,1},{4,6},{5,7},{6,4},{7,5},{8,10},{9,11},{10,... | collective-permute-start | bytes 1572872 | tf_op jit(solution)/shard_map/ppermute | solution.py:50
  18.7 0.0 collective-permute-start.3
  18.7 12.3 %collective-permute-done.4.refs_2_ = bf16[4,128,512]{2,1,0:T(8,128)(2,1)S(1)} collective-permute-done((bf16[4,128,512]{2,1,0:T(8,128)(2,1)S(1)}, bf16[4,128,512]{2,1,0:T(8,128)(2,1)S(1)}, u32[]{:S(2)}, u32[]{:S(2)}) %collective-permute-start.4) | collective-permute-done | bytes 524320 | tf_op jit(solution)/shard_map/ppermute | solution.py:50
  31.0 0.0 collective-permute-start.5
  31.0 0.0 collective-permute-done.3.refs_1_
  31.0 0.0 copy-start.14
  31.0 1.9 %collective-permute-done.5.refs_3_ = bf16[4,128,512]{2,1,0:T(8,128)(2,1)S(1)} collective-permute-done((bf16[4,128,512]{2,1,0:T(8,128)(2,1)S(1)}, bf16[4,128,512]{2,1,0:T(8,128)(2,1)S(1)}, u32[]{:S(2)}, u32[]{:S(2)}) %collective-permute-start.5) | collective-permute-done | bytes 524320 | tf_op jit(solution)/shard_map/ppermute | solution.py:50
  32.9 0.0 copy-start.15
  32.9 0.8 copy-done.15
  33.7 0.0 copy-done.13
  33.7 0.0 copy-done.14
  33.7 6.2 %mix_body.1 = (bf16[8,4,64,256]{3,2,1,0:T(8,128)(2,1)}, bf16[2048,256]{1,0:T(8,128)(2,1)}) custom-call(bf16[4,128,512]{2,1,0:T(8,128)(2,1)} %refs_0_.3, bf16[4,128,512]{2,1,0:T(8,128)(2,1)} %copy-done.14, bf16[4,128,512]{2,1,0:T(8,128)(2,1)} %copy-done.13, bf16[4,128,512]{2,1,0:T(8,128)(2,1)} %copy-done.15, bf16[2048,256]{1,0:T(8,128)(2,1)} %bitcast.15, ...), custom_call_target="tpu_custom_call" | custom-call | tf_op jit(solution)/shard_map/mix_body/pallas_call | solution.py:31
  40.0 3.3 %all-to-all-done.1.refs_0_ = bf16[8,4,64,256]{3,2,1,0:T(8,128)(2,1)S(1)} async-done(((bf16[8,4,64,256]{3,2,1,0:T(8,128)(2,1)}), bf16[8,4,64,256]{3,2,1,0:T(8,128)(2,1)S(1)}, u32[]{:S(2)}, u32[]{:S(2)}) %all-to-all-start.1) | async-done | bytes 1048608 | tf_op jit(solution)/shard_map/all_to_all | solution.py:337
  43.3 0.0 copy-start.2
  43.3 1.0 %copy-done.2 = bf16[8,4,64,256]{3,2,1,0:T(8,128)(2,1)} copy-done((bf16[8,4,64,256]{3,2,1,0:T(8,128)(2,1)}, bf16[8,4,64,256]{3,2,1,0:T(8,128)(2,1)S(1)}, u32[]{:S(2)}) %copy-start.2) | copy-done | bytes 1048600
  44.2 3.8 %all-to-all-start = ((bf16[8,4,64,256]{3,2,1,0:T(8,128)(2,1)}), bf16[8,4,64,256]{3,2,1,0:T(8,128)(2,1)S(1)}, u32[]{:S(2)}, u32[]{:S(2)}) async-start(bf16[8,4,64,256]{3,2,1,0:T(8,128)(2,1)} %get-tuple-element.27), calls=%async_computation | async-start | bytes 2097152 | tf_op jit(solution)/shard_map/all_to_all | solution.py:362
  48.0 0.0 copy-done.1
  48.0 0.0 copy-done.11
  48.0 0.0 copy-start.3
  48.0 1.2 %copy-done.3 = bf16[8,4,64,256]{3,2,1,0:T(8,128)(2,1)S(1)} copy-done((bf16[8,4,64,256]{3,2,1,0:T(8,128)(2,1)S(1)}, bf16[8,4,64,256]{3,2,1,0:T(8,128)(2,1)}, u32[]{:S(2)}) %copy-start.3) | copy-done | bytes 1048600
  49.2 2.9 %first_grad_body.1 = (bf16[4,128,512]{2,1,0:T(8,128)(2,1)S(1)}, bf16[4,128,512]{2,1,0:T(8,128)(2,1)S(1)}, bf16[4,128,512]{2,1,0:T(8,128)(2,1)S(1)}, bf16[4,128,5...) custom-call(bf16[8,4,64,256]{3,2,1,0:T(8,128)(2,1)S(1)} %copy-done.3, bf16[2048,256]{1,0:T(8,128)(2,1)S(1)} %bitcast.17, ...), custom_call_target="tpu_custom_call" | custom-call | tf_op jit(solution)/shard_map/first_grad_body/pallas_call | solution.py:31
  52.2 0.0 copy-start.7
  52.2 0.9 %copy-done.7 = bf16[4,512,256]{2,1,0:T(8,128)(2,1)} copy-done((bf16[4,512,256]{2,1,0:T(8,128)(2,1)}, bf16[4,512,256]{2,1,0:T(8,128)(2,1)S(1)}, u32[]{:S(2)}) %copy-start.7) | copy-done | bytes 1048600
  53.2 0.0 collective-permute-start.6
  53.2 0.5 collective-permute-start.7
  53.7 1.4 %collective-permute-done.6.got_a = bf16[4,128,512]{2,1,0:T(8,128)(2,1)S(1)} collective-permute-done((bf16[4,128,512]{2,1,0:T(8,128)(2,1)S(1)}, bf16[4,128,512]{2,1,0:T(8,128)(2,1)S(1)}, u32[]{:S(2)}, u32[]{:S(2)}) %collective-permute-start.6) | collective-permute-done | bytes 524320 | tf_op jit(solution)/shard_map/ppermute | solution.py:50
  55.1 0.7 collective-permute-done.7.got_b
  55.8 1.0 %pair_body.1 = (f32[4,128,512]{2,1,0:T(8,128)S(1)}, bf16[4,128,512]{2,1,0:T(8,128)(2,1)}) custom-call(bf16[4,128,512]{2,1,0:T(8,128)(2,1)S(1)} %get-tuple-element.30.own_a, bf16[4,128,512]{2,1,0:T(8,128)(2,1)S(1)} %get-tuple-element.31.own_b, bf16[4,128,512]{2,1,0:T(8,128)(2,1)S(1)} %collective-permute-done.6.got_a, ...), custom_call_target="tpu_custom_call" | custom-call | tf_op jit(solution)/shard_map/pair_body/pallas_call | solution.py:31
  56.8 1.4 %collective-permute-start.8 = (bf16[4,128,512]{2,1,0:T(8,128)(2,1)}, bf16[4,128,512]{2,1,0:T(8,128)(2,1)}, u32[]{:S(2)}, u32[]{:S(2)}) collective-permute-start(bf16[4,128,512]{2,1,0:T(8,128)(2,1)} %get-tuple-element.34), channel_id=1, source_target_pairs={{0,2},{1,3},{2,0},{3,1},{4,6},{5,7},{6,4},{7,5},{8,10},{9,11},{10,... | collective-permute-start | bytes 1572872 | tf_op jit(solution)/shard_map/ppermute | solution.py:50
  58.2 4.7 %mix_back_body.1.back_ref = bf16[2048,256]{1,0:T(8,128)(2,1)} custom-call(bf16[4,128,512]{2,1,0:T(8,128)(2,1)} %refs_0_.3, bf16[4,128,512]{2,1,0:T(8,128)(2,1)} %copy-done.14, bf16[4,128,512]{2,1,0:T(8,128)(2,1)} %copy-done.13, bf16[4,128,512]{2,1,0:T(8,128)(2,1)} %copy-done.15, bf16[4,512,256]{2,1,0:T(8,128)(2,1)} %copy-done.7), custom_call_target="tpu_custom_call" | custom-call | bytes 18000000 | tf_op jit(solution)/shard_map/mix_back_body/pallas_call | solution.py:31
  62.9 11.1 %all-to-all-done = bf16[8,4,64,256]{3,2,1,0:T(8,128)(2,1)S(1)} async-done(((bf16[8,4,64,256]{3,2,1,0:T(8,128)(2,1)}), bf16[8,4,64,256]{3,2,1,0:T(8,128)(2,1)S(1)}, u32[]{:S(2)}, u32[]{:S(2)}) %all-to-all-start) | async-done | bytes 1048608 | tf_op jit(solution)/shard_map/all_to_all | solution.py:362
  74.0 0.0 collective-permute-done.8.got
  74.0 1.9 %add_body.1 = bf16[4,128,512]{2,1,0:T(8,128)(2,1)} custom-call(f32[4,128,512]{2,1,0:T(8,128)S(1)} %get-tuple-element.37.own, bf16[4,128,512]{2,1,0:T(8,128)(2,1)} %collective-permute-done.8.got), custom_call_target="tpu_custom_call" | custom-call | bytes 18000000 | tf_op jit(solution)/shard_map/add_body/pallas_call | solution.py:31
  75.9 1.3 %second_grad_body.1 = (bf16[32,512]{1,0:T(8,128)(2,1)S(1)}, bf16[32,512]{1,0:T(8,128)(2,1)S(1)}, bf16[32,512]{1,0:T(8,128)(2,1)S(1)}, bf16[32,512]{1,0:T(8,128)(2,1)S(1)}) custom-call(bf16[32,64,256]{2,1,0:T(8,128)(2,1)S(1)} %bitcast.13, bf16[2048,256]{1,0:T(8,128)(2,1)S(1)} %gate_body.1.refs_4_.refs_1_), custom_call_target="tpu_custom_call" | custom-call | tf_op jit(solution)/shard_map/second_grad_body/pallas_call | solution.py:31
  77.2 0.1 collective-permute-start.9
  77.3 1.5 %collective-permute-start.10 = (bf16[32,512]{1,0:T(8,128)(2,1)S(1)}, bf16[32,512]{1,0:T(8,128)(2,1)S(1)}, u32[]{:S(2)}, u32[]{:S(2)}) collective-permute-start(bf16[32,512]{1,0:T(8,128)(2,1)S(1)} %get-tuple-element.43), channel_id=1, source_target_pairs={{0,2},{1,3},{2,0},{3,1},{4,6},{5,7},{6,4},{7,5},{8,10},{9,11},{10,... | collective-permute-start | bytes 98312 | tf_op jit(solution)/shard_map/ppermute | solution.py:50
  78.8 0.4 collective-permute-start.11
  79.2 0.0 copy-done.4
  79.2 0.0 copy-done.6
  79.2 0.7 copy-done.10
  79.9 2.5 %tokens_body.1 = bf16[2048,256]{1,0:T(8,128)(2,1)} custom-call(bf16[32,64,256]{2,1,0:T(8,128)(2,1)S(1)} %bitcast.14, bf16[4,32,512]{2,1,0:T(8,128)(2,1)S(1)} %get-tuple-element.39.second_ref, bf16[2048,256]{1,0:T(8,128)(2,1)S(1)} %copy-done.6, s32[1,256]{1,0:T(1,128)S(1)} %bitcast.23, bf16[2048,256]{1,0:T(8,128)(2,1)S(1)} %copy-done.4), custom_call_target="tpu_custom_call" | custom-call | tf_op jit(solution)/shard_map/tokens_body/pallas_call | solution.py:31
  82.3 0.0 collective-permute-done.9.refs_1_
  82.3 0.0 collective-permute-done.10.refs_2_
  82.3 0.0 collective-permute-done.11.refs_3_
  82.4 1.1 %unpack_body.1 = bf16[256,64]{1,0:T(8,128)(2,1)} custom-call(bf16[32,512]{1,0:T(8,128)(2,1)S(1)} %get-tuple-element.41.refs_0_, bf16[32,512]{1,0:T(8,128)(2,1)S(1)} %collective-permute-done.9.refs_1_, bf16[32,512]{1,0:T(8,128)(2,1)S(1)} %collective-permute-done.10.refs_2_, bf16[32,512]{1,0:T(8,128)(2,1)S(1)} %collective-permute-done.11.refs_3_), custom_call_target="tpu_custom_call" | custom-call | tf_op jit(solution)/shard_map/unpack_body/pallas_call | solution.py:31
  (7 shorter events, 0.0 us)
Async XLA Ops:
  0.6 0.8 %copy-start.8 = (bf16[64,8,32]{0,2,1:T(8,128)(2,1)S(1)}, bf16[64,8,32]{0,2,1:T(8,128)(2,1)}, u32[]{:S(2)}) copy-start(bf16[64,8,32]{0,2,1:T(8,128)(2,1)} %param.9) | copy-start | bytes 98308
  1.9 6.7 %collective-permute-start.2 = (bf16[32,512]{1,0:T(8,128)(2,1)S(1)}, bf16[32,512]{1,0:T(8,128)(2,1)S(1)}, u32[]{:S(2)}, u32[]{:S(2)}) collective-permute-start(bf16[32,512]{1,0:T(8,128)(2,1)S(1)} %pack_body.1.refs_0_), channel_id=1, source_target_pairs={{0,3},{1,2},{2,1},{3,0},{4,7},{5,6},{6,5},{7,4},{8,11},{9,10},{10,... | collective-permute-start | bytes 98312 | tf_op jit(solution)/shard_map/ppermute | solution.py:50
  4.3 4.3 %collective-permute-start.1 = (bf16[32,512]{1,0:T(8,128)(2,1)S(1)}, bf16[32,512]{1,0:T(8,128)(2,1)S(1)}, u32[]{:S(2)}, u32[]{:S(2)}) collective-permute-start(bf16[32,512]{1,0:T(8,128)(2,1)S(1)} %pack_body.1.refs_0_), channel_id=1, source_target_pairs={{0,2},{1,3},{2,0},{3,1},{4,6},{5,7},{6,4},{7,5},{8,10},{9,11},{10,... | collective-permute-start | bytes 98312 | tf_op jit(solution)/shard_map/ppermute | solution.py:50
  5.0 3.7 %collective-permute-start = (bf16[32,512]{1,0:T(8,128)(2,1)S(1)}, bf16[32,512]{1,0:T(8,128)(2,1)S(1)}, u32[]{:S(2)}, u32[]{:S(2)}) collective-permute-start(bf16[32,512]{1,0:T(8,128)(2,1)S(1)} %pack_body.1.refs_0_), channel_id=1, source_target_pairs={{0,1},{1,0},{2,3},{3,2},{4,5},{5,4},{6,7},{7,6},{8,9},{9,8},{10,11... | collective-permute-start | bytes 98312 | tf_op jit(solution)/shard_map/ppermute | solution.py:50
  5.0 0.7 copy-start.9
  5.7 1.2 %copy-start = (bf16[1,2048,256]{2,1,0:T(8,128)(2,1)S(1)}, bf16[1,2048,256]{2,1,0:T(8,128)(2,1)}, u32[]{:S(2)}) copy-start(bf16[1,2048,256]{2,1,0:T(8,128)(2,1)} %param.6) | copy-start | bytes 3145732
  6.9 1.2 %copy-start.5 = (bf16[1,2048,256]{2,1,0:T(8,128)(2,1)S(1)}, bf16[1,2048,256]{2,1,0:T(8,128)(2,1)}, u32[]{:S(2)}) copy-start(bf16[1,2048,256]{2,1,0:T(8,128)(2,1)} %param.7) | copy-start | bytes 3145732
  10.9 6.3 %copy-start.12 = (bf16[4,128,512]{2,1,0:T(8,128)(2,1)S(1)}, bf16[4,128,512]{2,1,0:T(8,128)(2,1)}, u32[]{:S(2)}) copy-start(bf16[4,128,512]{2,1,0:T(8,128)(2,1)} %refs_0_.3) | copy-start | bytes 1572868
  10.9 32.4 %all-to-all-start.1 = ((bf16[8,4,64,256]{3,2,1,0:T(8,128)(2,1)}), bf16[8,4,64,256]{3,2,1,0:T(8,128)(2,1)S(1)}, u32[]{:S(2)}, u32[]{:S(2)}) async-start(bf16[8,4,64,256]{3,2,1,0:T(8,128)(2,1)} %bitcast.6), calls=%async_computation.1 | async-start | bytes 2097152 | tf_op jit(solution)/shard_map/all_to_all | solution.py:337
  17.1 13.8 %collective-permute-start.4 = (bf16[4,128,512]{2,1,0:T(8,128)(2,1)S(1)}, bf16[4,128,512]{2,1,0:T(8,128)(2,1)S(1)}, u32[]{:S(2)}, u32[]{:S(2)}) collective-permute-start(bf16[4,128,512]{2,1,0:T(8,128)(2,1)S(1)} %copy-done.12), channel_id=1, source_target_pairs={{0,2},{1,3},{2,0},{3,1},{4,6},{5,7},{6,4},{7,5},{8,10},{9,11},{10,... | collective-permute-start | bytes 1572872 | tf_op jit(solution)/shard_map/ppermute | solution.py:50
  18.7 12.3 %collective-permute-start.3 = (bf16[4,128,512]{2,1,0:T(8,128)(2,1)S(1)}, bf16[4,128,512]{2,1,0:T(8,128)(2,1)S(1)}, u32[]{:S(2)}, u32[]{:S(2)}) collective-permute-start(bf16[4,128,512]{2,1,0:T(8,128)(2,1)S(1)} %copy-done.12), channel_id=1, source_target_pairs={{0,1},{1,0},{2,3},{3,2},{4,5},{5,4},{6,7},{7,6},{8,9},{9,8},{10,11... | collective-permute-start | bytes 1572872 | tf_op jit(solution)/shard_map/ppermute | solution.py:50
  31.0 2.7 %copy-start.13 = (bf16[4,128,512]{2,1,0:T(8,128)(2,1)}, bf16[4,128,512]{2,1,0:T(8,128)(2,1)S(1)}, u32[]{:S(2)}) copy-start(bf16[4,128,512]{2,1,0:T(8,128)(2,1)S(1)} %collective-permute-done.4.refs_2_) | copy-start | bytes 1572868
  31.0 1.9 %collective-permute-start.5 = (bf16[4,128,512]{2,1,0:T(8,128)(2,1)S(1)}, bf16[4,128,512]{2,1,0:T(8,128)(2,1)S(1)}, u32[]{:S(2)}, u32[]{:S(2)}) collective-permute-start(bf16[4,128,512]{2,1,0:T(8,128)(2,1)S(1)} %collective-permute-done.4.refs_2_), channel_id=1, source_target_pairs={{0,1},{1,0},{2,3},{3,2},{4,5},{5,4},{6,7},{7,6},{8,9},{9,8},{10,11... | collective-permute-start | bytes 1572872 | tf_op jit(solution)/shard_map/ppermute | solution.py:50
  31.0 2.7 %copy-start.14 = (bf16[4,128,512]{2,1,0:T(8,128)(2,1)}, bf16[4,128,512]{2,1,0:T(8,128)(2,1)S(1)}, u32[]{:S(2)}) copy-start(bf16[4,128,512]{2,1,0:T(8,128)(2,1)S(1)} %collective-permute-done.3.refs_1_) | copy-start | bytes 1572868
  32.9 0.8 copy-start.15
  43.3 1.0 %copy-start.2 = (bf16[8,4,64,256]{3,2,1,0:T(8,128)(2,1)}, bf16[8,4,64,256]{3,2,1,0:T(8,128)(2,1)S(1)}, u32[]{:S(2)}) copy-start(bf16[8,4,64,256]{3,2,1,0:T(8,128)(2,1)S(1)} %all-to-all-done.1.refs_0_) | copy-start | bytes 3145732
  44.2 3.8 %copy-start.1 = (bf16[1,2048,256]{2,1,0:T(8,128)(2,1)S(1)}, bf16[1,2048,256]{2,1,0:T(8,128)(2,1)}, u32[]{:S(2)}) copy-start(bf16[1,2048,256]{2,1,0:T(8,128)(2,1)} %param.6) | copy-start | bytes 3145732
  44.2 3.8 %copy-start.11 = (s32[512]{0:T(512)S(1)}, s32[512]{0:T(512)}, u32[]{:S(2)}) copy-start(s32[512]{0:T(512)} %param.11) | copy-start | bytes 6148
  44.2 29.7 %all-to-all-start = ((bf16[8,4,64,256]{3,2,1,0:T(8,128)(2,1)}), bf16[8,4,64,256]{3,2,1,0:T(8,128)(2,1)S(1)}, u32[]{:S(2)}, u32[]{:S(2)}) async-start(bf16[8,4,64,256]{3,2,1,0:T(8,128)(2,1)} %get-tuple-element.27), calls=%async_computation | async-start | bytes 2097152 | tf_op jit(solution)/shard_map/all_to_all | solution.py:362
  48.0 1.2 %copy-start.3 = (bf16[8,4,64,256]{3,2,1,0:T(8,128)(2,1)S(1)}, bf16[8,4,64,256]{3,2,1,0:T(8,128)(2,1)}, u32[]{:S(2)}) copy-start(bf16[8,4,64,256]{3,2,1,0:T(8,128)(2,1)} %copy-done.2) | copy-start | bytes 3145732
  52.2 1.0 %copy-start.7 = (bf16[4,512,256]{2,1,0:T(8,128)(2,1)}, bf16[4,512,256]{2,1,0:T(8,128)(2,1)S(1)}, u32[]{:S(2)}) copy-start(bf16[4,512,256]{2,1,0:T(8,128)(2,1)S(1)} %get-tuple-element.35.refs_4_) | copy-start | bytes 3145732
  53.2 1.9 %collective-permute-start.6 = (bf16[4,128,512]{2,1,0:T(8,128)(2,1)S(1)}, bf16[4,128,512]{2,1,0:T(8,128)(2,1)S(1)}, u32[]{:S(2)}, u32[]{:S(2)}) collective-permute-start(bf16[4,128,512]{2,1,0:T(8,128)(2,1)S(1)} %get-tuple-element.32), channel_id=1, source_target_pairs={{0,1},{1,0},{2,3},{3,2},{4,5},{5,4},{6,7},{7,6},{8,9},{9,8},{10,11... | collective-permute-start | bytes 1572872 | tf_op jit(solution)/shard_map/ppermute | solution.py:50
  53.2 2.7 %collective-permute-start.7 = (bf16[4,128,512]{2,1,0:T(8,128)(2,1)S(1)}, bf16[4,128,512]{2,1,0:T(8,128)(2,1)S(1)}, u32[]{:S(2)}, u32[]{:S(2)}) collective-permute-start(bf16[4,128,512]{2,1,0:T(8,128)(2,1)S(1)} %get-tuple-element.33), channel_id=1, source_target_pairs={{0,1},{1,0},{2,3},{3,2},{4,5},{5,4},{6,7},{7,6},{8,9},{9,8},{10,11... | collective-permute-start | bytes 1572872 | tf_op jit(solution)/shard_map/ppermute | solution.py:50
  56.8 17.2 %collective-permute-start.8 = (bf16[4,128,512]{2,1,0:T(8,128)(2,1)}, bf16[4,128,512]{2,1,0:T(8,128)(2,1)}, u32[]{:S(2)}, u32[]{:S(2)}) collective-permute-start(bf16[4,128,512]{2,1,0:T(8,128)(2,1)} %get-tuple-element.34), channel_id=1, source_target_pairs={{0,2},{1,3},{2,0},{3,1},{4,6},{5,7},{6,4},{7,5},{8,10},{9,11},{10,... | collective-permute-start | bytes 1572872 | tf_op jit(solution)/shard_map/ppermute | solution.py:50
  75.9 3.3 %copy-start.4 = (bf16[2048,256]{1,0:T(8,128)(2,1)S(1)}, bf16[2048,256]{1,0:T(8,128)(2,1)}, u32[]{:S(2)}) copy-start(bf16[2048,256]{1,0:T(8,128)(2,1)} %mix_back_body.1.back_ref) | copy-start | bytes 3145732
  75.9 3.3 %copy-start.6 = (bf16[2048,256]{1,0:T(8,128)(2,1)S(1)}, bf16[2048,256]{1,0:T(8,128)(2,1)}, u32[]{:S(2)}) copy-start(bf16[2048,256]{1,0:T(8,128)(2,1)} %get-tuple-element.40.h_ref) | copy-start | bytes 3145732
  77.2 5.1 %collective-permute-start.9 = (bf16[32,512]{1,0:T(8,128)(2,1)S(1)}, bf16[32,512]{1,0:T(8,128)(2,1)S(1)}, u32[]{:S(2)}, u32[]{:S(2)}) collective-permute-start(bf16[32,512]{1,0:T(8,128)(2,1)S(1)} %get-tuple-element.42), channel_id=1, source_target_pairs={{0,1},{1,0},{2,3},{3,2},{4,5},{5,4},{6,7},{7,6},{8,9},{9,8},{10,11... | collective-permute-start | bytes 98312 | tf_op jit(solution)/shard_map/ppermute | solution.py:50
  77.3 5.0 %collective-permute-start.10 = (bf16[32,512]{1,0:T(8,128)(2,1)S(1)}, bf16[32,512]{1,0:T(8,128)(2,1)S(1)}, u32[]{:S(2)}, u32[]{:S(2)}) collective-permute-start(bf16[32,512]{1,0:T(8,128)(2,1)S(1)} %get-tuple-element.43), channel_id=1, source_target_pairs={{0,2},{1,3},{2,0},{3,1},{4,6},{5,7},{6,4},{7,5},{8,10},{9,11},{10,... | collective-permute-start | bytes 98312 | tf_op jit(solution)/shard_map/ppermute | solution.py:50
  78.8 3.6 %collective-permute-start.11 = (bf16[32,512]{1,0:T(8,128)(2,1)S(1)}, bf16[32,512]{1,0:T(8,128)(2,1)S(1)}, u32[]{:S(2)}, u32[]{:S(2)}) collective-permute-start(bf16[32,512]{1,0:T(8,128)(2,1)S(1)} %get-tuple-element.44), channel_id=1, source_target_pairs={{0,3},{1,2},{2,1},{3,0},{4,7},{5,6},{6,5},{7,4},{8,11},{9,10},{10,... | collective-permute-start | bytes 98312 | tf_op jit(solution)/shard_map/ppermute | solution.py:50
  79.2 0.7 copy-start.10

commit v14 on v11

--- a/solution.py
+++ b/solution.py
@@ -251,9 +251,10 @@
         write.wait()
 
 
-def pair_body(own_a, own_b, got_a, got_b, out_a, out_b):
+def pair_body(own_a, own_b, got_a, got_b, out_a, *outs_b):
     out_a[...] = own_a[...].astype(F32) + got_a[...].astype(F32)
-    out_b[...] = (own_b[...].astype(F32) + got_b[...].astype(F32)).astype(BF16)
+    for n, out_b in enumerate(outs_b):
+        out_b[...] = (own_b[n].astype(F32) + got_b[n].astype(F32)).astype(BF16)
 
 
 def sum_body(own, *refs):
@@ -263,8 +264,9 @@
     refs[-1][...] = total.astype(BF16)
 
 
-def add_body(own, got, out):
-    out[...] = (own[...] + got[...].astype(F32)).astype(BF16)
+def add_body(own, *refs):
+    for n, got in enumerate(refs[:-1]):
+        refs[-1][n] = (own[n] + got[...].astype(F32)).astype(BF16)
 
 
 def unpack_body(order, *refs):
@@ -379,12 +381,15 @@
     if CFG['rsdirect']:
         (grad_one,) = call(sum_body, [of(parts[0].shape)], [dep("sum", parts[0]), *others])
     else:
-        kept, summed = call(
-            pair_body, [of(parts[0].shape, F32), of(parts[0].shape)], [dep("pair", parts[0]), parts[2], near, far], limit=40 << 20
+        kept, *summed = call(
+            pair_body,
+            [of(parts[0].shape, F32)] + [of((k_here, order))] * blocks,
+            [dep("pair", parts[0]), parts[2], near, far],
+            limit=40 << 20,
         )
-        keep("pair", summed)
-        rx = move("rx", summed, "batch", 2, batch)
-        (grad_one,) = call(add_body, [of(parts[0].shape)], [kept, rx])
+        keep("pair", summed[0])
+        across_sums = [move(f"rx{n}", summed[n], "batch", 2, batch) for n in range(blocks)]
+        (grad_one,) = call(add_body, [of(parts[0].shape)], [kept, *across_sums])
     (dmix_in,) = call(
         functools.partial(mix_back_body, batch),
         [of((rows_here, width))],

time: 83.9 us -> 82 us (0.977)
  waiting for transfers between devices: 30.7 us -> 27.3 us
  starting transfers between devices: 18.5 us -> 21.2 us
  Pallas kernels: 24.8 us -> 23.6 us
    all_to_all x1, waiting for transfers between devices: 11.1 us -> 2.25 us  [packed_shards(): lax.all_to_all(dep('H0', regrouped[0]), 'seq', 0, 0, tiled=True)]
    ppermute x12 -> x15, waiting for transfers between devices: 16.3 us -> 21.7 us  [swap(): return lax.ppermute(value, axis, [(p, p ^ step) for p in range(size)])]
    ppermute x12 -> x15, starting transfers between devices: 8.51 us -> 11.2 us  [swap(): return lax.ppermute(value, axis, [(p, p ^ step) for p in range(size)])]
    pallas_call x11, Pallas kernels: 24.8 us -> 23.6 us  [call(): pl.pallas_call(body, name=name, out_shape=outs, in_specs=[pl.BlockSpec(me...]
  transfers between devices with their start and end apart: 14 -> 17, of which waited for: 6 -> 9; matrix products, arithmetic and copies ran while one was open for 0% -> 0% of each run, Pallas kernels for 21% -> 23%
where the time goes in v14:
time: 82 us; the launch traced here: 81.5 us
  waiting for transfers between devices  27.3 us (33%)
  Pallas kernels  23.6 us (29%)
  starting transfers between devices  21.2 us (26%)
  local copies, waits for them, and re-layouts  8.63 us (11%)
    pallas_call x11, Pallas kernels, call(): pl.pallas_call(body, name=name, out_shape=outs, in_specs=[pl.BlockSpec(me...  23.6 us
    ppermute x15, waiting for transfers between devices, swap(): return lax.ppermute(value, axis, [(p, p ^ step) for p in range(size)])  21.7 us
    ppermute x15, starting transfers between devices, swap(): return lax.ppermute(value, axis, [(p, p ^ step) for p in range(size)])  11.2 us
    unnamed x32, local copies, waits for them, and re-layouts  8.63 us
    all_to_all x1, starting transfers between devices, packed_shards(): lax.all_to_all(dep('h0', back[0]).reshape(seq, blocks, j_here, width), 's...  6.24 us
    all_to_all x1, starting transfers between devices, packed_shards(): lax.all_to_all(dep('H0', regrouped[0]), 'seq', 0, 0, tiled=True)  3.77 us
    all_to_all x1, waiting for transfers between devices, packed_shards(): lax.all_to_all(dep('h0', back[0]).reshape(seq, blocks, j_here, width), 's...  3.33 us
    all_to_all x1, waiting for transfers between devices, packed_shards(): lax.all_to_all(dep('H0', regrouped[0]), 'seq', 0, 0, tiled=True)  2.25 us
  transfers between devices with their start and end apart: 17, of which 9 were waited for; matrix products, arithmetic and copies ran while one was open for 0% of the time, Pallas kernels for 23%

profile of v14, /device:TPU:0, one launch (start us, length us, event | category | flops | bytes accessed | tf_op | source)
XLA Modules:
  0.0 81.5 jit_solution(15974814594866051786)
XLA Ops:
  0.6 0.0 copy-start.8
  0.6 0.8 %copy-done.8 = bf16[64,8,32]{0,2,1:T(8,128)(2,1)S(1)} copy-done((bf16[64,8,32]{0,2,1:T(8,128)(2,1)S(1)}, bf16[64,8,32]{0,2,1:T(8,128)(2,1)}, u32[]{:S(2)}) %copy-start.8) | copy-done | bytes 32792
  1.5 0.4 pack_body.1.refs_0_
  1.9 2.4 %collective-permute-start.2 = (bf16[32,512]{1,0:T(8,128)(2,1)S(1)}, bf16[32,512]{1,0:T(8,128)(2,1)S(1)}, u32[]{:S(2)}, u32[]{:S(2)}) collective-permute-start(bf16[32,512]{1,0:T(8,128)(2,1)S(1)} %pack_body.1.refs_0_), channel_id=1, source_target_pairs={{0,3},{1,2},{2,1},{3,0},{4,7},{5,6},{6,5},{7,4},{8,11},{9,10},{10,... | collective-permute-start | bytes 98312 | tf_op jit(solution)/shard_map/ppermute | solution.py:50
  4.3 0.6 collective-permute-start.1
  5.0 0.0 collective-permute-start
  5.0 0.7 copy-done.9
  5.7 1.2 %copy-done = bf16[1,2048,256]{2,1,0:T(8,128)(2,1)S(1)} copy-done((bf16[1,2048,256]{2,1,0:T(8,128)(2,1)S(1)}, bf16[1,2048,256]{2,1,0:T(8,128)(2,1)}, u32[]{:S(2)}) %copy-start) | copy-done | bytes 1048600
  6.9 1.2 %copy-done.5 = bf16[1,2048,256]{2,1,0:T(8,128)(2,1)S(1)} copy-done((bf16[1,2048,256]{2,1,0:T(8,128)(2,1)S(1)}, bf16[1,2048,256]{2,1,0:T(8,128)(2,1)}, u32[]{:S(2)}) %copy-start.5) | copy-done | bytes 1048600
  8.1 0.5 gate_body.1.refs_4_.refs_1_
  8.6 0.0 collective-permute-done.2.refs_3_
  8.6 0.0 collective-permute-done.1.refs_2_
  8.7 0.0 collective-permute-done.refs_1_
  8.7 2.2 %regroup_back_body.1 = (bf16[32,64,256]{2,1,0:T(8,128)(2,1)}, bf16[4,32,512]{2,1,0:T(8,128)(2,1)S(1)}) custom-call(bf16[32,512]{1,0:T(8,128)(2,1)S(1)} %pack_body.1.refs_0_, bf16[32,512]{1,0:T(8,128)(2,1)S(1)} %collective-permute-done.refs_1_, bf16[32,512]{1,0:T(8,128)(2,1)S(1)} %collective-permute-done.1.refs_2_, ...), custom_call_target="tpu_custom_call" | custom-call | tf_op jit(solution)/shard_map/regroup_back_body/pallas_call | solution.py:31
  10.9 0.0 copy-start.12
  10.9 6.2 %all-to-all-start.1 = ((bf16[8,4,64,256]{3,2,1,0:T(8,128)(2,1)}), bf16[8,4,64,256]{3,2,1,0:T(8,128)(2,1)S(1)}, u32[]{:S(2)}, u32[]{:S(2)}) async-start(bf16[8,4,64,256]{3,2,1,0:T(8,128)(2,1)} %bitcast.6), calls=%async_computation.1 | async-start | bytes 2097152 | tf_op jit(solution)/shard_map/all_to_all | solution.py:339
  17.1 0.0 copy-done.12
  17.1 1.6 %collective-permute-start.4 = (bf16[4,128,512]{2,1,0:T(8,128)(2,1)S(1)}, bf16[4,128,512]{2,1,0:T(8,128)(2,1)S(1)}, u32[]{:S(2)}, u32[]{:S(2)}) collective-permute-start(bf16[4,128,512]{2,1,0:T(8,128)(2,1)S(1)} %copy-done.12), channel_id=1, source_target_pairs={{0,2},{1,3},{2,0},{3,1},{4,6},{5,7},{6,4},{7,5},{8,10},{9,11},{10,... | collective-permute-start | bytes 1572872 | tf_op jit(solution)/shard_map/ppermute | solution.py:50
  18.7 0.0 collective-permute-start.3
  18.7 12.3 %collective-permute-done.4.refs_2_ = bf16[4,128,512]{2,1,0:T(8,128)(2,1)S(1)} collective-permute-done((bf16[4,128,512]{2,1,0:T(8,128)(2,1)S(1)}, bf16[4,128,512]{2,1,0:T(8,128)(2,1)S(1)}, u32[]{:S(2)}, u32[]{:S(2)}) %collective-permute-start.4) | collective-permute-done | bytes 524320 | tf_op jit(solution)/shard_map/ppermute | solution.py:50
  31.0 0.0 collective-permute-start.5
  31.0 0.0 collective-permute-done.3.refs_1_
  31.0 0.0 copy-start.14
  31.0 1.9 %collective-permute-done.5.refs_3_ = bf16[4,128,512]{2,1,0:T(8,128)(2,1)S(1)} collective-permute-done((bf16[4,128,512]{2,1,0:T(8,128)(2,1)S(1)}, bf16[4,128,512]{2,1,0:T(8,128)(2,1)S(1)}, u32[]{:S(2)}, u32[]{:S(2)}) %collective-permute-start.5) | collective-permute-done | bytes 524320 | tf_op jit(solution)/shard_map/ppermute | solution.py:50
  32.9 0.8 copy-done.15
  33.7 0.0 copy-done.13
  33.7 0.0 copy-done.14
  33.7 6.3 %mix_body.1 = (bf16[8,4,64,256]{3,2,1,0:T(8,128)(2,1)}, bf16[2048,256]{1,0:T(8,128)(2,1)}) custom-call(bf16[4,128,512]{2,1,0:T(8,128)(2,1)} %refs_0_.3, bf16[4,128,512]{2,1,0:T(8,128)(2,1)} %copy-done.14, bf16[4,128,512]{2,1,0:T(8,128)(2,1)} %copy-done.13, bf16[4,128,512]{2,1,0:T(8,128)(2,1)} %copy-done.15, bf16[2048,256]{1,0:T(8,128)(2,1)} %bitcast.15, ...), custom_call_target="tpu_custom_call" | custom-call | tf_op jit(solution)/shard_map/mix_body/pallas_call | solution.py:31
  39.9 3.3 %all-to-all-done.1.refs_0_ = bf16[8,4,64,256]{3,2,1,0:T(8,128)(2,1)S(1)} async-done(((bf16[8,4,64,256]{3,2,1,0:T(8,128)(2,1)}), bf16[8,4,64,256]{3,2,1,0:T(8,128)(2,1)S(1)}, u32[]{:S(2)}, u32[]{:S(2)}) %all-to-all-start.1) | async-done | bytes 1048608 | tf_op jit(solution)/shard_map/all_to_all | solution.py:339
  43.3 1.0 %copy-done.2 = bf16[8,4,64,256]{3,2,1,0:T(8,128)(2,1)} copy-done((bf16[8,4,64,256]{3,2,1,0:T(8,128)(2,1)}, bf16[8,4,64,256]{3,2,1,0:T(8,128)(2,1)S(1)}, u32[]{:S(2)}) %copy-start.2) | copy-done | bytes 1048600
  44.2 3.8 %all-to-all-start = ((bf16[8,4,64,256]{3,2,1,0:T(8,128)(2,1)}), bf16[8,4,64,256]{3,2,1,0:T(8,128)(2,1)S(1)}, u32[]{:S(2)}, u32[]{:S(2)}) async-start(bf16[8,4,64,256]{3,2,1,0:T(8,128)(2,1)} %get-tuple-element.30), calls=%async_computation | async-start | bytes 2097152 | tf_op jit(solution)/shard_map/all_to_all | solution.py:364
  48.0 0.0 copy-done.1
  48.0 0.0 copy-done.11
  48.0 0.0 copy-start.3
  48.0 1.2 %copy-done.3 = bf16[8,4,64,256]{3,2,1,0:T(8,128)(2,1)S(1)} copy-done((bf16[8,4,64,256]{3,2,1,0:T(8,128)(2,1)S(1)}, bf16[8,4,64,256]{3,2,1,0:T(8,128)(2,1)}, u32[]{:S(2)}) %copy-start.3) | copy-done | bytes 1048600
  49.3 2.9 %first_grad_body.1 = (bf16[4,128,512]{2,1,0:T(8,128)(2,1)S(1)}, bf16[4,128,512]{2,1,0:T(8,128)(2,1)S(1)}, bf16[4,128,512]{2,1,0:T(8,128)(2,1)S(1)}, bf16[4,128,5...) custom-call(bf16[8,4,64,256]{3,2,1,0:T(8,128)(2,1)S(1)} %copy-done.3, bf16[2048,256]{1,0:T(8,128)(2,1)S(1)} %bitcast.17, ...), custom_call_target="tpu_custom_call" | custom-call | tf_op jit(solution)/shard_map/first_grad_body/pallas_call | solution.py:31
  52.2 1.0 %copy-done.7 = bf16[4,512,256]{2,1,0:T(8,128)(2,1)} copy-done((bf16[4,512,256]{2,1,0:T(8,128)(2,1)}, bf16[4,512,256]{2,1,0:T(8,128)(2,1)S(1)}, u32[]{:S(2)}) %copy-start.7) | copy-done | bytes 1048600
  53.2 0.0 collective-permute-start.6
  53.2 0.5 collective-permute-start.7
  53.7 1.4 %collective-permute-done.6.got_a = bf16[4,128,512]{2,1,0:T(8,128)(2,1)S(1)} collective-permute-done((bf16[4,128,512]{2,1,0:T(8,128)(2,1)S(1)}, bf16[4,128,512]{2,1,0:T(8,128)(2,1)S(1)}, u32[]{:S(2)}, u32[]{:S(2)}) %collective-permute-start.6) | collective-permute-done | bytes 524320 | tf_op jit(solution)/shard_map/ppermute | solution.py:50
  55.1 0.7 collective-permute-done.7.got_b
  55.9 0.8 pair_body.1
  56.7 1.4 %collective-permute-start.9 = (bf16[128,512]{1,0:T(8,128)(2,1)}, bf16[128,512]{1,0:T(8,128)(2,1)S(1)}, u32[]{:S(2)}, u32[]{:S(2)}) collective-permute-start(bf16[128,512]{1,0:T(8,128)(2,1)} %get-tuple-element.41), channel_id=1, source_target_pairs={{0,2},{1,3},{2,0},{3,1},{4,6},{5,7},{6,4},{7,5},{8,10},{9,11},{10,... | collective-permute-start | bytes 393224 | tf_op jit(solution)/shard_map/ppermute | solution.py:50
  58.0 0.6 collective-permute-start.10
  58.7 1.4 %collective-permute-start.11 = (bf16[128,512]{1,0:T(8,128)(2,1)S(1)}, bf16[128,512]{1,0:T(8,128)(2,1)S(1)}, u32[]{:S(2)}, u32[]{:S(2)}) collective-permute-start(bf16[128,512]{1,0:T(8,128)(2,1)S(1)} %get-tuple-element.43), channel_id=1, source_target_pairs={{0,2},{1,3},{2,0},{3,1},{4,6},{5,7},{6,4},{7,5},{8,10},{9,11},{10,... | collective-permute-start | bytes 393224 | tf_op jit(solution)/shard_map/ppermute | solution.py:50
  60.1 0.6 collective-permute-start.8
  60.7 4.7 %mix_back_body.1.back_ref = bf16[2048,256]{1,0:T(8,128)(2,1)} custom-call(bf16[4,128,512]{2,1,0:T(8,128)(2,1)} %refs_0_.3, bf16[4,128,512]{2,1,0:T(8,128)(2,1)} %copy-done.14, bf16[4,128,512]{2,1,0:T(8,128)(2,1)} %copy-done.13, bf16[4,128,512]{2,1,0:T(8,128)(2,1)} %copy-done.15, bf16[4,512,256]{2,1,0:T(8,128)(2,1)} %copy-done.7), custom_call_target="tpu_custom_call" | custom-call | tf_op jit(solution)/shard_map/mix_back_body/pallas_call | solution.py:31
  65.4 0.0 collective-permute-done.9.refs_1_
  65.4 0.6 collective-permute-done.10.refs_2_
  66.0 2.8 %collective-permute-done.11.refs_3_ = bf16[128,512]{1,0:T(8,128)(2,1)S(1)} collective-permute-done((bf16[128,512]{1,0:T(8,128)(2,1)S(1)}, bf16[128,512]{1,0:T(8,128)(2,1)S(1)}, u32[]{:S(2)}, u32[]{:S(2)}) %collective-permute-start.11) | collective-permute-done | bytes 131104 | tf_op jit(solution)/shard_map/ppermute | solution.py:50
  68.8 2.0 %collective-permute-done.8.refs_0_ = bf16[128,512]{1,0:T(8,128)(2,1)S(1)} collective-permute-done((bf16[128,512]{1,0:T(8,128)(2,1)S(1)}, bf16[128,512]{1,0:T(8,128)(2,1)S(1)}, u32[]{:S(2)}, u32[]{:S(2)}) %collective-permute-start.8) | collective-permute-done | bytes 131104 | tf_op jit(solution)/shard_map/ppermute | solution.py:50
  70.8 0.9 %add_body.1 = bf16[4,128,512]{2,1,0:T(8,128)(2,1)} custom-call(f32[4,128,512]{2,1,0:T(8,128)S(1)} %get-tuple-element.40.own, bf16[128,512]{1,0:T(8,128)(2,1)S(1)} %collective-permute-done.8.refs_0_, bf16[128,512]{1,0:T(8,128)(2,1)S(1)} %collective-permute-done.9.refs_1_, bf16[128,512]{1,0:T(8,128)(2,1)S(1)} %collective-permute-done.10.refs_2_, ...), custom_call_target="tpu_custom_call" | custom-call | tf_op jit(solution)/shard_map/add_body/pallas_call | solution.py:31
  71.7 2.2 %all-to-all-done = bf16[8,4,64,256]{3,2,1,0:T(8,128)(2,1)S(1)} async-done(((bf16[8,4,64,256]{3,2,1,0:T(8,128)(2,1)}), bf16[8,4,64,256]{3,2,1,0:T(8,128)(2,1)S(1)}, u32[]{:S(2)}, u32[]{:S(2)}) %all-to-all-start) | async-done | bytes 1048608 | tf_op jit(solution)/shard_map/all_to_all | solution.py:364
  74.0 1.3 %second_grad_body.1 = (bf16[32,512]{1,0:T(8,128)(2,1)S(1)}, bf16[32,512]{1,0:T(8,128)(2,1)S(1)}, bf16[32,512]{1,0:T(8,128)(2,1)S(1)}, bf16[32,512]{1,0:T(8,128)(2,1)S(1)}) custom-call(bf16[32,64,256]{2,1,0:T(8,128)(2,1)S(1)} %bitcast.13, bf16[2048,256]{1,0:T(8,128)(2,1)S(1)} %gate_body.1.refs_4_.refs_1_), custom_call_target="tpu_custom_call" | custom-call | tf_op jit(solution)/shard_map/second_grad_body/pallas_call | solution.py:31
  75.3 0.1 collective-permute-start.12
  75.4 1.5 %collective-permute-start.13 = (bf16[32,512]{1,0:T(8,128)(2,1)S(1)}, bf16[32,512]{1,0:T(8,128)(2,1)S(1)}, u32[]{:S(2)}, u32[]{:S(2)}) collective-permute-start(bf16[32,512]{1,0:T(8,128)(2,1)S(1)} %get-tuple-element.49), channel_id=1, source_target_pairs={{0,2},{1,3},{2,0},{3,1},{4,6},{5,7},{6,4},{7,5},{8,10},{9,11},{10,... | collective-permute-start | bytes 98312 | tf_op jit(solution)/shard_map/ppermute | solution.py:50
  76.9 0.4 collective-permute-start.14
  77.3 0.0 copy-done.6
  77.3 0.7 copy-done.10
  77.9 2.5 %tokens_body.1 = bf16[2048,256]{1,0:T(8,128)(2,1)} custom-call(bf16[32,64,256]{2,1,0:T(8,128)(2,1)S(1)} %bitcast.14, bf16[4,32,512]{2,1,0:T(8,128)(2,1)S(1)} %get-tuple-element.45.second_ref, bf16[2048,256]{1,0:T(8,128)(2,1)S(1)} %copy-done.6, s32[1,256]{1,0:T(1,128)S(1)} %bitcast.23, bf16[2048,256]{1,0:T(8,128)(2,1)S(1)} %copy-done.4), custom_call_target="tpu_custom_call" | custom-call | tf_op jit(solution)/shard_map/tokens_body/pallas_call | solution.py:31
  80.4 0.0 collective-permute-done.12.refs_1_
  80.4 0.0 collective-permute-done.13.refs_2_
  80.4 0.0 collective-permute-done.14.refs_3_
  80.4 1.1 %unpack_body.1 = bf16[256,64]{1,0:T(8,128)(2,1)} custom-call(bf16[32,512]{1,0:T(8,128)(2,1)S(1)} %get-tuple-element.47.refs_0_, bf16[32,512]{1,0:T(8,128)(2,1)S(1)} %collective-permute-done.12.refs_1_, bf16[32,512]{1,0:T(8,128)(2,1)S(1)} %collective-permute-done.13.refs_2_, bf16[32,512]{1,0:T(8,128)(2,1)S(1)} %collective-permute-done.14.refs_3_), custom_call_target="tpu_custom_call" | custom-call | tf_op jit(solution)/shard_map/unpack_body/pallas_call | solution.py:31
  (13 shorter events, 0.0 us)
Async XLA Ops:
  0.6 0.8 %copy-start.8 = (bf16[64,8,32]{0,2,1:T(8,128)(2,1)S(1)}, bf16[64,8,32]{0,2,1:T(8,128)(2,1)}, u32[]{:S(2)}) copy-start(bf16[64,8,32]{0,2,1:T(8,128)(2,1)} %param.9) | copy-start | bytes 98308
  1.9 6.7 %collective-permute-start.2 = (bf16[32,512]{1,0:T(8,128)(2,1)S(1)}, bf16[32,512]{1,0:T(8,128)(2,1)S(1)}, u32[]{:S(2)}, u32[]{:S(2)}) collective-permute-start(bf16[32,512]{1,0:T(8,128)(2,1)S(1)} %pack_body.1.refs_0_), channel_id=1, source_target_pairs={{0,3},{1,2},{2,1},{3,0},{4,7},{5,6},{6,5},{7,4},{8,11},{9,10},{10,... | collective-permute-start | bytes 98312 | tf_op jit(solution)/shard_map/ppermute | solution.py:50
  4.3 4.3 %collective-permute-start.1 = (bf16[32,512]{1,0:T(8,128)(2,1)S(1)}, bf16[32,512]{1,0:T(8,128)(2,1)S(1)}, u32[]{:S(2)}, u32[]{:S(2)}) collective-permute-start(bf16[32,512]{1,0:T(8,128)(2,1)S(1)} %pack_body.1.refs_0_), channel_id=1, source_target_pairs={{0,2},{1,3},{2,0},{3,1},{4,6},{5,7},{6,4},{7,5},{8,10},{9,11},{10,... | collective-permute-start | bytes 98312 | tf_op jit(solution)/shard_map/ppermute | solution.py:50
  5.0 3.7 %collective-permute-start = (bf16[32,512]{1,0:T(8,128)(2,1)S(1)}, bf16[32,512]{1,0:T(8,128)(2,1)S(1)}, u32[]{:S(2)}, u32[]{:S(2)}) collective-permute-start(bf16[32,512]{1,0:T(8,128)(2,1)S(1)} %pack_body.1.refs_0_), channel_id=1, source_target_pairs={{0,1},{1,0},{2,3},{3,2},{4,5},{5,4},{6,7},{7,6},{8,9},{9,8},{10,11... | collective-permute-start | bytes 98312 | tf_op jit(solution)/shard_map/ppermute | solution.py:50
  5.0 0.7 copy-start.9
  5.7 1.2 %copy-start = (bf16[1,2048,256]{2,1,0:T(8,128)(2,1)S(1)}, bf16[1,2048,256]{2,1,0:T(8,128)(2,1)}, u32[]{:S(2)}) copy-start(bf16[1,2048,256]{2,1,0:T(8,128)(2,1)} %param.6) | copy-start | bytes 3145732
  6.9 1.2 %copy-start.5 = (bf16[1,2048,256]{2,1,0:T(8,128)(2,1)S(1)}, bf16[1,2048,256]{2,1,0:T(8,128)(2,1)}, u32[]{:S(2)}) copy-start(bf16[1,2048,256]{2,1,0:T(8,128)(2,1)} %param.7) | copy-start | bytes 3145732
  10.9 6.3 %copy-start.12 = (bf16[4,128,512]{2,1,0:T(8,128)(2,1)S(1)}, bf16[4,128,512]{2,1,0:T(8,128)(2,1)}, u32[]{:S(2)}) copy-start(bf16[4,128,512]{2,1,0:T(8,128)(2,1)} %refs_0_.3) | copy-start | bytes 1572868
  10.9 32.4 %all-to-all-start.1 = ((bf16[8,4,64,256]{3,2,1,0:T(8,128)(2,1)}), bf16[8,4,64,256]{3,2,1,0:T(8,128)(2,1)S(1)}, u32[]{:S(2)}, u32[]{:S(2)}) async-start(bf16[8,4,64,256]{3,2,1,0:T(8,128)(2,1)} %bitcast.6), calls=%async_computation.1 | async-start | bytes 2097152 | tf_op jit(solution)/shard_map/all_to_all | solution.py:339
  17.1 13.8 %collective-permute-start.4 = (bf16[4,128,512]{2,1,0:T(8,128)(2,1)S(1)}, bf16[4,128,512]{2,1,0:T(8,128)(2,1)S(1)}, u32[]{:S(2)}, u32[]{:S(2)}) collective-permute-start(bf16[4,128,512]{2,1,0:T(8,128)(2,1)S(1)} %copy-done.12), channel_id=1, source_target_pairs={{0,2},{1,3},{2,0},{3,1},{4,6},{5,7},{6,4},{7,5},{8,10},{9,11},{10,... | collective-permute-start | bytes 1572872 | tf_op jit(solution)/shard_map/ppermute | solution.py:50
  18.7 12.3 %collective-permute-start.3 = (bf16[4,128,512]{2,1,0:T(8,128)(2,1)S(1)}, bf16[4,128,512]{2,1,0:T(8,128)(2,1)S(1)}, u32[]{:S(2)}, u32[]{:S(2)}) collective-permute-start(bf16[4,128,512]{2,1,0:T(8,128)(2,1)S(1)} %copy-done.12), channel_id=1, source_target_pairs={{0,1},{1,0},{2,3},{3,2},{4,5},{5,4},{6,7},{7,6},{8,9},{9,8},{10,11... | collective-permute-start | bytes 1572872 | tf_op jit(solution)/shard_map/ppermute | solution.py:50
  31.0 2.7 %copy-start.13 = (bf16[4,128,512]{2,1,0:T(8,128)(2,1)}, bf16[4,128,512]{2,1,0:T(8,128)(2,1)S(1)}, u32[]{:S(2)}) copy-start(bf16[4,128,512]{2,1,0:T(8,128)(2,1)S(1)} %collective-permute-done.4.refs_2_) | copy-start | bytes 1572868
  31.0 1.9 %collective-permute-start.5 = (bf16[4,128,512]{2,1,0:T(8,128)(2,1)S(1)}, bf16[4,128,512]{2,1,0:T(8,128)(2,1)S(1)}, u32[]{:S(2)}, u32[]{:S(2)}) collective-permute-start(bf16[4,128,512]{2,1,0:T(8,128)(2,1)S(1)} %collective-permute-done.4.refs_2_), channel_id=1, source_target_pairs={{0,1},{1,0},{2,3},{3,2},{4,5},{5,4},{6,7},{7,6},{8,9},{9,8},{10,11... | collective-permute-start | bytes 1572872 | tf_op jit(solution)/shard_map/ppermute | solution.py:50
  31.0 2.7 %copy-start.14 = (bf16[4,128,512]{2,1,0:T(8,128)(2,1)}, bf16[4,128,512]{2,1,0:T(8,128)(2,1)S(1)}, u32[]{:S(2)}) copy-start(bf16[4,128,512]{2,1,0:T(8,128)(2,1)S(1)} %collective-permute-done.3.refs_1_) | copy-start | bytes 1572868
  32.9 0.8 copy-start.15
  43.3 1.0 %copy-start.2 = (bf16[8,4,64,256]{3,2,1,0:T(8,128)(2,1)}, bf16[8,4,64,256]{3,2,1,0:T(8,128)(2,1)S(1)}, u32[]{:S(2)}) copy-start(bf16[8,4,64,256]{3,2,1,0:T(8,128)(2,1)S(1)} %all-to-all-done.1.refs_0_) | copy-start | bytes 3145732
  44.2 3.8 %copy-start.1 = (bf16[1,2048,256]{2,1,0:T(8,128)(2,1)S(1)}, bf16[1,2048,256]{2,1,0:T(8,128)(2,1)}, u32[]{:S(2)}) copy-start(bf16[1,2048,256]{2,1,0:T(8,128)(2,1)} %param.6) | copy-start | bytes 3145732
  44.2 3.8 %copy-start.11 = (s32[512]{0:T(512)S(1)}, s32[512]{0:T(512)}, u32[]{:S(2)}) copy-start(s32[512]{0:T(512)} %param.11) | copy-start | bytes 6148
  44.2 29.7 %all-to-all-start = ((bf16[8,4,64,256]{3,2,1,0:T(8,128)(2,1)}), bf16[8,4,64,256]{3,2,1,0:T(8,128)(2,1)S(1)}, u32[]{:S(2)}, u32[]{:S(2)}) async-start(bf16[8,4,64,256]{3,2,1,0:T(8,128)(2,1)} %get-tuple-element.30), calls=%async_computation | async-start | bytes 2097152 | tf_op jit(solution)/shard_map/all_to_all | solution.py:364
  48.0 1.2 %copy-start.3 = (bf16[8,4,64,256]{3,2,1,0:T(8,128)(2,1)S(1)}, bf16[8,4,64,256]{3,2,1,0:T(8,128)(2,1)}, u32[]{:S(2)}) copy-start(bf16[8,4,64,256]{3,2,1,0:T(8,128)(2,1)} %copy-done.2) | copy-start | bytes 3145732
  52.2 1.0 %copy-start.7 = (bf16[4,512,256]{2,1,0:T(8,128)(2,1)}, bf16[4,512,256]{2,1,0:T(8,128)(2,1)S(1)}, u32[]{:S(2)}) copy-start(bf16[4,512,256]{2,1,0:T(8,128)(2,1)S(1)} %get-tuple-element.38.refs_4_) | copy-start | bytes 3145732
  53.2 1.9 %collective-permute-start.6 = (bf16[4,128,512]{2,1,0:T(8,128)(2,1)S(1)}, bf16[4,128,512]{2,1,0:T(8,128)(2,1)S(1)}, u32[]{:S(2)}, u32[]{:S(2)}) collective-permute-start(bf16[4,128,512]{2,1,0:T(8,128)(2,1)S(1)} %get-tuple-element.35), channel_id=1, source_target_pairs={{0,1},{1,0},{2,3},{3,2},{4,5},{5,4},{6,7},{7,6},{8,9},{9,8},{10,11... | collective-permute-start | bytes 1572872 | tf_op jit(solution)/shard_map/ppermute | solution.py:50
  53.2 2.7 %collective-permute-start.7 = (bf16[4,128,512]{2,1,0:T(8,128)(2,1)S(1)}, bf16[4,128,512]{2,1,0:T(8,128)(2,1)S(1)}, u32[]{:S(2)}, u32[]{:S(2)}) collective-permute-start(bf16[4,128,512]{2,1,0:T(8,128)(2,1)S(1)} %get-tuple-element.36), channel_id=1, source_target_pairs={{0,1},{1,0},{2,3},{3,2},{4,5},{5,4},{6,7},{7,6},{8,9},{9,8},{10,11... | collective-permute-start | bytes 1572872 | tf_op jit(solution)/shard_map/ppermute | solution.py:50
  56.7 8.8 %collective-permute-start.9 = (bf16[128,512]{1,0:T(8,128)(2,1)}, bf16[128,512]{1,0:T(8,128)(2,1)S(1)}, u32[]{:S(2)}, u32[]{:S(2)}) collective-permute-start(bf16[128,512]{1,0:T(8,128)(2,1)} %get-tuple-element.41), channel_id=1, source_target_pairs={{0,2},{1,3},{2,0},{3,1},{4,6},{5,7},{6,4},{7,5},{8,10},{9,11},{10,... | collective-permute-start | bytes 393224 | tf_op jit(solution)/shard_map/ppermute | solution.py:50
  58.0 8.0 %collective-permute-start.10 = (bf16[128,512]{1,0:T(8,128)(2,1)}, bf16[128,512]{1,0:T(8,128)(2,1)S(1)}, u32[]{:S(2)}, u32[]{:S(2)}) collective-permute-start(bf16[128,512]{1,0:T(8,128)(2,1)} %get-tuple-element.42), channel_id=1, source_target_pairs={{0,2},{1,3},{2,0},{3,1},{4,6},{5,7},{6,4},{7,5},{8,10},{9,11},{10,... | collective-permute-start | bytes 393224 | tf_op jit(solution)/shard_map/ppermute | solution.py:50
  58.7 10.1 %collective-permute-start.11 = (bf16[128,512]{1,0:T(8,128)(2,1)S(1)}, bf16[128,512]{1,0:T(8,128)(2,1)S(1)}, u32[]{:S(2)}, u32[]{:S(2)}) collective-permute-start(bf16[128,512]{1,0:T(8,128)(2,1)S(1)} %get-tuple-element.43), channel_id=1, source_target_pairs={{0,2},{1,3},{2,0},{3,1},{4,6},{5,7},{6,4},{7,5},{8,10},{9,11},{10,... | collective-permute-start | bytes 393224 | tf_op jit(solution)/shard_map/ppermute | solution.py:50
  60.1 10.8 %collective-permute-start.8 = (bf16[128,512]{1,0:T(8,128)(2,1)S(1)}, bf16[128,512]{1,0:T(8,128)(2,1)S(1)}, u32[]{:S(2)}, u32[]{:S(2)}) collective-permute-start(bf16[128,512]{1,0:T(8,128)(2,1)S(1)} %get-tuple-element.37), channel_id=1, source_target_pairs={{0,2},{1,3},{2,0},{3,1},{4,6},{5,7},{6,4},{7,5},{8,10},{9,11},{10,... | collective-permute-start | bytes 393224 | tf_op jit(solution)/shard_map/ppermute | solution.py:50
  74.0 3.3 %copy-start.4 = (bf16[2048,256]{1,0:T(8,128)(2,1)S(1)}, bf16[2048,256]{1,0:T(8,128)(2,1)}, u32[]{:S(2)}) copy-start(bf16[2048,256]{1,0:T(8,128)(2,1)} %mix_back_body.1.back_ref) | copy-start | bytes 3145732
  74.0 3.3 %copy-start.6 = (bf16[2048,256]{1,0:T(8,128)(2,1)S(1)}, bf16[2048,256]{1,0:T(8,128)(2,1)}, u32[]{:S(2)}) copy-start(bf16[2048,256]{1,0:T(8,128)(2,1)} %get-tuple-element.46.h_ref) | copy-start | bytes 3145732
  75.3 5.1 %collective-permute-start.12 = (bf16[32,512]{1,0:T(8,128)(2,1)S(1)}, bf16[32,512]{1,0:T(8,128)(2,1)S(1)}, u32[]{:S(2)}, u32[]{:S(2)}) collective-permute-start(bf16[32,512]{1,0:T(8,128)(2,1)S(1)} %get-tuple-element.48), channel_id=1, source_target_pairs={{0,1},{1,0},{2,3},{3,2},{4,5},{5,4},{6,7},{7,6},{8,9},{9,8},{10,11... | collective-permute-start | bytes 98312 | tf_op jit(solution)/shard_map/ppermute | solution.py:50
  75.4 5.0 %collective-permute-start.13 = (bf16[32,512]{1,0:T(8,128)(2,1)S(1)}, bf16[32,512]{1,0:T(8,128)(2,1)S(1)}, u32[]{:S(2)}, u32[]{:S(2)}) collective-permute-start(bf16[32,512]{1,0:T(8,128)(2,1)S(1)} %get-tuple-element.49), channel_id=1, source_target_pairs={{0,2},{1,3},{2,0},{3,1},{4,6},{5,7},{6,4},{7,5},{8,10},{9,11},{10,... | collective-permute-start | bytes 98312 | tf_op jit(solution)/shard_map/ppermute | solution.py:50
  76.9 3.6 %collective-permute-start.14 = (bf16[32,512]{1,0:T(8,128)(2,1)S(1)}, bf16[32,512]{1,0:T(8,128)(2,1)S(1)}, u32[]{:S(2)}, u32[]{:S(2)}) collective-permute-start(bf16[32,512]{1,0:T(8,128)(2,1)S(1)} %get-tuple-element.50), channel_id=1, source_target_pairs={{0,3},{1,2},{2,1},{3,0},{4,7},{5,6},{6,5},{7,4},{8,11},{9,10},{10,... | collective-permute-start | bytes 98312 | tf_op jit(solution)/shard_map/ppermute | solution.py:50
  77.3 0.7 copy-start.10

commit v15 on v14

--- a/solution.py
+++ b/solution.py
@@ -48,6 +48,14 @@
 
 def swap(value, axis, step, size):
     return lax.ppermute(value, axis, [(p, p ^ step) for p in range(size)])
+
+
+def ring_at(place, size):
+    return jnp.where(place < size // 2, 2 * place, 2 * size - 1 - 2 * place)
+
+
+def ring_of(size):
+    return [2 * p if p < size // 2 else 2 * size - 1 - 2 * p for p in range(size)]
 
 
 def after(value, *earlier):
@@ -95,18 +103,26 @@
     tiled = one_hot((iota((order, lanes), 1) % order) == iota((order, lanes), 0))
     keep = (iota((lanes, lanes), 0) % LANE_GROUP) == (iota((lanes, lanes), 1) // order)
     writes = []
+    blocks = order // seq
+    part = lanes // seq
     for g in range(groups):
-        packed = d_scr[g].astype(BF16)
-        second_ref[g] = packed
+        wide = d_scr[g]
+        packed = wide.astype(BF16)
+        ringed = [wide[:, there * part : (there + 1) * part] for there in ring_of(seq)]
+        second_ref[g] = jnp.concatenate(ringed, axis=1).astype(BF16)
         weights = jnp.where(keep, dot(packed, tiled, 0, 0), 0.0).astype(BF16)
         result = dot(weights, dz_ref[g * lanes : (g + 1) * lanes, :]).astype(BF16)
         js = slice(g * LANE_GROUP, (g + 1) * LANE_GROUP)
         r_scr[:, js, :] = result.reshape(order, LANE_GROUP, width)
         if len(outs) == 1:
-            writes.append(pltpu.make_async_copy(r_scr.at[:, js, :], outs[0].at[:, js, :], sems.at[g]))
-            writes[g].start()
-
-    blocks = order // seq
+            for p, there in enumerate(ring_of(seq)):
+                source, target = pl.ds(there * blocks, blocks), pl.ds(p * blocks, blocks)
+                write = pltpu.make_async_copy(
+                    r_scr.at[source, js, :], outs[0].at[target, js, :], sems.at[g, p]
+                )
+                write.start()
+                writes.append(write)
+
     if len(outs) == 1:
         for write in writes:
             write.wait()
@@ -135,8 +151,10 @@
         result = dot(p_scr[...], mix_scr[...]).astype(BF16)
         if len(outs) == 1:
             reg_scr[i] = result.reshape(seq, j_here, width)
-            writes.append(pltpu.make_async_copy(reg_scr.at[i], outs[0].at[:, i], sems.at[i]))
-            writes[i].start()
+            for p, there in enumerate(ring_of(seq)):
+                write = pltpu.make_async_copy(reg_scr.at[i, there], outs[0].at[p, i], sems.at[i, p])
+                write.start()
+                writes.append(write)
         else:
             reg_scr[i] = result.reshape(seq, j_here, width)
             for d in range(seq):
@@ -162,7 +180,8 @@
     @pl.loop(0, blocks)
     def _(i):
         if count == 1:
-            reg_scr[...] = pieces[0][:, i].reshape(order, width)
+            for p, there in enumerate(ring_of(seq)):
+                reg_scr[there * j_here : (there + 1) * j_here, :] = pieces[0][p, i]
         else:
             for d in range(seq):
                 first = pl.multiple_of((here ^ d) * j_here, j_here)
@@ -235,13 +254,12 @@
     groups, lanes = j_here // LANE_GROUP, order * LANE_GROUP
     select = one_hot(iota((width, width), 0) == src_ref[...])
     col = iota((order, lanes), 1) % LANE_GROUP
+    masks = [one_hot(col == jj) for jj in range(LANE_GROUP)]
     writes = []
     for g in range(groups):
         reg = reg_ref[:, g * LANE_GROUP : (g + 1) * LANE_GROUP, :].reshape(lanes, width)
-        packed = second_ref[g].astype(F32)
-        weights = jnp.concatenate(
-            [jnp.where(col == jj, packed, 0.0).astype(BF16) for jj in range(LANE_GROUP)], axis=0
-        )
+        packed = second_ref[g]
+        weights = jnp.concatenate([packed * mask for mask in masks], axis=0)
         rows = slice(g * lanes, (g + 1) * lanes)
         dgate = (dot(weights, reg) * h_ref[rows, :].astype(F32)).astype(BF16)
         out_ref[rows, :] = (back_ref[rows, :].astype(F32) + dot(dgate, select, 1, 1)).astype(BF16)
@@ -269,7 +287,7 @@
         refs[-1][n] = (own[n] + got[...].astype(F32)).astype(BF16)
 
 
-def unpack_body(order, *refs):
+def unpack_body(order, seq, *refs):
     pieces, out_ref = refs[:-1], refs[-1]
     rows, j_here = out_ref.shape
     groups, lanes, m_here = j_here // LANE_GROUP, order * LANE_GROUP, rows // order
@@ -277,7 +295,9 @@
     for piece in pieces[1:]:
         total = total + piece[...].astype(F32)
     lane = iota((j_here, lanes), 1)
-    keep = (iota((rows, lanes), 0) % order) == (iota((rows, lanes), 1) // LANE_GROUP)
+    blocks = order // seq
+    place_i = iota((rows, lanes), 1) // LANE_GROUP
+    keep = (iota((rows, lanes), 0) % order) == ring_at(place_i // blocks, seq) * blocks + place_i % blocks
     result = jnp.zeros((rows, j_here), F32)
     for g in range(groups):
         place = one_hot(iota((j_here, lanes), 0) == g * LANE_GROUP + lane % LANE_GROUP)
@@ -324,7 +344,7 @@
         [
             pltpu.VMEM((groups, count, lanes), F32),
             pltpu.VMEM((count, j_here, width), BF16),
-            pltpu.SemaphoreType.DMA((groups,)),
+            pltpu.SemaphoreType.DMA((groups, seq)),
         ],
         far_outs=(0,) if CFG['a2a'][0] else (),
         limit=24 << 20,
@@ -337,7 +357,7 @@
     back_got = {0: back[0]}
     if CFG['a2a'][0]:
         back_got[0] = keep("h0", lax.all_to_all(
-            dep("h0", back[0]).reshape(seq, blocks, j_here, width), "seq", 0, 0, tiled=True
+            dep("h0", back[0]).reshape(seq, blocks, j_here, width), "seq", 0, 0, axis_index_groups=[ring_of(seq)], tiled=True
         ))
     else:
         for d in CFG['order'][0]:
@@ -353,7 +373,7 @@
             pltpu.VMEM((order, order), BF16),
             pltpu.VMEM((order, width), BF16),
             pltpu.VMEM((blocks, seq, j_here, width), BF16),
-            pltpu.SemaphoreType.DMA((blocks,)),
+            pltpu.SemaphoreType.DMA((blocks, seq)),
         ],
         far_outs=(0,) if CFG['a2a'][1] else (),
         limit=CFG['limit'],
@@ -361,7 +381,9 @@
     keep("M", regrouped[0])
     got = {0: regrouped[0]}
     if CFG['a2a'][1]:
-        got[0] = keep("H0", lax.all_to_all(dep("H0", regrouped[0]), "seq", 0, 0, tiled=True))
+        got[0] = keep("H0", lax.all_to_all(
+            dep("H0", regrouped[0]), "seq", 0, 0, axis_index_groups=[ring_of(seq)], tiled=True
+        ))
     else:
         for d in CFG['order'][1]:
             got[d] = move(f"H{d}", regrouped[d], "seq", d, seq)
@@ -418,7 +440,7 @@
         far_outs=(0,),
     )
     (grad_flat,) = call(
-        functools.partial(unpack_body, count), [of((m_here * count, j_here))], terms_got
+        functools.partial(unpack_body, count, seq), [of((m_here * count, j_here))], terms_got
     )
     grad_two = jnp.transpose(grad_flat.reshape(m_here, count, j_here), (2, 0, 1))
     return (grad_tokens[None], grad_one, grad_two)

time: 82 us -> 80.3 us (0.979)
  the two profiles are of different devices: /device:TPU:0 before, /device:TPU:9 now
where the time goes in v15:
time: 80.3 us; the launch traced here: 79.8 us
  Pallas kernels  24.1 us (30%)
  starting transfers between devices  23.4 us (29%)
  waiting for transfers between devices  22.9 us (29%)
  local copies, waits for them, and re-layouts  8.62 us (11%)
  between operations  0.82 us (1%)
    pallas_call x11, Pallas kernels, call(): pl.pallas_call(body, name=name, out_shape=outs, in_specs=[pl.BlockSpec(me...  24.1 us
    ppermute x15, waiting for transfers between devices, swap(): return lax.ppermute(value, axis, [(p, p ^ step) for p in range(size)])  19.8 us
    ppermute x15, starting transfers between devices, swap(): return lax.ppermute(value, axis, [(p, p ^ step) for p in range(size)])  13.9 us
    unnamed x32, local copies, waits for them, and re-layouts  8.62 us
    all_to_all x1, starting transfers between devices, packed_shards(): lax.all_to_all(dep('h0', back[0]).reshape(seq, blocks, j_here, width), 's...  5.86 us
    all_to_all x1, starting transfers between devices, packed_shards(): lax.all_to_all(dep('H0', regrouped[0]), 'seq', 0, 0, axis_index_groups=[r...  3.64 us
    all_to_all x1, waiting for transfers between devices, packed_shards(): lax.all_to_all(dep('h0', back[0]).reshape(seq, blocks, j_here, width), 's...  1.95 us
  transfers between devices with their start and end apart: 17, of which 9 were waited for; matrix products, arithmetic and copies ran while one was open for 0% of the time, Pallas kernels for 24%

profile of v15, /device:TPU:9, one launch (start us, length us, event | category | flops | bytes accessed | tf_op | source)
XLA Modules:
  0.0 79.8 jit_solution(16270537598844452493)
XLA Ops:
  0.6 0.0 copy-start.8
  0.6 0.8 %copy-done.8 = bf16[64,8,32]{0,2,1:T(8,128)(2,1)S(1)} copy-done((bf16[64,8,32]{0,2,1:T(8,128)(2,1)S(1)}, bf16[64,8,32]{0,2,1:T(8,128)(2,1)}, u32[]{:S(2)}) %copy-start.8) | copy-done | bytes 32792
  1.5 0.4 pack_body.1.refs_0_
  1.9 1.8 %collective-permute-start.2 = (bf16[32,512]{1,0:T(8,128)(2,1)S(1)}, bf16[32,512]{1,0:T(8,128)(2,1)S(1)}, u32[]{:S(2)}, u32[]{:S(2)}) collective-permute-start(bf16[32,512]{1,0:T(8,128)(2,1)S(1)} %pack_body.1.refs_0_), channel_id=1, source_target_pairs={{0,3},{1,2},{2,1},{3,0},{4,7},{5,6},{6,5},{7,4},{8,11},{9,10},{10,... | collective-permute-start | bytes 98312 | tf_op jit(solution)/shard_map/ppermute | solution.py:50
  3.7 0.3 collective-permute-start.1
  4.0 0.2 collective-permute-start
  4.2 0.7 copy-done.9
  4.9 1.2 %copy-done = bf16[1,2048,256]{2,1,0:T(8,128)(2,1)S(1)} copy-done((bf16[1,2048,256]{2,1,0:T(8,128)(2,1)S(1)}, bf16[1,2048,256]{2,1,0:T(8,128)(2,1)}, u32[]{:S(2)}) %copy-start) | copy-done | bytes 1048600
  6.1 1.2 %copy-done.5 = bf16[1,2048,256]{2,1,0:T(8,128)(2,1)S(1)} copy-done((bf16[1,2048,256]{2,1,0:T(8,128)(2,1)S(1)}, bf16[1,2048,256]{2,1,0:T(8,128)(2,1)}, u32[]{:S(2)}) %copy-start.5) | copy-done | bytes 1048600
  7.3 0.5 gate_body.1.refs_4_.refs_1_
  7.8 0.0 collective-permute-done.2.refs_3_
  7.8 0.0 collective-permute-done.1.refs_2_
  7.8 0.0 collective-permute-done.refs_1_
  7.9 2.4 %regroup_back_body.1 = (bf16[32,64,256]{2,1,0:T(8,128)(2,1)}, bf16[4,32,512]{2,1,0:T(8,128)(2,1)S(1)}) custom-call(bf16[32,512]{1,0:T(8,128)(2,1)S(1)} %pack_body.1.refs_0_, bf16[32,512]{1,0:T(8,128)(2,1)S(1)} %collective-permute-done.refs_1_, bf16[32,512]{1,0:T(8,128)(2,1)S(1)} %collective-permute-done.1.refs_2_, ...), custom_call_target="tpu_custom_call" | custom-call | tf_op jit(solution)/shard_map/regroup_back_body/pallas_call | solution.py:31
  10.3 0.0 copy-start.12
  10.3 5.9 %all-to-all-start.1 = ((bf16[8,4,64,256]{3,2,1,0:T(8,128)(2,1)}), bf16[8,4,64,256]{3,2,1,0:T(8,128)(2,1)S(1)}, u32[]{:S(2)}, u32[]{:S(2)}) async-start(bf16[8,4,64,256]{3,2,1,0:T(8,128)(2,1)} %bitcast.6), calls=%async_computation.1 | async-start | bytes 2097152 | tf_op jit(solution)/shard_map/all_to_all | solution.py:359
  16.2 0.0 copy-done.12
  16.2 1.1 %collective-permute-start.4 = (bf16[4,128,512]{2,1,0:T(8,128)(2,1)S(1)}, bf16[4,128,512]{2,1,0:T(8,128)(2,1)S(1)}, u32[]{:S(2)}, u32[]{:S(2)}) collective-permute-start(bf16[4,128,512]{2,1,0:T(8,128)(2,1)S(1)} %copy-done.12), channel_id=1, source_target_pairs={{0,2},{1,3},{2,0},{3,1},{4,6},{5,7},{6,4},{7,5},{8,10},{9,11},{10,... | collective-permute-start | bytes 1572872 | tf_op jit(solution)/shard_map/ppermute | solution.py:50
  17.3 1.2 %collective-permute-start.3 = (bf16[4,128,512]{2,1,0:T(8,128)(2,1)S(1)}, bf16[4,128,512]{2,1,0:T(8,128)(2,1)S(1)}, u32[]{:S(2)}, u32[]{:S(2)}) collective-permute-start(bf16[4,128,512]{2,1,0:T(8,128)(2,1)S(1)} %copy-done.12), channel_id=1, source_target_pairs={{0,1},{1,0},{2,3},{3,2},{4,5},{5,4},{6,7},{7,6},{8,9},{9,8},{10,11... | collective-permute-start | bytes 1572872 | tf_op jit(solution)/shard_map/ppermute | solution.py:50
  18.5 10.2 %collective-permute-done.4.refs_2_ = bf16[4,128,512]{2,1,0:T(8,128)(2,1)S(1)} collective-permute-done((bf16[4,128,512]{2,1,0:T(8,128)(2,1)S(1)}, bf16[4,128,512]{2,1,0:T(8,128)(2,1)S(1)}, u32[]{:S(2)}, u32[]{:S(2)}) %collective-permute-start.4) | collective-permute-done | bytes 524320 | tf_op jit(solution)/shard_map/ppermute | solution.py:50
  28.8 1.8 %collective-permute-start.5 = (bf16[4,128,512]{2,1,0:T(8,128)(2,1)S(1)}, bf16[4,128,512]{2,1,0:T(8,128)(2,1)S(1)}, u32[]{:S(2)}, u32[]{:S(2)}) collective-permute-start(bf16[4,128,512]{2,1,0:T(8,128)(2,1)S(1)} %collective-permute-done.4.refs_2_), channel_id=1, source_target_pairs={{0,1},{1,0},{2,3},{3,2},{4,5},{5,4},{6,7},{7,6},{8,9},{9,8},{10,11... | collective-permute-start | bytes 1572872 | tf_op jit(solution)/shard_map/ppermute | solution.py:50
  30.5 0.0 collective-permute-done.3.refs_1_
  30.5 1.5 %collective-permute-done.5.refs_3_ = bf16[4,128,512]{2,1,0:T(8,128)(2,1)S(1)} collective-permute-done((bf16[4,128,512]{2,1,0:T(8,128)(2,1)S(1)}, bf16[4,128,512]{2,1,0:T(8,128)(2,1)S(1)}, u32[]{:S(2)}, u32[]{:S(2)}) %collective-permute-start.5) | collective-permute-done | bytes 524320 | tf_op jit(solution)/shard_map/ppermute | solution.py:50
  32.1 0.8 copy-done.15
  32.9 0.0 copy-done.13
  32.9 0.0 copy-done.14
  32.9 6.5 %mix_body.1 = (bf16[8,4,64,256]{3,2,1,0:T(8,128)(2,1)}, bf16[2048,256]{1,0:T(8,128)(2,1)}) custom-call(bf16[4,128,512]{2,1,0:T(8,128)(2,1)} %refs_0_.3, bf16[4,128,512]{2,1,0:T(8,128)(2,1)} %copy-done.14, bf16[4,128,512]{2,1,0:T(8,128)(2,1)} %copy-done.13, bf16[4,128,512]{2,1,0:T(8,128)(2,1)} %copy-done.15, bf16[2048,256]{1,0:T(8,128)(2,1)} %bitcast.15, ...), custom_call_target="tpu_custom_call" | custom-call | tf_op jit(solution)/shard_map/mix_body/pallas_call | solution.py:31
  39.4 1.9 %all-to-all-done.1.refs_0_ = bf16[8,4,64,256]{3,2,1,0:T(8,128)(2,1)S(1)} async-done(((bf16[8,4,64,256]{3,2,1,0:T(8,128)(2,1)}), bf16[8,4,64,256]{3,2,1,0:T(8,128)(2,1)S(1)}, u32[]{:S(2)}, u32[]{:S(2)}) %all-to-all-start.1) | async-done | bytes 1048608 | tf_op jit(solution)/shard_map/all_to_all | solution.py:359
  41.3 1.0 %copy-done.2 = bf16[8,4,64,256]{3,2,1,0:T(8,128)(2,1)} copy-done((bf16[8,4,64,256]{3,2,1,0:T(8,128)(2,1)}, bf16[8,4,64,256]{3,2,1,0:T(8,128)(2,1)S(1)}, u32[]{:S(2)}) %copy-start.2) | copy-done | bytes 1048600
  42.3 3.6 %all-to-all-start = ((bf16[8,4,64,256]{3,2,1,0:T(8,128)(2,1)}), bf16[8,4,64,256]{3,2,1,0:T(8,128)(2,1)S(1)}, u32[]{:S(2)}, u32[]{:S(2)}) async-start(bf16[8,4,64,256]{3,2,1,0:T(8,128)(2,1)} %get-tuple-element.30), calls=%async_computation | async-start | bytes 2097152 | tf_op jit(solution)/shard_map/all_to_all | solution.py:384
  46.0 0.0 copy-done.1
  46.0 0.0 copy-done.11
  46.0 0.0 copy-start.3
  46.0 1.2 %copy-done.3 = bf16[8,4,64,256]{3,2,1,0:T(8,128)(2,1)S(1)} copy-done((bf16[8,4,64,256]{3,2,1,0:T(8,128)(2,1)S(1)}, bf16[8,4,64,256]{3,2,1,0:T(8,128)(2,1)}, u32[]{:S(2)}) %copy-start.3) | copy-done | bytes 1048600
  47.2 3.0 %first_grad_body.1 = (bf16[4,128,512]{2,1,0:T(8,128)(2,1)S(1)}, bf16[4,128,512]{2,1,0:T(8,128)(2,1)S(1)}, bf16[4,128,512]{2,1,0:T(8,128)(2,1)S(1)}, bf16[4,128,5...) custom-call(bf16[8,4,64,256]{3,2,1,0:T(8,128)(2,1)S(1)} %copy-done.3, bf16[2048,256]{1,0:T(8,128)(2,1)S(1)} %bitcast.17, ...), custom_call_target="tpu_custom_call" | custom-call | tf_op jit(solution)/shard_map/first_grad_body/pallas_call | solution.py:31
  50.2 0.0 copy-start.7
  50.2 1.0 %copy-done.7 = bf16[4,512,256]{2,1,0:T(8,128)(2,1)} copy-done((bf16[4,512,256]{2,1,0:T(8,128)(2,1)}, bf16[4,512,256]{2,1,0:T(8,128)(2,1)S(1)}, u32[]{:S(2)}) %copy-start.7) | copy-done | bytes 1048600
  51.1 1.3 %collective-permute-start.6 = (bf16[4,128,512]{2,1,0:T(8,128)(2,1)S(1)}, bf16[4,128,512]{2,1,0:T(8,128)(2,1)S(1)}, u32[]{:S(2)}, u32[]{:S(2)}) collective-permute-start(bf16[4,128,512]{2,1,0:T(8,128)(2,1)S(1)} %get-tuple-element.35), channel_id=1, source_target_pairs={{0,1},{1,0},{2,3},{3,2},{4,5},{5,4},{6,7},{7,6},{8,9},{9,8},{10,11... | collective-permute-start | bytes 1572872 | tf_op jit(solution)/shard_map/ppermute | solution.py:50
  52.5 0.0 collective-permute-start.7
  52.5 1.5 %collective-permute-done.6.got_a = bf16[4,128,512]{2,1,0:T(8,128)(2,1)S(1)} collective-permute-done((bf16[4,128,512]{2,1,0:T(8,128)(2,1)S(1)}, bf16[4,128,512]{2,1,0:T(8,128)(2,1)S(1)}, u32[]{:S(2)}, u32[]{:S(2)}) %collective-permute-start.6) | collective-permute-done | bytes 524320 | tf_op jit(solution)/shard_map/ppermute | solution.py:50
  54.0 0.7 collective-permute-done.7.got_b
  54.8 0.8 %pair_body.1 = (f32[4,128,512]{2,1,0:T(8,128)S(1)}, bf16[128,512]{1,0:T(8,128)(2,1)S(1)}, bf16[128,512]{1,0:T(8,128)(2,1)}, bf16[128,512]{1,0:T(8,128)(2,1)}, bf16[128,512]{1,0:T(8,128)(2,1)S(1)}) custom-call(bf16[4,128,512]{2,1,0:T(8,128)(2,1)S(1)} %get-tuple-element.33.own_a, bf16[4,128,512]{2,1,0:T(8,128)(2,1)S(1)} %get-tuple-element.34.own_b, ...), custom_call_target="tpu_custom_call" | custom-call | tf_op jit(solution)/shard_map/pair_body/pallas_call | solution.py:31
  55.6 1.1 %collective-permute-start.9 = (bf16[128,512]{1,0:T(8,128)(2,1)}, bf16[128,512]{1,0:T(8,128)(2,1)S(1)}, u32[]{:S(2)}, u32[]{:S(2)}) collective-permute-start(bf16[128,512]{1,0:T(8,128)(2,1)} %get-tuple-element.41), channel_id=1, source_target_pairs={{0,2},{1,3},{2,0},{3,1},{4,6},{5,7},{6,4},{7,5},{8,10},{9,11},{10,... | collective-permute-start | bytes 393224 | tf_op jit(solution)/shard_map/ppermute | solution.py:50
  56.7 0.4 collective-permute-start.10
  57.0 1.1 %collective-permute-start.11 = (bf16[128,512]{1,0:T(8,128)(2,1)S(1)}, bf16[128,512]{1,0:T(8,128)(2,1)S(1)}, u32[]{:S(2)}, u32[]{:S(2)}) collective-permute-start(bf16[128,512]{1,0:T(8,128)(2,1)S(1)} %get-tuple-element.43), channel_id=1, source_target_pairs={{0,2},{1,3},{2,0},{3,1},{4,6},{5,7},{6,4},{7,5},{8,10},{9,11},{10,... | collective-permute-start | bytes 393224 | tf_op jit(solution)/shard_map/ppermute | solution.py:50
  58.2 0.4 collective-permute-start.8
  58.5 4.7 %mix_back_body.1.back_ref = bf16[2048,256]{1,0:T(8,128)(2,1)} custom-call(bf16[4,128,512]{2,1,0:T(8,128)(2,1)} %refs_0_.3, bf16[4,128,512]{2,1,0:T(8,128)(2,1)} %copy-done.14, bf16[4,128,512]{2,1,0:T(8,128)(2,1)} %copy-done.13, bf16[4,128,512]{2,1,0:T(8,128)(2,1)} %copy-done.15, bf16[4,512,256]{2,1,0:T(8,128)(2,1)} %copy-done.7), custom_call_target="tpu_custom_call" | custom-call | tf_op jit(solution)/shard_map/mix_back_body/pallas_call | solution.py:31
  63.2 0.0 collective-permute-done.9.refs_1_
  63.2 0.1 collective-permute-done.10.refs_2_
  63.3 2.8 %collective-permute-done.11.refs_3_ = bf16[128,512]{1,0:T(8,128)(2,1)S(1)} collective-permute-done((bf16[128,512]{1,0:T(8,128)(2,1)S(1)}, bf16[128,512]{1,0:T(8,128)(2,1)S(1)}, u32[]{:S(2)}, u32[]{:S(2)}) %collective-permute-start.11) | collective-permute-done | bytes 131104 | tf_op jit(solution)/shard_map/ppermute | solution.py:50
  66.1 2.8 %collective-permute-done.8.refs_0_ = bf16[128,512]{1,0:T(8,128)(2,1)S(1)} collective-permute-done((bf16[128,512]{1,0:T(8,128)(2,1)S(1)}, bf16[128,512]{1,0:T(8,128)(2,1)S(1)}, u32[]{:S(2)}, u32[]{:S(2)}) %collective-permute-start.8) | collective-permute-done | bytes 131104 | tf_op jit(solution)/shard_map/ppermute | solution.py:50
  68.9 0.9 %add_body.1 = bf16[4,128,512]{2,1,0:T(8,128)(2,1)} custom-call(f32[4,128,512]{2,1,0:T(8,128)S(1)} %get-tuple-element.40.own, bf16[128,512]{1,0:T(8,128)(2,1)S(1)} %collective-permute-done.8.refs_0_, bf16[128,512]{1,0:T(8,128)(2,1)S(1)} %collective-permute-done.9.refs_1_, bf16[128,512]{1,0:T(8,128)(2,1)S(1)} %collective-permute-done.10.refs_2_, ...), custom_call_target="tpu_custom_call" | custom-call | tf_op jit(solution)/shard_map/add_body/pallas_call | solution.py:31
  69.8 1.2 %all-to-all-done = bf16[8,4,64,256]{3,2,1,0:T(8,128)(2,1)S(1)} async-done(((bf16[8,4,64,256]{3,2,1,0:T(8,128)(2,1)}), bf16[8,4,64,256]{3,2,1,0:T(8,128)(2,1)S(1)}, u32[]{:S(2)}, u32[]{:S(2)}) %all-to-all-start) | async-done | bytes 1048608 | tf_op jit(solution)/shard_map/all_to_all | solution.py:384
  71.0 1.3 %second_grad_body.1 = (bf16[32,512]{1,0:T(8,128)(2,1)S(1)}, bf16[32,512]{1,0:T(8,128)(2,1)S(1)}, bf16[32,512]{1,0:T(8,128)(2,1)S(1)}, bf16[32,512]{1,0:T(8,128)(2,1)S(1)}) custom-call(bf16[32,64,256]{2,1,0:T(8,128)(2,1)S(1)} %bitcast.13, bf16[2048,256]{1,0:T(8,128)(2,1)S(1)} %gate_body.1.refs_4_.refs_1_), custom_call_target="tpu_custom_call" | custom-call | tf_op jit(solution)/shard_map/second_grad_body/pallas_call | solution.py:31
  72.3 1.5 %collective-permute-start.12 = (bf16[32,512]{1,0:T(8,128)(2,1)S(1)}, bf16[32,512]{1,0:T(8,128)(2,1)S(1)}, u32[]{:S(2)}, u32[]{:S(2)}) collective-permute-start(bf16[32,512]{1,0:T(8,128)(2,1)S(1)} %get-tuple-element.48), channel_id=1, source_target_pairs={{0,1},{1,0},{2,3},{3,2},{4,5},{5,4},{6,7},{7,6},{8,9},{9,8},{10,11... | collective-permute-start | bytes 98312 | tf_op jit(solution)/shard_map/ppermute | solution.py:50
  73.8 1.1 %collective-permute-start.13 = (bf16[32,512]{1,0:T(8,128)(2,1)S(1)}, bf16[32,512]{1,0:T(8,128)(2,1)S(1)}, u32[]{:S(2)}, u32[]{:S(2)}) collective-permute-start(bf16[32,512]{1,0:T(8,128)(2,1)S(1)} %get-tuple-element.49), channel_id=1, source_target_pairs={{0,2},{1,3},{2,0},{3,1},{4,6},{5,7},{6,4},{7,5},{8,10},{9,11},{10,... | collective-permute-start | bytes 98312 | tf_op jit(solution)/shard_map/ppermute | solution.py:50
  75.0 0.6 collective-permute-start.14
  75.6 0.0 copy-done.4
  75.6 0.7 copy-done.10
  76.2 2.5 %tokens_body.1 = bf16[2048,256]{1,0:T(8,128)(2,1)} custom-call(bf16[32,64,256]{2,1,0:T(8,128)(2,1)S(1)} %bitcast.14, bf16[4,32,512]{2,1,0:T(8,128)(2,1)S(1)} %get-tuple-element.45.second_ref, bf16[2048,256]{1,0:T(8,128)(2,1)S(1)} %copy-done.6, s32[1,256]{1,0:T(1,128)S(1)} %bitcast.23, bf16[2048,256]{1,0:T(8,128)(2,1)S(1)} %copy-done.4), custom_call_target="tpu_custom_call" | custom-call | tf_op jit(solution)/shard_map/tokens_body/pallas_call | solution.py:31
  78.7 0.0 collective-permute-done.12.refs_1_
  78.7 0.0 collective-permute-done.13.refs_2_
  78.7 0.0 collective-permute-done.14.refs_3_
  78.7 1.1 %unpack_body.1 = bf16[256,64]{1,0:T(8,128)(2,1)} custom-call(bf16[32,512]{1,0:T(8,128)(2,1)S(1)} %get-tuple-element.47.refs_0_, bf16[32,512]{1,0:T(8,128)(2,1)S(1)} %collective-permute-done.12.refs_1_, bf16[32,512]{1,0:T(8,128)(2,1)S(1)} %collective-permute-done.13.refs_2_, bf16[32,512]{1,0:T(8,128)(2,1)S(1)} %collective-permute-done.14.refs_3_), custom_call_target="tpu_custom_call" | custom-call | tf_op jit(solution)/shard_map/unpack_body/pallas_call | solution.py:31
  (13 shorter events, 0.0 us)
Async XLA Ops:
  0.6 0.8 %copy-start.8 = (bf16[64,8,32]{0,2,1:T(8,128)(2,1)S(1)}, bf16[64,8,32]{0,2,1:T(8,128)(2,1)}, u32[]{:S(2)}) copy-start(bf16[64,8,32]{0,2,1:T(8,128)(2,1)} %param.9) | copy-start | bytes 98308
  1.9 5.9 %collective-permute-start.2 = (bf16[32,512]{1,0:T(8,128)(2,1)S(1)}, bf16[32,512]{1,0:T(8,128)(2,1)S(1)}, u32[]{:S(2)}, u32[]{:S(2)}) collective-permute-start(bf16[32,512]{1,0:T(8,128)(2,1)S(1)} %pack_body.1.refs_0_), channel_id=1, source_target_pairs={{0,3},{1,2},{2,1},{3,0},{4,7},{5,6},{6,5},{7,4},{8,11},{9,10},{10,... | collective-permute-start | bytes 98312 | tf_op jit(solution)/shard_map/ppermute | solution.py:50
  3.7 4.1 %collective-permute-start.1 = (bf16[32,512]{1,0:T(8,128)(2,1)S(1)}, bf16[32,512]{1,0:T(8,128)(2,1)S(1)}, u32[]{:S(2)}, u32[]{:S(2)}) collective-permute-start(bf16[32,512]{1,0:T(8,128)(2,1)S(1)} %pack_body.1.refs_0_), channel_id=1, source_target_pairs={{0,2},{1,3},{2,0},{3,1},{4,6},{5,7},{6,4},{7,5},{8,10},{9,11},{10,... | collective-permute-start | bytes 98312 | tf_op jit(solution)/shard_map/ppermute | solution.py:50
  4.0 3.9 %collective-permute-start = (bf16[32,512]{1,0:T(8,128)(2,1)S(1)}, bf16[32,512]{1,0:T(8,128)(2,1)S(1)}, u32[]{:S(2)}, u32[]{:S(2)}) collective-permute-start(bf16[32,512]{1,0:T(8,128)(2,1)S(1)} %pack_body.1.refs_0_), channel_id=1, source_target_pairs={{0,1},{1,0},{2,3},{3,2},{4,5},{5,4},{6,7},{7,6},{8,9},{9,8},{10,11... | collective-permute-start | bytes 98312 | tf_op jit(solution)/shard_map/ppermute | solution.py:50
  4.2 0.7 copy-start.9
  4.9 1.2 %copy-start = (bf16[1,2048,256]{2,1,0:T(8,128)(2,1)S(1)}, bf16[1,2048,256]{2,1,0:T(8,128)(2,1)}, u32[]{:S(2)}) copy-start(bf16[1,2048,256]{2,1,0:T(8,128)(2,1)} %param.6) | copy-start | bytes 3145732
  6.1 1.2 %copy-start.5 = (bf16[1,2048,256]{2,1,0:T(8,128)(2,1)S(1)}, bf16[1,2048,256]{2,1,0:T(8,128)(2,1)}, u32[]{:S(2)}) copy-start(bf16[1,2048,256]{2,1,0:T(8,128)(2,1)} %param.7) | copy-start | bytes 3145732
  10.3 5.9 %copy-start.12 = (bf16[4,128,512]{2,1,0:T(8,128)(2,1)S(1)}, bf16[4,128,512]{2,1,0:T(8,128)(2,1)}, u32[]{:S(2)}) copy-start(bf16[4,128,512]{2,1,0:T(8,128)(2,1)} %refs_0_.3) | copy-start | bytes 1572868
  10.3 31.0 %all-to-all-start.1 = ((bf16[8,4,64,256]{3,2,1,0:T(8,128)(2,1)}), bf16[8,4,64,256]{3,2,1,0:T(8,128)(2,1)S(1)}, u32[]{:S(2)}, u32[]{:S(2)}) async-start(bf16[8,4,64,256]{3,2,1,0:T(8,128)(2,1)} %bitcast.6), calls=%async_computation.1 | async-start | bytes 2097152 | tf_op jit(solution)/shard_map/all_to_all | solution.py:359
  16.2 12.6 %collective-permute-start.4 = (bf16[4,128,512]{2,1,0:T(8,128)(2,1)S(1)}, bf16[4,128,512]{2,1,0:T(8,128)(2,1)S(1)}, u32[]{:S(2)}, u32[]{:S(2)}) collective-permute-start(bf16[4,128,512]{2,1,0:T(8,128)(2,1)S(1)} %copy-done.12), channel_id=1, source_target_pairs={{0,2},{1,3},{2,0},{3,1},{4,6},{5,7},{6,4},{7,5},{8,10},{9,11},{10,... | collective-permute-start | bytes 1572872 | tf_op jit(solution)/shard_map/ppermute | solution.py:50
  17.3 13.2 %collective-permute-start.3 = (bf16[4,128,512]{2,1,0:T(8,128)(2,1)S(1)}, bf16[4,128,512]{2,1,0:T(8,128)(2,1)S(1)}, u32[]{:S(2)}, u32[]{:S(2)}) collective-permute-start(bf16[4,128,512]{2,1,0:T(8,128)(2,1)S(1)} %copy-done.12), channel_id=1, source_target_pairs={{0,1},{1,0},{2,3},{3,2},{4,5},{5,4},{6,7},{7,6},{8,9},{9,8},{10,11... | collective-permute-start | bytes 1572872 | tf_op jit(solution)/shard_map/ppermute | solution.py:50
  28.8 4.1 %copy-start.13 = (bf16[4,128,512]{2,1,0:T(8,128)(2,1)}, bf16[4,128,512]{2,1,0:T(8,128)(2,1)S(1)}, u32[]{:S(2)}) copy-start(bf16[4,128,512]{2,1,0:T(8,128)(2,1)S(1)} %collective-permute-done.4.refs_2_) | copy-start | bytes 1572868
  28.8 3.3 %collective-permute-start.5 = (bf16[4,128,512]{2,1,0:T(8,128)(2,1)S(1)}, bf16[4,128,512]{2,1,0:T(8,128)(2,1)S(1)}, u32[]{:S(2)}, u32[]{:S(2)}) collective-permute-start(bf16[4,128,512]{2,1,0:T(8,128)(2,1)S(1)} %collective-permute-done.4.refs_2_), channel_id=1, source_target_pairs={{0,1},{1,0},{2,3},{3,2},{4,5},{5,4},{6,7},{7,6},{8,9},{9,8},{10,11... | collective-permute-start | bytes 1572872 | tf_op jit(solution)/shard_map/ppermute | solution.py:50
  30.5 2.3 %copy-start.14 = (bf16[4,128,512]{2,1,0:T(8,128)(2,1)}, bf16[4,128,512]{2,1,0:T(8,128)(2,1)S(1)}, u32[]{:S(2)}) copy-start(bf16[4,128,512]{2,1,0:T(8,128)(2,1)S(1)} %collective-permute-done.3.refs_1_) | copy-start | bytes 1572868
  32.1 0.8 %copy-start.15 = (bf16[4,128,512]{2,1,0:T(8,128)(2,1)}, bf16[4,128,512]{2,1,0:T(8,128)(2,1)S(1)}, u32[]{:S(2)}) copy-start(bf16[4,128,512]{2,1,0:T(8,128)(2,1)S(1)} %collective-permute-done.5.refs_3_) | copy-start | bytes 1572868
  41.3 1.0 %copy-start.2 = (bf16[8,4,64,256]{3,2,1,0:T(8,128)(2,1)}, bf16[8,4,64,256]{3,2,1,0:T(8,128)(2,1)S(1)}, u32[]{:S(2)}) copy-start(bf16[8,4,64,256]{3,2,1,0:T(8,128)(2,1)S(1)} %all-to-all-done.1.refs_0_) | copy-start | bytes 3145732
  42.3 3.7 %copy-start.1 = (bf16[1,2048,256]{2,1,0:T(8,128)(2,1)S(1)}, bf16[1,2048,256]{2,1,0:T(8,128)(2,1)}, u32[]{:S(2)}) copy-start(bf16[1,2048,256]{2,1,0:T(8,128)(2,1)} %param.6) | copy-start | bytes 3145732
  42.3 3.7 %copy-start.11 = (s32[512]{0:T(512)S(1)}, s32[512]{0:T(512)}, u32[]{:S(2)}) copy-start(s32[512]{0:T(512)} %param.11) | copy-start | bytes 6148
  42.3 28.7 %all-to-all-start = ((bf16[8,4,64,256]{3,2,1,0:T(8,128)(2,1)}), bf16[8,4,64,256]{3,2,1,0:T(8,128)(2,1)S(1)}, u32[]{:S(2)}, u32[]{:S(2)}) async-start(bf16[8,4,64,256]{3,2,1,0:T(8,128)(2,1)} %get-tuple-element.30), calls=%async_computation | async-start | bytes 2097152 | tf_op jit(solution)/shard_map/all_to_all | solution.py:384
  46.0 1.2 %copy-start.3 = (bf16[8,4,64,256]{3,2,1,0:T(8,128)(2,1)S(1)}, bf16[8,4,64,256]{3,2,1,0:T(8,128)(2,1)}, u32[]{:S(2)}) copy-start(bf16[8,4,64,256]{3,2,1,0:T(8,128)(2,1)} %copy-done.2) | copy-start | bytes 3145732
  50.2 1.0 %copy-start.7 = (bf16[4,512,256]{2,1,0:T(8,128)(2,1)}, bf16[4,512,256]{2,1,0:T(8,128)(2,1)S(1)}, u32[]{:S(2)}) copy-start(bf16[4,512,256]{2,1,0:T(8,128)(2,1)S(1)} %get-tuple-element.38.refs_4_) | copy-start | bytes 3145732
  51.1 2.9 %collective-permute-start.6 = (bf16[4,128,512]{2,1,0:T(8,128)(2,1)S(1)}, bf16[4,128,512]{2,1,0:T(8,128)(2,1)S(1)}, u32[]{:S(2)}, u32[]{:S(2)}) collective-permute-start(bf16[4,128,512]{2,1,0:T(8,128)(2,1)S(1)} %get-tuple-element.35), channel_id=1, source_target_pairs={{0,1},{1,0},{2,3},{3,2},{4,5},{5,4},{6,7},{7,6},{8,9},{9,8},{10,11... | collective-permute-start | bytes 1572872 | tf_op jit(solution)/shard_map/ppermute | solution.py:50
  52.5 2.3 %collective-permute-start.7 = (bf16[4,128,512]{2,1,0:T(8,128)(2,1)S(1)}, bf16[4,128,512]{2,1,0:T(8,128)(2,1)S(1)}, u32[]{:S(2)}, u32[]{:S(2)}) collective-permute-start(bf16[4,128,512]{2,1,0:T(8,128)(2,1)S(1)} %get-tuple-element.36), channel_id=1, source_target_pairs={{0,1},{1,0},{2,3},{3,2},{4,5},{5,4},{6,7},{7,6},{8,9},{9,8},{10,11... | collective-permute-start | bytes 1572872 | tf_op jit(solution)/shard_map/ppermute | solution.py:50
  55.6 7.7 %collective-permute-start.9 = (bf16[128,512]{1,0:T(8,128)(2,1)}, bf16[128,512]{1,0:T(8,128)(2,1)S(1)}, u32[]{:S(2)}, u32[]{:S(2)}) collective-permute-start(bf16[128,512]{1,0:T(8,128)(2,1)} %get-tuple-element.41), channel_id=1, source_target_pairs={{0,2},{1,3},{2,0},{3,1},{4,6},{5,7},{6,4},{7,5},{8,10},{9,11},{10,... | collective-permute-start | bytes 393224 | tf_op jit(solution)/shard_map/ppermute | solution.py:50
  56.7 6.6 %collective-permute-start.10 = (bf16[128,512]{1,0:T(8,128)(2,1)}, bf16[128,512]{1,0:T(8,128)(2,1)S(1)}, u32[]{:S(2)}, u32[]{:S(2)}) collective-permute-start(bf16[128,512]{1,0:T(8,128)(2,1)} %get-tuple-element.42), channel_id=1, source_target_pairs={{0,2},{1,3},{2,0},{3,1},{4,6},{5,7},{6,4},{7,5},{8,10},{9,11},{10,... | collective-permute-start | bytes 393224 | tf_op jit(solution)/shard_map/ppermute | solution.py:50
  57.0 9.1 %collective-permute-start.11 = (bf16[128,512]{1,0:T(8,128)(2,1)S(1)}, bf16[128,512]{1,0:T(8,128)(2,1)S(1)}, u32[]{:S(2)}, u32[]{:S(2)}) collective-permute-start(bf16[128,512]{1,0:T(8,128)(2,1)S(1)} %get-tuple-element.43), channel_id=1, source_target_pairs={{0,2},{1,3},{2,0},{3,1},{4,6},{5,7},{6,4},{7,5},{8,10},{9,11},{10,... | collective-permute-start | bytes 393224 | tf_op jit(solution)/shard_map/ppermute | solution.py:50
  58.2 10.8 %collective-permute-start.8 = (bf16[128,512]{1,0:T(8,128)(2,1)S(1)}, bf16[128,512]{1,0:T(8,128)(2,1)S(1)}, u32[]{:S(2)}, u32[]{:S(2)}) collective-permute-start(bf16[128,512]{1,0:T(8,128)(2,1)S(1)} %get-tuple-element.37), channel_id=1, source_target_pairs={{0,2},{1,3},{2,0},{3,1},{4,6},{5,7},{6,4},{7,5},{8,10},{9,11},{10,... | collective-permute-start | bytes 393224 | tf_op jit(solution)/shard_map/ppermute | solution.py:50
  71.0 4.6 %copy-start.4 = (bf16[2048,256]{1,0:T(8,128)(2,1)S(1)}, bf16[2048,256]{1,0:T(8,128)(2,1)}, u32[]{:S(2)}) copy-start(bf16[2048,256]{1,0:T(8,128)(2,1)} %mix_back_body.1.back_ref) | copy-start | bytes 3145732
  71.0 4.6 %copy-start.6 = (bf16[2048,256]{1,0:T(8,128)(2,1)S(1)}, bf16[2048,256]{1,0:T(8,128)(2,1)}, u32[]{:S(2)}) copy-start(bf16[2048,256]{1,0:T(8,128)(2,1)} %get-tuple-element.46.h_ref) | copy-start | bytes 3145732
  72.3 6.4 %collective-permute-start.12 = (bf16[32,512]{1,0:T(8,128)(2,1)S(1)}, bf16[32,512]{1,0:T(8,128)(2,1)S(1)}, u32[]{:S(2)}, u32[]{:S(2)}) collective-permute-start(bf16[32,512]{1,0:T(8,128)(2,1)S(1)} %get-tuple-element.48), channel_id=1, source_target_pairs={{0,1},{1,0},{2,3},{3,2},{4,5},{5,4},{6,7},{7,6},{8,9},{9,8},{10,11... | collective-permute-start | bytes 98312 | tf_op jit(solution)/shard_map/ppermute | solution.py:50
  73.8 4.9 %collective-permute-start.13 = (bf16[32,512]{1,0:T(8,128)(2,1)S(1)}, bf16[32,512]{1,0:T(8,128)(2,1)S(1)}, u32[]{:S(2)}, u32[]{:S(2)}) collective-permute-start(bf16[32,512]{1,0:T(8,128)(2,1)S(1)} %get-tuple-element.49), channel_id=1, source_target_pairs={{0,2},{1,3},{2,0},{3,1},{4,6},{5,7},{6,4},{7,5},{8,10},{9,11},{10,... | collective-permute-start | bytes 98312 | tf_op jit(solution)/shard_map/ppermute | solution.py:50
  75.0 3.8 %collective-permute-start.14 = (bf16[32,512]{1,0:T(8,128)(2,1)S(1)}, bf16[32,512]{1,0:T(8,128)(2,1)S(1)}, u32[]{:S(2)}, u32[]{:S(2)}) collective-permute-start(bf16[32,512]{1,0:T(8,128)(2,1)S(1)} %get-tuple-element.50), channel_id=1, source_target_pairs={{0,3},{1,2},{2,1},{3,0},{4,7},{5,6},{6,5},{7,4},{8,11},{9,10},{10,... | collective-permute-start | bytes 98312 | tf_op jit(solution)/shard_map/ppermute | solution.py:50
  75.6 0.7 copy-start.10

commit v16 on v15

--- a/solution.py
+++ b/solution.py
@@ -132,53 +132,50 @@
 
 
 def mix_body(batch, seq, *refs):
-    pieces, x_ref, alt_ref, cot_ref, src_ref = refs[:batch], *refs[batch : batch + 4]
-    outs, h_ref, p_scr, mix_scr, reg_scr, sems = refs[batch + 4 : -5], *refs[-5:]
-    me, here = lax.axis_index("batch"), lax.axis_index("seq")
+    pieces, x_hbm, alt_ref, out_hbm = refs[:batch], *refs[batch : batch + 3]
+    f_scr, x_scr, p_scr, mix_scr, reg_scr, read_sems, write_sems = refs[batch + 3 :]
+    me = lax.axis_index("batch")
     blocks, rows, order = pieces[0].shape
     j_here = order // seq
-    width = x_ref.shape[1]
-    from_rows = jnp.where(iota((order, order), 0) == alt_ref[...], 1.0, 0.0)
-    p_scr[...] = from_rows.T.astype(BF16)
-    select = one_hot(iota((width, width), 0) == src_ref[...])
-
-    writes = []
+    width = x_scr.shape[1]
+    reads, writes = [], []
     for i in range(blocks):
-        x = x_ref[i * order : (i + 1) * order, :]
+        part = pl.ds(i * order, order)
+        reads.append([pltpu.make_async_copy(x_hbm.at[part, :], x_scr.at[part, :], read_sems.at[i, batch])])
+        for d in range(batch):
+            reads[i].append(pltpu.make_async_copy(pieces[d].at[i], f_scr.at[d, i], read_sems.at[i, d]))
+        for read in reads[i]:
+            read.start()
+    p_scr[...] = jnp.where(iota((order, order), 0) == alt_ref[...], 1.0, 0.0).T.astype(BF16)
+    for i in range(blocks):
+        for read in reads[i]:
+            read.wait()
+        x = x_scr[i * order : (i + 1) * order, :]
         for d in range(batch):
             first = pl.multiple_of((me ^ d) * rows, rows)
-            mix_scr[pl.ds(first, rows), :] = dot(pieces[d][i], x).astype(BF16)
-        result = dot(p_scr[...], mix_scr[...]).astype(BF16)
-        if len(outs) == 1:
-            reg_scr[i] = result.reshape(seq, j_here, width)
-            for p, there in enumerate(ring_of(seq)):
-                write = pltpu.make_async_copy(reg_scr.at[i, there], outs[0].at[p, i], sems.at[i, p])
-                write.start()
-                writes.append(write)
-        else:
-            reg_scr[i] = result.reshape(seq, j_here, width)
-            for d in range(seq):
-                outs[d][i] = reg_scr[i, here ^ d]
-        gate = jax.nn.sigmoid(dot(x, select))
-        cot = cot_ref[i * order : (i + 1) * order, :].astype(F32)
-        h_ref[i * order : (i + 1) * order, :] = (cot * gate * (1.0 - gate)).astype(BF16)
+            mix_scr[pl.ds(first, rows), :] = dot(f_scr[d, i], x).astype(BF16)
+        reg_scr[i] = dot(p_scr[...], mix_scr[...]).astype(BF16).reshape(seq, j_here, width)
+        for p, there in enumerate(ring_of(seq)):
+            write = pltpu.make_async_copy(reg_scr.at[i, there], out_hbm.at[p, i], write_sems.at[i, p])
+            write.start()
+            writes.append(write)
     for write in writes:
         write.wait()
 
 
 def first_grad_body(batch, seq, *refs):
-    count = len(refs) - batch - 6
+    count = len(refs) - batch - 8
     pieces, x_ref, alt_ref = refs[:count], refs[count], refs[count + 1]
-    outs, dmixed_ref = refs[count + 2 : count + 2 + batch], refs[count + 2 + batch]
-    p_scr, reg_scr, part_scr = refs[-3:]
+    outs, dmixed_hbm = refs[count + 2 : count + 2 + batch], refs[count + 2 + batch]
+    p_scr, reg_scr, part_scr, dmixed_ref, sems = refs[-5:]
     me, here = lax.axis_index("batch"), lax.axis_index("seq")
     blocks, j_here, width = pieces[0].shape[-3:]
     order = j_here * seq
     rows = order // batch
     p_scr[...] = one_hot(iota((order, order), 0) == alt_ref[...])
 
-    @pl.loop(0, blocks)
-    def _(i):
+    writes = []
+    for i in range(blocks):
         if count == 1:
             for p, there in enumerate(ring_of(seq)):
                 reg_scr[there * j_here : (there + 1) * j_here, :] = pieces[0][p, i]
@@ -188,26 +185,35 @@
                 reg_scr[pl.ds(first, j_here), :] = pieces[d][i]
         dmixed = dot(p_scr[...], reg_scr[...]).astype(BF16)
         dmixed_ref[i] = dmixed
-        x = x_ref[pl.ds(pl.multiple_of(i * order, order), order), :]
+        writes.append(pltpu.make_async_copy(dmixed_ref.at[i], dmixed_hbm.at[i], sems.at[i]))
+        writes[i].start()
+        x = x_ref[i * order : (i + 1) * order, :]
         part_scr[...] = dot(dmixed, x, 1, 1).astype(BF16)
         for d in range(batch):
             first = pl.multiple_of((me ^ d) * rows, rows)
             outs[d][i] = part_scr[pl.ds(first, rows), :]
+    for write in writes:
+        write.wait()
 
 
 def mix_back_body(batch, *refs):
-    pieces, dmixed_ref, out_ref = refs[:batch], *refs[batch:]
+    pieces, dmixed_ref, x_ref, cot_ref, src_ref, out_ref, h_ref = refs[:batch], *refs[batch:]
     me = lax.axis_index("batch")
     blocks, rows, order = pieces[0].shape
+    width = x_ref.shape[1]
+    select = one_hot(iota((width, width), 0) == src_ref[...])
 
     @pl.loop(0, blocks)
     def _(i):
+        part = pl.ds(pl.multiple_of(i * order, order), order)
         total = None
         for d in range(batch):
             first = pl.multiple_of((me ^ d) * rows, rows)
             term = dot(pieces[d][i], dmixed_ref[i, pl.ds(first, rows), :], 0, 0)
             total = term if total is None else total + term
-        out_ref[pl.ds(pl.multiple_of(i * order, order), order), :] = total.astype(BF16)
+        out_ref[part, :] = total.astype(BF16)
+        gate = jax.nn.sigmoid(dot(x_ref[part, :], select))
+        h_ref[part, :] = (cot_ref[part, :].astype(F32) * gate * (1.0 - gate)).astype(BF16)
 
 
 def gather_blocks(seq, pieces, scr):
@@ -271,8 +277,10 @@
 
 def pair_body(own_a, own_b, got_a, got_b, out_a, *outs_b):
     out_a[...] = own_a[...].astype(F32) + got_a[...].astype(F32)
+    step = outs_b[0].shape[0]
     for n, out_b in enumerate(outs_b):
-        out_b[...] = (own_b[n].astype(F32) + got_b[n].astype(F32)).astype(BF16)
+        part = slice(n * step, (n + 1) * step)
+        out_b[...] = (own_b[part].astype(F32) + got_b[part].astype(F32)).astype(BF16)
 
 
 def sum_body(own, *refs):
@@ -283,8 +291,10 @@
 
 
 def add_body(own, *refs):
+    step = refs[0].shape[0]
     for n, got in enumerate(refs[:-1]):
-        refs[-1][n] = (own[n] + got[...].astype(F32)).astype(BF16)
+        part = slice(n * step, (n + 1) * step)
+        refs[-1][part] = (own[part] + got[...].astype(F32)).astype(BF16)
 
 
 def unpack_body(order, seq, *refs):
@@ -365,17 +375,21 @@
     if direct is None:
         direct = move("fx", across, "batch", 1, batch)
     first = [first_factor, beside, across, direct]
-    *regrouped, h = call(
+    regrouped = call(
         functools.partial(mix_body, batch, seq),
-        ([of((seq, blocks, j_here, width))] if CFG['a2a'][1] else [piece] * seq) + [of((rows_here, width))],
-        [dep("M", first_factor), *first[1:], x, alt, cot, src],
+        [of((seq, blocks, j_here, width))],
+        [dep("M", first_factor), *first[1:], x, alt],
         [
+            pltpu.VMEM((batch, blocks, k_here, order), BF16),
+            pltpu.VMEM((rows_here, width), BF16),
             pltpu.VMEM((order, order), BF16),
             pltpu.VMEM((order, width), BF16),
             pltpu.VMEM((blocks, seq, j_here, width), BF16),
+            pltpu.SemaphoreType.DMA((blocks, batch + 1)),
             pltpu.SemaphoreType.DMA((blocks, seq)),
         ],
-        far_outs=(0,) if CFG['a2a'][1] else (),
+        spaces={n: pltpu.HBM for n in range(batch + 1)},
+        far_outs=(0,),
         limit=CFG['limit'],
     )
     keep("M", regrouped[0])
@@ -391,7 +405,14 @@
         functools.partial(first_grad_body, batch, seq),
         [of((blocks, k_here, order))] * batch + [of((blocks, order, width))],
         [dep("F1", back_got[0]), *[back_got[d] for d in range(1, seq) if d in back_got], x, alt],
-        [pltpu.VMEM((order, order), BF16), pltpu.VMEM((order, width), BF16), pltpu.VMEM((order, order), BF16)],
+        [
+            pltpu.VMEM((order, order), BF16),
+            pltpu.VMEM((order, width), BF16),
+            pltpu.VMEM((order, order), BF16),
+            pltpu.VMEM((blocks, order, width), BF16),
+            pltpu.SemaphoreType.DMA((blocks,)),
+        ],
+        far_outs=(batch,),
         limit=40 << 20,
     )
     keep("F1", dmixed)
@@ -403,19 +424,20 @@
     if CFG['rsdirect']:
         (grad_one,) = call(sum_body, [of(parts[0].shape)], [dep("sum", parts[0]), *others])
     else:
+        halves = 4 if blocks % 4 == 0 else 1
         kept, *summed = call(
             pair_body,
-            [of(parts[0].shape, F32)] + [of((k_here, order))] * blocks,
+            [of(parts[0].shape, F32)] + [of((blocks // halves, k_here, order))] * halves,
             [dep("pair", parts[0]), parts[2], near, far],
             limit=40 << 20,
         )
         keep("pair", summed[0])
-        across_sums = [move(f"rx{n}", summed[n], "batch", 2, batch) for n in range(blocks)]
+        across_sums = [move(f"rx{n}", summed[n], "batch", 2, batch) for n in range(halves)]
         (grad_one,) = call(add_body, [of(parts[0].shape)], [kept, *across_sums])
-    (dmix_in,) = call(
+    dmix_in, h = call(
         functools.partial(mix_back_body, batch),
-        [of((rows_here, width))],
-        [*first, dep("F2", dmixed)],
+        [of((rows_here, width))] * 2,
+        [*first, dep("F2", dmixed), x, cot, src],
         limit=CFG['limit'],
     )
     keep("F2", dmix_in)

time: 80.3 us -> 79.9 us (level)
    ppermute x15, waiting for transfers between devices: 19.8 us -> 18.5 us  [swap(): return lax.ppermute(value, axis, [(p, p ^ step) for p in range(size)])]
  transfers between devices with their start and end apart: 17 -> 17, of which waited for: 9 -> 8; matrix products, arithmetic and copies ran while one was open for 0% -> 0% of each run, Pallas kernels for 24% -> 24%
where the time goes in v16:
time: 79.9 us; the launch traced here: 79.4 us
  Pallas kernels  24.5 us (31%)
  starting transfers between devices  23.3 us (29%)
  waiting for transfers between devices  22.1 us (28%)
  local copies, waits for them, and re-layouts  8.64 us (11%)
  between operations  0.83 us (1%)
    pallas_call x11, Pallas kernels, call(): pl.pallas_call(body, name=name, out_shape=outs, in_specs=[pl.BlockSpec(me...  24.5 us
    ppermute x15, waiting for transfers between devices, swap(): return lax.ppermute(value, axis, [(p, p ^ step) for p in range(size)])  18.5 us
    ppermute x15, starting transfers between devices, swap(): return lax.ppermute(value, axis, [(p, p ^ step) for p in range(size)])  13.9 us
    unnamed x32, local copies, waits for them, and re-layouts  8.64 us
    all_to_all x1, starting transfers between devices, packed_shards(): lax.all_to_all(dep('h0', back[0]).reshape(seq, blocks, j_here, width), 's...  5.86 us
    all_to_all x1, starting transfers between devices, packed_shards(): lax.all_to_all(dep('H0', regrouped[0]), 'seq', 0, 0, axis_index_groups=[r...  3.51 us
    all_to_all x1, waiting for transfers between devices, packed_shards(): lax.all_to_all(dep('h0', back[0]).reshape(seq, blocks, j_here, width), 's...  2.26 us
  transfers between devices with their start and end apart: 17, of which 8 were waited for; matrix products, arithmetic and copies ran while one was open for 0% of the time, Pallas kernels for 24%

profile of v16, /device:TPU:9, one launch (start us, length us, event | category | flops | bytes accessed | tf_op | source)
XLA Modules:
  0.0 79.4 jit_solution(5360350706492157375)
XLA Ops:
  0.6 0.0 copy-start.8
  0.6 0.8 %copy-done.8 = bf16[64,8,32]{0,2,1:T(8,128)(2,1)S(1)} copy-done((bf16[64,8,32]{0,2,1:T(8,128)(2,1)S(1)}, bf16[64,8,32]{0,2,1:T(8,128)(2,1)}, u32[]{:S(2)}) %copy-start.8) | copy-done | bytes 32792
  1.5 0.4 pack_body.1.refs_0_
  1.9 1.8 %collective-permute-start.2 = (bf16[32,512]{1,0:T(8,128)(2,1)S(1)}, bf16[32,512]{1,0:T(8,128)(2,1)S(1)}, u32[]{:S(2)}, u32[]{:S(2)}) collective-permute-start(bf16[32,512]{1,0:T(8,128)(2,1)S(1)} %pack_body.1.refs_0_), channel_id=1, source_target_pairs={{0,3},{1,2},{2,1},{3,0},{4,7},{5,6},{6,5},{7,4},{8,11},{9,10},{10,... | collective-permute-start | bytes 98312 | tf_op jit(solution)/shard_map/ppermute | solution.py:50
  3.7 0.3 collective-permute-start.1
  4.0 0.2 collective-permute-start
  4.2 0.7 copy-done.9
  4.9 1.2 %copy-done = bf16[1,2048,256]{2,1,0:T(8,128)(2,1)S(1)} copy-done((bf16[1,2048,256]{2,1,0:T(8,128)(2,1)S(1)}, bf16[1,2048,256]{2,1,0:T(8,128)(2,1)}, u32[]{:S(2)}) %copy-start) | copy-done | bytes 1048600
  6.1 1.2 %copy-done.4 = bf16[1,2048,256]{2,1,0:T(8,128)(2,1)S(1)} copy-done((bf16[1,2048,256]{2,1,0:T(8,128)(2,1)S(1)}, bf16[1,2048,256]{2,1,0:T(8,128)(2,1)}, u32[]{:S(2)}) %copy-start.4) | copy-done | bytes 1048600
  7.3 0.5 gate_body.1.refs_4_.refs_1_
  7.8 0.0 collective-permute-done.2.refs_3_
  7.8 0.0 collective-permute-done.1.refs_2_
  7.8 0.0 collective-permute-done.refs_1_
  7.9 2.4 %regroup_back_body.1 = (bf16[32,64,256]{2,1,0:T(8,128)(2,1)}, bf16[4,32,512]{2,1,0:T(8,128)(2,1)S(1)}) custom-call(bf16[32,512]{1,0:T(8,128)(2,1)S(1)} %pack_body.1.refs_0_, bf16[32,512]{1,0:T(8,128)(2,1)S(1)} %collective-permute-done.refs_1_, bf16[32,512]{1,0:T(8,128)(2,1)S(1)} %collective-permute-done.1.refs_2_, ...), custom_call_target="tpu_custom_call" | custom-call | tf_op jit(solution)/shard_map/regroup_back_body/pallas_call | solution.py:31
  10.3 0.0 copy-start.12
  10.3 5.9 %all-to-all-start.1 = ((bf16[8,4,64,256]{3,2,1,0:T(8,128)(2,1)}), bf16[8,4,64,256]{3,2,1,0:T(8,128)(2,1)S(1)}, u32[]{:S(2)}, u32[]{:S(2)}) async-start(bf16[8,4,64,256]{3,2,1,0:T(8,128)(2,1)} %bitcast.6), calls=%async_computation.1 | async-start | bytes 2097152 | tf_op jit(solution)/shard_map/all_to_all | solution.py:369
  16.2 0.0 copy-done.12
  16.2 1.1 %collective-permute-start.4 = (bf16[4,128,512]{2,1,0:T(8,128)(2,1)S(1)}, bf16[4,128,512]{2,1,0:T(8,128)(2,1)S(1)}, u32[]{:S(2)}, u32[]{:S(2)}) collective-permute-start(bf16[4,128,512]{2,1,0:T(8,128)(2,1)S(1)} %copy-done.12), channel_id=1, source_target_pairs={{0,2},{1,3},{2,0},{3,1},{4,6},{5,7},{6,4},{7,5},{8,10},{9,11},{10,... | collective-permute-start | bytes 1572872 | tf_op jit(solution)/shard_map/ppermute | solution.py:50
  17.3 1.2 %collective-permute-start.3 = (bf16[4,128,512]{2,1,0:T(8,128)(2,1)S(1)}, bf16[4,128,512]{2,1,0:T(8,128)(2,1)S(1)}, u32[]{:S(2)}, u32[]{:S(2)}) collective-permute-start(bf16[4,128,512]{2,1,0:T(8,128)(2,1)S(1)} %copy-done.12), channel_id=1, source_target_pairs={{0,1},{1,0},{2,3},{3,2},{4,5},{5,4},{6,7},{7,6},{8,9},{9,8},{10,11... | collective-permute-start | bytes 1572872 | tf_op jit(solution)/shard_map/ppermute | solution.py:50
  18.5 10.2 %collective-permute-done.4.refs_2_ = bf16[4,128,512]{2,1,0:T(8,128)(2,1)S(1)} collective-permute-done((bf16[4,128,512]{2,1,0:T(8,128)(2,1)S(1)}, bf16[4,128,512]{2,1,0:T(8,128)(2,1)S(1)}, u32[]{:S(2)}, u32[]{:S(2)}) %collective-permute-start.4) | collective-permute-done | bytes 524320 | tf_op jit(solution)/shard_map/ppermute | solution.py:50
  28.8 1.8 %collective-permute-start.5 = (bf16[4,128,512]{2,1,0:T(8,128)(2,1)S(1)}, bf16[4,128,512]{2,1,0:T(8,128)(2,1)S(1)}, u32[]{:S(2)}, u32[]{:S(2)}) collective-permute-start(bf16[4,128,512]{2,1,0:T(8,128)(2,1)S(1)} %collective-permute-done.4.refs_2_), channel_id=1, source_target_pairs={{0,1},{1,0},{2,3},{3,2},{4,5},{5,4},{6,7},{7,6},{8,9},{9,8},{10,11... | collective-permute-start | bytes 1572872 | tf_op jit(solution)/shard_map/ppermute | solution.py:50
  30.5 0.0 collective-permute-done.3.refs_1_
  30.5 1.5 %collective-permute-done.5.refs_3_ = bf16[4,128,512]{2,1,0:T(8,128)(2,1)S(1)} collective-permute-done((bf16[4,128,512]{2,1,0:T(8,128)(2,1)S(1)}, bf16[4,128,512]{2,1,0:T(8,128)(2,1)S(1)}, u32[]{:S(2)}, u32[]{:S(2)}) %collective-permute-start.5) | collective-permute-done | bytes 524320 | tf_op jit(solution)/shard_map/ppermute | solution.py:50
  32.1 0.8 %copy-done.15 = bf16[4,128,512]{2,1,0:T(8,128)(2,1)} copy-done((bf16[4,128,512]{2,1,0:T(8,128)(2,1)}, bf16[4,128,512]{2,1,0:T(8,128)(2,1)S(1)}, u32[]{:S(2)}) %copy-start.15) | copy-done | bytes 524312
  32.9 0.0 copy-done.13
  32.9 0.0 copy-done.14
  32.9 6.2 %mix_body.1 = bf16[8,4,64,256]{3,2,1,0:T(8,128)(2,1)} custom-call(bf16[4,128,512]{2,1,0:T(8,128)(2,1)} %refs_0_.3, bf16[4,128,512]{2,1,0:T(8,128)(2,1)} %copy-done.14, bf16[4,128,512]{2,1,0:T(8,128)(2,1)} %copy-done.13, bf16[4,128,512]{2,1,0:T(8,128)(2,1)} %copy-done.15, bf16[2048,256]{1,0:T(8,128)(2,1)} %bitcast.13, s32[1,512]{1,0:T(1,128)} %bitcast.25), custom_call_target="tpu_custom_call" | custom-call | tf_op jit(solution)/shard_map/mix_body/pallas_call | solution.py:31
  39.0 0.0 copy-start.1
  39.0 0.0 copy-start.11
  39.1 2.3 %all-to-all-done.1.refs_0_ = bf16[8,4,64,256]{3,2,1,0:T(8,128)(2,1)S(1)} async-done(((bf16[8,4,64,256]{3,2,1,0:T(8,128)(2,1)}), bf16[8,4,64,256]{3,2,1,0:T(8,128)(2,1)S(1)}, u32[]{:S(2)}, u32[]{:S(2)}) %all-to-all-start.1) | async-done | bytes 1048608 | tf_op jit(solution)/shard_map/all_to_all | solution.py:369
  41.3 1.0 %copy-done.2 = bf16[8,4,64,256]{3,2,1,0:T(8,128)(2,1)} copy-done((bf16[8,4,64,256]{3,2,1,0:T(8,128)(2,1)}, bf16[8,4,64,256]{3,2,1,0:T(8,128)(2,1)S(1)}, u32[]{:S(2)}) %copy-start.2) | copy-done | bytes 1048600
  42.3 3.5 %all-to-all-start = ((bf16[8,4,64,256]{3,2,1,0:T(8,128)(2,1)}), bf16[8,4,64,256]{3,2,1,0:T(8,128)(2,1)S(1)}, u32[]{:S(2)}, u32[]{:S(2)}) async-start(bf16[8,4,64,256]{3,2,1,0:T(8,128)(2,1)} %mix_body.1), calls=%async_computation | async-start | bytes 2097152 | tf_op jit(solution)/shard_map/all_to_all | solution.py:398
  45.8 0.0 copy-done.1
  45.8 1.2 %copy-done.3 = bf16[8,4,64,256]{3,2,1,0:T(8,128)(2,1)S(1)} copy-done((bf16[8,4,64,256]{3,2,1,0:T(8,128)(2,1)S(1)}, bf16[8,4,64,256]{3,2,1,0:T(8,128)(2,1)}, u32[]{:S(2)}) %copy-start.3) | copy-done | bytes 1048600
  47.1 2.5 %first_grad_body.1 = (bf16[4,128,512]{2,1,0:T(8,128)(2,1)S(1)}, bf16[4,128,512]{2,1,0:T(8,128)(2,1)S(1)}, bf16[4,128,512]{2,1,0:T(8,128)(2,1)S(1)}, bf16[4,128,5...) custom-call(bf16[8,4,64,256]{3,2,1,0:T(8,128)(2,1)S(1)} %copy-done.3, bf16[2048,256]{1,0:T(8,128)(2,1)S(1)} %bitcast.16, ...), custom_call_target="tpu_custom_call" | custom-call | tf_op jit(solution)/shard_map/first_grad_body/pallas_call | solution.py:31
  49.6 0.0 copy-start.7
  49.6 1.0 %copy-done.7 = bf16[4,512,256]{2,1,0:T(8,128)(2,1)} copy-done((bf16[4,512,256]{2,1,0:T(8,128)(2,1)}, bf16[4,512,256]{2,1,0:T(8,128)(2,1)S(1)}, u32[]{:S(2)}) %copy-start.7) | copy-done | bytes 1048600
  50.6 1.4 %collective-permute-start.6 = (bf16[4,128,512]{2,1,0:T(8,128)(2,1)S(1)}, bf16[4,128,512]{2,1,0:T(8,128)(2,1)S(1)}, u32[]{:S(2)}, u32[]{:S(2)}) collective-permute-start(bf16[4,128,512]{2,1,0:T(8,128)(2,1)S(1)} %get-tuple-element.34), channel_id=1, source_target_pairs={{0,1},{1,0},{2,3},{3,2},{4,5},{5,4},{6,7},{7,6},{8,9},{9,8},{10,11... | collective-permute-start | bytes 1572872 | tf_op jit(solution)/shard_map/ppermute | solution.py:50
  51.9 0.0 collective-permute-start.7
  51.9 1.5 %collective-permute-done.6.got_a = bf16[4,128,512]{2,1,0:T(8,128)(2,1)S(1)} collective-permute-done((bf16[4,128,512]{2,1,0:T(8,128)(2,1)S(1)}, bf16[4,128,512]{2,1,0:T(8,128)(2,1)S(1)}, u32[]{:S(2)}, u32[]{:S(2)}) %collective-permute-start.6) | collective-permute-done | bytes 524320 | tf_op jit(solution)/shard_map/ppermute | solution.py:50
  53.5 0.7 collective-permute-done.7.got_b
  54.2 0.8 %pair_body.1 = (f32[4,128,512]{2,1,0:T(8,128)S(1)}, bf16[1,128,512]{2,1,0:T(8,128)(2,1)S(1)}, bf16[1,128,512]{2,1,0:T(8,128)(2,1)}, bf16[1,128,512]{2,1,0:T(8,128)(2,1)}, bf16[1,128,512]{2,1,0:T(8,128)(2,1)S(1)}) custom-call(bf16[4,128,512]{2,1,0:T(8,128)(2,1)S(1)} %get-tuple-element.32.own_a, bf16[4,128,512]{2,1,0:T(8,128)(2,1)S(1)} %get-tuple-element.33.own_b, ...), custom_call_target="tpu_custom_call" | custom-call | tf_op jit(solution)/shard_map/pair_body/pallas_call | solution.py:31
  55.0 1.1 %collective-permute-start.9 = (bf16[1,128,512]{2,1,0:T(8,128)(2,1)}, bf16[1,128,512]{2,1,0:T(8,128)(2,1)S(1)}, u32[]{:S(2)}, u32[]{:S(2)}) collective-permute-start(bf16[1,128,512]{2,1,0:T(8,128)(2,1)} %get-tuple-element.41), channel_id=1, source_target_pairs={{0,2},{1,3},{2,0},{3,1},{4,6},{5,7},{6,4},{7,5},{8,10},{9,11},{10,... | collective-permute-start | bytes 393224 | tf_op jit(solution)/shard_map/ppermute | solution.py:50
  56.1 0.4 collective-permute-start.10
  56.5 1.1 %collective-permute-start.11 = (bf16[1,128,512]{2,1,0:T(8,128)(2,1)S(1)}, bf16[1,128,512]{2,1,0:T(8,128)(2,1)S(1)}, u32[]{:S(2)}, u32[]{:S(2)}) collective-permute-start(bf16[1,128,512]{2,1,0:T(8,128)(2,1)S(1)} %get-tuple-element.43), channel_id=1, source_target_pairs={{0,2},{1,3},{2,0},{3,1},{4,6},{5,7},{6,4},{7,5},{8,10},{9,11},{10,... | collective-permute-start | bytes 393224 | tf_op jit(solution)/shard_map/ppermute | solution.py:50
  57.6 0.4 collective-permute-start.8
  57.9 6.0 %mix_back_body.1 = (bf16[2048,256]{1,0:T(8,128)(2,1)}, bf16[2048,256]{1,0:T(8,128)(2,1)}) custom-call(bf16[4,128,512]{2,1,0:T(8,128)(2,1)} %refs_0_.3, bf16[4,128,512]{2,1,0:T(8,128)(2,1)} %copy-done.14, bf16[4,128,512]{2,1,0:T(8,128)(2,1)} %copy-done.13, bf16[4,128,512]{2,1,0:T(8,128)(2,1)} %copy-done.15, bf16[4,512,256]{2,1,0:T(8,128)(2,1)} %copy-done.7, ...), custom_call_target="tpu_custom_call" | custom-call | tf_op jit(solution)/shard_map/mix_back_body/pallas_call | solution.py:31
  63.9 0.0 collective-permute-done.9.refs_1_
  63.9 0.0 collective-permute-done.10.refs_2_
  63.9 1.6 %collective-permute-done.11.refs_3_ = bf16[1,128,512]{2,1,0:T(8,128)(2,1)S(1)} collective-permute-done((bf16[1,128,512]{2,1,0:T(8,128)(2,1)S(1)}, bf16[1,128,512]{2,1,0:T(8,128)(2,1)S(1)}, u32[]{:S(2)}, u32[]{:S(2)}) %collective-permute-start.11) | collective-permute-done | bytes 131104 | tf_op jit(solution)/shard_map/ppermute | solution.py:50
  65.5 2.8 %collective-permute-done.8.refs_0_ = bf16[1,128,512]{2,1,0:T(8,128)(2,1)S(1)} collective-permute-done((bf16[1,128,512]{2,1,0:T(8,128)(2,1)S(1)}, bf16[1,128,512]{2,1,0:T(8,128)(2,1)S(1)}, u32[]{:S(2)}, u32[]{:S(2)}) %collective-permute-start.8) | collective-permute-done | bytes 131104 | tf_op jit(solution)/shard_map/ppermute | solution.py:50
  68.4 0.9 %add_body.1 = bf16[4,128,512]{2,1,0:T(8,128)(2,1)} custom-call(f32[4,128,512]{2,1,0:T(8,128)S(1)} %get-tuple-element.40.own, bf16[1,128,512]{2,1,0:T(8,128)(2,1)S(1)} %collective-permute-done.8.refs_0_, bf16[1,128,512]{2,1,0:T(8,128)(2,1)S(1)} %collective-permute-done.9.refs_1_, bf16[1,128,512]{2,1,0:T(8,128)(2,1)S(1)} %collective-permute-done.10.refs_2_, ...), custom_call_target="tpu_custom_call" | custom-call | tf_op jit(solution)/shard_map/add_body/pallas_call | solution.py:31
  69.2 1.4 %all-to-all-done = bf16[8,4,64,256]{3,2,1,0:T(8,128)(2,1)S(1)} async-done(((bf16[8,4,64,256]{3,2,1,0:T(8,128)(2,1)}), bf16[8,4,64,256]{3,2,1,0:T(8,128)(2,1)S(1)}, u32[]{:S(2)}, u32[]{:S(2)}) %all-to-all-start) | async-done | bytes 1048608 | tf_op jit(solution)/shard_map/all_to_all | solution.py:398
  70.6 1.3 %second_grad_body.1 = (bf16[32,512]{1,0:T(8,128)(2,1)S(1)}, bf16[32,512]{1,0:T(8,128)(2,1)S(1)}, bf16[32,512]{1,0:T(8,128)(2,1)S(1)}, bf16[32,512]{1,0:T(8,128)(2,1)S(1)}) custom-call(bf16[32,64,256]{2,1,0:T(8,128)(2,1)S(1)} %bitcast.17, bf16[2048,256]{1,0:T(8,128)(2,1)S(1)} %gate_body.1.refs_4_.refs_1_), custom_call_target="tpu_custom_call" | custom-call | tf_op jit(solution)/shard_map/second_grad_body/pallas_call | solution.py:31
  71.9 1.5 %collective-permute-start.12 = (bf16[32,512]{1,0:T(8,128)(2,1)S(1)}, bf16[32,512]{1,0:T(8,128)(2,1)S(1)}, u32[]{:S(2)}, u32[]{:S(2)}) collective-permute-start(bf16[32,512]{1,0:T(8,128)(2,1)S(1)} %get-tuple-element.48), channel_id=1, source_target_pairs={{0,1},{1,0},{2,3},{3,2},{4,5},{5,4},{6,7},{7,6},{8,9},{9,8},{10,11... | collective-permute-start | bytes 98312 | tf_op jit(solution)/shard_map/ppermute | solution.py:50
  73.5 1.1 %collective-permute-start.13 = (bf16[32,512]{1,0:T(8,128)(2,1)S(1)}, bf16[32,512]{1,0:T(8,128)(2,1)S(1)}, u32[]{:S(2)}, u32[]{:S(2)}) collective-permute-start(bf16[32,512]{1,0:T(8,128)(2,1)S(1)} %get-tuple-element.49), channel_id=1, source_target_pairs={{0,2},{1,3},{2,0},{3,1},{4,6},{5,7},{6,4},{7,5},{8,10},{9,11},{10,... | collective-permute-start | bytes 98312 | tf_op jit(solution)/shard_map/ppermute | solution.py:50
  74.6 0.6 collective-permute-start.14
  75.2 0.0 copy-done.5
  75.2 0.7 copy-done.10
  75.9 2.5 %tokens_body.1 = bf16[2048,256]{1,0:T(8,128)(2,1)} custom-call(bf16[32,64,256]{2,1,0:T(8,128)(2,1)S(1)} %bitcast.18, bf16[4,32,512]{2,1,0:T(8,128)(2,1)S(1)} %get-tuple-element.45.second_ref, bf16[2048,256]{1,0:T(8,128)(2,1)S(1)} %copy-done.6, s32[1,256]{1,0:T(1,128)S(1)} %bitcast.24, bf16[2048,256]{1,0:T(8,128)(2,1)S(1)} %copy-done.5), custom_call_target="tpu_custom_call" | custom-call | tf_op jit(solution)/shard_map/tokens_body/pallas_call | solution.py:31
  78.3 0.0 collective-permute-done.12.refs_1_
  78.3 0.0 collective-permute-done.13.refs_2_
  78.3 0.0 collective-permute-done.14.refs_3_
  78.4 1.1 %unpack_body.1 = bf16[256,64]{1,0:T(8,128)(2,1)} custom-call(bf16[32,512]{1,0:T(8,128)(2,1)S(1)} %get-tuple-element.47.refs_0_, bf16[32,512]{1,0:T(8,128)(2,1)S(1)} %collective-permute-done.12.refs_1_, bf16[32,512]{1,0:T(8,128)(2,1)S(1)} %collective-permute-done.13.refs_2_, bf16[32,512]{1,0:T(8,128)(2,1)S(1)} %collective-permute-done.14.refs_3_), custom_call_target="tpu_custom_call" | custom-call | tf_op jit(solution)/shard_map/unpack_body/pallas_call | solution.py:31
  (13 shorter events, 0.0 us)
Async XLA Ops:
  0.6 0.8 %copy-start.8 = (bf16[64,8,32]{0,2,1:T(8,128)(2,1)S(1)}, bf16[64,8,32]{0,2,1:T(8,128)(2,1)}, u32[]{:S(2)}) copy-start(bf16[64,8,32]{0,2,1:T(8,128)(2,1)} %param.9) | copy-start | bytes 98308
  1.9 5.9 %collective-permute-start.2 = (bf16[32,512]{1,0:T(8,128)(2,1)S(1)}, bf16[32,512]{1,0:T(8,128)(2,1)S(1)}, u32[]{:S(2)}, u32[]{:S(2)}) collective-permute-start(bf16[32,512]{1,0:T(8,128)(2,1)S(1)} %pack_body.1.refs_0_), channel_id=1, source_target_pairs={{0,3},{1,2},{2,1},{3,0},{4,7},{5,6},{6,5},{7,4},{8,11},{9,10},{10,... | collective-permute-start | bytes 98312 | tf_op jit(solution)/shard_map/ppermute | solution.py:50
  3.7 4.1 %collective-permute-start.1 = (bf16[32,512]{1,0:T(8,128)(2,1)S(1)}, bf16[32,512]{1,0:T(8,128)(2,1)S(1)}, u32[]{:S(2)}, u32[]{:S(2)}) collective-permute-start(bf16[32,512]{1,0:T(8,128)(2,1)S(1)} %pack_body.1.refs_0_), channel_id=1, source_target_pairs={{0,2},{1,3},{2,0},{3,1},{4,6},{5,7},{6,4},{7,5},{8,10},{9,11},{10,... | collective-permute-start | bytes 98312 | tf_op jit(solution)/shard_map/ppermute | solution.py:50
  4.0 3.9 %collective-permute-start = (bf16[32,512]{1,0:T(8,128)(2,1)S(1)}, bf16[32,512]{1,0:T(8,128)(2,1)S(1)}, u32[]{:S(2)}, u32[]{:S(2)}) collective-permute-start(bf16[32,512]{1,0:T(8,128)(2,1)S(1)} %pack_body.1.refs_0_), channel_id=1, source_target_pairs={{0,1},{1,0},{2,3},{3,2},{4,5},{5,4},{6,7},{7,6},{8,9},{9,8},{10,11... | collective-permute-start | bytes 98312 | tf_op jit(solution)/shard_map/ppermute | solution.py:50
  4.2 0.7 copy-start.9
  4.9 1.2 %copy-start = (bf16[1,2048,256]{2,1,0:T(8,128)(2,1)S(1)}, bf16[1,2048,256]{2,1,0:T(8,128)(2,1)}, u32[]{:S(2)}) copy-start(bf16[1,2048,256]{2,1,0:T(8,128)(2,1)} %param.6) | copy-start | bytes 3145732
  6.1 1.2 %copy-start.4 = (bf16[1,2048,256]{2,1,0:T(8,128)(2,1)S(1)}, bf16[1,2048,256]{2,1,0:T(8,128)(2,1)}, u32[]{:S(2)}) copy-start(bf16[1,2048,256]{2,1,0:T(8,128)(2,1)} %param.7) | copy-start | bytes 3145732
  10.3 5.9 %copy-start.12 = (bf16[4,128,512]{2,1,0:T(8,128)(2,1)S(1)}, bf16[4,128,512]{2,1,0:T(8,128)(2,1)}, u32[]{:S(2)}) copy-start(bf16[4,128,512]{2,1,0:T(8,128)(2,1)} %refs_0_.3) | copy-start | bytes 1572868
  10.3 31.0 %all-to-all-start.1 = ((bf16[8,4,64,256]{3,2,1,0:T(8,128)(2,1)}), bf16[8,4,64,256]{3,2,1,0:T(8,128)(2,1)S(1)}, u32[]{:S(2)}, u32[]{:S(2)}) async-start(bf16[8,4,64,256]{3,2,1,0:T(8,128)(2,1)} %bitcast.6), calls=%async_computation.1 | async-start | bytes 2097152 | tf_op jit(solution)/shard_map/all_to_all | solution.py:369
  16.2 12.6 %collective-permute-start.4 = (bf16[4,128,512]{2,1,0:T(8,128)(2,1)S(1)}, bf16[4,128,512]{2,1,0:T(8,128)(2,1)S(1)}, u32[]{:S(2)}, u32[]{:S(2)}) collective-permute-start(bf16[4,128,512]{2,1,0:T(8,128)(2,1)S(1)} %copy-done.12), channel_id=1, source_target_pairs={{0,2},{1,3},{2,0},{3,1},{4,6},{5,7},{6,4},{7,5},{8,10},{9,11},{10,... | collective-permute-start | bytes 1572872 | tf_op jit(solution)/shard_map/ppermute | solution.py:50
  17.3 13.2 %collective-permute-start.3 = (bf16[4,128,512]{2,1,0:T(8,128)(2,1)S(1)}, bf16[4,128,512]{2,1,0:T(8,128)(2,1)S(1)}, u32[]{:S(2)}, u32[]{:S(2)}) collective-permute-start(bf16[4,128,512]{2,1,0:T(8,128)(2,1)S(1)} %copy-done.12), channel_id=1, source_target_pairs={{0,1},{1,0},{2,3},{3,2},{4,5},{5,4},{6,7},{7,6},{8,9},{9,8},{10,11... | collective-permute-start | bytes 1572872 | tf_op jit(solution)/shard_map/ppermute | solution.py:50
  28.8 4.1 %copy-start.13 = (bf16[4,128,512]{2,1,0:T(8,128)(2,1)}, bf16[4,128,512]{2,1,0:T(8,128)(2,1)S(1)}, u32[]{:S(2)}) copy-start(bf16[4,128,512]{2,1,0:T(8,128)(2,1)S(1)} %collective-permute-done.4.refs_2_) | copy-start | bytes 1572868
  28.8 3.3 %collective-permute-start.5 = (bf16[4,128,512]{2,1,0:T(8,128)(2,1)S(1)}, bf16[4,128,512]{2,1,0:T(8,128)(2,1)S(1)}, u32[]{:S(2)}, u32[]{:S(2)}) collective-permute-start(bf16[4,128,512]{2,1,0:T(8,128)(2,1)S(1)} %collective-permute-done.4.refs_2_), channel_id=1, source_target_pairs={{0,1},{1,0},{2,3},{3,2},{4,5},{5,4},{6,7},{7,6},{8,9},{9,8},{10,11... | collective-permute-start | bytes 1572872 | tf_op jit(solution)/shard_map/ppermute | solution.py:50
  30.5 2.3 %copy-start.14 = (bf16[4,128,512]{2,1,0:T(8,128)(2,1)}, bf16[4,128,512]{2,1,0:T(8,128)(2,1)S(1)}, u32[]{:S(2)}) copy-start(bf16[4,128,512]{2,1,0:T(8,128)(2,1)S(1)} %collective-permute-done.3.refs_1_) | copy-start | bytes 1572868
  32.1 0.8 %copy-start.15 = (bf16[4,128,512]{2,1,0:T(8,128)(2,1)}, bf16[4,128,512]{2,1,0:T(8,128)(2,1)S(1)}, u32[]{:S(2)}) copy-start(bf16[4,128,512]{2,1,0:T(8,128)(2,1)S(1)} %collective-permute-done.5.refs_3_) | copy-start | bytes 1572868
  39.0 6.8 %copy-start.1 = (bf16[1,2048,256]{2,1,0:T(8,128)(2,1)S(1)}, bf16[1,2048,256]{2,1,0:T(8,128)(2,1)}, u32[]{:S(2)}) copy-start(bf16[1,2048,256]{2,1,0:T(8,128)(2,1)} %param.6) | copy-start | bytes 3145732
  39.0 6.8 %copy-start.11 = (s32[512]{0:T(512)S(1)}, s32[512]{0:T(512)}, u32[]{:S(2)}) copy-start(s32[512]{0:T(512)} %param.11) | copy-start | bytes 6148
  41.3 1.0 %copy-start.2 = (bf16[8,4,64,256]{3,2,1,0:T(8,128)(2,1)}, bf16[8,4,64,256]{3,2,1,0:T(8,128)(2,1)S(1)}, u32[]{:S(2)}) copy-start(bf16[8,4,64,256]{3,2,1,0:T(8,128)(2,1)S(1)} %all-to-all-done.1.refs_0_) | copy-start | bytes 3145732
  42.3 28.3 %all-to-all-start = ((bf16[8,4,64,256]{3,2,1,0:T(8,128)(2,1)}), bf16[8,4,64,256]{3,2,1,0:T(8,128)(2,1)S(1)}, u32[]{:S(2)}, u32[]{:S(2)}) async-start(bf16[8,4,64,256]{3,2,1,0:T(8,128)(2,1)} %mix_body.1), calls=%async_computation | async-start | bytes 2097152 | tf_op jit(solution)/shard_map/all_to_all | solution.py:398
  45.8 1.2 %copy-start.3 = (bf16[8,4,64,256]{3,2,1,0:T(8,128)(2,1)S(1)}, bf16[8,4,64,256]{3,2,1,0:T(8,128)(2,1)}, u32[]{:S(2)}) copy-start(bf16[8,4,64,256]{3,2,1,0:T(8,128)(2,1)} %copy-done.2) | copy-start | bytes 3145732
  49.6 1.0 %copy-start.7 = (bf16[4,512,256]{2,1,0:T(8,128)(2,1)}, bf16[4,512,256]{2,1,0:T(8,128)(2,1)S(1)}, u32[]{:S(2)}) copy-start(bf16[4,512,256]{2,1,0:T(8,128)(2,1)S(1)} %get-tuple-element.37.refs_4_) | copy-start | bytes 3145732
  50.6 2.9 %collective-permute-start.6 = (bf16[4,128,512]{2,1,0:T(8,128)(2,1)S(1)}, bf16[4,128,512]{2,1,0:T(8,128)(2,1)S(1)}, u32[]{:S(2)}, u32[]{:S(2)}) collective-permute-start(bf16[4,128,512]{2,1,0:T(8,128)(2,1)S(1)} %get-tuple-element.34), channel_id=1, source_target_pairs={{0,1},{1,0},{2,3},{3,2},{4,5},{5,4},{6,7},{7,6},{8,9},{9,8},{10,11... | collective-permute-start | bytes 1572872 | tf_op jit(solution)/shard_map/ppermute | solution.py:50
  51.9 2.3 %collective-permute-start.7 = (bf16[4,128,512]{2,1,0:T(8,128)(2,1)S(1)}, bf16[4,128,512]{2,1,0:T(8,128)(2,1)S(1)}, u32[]{:S(2)}, u32[]{:S(2)}) collective-permute-start(bf16[4,128,512]{2,1,0:T(8,128)(2,1)S(1)} %get-tuple-element.35), channel_id=1, source_target_pairs={{0,1},{1,0},{2,3},{3,2},{4,5},{5,4},{6,7},{7,6},{8,9},{9,8},{10,11... | collective-permute-start | bytes 1572872 | tf_op jit(solution)/shard_map/ppermute | solution.py:50
  55.0 8.9 %collective-permute-start.9 = (bf16[1,128,512]{2,1,0:T(8,128)(2,1)}, bf16[1,128,512]{2,1,0:T(8,128)(2,1)S(1)}, u32[]{:S(2)}, u32[]{:S(2)}) collective-permute-start(bf16[1,128,512]{2,1,0:T(8,128)(2,1)} %get-tuple-element.41), channel_id=1, source_target_pairs={{0,2},{1,3},{2,0},{3,1},{4,6},{5,7},{6,4},{7,5},{8,10},{9,11},{10,... | collective-permute-start | bytes 393224 | tf_op jit(solution)/shard_map/ppermute | solution.py:50
  56.1 7.8 %collective-permute-start.10 = (bf16[1,128,512]{2,1,0:T(8,128)(2,1)}, bf16[1,128,512]{2,1,0:T(8,128)(2,1)S(1)}, u32[]{:S(2)}, u32[]{:S(2)}) collective-permute-start(bf16[1,128,512]{2,1,0:T(8,128)(2,1)} %get-tuple-element.42), channel_id=1, source_target_pairs={{0,2},{1,3},{2,0},{3,1},{4,6},{5,7},{6,4},{7,5},{8,10},{9,11},{10,... | collective-permute-start | bytes 393224 | tf_op jit(solution)/shard_map/ppermute | solution.py:50
  56.5 9.1 %collective-permute-start.11 = (bf16[1,128,512]{2,1,0:T(8,128)(2,1)S(1)}, bf16[1,128,512]{2,1,0:T(8,128)(2,1)S(1)}, u32[]{:S(2)}, u32[]{:S(2)}) collective-permute-start(bf16[1,128,512]{2,1,0:T(8,128)(2,1)S(1)} %get-tuple-element.43), channel_id=1, source_target_pairs={{0,2},{1,3},{2,0},{3,1},{4,6},{5,7},{6,4},{7,5},{8,10},{9,11},{10,... | collective-permute-start | bytes 393224 | tf_op jit(solution)/shard_map/ppermute | solution.py:50
  57.6 10.8 %collective-permute-start.8 = (bf16[1,128,512]{2,1,0:T(8,128)(2,1)S(1)}, bf16[1,128,512]{2,1,0:T(8,128)(2,1)S(1)}, u32[]{:S(2)}, u32[]{:S(2)}) collective-permute-start(bf16[1,128,512]{2,1,0:T(8,128)(2,1)S(1)} %get-tuple-element.36), channel_id=1, source_target_pairs={{0,2},{1,3},{2,0},{3,1},{4,6},{5,7},{6,4},{7,5},{8,10},{9,11},{10,... | collective-permute-start | bytes 393224 | tf_op jit(solution)/shard_map/ppermute | solution.py:50
  70.6 4.6 %copy-start.5 = (bf16[2048,256]{1,0:T(8,128)(2,1)S(1)}, bf16[2048,256]{1,0:T(8,128)(2,1)}, u32[]{:S(2)}) copy-start(bf16[2048,256]{1,0:T(8,128)(2,1)} %get-tuple-element.38.back_ref) | copy-start | bytes 3145732
  70.6 4.6 %copy-start.6 = (bf16[2048,256]{1,0:T(8,128)(2,1)S(1)}, bf16[2048,256]{1,0:T(8,128)(2,1)}, u32[]{:S(2)}) copy-start(bf16[2048,256]{1,0:T(8,128)(2,1)} %get-tuple-element.46.h_ref) | copy-start | bytes 3145732
  71.9 6.4 %collective-permute-start.12 = (bf16[32,512]{1,0:T(8,128)(2,1)S(1)}, bf16[32,512]{1,0:T(8,128)(2,1)S(1)}, u32[]{:S(2)}, u32[]{:S(2)}) collective-permute-start(bf16[32,512]{1,0:T(8,128)(2,1)S(1)} %get-tuple-element.48), channel_id=1, source_target_pairs={{0,1},{1,0},{2,3},{3,2},{4,5},{5,4},{6,7},{7,6},{8,9},{9,8},{10,11... | collective-permute-start | bytes 98312 | tf_op jit(solution)/shard_map/ppermute | solution.py:50
  73.5 4.9 %collective-permute-start.13 = (bf16[32,512]{1,0:T(8,128)(2,1)S(1)}, bf16[32,512]{1,0:T(8,128)(2,1)S(1)}, u32[]{:S(2)}, u32[]{:S(2)}) collective-permute-start(bf16[32,512]{1,0:T(8,128)(2,1)S(1)} %get-tuple-element.49), channel_id=1, source_target_pairs={{0,2},{1,3},{2,0},{3,1},{4,6},{5,7},{6,4},{7,5},{8,10},{9,11},{10,... | collective-permute-start | bytes 98312 | tf_op jit(solution)/shard_map/ppermute | solution.py:50
  74.6 3.8 %collective-permute-start.14 = (bf16[32,512]{1,0:T(8,128)(2,1)S(1)}, bf16[32,512]{1,0:T(8,128)(2,1)S(1)}, u32[]{:S(2)}, u32[]{:S(2)}) collective-permute-start(bf16[32,512]{1,0:T(8,128)(2,1)S(1)} %get-tuple-element.50), channel_id=1, source_target_pairs={{0,3},{1,2},{2,1},{3,0},{4,7},{5,6},{6,5},{7,4},{8,11},{9,10},{10,... | collective-permute-start | bytes 98312 | tf_op jit(solution)/shard_map/ppermute | solution.py:50
  75.2 0.7 copy-start.10

commit v17 on v16

--- a/solution.py
+++ b/solution.py
@@ -50,12 +50,11 @@
     return lax.ppermute(value, axis, [(p, p ^ step) for p in range(size)])
 
 
-def ring_at(place, size):
-    return jnp.where(place < size // 2, 2 * place, 2 * size - 1 - 2 * place)
-
-
 def ring_of(size):
-    return [2 * p if p < size // 2 else 2 * size - 1 - 2 * p for p in range(size)]
+    low, high = list(range(0, size // 2, 2)), list(range(size // 2, size, 2))
+    up = [v for pair in zip(low, high) for v in pair]
+    down = [v + 1 for pair in zip(low[::-1], high[::-1]) for v in pair]
+    return up + down
 
 
 def after(value, *earlier):
@@ -306,8 +305,11 @@
         total = total + piece[...].astype(F32)
     lane = iota((j_here, lanes), 1)
     blocks = order // seq
-    place_i = iota((rows, lanes), 1) // LANE_GROUP
-    keep = (iota((rows, lanes), 0) % order) == ring_at(place_i // blocks, seq) * blocks + place_i % blocks
+    place_i = iota((1, lanes), 1) // LANE_GROUP
+    actual = place_i % blocks
+    for p, there in enumerate(ring_of(seq)):
+        actual = jnp.where(place_i // blocks == p, actual + there * blocks, actual)
+    keep = (iota((rows, lanes), 0) % order) == actual
     result = jnp.zeros((rows, j_here), F32)
     for g in range(groups):
         place = one_hot(iota((j_here, lanes), 0) == g * LANE_GROUP + lane % LANE_GROUP)
@@ -510,7 +512,7 @@
 
     def shards(*args):
         j_here, m_here, count = args[3].shape
-        if batch == 4 and seq & (seq - 1) == 0 and j_here % LANE_GROUP == 0 and m_here % 8 == 0 and count <= 32:
+        if batch == 4 and seq & (seq - 1) == 0 and seq % 4 == 0 and j_here % LANE_GROUP == 0 and m_here % 8 == 0 and count <= 32:
             return packed_shards(*args, batch, seq)
         return wide_shards(*args)
 

time: 79.9 us -> 83.9 us (1.050)
  the two profiles are of different devices: /device:TPU:9 before, /device:TPU:0 now
where the time goes in v17:
time: 83.9 us; the launch traced here: 83.4 us
  waiting for transfers between devices  28.3 us (34%)
  Pallas kernels  24.5 us (29%)
  starting transfers between devices  21 us (25%)
  local copies, waits for them, and re-layouts  8.64 us (10%)
  between operations  0.84 us (1%)
    pallas_call x11, Pallas kernels, call(): pl.pallas_call(body, name=name, out_shape=outs, in_specs=[pl.BlockSpec(me...  24.5 us
    ppermute x15, waiting for transfers between devices, swap(): return lax.ppermute(value, axis, [(p, p ^ step) for p in range(size)])  20.5 us
    ppermute x15, starting transfers between devices, swap(): return lax.ppermute(value, axis, [(p, p ^ step) for p in range(size)])  11.2 us
    unnamed x32, local copies, waits for them, and re-layouts  8.64 us
    all_to_all x1, starting transfers between devices, packed_shards(): lax.all_to_all(dep('h0', back[0]).reshape(seq, blocks, j_here, width), 's...  6.24 us
    all_to_all x1, waiting for transfers between devices, packed_shards(): lax.all_to_all(dep('h0', back[0]).reshape(seq, blocks, j_here, width), 's...  4.3 us
    all_to_all x1, starting transfers between devices, packed_shards(): lax.all_to_all(dep('H0', regrouped[0]), 'seq', 0, 0, axis_index_groups=[r...  3.63 us
    all_to_all x1, waiting for transfers between devices, packed_shards(): lax.all_to_all(dep('H0', regrouped[0]), 'seq', 0, 0, axis_index_groups=[r...  3.58 us
  transfers between devices with their start and end apart: 17, of which 8 were waited for; matrix products, arithmetic and copies ran while one was open for 0% of the time, Pallas kernels for 23%

profile of v17, /device:TPU:0, one launch (start us, length us, event | category | flops | bytes accessed | tf_op | source)
XLA Modules:
  0.0 83.4 jit_solution(7731041716138415747)
XLA Ops:
  0.6 0.0 copy-start.8
  0.6 0.8 copy-done.8
  1.5 0.4 pack_body.1.refs_0_
  1.9 2.4 %collective-permute-start.2 = (bf16[32,512]{1,0:T(8,128)(2,1)S(1)}, bf16[32,512]{1,0:T(8,128)(2,1)S(1)}, u32[]{:S(2)}, u32[]{:S(2)}) collective-permute-start(bf16[32,512]{1,0:T(8,128)(2,1)S(1)} %pack_body.1.refs_0_), channel_id=1, source_target_pairs={{0,3},{1,2},{2,1},{3,0},{4,7},{5,6},{6,5},{7,4},{8,11},{9,10},{10,... | collective-permute-start | bytes 98312 | tf_op jit(solution)/shard_map/ppermute | solution.py:50
  4.3 0.6 collective-permute-start.1
  5.0 0.0 collective-permute-start
  5.0 0.7 copy-done.9
  5.7 1.2 %copy-done = bf16[1,2048,256]{2,1,0:T(8,128)(2,1)S(1)} copy-done((bf16[1,2048,256]{2,1,0:T(8,128)(2,1)S(1)}, bf16[1,2048,256]{2,1,0:T(8,128)(2,1)}, u32[]{:S(2)}) %copy-start) | copy-done | bytes 1048600
  6.9 1.2 %copy-done.4 = bf16[1,2048,256]{2,1,0:T(8,128)(2,1)S(1)} copy-done((bf16[1,2048,256]{2,1,0:T(8,128)(2,1)S(1)}, bf16[1,2048,256]{2,1,0:T(8,128)(2,1)}, u32[]{:S(2)}) %copy-start.4) | copy-done | bytes 1048600
  8.1 0.5 gate_body.1.refs_4_.refs_1_
  8.6 0.0 collective-permute-done.2.refs_3_
  8.6 0.0 collective-permute-done.1.refs_2_
  8.7 0.0 collective-permute-done.refs_1_
  8.7 2.4 %regroup_back_body.1 = (bf16[32,64,256]{2,1,0:T(8,128)(2,1)}, bf16[4,32,512]{2,1,0:T(8,128)(2,1)S(1)}) custom-call(bf16[32,512]{1,0:T(8,128)(2,1)S(1)} %pack_body.1.refs_0_, bf16[32,512]{1,0:T(8,128)(2,1)S(1)} %collective-permute-done.refs_1_, bf16[32,512]{1,0:T(8,128)(2,1)S(1)} %collective-permute-done.1.refs_2_, ...), custom_call_target="tpu_custom_call" | custom-call | tf_op jit(solution)/shard_map/regroup_back_body/pallas_call | solution.py:31
  11.1 0.0 copy-start.12
  11.1 6.2 %all-to-all-start.1 = ((bf16[8,4,64,256]{3,2,1,0:T(8,128)(2,1)}), bf16[8,4,64,256]{3,2,1,0:T(8,128)(2,1)S(1)}, u32[]{:S(2)}, u32[]{:S(2)}) async-start(bf16[8,4,64,256]{3,2,1,0:T(8,128)(2,1)} %bitcast.6), calls=%async_computation.1 | async-start | bytes 2097152 | tf_op jit(solution)/shard_map/all_to_all | solution.py:371
  17.4 0.0 copy-done.12
  17.4 1.6 %collective-permute-start.4 = (bf16[4,128,512]{2,1,0:T(8,128)(2,1)S(1)}, bf16[4,128,512]{2,1,0:T(8,128)(2,1)S(1)}, u32[]{:S(2)}, u32[]{:S(2)}) collective-permute-start(bf16[4,128,512]{2,1,0:T(8,128)(2,1)S(1)} %copy-done.12), channel_id=1, source_target_pairs={{0,2},{1,3},{2,0},{3,1},{4,6},{5,7},{6,4},{7,5},{8,10},{9,11},{10,... | collective-permute-start | bytes 1572872 | tf_op jit(solution)/shard_map/ppermute | solution.py:50
  18.9 0.0 collective-permute-start.3
  18.9 12.3 %collective-permute-done.4.refs_2_ = bf16[4,128,512]{2,1,0:T(8,128)(2,1)S(1)} collective-permute-done((bf16[4,128,512]{2,1,0:T(8,128)(2,1)S(1)}, bf16[4,128,512]{2,1,0:T(8,128)(2,1)S(1)}, u32[]{:S(2)}, u32[]{:S(2)}) %collective-permute-start.4) | collective-permute-done | bytes 524320 | tf_op jit(solution)/shard_map/ppermute | solution.py:50
  31.2 0.0 collective-permute-start.5
  31.2 0.0 collective-permute-done.3.refs_1_
  31.2 0.0 copy-start.14
  31.2 1.9 %collective-permute-done.5.refs_3_ = bf16[4,128,512]{2,1,0:T(8,128)(2,1)S(1)} collective-permute-done((bf16[4,128,512]{2,1,0:T(8,128)(2,1)S(1)}, bf16[4,128,512]{2,1,0:T(8,128)(2,1)S(1)}, u32[]{:S(2)}, u32[]{:S(2)}) %collective-permute-start.5) | collective-permute-done | bytes 524320 | tf_op jit(solution)/shard_map/ppermute | solution.py:50
  33.1 0.8 copy-done.15
  33.9 0.0 copy-done.13
  33.9 0.0 copy-done.14
  33.9 6.2 %mix_body.1 = bf16[8,4,64,256]{3,2,1,0:T(8,128)(2,1)} custom-call(bf16[4,128,512]{2,1,0:T(8,128)(2,1)} %refs_0_.3, bf16[4,128,512]{2,1,0:T(8,128)(2,1)} %copy-done.14, bf16[4,128,512]{2,1,0:T(8,128)(2,1)} %copy-done.13, bf16[4,128,512]{2,1,0:T(8,128)(2,1)} %copy-done.15, bf16[2048,256]{1,0:T(8,128)(2,1)} %bitcast.13, s32[1,512]{1,0:T(1,128)} %bitcast.25), custom_call_target="tpu_custom_call" | custom-call | tf_op jit(solution)/shard_map/mix_body/pallas_call | solution.py:31
  40.1 0.0 copy-start.1
  40.1 0.0 copy-start.11
  40.1 4.3 %all-to-all-done.1.refs_0_ = bf16[8,4,64,256]{3,2,1,0:T(8,128)(2,1)S(1)} async-done(((bf16[8,4,64,256]{3,2,1,0:T(8,128)(2,1)}), bf16[8,4,64,256]{3,2,1,0:T(8,128)(2,1)S(1)}, u32[]{:S(2)}, u32[]{:S(2)}) %all-to-all-start.1) | async-done | bytes 1048608 | tf_op jit(solution)/shard_map/all_to_all | solution.py:371
  44.4 1.0 %copy-done.2 = bf16[8,4,64,256]{3,2,1,0:T(8,128)(2,1)} copy-done((bf16[8,4,64,256]{3,2,1,0:T(8,128)(2,1)}, bf16[8,4,64,256]{3,2,1,0:T(8,128)(2,1)S(1)}, u32[]{:S(2)}) %copy-start.2) | copy-done | bytes 1048600
  45.4 3.6 %all-to-all-start = ((bf16[8,4,64,256]{3,2,1,0:T(8,128)(2,1)}), bf16[8,4,64,256]{3,2,1,0:T(8,128)(2,1)S(1)}, u32[]{:S(2)}, u32[]{:S(2)}) async-start(bf16[8,4,64,256]{3,2,1,0:T(8,128)(2,1)} %mix_body.1), calls=%async_computation | async-start | bytes 2097152 | tf_op jit(solution)/shard_map/all_to_all | solution.py:400
  49.0 0.0 copy-done.1
  49.0 1.2 %copy-done.3 = bf16[8,4,64,256]{3,2,1,0:T(8,128)(2,1)S(1)} copy-done((bf16[8,4,64,256]{3,2,1,0:T(8,128)(2,1)S(1)}, bf16[8,4,64,256]{3,2,1,0:T(8,128)(2,1)}, u32[]{:S(2)}) %copy-start.3) | copy-done | bytes 1048600
  50.3 2.5 %first_grad_body.1 = (bf16[4,128,512]{2,1,0:T(8,128)(2,1)S(1)}, bf16[4,128,512]{2,1,0:T(8,128)(2,1)S(1)}, bf16[4,128,512]{2,1,0:T(8,128)(2,1)S(1)}, bf16[4,128,5...) custom-call(bf16[8,4,64,256]{3,2,1,0:T(8,128)(2,1)S(1)} %copy-done.3, bf16[2048,256]{1,0:T(8,128)(2,1)S(1)} %bitcast.16, ...), custom_call_target="tpu_custom_call" | custom-call | tf_op jit(solution)/shard_map/first_grad_body/pallas_call | solution.py:31
  52.8 1.0 %copy-done.7 = bf16[4,512,256]{2,1,0:T(8,128)(2,1)} copy-done((bf16[4,512,256]{2,1,0:T(8,128)(2,1)}, bf16[4,512,256]{2,1,0:T(8,128)(2,1)S(1)}, u32[]{:S(2)}) %copy-start.7) | copy-done | bytes 1048600
  53.8 0.0 collective-permute-start.6
  53.8 0.5 collective-permute-start.7
  54.3 1.4 %collective-permute-done.6.got_a = bf16[4,128,512]{2,1,0:T(8,128)(2,1)S(1)} collective-permute-done((bf16[4,128,512]{2,1,0:T(8,128)(2,1)S(1)}, bf16[4,128,512]{2,1,0:T(8,128)(2,1)S(1)}, u32[]{:S(2)}, u32[]{:S(2)}) %collective-permute-start.6) | collective-permute-done | bytes 524320 | tf_op jit(solution)/shard_map/ppermute | solution.py:50
  55.7 0.7 collective-permute-done.7.got_b
  56.4 0.8 pair_body.1
  57.2 1.4 %collective-permute-start.9 = (bf16[1,128,512]{2,1,0:T(8,128)(2,1)}, bf16[1,128,512]{2,1,0:T(8,128)(2,1)S(1)}, u32[]{:S(2)}, u32[]{:S(2)}) collective-permute-start(bf16[1,128,512]{2,1,0:T(8,128)(2,1)} %get-tuple-element.41), channel_id=1, source_target_pairs={{0,2},{1,3},{2,0},{3,1},{4,6},{5,7},{6,4},{7,5},{8,10},{9,11},{10,... | collective-permute-start | bytes 393224 | tf_op jit(solution)/shard_map/ppermute | solution.py:50
  58.6 0.6 collective-permute-start.10
  59.2 1.4 %collective-permute-start.11 = (bf16[1,128,512]{2,1,0:T(8,128)(2,1)S(1)}, bf16[1,128,512]{2,1,0:T(8,128)(2,1)S(1)}, u32[]{:S(2)}, u32[]{:S(2)}) collective-permute-start(bf16[1,128,512]{2,1,0:T(8,128)(2,1)S(1)} %get-tuple-element.43), channel_id=1, source_target_pairs={{0,2},{1,3},{2,0},{3,1},{4,6},{5,7},{6,4},{7,5},{8,10},{9,11},{10,... | collective-permute-start | bytes 393224 | tf_op jit(solution)/shard_map/ppermute | solution.py:50
  60.6 0.6 collective-permute-start.8
  61.3 6.0 %mix_back_body.1 = (bf16[2048,256]{1,0:T(8,128)(2,1)}, bf16[2048,256]{1,0:T(8,128)(2,1)}) custom-call(bf16[4,128,512]{2,1,0:T(8,128)(2,1)} %refs_0_.3, bf16[4,128,512]{2,1,0:T(8,128)(2,1)} %copy-done.14, bf16[4,128,512]{2,1,0:T(8,128)(2,1)} %copy-done.13, bf16[4,128,512]{2,1,0:T(8,128)(2,1)} %copy-done.15, bf16[4,512,256]{2,1,0:T(8,128)(2,1)} %copy-done.7, ...), custom_call_target="tpu_custom_call" | custom-call | tf_op jit(solution)/shard_map/mix_back_body/pallas_call | solution.py:31
  67.3 0.0 collective-permute-done.9.refs_1_
  67.3 0.0 collective-permute-done.10.refs_2_
  67.3 2.1 %collective-permute-done.11.refs_3_ = bf16[1,128,512]{2,1,0:T(8,128)(2,1)S(1)} collective-permute-done((bf16[1,128,512]{2,1,0:T(8,128)(2,1)S(1)}, bf16[1,128,512]{2,1,0:T(8,128)(2,1)S(1)}, u32[]{:S(2)}, u32[]{:S(2)}) %collective-permute-start.11) | collective-permute-done | bytes 131104 | tf_op jit(solution)/shard_map/ppermute | solution.py:50
  69.4 2.0 %collective-permute-done.8.refs_0_ = bf16[1,128,512]{2,1,0:T(8,128)(2,1)S(1)} collective-permute-done((bf16[1,128,512]{2,1,0:T(8,128)(2,1)S(1)}, bf16[1,128,512]{2,1,0:T(8,128)(2,1)S(1)}, u32[]{:S(2)}, u32[]{:S(2)}) %collective-permute-start.8) | collective-permute-done | bytes 131104 | tf_op jit(solution)/shard_map/ppermute | solution.py:50
  71.4 0.9 %add_body.1 = bf16[4,128,512]{2,1,0:T(8,128)(2,1)} custom-call(f32[4,128,512]{2,1,0:T(8,128)S(1)} %get-tuple-element.40.own, bf16[1,128,512]{2,1,0:T(8,128)(2,1)S(1)} %collective-permute-done.8.refs_0_, bf16[1,128,512]{2,1,0:T(8,128)(2,1)S(1)} %collective-permute-done.9.refs_1_, bf16[1,128,512]{2,1,0:T(8,128)(2,1)S(1)} %collective-permute-done.10.refs_2_, ...), custom_call_target="tpu_custom_call" | custom-call | tf_op jit(solution)/shard_map/add_body/pallas_call | solution.py:31
  72.3 3.6 %all-to-all-done = bf16[8,4,64,256]{3,2,1,0:T(8,128)(2,1)S(1)} async-done(((bf16[8,4,64,256]{3,2,1,0:T(8,128)(2,1)}), bf16[8,4,64,256]{3,2,1,0:T(8,128)(2,1)S(1)}, u32[]{:S(2)}, u32[]{:S(2)}) %all-to-all-start) | async-done | bytes 1048608 | tf_op jit(solution)/shard_map/all_to_all | solution.py:400
  75.9 1.3 %second_grad_body.1 = (bf16[32,512]{1,0:T(8,128)(2,1)S(1)}, bf16[32,512]{1,0:T(8,128)(2,1)S(1)}, bf16[32,512]{1,0:T(8,128)(2,1)S(1)}, bf16[32,512]{1,0:T(8,128)(2,1)S(1)}) custom-call(bf16[32,64,256]{2,1,0:T(8,128)(2,1)S(1)} %bitcast.17, bf16[2048,256]{1,0:T(8,128)(2,1)S(1)} %gate_body.1.refs_4_.refs_1_), custom_call_target="tpu_custom_call" | custom-call | tf_op jit(solution)/shard_map/second_grad_body/pallas_call | solution.py:31
  77.2 0.1 collective-permute-start.12
  77.3 1.5 %collective-permute-start.13 = (bf16[32,512]{1,0:T(8,128)(2,1)S(1)}, bf16[32,512]{1,0:T(8,128)(2,1)S(1)}, u32[]{:S(2)}, u32[]{:S(2)}) collective-permute-start(bf16[32,512]{1,0:T(8,128)(2,1)S(1)} %get-tuple-element.49), channel_id=1, source_target_pairs={{0,2},{1,3},{2,0},{3,1},{4,6},{5,7},{6,4},{7,5},{8,10},{9,11},{10,... | collective-permute-start | bytes 98312 | tf_op jit(solution)/shard_map/ppermute | solution.py:50
  78.7 0.4 collective-permute-start.14
  79.2 0.0 copy-done.5
  79.2 0.7 copy-done.10
  79.8 2.5 %tokens_body.1 = bf16[2048,256]{1,0:T(8,128)(2,1)} custom-call(bf16[32,64,256]{2,1,0:T(8,128)(2,1)S(1)} %bitcast.18, bf16[4,32,512]{2,1,0:T(8,128)(2,1)S(1)} %get-tuple-element.45.second_ref, bf16[2048,256]{1,0:T(8,128)(2,1)S(1)} %copy-done.6, s32[1,256]{1,0:T(1,128)S(1)} %bitcast.24, bf16[2048,256]{1,0:T(8,128)(2,1)S(1)} %copy-done.5), custom_call_target="tpu_custom_call" | custom-call | tf_op jit(solution)/shard_map/tokens_body/pallas_call | solution.py:31
  82.3 0.0 collective-permute-done.12.refs_1_
  82.3 0.0 collective-permute-done.13.refs_2_
  82.3 0.0 collective-permute-done.14.refs_3_
  82.3 1.1 %unpack_body.1 = bf16[256,64]{1,0:T(8,128)(2,1)} custom-call(bf16[32,512]{1,0:T(8,128)(2,1)S(1)} %get-tuple-element.47.refs_0_, bf16[32,512]{1,0:T(8,128)(2,1)S(1)} %collective-permute-done.12.refs_1_, bf16[32,512]{1,0:T(8,128)(2,1)S(1)} %collective-permute-done.13.refs_2_, bf16[32,512]{1,0:T(8,128)(2,1)S(1)} %collective-permute-done.14.refs_3_), custom_call_target="tpu_custom_call" | custom-call | tf_op jit(solution)/shard_map/unpack_body/pallas_call | solution.py:31
  (13 shorter events, 0.0 us)
Async XLA Ops:
  0.6 0.8 %copy-start.8 = (bf16[64,8,32]{0,2,1:T(8,128)(2,1)S(1)}, bf16[64,8,32]{0,2,1:T(8,128)(2,1)}, u32[]{:S(2)}) copy-start(bf16[64,8,32]{0,2,1:T(8,128)(2,1)} %param.9) | copy-start | bytes 98308
  1.9 6.7 %collective-permute-start.2 = (bf16[32,512]{1,0:T(8,128)(2,1)S(1)}, bf16[32,512]{1,0:T(8,128)(2,1)S(1)}, u32[]{:S(2)}, u32[]{:S(2)}) collective-permute-start(bf16[32,512]{1,0:T(8,128)(2,1)S(1)} %pack_body.1.refs_0_), channel_id=1, source_target_pairs={{0,3},{1,2},{2,1},{3,0},{4,7},{5,6},{6,5},{7,4},{8,11},{9,10},{10,... | collective-permute-start | bytes 98312 | tf_op jit(solution)/shard_map/ppermute | solution.py:50
  4.3 4.3 %collective-permute-start.1 = (bf16[32,512]{1,0:T(8,128)(2,1)S(1)}, bf16[32,512]{1,0:T(8,128)(2,1)S(1)}, u32[]{:S(2)}, u32[]{:S(2)}) collective-permute-start(bf16[32,512]{1,0:T(8,128)(2,1)S(1)} %pack_body.1.refs_0_), channel_id=1, source_target_pairs={{0,2},{1,3},{2,0},{3,1},{4,6},{5,7},{6,4},{7,5},{8,10},{9,11},{10,... | collective-permute-start | bytes 98312 | tf_op jit(solution)/shard_map/ppermute | solution.py:50
  5.0 3.7 %collective-permute-start = (bf16[32,512]{1,0:T(8,128)(2,1)S(1)}, bf16[32,512]{1,0:T(8,128)(2,1)S(1)}, u32[]{:S(2)}, u32[]{:S(2)}) collective-permute-start(bf16[32,512]{1,0:T(8,128)(2,1)S(1)} %pack_body.1.refs_0_), channel_id=1, source_target_pairs={{0,1},{1,0},{2,3},{3,2},{4,5},{5,4},{6,7},{7,6},{8,9},{9,8},{10,11... | collective-permute-start | bytes 98312 | tf_op jit(solution)/shard_map/ppermute | solution.py:50
  5.0 0.7 copy-start.9
  5.7 1.2 %copy-start = (bf16[1,2048,256]{2,1,0:T(8,128)(2,1)S(1)}, bf16[1,2048,256]{2,1,0:T(8,128)(2,1)}, u32[]{:S(2)}) copy-start(bf16[1,2048,256]{2,1,0:T(8,128)(2,1)} %param.6) | copy-start | bytes 3145732
  6.9 1.2 %copy-start.4 = (bf16[1,2048,256]{2,1,0:T(8,128)(2,1)S(1)}, bf16[1,2048,256]{2,1,0:T(8,128)(2,1)}, u32[]{:S(2)}) copy-start(bf16[1,2048,256]{2,1,0:T(8,128)(2,1)} %param.7) | copy-start | bytes 3145732
  11.1 6.3 %copy-start.12 = (bf16[4,128,512]{2,1,0:T(8,128)(2,1)S(1)}, bf16[4,128,512]{2,1,0:T(8,128)(2,1)}, u32[]{:S(2)}) copy-start(bf16[4,128,512]{2,1,0:T(8,128)(2,1)} %refs_0_.3) | copy-start | bytes 1572868
  11.1 33.3 %all-to-all-start.1 = ((bf16[8,4,64,256]{3,2,1,0:T(8,128)(2,1)}), bf16[8,4,64,256]{3,2,1,0:T(8,128)(2,1)S(1)}, u32[]{:S(2)}, u32[]{:S(2)}) async-start(bf16[8,4,64,256]{3,2,1,0:T(8,128)(2,1)} %bitcast.6), calls=%async_computation.1 | async-start | bytes 2097152 | tf_op jit(solution)/shard_map/all_to_all | solution.py:371
  17.4 13.8 %collective-permute-start.4 = (bf16[4,128,512]{2,1,0:T(8,128)(2,1)S(1)}, bf16[4,128,512]{2,1,0:T(8,128)(2,1)S(1)}, u32[]{:S(2)}, u32[]{:S(2)}) collective-permute-start(bf16[4,128,512]{2,1,0:T(8,128)(2,1)S(1)} %copy-done.12), channel_id=1, source_target_pairs={{0,2},{1,3},{2,0},{3,1},{4,6},{5,7},{6,4},{7,5},{8,10},{9,11},{10,... | collective-permute-start | bytes 1572872 | tf_op jit(solution)/shard_map/ppermute | solution.py:50
  18.9 12.3 %collective-permute-start.3 = (bf16[4,128,512]{2,1,0:T(8,128)(2,1)S(1)}, bf16[4,128,512]{2,1,0:T(8,128)(2,1)S(1)}, u32[]{:S(2)}, u32[]{:S(2)}) collective-permute-start(bf16[4,128,512]{2,1,0:T(8,128)(2,1)S(1)} %copy-done.12), channel_id=1, source_target_pairs={{0,1},{1,0},{2,3},{3,2},{4,5},{5,4},{6,7},{7,6},{8,9},{9,8},{10,11... | collective-permute-start | bytes 1572872 | tf_op jit(solution)/shard_map/ppermute | solution.py:50
  31.2 2.7 %copy-start.13 = (bf16[4,128,512]{2,1,0:T(8,128)(2,1)}, bf16[4,128,512]{2,1,0:T(8,128)(2,1)S(1)}, u32[]{:S(2)}) copy-start(bf16[4,128,512]{2,1,0:T(8,128)(2,1)S(1)} %collective-permute-done.4.refs_2_) | copy-start | bytes 1572868
  31.2 1.9 %collective-permute-start.5 = (bf16[4,128,512]{2,1,0:T(8,128)(2,1)S(1)}, bf16[4,128,512]{2,1,0:T(8,128)(2,1)S(1)}, u32[]{:S(2)}, u32[]{:S(2)}) collective-permute-start(bf16[4,128,512]{2,1,0:T(8,128)(2,1)S(1)} %collective-permute-done.4.refs_2_), channel_id=1, source_target_pairs={{0,1},{1,0},{2,3},{3,2},{4,5},{5,4},{6,7},{7,6},{8,9},{9,8},{10,11... | collective-permute-start | bytes 1572872 | tf_op jit(solution)/shard_map/ppermute | solution.py:50
  31.2 2.7 %copy-start.14 = (bf16[4,128,512]{2,1,0:T(8,128)(2,1)}, bf16[4,128,512]{2,1,0:T(8,128)(2,1)S(1)}, u32[]{:S(2)}) copy-start(bf16[4,128,512]{2,1,0:T(8,128)(2,1)S(1)} %collective-permute-done.3.refs_1_) | copy-start | bytes 1572868
  33.1 0.8 copy-start.15
  40.1 8.9 %copy-start.1 = (bf16[1,2048,256]{2,1,0:T(8,128)(2,1)S(1)}, bf16[1,2048,256]{2,1,0:T(8,128)(2,1)}, u32[]{:S(2)}) copy-start(bf16[1,2048,256]{2,1,0:T(8,128)(2,1)} %param.6) | copy-start | bytes 3145732
  40.1 8.9 %copy-start.11 = (s32[512]{0:T(512)S(1)}, s32[512]{0:T(512)}, u32[]{:S(2)}) copy-start(s32[512]{0:T(512)} %param.11) | copy-start | bytes 6148
  44.4 1.0 %copy-start.2 = (bf16[8,4,64,256]{3,2,1,0:T(8,128)(2,1)}, bf16[8,4,64,256]{3,2,1,0:T(8,128)(2,1)S(1)}, u32[]{:S(2)}) copy-start(bf16[8,4,64,256]{3,2,1,0:T(8,128)(2,1)S(1)} %all-to-all-done.1.refs_0_) | copy-start | bytes 3145732
  45.4 30.5 %all-to-all-start = ((bf16[8,4,64,256]{3,2,1,0:T(8,128)(2,1)}), bf16[8,4,64,256]{3,2,1,0:T(8,128)(2,1)S(1)}, u32[]{:S(2)}, u32[]{:S(2)}) async-start(bf16[8,4,64,256]{3,2,1,0:T(8,128)(2,1)} %mix_body.1), calls=%async_computation | async-start | bytes 2097152 | tf_op jit(solution)/shard_map/all_to_all | solution.py:400
  49.0 1.2 %copy-start.3 = (bf16[8,4,64,256]{3,2,1,0:T(8,128)(2,1)S(1)}, bf16[8,4,64,256]{3,2,1,0:T(8,128)(2,1)}, u32[]{:S(2)}) copy-start(bf16[8,4,64,256]{3,2,1,0:T(8,128)(2,1)} %copy-done.2) | copy-start | bytes 3145732
  52.8 1.0 %copy-start.7 = (bf16[4,512,256]{2,1,0:T(8,128)(2,1)}, bf16[4,512,256]{2,1,0:T(8,128)(2,1)S(1)}, u32[]{:S(2)}) copy-start(bf16[4,512,256]{2,1,0:T(8,128)(2,1)S(1)} %get-tuple-element.37.refs_4_) | copy-start | bytes 3145732
  53.8 1.9 %collective-permute-start.6 = (bf16[4,128,512]{2,1,0:T(8,128)(2,1)S(1)}, bf16[4,128,512]{2,1,0:T(8,128)(2,1)S(1)}, u32[]{:S(2)}, u32[]{:S(2)}) collective-permute-start(bf16[4,128,512]{2,1,0:T(8,128)(2,1)S(1)} %get-tuple-element.34), channel_id=1, source_target_pairs={{0,1},{1,0},{2,3},{3,2},{4,5},{5,4},{6,7},{7,6},{8,9},{9,8},{10,11... | collective-permute-start | bytes 1572872 | tf_op jit(solution)/shard_map/ppermute | solution.py:50
  53.8 2.7 %collective-permute-start.7 = (bf16[4,128,512]{2,1,0:T(8,128)(2,1)S(1)}, bf16[4,128,512]{2,1,0:T(8,128)(2,1)S(1)}, u32[]{:S(2)}, u32[]{:S(2)}) collective-permute-start(bf16[4,128,512]{2,1,0:T(8,128)(2,1)S(1)} %get-tuple-element.35), channel_id=1, source_target_pairs={{0,1},{1,0},{2,3},{3,2},{4,5},{5,4},{6,7},{7,6},{8,9},{9,8},{10,11... | collective-permute-start | bytes 1572872 | tf_op jit(solution)/shard_map/ppermute | solution.py:50
  57.2 10.0 %collective-permute-start.9 = (bf16[1,128,512]{2,1,0:T(8,128)(2,1)}, bf16[1,128,512]{2,1,0:T(8,128)(2,1)S(1)}, u32[]{:S(2)}, u32[]{:S(2)}) collective-permute-start(bf16[1,128,512]{2,1,0:T(8,128)(2,1)} %get-tuple-element.41), channel_id=1, source_target_pairs={{0,2},{1,3},{2,0},{3,1},{4,6},{5,7},{6,4},{7,5},{8,10},{9,11},{10,... | collective-permute-start | bytes 393224 | tf_op jit(solution)/shard_map/ppermute | solution.py:50
  58.6 8.7 %collective-permute-start.10 = (bf16[1,128,512]{2,1,0:T(8,128)(2,1)}, bf16[1,128,512]{2,1,0:T(8,128)(2,1)S(1)}, u32[]{:S(2)}, u32[]{:S(2)}) collective-permute-start(bf16[1,128,512]{2,1,0:T(8,128)(2,1)} %get-tuple-element.42), channel_id=1, source_target_pairs={{0,2},{1,3},{2,0},{3,1},{4,6},{5,7},{6,4},{7,5},{8,10},{9,11},{10,... | collective-permute-start | bytes 393224 | tf_op jit(solution)/shard_map/ppermute | solution.py:50
  59.2 10.1 %collective-permute-start.11 = (bf16[1,128,512]{2,1,0:T(8,128)(2,1)S(1)}, bf16[1,128,512]{2,1,0:T(8,128)(2,1)S(1)}, u32[]{:S(2)}, u32[]{:S(2)}) collective-permute-start(bf16[1,128,512]{2,1,0:T(8,128)(2,1)S(1)} %get-tuple-element.43), channel_id=1, source_target_pairs={{0,2},{1,3},{2,0},{3,1},{4,6},{5,7},{6,4},{7,5},{8,10},{9,11},{10,... | collective-permute-start | bytes 393224 | tf_op jit(solution)/shard_map/ppermute | solution.py:50
  60.6 10.8 %collective-permute-start.8 = (bf16[1,128,512]{2,1,0:T(8,128)(2,1)S(1)}, bf16[1,128,512]{2,1,0:T(8,128)(2,1)S(1)}, u32[]{:S(2)}, u32[]{:S(2)}) collective-permute-start(bf16[1,128,512]{2,1,0:T(8,128)(2,1)S(1)} %get-tuple-element.36), channel_id=1, source_target_pairs={{0,2},{1,3},{2,0},{3,1},{4,6},{5,7},{6,4},{7,5},{8,10},{9,11},{10,... | collective-permute-start | bytes 393224 | tf_op jit(solution)/shard_map/ppermute | solution.py:50
  75.9 3.3 %copy-start.5 = (bf16[2048,256]{1,0:T(8,128)(2,1)S(1)}, bf16[2048,256]{1,0:T(8,128)(2,1)}, u32[]{:S(2)}) copy-start(bf16[2048,256]{1,0:T(8,128)(2,1)} %get-tuple-element.38.back_ref) | copy-start | bytes 3145732
  75.9 3.3 %copy-start.6 = (bf16[2048,256]{1,0:T(8,128)(2,1)S(1)}, bf16[2048,256]{1,0:T(8,128)(2,1)}, u32[]{:S(2)}) copy-start(bf16[2048,256]{1,0:T(8,128)(2,1)} %get-tuple-element.46.h_ref) | copy-start | bytes 3145732
  77.2 5.1 %collective-permute-start.12 = (bf16[32,512]{1,0:T(8,128)(2,1)S(1)}, bf16[32,512]{1,0:T(8,128)(2,1)S(1)}, u32[]{:S(2)}, u32[]{:S(2)}) collective-permute-start(bf16[32,512]{1,0:T(8,128)(2,1)S(1)} %get-tuple-element.48), channel_id=1, source_target_pairs={{0,1},{1,0},{2,3},{3,2},{4,5},{5,4},{6,7},{7,6},{8,9},{9,8},{10,11... | collective-permute-start | bytes 98312 | tf_op jit(solution)/shard_map/ppermute | solution.py:50
  77.3 5.0 %collective-permute-start.13 = (bf16[32,512]{1,0:T(8,128)(2,1)S(1)}, bf16[32,512]{1,0:T(8,128)(2,1)S(1)}, u32[]{:S(2)}, u32[]{:S(2)}) collective-permute-start(bf16[32,512]{1,0:T(8,128)(2,1)S(1)} %get-tuple-element.49), channel_id=1, source_target_pairs={{0,2},{1,3},{2,0},{3,1},{4,6},{5,7},{6,4},{7,5},{8,10},{9,11},{10,... | collective-permute-start | bytes 98312 | tf_op jit(solution)/shard_map/ppermute | solution.py:50
  78.7 3.6 %collective-permute-start.14 = (bf16[32,512]{1,0:T(8,128)(2,1)S(1)}, bf16[32,512]{1,0:T(8,128)(2,1)S(1)}, u32[]{:S(2)}, u32[]{:S(2)}) collective-permute-start(bf16[32,512]{1,0:T(8,128)(2,1)S(1)} %get-tuple-element.50), channel_id=1, source_target_pairs={{0,3},{1,2},{2,1},{3,0},{4,7},{5,6},{6,5},{7,4},{8,11},{9,10},{10,... | collective-permute-start | bytes 98312 | tf_op jit(solution)/shard_map/ppermute | solution.py:50
  79.2 0.7 copy-start.10

commit v18 on v16

--- a/solution.py
+++ b/solution.py
@@ -90,7 +90,7 @@
 def regroup_back_body(batch, seq, order, *refs):
     pieces, dz_ref = refs[:batch], refs[batch]
     outs, second_ref, d_scr, r_scr, sems = refs[batch + 1 : -4], *refs[-4:]
-    me, here = lax.axis_index("batch"), lax.axis_index("seq")
+    me = lax.axis_index("batch")
     groups = second_ref.shape[0]
     lanes = order * LANE_GROUP
     m_here = order // batch
@@ -103,32 +103,20 @@
     tiled = one_hot((iota((order, lanes), 1) % order) == iota((order, lanes), 0))
     keep = (iota((lanes, lanes), 0) % LANE_GROUP) == (iota((lanes, lanes), 1) // order)
     writes = []
-    blocks = order // seq
     part = lanes // seq
     for g in range(groups):
         wide = d_scr[g]
-        packed = wide.astype(BF16)
         ringed = [wide[:, there * part : (there + 1) * part] for there in ring_of(seq)]
-        second_ref[g] = jnp.concatenate(ringed, axis=1).astype(BF16)
+        packed = jnp.concatenate(ringed, axis=1).astype(BF16)
+        second_ref[g] = packed
         weights = jnp.where(keep, dot(packed, tiled, 0, 0), 0.0).astype(BF16)
         result = dot(weights, dz_ref[g * lanes : (g + 1) * lanes, :]).astype(BF16)
         js = slice(g * LANE_GROUP, (g + 1) * LANE_GROUP)
         r_scr[:, js, :] = result.reshape(order, LANE_GROUP, width)
-        if len(outs) == 1:
-            for p, there in enumerate(ring_of(seq)):
-                source, target = pl.ds(there * blocks, blocks), pl.ds(p * blocks, blocks)
-                write = pltpu.make_async_copy(
-                    r_scr.at[source, js, :], outs[0].at[target, js, :], sems.at[g, p]
-                )
-                write.start()
-                writes.append(write)
-
-    if len(outs) == 1:
-        for write in writes:
-            write.wait()
-    else:
-        for d in range(seq):
-            outs[d][...] = r_scr[pl.ds((here ^ d) * blocks, blocks)]
+        writes.append(pltpu.make_async_copy(r_scr.at[:, js, :], outs[0].at[:, js, :], sems.at[g]))
+        writes[g].start()
+    for write in writes:
+        write.wait()
 
 
 def mix_body(batch, seq, *refs):
@@ -354,7 +342,7 @@
         [
             pltpu.VMEM((groups, count, lanes), F32),
             pltpu.VMEM((count, j_here, width), BF16),
-            pltpu.SemaphoreType.DMA((groups, seq)),
+            pltpu.SemaphoreType.DMA((groups,)),
         ],
         far_outs=(0,) if CFG['a2a'][0] else (),
         limit=24 << 20,

time: 79.9 us -> 79.7 us (level)
  no operation moved by 1% of the time
where the time goes in v18:
time: 79.7 us; the launch traced here: 79.3 us
  Pallas kernels  24.4 us (31%)
  starting transfers between devices  23.3 us (29%)
  waiting for transfers between devices  22.1 us (28%)
  local copies, waits for them, and re-layouts  8.64 us (11%)
  between operations  0.83 us (1%)
    pallas_call x11, Pallas kernels, call(): pl.pallas_call(body, name=name, out_shape=outs, in_specs=[pl.BlockSpec(me...  24.4 us
    ppermute x15, waiting for transfers between devices, swap(): return lax.ppermute(value, axis, [(p, p ^ step) for p in range(size)])  18.5 us
    ppermute x15, starting transfers between devices, swap(): return lax.ppermute(value, axis, [(p, p ^ step) for p in range(size)])  13.9 us
    unnamed x32, local copies, waits for them, and re-layouts  8.64 us
    all_to_all x1, starting transfers between devices, packed_shards(): lax.all_to_all(dep('h0', back[0]).reshape(seq, blocks, j_here, width), 's...  5.86 us
    all_to_all x1, starting transfers between devices, packed_shards(): lax.all_to_all(dep('H0', regrouped[0]), 'seq', 0, 0, axis_index_groups=[r...  3.51 us
    all_to_all x1, waiting for transfers between devices, packed_shards(): lax.all_to_all(dep('h0', back[0]).reshape(seq, blocks, j_here, width), 's...  2.26 us
  transfers between devices with their start and end apart: 17, of which 8 were waited for; matrix products, arithmetic and copies ran while one was open for 0% of the time, Pallas kernels for 24%

profile of v18, /device:TPU:9, one launch (start us, length us, event | category | flops | bytes accessed | tf_op | source)
XLA Modules:
  0.0 79.3 jit_solution(17160309508284000376)
XLA Ops:
  0.6 0.0 copy-start.8
  0.6 0.8 %copy-done.8 = bf16[64,8,32]{0,2,1:T(8,128)(2,1)S(1)} copy-done((bf16[64,8,32]{0,2,1:T(8,128)(2,1)S(1)}, bf16[64,8,32]{0,2,1:T(8,128)(2,1)}, u32[]{:S(2)}) %copy-start.8) | copy-done | bytes 32792
  1.5 0.4 pack_body.1.refs_0_
  1.9 1.8 %collective-permute-start.2 = (bf16[32,512]{1,0:T(8,128)(2,1)S(1)}, bf16[32,512]{1,0:T(8,128)(2,1)S(1)}, u32[]{:S(2)}, u32[]{:S(2)}) collective-permute-start(bf16[32,512]{1,0:T(8,128)(2,1)S(1)} %pack_body.1.refs_0_), channel_id=1, source_target_pairs={{0,3},{1,2},{2,1},{3,0},{4,7},{5,6},{6,5},{7,4},{8,11},{9,10},{10,... | collective-permute-start | bytes 98312 | tf_op jit(solution)/shard_map/ppermute | solution.py:50
  3.7 0.3 collective-permute-start.1
  4.0 0.2 collective-permute-start
  4.2 0.7 copy-done.9
  4.9 1.2 %copy-done = bf16[1,2048,256]{2,1,0:T(8,128)(2,1)S(1)} copy-done((bf16[1,2048,256]{2,1,0:T(8,128)(2,1)S(1)}, bf16[1,2048,256]{2,1,0:T(8,128)(2,1)}, u32[]{:S(2)}) %copy-start) | copy-done | bytes 1048600
  6.1 1.2 %copy-done.4 = bf16[1,2048,256]{2,1,0:T(8,128)(2,1)S(1)} copy-done((bf16[1,2048,256]{2,1,0:T(8,128)(2,1)S(1)}, bf16[1,2048,256]{2,1,0:T(8,128)(2,1)}, u32[]{:S(2)}) %copy-start.4) | copy-done | bytes 1048600
  7.3 0.5 gate_body.1.refs_4_.refs_1_
  7.8 0.0 collective-permute-done.2.refs_3_
  7.8 0.0 collective-permute-done.1.refs_2_
  7.8 0.0 collective-permute-done.refs_1_
  7.9 2.3 %regroup_back_body.1 = (bf16[32,64,256]{2,1,0:T(8,128)(2,1)}, bf16[4,32,512]{2,1,0:T(8,128)(2,1)S(1)}) custom-call(bf16[32,512]{1,0:T(8,128)(2,1)S(1)} %pack_body.1.refs_0_, bf16[32,512]{1,0:T(8,128)(2,1)S(1)} %collective-permute-done.refs_1_, bf16[32,512]{1,0:T(8,128)(2,1)S(1)} %collective-permute-done.1.refs_2_, ...), custom_call_target="tpu_custom_call" | custom-call | tf_op jit(solution)/shard_map/regroup_back_body/pallas_call | solution.py:31
  10.1 0.0 copy-start.12
  10.1 5.9 %all-to-all-start.1 = ((bf16[8,4,64,256]{3,2,1,0:T(8,128)(2,1)}), bf16[8,4,64,256]{3,2,1,0:T(8,128)(2,1)S(1)}, u32[]{:S(2)}, u32[]{:S(2)}) async-start(bf16[8,4,64,256]{3,2,1,0:T(8,128)(2,1)} %bitcast.6), calls=%async_computation.1 | async-start | bytes 2097152 | tf_op jit(solution)/shard_map/all_to_all | solution.py:357
  16.0 0.0 copy-done.12
  16.0 1.1 %collective-permute-start.4 = (bf16[4,128,512]{2,1,0:T(8,128)(2,1)S(1)}, bf16[4,128,512]{2,1,0:T(8,128)(2,1)S(1)}, u32[]{:S(2)}, u32[]{:S(2)}) collective-permute-start(bf16[4,128,512]{2,1,0:T(8,128)(2,1)S(1)} %copy-done.12), channel_id=1, source_target_pairs={{0,2},{1,3},{2,0},{3,1},{4,6},{5,7},{6,4},{7,5},{8,10},{9,11},{10,... | collective-permute-start | bytes 1572872 | tf_op jit(solution)/shard_map/ppermute | solution.py:50
  17.1 1.2 %collective-permute-start.3 = (bf16[4,128,512]{2,1,0:T(8,128)(2,1)S(1)}, bf16[4,128,512]{2,1,0:T(8,128)(2,1)S(1)}, u32[]{:S(2)}, u32[]{:S(2)}) collective-permute-start(bf16[4,128,512]{2,1,0:T(8,128)(2,1)S(1)} %copy-done.12), channel_id=1, source_target_pairs={{0,1},{1,0},{2,3},{3,2},{4,5},{5,4},{6,7},{7,6},{8,9},{9,8},{10,11... | collective-permute-start | bytes 1572872 | tf_op jit(solution)/shard_map/ppermute | solution.py:50
  18.4 10.2 %collective-permute-done.4.refs_2_ = bf16[4,128,512]{2,1,0:T(8,128)(2,1)S(1)} collective-permute-done((bf16[4,128,512]{2,1,0:T(8,128)(2,1)S(1)}, bf16[4,128,512]{2,1,0:T(8,128)(2,1)S(1)}, u32[]{:S(2)}, u32[]{:S(2)}) %collective-permute-start.4) | collective-permute-done | bytes 524320 | tf_op jit(solution)/shard_map/ppermute | solution.py:50
  28.6 1.8 %collective-permute-start.5 = (bf16[4,128,512]{2,1,0:T(8,128)(2,1)S(1)}, bf16[4,128,512]{2,1,0:T(8,128)(2,1)S(1)}, u32[]{:S(2)}, u32[]{:S(2)}) collective-permute-start(bf16[4,128,512]{2,1,0:T(8,128)(2,1)S(1)} %collective-permute-done.4.refs_2_), channel_id=1, source_target_pairs={{0,1},{1,0},{2,3},{3,2},{4,5},{5,4},{6,7},{7,6},{8,9},{9,8},{10,11... | collective-permute-start | bytes 1572872 | tf_op jit(solution)/shard_map/ppermute | solution.py:50
  30.4 0.0 collective-permute-done.3.refs_1_
  30.4 1.5 %collective-permute-done.5.refs_3_ = bf16[4,128,512]{2,1,0:T(8,128)(2,1)S(1)} collective-permute-done((bf16[4,128,512]{2,1,0:T(8,128)(2,1)S(1)}, bf16[4,128,512]{2,1,0:T(8,128)(2,1)S(1)}, u32[]{:S(2)}, u32[]{:S(2)}) %collective-permute-start.5) | collective-permute-done | bytes 524320 | tf_op jit(solution)/shard_map/ppermute | solution.py:50
  31.9 0.8 %copy-done.15 = bf16[4,128,512]{2,1,0:T(8,128)(2,1)} copy-done((bf16[4,128,512]{2,1,0:T(8,128)(2,1)}, bf16[4,128,512]{2,1,0:T(8,128)(2,1)S(1)}, u32[]{:S(2)}) %copy-start.15) | copy-done | bytes 524312
  32.7 0.0 copy-done.13
  32.7 0.0 copy-done.14
  32.7 6.2 %mix_body.1 = bf16[8,4,64,256]{3,2,1,0:T(8,128)(2,1)} custom-call(bf16[4,128,512]{2,1,0:T(8,128)(2,1)} %refs_0_.3, bf16[4,128,512]{2,1,0:T(8,128)(2,1)} %copy-done.14, bf16[4,128,512]{2,1,0:T(8,128)(2,1)} %copy-done.13, bf16[4,128,512]{2,1,0:T(8,128)(2,1)} %copy-done.15, bf16[2048,256]{1,0:T(8,128)(2,1)} %bitcast.13, s32[1,512]{1,0:T(1,128)} %bitcast.25), custom_call_target="tpu_custom_call" | custom-call | tf_op jit(solution)/shard_map/mix_body/pallas_call | solution.py:31
  38.9 0.0 copy-start.1
  38.9 0.0 copy-start.11
  38.9 2.3 %all-to-all-done.1.refs_0_ = bf16[8,4,64,256]{3,2,1,0:T(8,128)(2,1)S(1)} async-done(((bf16[8,4,64,256]{3,2,1,0:T(8,128)(2,1)}), bf16[8,4,64,256]{3,2,1,0:T(8,128)(2,1)S(1)}, u32[]{:S(2)}, u32[]{:S(2)}) %all-to-all-start.1) | async-done | bytes 1048608 | tf_op jit(solution)/shard_map/all_to_all | solution.py:357
  41.2 1.0 %copy-done.2 = bf16[8,4,64,256]{3,2,1,0:T(8,128)(2,1)} copy-done((bf16[8,4,64,256]{3,2,1,0:T(8,128)(2,1)}, bf16[8,4,64,256]{3,2,1,0:T(8,128)(2,1)S(1)}, u32[]{:S(2)}) %copy-start.2) | copy-done | bytes 1048600
  42.1 3.5 %all-to-all-start = ((bf16[8,4,64,256]{3,2,1,0:T(8,128)(2,1)}), bf16[8,4,64,256]{3,2,1,0:T(8,128)(2,1)S(1)}, u32[]{:S(2)}, u32[]{:S(2)}) async-start(bf16[8,4,64,256]{3,2,1,0:T(8,128)(2,1)} %mix_body.1), calls=%async_computation | async-start | bytes 2097152 | tf_op jit(solution)/shard_map/all_to_all | solution.py:386
  45.6 0.0 copy-done.1
  45.7 0.0 copy-done.11
  45.7 0.0 copy-start.3
  45.7 1.2 %copy-done.3 = bf16[8,4,64,256]{3,2,1,0:T(8,128)(2,1)S(1)} copy-done((bf16[8,4,64,256]{3,2,1,0:T(8,128)(2,1)S(1)}, bf16[8,4,64,256]{3,2,1,0:T(8,128)(2,1)}, u32[]{:S(2)}) %copy-start.3) | copy-done | bytes 1048600
  46.9 2.5 %first_grad_body.1 = (bf16[4,128,512]{2,1,0:T(8,128)(2,1)S(1)}, bf16[4,128,512]{2,1,0:T(8,128)(2,1)S(1)}, bf16[4,128,512]{2,1,0:T(8,128)(2,1)S(1)}, bf16[4,128,5...) custom-call(bf16[8,4,64,256]{3,2,1,0:T(8,128)(2,1)S(1)} %copy-done.3, bf16[2048,256]{1,0:T(8,128)(2,1)S(1)} %bitcast.16, ...), custom_call_target="tpu_custom_call" | custom-call | tf_op jit(solution)/shard_map/first_grad_body/pallas_call | solution.py:31
  49.4 1.0 %copy-done.7 = bf16[4,512,256]{2,1,0:T(8,128)(2,1)} copy-done((bf16[4,512,256]{2,1,0:T(8,128)(2,1)}, bf16[4,512,256]{2,1,0:T(8,128)(2,1)S(1)}, u32[]{:S(2)}) %copy-start.7) | copy-done | bytes 1048600
  50.4 1.3 %collective-permute-start.6 = (bf16[4,128,512]{2,1,0:T(8,128)(2,1)S(1)}, bf16[4,128,512]{2,1,0:T(8,128)(2,1)S(1)}, u32[]{:S(2)}, u32[]{:S(2)}) collective-permute-start(bf16[4,128,512]{2,1,0:T(8,128)(2,1)S(1)} %get-tuple-element.34), channel_id=1, source_target_pairs={{0,1},{1,0},{2,3},{3,2},{4,5},{5,4},{6,7},{7,6},{8,9},{9,8},{10,11... | collective-permute-start | bytes 1572872 | tf_op jit(solution)/shard_map/ppermute | solution.py:50
  51.7 0.0 collective-permute-start.7
  51.7 1.5 %collective-permute-done.6.got_a = bf16[4,128,512]{2,1,0:T(8,128)(2,1)S(1)} collective-permute-done((bf16[4,128,512]{2,1,0:T(8,128)(2,1)S(1)}, bf16[4,128,512]{2,1,0:T(8,128)(2,1)S(1)}, u32[]{:S(2)}, u32[]{:S(2)}) %collective-permute-start.6) | collective-permute-done | bytes 524320 | tf_op jit(solution)/shard_map/ppermute | solution.py:50
  53.3 0.7 collective-permute-done.7.got_b
  54.0 0.8 %pair_body.1 = (f32[4,128,512]{2,1,0:T(8,128)S(1)}, bf16[1,128,512]{2,1,0:T(8,128)(2,1)S(1)}, bf16[1,128,512]{2,1,0:T(8,128)(2,1)}, bf16[1,128,512]{2,1,0:T(8,128)(2,1)}, bf16[1,128,512]{2,1,0:T(8,128)(2,1)S(1)}) custom-call(bf16[4,128,512]{2,1,0:T(8,128)(2,1)S(1)} %get-tuple-element.32.own_a, bf16[4,128,512]{2,1,0:T(8,128)(2,1)S(1)} %get-tuple-element.33.own_b, ...), custom_call_target="tpu_custom_call" | custom-call | tf_op jit(solution)/shard_map/pair_body/pallas_call | solution.py:31
  54.8 1.1 %collective-permute-start.9 = (bf16[1,128,512]{2,1,0:T(8,128)(2,1)}, bf16[1,128,512]{2,1,0:T(8,128)(2,1)S(1)}, u32[]{:S(2)}, u32[]{:S(2)}) collective-permute-start(bf16[1,128,512]{2,1,0:T(8,128)(2,1)} %get-tuple-element.41), channel_id=1, source_target_pairs={{0,2},{1,3},{2,0},{3,1},{4,6},{5,7},{6,4},{7,5},{8,10},{9,11},{10,... | collective-permute-start | bytes 393224 | tf_op jit(solution)/shard_map/ppermute | solution.py:50
  55.9 0.4 collective-permute-start.10
  56.3 1.1 %collective-permute-start.11 = (bf16[1,128,512]{2,1,0:T(8,128)(2,1)S(1)}, bf16[1,128,512]{2,1,0:T(8,128)(2,1)S(1)}, u32[]{:S(2)}, u32[]{:S(2)}) collective-permute-start(bf16[1,128,512]{2,1,0:T(8,128)(2,1)S(1)} %get-tuple-element.43), channel_id=1, source_target_pairs={{0,2},{1,3},{2,0},{3,1},{4,6},{5,7},{6,4},{7,5},{8,10},{9,11},{10,... | collective-permute-start | bytes 393224 | tf_op jit(solution)/shard_map/ppermute | solution.py:50
  57.4 0.4 collective-permute-start.8
  57.8 6.0 %mix_back_body.1 = (bf16[2048,256]{1,0:T(8,128)(2,1)}, bf16[2048,256]{1,0:T(8,128)(2,1)}) custom-call(bf16[4,128,512]{2,1,0:T(8,128)(2,1)} %refs_0_.3, bf16[4,128,512]{2,1,0:T(8,128)(2,1)} %copy-done.14, bf16[4,128,512]{2,1,0:T(8,128)(2,1)} %copy-done.13, bf16[4,128,512]{2,1,0:T(8,128)(2,1)} %copy-done.15, bf16[4,512,256]{2,1,0:T(8,128)(2,1)} %copy-done.7, ...), custom_call_target="tpu_custom_call" | custom-call | tf_op jit(solution)/shard_map/mix_back_body/pallas_call | solution.py:31
  63.8 0.0 collective-permute-done.9.refs_1_
  63.8 0.0 collective-permute-done.10.refs_2_
  63.8 1.6 %collective-permute-done.11.refs_3_ = bf16[1,128,512]{2,1,0:T(8,128)(2,1)S(1)} collective-permute-done((bf16[1,128,512]{2,1,0:T(8,128)(2,1)S(1)}, bf16[1,128,512]{2,1,0:T(8,128)(2,1)S(1)}, u32[]{:S(2)}, u32[]{:S(2)}) %collective-permute-start.11) | collective-permute-done | bytes 131104 | tf_op jit(solution)/shard_map/ppermute | solution.py:50
  65.4 2.8 %collective-permute-done.8.refs_0_ = bf16[1,128,512]{2,1,0:T(8,128)(2,1)S(1)} collective-permute-done((bf16[1,128,512]{2,1,0:T(8,128)(2,1)S(1)}, bf16[1,128,512]{2,1,0:T(8,128)(2,1)S(1)}, u32[]{:S(2)}, u32[]{:S(2)}) %collective-permute-start.8) | collective-permute-done | bytes 131104 | tf_op jit(solution)/shard_map/ppermute | solution.py:50
  68.2 0.9 %add_body.1 = bf16[4,128,512]{2,1,0:T(8,128)(2,1)} custom-call(f32[4,128,512]{2,1,0:T(8,128)S(1)} %get-tuple-element.40.own, bf16[1,128,512]{2,1,0:T(8,128)(2,1)S(1)} %collective-permute-done.8.refs_0_, bf16[1,128,512]{2,1,0:T(8,128)(2,1)S(1)} %collective-permute-done.9.refs_1_, bf16[1,128,512]{2,1,0:T(8,128)(2,1)S(1)} %collective-permute-done.10.refs_2_, ...), custom_call_target="tpu_custom_call" | custom-call | tf_op jit(solution)/shard_map/add_body/pallas_call | solution.py:31
  69.1 1.4 %all-to-all-done = bf16[8,4,64,256]{3,2,1,0:T(8,128)(2,1)S(1)} async-done(((bf16[8,4,64,256]{3,2,1,0:T(8,128)(2,1)}), bf16[8,4,64,256]{3,2,1,0:T(8,128)(2,1)S(1)}, u32[]{:S(2)}, u32[]{:S(2)}) %all-to-all-start) | async-done | bytes 1048608 | tf_op jit(solution)/shard_map/all_to_all | solution.py:386
  70.4 1.3 %second_grad_body.1 = (bf16[32,512]{1,0:T(8,128)(2,1)S(1)}, bf16[32,512]{1,0:T(8,128)(2,1)S(1)}, bf16[32,512]{1,0:T(8,128)(2,1)S(1)}, bf16[32,512]{1,0:T(8,128)(2,1)S(1)}) custom-call(bf16[32,64,256]{2,1,0:T(8,128)(2,1)S(1)} %bitcast.17, bf16[2048,256]{1,0:T(8,128)(2,1)S(1)} %gate_body.1.refs_4_.refs_1_), custom_call_target="tpu_custom_call" | custom-call | tf_op jit(solution)/shard_map/second_grad_body/pallas_call | solution.py:31
  71.8 1.5 %collective-permute-start.12 = (bf16[32,512]{1,0:T(8,128)(2,1)S(1)}, bf16[32,512]{1,0:T(8,128)(2,1)S(1)}, u32[]{:S(2)}, u32[]{:S(2)}) collective-permute-start(bf16[32,512]{1,0:T(8,128)(2,1)S(1)} %get-tuple-element.48), channel_id=1, source_target_pairs={{0,1},{1,0},{2,3},{3,2},{4,5},{5,4},{6,7},{7,6},{8,9},{9,8},{10,11... | collective-permute-start | bytes 98312 | tf_op jit(solution)/shard_map/ppermute | solution.py:50
  73.3 1.1 %collective-permute-start.13 = (bf16[32,512]{1,0:T(8,128)(2,1)S(1)}, bf16[32,512]{1,0:T(8,128)(2,1)S(1)}, u32[]{:S(2)}, u32[]{:S(2)}) collective-permute-start(bf16[32,512]{1,0:T(8,128)(2,1)S(1)} %get-tuple-element.49), channel_id=1, source_target_pairs={{0,2},{1,3},{2,0},{3,1},{4,6},{5,7},{6,4},{7,5},{8,10},{9,11},{10,... | collective-permute-start | bytes 98312 | tf_op jit(solution)/shard_map/ppermute | solution.py:50
  74.4 0.6 collective-permute-start.14
  75.0 0.7 copy-done.10
  75.7 2.5 %tokens_body.1 = bf16[2048,256]{1,0:T(8,128)(2,1)} custom-call(bf16[32,64,256]{2,1,0:T(8,128)(2,1)S(1)} %bitcast.18, bf16[4,32,512]{2,1,0:T(8,128)(2,1)S(1)} %get-tuple-element.45.second_ref, bf16[2048,256]{1,0:T(8,128)(2,1)S(1)} %copy-done.6, s32[1,256]{1,0:T(1,128)S(1)} %bitcast.24, bf16[2048,256]{1,0:T(8,128)(2,1)S(1)} %copy-done.5), custom_call_target="tpu_custom_call" | custom-call | tf_op jit(solution)/shard_map/tokens_body/pallas_call | solution.py:31
  78.2 0.0 collective-permute-done.12.refs_1_
  78.2 0.0 collective-permute-done.13.refs_2_
  78.2 0.0 collective-permute-done.14.refs_3_
  78.2 1.1 %unpack_body.1 = bf16[256,64]{1,0:T(8,128)(2,1)} custom-call(bf16[32,512]{1,0:T(8,128)(2,1)S(1)} %get-tuple-element.47.refs_0_, bf16[32,512]{1,0:T(8,128)(2,1)S(1)} %collective-permute-done.12.refs_1_, bf16[32,512]{1,0:T(8,128)(2,1)S(1)} %collective-permute-done.13.refs_2_, bf16[32,512]{1,0:T(8,128)(2,1)S(1)} %collective-permute-done.14.refs_3_), custom_call_target="tpu_custom_call" | custom-call | tf_op jit(solution)/shard_map/unpack_body/pallas_call | solution.py:31
  (13 shorter events, 0.0 us)
Async XLA Ops:
  0.6 0.8 %copy-start.8 = (bf16[64,8,32]{0,2,1:T(8,128)(2,1)S(1)}, bf16[64,8,32]{0,2,1:T(8,128)(2,1)}, u32[]{:S(2)}) copy-start(bf16[64,8,32]{0,2,1:T(8,128)(2,1)} %param.9) | copy-start | bytes 98308
  1.9 5.9 %collective-permute-start.2 = (bf16[32,512]{1,0:T(8,128)(2,1)S(1)}, bf16[32,512]{1,0:T(8,128)(2,1)S(1)}, u32[]{:S(2)}, u32[]{:S(2)}) collective-permute-start(bf16[32,512]{1,0:T(8,128)(2,1)S(1)} %pack_body.1.refs_0_), channel_id=1, source_target_pairs={{0,3},{1,2},{2,1},{3,0},{4,7},{5,6},{6,5},{7,4},{8,11},{9,10},{10,... | collective-permute-start | bytes 98312 | tf_op jit(solution)/shard_map/ppermute | solution.py:50
  3.7 4.1 %collective-permute-start.1 = (bf16[32,512]{1,0:T(8,128)(2,1)S(1)}, bf16[32,512]{1,0:T(8,128)(2,1)S(1)}, u32[]{:S(2)}, u32[]{:S(2)}) collective-permute-start(bf16[32,512]{1,0:T(8,128)(2,1)S(1)} %pack_body.1.refs_0_), channel_id=1, source_target_pairs={{0,2},{1,3},{2,0},{3,1},{4,6},{5,7},{6,4},{7,5},{8,10},{9,11},{10,... | collective-permute-start | bytes 98312 | tf_op jit(solution)/shard_map/ppermute | solution.py:50
  4.0 3.9 %collective-permute-start = (bf16[32,512]{1,0:T(8,128)(2,1)S(1)}, bf16[32,512]{1,0:T(8,128)(2,1)S(1)}, u32[]{:S(2)}, u32[]{:S(2)}) collective-permute-start(bf16[32,512]{1,0:T(8,128)(2,1)S(1)} %pack_body.1.refs_0_), channel_id=1, source_target_pairs={{0,1},{1,0},{2,3},{3,2},{4,5},{5,4},{6,7},{7,6},{8,9},{9,8},{10,11... | collective-permute-start | bytes 98312 | tf_op jit(solution)/shard_map/ppermute | solution.py:50
  4.2 0.7 copy-start.9
  4.9 1.2 %copy-start = (bf16[1,2048,256]{2,1,0:T(8,128)(2,1)S(1)}, bf16[1,2048,256]{2,1,0:T(8,128)(2,1)}, u32[]{:S(2)}) copy-start(bf16[1,2048,256]{2,1,0:T(8,128)(2,1)} %param.6) | copy-start | bytes 3145732
  6.1 1.2 %copy-start.4 = (bf16[1,2048,256]{2,1,0:T(8,128)(2,1)S(1)}, bf16[1,2048,256]{2,1,0:T(8,128)(2,1)}, u32[]{:S(2)}) copy-start(bf16[1,2048,256]{2,1,0:T(8,128)(2,1)} %param.7) | copy-start | bytes 3145732
  10.1 5.9 %copy-start.12 = (bf16[4,128,512]{2,1,0:T(8,128)(2,1)S(1)}, bf16[4,128,512]{2,1,0:T(8,128)(2,1)}, u32[]{:S(2)}) copy-start(bf16[4,128,512]{2,1,0:T(8,128)(2,1)} %refs_0_.3) | copy-start | bytes 1572868
  10.1 31.0 %all-to-all-start.1 = ((bf16[8,4,64,256]{3,2,1,0:T(8,128)(2,1)}), bf16[8,4,64,256]{3,2,1,0:T(8,128)(2,1)S(1)}, u32[]{:S(2)}, u32[]{:S(2)}) async-start(bf16[8,4,64,256]{3,2,1,0:T(8,128)(2,1)} %bitcast.6), calls=%async_computation.1 | async-start | bytes 2097152 | tf_op jit(solution)/shard_map/all_to_all | solution.py:357
  16.0 12.6 %collective-permute-start.4 = (bf16[4,128,512]{2,1,0:T(8,128)(2,1)S(1)}, bf16[4,128,512]{2,1,0:T(8,128)(2,1)S(1)}, u32[]{:S(2)}, u32[]{:S(2)}) collective-permute-start(bf16[4,128,512]{2,1,0:T(8,128)(2,1)S(1)} %copy-done.12), channel_id=1, source_target_pairs={{0,2},{1,3},{2,0},{3,1},{4,6},{5,7},{6,4},{7,5},{8,10},{9,11},{10,... | collective-permute-start | bytes 1572872 | tf_op jit(solution)/shard_map/ppermute | solution.py:50
  17.1 13.2 %collective-permute-start.3 = (bf16[4,128,512]{2,1,0:T(8,128)(2,1)S(1)}, bf16[4,128,512]{2,1,0:T(8,128)(2,1)S(1)}, u32[]{:S(2)}, u32[]{:S(2)}) collective-permute-start(bf16[4,128,512]{2,1,0:T(8,128)(2,1)S(1)} %copy-done.12), channel_id=1, source_target_pairs={{0,1},{1,0},{2,3},{3,2},{4,5},{5,4},{6,7},{7,6},{8,9},{9,8},{10,11... | collective-permute-start | bytes 1572872 | tf_op jit(solution)/shard_map/ppermute | solution.py:50
  28.6 4.1 %copy-start.13 = (bf16[4,128,512]{2,1,0:T(8,128)(2,1)}, bf16[4,128,512]{2,1,0:T(8,128)(2,1)S(1)}, u32[]{:S(2)}) copy-start(bf16[4,128,512]{2,1,0:T(8,128)(2,1)S(1)} %collective-permute-done.4.refs_2_) | copy-start | bytes 1572868
  28.6 3.3 %collective-permute-start.5 = (bf16[4,128,512]{2,1,0:T(8,128)(2,1)S(1)}, bf16[4,128,512]{2,1,0:T(8,128)(2,1)S(1)}, u32[]{:S(2)}, u32[]{:S(2)}) collective-permute-start(bf16[4,128,512]{2,1,0:T(8,128)(2,1)S(1)} %collective-permute-done.4.refs_2_), channel_id=1, source_target_pairs={{0,1},{1,0},{2,3},{3,2},{4,5},{5,4},{6,7},{7,6},{8,9},{9,8},{10,11... | collective-permute-start | bytes 1572872 | tf_op jit(solution)/shard_map/ppermute | solution.py:50
  30.4 2.3 %copy-start.14 = (bf16[4,128,512]{2,1,0:T(8,128)(2,1)}, bf16[4,128,512]{2,1,0:T(8,128)(2,1)S(1)}, u32[]{:S(2)}) copy-start(bf16[4,128,512]{2,1,0:T(8,128)(2,1)S(1)} %collective-permute-done.3.refs_1_) | copy-start | bytes 1572868
  31.9 0.8 %copy-start.15 = (bf16[4,128,512]{2,1,0:T(8,128)(2,1)}, bf16[4,128,512]{2,1,0:T(8,128)(2,1)S(1)}, u32[]{:S(2)}) copy-start(bf16[4,128,512]{2,1,0:T(8,128)(2,1)S(1)} %collective-permute-done.5.refs_3_) | copy-start | bytes 1572868
  38.9 6.8 %copy-start.1 = (bf16[1,2048,256]{2,1,0:T(8,128)(2,1)S(1)}, bf16[1,2048,256]{2,1,0:T(8,128)(2,1)}, u32[]{:S(2)}) copy-start(bf16[1,2048,256]{2,1,0:T(8,128)(2,1)} %param.6) | copy-start | bytes 3145732
  38.9 6.8 %copy-start.11 = (s32[512]{0:T(512)S(1)}, s32[512]{0:T(512)}, u32[]{:S(2)}) copy-start(s32[512]{0:T(512)} %param.11) | copy-start | bytes 6148
  41.2 1.0 %copy-start.2 = (bf16[8,4,64,256]{3,2,1,0:T(8,128)(2,1)}, bf16[8,4,64,256]{3,2,1,0:T(8,128)(2,1)S(1)}, u32[]{:S(2)}) copy-start(bf16[8,4,64,256]{3,2,1,0:T(8,128)(2,1)S(1)} %all-to-all-done.1.refs_0_) | copy-start | bytes 3145732
  42.1 28.3 %all-to-all-start = ((bf16[8,4,64,256]{3,2,1,0:T(8,128)(2,1)}), bf16[8,4,64,256]{3,2,1,0:T(8,128)(2,1)S(1)}, u32[]{:S(2)}, u32[]{:S(2)}) async-start(bf16[8,4,64,256]{3,2,1,0:T(8,128)(2,1)} %mix_body.1), calls=%async_computation | async-start | bytes 2097152 | tf_op jit(solution)/shard_map/all_to_all | solution.py:386
  45.7 1.2 %copy-start.3 = (bf16[8,4,64,256]{3,2,1,0:T(8,128)(2,1)S(1)}, bf16[8,4,64,256]{3,2,1,0:T(8,128)(2,1)}, u32[]{:S(2)}) copy-start(bf16[8,4,64,256]{3,2,1,0:T(8,128)(2,1)} %copy-done.2) | copy-start | bytes 3145732
  49.4 1.0 %copy-start.7 = (bf16[4,512,256]{2,1,0:T(8,128)(2,1)}, bf16[4,512,256]{2,1,0:T(8,128)(2,1)S(1)}, u32[]{:S(2)}) copy-start(bf16[4,512,256]{2,1,0:T(8,128)(2,1)S(1)} %get-tuple-element.37.refs_4_) | copy-start | bytes 3145732
  50.4 2.9 %collective-permute-start.6 = (bf16[4,128,512]{2,1,0:T(8,128)(2,1)S(1)}, bf16[4,128,512]{2,1,0:T(8,128)(2,1)S(1)}, u32[]{:S(2)}, u32[]{:S(2)}) collective-permute-start(bf16[4,128,512]{2,1,0:T(8,128)(2,1)S(1)} %get-tuple-element.34), channel_id=1, source_target_pairs={{0,1},{1,0},{2,3},{3,2},{4,5},{5,4},{6,7},{7,6},{8,9},{9,8},{10,11... | collective-permute-start | bytes 1572872 | tf_op jit(solution)/shard_map/ppermute | solution.py:50
  51.7 2.3 %collective-permute-start.7 = (bf16[4,128,512]{2,1,0:T(8,128)(2,1)S(1)}, bf16[4,128,512]{2,1,0:T(8,128)(2,1)S(1)}, u32[]{:S(2)}, u32[]{:S(2)}) collective-permute-start(bf16[4,128,512]{2,1,0:T(8,128)(2,1)S(1)} %get-tuple-element.35), channel_id=1, source_target_pairs={{0,1},{1,0},{2,3},{3,2},{4,5},{5,4},{6,7},{7,6},{8,9},{9,8},{10,11... | collective-permute-start | bytes 1572872 | tf_op jit(solution)/shard_map/ppermute | solution.py:50
  54.8 8.9 %collective-permute-start.9 = (bf16[1,128,512]{2,1,0:T(8,128)(2,1)}, bf16[1,128,512]{2,1,0:T(8,128)(2,1)S(1)}, u32[]{:S(2)}, u32[]{:S(2)}) collective-permute-start(bf16[1,128,512]{2,1,0:T(8,128)(2,1)} %get-tuple-element.41), channel_id=1, source_target_pairs={{0,2},{1,3},{2,0},{3,1},{4,6},{5,7},{6,4},{7,5},{8,10},{9,11},{10,... | collective-permute-start | bytes 393224 | tf_op jit(solution)/shard_map/ppermute | solution.py:50
  55.9 7.8 %collective-permute-start.10 = (bf16[1,128,512]{2,1,0:T(8,128)(2,1)}, bf16[1,128,512]{2,1,0:T(8,128)(2,1)S(1)}, u32[]{:S(2)}, u32[]{:S(2)}) collective-permute-start(bf16[1,128,512]{2,1,0:T(8,128)(2,1)} %get-tuple-element.42), channel_id=1, source_target_pairs={{0,2},{1,3},{2,0},{3,1},{4,6},{5,7},{6,4},{7,5},{8,10},{9,11},{10,... | collective-permute-start | bytes 393224 | tf_op jit(solution)/shard_map/ppermute | solution.py:50
  56.3 9.1 %collective-permute-start.11 = (bf16[1,128,512]{2,1,0:T(8,128)(2,1)S(1)}, bf16[1,128,512]{2,1,0:T(8,128)(2,1)S(1)}, u32[]{:S(2)}, u32[]{:S(2)}) collective-permute-start(bf16[1,128,512]{2,1,0:T(8,128)(2,1)S(1)} %get-tuple-element.43), channel_id=1, source_target_pairs={{0,2},{1,3},{2,0},{3,1},{4,6},{5,7},{6,4},{7,5},{8,10},{9,11},{10,... | collective-permute-start | bytes 393224 | tf_op jit(solution)/shard_map/ppermute | solution.py:50
  57.4 10.8 %collective-permute-start.8 = (bf16[1,128,512]{2,1,0:T(8,128)(2,1)S(1)}, bf16[1,128,512]{2,1,0:T(8,128)(2,1)S(1)}, u32[]{:S(2)}, u32[]{:S(2)}) collective-permute-start(bf16[1,128,512]{2,1,0:T(8,128)(2,1)S(1)} %get-tuple-element.36), channel_id=1, source_target_pairs={{0,2},{1,3},{2,0},{3,1},{4,6},{5,7},{6,4},{7,5},{8,10},{9,11},{10,... | collective-permute-start | bytes 393224 | tf_op jit(solution)/shard_map/ppermute | solution.py:50
  70.4 4.6 %copy-start.5 = (bf16[2048,256]{1,0:T(8,128)(2,1)S(1)}, bf16[2048,256]{1,0:T(8,128)(2,1)}, u32[]{:S(2)}) copy-start(bf16[2048,256]{1,0:T(8,128)(2,1)} %get-tuple-element.38.back_ref) | copy-start | bytes 3145732
  70.4 4.6 %copy-start.6 = (bf16[2048,256]{1,0:T(8,128)(2,1)S(1)}, bf16[2048,256]{1,0:T(8,128)(2,1)}, u32[]{:S(2)}) copy-start(bf16[2048,256]{1,0:T(8,128)(2,1)} %get-tuple-element.46.h_ref) | copy-start | bytes 3145732
  71.8 6.4 %collective-permute-start.12 = (bf16[32,512]{1,0:T(8,128)(2,1)S(1)}, bf16[32,512]{1,0:T(8,128)(2,1)S(1)}, u32[]{:S(2)}, u32[]{:S(2)}) collective-permute-start(bf16[32,512]{1,0:T(8,128)(2,1)S(1)} %get-tuple-element.48), channel_id=1, source_target_pairs={{0,1},{1,0},{2,3},{3,2},{4,5},{5,4},{6,7},{7,6},{8,9},{9,8},{10,11... | collective-permute-start | bytes 98312 | tf_op jit(solution)/shard_map/ppermute | solution.py:50
  73.3 4.9 %collective-permute-start.13 = (bf16[32,512]{1,0:T(8,128)(2,1)S(1)}, bf16[32,512]{1,0:T(8,128)(2,1)S(1)}, u32[]{:S(2)}, u32[]{:S(2)}) collective-permute-start(bf16[32,512]{1,0:T(8,128)(2,1)S(1)} %get-tuple-element.49), channel_id=1, source_target_pairs={{0,2},{1,3},{2,0},{3,1},{4,6},{5,7},{6,4},{7,5},{8,10},{9,11},{10,... | collective-permute-start | bytes 98312 | tf_op jit(solution)/shard_map/ppermute | solution.py:50
  74.4 3.8 %collective-permute-start.14 = (bf16[32,512]{1,0:T(8,128)(2,1)S(1)}, bf16[32,512]{1,0:T(8,128)(2,1)S(1)}, u32[]{:S(2)}, u32[]{:S(2)}) collective-permute-start(bf16[32,512]{1,0:T(8,128)(2,1)S(1)} %get-tuple-element.50), channel_id=1, source_target_pairs={{0,3},{1,2},{2,1},{3,0},{4,7},{5,6},{6,5},{7,4},{8,11},{9,10},{10,... | collective-permute-start | bytes 98312 | tf_op jit(solution)/shard_map/ppermute | solution.py:50
  75.0 0.7 copy-start.10

commit v19 on v18

--- a/solution.py
+++ b/solution.py
@@ -51,11 +51,11 @@
 
 
 def ring_at(place, size):
-    return jnp.where(place < size // 2, 2 * place, 2 * size - 1 - 2 * place)
+    return jnp.where(place < size // 2, 2 * place + 1, 2 * size - 2 - 2 * place)
 
 
 def ring_of(size):
-    return [2 * p if p < size // 2 else 2 * size - 1 - 2 * p for p in range(size)]
+    return [2 * p + 1 if p < size // 2 else 2 * size - 2 - 2 * p for p in range(size)]
 
 
 def after(value, *earlier):

time: 79.7 us -> 79.3 us (level)
  the two profiles are of different devices: /device:TPU:9 before, /device:TPU:0 now
where the time goes in v19:
time: 79.3 us; the launch traced here: 78.8 us
  Pallas kernels  24.4 us (31%)
  starting transfers between devices  23.1 us (29%)
  waiting for transfers between devices  21.9 us (28%)
  local copies, waits for them, and re-layouts  8.64 us (11%)
  between operations  0.83 us (1%)
    pallas_call x11, Pallas kernels, call(): pl.pallas_call(body, name=name, out_shape=outs, in_specs=[pl.BlockSpec(me...  24.4 us
    ppermute x15, waiting for transfers between devices, swap(): return lax.ppermute(value, axis, [(p, p ^ step) for p in range(size)])  20.2 us
    ppermute x15, starting transfers between devices, swap(): return lax.ppermute(value, axis, [(p, p ^ step) for p in range(size)])  11.1 us
    unnamed x32, local copies, waits for them, and re-layouts  8.64 us
    all_to_all x1, starting transfers between devices, packed_shards(): lax.all_to_all(dep('h0', back[0]).reshape(seq, blocks, j_here, width), 's...  6.8 us
    all_to_all x1, starting transfers between devices, packed_shards(): lax.all_to_all(dep('H0', regrouped[0]), 'seq', 0, 0, axis_index_groups=[r...  5.17 us
  transfers between devices with their start and end apart: 17, of which 8 were waited for; matrix products, arithmetic and copies ran while one was open for 0% of the time, Pallas kernels for 24%

profile of v19, /device:TPU:0, one launch (start us, length us, event | category | flops | bytes accessed | tf_op | source)
XLA Modules:
  0.0 78.8 jit_solution(1060935775331695508)
XLA Ops:
  0.6 0.0 copy-start.8
  0.6 0.8 %copy-done.8 = bf16[64,8,32]{0,2,1:T(8,128)(2,1)S(1)} copy-done((bf16[64,8,32]{0,2,1:T(8,128)(2,1)S(1)}, bf16[64,8,32]{0,2,1:T(8,128)(2,1)}, u32[]{:S(2)}) %copy-start.8) | copy-done | bytes 32792
  1.5 0.4 pack_body.1.refs_0_
  1.9 2.4 %collective-permute-start.2 = (bf16[32,512]{1,0:T(8,128)(2,1)S(1)}, bf16[32,512]{1,0:T(8,128)(2,1)S(1)}, u32[]{:S(2)}, u32[]{:S(2)}) collective-permute-start(bf16[32,512]{1,0:T(8,128)(2,1)S(1)} %pack_body.1.refs_0_), channel_id=1, source_target_pairs={{0,3},{1,2},{2,1},{3,0},{4,7},{5,6},{6,5},{7,4},{8,11},{9,10},{10,... | collective-permute-start | bytes 98312 | tf_op jit(solution)/shard_map/ppermute | solution.py:50
  4.3 0.6 collective-permute-start.1
  5.0 0.0 collective-permute-start
  5.0 0.7 copy-done.9
  5.7 1.2 %copy-done = bf16[1,2048,256]{2,1,0:T(8,128)(2,1)S(1)} copy-done((bf16[1,2048,256]{2,1,0:T(8,128)(2,1)S(1)}, bf16[1,2048,256]{2,1,0:T(8,128)(2,1)}, u32[]{:S(2)}) %copy-start) | copy-done | bytes 1048600
  6.9 1.2 %copy-done.4 = bf16[1,2048,256]{2,1,0:T(8,128)(2,1)S(1)} copy-done((bf16[1,2048,256]{2,1,0:T(8,128)(2,1)S(1)}, bf16[1,2048,256]{2,1,0:T(8,128)(2,1)}, u32[]{:S(2)}) %copy-start.4) | copy-done | bytes 1048600
  8.1 0.5 gate_body.1.refs_4_.refs_1_
  8.6 0.0 collective-permute-done.2.refs_3_
  8.6 0.0 collective-permute-done.1.refs_2_
  8.7 0.0 collective-permute-done.refs_1_
  8.7 2.3 %regroup_back_body.1 = (bf16[32,64,256]{2,1,0:T(8,128)(2,1)}, bf16[4,32,512]{2,1,0:T(8,128)(2,1)S(1)}) custom-call(bf16[32,512]{1,0:T(8,128)(2,1)S(1)} %pack_body.1.refs_0_, bf16[32,512]{1,0:T(8,128)(2,1)S(1)} %collective-permute-done.refs_1_, bf16[32,512]{1,0:T(8,128)(2,1)S(1)} %collective-permute-done.1.refs_2_, ...), custom_call_target="tpu_custom_call" | custom-call | tf_op jit(solution)/shard_map/regroup_back_body/pallas_call | solution.py:31
  10.9 0.0 copy-start.12
  11.0 6.8 %all-to-all-start.1 = ((bf16[8,4,64,256]{3,2,1,0:T(8,128)(2,1)}), bf16[8,4,64,256]{3,2,1,0:T(8,128)(2,1)S(1)}, u32[]{:S(2)}, u32[]{:S(2)}) async-start(bf16[8,4,64,256]{3,2,1,0:T(8,128)(2,1)} %bitcast.6), calls=%async_computation.1 | async-start | bytes 2097152 | tf_op jit(solution)/shard_map/all_to_all | solution.py:357
  17.8 0.0 copy-done.12
  17.8 1.5 %collective-permute-start.4 = (bf16[4,128,512]{2,1,0:T(8,128)(2,1)S(1)}, bf16[4,128,512]{2,1,0:T(8,128)(2,1)S(1)}, u32[]{:S(2)}, u32[]{:S(2)}) collective-permute-start(bf16[4,128,512]{2,1,0:T(8,128)(2,1)S(1)} %copy-done.12), channel_id=1, source_target_pairs={{0,2},{1,3},{2,0},{3,1},{4,6},{5,7},{6,4},{7,5},{8,10},{9,11},{10,... | collective-permute-start | bytes 1572872 | tf_op jit(solution)/shard_map/ppermute | solution.py:50
  19.2 0.0 collective-permute-start.3
  19.2 12.0 %collective-permute-done.4.refs_2_ = bf16[4,128,512]{2,1,0:T(8,128)(2,1)S(1)} collective-permute-done((bf16[4,128,512]{2,1,0:T(8,128)(2,1)S(1)}, bf16[4,128,512]{2,1,0:T(8,128)(2,1)S(1)}, u32[]{:S(2)}, u32[]{:S(2)}) %collective-permute-start.4) | collective-permute-done | bytes 524320 | tf_op jit(solution)/shard_map/ppermute | solution.py:50
  31.2 0.0 collective-permute-start.5
  31.2 0.0 collective-permute-done.3.refs_1_
  31.3 0.0 copy-start.14
  31.3 1.9 %collective-permute-done.5.refs_3_ = bf16[4,128,512]{2,1,0:T(8,128)(2,1)S(1)} collective-permute-done((bf16[4,128,512]{2,1,0:T(8,128)(2,1)S(1)}, bf16[4,128,512]{2,1,0:T(8,128)(2,1)S(1)}, u32[]{:S(2)}, u32[]{:S(2)}) %collective-permute-start.5) | collective-permute-done | bytes 524320 | tf_op jit(solution)/shard_map/ppermute | solution.py:50
  33.2 0.8 %copy-done.15 = bf16[4,128,512]{2,1,0:T(8,128)(2,1)} copy-done((bf16[4,128,512]{2,1,0:T(8,128)(2,1)}, bf16[4,128,512]{2,1,0:T(8,128)(2,1)S(1)}, u32[]{:S(2)}) %copy-start.15) | copy-done | bytes 524312
  34.0 0.0 copy-done.13
  34.0 0.0 copy-done.14
  34.0 6.2 %mix_body.1 = bf16[8,4,64,256]{3,2,1,0:T(8,128)(2,1)} custom-call(bf16[4,128,512]{2,1,0:T(8,128)(2,1)} %refs_0_.3, bf16[4,128,512]{2,1,0:T(8,128)(2,1)} %copy-done.14, bf16[4,128,512]{2,1,0:T(8,128)(2,1)} %copy-done.13, bf16[4,128,512]{2,1,0:T(8,128)(2,1)} %copy-done.15, bf16[2048,256]{1,0:T(8,128)(2,1)} %bitcast.13, s32[1,512]{1,0:T(1,128)} %bitcast.25), custom_call_target="tpu_custom_call" | custom-call | tf_op jit(solution)/shard_map/mix_body/pallas_call | solution.py:31
  40.1 0.0 copy-start.1
  40.1 0.0 copy-start.11
  40.1 1.4 %all-to-all-done.1.refs_0_ = bf16[8,4,64,256]{3,2,1,0:T(8,128)(2,1)S(1)} async-done(((bf16[8,4,64,256]{3,2,1,0:T(8,128)(2,1)}), bf16[8,4,64,256]{3,2,1,0:T(8,128)(2,1)S(1)}, u32[]{:S(2)}, u32[]{:S(2)}) %all-to-all-start.1) | async-done | bytes 1048608 | tf_op jit(solution)/shard_map/all_to_all | solution.py:357
  41.5 1.0 %copy-done.2 = bf16[8,4,64,256]{3,2,1,0:T(8,128)(2,1)} copy-done((bf16[8,4,64,256]{3,2,1,0:T(8,128)(2,1)}, bf16[8,4,64,256]{3,2,1,0:T(8,128)(2,1)S(1)}, u32[]{:S(2)}) %copy-start.2) | copy-done | bytes 1048600
  42.5 5.2 %all-to-all-start = ((bf16[8,4,64,256]{3,2,1,0:T(8,128)(2,1)}), bf16[8,4,64,256]{3,2,1,0:T(8,128)(2,1)S(1)}, u32[]{:S(2)}, u32[]{:S(2)}) async-start(bf16[8,4,64,256]{3,2,1,0:T(8,128)(2,1)} %mix_body.1), calls=%async_computation | async-start | bytes 2097152 | tf_op jit(solution)/shard_map/all_to_all | solution.py:386
  47.7 0.0 copy-done.1
  47.7 0.0 copy-done.11
  47.7 1.2 %copy-done.3 = bf16[8,4,64,256]{3,2,1,0:T(8,128)(2,1)S(1)} copy-done((bf16[8,4,64,256]{3,2,1,0:T(8,128)(2,1)S(1)}, bf16[8,4,64,256]{3,2,1,0:T(8,128)(2,1)}, u32[]{:S(2)}) %copy-start.3) | copy-done | bytes 1048600
  48.9 2.5 %first_grad_body.1 = (bf16[4,128,512]{2,1,0:T(8,128)(2,1)S(1)}, bf16[4,128,512]{2,1,0:T(8,128)(2,1)S(1)}, bf16[4,128,512]{2,1,0:T(8,128)(2,1)S(1)}, bf16[4,128,5...) custom-call(bf16[8,4,64,256]{3,2,1,0:T(8,128)(2,1)S(1)} %copy-done.3, bf16[2048,256]{1,0:T(8,128)(2,1)S(1)} %bitcast.16, ...), custom_call_target="tpu_custom_call" | custom-call | tf_op jit(solution)/shard_map/first_grad_body/pallas_call | solution.py:31
  51.4 1.0 %copy-done.7 = bf16[4,512,256]{2,1,0:T(8,128)(2,1)} copy-done((bf16[4,512,256]{2,1,0:T(8,128)(2,1)}, bf16[4,512,256]{2,1,0:T(8,128)(2,1)S(1)}, u32[]{:S(2)}) %copy-start.7) | copy-done | bytes 1048600
  52.4 0.0 collective-permute-start.6
  52.4 0.5 collective-permute-start.7
  52.9 1.4 %collective-permute-done.6.got_a = bf16[4,128,512]{2,1,0:T(8,128)(2,1)S(1)} collective-permute-done((bf16[4,128,512]{2,1,0:T(8,128)(2,1)S(1)}, bf16[4,128,512]{2,1,0:T(8,128)(2,1)S(1)}, u32[]{:S(2)}, u32[]{:S(2)}) %collective-permute-start.6) | collective-permute-done | bytes 524320 | tf_op jit(solution)/shard_map/ppermute | solution.py:50
  54.3 0.7 collective-permute-done.7.got_b
  55.1 0.8 %pair_body.1 = (f32[4,128,512]{2,1,0:T(8,128)S(1)}, bf16[1,128,512]{2,1,0:T(8,128)(2,1)S(1)}, bf16[1,128,512]{2,1,0:T(8,128)(2,1)}, bf16[1,128,512]{2,1,0:T(8,128)(2,1)}, bf16[1,128,512]{2,1,0:T(8,128)(2,1)S(1)}) custom-call(bf16[4,128,512]{2,1,0:T(8,128)(2,1)S(1)} %get-tuple-element.32.own_a, bf16[4,128,512]{2,1,0:T(8,128)(2,1)S(1)} %get-tuple-element.33.own_b, ...), custom_call_target="tpu_custom_call" | custom-call | tf_op jit(solution)/shard_map/pair_body/pallas_call | solution.py:31
  55.9 1.4 %collective-permute-start.9 = (bf16[1,128,512]{2,1,0:T(8,128)(2,1)}, bf16[1,128,512]{2,1,0:T(8,128)(2,1)S(1)}, u32[]{:S(2)}, u32[]{:S(2)}) collective-permute-start(bf16[1,128,512]{2,1,0:T(8,128)(2,1)} %get-tuple-element.41), channel_id=1, source_target_pairs={{0,2},{1,3},{2,0},{3,1},{4,6},{5,7},{6,4},{7,5},{8,10},{9,11},{10,... | collective-permute-start | bytes 393224 | tf_op jit(solution)/shard_map/ppermute | solution.py:50
  57.3 0.6 collective-permute-start.10
  57.9 1.4 %collective-permute-start.11 = (bf16[1,128,512]{2,1,0:T(8,128)(2,1)S(1)}, bf16[1,128,512]{2,1,0:T(8,128)(2,1)S(1)}, u32[]{:S(2)}, u32[]{:S(2)}) collective-permute-start(bf16[1,128,512]{2,1,0:T(8,128)(2,1)S(1)} %get-tuple-element.43), channel_id=1, source_target_pairs={{0,2},{1,3},{2,0},{3,1},{4,6},{5,7},{6,4},{7,5},{8,10},{9,11},{10,... | collective-permute-start | bytes 393224 | tf_op jit(solution)/shard_map/ppermute | solution.py:50
  59.3 0.6 collective-permute-start.8
  59.9 6.0 %mix_back_body.1 = (bf16[2048,256]{1,0:T(8,128)(2,1)}, bf16[2048,256]{1,0:T(8,128)(2,1)}) custom-call(bf16[4,128,512]{2,1,0:T(8,128)(2,1)} %refs_0_.3, bf16[4,128,512]{2,1,0:T(8,128)(2,1)} %copy-done.14, bf16[4,128,512]{2,1,0:T(8,128)(2,1)} %copy-done.13, bf16[4,128,512]{2,1,0:T(8,128)(2,1)} %copy-done.15, bf16[4,512,256]{2,1,0:T(8,128)(2,1)} %copy-done.7, ...), custom_call_target="tpu_custom_call" | custom-call | tf_op jit(solution)/shard_map/mix_back_body/pallas_call | solution.py:31
  65.9 0.0 collective-permute-done.9.refs_1_
  65.9 0.0 collective-permute-done.10.refs_2_
  65.9 2.1 %collective-permute-done.11.refs_3_ = bf16[1,128,512]{2,1,0:T(8,128)(2,1)S(1)} collective-permute-done((bf16[1,128,512]{2,1,0:T(8,128)(2,1)S(1)}, bf16[1,128,512]{2,1,0:T(8,128)(2,1)S(1)}, u32[]{:S(2)}, u32[]{:S(2)}) %collective-permute-start.11) | collective-permute-done | bytes 131104 | tf_op jit(solution)/shard_map/ppermute | solution.py:50
  68.0 2.0 %collective-permute-done.8.refs_0_ = bf16[1,128,512]{2,1,0:T(8,128)(2,1)S(1)} collective-permute-done((bf16[1,128,512]{2,1,0:T(8,128)(2,1)S(1)}, bf16[1,128,512]{2,1,0:T(8,128)(2,1)S(1)}, u32[]{:S(2)}, u32[]{:S(2)}) %collective-permute-start.8) | collective-permute-done | bytes 131104 | tf_op jit(solution)/shard_map/ppermute | solution.py:50
  70.0 0.9 %add_body.1 = bf16[4,128,512]{2,1,0:T(8,128)(2,1)} custom-call(f32[4,128,512]{2,1,0:T(8,128)S(1)} %get-tuple-element.40.own, bf16[1,128,512]{2,1,0:T(8,128)(2,1)S(1)} %collective-permute-done.8.refs_0_, bf16[1,128,512]{2,1,0:T(8,128)(2,1)S(1)} %collective-permute-done.9.refs_1_, bf16[1,128,512]{2,1,0:T(8,128)(2,1)S(1)} %collective-permute-done.10.refs_2_, ...), custom_call_target="tpu_custom_call" | custom-call | tf_op jit(solution)/shard_map/add_body/pallas_call | solution.py:31
  70.9 0.3 all-to-all-done
  71.3 1.3 %second_grad_body.1 = (bf16[32,512]{1,0:T(8,128)(2,1)S(1)}, bf16[32,512]{1,0:T(8,128)(2,1)S(1)}, bf16[32,512]{1,0:T(8,128)(2,1)S(1)}, bf16[32,512]{1,0:T(8,128)(2,1)S(1)}) custom-call(bf16[32,64,256]{2,1,0:T(8,128)(2,1)S(1)} %bitcast.17, bf16[2048,256]{1,0:T(8,128)(2,1)S(1)} %gate_body.1.refs_4_.refs_1_), custom_call_target="tpu_custom_call" | custom-call | tf_op jit(solution)/shard_map/second_grad_body/pallas_call | solution.py:31
  72.6 0.1 collective-permute-start.12
  72.7 1.5 %collective-permute-start.13 = (bf16[32,512]{1,0:T(8,128)(2,1)S(1)}, bf16[32,512]{1,0:T(8,128)(2,1)S(1)}, u32[]{:S(2)}, u32[]{:S(2)}) collective-permute-start(bf16[32,512]{1,0:T(8,128)(2,1)S(1)} %get-tuple-element.49), channel_id=1, source_target_pairs={{0,2},{1,3},{2,0},{3,1},{4,6},{5,7},{6,4},{7,5},{8,10},{9,11},{10,... | collective-permute-start | bytes 98312 | tf_op jit(solution)/shard_map/ppermute | solution.py:50
  74.2 0.4 collective-permute-start.14
  74.6 0.7 copy-done.10
  75.2 2.5 %tokens_body.1 = bf16[2048,256]{1,0:T(8,128)(2,1)} custom-call(bf16[32,64,256]{2,1,0:T(8,128)(2,1)S(1)} %bitcast.18, bf16[4,32,512]{2,1,0:T(8,128)(2,1)S(1)} %get-tuple-element.45.second_ref, bf16[2048,256]{1,0:T(8,128)(2,1)S(1)} %copy-done.6, s32[1,256]{1,0:T(1,128)S(1)} %bitcast.24, bf16[2048,256]{1,0:T(8,128)(2,1)S(1)} %copy-done.5), custom_call_target="tpu_custom_call" | custom-call | tf_op jit(solution)/shard_map/tokens_body/pallas_call | solution.py:31
  77.7 0.0 collective-permute-done.12.refs_1_
  77.7 0.0 collective-permute-done.13.refs_2_
  77.7 0.0 collective-permute-done.14.refs_3_
  77.7 1.1 %unpack_body.1 = bf16[256,64]{1,0:T(8,128)(2,1)} custom-call(bf16[32,512]{1,0:T(8,128)(2,1)S(1)} %get-tuple-element.47.refs_0_, bf16[32,512]{1,0:T(8,128)(2,1)S(1)} %collective-permute-done.12.refs_1_, bf16[32,512]{1,0:T(8,128)(2,1)S(1)} %collective-permute-done.13.refs_2_, bf16[32,512]{1,0:T(8,128)(2,1)S(1)} %collective-permute-done.14.refs_3_), custom_call_target="tpu_custom_call" | custom-call | tf_op jit(solution)/shard_map/unpack_body/pallas_call | solution.py:31
  (13 shorter events, 0.0 us)
Async XLA Ops:
  0.6 0.8 %copy-start.8 = (bf16[64,8,32]{0,2,1:T(8,128)(2,1)S(1)}, bf16[64,8,32]{0,2,1:T(8,128)(2,1)}, u32[]{:S(2)}) copy-start(bf16[64,8,32]{0,2,1:T(8,128)(2,1)} %param.9) | copy-start | bytes 98308
  1.9 6.7 %collective-permute-start.2 = (bf16[32,512]{1,0:T(8,128)(2,1)S(1)}, bf16[32,512]{1,0:T(8,128)(2,1)S(1)}, u32[]{:S(2)}, u32[]{:S(2)}) collective-permute-start(bf16[32,512]{1,0:T(8,128)(2,1)S(1)} %pack_body.1.refs_0_), channel_id=1, source_target_pairs={{0,3},{1,2},{2,1},{3,0},{4,7},{5,6},{6,5},{7,4},{8,11},{9,10},{10,... | collective-permute-start | bytes 98312 | tf_op jit(solution)/shard_map/ppermute | solution.py:50
  4.3 4.3 %collective-permute-start.1 = (bf16[32,512]{1,0:T(8,128)(2,1)S(1)}, bf16[32,512]{1,0:T(8,128)(2,1)S(1)}, u32[]{:S(2)}, u32[]{:S(2)}) collective-permute-start(bf16[32,512]{1,0:T(8,128)(2,1)S(1)} %pack_body.1.refs_0_), channel_id=1, source_target_pairs={{0,2},{1,3},{2,0},{3,1},{4,6},{5,7},{6,4},{7,5},{8,10},{9,11},{10,... | collective-permute-start | bytes 98312 | tf_op jit(solution)/shard_map/ppermute | solution.py:50
  5.0 3.7 %collective-permute-start = (bf16[32,512]{1,0:T(8,128)(2,1)S(1)}, bf16[32,512]{1,0:T(8,128)(2,1)S(1)}, u32[]{:S(2)}, u32[]{:S(2)}) collective-permute-start(bf16[32,512]{1,0:T(8,128)(2,1)S(1)} %pack_body.1.refs_0_), channel_id=1, source_target_pairs={{0,1},{1,0},{2,3},{3,2},{4,5},{5,4},{6,7},{7,6},{8,9},{9,8},{10,11... | collective-permute-start | bytes 98312 | tf_op jit(solution)/shard_map/ppermute | solution.py:50
  5.0 0.7 copy-start.9
  5.7 1.2 %copy-start = (bf16[1,2048,256]{2,1,0:T(8,128)(2,1)S(1)}, bf16[1,2048,256]{2,1,0:T(8,128)(2,1)}, u32[]{:S(2)}) copy-start(bf16[1,2048,256]{2,1,0:T(8,128)(2,1)} %param.6) | copy-start | bytes 3145732
  6.9 1.2 %copy-start.4 = (bf16[1,2048,256]{2,1,0:T(8,128)(2,1)S(1)}, bf16[1,2048,256]{2,1,0:T(8,128)(2,1)}, u32[]{:S(2)}) copy-start(bf16[1,2048,256]{2,1,0:T(8,128)(2,1)} %param.7) | copy-start | bytes 3145732
  10.9 6.8 %copy-start.12 = (bf16[4,128,512]{2,1,0:T(8,128)(2,1)S(1)}, bf16[4,128,512]{2,1,0:T(8,128)(2,1)}, u32[]{:S(2)}) copy-start(bf16[4,128,512]{2,1,0:T(8,128)(2,1)} %refs_0_.3) | copy-start | bytes 1572868
  11.0 30.6 %all-to-all-start.1 = ((bf16[8,4,64,256]{3,2,1,0:T(8,128)(2,1)}), bf16[8,4,64,256]{3,2,1,0:T(8,128)(2,1)S(1)}, u32[]{:S(2)}, u32[]{:S(2)}) async-start(bf16[8,4,64,256]{3,2,1,0:T(8,128)(2,1)} %bitcast.6), calls=%async_computation.1 | async-start | bytes 2097152 | tf_op jit(solution)/shard_map/all_to_all | solution.py:357
  17.8 13.5 %collective-permute-start.4 = (bf16[4,128,512]{2,1,0:T(8,128)(2,1)S(1)}, bf16[4,128,512]{2,1,0:T(8,128)(2,1)S(1)}, u32[]{:S(2)}, u32[]{:S(2)}) collective-permute-start(bf16[4,128,512]{2,1,0:T(8,128)(2,1)S(1)} %copy-done.12), channel_id=1, source_target_pairs={{0,2},{1,3},{2,0},{3,1},{4,6},{5,7},{6,4},{7,5},{8,10},{9,11},{10,... | collective-permute-start | bytes 1572872 | tf_op jit(solution)/shard_map/ppermute | solution.py:50
  19.2 12.0 %collective-permute-start.3 = (bf16[4,128,512]{2,1,0:T(8,128)(2,1)S(1)}, bf16[4,128,512]{2,1,0:T(8,128)(2,1)S(1)}, u32[]{:S(2)}, u32[]{:S(2)}) collective-permute-start(bf16[4,128,512]{2,1,0:T(8,128)(2,1)S(1)} %copy-done.12), channel_id=1, source_target_pairs={{0,1},{1,0},{2,3},{3,2},{4,5},{5,4},{6,7},{7,6},{8,9},{9,8},{10,11... | collective-permute-start | bytes 1572872 | tf_op jit(solution)/shard_map/ppermute | solution.py:50
  31.2 2.7 %copy-start.13 = (bf16[4,128,512]{2,1,0:T(8,128)(2,1)}, bf16[4,128,512]{2,1,0:T(8,128)(2,1)S(1)}, u32[]{:S(2)}) copy-start(bf16[4,128,512]{2,1,0:T(8,128)(2,1)S(1)} %collective-permute-done.4.refs_2_) | copy-start | bytes 1572868
  31.2 1.9 %collective-permute-start.5 = (bf16[4,128,512]{2,1,0:T(8,128)(2,1)S(1)}, bf16[4,128,512]{2,1,0:T(8,128)(2,1)S(1)}, u32[]{:S(2)}, u32[]{:S(2)}) collective-permute-start(bf16[4,128,512]{2,1,0:T(8,128)(2,1)S(1)} %collective-permute-done.4.refs_2_), channel_id=1, source_target_pairs={{0,1},{1,0},{2,3},{3,2},{4,5},{5,4},{6,7},{7,6},{8,9},{9,8},{10,11... | collective-permute-start | bytes 1572872 | tf_op jit(solution)/shard_map/ppermute | solution.py:50
  31.3 2.7 %copy-start.14 = (bf16[4,128,512]{2,1,0:T(8,128)(2,1)}, bf16[4,128,512]{2,1,0:T(8,128)(2,1)S(1)}, u32[]{:S(2)}) copy-start(bf16[4,128,512]{2,1,0:T(8,128)(2,1)S(1)} %collective-permute-done.3.refs_1_) | copy-start | bytes 1572868
  33.2 0.8 %copy-start.15 = (bf16[4,128,512]{2,1,0:T(8,128)(2,1)}, bf16[4,128,512]{2,1,0:T(8,128)(2,1)S(1)}, u32[]{:S(2)}) copy-start(bf16[4,128,512]{2,1,0:T(8,128)(2,1)S(1)} %collective-permute-done.5.refs_3_) | copy-start | bytes 1572868
  40.1 7.5 %copy-start.1 = (bf16[1,2048,256]{2,1,0:T(8,128)(2,1)S(1)}, bf16[1,2048,256]{2,1,0:T(8,128)(2,1)}, u32[]{:S(2)}) copy-start(bf16[1,2048,256]{2,1,0:T(8,128)(2,1)} %param.6) | copy-start | bytes 3145732
  40.1 7.5 %copy-start.11 = (s32[512]{0:T(512)S(1)}, s32[512]{0:T(512)}, u32[]{:S(2)}) copy-start(s32[512]{0:T(512)} %param.11) | copy-start | bytes 6148
  41.5 1.0 %copy-start.2 = (bf16[8,4,64,256]{3,2,1,0:T(8,128)(2,1)}, bf16[8,4,64,256]{3,2,1,0:T(8,128)(2,1)S(1)}, u32[]{:S(2)}) copy-start(bf16[8,4,64,256]{3,2,1,0:T(8,128)(2,1)S(1)} %all-to-all-done.1.refs_0_) | copy-start | bytes 3145732
  42.5 28.8 %all-to-all-start = ((bf16[8,4,64,256]{3,2,1,0:T(8,128)(2,1)}), bf16[8,4,64,256]{3,2,1,0:T(8,128)(2,1)S(1)}, u32[]{:S(2)}, u32[]{:S(2)}) async-start(bf16[8,4,64,256]{3,2,1,0:T(8,128)(2,1)} %mix_body.1), calls=%async_computation | async-start | bytes 2097152 | tf_op jit(solution)/shard_map/all_to_all | solution.py:386
  47.7 1.2 %copy-start.3 = (bf16[8,4,64,256]{3,2,1,0:T(8,128)(2,1)S(1)}, bf16[8,4,64,256]{3,2,1,0:T(8,128)(2,1)}, u32[]{:S(2)}) copy-start(bf16[8,4,64,256]{3,2,1,0:T(8,128)(2,1)} %copy-done.2) | copy-start | bytes 3145732
  51.4 1.0 %copy-start.7 = (bf16[4,512,256]{2,1,0:T(8,128)(2,1)}, bf16[4,512,256]{2,1,0:T(8,128)(2,1)S(1)}, u32[]{:S(2)}) copy-start(bf16[4,512,256]{2,1,0:T(8,128)(2,1)S(1)} %get-tuple-element.37.refs_4_) | copy-start | bytes 3145732
  52.4 1.9 %collective-permute-start.6 = (bf16[4,128,512]{2,1,0:T(8,128)(2,1)S(1)}, bf16[4,128,512]{2,1,0:T(8,128)(2,1)S(1)}, u32[]{:S(2)}, u32[]{:S(2)}) collective-permute-start(bf16[4,128,512]{2,1,0:T(8,128)(2,1)S(1)} %get-tuple-element.34), channel_id=1, source_target_pairs={{0,1},{1,0},{2,3},{3,2},{4,5},{5,4},{6,7},{7,6},{8,9},{9,8},{10,11... | collective-permute-start | bytes 1572872 | tf_op jit(solution)/shard_map/ppermute | solution.py:50
  52.4 2.7 %collective-permute-start.7 = (bf16[4,128,512]{2,1,0:T(8,128)(2,1)S(1)}, bf16[4,128,512]{2,1,0:T(8,128)(2,1)S(1)}, u32[]{:S(2)}, u32[]{:S(2)}) collective-permute-start(bf16[4,128,512]{2,1,0:T(8,128)(2,1)S(1)} %get-tuple-element.35), channel_id=1, source_target_pairs={{0,1},{1,0},{2,3},{3,2},{4,5},{5,4},{6,7},{7,6},{8,9},{9,8},{10,11... | collective-permute-start | bytes 1572872 | tf_op jit(solution)/shard_map/ppermute | solution.py:50
  55.9 10.0 %collective-permute-start.9 = (bf16[1,128,512]{2,1,0:T(8,128)(2,1)}, bf16[1,128,512]{2,1,0:T(8,128)(2,1)S(1)}, u32[]{:S(2)}, u32[]{:S(2)}) collective-permute-start(bf16[1,128,512]{2,1,0:T(8,128)(2,1)} %get-tuple-element.41), channel_id=1, source_target_pairs={{0,2},{1,3},{2,0},{3,1},{4,6},{5,7},{6,4},{7,5},{8,10},{9,11},{10,... | collective-permute-start | bytes 393224 | tf_op jit(solution)/shard_map/ppermute | solution.py:50
  57.3 8.7 %collective-permute-start.10 = (bf16[1,128,512]{2,1,0:T(8,128)(2,1)}, bf16[1,128,512]{2,1,0:T(8,128)(2,1)S(1)}, u32[]{:S(2)}, u32[]{:S(2)}) collective-permute-start(bf16[1,128,512]{2,1,0:T(8,128)(2,1)} %get-tuple-element.42), channel_id=1, source_target_pairs={{0,2},{1,3},{2,0},{3,1},{4,6},{5,7},{6,4},{7,5},{8,10},{9,11},{10,... | collective-permute-start | bytes 393224 | tf_op jit(solution)/shard_map/ppermute | solution.py:50
  57.9 10.1 %collective-permute-start.11 = (bf16[1,128,512]{2,1,0:T(8,128)(2,1)S(1)}, bf16[1,128,512]{2,1,0:T(8,128)(2,1)S(1)}, u32[]{:S(2)}, u32[]{:S(2)}) collective-permute-start(bf16[1,128,512]{2,1,0:T(8,128)(2,1)S(1)} %get-tuple-element.43), channel_id=1, source_target_pairs={{0,2},{1,3},{2,0},{3,1},{4,6},{5,7},{6,4},{7,5},{8,10},{9,11},{10,... | collective-permute-start | bytes 393224 | tf_op jit(solution)/shard_map/ppermute | solution.py:50
  59.3 10.8 %collective-permute-start.8 = (bf16[1,128,512]{2,1,0:T(8,128)(2,1)S(1)}, bf16[1,128,512]{2,1,0:T(8,128)(2,1)S(1)}, u32[]{:S(2)}, u32[]{:S(2)}) collective-permute-start(bf16[1,128,512]{2,1,0:T(8,128)(2,1)S(1)} %get-tuple-element.36), channel_id=1, source_target_pairs={{0,2},{1,3},{2,0},{3,1},{4,6},{5,7},{6,4},{7,5},{8,10},{9,11},{10,... | collective-permute-start | bytes 393224 | tf_op jit(solution)/shard_map/ppermute | solution.py:50
  71.3 3.3 %copy-start.5 = (bf16[2048,256]{1,0:T(8,128)(2,1)S(1)}, bf16[2048,256]{1,0:T(8,128)(2,1)}, u32[]{:S(2)}) copy-start(bf16[2048,256]{1,0:T(8,128)(2,1)} %get-tuple-element.38.back_ref) | copy-start | bytes 3145732
  71.3 3.3 %copy-start.6 = (bf16[2048,256]{1,0:T(8,128)(2,1)S(1)}, bf16[2048,256]{1,0:T(8,128)(2,1)}, u32[]{:S(2)}) copy-start(bf16[2048,256]{1,0:T(8,128)(2,1)} %get-tuple-element.46.h_ref) | copy-start | bytes 3145732
  72.6 5.1 %collective-permute-start.12 = (bf16[32,512]{1,0:T(8,128)(2,1)S(1)}, bf16[32,512]{1,0:T(8,128)(2,1)S(1)}, u32[]{:S(2)}, u32[]{:S(2)}) collective-permute-start(bf16[32,512]{1,0:T(8,128)(2,1)S(1)} %get-tuple-element.48), channel_id=1, source_target_pairs={{0,1},{1,0},{2,3},{3,2},{4,5},{5,4},{6,7},{7,6},{8,9},{9,8},{10,11... | collective-permute-start | bytes 98312 | tf_op jit(solution)/shard_map/ppermute | solution.py:50
  72.7 5.0 %collective-permute-start.13 = (bf16[32,512]{1,0:T(8,128)(2,1)S(1)}, bf16[32,512]{1,0:T(8,128)(2,1)S(1)}, u32[]{:S(2)}, u32[]{:S(2)}) collective-permute-start(bf16[32,512]{1,0:T(8,128)(2,1)S(1)} %get-tuple-element.49), channel_id=1, source_target_pairs={{0,2},{1,3},{2,0},{3,1},{4,6},{5,7},{6,4},{7,5},{8,10},{9,11},{10,... | collective-permute-start | bytes 98312 | tf_op jit(solution)/shard_map/ppermute | solution.py:50
  74.2 3.6 %collective-permute-start.14 = (bf16[32,512]{1,0:T(8,128)(2,1)S(1)}, bf16[32,512]{1,0:T(8,128)(2,1)S(1)}, u32[]{:S(2)}, u32[]{:S(2)}) collective-permute-start(bf16[32,512]{1,0:T(8,128)(2,1)S(1)} %get-tuple-element.50), channel_id=1, source_target_pairs={{0,3},{1,2},{2,1},{3,0},{4,7},{5,6},{6,5},{7,4},{8,11},{9,10},{10,... | collective-permute-start | bytes 98312 | tf_op jit(solution)/shard_map/ppermute | solution.py:50
  74.6 0.7 copy-start.10
